TPU v7x, 32 devices: a whole 2x2x4 slice. The times are simulated.
32 devices in a mesh: seq: 8 (over y, x, core), tensor: 4 (over z).
Axes of the slice: x: 2, y: 2, z: 4, core: 2. Of those that a mesh axis runs over, the one named last changes fastest.
Arguments:
- hidden: bfloat16 [4096, 4096], P('seq', 'tensor'), may hold values from -64 to 64
- depth: int32 [4096], P('seq'), may hold values from 1 to 4, as said below
- norm_gain: float32 [4096], replicated, may hold values from 0.1 to 1.9
- w_query: bfloat16 [4096, 2048], P(None, 'tensor'), may hold values from -1 to 1
- w_key: bfloat16 [4096, 2048], P(None, 'tensor'), may hold values from -12 to 12
- w_value: bfloat16 [4096, 2048], P(None, 'tensor'), may hold values from -0.09375 to 0.09375
- w_out: bfloat16 [2048, 4096], P('tensor'), may hold values from -0.125 to 0.125
Outputs:
- updated: bfloat16 [4096, 4096], P('seq', 'tensor')
Inputs may be any that keep to these rules, and one draw needn't show every extreme that they name: A token takes part in recursion two when its depth is 2 or more; exactly half of the 4096 tokens take part, and the share of such tokens differs between blocks of 512 tokens.
All inputs are finite; a program needn't handle non-finite values.
Results may differ from a plain program's by a relative error of at most 0.006.
Values may be sent and summed in bfloat16 or wider, within the bound.
No kernel may reach another device: no remote copies, remote signals or barrier semaphores. Data moves between devices by JAX's collectives and lax.ppermute only.
A program may use at most 128 MiB of HBM per device.

v0:
```python
from functools import partial
import math

import jax
import jax.numpy as jnp
from jax import lax
from jax.sharding import PartitionSpec as P

HEAD = 128


def attend(carry, piece, start, queries, query_place, scale):
    keys, values, key_place = piece
    count = keys.shape[0]
    span = math.gcd(count, 1024)
    heads = queries.shape[1]
    keys = keys.reshape(count // span, span, heads, HEAD)
    values = values.reshape(count // span, span, heads, HEAD)
    key_place = key_place.reshape(count // span, span)

    def step(state, block):
        best, total, summed = state
        key_part, value_part, place_part = block
        scores = (
            jnp.einsum("qhd,khd->hqk", queries, key_part, preferred_element_type=jnp.float32)
            * scale
        )
        allowed = place_part[None, None, :] <= query_place[None, :, None]
        scores = jnp.where(allowed, scores, -1e30)
        newbest = jnp.maximum(best, jnp.max(scores, axis=2))
        factor = jnp.exp(best - newbest)
        weights = jnp.exp(scores - newbest[:, :, None])
        total = total * factor + jnp.sum(weights, axis=2)
        summed = summed * jnp.transpose(factor)[:, :, None] + jnp.einsum(
            "hqk,khd->qhd",
            weights.astype(jnp.bfloat16),
            value_part,
            preferred_element_type=jnp.float32,
        )
        return ((newbest, total, summed), None)

    carry, unused = lax.scan(step, carry, (keys, values, key_place))
    return carry


def shards(hidden, depth, norm_gain, w_query, w_key, w_value, w_out):
    rows = hidden.shape[0]
    seq_count = lax.axis_size("seq")
    beyond = rows * seq_count
    order = jnp.arange(rows, dtype=jnp.int32)
    places = lax.axis_index("seq") * rows + order
    active = depth >= 2
    key_place = jnp.where(active, places, beyond)
    work_rows, query_place, work_keys = (hidden, places, key_place)
    rows_here = work_rows.shape[0]
    whole = lax.all_gather(work_rows, "tensor", axis=1, tiled=True)
    values32 = whole.astype(jnp.float32)
    row_scale = lax.rsqrt(jnp.mean(values32 * values32, axis=1) + 1e-05)
    normed = (values32 * row_scale[:, None] * norm_gain[None, :]).astype(jnp.bfloat16)
    query_sum = jnp.dot(normed, w_query, preferred_element_type=jnp.float32)
    key_sum = jnp.dot(normed, w_key, preferred_element_type=jnp.float32)
    value_sum = jnp.dot(normed, w_value, preferred_element_type=jnp.float32)
    queries = query_sum.astype(jnp.bfloat16).reshape(rows_here, -1, HEAD)
    keys = key_sum.astype(jnp.bfloat16)
    values = value_sum.astype(jnp.bfloat16)
    heads_here = queries.shape[1]
    start_state = (
        jnp.full((heads_here, rows_here), -1e30, jnp.float32),
        jnp.zeros((heads_here, rows_here), jnp.float32),
        jnp.zeros((rows_here, heads_here, HEAD), jnp.float32),
    )
    folding = partial(attend, queries=queries, query_place=query_place, scale=1.0 / math.sqrt(HEAD))
    best, total, summed = folding(
        start_state,
        (
            lax.all_gather(keys, "seq", axis=0, tiled=True),
            lax.all_gather(values, "seq", axis=0, tiled=True),
            lax.all_gather(work_keys, "seq", axis=0, tiled=True),
        ),
        jnp.int32(0),
    )
    attended = (
        (summed / jnp.transpose(total)[:, :, None])
        .reshape(rows_here, heads_here * HEAD)
        .astype(jnp.bfloat16)
    )
    all_heads = lax.all_gather(attended, "tensor", axis=1, tiled=True)
    out_part = lax.all_to_all(w_out, "tensor", split_axis=1, concat_axis=0, tiled=True)
    shares = jnp.dot(all_heads, out_part, preferred_element_type=jnp.float32)
    renewed = (work_rows.astype(jnp.float32) + shares).astype(jnp.bfloat16)
    return jnp.where(active[:, None], renewed, hidden)


def solution(mesh):
    return jax.shard_map(
        shards,
        mesh=mesh,
        in_specs=(
            P("seq", "tensor"),
            P("seq"),
            P(),
            P(None, "tensor"),
            P(None, "tensor"),
            P(None, "tensor"),
            P("tensor", None),
        ),
        out_specs=P("seq", "tensor"),
        check_vma=False,
    )
```

profile of v0, /device:TPU:0, one launch (start us, length us, event | category | flops | bytes accessed | tf_op | source)
XLA Modules:
  0.0 284.8 jit_solution(15627896989990804317)
XLA Ops:
  6.5 0.0 all-gather.6.cloned.1.call-start
  6.5 0.7 all-gather.6.cloned.1.call-update
  7.3 0.0 all-gather.8.cloned.1.call-start
  7.3 85.1 %all-gather.6.cloned.1.call-done = bf16[512,4096]{1,0:T(8,128)(2,1)} async-done(((bf16[512,1024]{1,0:T(8,128)(2,1)}), bf16[512,4096]{1,0:T(8,128)(2,1)}) %all-gather.6.cloned.1.call-update) | async-done | bytes 4194320 | tf_op jit(solution)/shard_map/all_gather | solution.py:56
  92.4 3.2 %fusion.20 = f32[512]{0:T(512)S(1)} fusion(bf16[512,4096]{1,0:T(8,128)(2,1)} %all-gather.6.cloned.1.call-done), kind=kLoop, calls=%fused_computation.28 | loop fusion | flops 6290944 | bytes 4196352 | tf_op jit(solution)/shard_map/reduce_sum | solution.py:58
  95.7 0.0 copy-done.6
  95.7 0.2 copy-done.1
  95.9 5.4 %convolution_convert_fusion.2 = bf16[512,512]{1,0:T(8,128)(2,1)} fusion(bf16[4096,512]{1,0:T(8,128)(2,1)} %param.13, bf16[512,4096]{1,0:T(8,128)(2,1)S(1)} %copy-done.1, f32[4096]{0:T(1024)S(1)} %copy-done.6, f32[512]{0:T(512)S(1)} %add_rsqrt_fusion), kind=kOutput, calls=%fused_computation.35 | convolution fusion | flops 2156134400 | bytes 8931328 | tf_op jit(solution)/shard_map/dot_general | solution.py:61
  101.2 0.0 all-gather.8.cloned.1.call-update
  101.3 0.0 all-gather.10.cloned.1.call-start
  101.3 6.7 %convolution_convert_fusion = bf16[512,512]{1,0:T(8,128)(2,1)} fusion(bf16[4096,512]{1,0:T(8,128)(2,1)} %param.14, bf16[512,4096]{1,0:T(8,128)(2,1)} %all-gather.6.cloned.1.call-done, f32[4096]{0:T(1024)S(1)} %copy-done.6, f32[512]{0:T(512)S(1)} %add_rsqrt_fusion), kind=kOutput, calls=%fused_computation.33 | convolution fusion | flops 2156134400 | bytes 8931328 | tf_op jit(solution)/shard_map/dot_general | solution.py:62
  108.0 0.0 all-gather.10.cloned.1.call-update
  108.0 6.6 %copy.26 = bf16[512,4096]{0,1:T(8,128)(2,1)} copy(bf16[512,4096]{1,0:T(8,128)(2,1)} %param.15) | data formatting | bytes 8388608 | tf_op args[6]
  114.6 5.0 %all-to-all-start = ((bf16[512,4,1024]{0,2,1:T(8,128)(2,1)}), bf16[512,4,1024]{0,2,1:T(8,128)(2,1)}, u32[]{:S(2)}, u32[]{:S(2)}) async-start(bf16[512,4,1024]{0,2,1:T(8,128)(2,1)} %bitcast.59), calls=%async_computation | async-start | bytes 8388608 | tf_op jit(solution)/shard_map/all_to_all | solution.py:88
  119.5 0.0 all-gather.12.cloned.1.call-start
  119.6 0.0 copy-done.5
  119.7 9.1 %all-gather = s32[8,1,512]{2,1,0:T(1,128)S(1)} all-gather(s32[1,1,512]{2,1,0:T(1,128)S(1)} %bitcast.65), channel_id=1, replica_groups=mesh['seq'=8,'tensor'=4] {'seq'}, dimensions={0}, use_global_device_ids=true | all-gather | bytes 18432 | tf_op jit(solution)/shard_map/all_gather | solution.py:78
  128.8 6.0 %convolution_convert_fusion.1 = bf16[512,512]{0,1:T(8,128)(2,1)S(1)} fusion(bf16[4096,512]{1,0:T(8,128)(2,1)} %param.12, bf16[512,4096]{1,0:T(8,128)(2,1)} %all-gather.6.cloned.1.call-done, f32[4096]{0:T(1024)S(1)} %copy-done.6, f32[512]{0:T(512)S(1)} %add_rsqrt_fusion), kind=kOutput, calls=%fused_computation.34 | convolution fusion | flops 2156134400 | bytes 8931328 | tf_op jit(solution)/shard_map/dot_general | solution.py:60
  134.8 0.3 copy.24
  135.1 1.7 all-gather.8.cloned.1.call-done
  136.7 6.9 %reshape.63 = bf16[4,1024,4,128]{3,2,1,0:T(4,128)(2,1)} reshape(bf16[4096,512]{1,0:T(8,128)(2,1)} %all-gather.8.cloned.1.call-done) | data formatting | bytes 8388608 | tf_op jit(solution)/shard_map/reshape | solution.py:17
  143.6 31.8 %all-gather.10.cloned.1.call-done = bf16[4096,512]{1,0:T(8,128)(2,1)} async-done(((bf16[512,512]{1,0:T(8,128)(2,1)}), bf16[4096,512]{1,0:T(8,128)(2,1)}) %all-gather.10.cloned.1.call-update) | async-done | bytes 4194320 | tf_op jit(solution)/shard_map/all_gather | solution.py:77
  175.4 6.9 %reshape.65 = bf16[4,1024,4,128]{3,2,1,0:T(4,128)(2,1)} reshape(bf16[4096,512]{1,0:T(8,128)(2,1)} %all-gather.10.cloned.1.call-done) | data formatting | bytes 8388608 | tf_op jit(solution)/shard_map/reshape | solution.py:18
  182.3 41.6 %while.15 = (s32[]{:T(128)}, f32[4,512]{1,0:T(4,128)S(1)}, f32[4,512]{1,0:T(4,128)S(1)}, f32[512,4,128]{0,2,1:T(8,128)}, s32[4,1024]{1,0:T(4,128)S(1)}, /*index=...) while((s32[]{:T(128)}, f32[4,512]{1,0:T(4,128)S(1)}, ...), condition=%wide.region_4.5_spmd.clone, body=%wide.region_1.4_spmd.clone.sunk | while | flops 1098134016 | bytes 51003616 | solution.py:42
  182.3 0.4 broadcast_compare_fusion.4
  182.7 2.3 constant_dynamic-slice_fusion.6
  184.9 1.5 copy.38
  186.5 1.7 fusion.44
  188.1 0.0 copy-done
  188.2 0.0 copy-done.2
  188.2 2.6 fusion.48
  190.8 0.0 copy-start.3
  190.8 1.8 fusion.46
  192.6 0.0 copy-done.3
  192.7 0.4 broadcast_compare_fusion.4
  193.1 2.3 constant_dynamic-slice_fusion.6
  195.4 1.5 copy.38
  196.9 1.7 fusion.44
  198.6 2.6 fusion.48
  201.2 0.0 copy-start.3
  201.2 1.8 fusion.46
  203.1 0.4 broadcast_compare_fusion.4
  203.5 2.3 constant_dynamic-slice_fusion.6
  205.8 1.5 copy.38
  207.3 1.7 fusion.44
  209.0 2.6 fusion.48
  211.6 0.0 copy-start.3
  211.6 1.8 fusion.46
  213.5 0.4 broadcast_compare_fusion.4
  213.9 2.3 constant_dynamic-slice_fusion.6
  216.2 1.5 copy.38
  217.7 1.7 fusion.44
  219.4 2.6 fusion.48
  222.0 0.0 copy-start.3
  222.0 1.8 fusion.46
  223.8 0.0 copy-done.3
  223.9 2.1 divide_convert_fusion
  226.1 0.0 all-gather.12.cloned.1.call-update
  226.1 0.0 all-to-all-done
  226.1 0.0 copy-start.4
  226.1 6.4 %copy.27 = bf16[4,512,1024]{2,1,0:T(8,128)(2,1)} copy(bf16[4,512,1024]{1,2,0:T(8,128)(2,1)} %bitcast.5) | data formatting | bytes 8388608 | tf_op jit(solution)/shard_map/all_to_all | solution.py:88
  232.5 39.7 %all-gather.12.cloned.1.call-done = bf16[512,2048]{0,1:T(8,128)(2,1)} async-done(((bf16[512,512]{0,1:T(8,128)(2,1)}), bf16[512,2048]{0,1:T(8,128)(2,1)}) %all-gather.12.cloned.1.call-update) | async-done | bytes 2097168 | tf_op jit(solution)/shard_map/all_gather | solution.py:87
  272.2 0.0 copy-done.4
  272.2 6.1 %fusion.23 = bf16[512,1024]{1,0:T(8,128)(2,1)} fusion(bf16[512,1024]{1,0:T(8,128)(2,1)S(1)} %copy-done.4, bf16[512,2048]{0,1:T(8,128)(2,1)} %all-gather.12.cloned.1.call-done, bf16[2048,1024]{1,0:T(8,128)(2,1)} %bitcast.60, pred[512]{0:T(512)(128)(4,1)S(1)} %get-tuple-element.145), kind=kOutput, calls=%fused_computation.32 | convolution fusion | flops 2149580800 | bytes 8389120 | tf_op jit(solution)/shard_map/dot_general | solution.py:89
  (46 shorter events, 0.3 us)
Async XLA Ops:
  6.5 89.1 %copy-start.6 = (f32[4096]{0:T(1024)S(1)}, f32[4096]{0:T(1024)}, u32[]{:S(2)}) copy-start(f32[4096]{0:T(1024)} %param.11) | copy-start | bytes 49156
  6.5 85.9 %all-gather.6.cloned.1.call-start = ((), (), s32[]{:S(2)}) async-start(), calls=%async_computation.1 | async-start | bytes 5242880 | tf_op jit(solution)/shard_map/all_gather | solution.py:56
  7.3 129.5 %all-gather.8.cloned.1.call-start = ((), (), s32[]{:S(2)}) async-start(), calls=%async_computation.2 | async-start | bytes 4718592 | tf_op jit(solution)/shard_map/all_gather | solution.py:76
  92.4 3.4 %copy-start.1 = (bf16[512,4096]{1,0:T(8,128)(2,1)S(1)}, bf16[512,4096]{1,0:T(8,128)(2,1)}, u32[]{:S(2)}) copy-start(bf16[512,4096]{1,0:T(8,128)(2,1)} %all-gather.6.cloned.1.call-done) | copy-start | bytes 12582916
  101.3 74.1 %all-gather.10.cloned.1.call-start = ((), (), s32[]{:S(2)}) async-start(), calls=%async_computation.3 | async-start | bytes 4718592 | tf_op jit(solution)/shard_map/all_gather | solution.py:77
  114.6 5.1 %copy-start.5 = (s32[512]{0:T(512)S(1)}, s32[512]{0:T(512)}, u32[]{:S(2)}) copy-start(s32[512]{0:T(512)} %param.10) | copy-start | bytes 6148
  114.6 111.5 %all-to-all-start = ((bf16[512,4,1024]{0,2,1:T(8,128)(2,1)}), bf16[512,4,1024]{0,2,1:T(8,128)(2,1)}, u32[]{:S(2)}, u32[]{:S(2)}) async-start(bf16[512,4,1024]{0,2,1:T(8,128)(2,1)} %bitcast.59), calls=%async_computation | async-start | bytes 8388608 | tf_op jit(solution)/shard_map/all_to_all | solution.py:88
  119.5 152.6 %all-gather.12.cloned.1.call-start = ((), (), s32[]{:S(2)}) async-start(), calls=%async_computation.4 | async-start | bytes 2621440 | tf_op jit(solution)/shard_map/all_gather | solution.py:87
  186.5 1.7 copy-start
  186.5 1.7 copy-start.2
  190.8 1.9 copy-start.3
  196.9 1.7 copy-start
  196.9 1.7 copy-start.2
  201.2 1.9 copy-start.3
  207.3 1.7 copy-start
  207.3 1.7 copy-start.2
  211.6 1.9 copy-start.3
  217.7 1.7 copy-start
  217.7 1.7 copy-start.2
  222.0 1.9 copy-start.3
  226.1 46.1 %copy-start.4 = (bf16[512,1024]{1,0:T(8,128)(2,1)S(1)}, bf16[512,1024]{1,0:T(8,128)(2,1)}, u32[]{:S(2)}) copy-start(bf16[512,1024]{1,0:T(8,128)(2,1)} %param.9) | copy-start | bytes 3145732
Sparse Core Ops, SparseCore 0:
  8.9 83.4 all-gather.5
  101.4 35.2 all-gather.7
  138.6 36.7 all-gather.9
  226.2 45.9 all-gather.11
where the time goes:
time: 286 us; the launch traced here: 285 us
  waiting for transfers between devices  159 us (56%)
  local copies, waits for them, and re-layouts  42.5 us (15%)
  matrix products  41.2 us (14%)
  other arithmetic  14.4 us (5%)
  between operations  13.2 us (5%)
  blocking collectives  9.06 us (3%)
  starting transfers between devices  5.11 us (2%)
    all_gather x1, waiting for transfers between devices, shards(): whole = lax.all_gather(work_rows, 'tensor', axis=1, tiled=True)  85.1 us
    all_gather x1, waiting for transfers between devices, shards(): all_heads = lax.all_gather(attended, 'tensor', axis=1, tiled=True)  39.7 us
    all_gather x1, waiting for transfers between devices, shards(): lax.all_gather(values, 'seq', axis=0, tiled=True)  31.8 us
    dynamic_slice x12, local copies, waits for them, and re-layouts, attend(): carry, unused = lax.scan(step, carry, (keys, values, key_place))  15.1 us
    dot_general x4, matrix products, step(): jnp.einsum('hqk,khd->qhd', weights.astype(jnp.bfloat16), value_part, pref...  10.4 us
    all_gather x1, blocking collectives, shards(): lax.all_gather(work_keys, 'seq', axis=0, tiled=True)  9.06 us
    reduce_sum x4, other arithmetic, step(): total = total * factor + jnp.sum(weights, axis=2)  7.38 us
    unnamed x10, local copies, waits for them, and re-layouts  7.04 us
  transfers between devices with their start and end apart: 5, of which 4 were waited for; matrix products, arithmetic and copies ran while one was open for 29% of the time, Pallas kernels for 0%

commit v1 on v0

v1 whole, which is shorter than its diff:
```python
import math
from functools import partial

import jax
import jax.numpy as jnp
from jax import lax
from jax.experimental import pallas as pl
from jax.experimental.pallas import tpu as pltpu
from jax.sharding import PartitionSpec as P

HEAD = 128
MASKED = -1e30
BACK = 2


def project_kernel(group, x_ref, gain_ref, wq_ref, wk_ref, wv_ref, out_ref, normed):
    @pl.when(pl.program_id(0) == 0)
    def _():
        values = x_ref[...].astype(jnp.float32)
        mean = jnp.mean(values * values, axis=1, keepdims=True)
        normed[...] = (values * lax.rsqrt(mean + 1e-05) * gain_ref[...]).astype(jnp.bfloat16)

    part_rows = out_ref.shape[1]
    heads = wq_ref.shape[1] // HEAD
    for which, weight in enumerate((wq_ref, wk_ref, wv_ref)):
        product = jnp.dot(normed[...], weight[...], preferred_element_type=jnp.float32)
        product = product.astype(jnp.bfloat16)
        for head in range(heads):
            for part in range(group):
                out_ref[head * group + part, :, which * HEAD : (which + 1) * HEAD] = product[
                    part * part_rows : (part + 1) * part_rows, head * HEAD : (head + 1) * HEAD
                ]


def project(x, gain, wq, wk, wv, seq_count, group):
    rows, features = x.shape
    width = wq.shape[1]
    block = min(256, width)
    per_step = block // HEAD * group
    part_rows = rows // group
    weight_spec = pl.BlockSpec((features, block), lambda j: (0, j))
    return pl.pallas_call(
        partial(project_kernel, group),
        grid=(width // block,),
        in_specs=[
            pl.BlockSpec((rows, features), lambda j: (0, 0)),
            pl.BlockSpec((1, features), lambda j: (0, 0)),
            weight_spec,
            weight_spec,
            weight_spec,
        ],
        out_specs=pl.BlockSpec((per_step, part_rows, 3 * HEAD), lambda j: (j, 0, 0)),
        out_shape=jax.ShapeDtypeStruct((seq_count, part_rows, 3 * HEAD), jnp.bfloat16),
        scratch_shapes=[pltpu.VMEM((rows, features), jnp.bfloat16)],
        compiler_params=pltpu.CompilerParams(vmem_limit_bytes=44 * 2**20),
        cost_estimate=pl.CostEstimate(
            flops=6 * rows * features * width,
            bytes_accessed=6 * features * width + 2 * rows * (features + 3 * width),
            transcendentals=0,
        ),
    )(x, gain, wq, wk, wv)


def attend_kernel(chunks, group, mine, part_ref, bias_ref, *refs):
    pieces = refs[: chunks * group]
    out_ref, keys, values = refs[chunks * group :]
    seq_count, part_rows, _ = pieces[0].shape
    rows = bias_ref.shape[1]
    chunk_rows = rows // chunks
    part = part_ref[0]

    def place(home, _):
        for chunk in range(chunks):
            for step in range(group):
                owner = lax.rem(part + step, group)
                at = pl.multiple_of(home * rows + chunk * chunk_rows + owner * part_rows, part_rows)
                piece = pieces[chunk * group + step]
                keys[pl.ds(at, part_rows), :] = piece[home, :, HEAD : 2 * HEAD]
                values[pl.ds(at, part_rows), :] = piece[home, :, 2 * HEAD :]
        return 0

    lax.fori_loop(0, seq_count, place, 0)
    scale = math.log2(math.e) / math.sqrt(HEAD)
    count = len(mine) * part_rows

    def one_home(home, _):
        queries = jnp.concatenate([pieces[c * group][home, :, :HEAD] for c in mine], axis=0)

        def fold(other, carry, diagonal):
            best, total, summed = carry
            at = pl.multiple_of(other * rows, rows)
            scores = lax.dot_general(
                queries,
                keys[pl.ds(at, rows), :],
                (((1,), (1,)), ((), ())),
                preferred_element_type=jnp.float32,
            )
            scores = scores * scale + bias_ref[pl.ds(other, 1), :]
            if diagonal:
                order = lax.broadcasted_iota(jnp.int32, (count, rows), 0)
                place_in = lax.broadcasted_iota(jnp.int32, (count, rows), 1)
                own = order % part_rows + part * part_rows
                for at_chunk, chunk in enumerate(mine):
                    own = jnp.where(order // part_rows == at_chunk, own + chunk * chunk_rows, own)
                scores = jnp.where(place_in <= own, scores, MASKED)
            newbest = jnp.maximum(best, jnp.max(scores, axis=1, keepdims=True))
            factor = jnp.exp2(best - newbest)
            weights = jnp.exp2(scores - newbest)
            total = total * factor + jnp.sum(weights, axis=1, keepdims=True)
            summed = summed * factor + jnp.dot(
                weights.astype(jnp.bfloat16),
                values[pl.ds(at, rows), :],
                preferred_element_type=jnp.float32,
            )
            return newbest, total, summed

        start = (
            jnp.full((count, 1), MASKED, jnp.float32),
            jnp.zeros((count, 1), jnp.float32),
            jnp.zeros((count, HEAD), jnp.float32),
        )
        carry = fold(home, start, True)
        carry = lax.fori_loop(0, home, lambda other, c: fold(other, c, False), carry)
        _, total, summed = carry
        out_ref[home] = (summed / total).astype(jnp.bfloat16)
        return 0

    lax.fori_loop(0, seq_count, one_home, 0)


def attend(part, bias, pieces, chunks, group, mine):
    seq_count, part_rows, _ = pieces[0].shape
    rows = bias.shape[1]
    count = len(mine) * part_rows
    vmem = pl.BlockSpec(memory_space=pltpu.VMEM)
    pairs = seq_count * (seq_count + 1) // 2
    return pl.pallas_call(
        partial(attend_kernel, chunks, group, mine),
        in_specs=[pl.BlockSpec(memory_space=pltpu.SMEM), vmem] + [vmem] * len(pieces),
        out_specs=vmem,
        out_shape=jax.ShapeDtypeStruct((seq_count, count, HEAD), jnp.bfloat16),
        scratch_shapes=[
            pltpu.VMEM((seq_count * rows, HEAD), jnp.bfloat16),
            pltpu.VMEM((seq_count * rows, HEAD), jnp.bfloat16),
        ],
        compiler_params=pltpu.CompilerParams(vmem_limit_bytes=56 * 2**20),
        cost_estimate=pl.CostEstimate(
            flops=4 * pairs * count * rows * HEAD,
            bytes_accessed=8 * seq_count * rows * HEAD,
            transcendentals=pairs * count * rows,
        ),
    )(part, bias, *pieces)


def output_kernel(chunks, group, *refs):
    attended_ref, weight_ref, hidden_ref, active_ref = refs[:4]
    out_ref, rows_in = refs[-2:]
    tensor_count, seq_count, count, _ = attended_ref.shape
    heads = seq_count // group
    part_rows = count // chunks
    chunk_rows = part_rows * group

    @pl.when(pl.program_id(0) == 0)
    def _():
        def place(tensor, _):
            for head in range(heads):
                at = pl.multiple_of((tensor * heads + head) * HEAD, HEAD)
                for part in range(group):
                    for chunk in range(chunks):
                        first = chunk * chunk_rows + part * part_rows
                        rows_in[first : first + part_rows, pl.ds(at, HEAD)] = attended_ref[
                            tensor, head * group + part, chunk * part_rows : (chunk + 1) * part_rows, :
                        ]
            return 0

        lax.fori_loop(0, tensor_count, place, 0)

    shares = jnp.dot(rows_in[...], weight_ref[...], preferred_element_type=jnp.float32)
    hidden = hidden_ref[...]
    renewed = (hidden.astype(jnp.float32) + shares).astype(jnp.bfloat16)
    out_ref[...] = jnp.where(active_ref[...] > 0, renewed, hidden)


def output(attended, weight, hidden, active, so_far, which, parts, chunks, group):
    rows, columns = hidden.shape
    here = rows // parts
    depth = weight.shape[0]
    block = min(256, columns)
    operands = [attended, weight, hidden, active]
    whole = lambda j: (0, 0, 0, 0)
    in_specs = [
        pl.BlockSpec(attended.shape, whole),
        pl.BlockSpec((depth, block), lambda j: (0, j)),
        pl.BlockSpec((here, block), lambda j: (which, j)),
        pl.BlockSpec((here, 1), lambda j: (which, 0)),
    ]
    aliases = {}
    if so_far is not None:
        operands.append(so_far)
        in_specs.append(pl.BlockSpec(memory_space=pl.ANY))
        aliases = {4: 0}
    return pl.pallas_call(
        partial(output_kernel, chunks, group),
        grid=(columns // block,),
        in_specs=in_specs,
        out_specs=pl.BlockSpec((here, block), lambda j: (which, j)),
        out_shape=jax.ShapeDtypeStruct((rows, columns), jnp.bfloat16),
        scratch_shapes=[pltpu.VMEM((here, depth), jnp.bfloat16)],
        input_output_aliases=aliases,
        compiler_params=pltpu.CompilerParams(vmem_limit_bytes=40 * 2**20),
        cost_estimate=pl.CostEstimate(
            flops=2 * here * depth * columns,
            bytes_accessed=2 * (here * depth + depth * columns + 2 * here * columns),
            transcendentals=0,
        ),
    )(*operands)


def output_weight(w_out, seq_count, tensor_count, columns):
    heads = w_out.shape[0] // HEAD
    cuts = seq_count // heads
    width = columns // cuts
    if width % HEAD:
        return lax.all_to_all(w_out, "tensor", split_axis=1, concat_axis=0, tiled=True)
    me = lax.axis_index("seq")
    by_owner = w_out.reshape(w_out.shape[0], tensor_count, columns)
    share = lax.dynamic_slice(
        by_owner, ((me // cuts) * HEAD, 0, (me % cuts) * width), (HEAD, tensor_count, width)
    )
    share = jnp.transpose(share, (1, 0, 2))
    share = lax.all_to_all(share, "tensor", split_axis=0, concat_axis=0)
    whole = lax.all_gather(share, "seq", axis=0)
    whole = whole.reshape(heads, cuts, tensor_count, HEAD, width)
    return jnp.transpose(whole, (2, 0, 3, 1, 4)).reshape(tensor_count * heads * HEAD, columns)


def shards(hidden, depth, norm_gain, w_query, w_key, w_value, w_out):
    rows, columns = hidden.shape
    seq_count = lax.axis_size("seq")
    tensor_count = lax.axis_size("tensor")
    heads = w_query.shape[1] // HEAD
    group = seq_count // heads
    chunks = min(4, rows // (16 * group))
    chunk_rows = rows // chunks
    back = min(BACK, chunks)
    part = (lax.axis_index("seq") % group).astype(jnp.int32).reshape(1)
    gain = norm_gain.reshape(1, -1)

    wholes = [
        lax.all_gather(hidden[c * chunk_rows : (c + 1) * chunk_rows], "tensor", axis=1, tiled=True)
        for c in range(chunks)
    ]
    depths = lax.all_gather(depth, "seq", axis=0)
    bias = jnp.where(depths >= 2, 0.0, MASKED).astype(jnp.float32)
    active = (depth >= 2).astype(jnp.int32).reshape(rows, 1)

    pieces = []
    for whole in wholes:
        sent = project(whole, gain, w_query, w_key, w_value, seq_count, group)
        got = lax.all_to_all(sent, "seq", split_axis=0, concat_axis=0)
        pieces.append(got)
        for step in range(1, group):
            ring = [
                (d, d - d % group + (d - step) % group) for d in range(seq_count)
            ]
            pieces.append(lax.ppermute(got, "seq", ring))

    weight = output_weight(w_out, seq_count, tensor_count, columns)
    updated = None
    each = chunks // back
    for which in range(back):
        mine = tuple(range(which * each, (which + 1) * each))
        out = attend(part, bias, pieces, chunks, group, mine)
        home = lax.all_to_all(out, "seq", split_axis=0, concat_axis=0)
        attended = lax.all_gather(home, "tensor", axis=0)
        updated = output(attended, weight, hidden, active, updated, which, back, each, group)
    return updated


def solution(mesh):
    return jax.shard_map(
        shards,
        mesh=mesh,
        in_specs=(
            P("seq", "tensor"),
            P("seq"),
            P(),
            P(None, "tensor"),
            P(None, "tensor"),
            P(None, "tensor"),
            P("tensor", None),
        ),
        out_specs=P("seq", "tensor"),
        check_vma=False,
    )
```

time: 286 us -> 272 us (0.951)
  waiting for transfers between devices: 159 us -> 57.4 us
  Pallas kernels: 0 us -> 64.7 us
  blocking collectives: 9.06 us -> 62.4 us
  matrix products: 41.2 us -> 0 us
  other arithmetic: 14.4 us -> 0.6 us
  local copies, waits for them, and re-layouts: 42.5 us -> 55.3 us
  starting transfers between devices: 5.11 us -> 15.9 us
    all_gather x4 -> x7, waiting for transfers between devices: 158 us -> 48.2 us  [the longest x4 42.3 us: shards(): lax.all_gather(hidden[c * chunk_rows:(c + 1) * chunk_rows], 'tensor', axi...]
    pallas_call x0 -> x8, Pallas kernels: none -> 64.7 us  [the longest x2 37.2 us: attend(): pl.pallas_call(partial(attend_kernel, chunks, group, mine), in_specs=[pl....]
    all_to_all x0 -> x3, blocking collectives: none -> 54.4 us  [the longest x1 32.5 us: output_weight(): share = lax.all_to_all(share, 'tensor', split_axis=0, concat_axis=0)]
    dot_general x12 -> x0, matrix products: 41.2 us -> none  [the longest x4 10.4 us: step(): jnp.einsum('hqk,khd->qhd', weights.astype(jnp.bfloat16), value_part, pref...]
    unnamed x10 -> x56, local copies, waits for them, and re-layouts: 7.04 us -> 42.4 us
    dynamic_slice x12 -> x0, local copies, waits for them, and re-layouts: 15.1 us -> none  [attend(): carry, unused = lax.scan(step, carry, (keys, values, key_place))]
    reshape x3 -> x1, local copies, waits for them, and re-layouts: 13.8 us -> 0.14 us  [shards(): active = (depth >= 2).astype(jnp.int32).reshape(rows, 1)]
    reduce_sum x5 -> x0, other arithmetic: 10.6 us -> none  [the longest x4 7.38 us: step(): total = total * factor + jnp.sum(weights, axis=2)]
  transfers between devices with their start and end apart: 5 -> 15, of which waited for: 4 -> 5; matrix products, arithmetic and copies ran while one was open for 29% -> 9% of each run, Pallas kernels for 0% -> 23%
where the time goes in v1:
time: 272 us; the launch traced here: 270 us
  Pallas kernels  64.7 us (24%)
  blocking collectives  62.4 us (23%)
  waiting for transfers between devices  57.4 us (21%)
  local copies, waits for them, and re-layouts  55.3 us (20%)
  starting transfers between devices  15.9 us (6%)
  between operations  13.7 us (5%)
    unnamed x56, local copies, waits for them, and re-layouts  42.4 us
    all_gather x4, waiting for transfers between devices, shards(): lax.all_gather(hidden[c * chunk_rows:(c + 1) * chunk_rows], 'tensor', axi...  42.3 us
    pallas_call x2, Pallas kernels, attend(): pl.pallas_call(partial(attend_kernel, chunks, group, mine), in_specs=[pl....  37.2 us
    all_to_all x1, blocking collectives, output_weight(): share = lax.all_to_all(share, 'tensor', split_axis=0, concat_axis=0)  32.5 us
    all_to_all x2, blocking collectives, shards(): home = lax.all_to_all(out, 'seq', split_axis=0, concat_axis=0)  21.9 us
    pallas_call x4, Pallas kernels, project(): pl.pallas_call(partial(project_kernel, group), grid=(width // block,), in...  20.6 us
    all_to_all x4, starting transfers between devices, shards(): got = lax.all_to_all(sent, 'seq', split_axis=0, concat_axis=0)  14.6 us
    transpose x1, local copies, waits for them, and re-layouts, output_weight(): jnp.transpose(whole, (2, 0, 3, 1, 4))  8.51 us
  transfers between devices with their start and end apart: 15, of which 5 were waited for; matrix products, arithmetic and copies ran while one was open for 9% of the time, Pallas kernels for 23%

profile of v1, /device:TPU:0, one launch (start us, length us, event | category | flops | bytes accessed | tf_op | source)
XLA Modules:
  0.0 270.0 jit_solution(15313168864171800440)
XLA Ops:
  6.5 2.2 fusion
  8.7 0.0 all-gather.15.cloned.1.call-start
  8.8 0.7 all-gather.15.cloned.1.call-update
  9.5 0.0 all-gather.17.cloned.1.call-start
  9.5 0.7 all-gather.17.cloned.1.call-update
  10.2 0.0 all-gather.19.cloned.1.call-start
  10.3 0.5 all-gather.19.cloned.1.call-update
  10.8 0.0 all-gather.23.cloned.1.call-start
  10.9 6.5 %copy.18 = bf16[512,4096]{0,1:T(8,128)(2,1)} copy(bf16[512,4096]{1,0:T(8,128)(2,1)} %param.13) | data formatting | bytes 8388608 | tf_op args[6]
  17.4 1.1 dynamic-slice_bitcast_fusion
  18.5 32.5 %all_to_all.35 = bf16[4,128,512]{1,2,0:T(8,128)(2,1)S(1)} all-to-all(bf16[4,128,512]{1,2,0:T(8,128)(2,1)S(1)} %dynamic-slice_bitcast_fusion), channel_id=1, replica_groups=mesh['seq'=8,'tensor'=4] {'tensor'}, dimensions={0} | all-to-all | bytes 1048576 | tf_op jit(solution)/shard_map/all_to_all | solution.py:231
  51.0 1.0 copy.19
  52.0 0.0 all-gather.13.cloned.1.call-done.x_ref
  52.1 2.2 copy-done
  54.3 2.2 copy-done.4
  56.5 1.2 copy-done.15
  57.7 5.2 %shard_map.73 = bf16[8,64,384]{2,1,0:T(8,128)(2,1)} custom-call(bf16[128,4096]{1,0:T(8,128)(2,1)S(1)} %copy-done.15, f32[1,4096]{1,0:T(1,128)S(1)} %bitcast.21, bf16[4096,512]{1,0:T(8,128)(2,1)S(1)} %copy-done, bf16[4096,512]{1,0:T(8,128)(2,1)S(1)} %copy-done.4, bf16[4096,512]{1,0:T(8,128)(2,1)} %wv_ref.7), custom_call_target="tpu_custom_call" | custom-call | flops 1610612736 | bytes 14024704 | tf_op jit(solution)/shard_map/pallas_call | solution.py:42
  62.9 3.6 %all-to-all-start = ((bf16[8,64,384]{2,1,0:T(8,128)(2,1)}), bf16[8,64,384]{2,1,0:T(8,128)(2,1)S(1)}, u32[]{:S(2)}, u32[]{:S(2)}) async-start(bf16[8,64,384]{2,1,0:T(8,128)(2,1)} %shard_map.73), calls=%async_computation | async-start | bytes 786432 | tf_op jit(solution)/shard_map/all_to_all | solution.py:260
  66.5 13.2 %all-gather.15.cloned.1.call-done.x_ref = bf16[128,4096]{1,0:T(8,128)(2,1)} async-done(((bf16[128,1024]{1,0:T(8,128)(2,1)}), bf16[128,4096]{1,0:T(8,128)(2,1)}) %all-gather.15.cloned.1.call-update) | async-done | bytes 1048592 | tf_op jit(solution)/shard_map/all_gather | solution.py:250
  79.7 2.2 copy-done.1
  81.9 2.2 copy-done.5
  84.1 1.2 copy-done.14
  85.3 5.1 %shard_map.74 = bf16[8,64,384]{2,1,0:T(8,128)(2,1)} custom-call(bf16[128,4096]{1,0:T(8,128)(2,1)S(1)} %copy-done.14, f32[1,4096]{1,0:T(1,128)S(1)} %bitcast.22, bf16[4096,512]{1,0:T(8,128)(2,1)S(1)} %copy-done.1, bf16[4096,512]{1,0:T(8,128)(2,1)S(1)} %copy-done.5, bf16[4096,512]{1,0:T(8,128)(2,1)} %wv_ref.7), custom_call_target="tpu_custom_call" | custom-call | flops 1610612736 | bytes 14024704 | tf_op jit(solution)/shard_map/pallas_call | solution.py:42
  90.4 3.7 %all-to-all-start.1 = ((bf16[8,64,384]{2,1,0:T(8,128)(2,1)}), bf16[8,64,384]{2,1,0:T(8,128)(2,1)S(1)}, u32[]{:S(2)}, u32[]{:S(2)}) async-start(bf16[8,64,384]{2,1,0:T(8,128)(2,1)} %shard_map.74), calls=%async_computation.1 | async-start | bytes 786432 | tf_op jit(solution)/shard_map/all_to_all | solution.py:260
  94.1 14.6 %all-gather.17.cloned.1.call-done.x_ref = bf16[128,4096]{1,0:T(8,128)(2,1)} async-done(((bf16[128,1024]{1,0:T(8,128)(2,1)}), bf16[128,4096]{1,0:T(8,128)(2,1)}) %all-gather.17.cloned.1.call-update) | async-done | bytes 1048592 | tf_op jit(solution)/shard_map/all_gather | solution.py:250
  108.7 2.2 copy-done.2
  110.9 2.2 copy-done.6
  113.1 1.2 copy-done.13
  114.3 5.1 %shard_map.75 = bf16[8,64,384]{2,1,0:T(8,128)(2,1)} custom-call(bf16[128,4096]{1,0:T(8,128)(2,1)S(1)} %copy-done.13, f32[1,4096]{1,0:T(1,128)S(1)} %bitcast.23, bf16[4096,512]{1,0:T(8,128)(2,1)S(1)} %copy-done.2, bf16[4096,512]{1,0:T(8,128)(2,1)S(1)} %copy-done.6, bf16[4096,512]{1,0:T(8,128)(2,1)} %wv_ref.7), custom_call_target="tpu_custom_call" | custom-call | flops 1610612736 | bytes 14024704 | tf_op jit(solution)/shard_map/pallas_call | solution.py:42
  119.5 3.6 %all-to-all-start.2 = ((bf16[8,64,384]{2,1,0:T(8,128)(2,1)}), bf16[8,64,384]{2,1,0:T(8,128)(2,1)S(1)}, u32[]{:S(2)}, u32[]{:S(2)}) async-start(bf16[8,64,384]{2,1,0:T(8,128)(2,1)} %shard_map.75), calls=%async_computation.2 | async-start | bytes 786432 | tf_op jit(solution)/shard_map/all_to_all | solution.py:260
  123.1 14.5 %all-gather.19.cloned.1.call-done.x_ref = bf16[128,4096]{1,0:T(8,128)(2,1)} async-done(((bf16[128,1024]{1,0:T(8,128)(2,1)}), bf16[128,4096]{1,0:T(8,128)(2,1)}) %all-gather.19.cloned.1.call-update) | async-done | bytes 1048592 | tf_op jit(solution)/shard_map/all_gather | solution.py:250
  137.6 2.2 copy-done.3
  139.8 2.2 copy-done.7
  142.0 1.2 copy-done.12
  143.2 5.1 %shard_map.76 = bf16[8,64,384]{2,1,0:T(8,128)(2,1)} custom-call(bf16[128,4096]{1,0:T(8,128)(2,1)S(1)} %copy-done.12, f32[1,4096]{1,0:T(1,128)S(1)} %bitcast.24, bf16[4096,512]{1,0:T(8,128)(2,1)S(1)} %copy-done.3, bf16[4096,512]{1,0:T(8,128)(2,1)S(1)} %copy-done.7, bf16[4096,512]{1,0:T(8,128)(2,1)} %wv_ref.7), custom_call_target="tpu_custom_call" | custom-call | flops 1610612736 | bytes 14024704 | tf_op jit(solution)/shard_map/pallas_call | solution.py:42
  148.3 3.7 %all-to-all-start.3 = ((bf16[8,64,384]{2,1,0:T(8,128)(2,1)}), bf16[8,64,384]{2,1,0:T(8,128)(2,1)S(1)}, u32[]{:S(2)}, u32[]{:S(2)}) async-start(bf16[8,64,384]{2,1,0:T(8,128)(2,1)} %shard_map.76), calls=%async_computation.3 | async-start | bytes 786432 | tf_op jit(solution)/shard_map/all_to_all | solution.py:260
  152.0 0.0 all-gather.25.cloned.1.call-start
  152.1 0.5 collective-permute-start
  152.6 0.1 collective-permute-start.1
  152.7 0.4 collective-permute-start.2
  153.1 7.2 %all-to-all-done.3.refs_6_ = bf16[8,64,384]{2,1,0:T(8,128)(2,1)S(1)} async-done(((bf16[8,64,384]{2,1,0:T(8,128)(2,1)}), bf16[8,64,384]{2,1,0:T(8,128)(2,1)S(1)}, u32[]{:S(2)}, u32[]{:S(2)}) %all-to-all-start.3) | async-done | bytes 393248 | tf_op jit(solution)/shard_map/all_to_all | solution.py:260
  160.4 8.0 %all-gather.4 = s32[8,1,512]{2,1,0:T(1,128)S(1)} all-gather(s32[1,1,512]{2,1,0:T(1,128)S(1)} %bitcast.29), channel_id=2, replica_groups=mesh['seq'=8,'tensor'=4] {'seq'}, dimensions={0}, use_global_device_ids=true | all-gather | bytes 18432 | tf_op jit(solution)/shard_map/all_gather | solution.py:253
  168.4 0.6 select_bitcast_fusion.bias_ref
  169.0 0.7 copy-done.23
  169.7 0.2 copy-done.24
  169.9 0.1 copy-done.25
  170.0 0.2 copy-done.26
  170.2 18.6 %shard_map.78 = bf16[8,128,128]{2,1,0:T(8,128)(2,1)} custom-call(s32[1]{0:T(128)} %bitcast.part_ref, f32[8,512]{1,0:T(8,128)} %select_bitcast_fusion.bias_ref, bf16[8,64,384]{2,1,0:T(8,128)(2,1)} %copy-done.18, bf16[8,64,384]{2,1,0:T(8,128)(2,1)} %copy-done.23, bf16[8,64,384]{2,1,0:T(8,128)(2,1)} %copy-done.19, bf16[8,64,384]{2,1,0:T(8,128)(2,1)} %copy-done.24, ...), custom_call_target="tpu_custom_call" | custom-call | flops 1207959552 | bytes 4194304 | tf_op jit(solution)/shard_map/pallas_call | solution.py:137
  188.8 11.0 %all_to_all.36 = bf16[8,128,128]{2,1,0:T(8,128)(2,1)} all-to-all(bf16[8,128,128]{2,1,0:T(8,128)(2,1)} %shard_map.78), channel_id=1, replica_groups=mesh['seq'=8,'tensor'=4] {'seq'}, dimensions={0} | all-to-all | bytes 524288 | tf_op jit(solution)/shard_map/all_to_all | solution.py:274
  199.8 0.0 all-gather.25.cloned.1.call-update
  199.8 0.0 all-gather.21.cloned.1.call-start
  199.9 18.6 %shard_map.77 = bf16[8,128,128]{2,1,0:T(8,128)(2,1)} custom-call(s32[1]{0:T(128)} %bitcast.part_ref, f32[8,512]{1,0:T(8,128)} %select_bitcast_fusion.bias_ref, bf16[8,64,384]{2,1,0:T(8,128)(2,1)} %copy-done.18, bf16[8,64,384]{2,1,0:T(8,128)(2,1)} %copy-done.23, bf16[8,64,384]{2,1,0:T(8,128)(2,1)} %copy-done.19, bf16[8,64,384]{2,1,0:T(8,128)(2,1)} %copy-done.24, ...), custom_call_target="tpu_custom_call" | custom-call | flops 1207959552 | bytes 4194304 | tf_op jit(solution)/shard_map/pallas_call | solution.py:137
  218.5 11.0 %all_to_all.37 = bf16[8,128,128]{2,1,0:T(8,128)(2,1)} all-to-all(bf16[8,128,128]{2,1,0:T(8,128)(2,1)} %shard_map.77), channel_id=1, replica_groups=mesh['seq'=8,'tensor'=4] {'seq'}, dimensions={0} | all-to-all | bytes 524288 | tf_op jit(solution)/shard_map/all_to_all | solution.py:274
  229.5 0.1 copy.22.refs_3_
  229.6 0.0 all-gather.23.cloned.1.call-done
  229.6 8.5 %copy.20 = bf16[4,4,128,2,512]{4,3,2,1,0:T(2,128)(2,1)} copy(bf16[4,4,128,2,512]{4,2,0,3,1:T(8,128)(2,1)} %bitcast.27) | data formatting | bytes 8388608 | tf_op jit(solution)/shard_map/transpose | solution.py:234
  238.2 5.5 %copy.23 = bf16[256,8,2,512]{3,1,2,0:T(8,128)(2,1)} copy(bf16[256,8,2,512]{3,2,1,0:T(2,128)(2,1)} %bitcast.25) | data formatting | bytes 8388608
  243.6 2.2 copy-done.8
  245.8 1.2 copy-done.16
  247.1 3.4 %shard_map.79.refs_4_ = bf16[512,1024]{1,0:T(8,128)(2,1)} custom-call(bf16[4,8,128,128]{3,2,1,0:T(8,128)(2,1)S(1)} %bitcast.20, bf16[2048,1024]{1,0:T(8,128)(2,1)S(1)} %bitcast.17, bf16[512,1024]{1,0:T(8,128)(2,1)S(1)} %copy-done.10, s32[512,1]{1,0:T(8,128)S(1)} %copy.22.refs_3_), custom_call_target="tpu_custom_call" | custom-call | flops 1073741824 | bytes 6291456 | tf_op jit(solution)/shard_map/pallas_call | solution.py:202
  250.5 5.8 %all-gather.21.cloned.1.call-done = bf16[32,128,128]{2,1,0:T(8,128)(2,1)} async-done(((bf16[8,128,128]{2,1,0:T(8,128)(2,1)}), bf16[32,128,128]{2,1,0:T(8,128)(2,1)}) %all-gather.21.cloned.1.call-update) | async-done | bytes 1048592 | tf_op jit(solution)/shard_map/all_gather | solution.py:275
  256.3 2.2 copy-done.9
  258.5 1.2 copy-done.11
  259.7 3.4 %shard_map.80 = bf16[512,1024]{1,0:T(8,128)(2,1)} custom-call(bf16[4,8,128,128]{3,2,1,0:T(8,128)(2,1)S(1)} %bitcast.19, bf16[2048,1024]{1,0:T(8,128)(2,1)S(1)} %bitcast.18, bf16[512,1024]{1,0:T(8,128)(2,1)S(1)} %copy-done.10, s32[512,1]{1,0:T(8,128)S(1)} %copy.22.refs_3_, bf16[512,1024]{1,0:T(8,128)(2,1)} %shard_map.79.refs_4_), custom_call_target="tpu_custom_call", output_to_operand_aliasing={{}: (4, {})} | custom-call | flops 1073741824 | bytes 6291456 | tf_op jit(solution)/shard_map/pallas_call | solution.py:202
  (48 shorter events, 0.1 us)
Async XLA Ops:
  6.5 45.5 %all-gather.13.cloned.1.call-start = ((), (), s32[]{:S(2)}) async-start(), calls=%async_computation.7 | async-start | bytes 1310720 | tf_op jit(solution)/shard_map/all_gather | solution.py:250
  8.7 71.0 %all-gather.15.cloned.1.call-start = ((), (), s32[]{:S(2)}) async-start(), calls=%async_computation.8 | async-start | bytes 1310720 | tf_op jit(solution)/shard_map/all_gather | solution.py:250
  9.5 99.3 %all-gather.17.cloned.1.call-start = ((), (), s32[]{:S(2)}) async-start(), calls=%async_computation.9 | async-start | bytes 1310720 | tf_op jit(solution)/shard_map/all_gather | solution.py:250
  10.2 127.4 %all-gather.19.cloned.1.call-start = ((), (), s32[]{:S(2)}) async-start(), calls=%async_computation.10 | async-start | bytes 1310720 | tf_op jit(solution)/shard_map/all_gather | solution.py:250
  10.8 218.9 %all-gather.23.cloned.1.call-start = ((), (), s32[]{:S(2)}) async-start(), calls=%async_computation.12 | async-start | bytes 4718592 | tf_op jit(solution)/shard_map/all_gather | solution.py:232
  10.9 41.2 %copy-start.17 = (f32[4096]{0:T(1024)S(1)}, f32[4096]{0:T(1024)}, u32[]{:S(2)}) copy-start(f32[4096]{0:T(1024)} %param.9) | copy-start | bytes 49156
  52.1 2.2 copy-start
  54.3 2.2 copy-start.4
  56.5 1.2 copy-start.15
  62.9 27.5 %all-to-all-start = ((bf16[8,64,384]{2,1,0:T(8,128)(2,1)}), bf16[8,64,384]{2,1,0:T(8,128)(2,1)S(1)}, u32[]{:S(2)}, u32[]{:S(2)}) async-start(bf16[8,64,384]{2,1,0:T(8,128)(2,1)} %shard_map.73), calls=%async_computation | async-start | bytes 786432 | tf_op jit(solution)/shard_map/all_to_all | solution.py:260
  79.7 2.2 copy-start.1
  81.9 2.2 copy-start.5
  84.1 1.2 copy-start.14
  90.4 61.6 %copy-start.18 = (bf16[8,64,384]{2,1,0:T(8,128)(2,1)}, bf16[8,64,384]{2,1,0:T(8,128)(2,1)S(1)}, u32[]{:S(2)}) copy-start(bf16[8,64,384]{2,1,0:T(8,128)(2,1)S(1)} %all-to-all-done.refs_0_) | copy-start | bytes 1179652
  90.4 29.0 %all-to-all-start.1 = ((bf16[8,64,384]{2,1,0:T(8,128)(2,1)}), bf16[8,64,384]{2,1,0:T(8,128)(2,1)S(1)}, u32[]{:S(2)}, u32[]{:S(2)}) async-start(bf16[8,64,384]{2,1,0:T(8,128)(2,1)} %shard_map.74), calls=%async_computation.1 | async-start | bytes 786432 | tf_op jit(solution)/shard_map/all_to_all | solution.py:260
  108.7 2.2 copy-start.2
  110.9 2.2 copy-start.6
  113.1 1.2 copy-start.13
  119.5 33.1 %copy-start.19 = (bf16[8,64,384]{2,1,0:T(8,128)(2,1)}, bf16[8,64,384]{2,1,0:T(8,128)(2,1)S(1)}, u32[]{:S(2)}) copy-start(bf16[8,64,384]{2,1,0:T(8,128)(2,1)S(1)} %all-to-all-done.1.refs_2_) | copy-start | bytes 1179652
  119.5 28.9 %all-to-all-start.2 = ((bf16[8,64,384]{2,1,0:T(8,128)(2,1)}), bf16[8,64,384]{2,1,0:T(8,128)(2,1)S(1)}, u32[]{:S(2)}, u32[]{:S(2)}) async-start(bf16[8,64,384]{2,1,0:T(8,128)(2,1)} %shard_map.75), calls=%async_computation.2 | async-start | bytes 786432 | tf_op jit(solution)/shard_map/all_to_all | solution.py:260
  137.6 2.2 copy-start.3
  139.8 2.2 copy-start.7
  142.0 1.2 copy-start.12
  143.2 17.1 %copy-start.22 = (s32[512]{0:T(512)S(1)}, s32[512]{0:T(512)}, u32[]{:S(2)}) copy-start(s32[512]{0:T(512)} %param.8) | copy-start | bytes 6148
  148.3 20.7 %copy-start.20 = (bf16[8,64,384]{2,1,0:T(8,128)(2,1)}, bf16[8,64,384]{2,1,0:T(8,128)(2,1)S(1)}, u32[]{:S(2)}) copy-start(bf16[8,64,384]{2,1,0:T(8,128)(2,1)S(1)} %all-to-all-done.2.refs_4_) | copy-start | bytes 1179652
  148.3 12.0 %all-to-all-start.3 = ((bf16[8,64,384]{2,1,0:T(8,128)(2,1)}), bf16[8,64,384]{2,1,0:T(8,128)(2,1)S(1)}, u32[]{:S(2)}, u32[]{:S(2)}) async-start(bf16[8,64,384]{2,1,0:T(8,128)(2,1)} %shard_map.76), calls=%async_computation.3 | async-start | bytes 786432 | tf_op jit(solution)/shard_map/all_to_all | solution.py:260
  152.0 91.6 %all-gather.25.cloned.1.call-start = ((), (), s32[]{:S(2)}) async-start(), calls=%async_computation.13 | async-start | bytes 1310720 | tf_op jit(solution)/shard_map/all_gather | solution.py:275
  152.1 16.9 %collective-permute-start = (bf16[8,64,384]{2,1,0:T(8,128)(2,1)S(1)}, bf16[8,64,384]{2,1,0:T(8,128)(2,1)S(1)}, u32[]{:S(2)}, u32[]{:S(2)}) collective-permute-start(bf16[8,64,384]{2,1,0:T(8,128)(2,1)S(1)} %all-to-all-done.refs_0_), channel_id=1, source_target_pairs={{0,4},{4,0},{8,12},{12,8},{16,20},{20,16},{24,28},{28,24},{1,5},{5... | collective-permute-start | bytes 1179656 | tf_op jit(solution)/shard_map/ppermute | solution.py:266
  152.6 16.4 %collective-permute-start.1 = (bf16[8,64,384]{2,1,0:T(8,128)(2,1)S(1)}, bf16[8,64,384]{2,1,0:T(8,128)(2,1)S(1)}, u32[]{:S(2)}, u32[]{:S(2)}) collective-permute-start(bf16[8,64,384]{2,1,0:T(8,128)(2,1)S(1)} %all-to-all-done.1.refs_2_), channel_id=1, source_target_pairs={{0,4},{4,0},{8,12},{12,8},{16,20},{20,16},{24,28},{28,24},{1,5},{5... | collective-permute-start | bytes 1179656 | tf_op jit(solution)/shard_map/ppermute | solution.py:266
  152.7 16.3 %collective-permute-start.2 = (bf16[8,64,384]{2,1,0:T(8,128)(2,1)S(1)}, bf16[8,64,384]{2,1,0:T(8,128)(2,1)S(1)}, u32[]{:S(2)}, u32[]{:S(2)}) collective-permute-start(bf16[8,64,384]{2,1,0:T(8,128)(2,1)S(1)} %all-to-all-done.2.refs_4_), channel_id=1, source_target_pairs={{0,4},{4,0},{8,12},{12,8},{16,20},{20,16},{24,28},{28,24},{1,5},{5... | collective-permute-start | bytes 1179656 | tf_op jit(solution)/shard_map/ppermute | solution.py:266
  160.3 8.7 %copy-start.21 = (bf16[8,64,384]{2,1,0:T(8,128)(2,1)}, bf16[8,64,384]{2,1,0:T(8,128)(2,1)S(1)}, u32[]{:S(2)}) copy-start(bf16[8,64,384]{2,1,0:T(8,128)(2,1)S(1)} %all-to-all-done.3.refs_6_) | copy-start | bytes 1179652
  160.3 8.7 %collective-permute-start.3 = (bf16[8,64,384]{2,1,0:T(8,128)(2,1)S(1)}, bf16[8,64,384]{2,1,0:T(8,128)(2,1)S(1)}, u32[]{:S(2)}, u32[]{:S(2)}) collective-permute-start(bf16[8,64,384]{2,1,0:T(8,128)(2,1)S(1)} %all-to-all-done.3.refs_6_), channel_id=1, source_target_pairs={{0,4},{4,0},{8,12},{12,8},{16,20},{20,16},{24,28},{28,24},{1,5},{5... | collective-permute-start | bytes 1179656 | tf_op jit(solution)/shard_map/ppermute | solution.py:266
  169.0 0.8 copy-start.23
  169.0 0.9 copy-start.24
  169.0 1.0 copy-start.25
  169.0 1.2 copy-start.26
  199.8 56.5 %all-gather.21.cloned.1.call-start = ((), (), s32[]{:S(2)}) async-start(), calls=%async_computation.11 | async-start | bytes 1310720 | tf_op jit(solution)/shard_map/all_gather | solution.py:275
  238.2 5.5 %copy-start.10 = (bf16[512,1024]{1,0:T(8,128)(2,1)S(1)}, bf16[512,1024]{1,0:T(8,128)(2,1)}, u32[]{:S(2)}) copy-start(bf16[512,1024]{1,0:T(8,128)(2,1)} %refs_2_.3) | copy-start | bytes 3145732
  243.6 2.2 copy-start.8
  245.8 1.2 copy-start.16
  256.3 2.2 copy-start.9
  258.5 1.2 copy-start.11
Sparse Core Ops, SparseCore 0:
  8.9 42.3 all-gather.12
  52.9 26.7 all-gather.14
  81.3 27.4 all-gather.16
  110.2 27.4 all-gather.18
  139.4 39.7 all-gather.22
  199.9 26.8 all-gather.24
  229.6 26.7 all-gather.20

commit v2 on v1

v2 whole, which is shorter than its diff:
```python
import math
from functools import partial

import jax
import jax.numpy as jnp
from jax import lax
from jax.experimental import pallas as pl
from jax.experimental.pallas import tpu as pltpu
from jax.sharding import PartitionSpec as P

HEAD = 128
MASKED = -1e30
BACK = 2
LIMIT = 60 * 2**20


def sources(me, count):
    found = [(me, None)]
    for step in range(count - 1):
        found.append((me - 1 - step, me - 1 - step >= 0))
        found.append((me + 1 + step, me + 1 + step < count))
    return found


def line_gather(chunks, count):
    right = [(d, d + 1) for d in range(count - 1)]
    left = [(d + 1, d) for d in range(count - 1)]
    found = [[chunk] for chunk in chunks]
    last = [(chunk, chunk) for chunk in chunks]
    for step in range(count - 1):
        for at, (from_left, from_right) in enumerate(last):
            from_left = lax.ppermute(from_left, "tensor", right[step:])
            from_right = lax.ppermute(from_right, "tensor", left[: count - 1 - step])
            last[at] = (from_left, from_right)
            found[at] += [from_left, from_right]
    return found


def project_kernel(group, count, me_ref, gain_ref, wq_ref, wk_ref, wv_ref, *refs):
    pieces = refs[:-3]
    out_ref, raw, normed = refs[-3:]
    width = pieces[0].shape[1]

    @pl.when(pl.program_id(0) == 0)
    def _():
        for piece, (source, there) in zip(pieces, sources(me_ref[0], count)):
            def place(piece=piece, source=source):
                raw[:, pl.ds(pl.multiple_of(source * width, width), width)] = piece[...]

            if there is None:
                place()
            else:
                pl.when(there)(place)
        values = raw[...].astype(jnp.float32)
        mean = jnp.mean(values * values, axis=1, keepdims=True)
        normed[...] = (values * lax.rsqrt(mean + 1e-05) * gain_ref[...]).astype(jnp.bfloat16)

    part_rows = out_ref.shape[1]
    heads = wq_ref.shape[1] // HEAD
    for which, weight in enumerate((wq_ref, wk_ref, wv_ref)):
        product = jnp.dot(normed[...], weight[...], preferred_element_type=jnp.float32)
        product = product.astype(jnp.bfloat16)
        for head in range(heads):
            for part in range(group):
                out_ref[head * group + part, :, which * HEAD : (which + 1) * HEAD] = product[
                    part * part_rows : (part + 1) * part_rows, head * HEAD : (head + 1) * HEAD
                ]


def project(me, pieces, gain, wq, wk, wv, seq_count, group):
    rows, columns = pieces[0].shape
    features, width = wq.shape
    block = min(256, width)
    per_step = block // HEAD * group
    part_rows = rows // group
    weight_spec = pl.BlockSpec((features, block), lambda j: (0, j))
    return pl.pallas_call(
        partial(project_kernel, group, features // columns),
        grid=(width // block,),
        in_specs=[
            pl.BlockSpec(memory_space=pltpu.SMEM),
            pl.BlockSpec((1, features), lambda j: (0, 0)),
            weight_spec,
            weight_spec,
            weight_spec,
        ]
        + [pl.BlockSpec((rows, columns), lambda j: (0, 0))] * len(pieces),
        out_specs=pl.BlockSpec((per_step, part_rows, 3 * HEAD), lambda j: (j, 0, 0)),
        out_shape=jax.ShapeDtypeStruct((seq_count, part_rows, 3 * HEAD), jnp.bfloat16),
        scratch_shapes=[
            pltpu.VMEM((rows, features), jnp.bfloat16),
            pltpu.VMEM((rows, features), jnp.bfloat16),
        ],
        compiler_params=pltpu.CompilerParams(vmem_limit_bytes=LIMIT),
        cost_estimate=pl.CostEstimate(
            flops=6 * rows * features * width,
            bytes_accessed=6 * features * width + 2 * rows * (features + 3 * width),
            transcendentals=0,
        ),
    )(me, gain, wq, wk, wv, *pieces)


def attend_kernel(chunks, group, mine, part_ref, bias_ref, *refs):
    pieces = refs[: chunks * group]
    out_ref, keys, values = refs[chunks * group :]
    seq_count, part_rows, _ = pieces[0].shape
    rows = bias_ref.shape[1]
    chunk_rows = rows // chunks
    part = part_ref[0]

    def place(home, _):
        for chunk in range(chunks):
            for step in range(group):
                owner = lax.rem(part + step, group)
                at = pl.multiple_of(home * rows + chunk * chunk_rows + owner * part_rows, part_rows)
                piece = pieces[chunk * group + step]
                keys[pl.ds(at, part_rows), :] = piece[home, :, HEAD : 2 * HEAD]
                values[pl.ds(at, part_rows), :] = piece[home, :, 2 * HEAD :]
        return 0

    lax.fori_loop(0, seq_count, place, 0)
    scale = math.log2(math.e) / math.sqrt(HEAD)
    count = len(mine) * part_rows

    def own_places():
        order = lax.broadcasted_iota(jnp.int32, (count, rows), 0)
        own = order % part_rows + part * part_rows
        for at_chunk, chunk in enumerate(mine):
            own = jnp.where(order // part_rows == at_chunk, own + chunk * chunk_rows, own)
        return own

    if seq_count <= 8:
        later = lax.broadcasted_iota(jnp.int32, (count, rows), 1) > own_places()
        for home in range(seq_count):
            queries = jnp.concatenate([pieces[c * group][home, :, :HEAD] for c in mine], axis=0)
            blocks = []
            for other in range(home + 1):
                scores = lax.dot_general(
                    queries,
                    keys[other * rows : (other + 1) * rows, :],
                    (((1,), (1,)), ((), ())),
                    preferred_element_type=jnp.float32,
                )
                scores = scores * scale + bias_ref[other : other + 1, :]
                if other == home:
                    scores = jnp.where(later, MASKED, scores)
                blocks.append(scores)
            scores = jnp.concatenate(blocks, axis=1)
            best = jnp.max(scores, axis=1, keepdims=True)
            weights = jnp.exp2(scores - best)
            total = jnp.sum(weights, axis=1, keepdims=True)
            summed = jnp.dot(
                weights.astype(jnp.bfloat16),
                values[: (home + 1) * rows, :],
                preferred_element_type=jnp.float32,
            )
            out_ref[home] = (summed / total).astype(jnp.bfloat16)
        return

    def one_home(home, _):
        queries = jnp.concatenate([pieces[c * group][home, :, :HEAD] for c in mine], axis=0)

        def fold(other, carry, diagonal):
            best, total, summed = carry
            at = pl.multiple_of(other * rows, rows)
            scores = lax.dot_general(
                queries,
                keys[pl.ds(at, rows), :],
                (((1,), (1,)), ((), ())),
                preferred_element_type=jnp.float32,
            )
            scores = scores * scale + bias_ref[pl.ds(other, 1), :]
            if diagonal:
                place_in = lax.broadcasted_iota(jnp.int32, (count, rows), 1)
                scores = jnp.where(place_in <= own_places(), scores, MASKED)
            newbest = jnp.maximum(best, jnp.max(scores, axis=1, keepdims=True))
            factor = jnp.exp2(best - newbest)
            weights = jnp.exp2(scores - newbest)
            total = total * factor + jnp.sum(weights, axis=1, keepdims=True)
            summed = summed * factor + jnp.dot(
                weights.astype(jnp.bfloat16),
                values[pl.ds(at, rows), :],
                preferred_element_type=jnp.float32,
            )
            return newbest, total, summed

        start = (
            jnp.full((count, 1), MASKED, jnp.float32),
            jnp.zeros((count, 1), jnp.float32),
            jnp.zeros((count, HEAD), jnp.float32),
        )
        carry = fold(home, start, True)
        carry = lax.fori_loop(0, home, lambda other, c: fold(other, c, False), carry)
        _, total, summed = carry
        out_ref[home] = (summed / total).astype(jnp.bfloat16)
        return 0

    lax.fori_loop(0, seq_count, one_home, 0)


def attend(part, bias, pieces, chunks, group, mine):
    seq_count, part_rows, _ = pieces[0].shape
    rows = bias.shape[1]
    count = len(mine) * part_rows
    vmem = pl.BlockSpec(memory_space=pltpu.VMEM)
    pairs = seq_count * (seq_count + 1) // 2
    return pl.pallas_call(
        partial(attend_kernel, chunks, group, mine),
        in_specs=[pl.BlockSpec(memory_space=pltpu.SMEM), vmem] + [vmem] * len(pieces),
        out_specs=vmem,
        out_shape=jax.ShapeDtypeStruct((seq_count, count, HEAD), jnp.bfloat16),
        scratch_shapes=[
            pltpu.VMEM((seq_count * rows, HEAD), jnp.bfloat16),
            pltpu.VMEM((seq_count * rows, HEAD), jnp.bfloat16),
        ],
        compiler_params=pltpu.CompilerParams(vmem_limit_bytes=LIMIT),
        cost_estimate=pl.CostEstimate(
            flops=4 * pairs * count * rows * HEAD,
            bytes_accessed=8 * seq_count * rows * HEAD,
            transcendentals=pairs * count * rows,
        ),
    )(part, bias, *pieces)


def output_kernel(chunks, group, count, cuts, me_ref, at_ref, hidden_ref, active_ref, *refs):
    weights = refs[:cuts]
    pieces = refs[cuts : cuts + 2 * count - 1]
    out_ref, rows_in = refs[-2:]
    seq_count, piece_rows, _ = pieces[0].shape
    heads = seq_count // group
    part_rows = piece_rows // chunks
    chunk_rows = part_rows * group
    width = weights[0].shape[1]

    for piece, (source, there) in zip(pieces, sources(me_ref[0], count)):
        def place(piece=piece, source=source):
            for head in range(heads):
                at = pl.multiple_of(at_ref[source * heads + head] * HEAD, HEAD)
                for part in range(group):
                    for chunk in range(chunks):
                        first = chunk * chunk_rows + part * part_rows
                        rows_in[first : first + part_rows, pl.ds(at, HEAD)] = piece[
                            head * group + part, chunk * part_rows : (chunk + 1) * part_rows, :
                        ]

        if there is None:
            place()
        else:
            pl.when(there)(place)

    for cut, weight in enumerate(weights):
        columns = pl.ds(pl.multiple_of(me_ref[1 + cut] * width, width), width)
        shares = jnp.dot(rows_in[...], weight[...], preferred_element_type=jnp.float32)
        hidden = hidden_ref[:, columns]
        renewed = (hidden.astype(jnp.float32) + shares).astype(jnp.bfloat16)
        out_ref[:, columns] = jnp.where(active_ref[...] > 0, renewed, hidden)


def output(scalars, at, pieces, weights, hidden, active, so_far, which, parts, chunks, group):
    rows, columns = hidden.shape
    here = rows // parts
    depth = weights[0].shape[0]
    smem = pl.BlockSpec(memory_space=pltpu.SMEM)
    row_block = pl.BlockSpec((here, columns), lambda j: (which, 0))
    operands = [scalars, at, hidden, active, *weights, *pieces]
    in_specs = [smem, smem, row_block, pl.BlockSpec((here, 1), lambda j: (which, 0))]
    in_specs += [pl.BlockSpec(w.shape, lambda j: (0, 0)) for w in weights]
    in_specs += [pl.BlockSpec(p.shape, lambda j: (0, 0, 0)) for p in pieces]
    aliases = {}
    if so_far is not None:
        aliases = {len(operands): 0}
        operands.append(so_far)
        in_specs.append(pl.BlockSpec(memory_space=pl.ANY))
    return pl.pallas_call(
        partial(output_kernel, chunks, group, len(pieces) // 2 + 1, len(weights)),
        grid=(1,),
        in_specs=in_specs,
        out_specs=row_block,
        out_shape=jax.ShapeDtypeStruct((rows, columns), jnp.bfloat16),
        scratch_shapes=[pltpu.VMEM((here, depth), jnp.bfloat16)],
        input_output_aliases=aliases,
        compiler_params=pltpu.CompilerParams(vmem_limit_bytes=LIMIT),
        cost_estimate=pl.CostEstimate(
            flops=2 * here * depth * columns,
            bytes_accessed=2 * (here * depth + depth * columns + 2 * here * columns),
            transcendentals=0,
        ),
    )(*operands)


def output_weight(w_out, seq_count, tensor_count, columns, after):
    heads = w_out.shape[0] // HEAD
    cuts = seq_count // heads
    width = columns // cuts
    row = jnp.arange(tensor_count * heads, dtype=jnp.int32)
    if width % HEAD:
        weight = lax.all_to_all(w_out, "tensor", split_axis=1, concat_axis=0, tiled=True)
        return [weight], [jnp.int32(0)], row
    seq_me = lax.axis_index("seq").astype(jnp.int32)
    me = lax.axis_index("tensor").astype(jnp.int32)
    head, cut = seq_me // cuts, seq_me % cuts
    w_out, after = lax.optimization_barrier((w_out, after))

    def share(to):
        return lax.dynamic_slice(w_out, (head * HEAD, to * columns + cut * width), (HEAD, width))

    shares = [share(me)]
    for step in range(1, tensor_count):
        ring = [(d, (d + step) % tensor_count) for d in range(tensor_count)]
        shares.append(lax.ppermute(share((me + step) % tensor_count), "tensor", ring))
    held = jnp.concatenate(shares, axis=0)
    flip = seq_count // 2
    while flip >= cuts:
        pairs = [(d, d ^ flip) for d in range(seq_count)]
        held = jnp.concatenate([held, lax.ppermute(held, "seq", pairs)], axis=0)
        flip //= 2
    weights, which = [held], [cut]
    for step in range(1, cuts):
        ring = [(d, d - d % cuts + (d - step) % cuts) for d in range(seq_count)]
        weights.append(lax.ppermute(held, "seq", ring))
        which.append((cut + step) % cuts)
    tensor, of = row // heads, row % heads
    apart = of ^ head
    turned, bit, size = jnp.zeros_like(apart), 1, heads
    while bit < heads:
        turned = turned + jnp.where((apart & bit) > 0, heads // (2 * bit), 0)
        bit *= 2
    at = turned * tensor_count + (me - tensor) % tensor_count
    return weights, which, at


def shards(hidden, depth, norm_gain, w_query, w_key, w_value, w_out):
    rows, columns = hidden.shape
    seq_count = lax.axis_size("seq")
    tensor_count = lax.axis_size("tensor")
    heads = w_query.shape[1] // HEAD
    group = seq_count // heads
    chunks = min(4, rows // (16 * group))
    chunk_rows = rows // chunks
    back = min(BACK, chunks)
    part = (lax.axis_index("seq") % group).astype(jnp.int32).reshape(1)
    me = lax.axis_index("tensor").astype(jnp.int32)
    gain = norm_gain.reshape(1, -1)

    gathered = line_gather(
        [hidden[c * chunk_rows : (c + 1) * chunk_rows] for c in range(chunks)], tensor_count
    )
    depths = lax.all_gather(depth, "seq", axis=0)
    bias = jnp.where(depths >= 2, 0.0, MASKED).astype(jnp.float32)
    active = (depth >= 2).astype(jnp.int32).reshape(rows, 1)

    pieces = []
    for found in gathered:
        sent = project(me.reshape(1), found, gain, w_query, w_key, w_value, seq_count, group)
        got = lax.all_to_all(sent, "seq", split_axis=0, concat_axis=0)
        pieces.append(got)
        for step in range(1, group):
            ring = [(d, d - d % group + (d - step) % group) for d in range(seq_count)]
            pieces.append(lax.ppermute(got, "seq", ring))

    weights, cut_of, at = output_weight(w_out, seq_count, tensor_count, columns, gathered[-1][-1])
    scalars = jnp.stack([me, *cut_of])
    updated = None
    each = chunks // back
    for which in range(back):
        mine = tuple(range(which * each, (which + 1) * each))
        out = attend(part, bias, pieces, chunks, group, mine)
        home = lax.all_to_all(out, "seq", split_axis=0, concat_axis=0)
        (found,) = line_gather([home], tensor_count)
        updated = output(
            scalars, at, found, weights, hidden, active, updated, which, back, each, group
        )
    return updated


def solution(mesh):
    return jax.shard_map(
        shards,
        mesh=mesh,
        in_specs=(
            P("seq", "tensor"),
            P("seq"),
            P(),
            P(None, "tensor"),
            P(None, "tensor"),
            P(None, "tensor"),
            P("tensor", None),
        ),
        out_specs=P("seq", "tensor"),
        check_vma=False,
    )
```

time: 272 us -> 235 us (0.86)
  starting transfers between devices: 15.9 us -> 103 us
  blocking collectives: 62.4 us -> 8.18 us
  local copies, waits for them, and re-layouts: 55.3 us -> 9.39 us
  between operations: 13.7 us -> 0.74 us
  Pallas kernels: 64.7 us -> 55.4 us
  waiting for transfers between devices: 57.4 us -> 54.4 us
    ppermute x0 -> x42, starting transfers between devices: none -> 79.3 us  [the longest x18 49.5 us: line_gather(): from_left = lax.ppermute(from_left, 'tensor', right[step:])]
    all_to_all x3 -> x0, blocking collectives: 54.4 us -> none  [the longest x1 32.5 us: output_weight(): share = lax.all_to_all(share, 'tensor', split_axis=0, concat_axis=0)]
    all_gather x7 -> x0, waiting for transfers between devices: 48.2 us -> none  [the longest x4 42.3 us: shards(): lax.all_gather(hidden[c * chunk_rows:(c + 1) * chunk_rows], 'tensor', axi...]
    ppermute x0 -> x42, waiting for transfers between devices: none -> 46.8 us  [the longest x18 46.3 us: line_gather(): from_right = lax.ppermute(from_right, 'tensor', left[:count - 1 - step])]
    unnamed x56 -> x58, local copies, waits for them, and re-layouts: 42.4 us -> 4.42 us
    pallas_call x2, Pallas kernels: 37.2 us -> 15.4 us  [attend(): pl.pallas_call(partial(attend_kernel, chunks, group, mine), in_specs=[pl....]
    pallas_call x6, Pallas kernels: 27.5 us -> 40.1 us  [the longest x4 29.4 us: project(): pl.pallas_call(partial(project_kernel, group, features // columns), grid=...]
    transpose x2 -> x0, local copies, waits for them, and re-layouts: 9.64 us -> none  [the longest x1 8.51 us: output_weight(): jnp.transpose(whole, (2, 0, 3, 1, 4))]
  transfers between devices with their start and end apart: 15 -> 52, of which waited for: 5 -> 14; matrix products, arithmetic and copies ran while one was open for 9% -> 2% of each run, Pallas kernels for 23% -> 21%
where the time goes in v2:
time: 235 us; the launch traced here: 233 us
  starting transfers between devices  103 us (44%)
  Pallas kernels  55.4 us (24%)
  waiting for transfers between devices  54.4 us (23%)
  local copies, waits for them, and re-layouts  9.39 us (4%)
  blocking collectives  8.18 us (3%)
    ppermute x18, starting transfers between devices, line_gather(): from_left = lax.ppermute(from_left, 'tensor', right[step:])  49.5 us
    ppermute x18, waiting for transfers between devices, line_gather(): from_right = lax.ppermute(from_right, 'tensor', left[:count - 1 - step])  46.3 us
    pallas_call x4, Pallas kernels, project(): pl.pallas_call(partial(project_kernel, group, features // columns), grid=...  29.4 us
    ppermute x18, starting transfers between devices, line_gather(): from_right = lax.ppermute(from_right, 'tensor', left[:count - 1 - step])  23.1 us
    all_to_all x4, starting transfers between devices, shards(): got = lax.all_to_all(sent, 'seq', split_axis=0, concat_axis=0)  15.6 us
    pallas_call x2, Pallas kernels, attend(): pl.pallas_call(partial(attend_kernel, chunks, group, mine), in_specs=[pl....  15.4 us
    pallas_call x2, Pallas kernels, output(): pl.pallas_call(partial(output_kernel, chunks, group, len(pieces) // 2 + 1...  10.6 us
    all_gather x1, blocking collectives, shards(): depths = lax.all_gather(depth, 'seq', axis=0)  8.18 us
  transfers between devices with their start and end apart: 52, of which 14 were waited for; matrix products, arithmetic and copies ran while one was open for 2% of the time, Pallas kernels for 21%

profile of v2, /device:TPU:0, one launch (start us, length us, event | category | flops | bytes accessed | tf_op | source)
XLA Modules:
  0.0 233.4 jit_solution(15686221978720068995)
XLA Ops:
  0.0 1.3 fusion.6
  1.3 1.3 collective-permute-start
  2.6 9.9 %collective-permute-done.refs_2_ = bf16[128,1024]{1,0:T(8,128)(2,1)S(1)} collective-permute-done((bf16[128,1024]{1,0:T(8,128)(2,1)S(1)}, bf16[128,1024]{1,0:T(8,128)(2,1)S(1)}, u32[]{:S(2)}, u32[]{:S(2)}) %collective-permute-start) | collective-permute-done | bytes 262176 | tf_op jit(solution)/shard_map/ppermute | solution.py:33
  13.2 1.3 collective-permute-start.1
  14.5 8.1 %collective-permute-done.1.refs_4_ = bf16[128,1024]{1,0:T(8,128)(2,1)S(1)} collective-permute-done((bf16[128,1024]{1,0:T(8,128)(2,1)S(1)}, bf16[128,1024]{1,0:T(8,128)(2,1)S(1)}, u32[]{:S(2)}, u32[]{:S(2)}) %collective-permute-start.1) | collective-permute-done | bytes 262176 | tf_op jit(solution)/shard_map/ppermute | solution.py:33
  22.6 1.3 collective-permute-start.2
  24.0 7.1 %collective-permute-done.2.refs_6_ = bf16[128,1024]{1,0:T(8,128)(2,1)S(1)} collective-permute-done((bf16[128,1024]{1,0:T(8,128)(2,1)S(1)}, bf16[128,1024]{1,0:T(8,128)(2,1)S(1)}, u32[]{:S(2)}, u32[]{:S(2)}) %collective-permute-start.2) | collective-permute-done | bytes 262176 | tf_op jit(solution)/shard_map/ppermute | solution.py:33
  31.1 1.9 fusion.5
  33.0 3.8 %collective-permute-start.5 = (bf16[128,512]{1,0:T(8,128)(2,1)S(1)}, bf16[128,512]{1,0:T(8,128)(2,1)S(1)}, u32[]{:S(2)}, u32[]{:S(2)}) collective-permute-start(bf16[128,512]{1,0:T(8,128)(2,1)S(1)} %get-tuple-element.9), channel_id=1, source_target_pairs={{0,3},{1,0},{2,1},{3,2},{4,7},{5,4},{6,5},{7,6},{8,11},{9,8},{10,9... | collective-permute-start | bytes 393224 | tf_op jit(solution)/shard_map/ppermute | solution.py:310
  36.8 2.5 %collective-permute-start.9 = (bf16[128,1024]{1,0:T(8,128)(2,1)S(1)}, bf16[128,1024]{1,0:T(8,128)(2,1)S(1)}, u32[]{:S(2)}, u32[]{:S(2)}) collective-permute-start(bf16[128,1024]{1,0:T(8,128)(2,1)S(1)} %get-tuple-element.16.refs_0_), channel_id=1, source_target_pairs={{0,1},{1,2},{2,3},{4,5},{5,6},{6,7},{8,9},{9,10},{10,11},{12,13},{... | collective-permute-start | bytes 786440 | tf_op jit(solution)/shard_map/ppermute | solution.py:32
  39.3 1.3 collective-permute-start.10
  40.6 4.5 %collective-permute-start.16 = (bf16[128,1024]{1,0:T(8,128)(2,1)S(1)}, bf16[128,1024]{1,0:T(8,128)(2,1)S(1)}, u32[]{:S(2)}, u32[]{:S(2)}) collective-permute-start(bf16[128,1024]{1,0:T(8,128)(2,1)S(1)} %get-tuple-element.15.refs_0_), channel_id=1, source_target_pairs={{0,1},{1,2},{2,3},{4,5},{5,6},{6,7},{8,9},{9,10},{10,11},{12,13},{... | collective-permute-start | bytes 786440 | tf_op jit(solution)/shard_map/ppermute | solution.py:32
  45.2 1.3 collective-permute-start.17
  46.5 1.2 collective-permute-start.6
  48.1 5.1 %collective-permute-start.23 = (bf16[128,1024]{1,0:T(8,128)(2,1)S(1)}, bf16[128,1024]{1,0:T(8,128)(2,1)}, u32[]{:S(2)}, u32[]{:S(2)}) collective-permute-start(bf16[128,1024]{1,0:T(8,128)(2,1)S(1)} %get-tuple-element.14.refs_0_), channel_id=1, source_target_pairs={{0,1},{1,2},{2,3},{4,5},{5,6},{6,7},{8,9},{9,10},{10,11},{12,13},{... | collective-permute-start | bytes 786440 | tf_op jit(solution)/shard_map/ppermute | solution.py:32
  53.2 1.3 collective-permute-start.24
  55.2 1.3 collective-permute-start.12
  57.2 7.9 %collective-permute-start.30 = (bf16[128,1024]{1,0:T(8,128)(2,1)S(1)}, bf16[128,1024]{1,0:T(8,128)(2,1)S(1)}, u32[]{:S(2)}, u32[]{:S(2)}) collective-permute-start(bf16[128,1024]{1,0:T(8,128)(2,1)S(1)} %get-tuple-element.17.refs_0_), channel_id=1, source_target_pairs={{0,1},{1,2},{2,3},{4,5},{5,6},{6,7},{8,9},{9,10},{10,11},{12,13},{... | collective-permute-start | bytes 786440 | tf_op jit(solution)/shard_map/ppermute | solution.py:32
  66.5 1.4 collective-permute-start.18
  67.9 1.3 collective-permute-start.19
  69.9 1.3 collective-permute-start.14
  72.8 1.1 collective-permute-start.7
  74.0 1.4 collective-permute-start.25
  75.3 3.6 %collective-permute-done.19.refs_4_ = bf16[128,1024]{1,0:T(8,128)(2,1)} collective-permute-done((bf16[128,1024]{1,0:T(8,128)(2,1)S(1)}, bf16[128,1024]{1,0:T(8,128)(2,1)}, u32[]{:S(2)}, u32[]{:S(2)}) %collective-permute-start.19) | collective-permute-done | bytes 262176 | tf_op jit(solution)/shard_map/ppermute | solution.py:33
  78.9 1.3 collective-permute-start.26
  80.2 1.4 collective-permute-start.20
  81.6 1.3 collective-permute-start.21
  82.9 7.3 %shard_map.73 = bf16[8,64,384]{2,1,0:T(8,128)(2,1)} custom-call(s32[1]{0:T(128)} %bitcast.me_ref, f32[1,4096]{1,0:T(1,128)} %bitcast.8, bf16[4096,512]{1,0:T(8,128)(2,1)} %wq_ref.7, bf16[4096,512]{1,0:T(8,128)(2,1)} %wk_ref.7, bf16[4096,512]{1,0:T(8,128)(2,1)} %wv_ref.7, bf16[128,1024]{1,0:T(8,128)(2,1)} %copy-done.4, bf16[128,1024]{1,0:T(8,128)(2,1)} %copy-done.15, ...), custom_call_target="tpu_custom_call" | custom-call | flops 1610612736 | bytes 14024704 | tf_op jit(solution)/shard_map/pallas_call | solution.py:77
  90.3 3.5 %all-to-all-start = ((bf16[8,64,384]{2,1,0:T(8,128)(2,1)}), bf16[8,64,384]{2,1,0:T(8,128)(2,1)S(1)}, u32[]{:S(2)}, u32[]{:S(2)}) async-start(bf16[8,64,384]{2,1,0:T(8,128)(2,1)} %shard_map.73), calls=%async_computation | async-start | bytes 786432 | tf_op jit(solution)/shard_map/all_to_all | solution.py:355
  93.7 1.4 collective-permute-start.31
  95.2 1.4 collective-permute-start.27
  96.5 1.3 collective-permute-start.28
  97.8 7.3 %shard_map.74 = bf16[8,64,384]{2,1,0:T(8,128)(2,1)} custom-call(s32[1]{0:T(128)} %bitcast.me_ref, f32[1,4096]{1,0:T(1,128)} %bitcast.9, bf16[4096,512]{1,0:T(8,128)(2,1)} %wq_ref.7, bf16[4096,512]{1,0:T(8,128)(2,1)} %wk_ref.7, bf16[4096,512]{1,0:T(8,128)(2,1)} %wv_ref.7, bf16[128,1024]{1,0:T(8,128)(2,1)} %copy-done.3, bf16[128,1024]{1,0:T(8,128)(2,1)} %copy-done.13, ...), custom_call_target="tpu_custom_call" | custom-call | flops 1610612736 | bytes 14024704 | tf_op jit(solution)/shard_map/pallas_call | solution.py:77
  105.1 4.1 %all-to-all-start.1 = ((bf16[8,64,384]{2,1,0:T(8,128)(2,1)}), bf16[8,64,384]{2,1,0:T(8,128)(2,1)}, u32[]{:S(2)}, u32[]{:S(2)}) async-start(bf16[8,64,384]{2,1,0:T(8,128)(2,1)} %shard_map.74), calls=%async_computation.1 | async-start | bytes 786432 | tf_op jit(solution)/shard_map/all_to_all | solution.py:355
  109.3 1.4 collective-permute-start.32
  110.7 3.6 %collective-permute-done.28.refs_6_ = bf16[128,1024]{1,0:T(8,128)(2,1)} collective-permute-done((bf16[128,1024]{1,0:T(8,128)(2,1)}, bf16[128,1024]{1,0:T(8,128)(2,1)}, u32[]{:S(2)}, u32[]{:S(2)}) %collective-permute-start.28) | collective-permute-done | bytes 262176 | tf_op jit(solution)/shard_map/ppermute | solution.py:33
  114.3 7.3 %shard_map.75 = bf16[8,64,384]{2,1,0:T(8,128)(2,1)} custom-call(s32[1]{0:T(128)} %bitcast.me_ref, f32[1,4096]{1,0:T(1,128)} %bitcast.10, bf16[4096,512]{1,0:T(8,128)(2,1)} %wq_ref.7, bf16[4096,512]{1,0:T(8,128)(2,1)} %wk_ref.7, bf16[4096,512]{1,0:T(8,128)(2,1)} %wv_ref.7, bf16[128,1024]{1,0:T(8,128)(2,1)} %copy-done.2, ...), custom_call_target="tpu_custom_call" | custom-call | flops 1610612736 | bytes 14024704 | tf_op jit(solution)/shard_map/pallas_call | solution.py:77
  121.5 4.1 %all-to-all-start.2 = ((bf16[8,64,384]{2,1,0:T(8,128)(2,1)}), bf16[8,64,384]{2,1,0:T(8,128)(2,1)}, u32[]{:S(2)}, u32[]{:S(2)}) async-start(bf16[8,64,384]{2,1,0:T(8,128)(2,1)} %shard_map.75), calls=%async_computation.2 | async-start | bytes 786432 | tf_op jit(solution)/shard_map/all_to_all | solution.py:355
  126.2 7.5 %shard_map.76 = bf16[8,64,384]{2,1,0:T(8,128)(2,1)} custom-call(s32[1]{0:T(128)} %bitcast.me_ref, f32[1,4096]{1,0:T(1,128)} %bitcast.11, bf16[4096,512]{1,0:T(8,128)(2,1)} %wq_ref.7, bf16[4096,512]{1,0:T(8,128)(2,1)} %wk_ref.7, bf16[4096,512]{1,0:T(8,128)(2,1)} %wv_ref.7, bf16[128,1024]{1,0:T(8,128)(2,1)} %copy-done.1, bf16[128,1024]{1,0:T(8,128)(2,1)} %copy-done.12, ...), custom_call_target="tpu_custom_call" | custom-call | flops 1610612736 | bytes 14024704 | tf_op jit(solution)/shard_map/pallas_call | solution.py:77
  134.0 3.9 %all-to-all-start.3 = ((bf16[8,64,384]{2,1,0:T(8,128)(2,1)}), bf16[8,64,384]{2,1,0:T(8,128)(2,1)S(1)}, u32[]{:S(2)}, u32[]{:S(2)}) async-start(bf16[8,64,384]{2,1,0:T(8,128)(2,1)} %shard_map.76), calls=%async_computation.3 | async-start | bytes 786432 | tf_op jit(solution)/shard_map/all_to_all | solution.py:355
  138.9 7.3 %all-to-all-done.3.refs_6_ = bf16[8,64,384]{2,1,0:T(8,128)(2,1)S(1)} async-done(((bf16[8,64,384]{2,1,0:T(8,128)(2,1)}), bf16[8,64,384]{2,1,0:T(8,128)(2,1)S(1)}, u32[]{:S(2)}, u32[]{:S(2)}) %all-to-all-start.3) | async-done | bytes 393248 | tf_op jit(solution)/shard_map/all_to_all | solution.py:355
  146.2 8.2 %all-gather.1 = s32[8,1,512]{2,1,0:T(1,128)S(1)} all-gather(s32[1,1,512]{2,1,0:T(1,128)S(1)} %bitcast.13), channel_id=2, replica_groups=mesh['seq'=8,'tensor'=4] {'seq'}, dimensions={0}, use_global_device_ids=true | all-gather | bytes 18432 | tf_op jit(solution)/shard_map/all_gather | solution.py:348
  155.9 7.7 %shard_map.78 = bf16[8,128,128]{2,1,0:T(8,128)(2,1)} custom-call(s32[1]{0:T(128)} %bitcast.1.part_ref, f32[8,512]{1,0:T(8,128)} %select_bitcast_fusion.bias_ref, bf16[8,64,384]{2,1,0:T(8,128)(2,1)} %copy-done.7, bf16[8,64,384]{2,1,0:T(8,128)(2,1)} %copy-done.25, bf16[8,64,384]{2,1,0:T(8,128)(2,1)} %all-to-all-done.1.refs_2_, ...), custom_call_target="tpu_custom_call" | custom-call | flops 1207959552 | bytes 4194304 | tf_op jit(solution)/shard_map/pallas_call | solution.py:207
  163.6 3.4 %all-to-all-start.5 = ((bf16[8,128,128]{2,1,0:T(8,128)(2,1)}), bf16[8,128,128]{2,1,0:T(8,128)(2,1)S(1)}, u32[]{:S(2)}, u32[]{:S(2)}) async-start(bf16[8,128,128]{2,1,0:T(8,128)(2,1)} %shard_map.78), calls=%async_computation.5 | async-start | bytes 524288 | tf_op jit(solution)/shard_map/all_to_all | solution.py:368
  167.0 7.7 %shard_map.77 = bf16[8,128,128]{2,1,0:T(8,128)(2,1)} custom-call(s32[1]{0:T(128)} %bitcast.1.part_ref, f32[8,512]{1,0:T(8,128)} %select_bitcast_fusion.bias_ref, bf16[8,64,384]{2,1,0:T(8,128)(2,1)} %copy-done.7, bf16[8,64,384]{2,1,0:T(8,128)(2,1)} %copy-done.25, bf16[8,64,384]{2,1,0:T(8,128)(2,1)} %all-to-all-done.1.refs_2_, ...), custom_call_target="tpu_custom_call" | custom-call | flops 1207959552 | bytes 4194304 | tf_op jit(solution)/shard_map/pallas_call | solution.py:207
  174.7 4.1 %all-to-all-start.4 = ((bf16[8,128,128]{2,1,0:T(8,128)(2,1)}), bf16[8,128,128]{2,1,0:T(8,128)(2,1)S(1)}, u32[]{:S(2)}, u32[]{:S(2)}) async-start(bf16[8,128,128]{2,1,0:T(8,128)(2,1)} %shard_map.77), calls=%async_computation.4 | async-start | bytes 524288 | tf_op jit(solution)/shard_map/all_to_all | solution.py:368
  178.9 8.7 %collective-permute-start.40 = (bf16[8,128,128]{2,1,0:T(8,128)(2,1)S(1)}, bf16[8,128,128]{2,1,0:T(8,128)(2,1)S(1)}, u32[]{:S(2)}, u32[]{:S(2)}) collective-permute-start(bf16[8,128,128]{2,1,0:T(8,128)(2,1)S(1)} %all-to-all-done.5.refs_2_), channel_id=1, source_target_pairs={{0,1},{1,2},{2,3},{4,5},{5,6},{6,7},{8,9},{9,10},{10,11},{12,13},{... | collective-permute-start | bytes 786440 | tf_op jit(solution)/shard_map/ppermute | solution.py:32
  187.6 1.3 collective-permute-start.41
  188.9 5.6 %collective-permute-start.34 = (bf16[8,128,128]{2,1,0:T(8,128)(2,1)S(1)}, bf16[8,128,128]{2,1,0:T(8,128)(2,1)S(1)}, u32[]{:S(2)}, u32[]{:S(2)}) collective-permute-start(bf16[8,128,128]{2,1,0:T(8,128)(2,1)S(1)} %all-to-all-done.4.refs_2_), channel_id=1, source_target_pairs={{0,1},{1,2},{2,3},{4,5},{5,6},{6,7},{8,9},{9,10},{10,11},{12,13},{... | collective-permute-start | bytes 786440 | tf_op jit(solution)/shard_map/ppermute | solution.py:32
  194.5 1.3 collective-permute-start.35
  195.9 1.4 collective-permute-start.42
  198.0 1.3 collective-permute-start.43
  199.4 1.4 collective-permute-start.36
  200.8 3.5 %collective-permute-done.35.refs_4_ = bf16[8,128,128]{2,1,0:T(8,128)(2,1)S(1)} collective-permute-done((bf16[8,128,128]{2,1,0:T(8,128)(2,1)S(1)}, bf16[8,128,128]{2,1,0:T(8,128)(2,1)S(1)}, u32[]{:S(2)}, u32[]{:S(2)}) %collective-permute-start.35) | collective-permute-done | bytes 262176 | tf_op jit(solution)/shard_map/ppermute | solution.py:33
  204.3 1.3 collective-permute-start.37
  205.6 1.4 collective-permute-start.44
  207.0 2.3 collective-permute-done.43.refs_6_
  209.3 1.3 collective-permute-start.45
  210.6 1.4 collective-permute-start.38
  212.0 5.1 %collective-permute-done.37.refs_6_ = bf16[8,128,128]{2,1,0:T(8,128)(2,1)} collective-permute-done((bf16[8,128,128]{2,1,0:T(8,128)(2,1)S(1)}, bf16[8,128,128]{2,1,0:T(8,128)(2,1)}, u32[]{:S(2)}, u32[]{:S(2)}) %collective-permute-start.37) | collective-permute-done | bytes 262176 | tf_op jit(solution)/shard_map/ppermute | solution.py:33
  217.1 1.3 collective-permute-start.39
  220.4 2.3 collective-permute-done.45.refs_8_
  222.7 5.3 %shard_map.79.refs_9_ = bf16[512,1024]{1,0:T(8,128)(2,1)} custom-call(s32[3]{0:T(128)} %pad_add_fusion.me_ref, s32[16]{0:T(128)} %fusion.at_ref, bf16[512,1024]{1,0:T(8,128)(2,1)} %hidden_ref.3, s32[512,1]{1,0:T(8,128)} %copy.13.active_ref, bf16[2048,512]{1,0:T(8,128)(2,1)} %copy-done, bf16[2048,512]{1,0:T(8,128)(2,1)} %collective-permute-done.8.refs_1_, ...), custom_call_target="tpu_custom_call" | custom-call | flops 1073741824 | bytes 6291456 | tf_op jit(solution)/shard_map/pallas_call | solution.py:274
  228.1 5.3 %shard_map.80 = bf16[512,1024]{1,0:T(8,128)(2,1)} custom-call(s32[3]{0:T(128)} %pad_add_fusion.me_ref, s32[16]{0:T(128)} %fusion.at_ref, bf16[512,1024]{1,0:T(8,128)(2,1)} %hidden_ref.3, s32[512,1]{1,0:T(8,128)} %copy.13.active_ref, bf16[2048,512]{1,0:T(8,128)(2,1)} %copy-done, ...), custom_call_target="tpu_custom_call", output_to_operand_aliasing={{}: (13, {})} | custom-call | flops 1073741824 | bytes 6291456 | tf_op jit(solution)/shard_map/pallas_call | solution.py:274
  (117 shorter events, 12.5 us)
Async XLA Ops:
  1.3 70.8 %copy-start.1 = (bf16[128,1024]{1,0:T(8,128)(2,1)}, bf16[128,1024]{1,0:T(8,128)(2,1)S(1)}, u32[]{:S(2)}) copy-start(bf16[128,1024]{1,0:T(8,128)(2,1)S(1)} %get-tuple-element.17.refs_0_) | copy-start | bytes 786436
  1.3 70.8 %copy-start.2 = (bf16[128,1024]{1,0:T(8,128)(2,1)}, bf16[128,1024]{1,0:T(8,128)(2,1)S(1)}, u32[]{:S(2)}) copy-start(bf16[128,1024]{1,0:T(8,128)(2,1)S(1)} %get-tuple-element.14.refs_0_) | copy-start | bytes 786436
  1.3 70.8 %copy-start.3 = (bf16[128,1024]{1,0:T(8,128)(2,1)}, bf16[128,1024]{1,0:T(8,128)(2,1)S(1)}, u32[]{:S(2)}) copy-start(bf16[128,1024]{1,0:T(8,128)(2,1)S(1)} %get-tuple-element.15.refs_0_) | copy-start | bytes 786436
  1.3 70.8 %copy-start.4 = (bf16[128,1024]{1,0:T(8,128)(2,1)}, bf16[128,1024]{1,0:T(8,128)(2,1)S(1)}, u32[]{:S(2)}) copy-start(bf16[128,1024]{1,0:T(8,128)(2,1)S(1)} %get-tuple-element.16.refs_0_) | copy-start | bytes 786436
  1.3 11.2 %collective-permute-start = (bf16[128,1024]{1,0:T(8,128)(2,1)S(1)}, bf16[128,1024]{1,0:T(8,128)(2,1)S(1)}, u32[]{:S(2)}, u32[]{:S(2)}) collective-permute-start(bf16[128,1024]{1,0:T(8,128)(2,1)S(1)} %get-tuple-element.17.refs_0_), channel_id=1, source_target_pairs={{1,0},{2,1},{3,2},{5,4},{6,5},{7,6},{9,8},{10,9},{11,10},{13,12},{... | collective-permute-start | bytes 786440 | tf_op jit(solution)/shard_map/ppermute | solution.py:33
  13.2 9.4 %collective-permute-start.1 = (bf16[128,1024]{1,0:T(8,128)(2,1)S(1)}, bf16[128,1024]{1,0:T(8,128)(2,1)S(1)}, u32[]{:S(2)}, u32[]{:S(2)}) collective-permute-start(bf16[128,1024]{1,0:T(8,128)(2,1)S(1)} %collective-permute-done.refs_2_), channel_id=1, source_target_pairs={{1,0},{2,1},{5,4},{6,5},{9,8},{10,9},{13,12},{14,13},{17,16},{18,1... | collective-permute-start | bytes 786440 | tf_op jit(solution)/shard_map/ppermute | solution.py:33
  22.6 25.5 %copy-start.10 = (bf16[128,1024]{1,0:T(8,128)(2,1)}, bf16[128,1024]{1,0:T(8,128)(2,1)S(1)}, u32[]{:S(2)}) copy-start(bf16[128,1024]{1,0:T(8,128)(2,1)S(1)} %collective-permute-done.1.refs_4_) | copy-start | bytes 786436
  22.6 8.5 %collective-permute-start.2 = (bf16[128,1024]{1,0:T(8,128)(2,1)S(1)}, bf16[128,1024]{1,0:T(8,128)(2,1)S(1)}, u32[]{:S(2)}, u32[]{:S(2)}) collective-permute-start(bf16[128,1024]{1,0:T(8,128)(2,1)S(1)} %collective-permute-done.1.refs_4_), channel_id=1, source_target_pairs={{1,0},{5,4},{9,8},{13,12},{17,16},{21,20},{25,24},{29,28}} | collective-permute-start | bytes 786440 | tf_op jit(solution)/shard_map/ppermute | solution.py:33
  33.0 7.7 %collective-permute-start.3 = (bf16[128,512]{1,0:T(8,128)(2,1)S(1)}, bf16[128,512]{1,0:T(8,128)(2,1)S(1)}, u32[]{:S(2)}, u32[]{:S(2)}) collective-permute-start(bf16[128,512]{1,0:T(8,128)(2,1)S(1)} %get-tuple-element.11), channel_id=1, source_target_pairs={{0,1},{1,2},{2,3},{3,0},{4,5},{5,6},{6,7},{7,4},{8,9},{9,10},{10,1... | collective-permute-start | bytes 393224 | tf_op jit(solution)/shard_map/ppermute | solution.py:310
  33.0 12.2 %collective-permute-start.4 = (bf16[128,512]{1,0:T(8,128)(2,1)S(1)}, bf16[128,512]{1,0:T(8,128)(2,1)S(1)}, u32[]{:S(2)}, u32[]{:S(2)}) collective-permute-start(bf16[128,512]{1,0:T(8,128)(2,1)S(1)} %get-tuple-element.10), channel_id=1, source_target_pairs={{0,2},{1,3},{2,0},{3,1},{4,6},{5,7},{6,4},{7,5},{8,10},{9,11},{10,... | collective-permute-start | bytes 393224 | tf_op jit(solution)/shard_map/ppermute | solution.py:310
  33.0 13.5 %collective-permute-start.5 = (bf16[128,512]{1,0:T(8,128)(2,1)S(1)}, bf16[128,512]{1,0:T(8,128)(2,1)S(1)}, u32[]{:S(2)}, u32[]{:S(2)}) collective-permute-start(bf16[128,512]{1,0:T(8,128)(2,1)S(1)} %get-tuple-element.9), channel_id=1, source_target_pairs={{0,3},{1,0},{2,1},{3,2},{4,7},{5,4},{6,5},{7,6},{8,11},{9,8},{10,9... | collective-permute-start | bytes 393224 | tf_op jit(solution)/shard_map/ppermute | solution.py:310
  36.8 11.3 %collective-permute-start.9 = (bf16[128,1024]{1,0:T(8,128)(2,1)S(1)}, bf16[128,1024]{1,0:T(8,128)(2,1)S(1)}, u32[]{:S(2)}, u32[]{:S(2)}) collective-permute-start(bf16[128,1024]{1,0:T(8,128)(2,1)S(1)} %get-tuple-element.16.refs_0_), channel_id=1, source_target_pairs={{0,1},{1,2},{2,3},{4,5},{5,6},{6,7},{8,9},{9,10},{10,11},{12,13},{... | collective-permute-start | bytes 786440 | tf_op jit(solution)/shard_map/ppermute | solution.py:32
  39.3 13.9 %collective-permute-start.10 = (bf16[128,1024]{1,0:T(8,128)(2,1)S(1)}, bf16[128,1024]{1,0:T(8,128)(2,1)S(1)}, u32[]{:S(2)}, u32[]{:S(2)}) collective-permute-start(bf16[128,1024]{1,0:T(8,128)(2,1)S(1)} %get-tuple-element.16.refs_0_), channel_id=1, source_target_pairs={{1,0},{2,1},{3,2},{5,4},{6,5},{7,6},{9,8},{10,9},{11,10},{13,12},{... | collective-permute-start | bytes 786440 | tf_op jit(solution)/shard_map/ppermute | solution.py:33
  40.6 13.9 %collective-permute-start.16 = (bf16[128,1024]{1,0:T(8,128)(2,1)S(1)}, bf16[128,1024]{1,0:T(8,128)(2,1)S(1)}, u32[]{:S(2)}, u32[]{:S(2)}) collective-permute-start(bf16[128,1024]{1,0:T(8,128)(2,1)S(1)} %get-tuple-element.15.refs_0_), channel_id=1, source_target_pairs={{0,1},{1,2},{2,3},{4,5},{5,6},{6,7},{8,9},{9,10},{10,11},{12,13},{... | collective-permute-start | bytes 786440 | tf_op jit(solution)/shard_map/ppermute | solution.py:32
  45.2 10.1 %collective-permute-start.17 = (bf16[128,1024]{1,0:T(8,128)(2,1)S(1)}, bf16[128,1024]{1,0:T(8,128)(2,1)S(1)}, u32[]{:S(2)}, u32[]{:S(2)}) collective-permute-start(bf16[128,1024]{1,0:T(8,128)(2,1)S(1)} %get-tuple-element.15.refs_0_), channel_id=1, source_target_pairs={{1,0},{2,1},{3,2},{5,4},{6,5},{7,6},{9,8},{10,9},{11,10},{13,12},{... | collective-permute-start | bytes 786440 | tf_op jit(solution)/shard_map/ppermute | solution.py:33
  46.5 23.4 %collective-permute-start.6 = (bf16[512,512]{1,0:T(8,128)(2,1)S(1)}, bf16[512,512]{1,0:T(8,128)(2,1)S(1)}, u32[]{:S(2)}, u32[]{:S(2)}) collective-permute-start(bf16[512,512]{1,0:T(8,128)(2,1)S(1)} %pad_maximum_fusion), channel_id=1, source_target_pairs={{0,16},{4,20},{8,24},{12,28},{16,0},{20,4},{24,8},{28,12},{1,17},{... | collective-permute-start | bytes 1572872 | tf_op jit(solution)/shard_map/ppermute | solution.py:315
  48.1 34.8 %copy-start.15 = (bf16[128,1024]{1,0:T(8,128)(2,1)}, bf16[128,1024]{1,0:T(8,128)(2,1)S(1)}, u32[]{:S(2)}) copy-start(bf16[128,1024]{1,0:T(8,128)(2,1)S(1)} %collective-permute-done.9.refs_1_) | copy-start | bytes 786436
  48.1 9.1 %collective-permute-start.23 = (bf16[128,1024]{1,0:T(8,128)(2,1)S(1)}, bf16[128,1024]{1,0:T(8,128)(2,1)}, u32[]{:S(2)}, u32[]{:S(2)}) collective-permute-start(bf16[128,1024]{1,0:T(8,128)(2,1)S(1)} %get-tuple-element.14.refs_0_), channel_id=1, source_target_pairs={{0,1},{1,2},{2,3},{4,5},{5,6},{6,7},{8,9},{9,10},{10,11},{12,13},{... | collective-permute-start | bytes 786440 | tf_op jit(solution)/shard_map/ppermute | solution.py:32
  53.2 29.7 %copy-start.16 = (bf16[128,1024]{1,0:T(8,128)(2,1)}, bf16[128,1024]{1,0:T(8,128)(2,1)S(1)}, u32[]{:S(2)}) copy-start(bf16[128,1024]{1,0:T(8,128)(2,1)S(1)} %collective-permute-done.10.refs_2_) | copy-start | bytes 786436
  53.2 13.3 %collective-permute-start.24 = (bf16[128,1024]{1,0:T(8,128)(2,1)S(1)}, bf16[128,1024]{1,0:T(8,128)(2,1)}, u32[]{:S(2)}, u32[]{:S(2)}) collective-permute-start(bf16[128,1024]{1,0:T(8,128)(2,1)S(1)} %get-tuple-element.14.refs_0_), channel_id=1, source_target_pairs={{1,0},{2,1},{3,2},{5,4},{6,5},{7,6},{9,8},{10,9},{11,10},{13,12},{... | collective-permute-start | bytes 786440 | tf_op jit(solution)/shard_map/ppermute | solution.py:33
  54.5 13.4 %collective-permute-start.11 = (bf16[128,1024]{1,0:T(8,128)(2,1)S(1)}, bf16[128,1024]{1,0:T(8,128)(2,1)S(1)}, u32[]{:S(2)}, u32[]{:S(2)}) collective-permute-start(bf16[128,1024]{1,0:T(8,128)(2,1)S(1)} %collective-permute-done.9.refs_1_), channel_id=1, source_target_pairs={{1,2},{2,3},{5,6},{6,7},{9,10},{10,11},{13,14},{14,15},{17,18},{18... | collective-permute-start | bytes 786440 | tf_op jit(solution)/shard_map/ppermute | solution.py:32
  55.2 13.9 %collective-permute-start.12 = (bf16[128,1024]{1,0:T(8,128)(2,1)S(1)}, bf16[128,1024]{1,0:T(8,128)(2,1)S(1)}, u32[]{:S(2)}, u32[]{:S(2)}) collective-permute-start(bf16[128,1024]{1,0:T(8,128)(2,1)S(1)} %collective-permute-done.10.refs_2_), channel_id=1, source_target_pairs={{1,0},{2,1},{5,4},{6,5},{9,8},{10,9},{13,12},{14,13},{17,16},{18,1... | collective-permute-start | bytes 786440 | tf_op jit(solution)/shard_map/ppermute | solution.py:33
  57.2 14.9 %collective-permute-start.30 = (bf16[128,1024]{1,0:T(8,128)(2,1)S(1)}, bf16[128,1024]{1,0:T(8,128)(2,1)S(1)}, u32[]{:S(2)}, u32[]{:S(2)}) collective-permute-start(bf16[128,1024]{1,0:T(8,128)(2,1)S(1)} %get-tuple-element.17.refs_0_), channel_id=1, source_target_pairs={{0,1},{1,2},{2,3},{4,5},{5,6},{6,7},{8,9},{9,10},{10,11},{12,13},{... | collective-permute-start | bytes 786440 | tf_op jit(solution)/shard_map/ppermute | solution.py:32
  66.5 7.5 %collective-permute-start.18 = (bf16[128,1024]{1,0:T(8,128)(2,1)S(1)}, bf16[128,1024]{1,0:T(8,128)(2,1)}, u32[]{:S(2)}, u32[]{:S(2)}) collective-permute-start(bf16[128,1024]{1,0:T(8,128)(2,1)S(1)} %collective-permute-done.16.refs_1_), channel_id=1, source_target_pairs={{1,2},{2,3},{5,6},{6,7},{9,10},{10,11},{13,14},{14,15},{17,18},{18... | collective-permute-start | bytes 786440 | tf_op jit(solution)/shard_map/ppermute | solution.py:32
  67.9 11.0 %collective-permute-start.19 = (bf16[128,1024]{1,0:T(8,128)(2,1)S(1)}, bf16[128,1024]{1,0:T(8,128)(2,1)}, u32[]{:S(2)}, u32[]{:S(2)}) collective-permute-start(bf16[128,1024]{1,0:T(8,128)(2,1)S(1)} %collective-permute-done.17.refs_2_), channel_id=1, source_target_pairs={{1,0},{2,1},{5,4},{6,5},{9,8},{10,9},{13,12},{14,13},{17,16},{18,1... | collective-permute-start | bytes 786440 | tf_op jit(solution)/shard_map/ppermute | solution.py:33
  69.2 11.0 %collective-permute-start.13 = (bf16[128,1024]{1,0:T(8,128)(2,1)S(1)}, bf16[128,1024]{1,0:T(8,128)(2,1)S(1)}, u32[]{:S(2)}, u32[]{:S(2)}) collective-permute-start(bf16[128,1024]{1,0:T(8,128)(2,1)S(1)} %collective-permute-done.11.refs_3_), channel_id=1, source_target_pairs={{2,3},{6,7},{10,11},{14,15},{18,19},{22,23},{26,27},{30,31}} | collective-permute-start | bytes 786440 | tf_op jit(solution)/shard_map/ppermute | solution.py:32
  69.9 11.7 %collective-permute-start.14 = (bf16[128,1024]{1,0:T(8,128)(2,1)S(1)}, bf16[128,1024]{1,0:T(8,128)(2,1)S(1)}, u32[]{:S(2)}, u32[]{:S(2)}) collective-permute-start(bf16[128,1024]{1,0:T(8,128)(2,1)S(1)} %collective-permute-done.12.refs_4_), channel_id=1, source_target_pairs={{1,0},{5,4},{9,8},{13,12},{17,16},{21,20},{25,24},{29,28}} | collective-permute-start | bytes 786440 | tf_op jit(solution)/shard_map/ppermute | solution.py:33
  72.8 52.8 %collective-permute-start.7 = (bf16[1024,512]{1,0:T(8,128)(2,1)}, bf16[1024,512]{1,0:T(8,128)(2,1)S(1)}, u32[]{:S(2)}, u32[]{:S(2)}) collective-permute-start(bf16[1024,512]{1,0:T(8,128)(2,1)} %get-tuple-element.18), channel_id=1, source_target_pairs={{0,8},{4,12},{8,0},{12,4},{16,24},{20,28},{24,16},{28,20},{1,9},{5... | collective-permute-start | bytes 3145736 | tf_op jit(solution)/shard_map/ppermute | solution.py:315
  74.0 19.8 %collective-permute-start.25 = (bf16[128,1024]{1,0:T(8,128)(2,1)}, bf16[128,1024]{1,0:T(8,128)(2,1)}, u32[]{:S(2)}, u32[]{:S(2)}) collective-permute-start(bf16[128,1024]{1,0:T(8,128)(2,1)} %collective-permute-done.23.refs_1_), channel_id=1, source_target_pairs={{1,2},{2,3},{5,6},{6,7},{9,10},{10,11},{13,14},{14,15},{17,18},{18... | collective-permute-start | bytes 786440 | tf_op jit(solution)/shard_map/ppermute | solution.py:32
  78.9 16.3 %collective-permute-start.26 = (bf16[128,1024]{1,0:T(8,128)(2,1)}, bf16[128,1024]{1,0:T(8,128)(2,1)}, u32[]{:S(2)}, u32[]{:S(2)}) collective-permute-start(bf16[128,1024]{1,0:T(8,128)(2,1)} %collective-permute-done.24.refs_2_), channel_id=1, source_target_pairs={{1,0},{2,1},{5,4},{6,5},{9,8},{10,9},{13,12},{14,13},{17,16},{18,1... | collective-permute-start | bytes 786440 | tf_op jit(solution)/shard_map/ppermute | solution.py:33
  80.2 16.3 %collective-permute-start.20 = (bf16[128,1024]{1,0:T(8,128)(2,1)}, bf16[128,1024]{1,0:T(8,128)(2,1)}, u32[]{:S(2)}, u32[]{:S(2)}) collective-permute-start(bf16[128,1024]{1,0:T(8,128)(2,1)} %collective-permute-done.18.refs_3_), channel_id=1, source_target_pairs={{2,3},{6,7},{10,11},{14,15},{18,19},{22,23},{26,27},{30,31}} | collective-permute-start | bytes 786440 | tf_op jit(solution)/shard_map/ppermute | solution.py:32
  81.6 16.2 %collective-permute-start.21 = (bf16[128,1024]{1,0:T(8,128)(2,1)}, bf16[128,1024]{1,0:T(8,128)(2,1)}, u32[]{:S(2)}, u32[]{:S(2)}) collective-permute-start(bf16[128,1024]{1,0:T(8,128)(2,1)} %collective-permute-done.19.refs_4_), channel_id=1, source_target_pairs={{1,0},{5,4},{9,8},{13,12},{17,16},{21,20},{25,24},{29,28}} | collective-permute-start | bytes 786440 | tf_op jit(solution)/shard_map/ppermute | solution.py:33
  90.3 14.9 %all-to-all-start = ((bf16[8,64,384]{2,1,0:T(8,128)(2,1)}), bf16[8,64,384]{2,1,0:T(8,128)(2,1)S(1)}, u32[]{:S(2)}, u32[]{:S(2)}) async-start(bf16[8,64,384]{2,1,0:T(8,128)(2,1)} %shard_map.73), calls=%async_computation | async-start | bytes 786432 | tf_op jit(solution)/shard_map/all_to_all | solution.py:355
  93.7 15.5 %collective-permute-start.31 = (bf16[128,1024]{1,0:T(8,128)(2,1)}, bf16[128,1024]{1,0:T(8,128)(2,1)}, u32[]{:S(2)}, u32[]{:S(2)}) collective-permute-start(bf16[128,1024]{1,0:T(8,128)(2,1)} %copy-done.12), channel_id=1, source_target_pairs={{1,2},{2,3},{5,6},{6,7},{9,10},{10,11},{13,14},{14,15},{17,18},{18... | collective-permute-start | bytes 786440 | tf_op jit(solution)/shard_map/ppermute | solution.py:32
  95.2 15.5 %collective-permute-start.27 = (bf16[128,1024]{1,0:T(8,128)(2,1)}, bf16[128,1024]{1,0:T(8,128)(2,1)}, u32[]{:S(2)}, u32[]{:S(2)}) collective-permute-start(bf16[128,1024]{1,0:T(8,128)(2,1)} %collective-permute-done.25.refs_3_), channel_id=1, source_target_pairs={{2,3},{6,7},{10,11},{14,15},{18,19},{22,23},{26,27},{30,31}} | collective-permute-start | bytes 786440 | tf_op jit(solution)/shard_map/ppermute | solution.py:32
  96.5 17.7 %collective-permute-start.28 = (bf16[128,1024]{1,0:T(8,128)(2,1)}, bf16[128,1024]{1,0:T(8,128)(2,1)}, u32[]{:S(2)}, u32[]{:S(2)}) collective-permute-start(bf16[128,1024]{1,0:T(8,128)(2,1)} %collective-permute-done.26.refs_4_), channel_id=1, source_target_pairs={{1,0},{5,4},{9,8},{13,12},{17,16},{21,20},{25,24},{29,28}} | collective-permute-start | bytes 786440 | tf_op jit(solution)/shard_map/ppermute | solution.py:33
  105.1 32.8 %copy-start.7 = (bf16[8,64,384]{2,1,0:T(8,128)(2,1)}, bf16[8,64,384]{2,1,0:T(8,128)(2,1)S(1)}, u32[]{:S(2)}) copy-start(bf16[8,64,384]{2,1,0:T(8,128)(2,1)S(1)} %all-to-all-done.refs_0_) | copy-start | bytes 1179652
  105.1 16.4 %all-to-all-start.1 = ((bf16[8,64,384]{2,1,0:T(8,128)(2,1)}), bf16[8,64,384]{2,1,0:T(8,128)(2,1)}, u32[]{:S(2)}, u32[]{:S(2)}) async-start(bf16[8,64,384]{2,1,0:T(8,128)(2,1)} %shard_map.74), calls=%async_computation.1 | async-start | bytes 786432 | tf_op jit(solution)/shard_map/all_to_all | solution.py:355
  109.3 16.9 %collective-permute-start.32 = (bf16[128,1024]{1,0:T(8,128)(2,1)}, bf16[128,1024]{1,0:T(8,128)(2,1)}, u32[]{:S(2)}, u32[]{:S(2)}) collective-permute-start(bf16[128,1024]{1,0:T(8,128)(2,1)} %collective-permute-done.31.refs_3_), channel_id=1, source_target_pairs={{2,3},{6,7},{10,11},{14,15},{18,19},{22,23},{26,27},{30,31}} | collective-permute-start | bytes 786440 | tf_op jit(solution)/shard_map/ppermute | solution.py:32
  121.5 12.5 %all-to-all-start.2 = ((bf16[8,64,384]{2,1,0:T(8,128)(2,1)}), bf16[8,64,384]{2,1,0:T(8,128)(2,1)}, u32[]{:S(2)}, u32[]{:S(2)}) async-start(bf16[8,64,384]{2,1,0:T(8,128)(2,1)} %shard_map.75), calls=%async_computation.2 | async-start | bytes 786432 | tf_op jit(solution)/shard_map/all_to_all | solution.py:355
  125.8 96.9 %collective-permute-start.8 = (bf16[2048,512]{1,0:T(8,128)(2,1)S(1)}, bf16[2048,512]{1,0:T(8,128)(2,1)}, u32[]{:S(2)}, u32[]{:S(2)}) collective-permute-start(bf16[2048,512]{1,0:T(8,128)(2,1)S(1)} %constant_dynamic-update-slice_fusion.5.refs_0_), channel_id=1, source_target_pairs={{0,4},{4,0},{8,12},{12,8},{16,20},{20,16},{24,28},{28,24},{1,5},{5... | collective-permute-start | bytes 6291464 | tf_op jit(solution)/shard_map/ppermute | solution.py:320
  134.0 12.2 %all-to-all-start.3 = ((bf16[8,64,384]{2,1,0:T(8,128)(2,1)}), bf16[8,64,384]{2,1,0:T(8,128)(2,1)S(1)}, u32[]{:S(2)}, u32[]{:S(2)}) async-start(bf16[8,64,384]{2,1,0:T(8,128)(2,1)} %shard_map.76), calls=%async_computation.3 | async-start | bytes 786432 | tf_op jit(solution)/shard_map/all_to_all | solution.py:355
  137.9 17.1 %collective-permute-start.15 = (bf16[8,64,384]{2,1,0:T(8,128)(2,1)S(1)}, bf16[8,64,384]{2,1,0:T(8,128)(2,1)S(1)}, u32[]{:S(2)}, u32[]{:S(2)}) collective-permute-start(bf16[8,64,384]{2,1,0:T(8,128)(2,1)S(1)} %all-to-all-done.refs_0_), channel_id=1, source_target_pairs={{0,4},{4,0},{8,12},{12,8},{16,20},{20,16},{24,28},{28,24},{1,5},{5... | collective-permute-start | bytes 1179656 | tf_op jit(solution)/shard_map/ppermute | solution.py:359
  138.4 16.6 %collective-permute-start.22 = (bf16[8,64,384]{2,1,0:T(8,128)(2,1)}, bf16[8,64,384]{2,1,0:T(8,128)(2,1)}, u32[]{:S(2)}, u32[]{:S(2)}) collective-permute-start(bf16[8,64,384]{2,1,0:T(8,128)(2,1)} %all-to-all-done.1.refs_2_), channel_id=1, source_target_pairs={{0,4},{4,0},{8,12},{12,8},{16,20},{20,16},{24,28},{28,24},{1,5},{5... | collective-permute-start | bytes 1179656 | tf_op jit(solution)/shard_map/ppermute | solution.py:359
  138.5 16.6 %collective-permute-start.29 = (bf16[8,64,384]{2,1,0:T(8,128)(2,1)}, bf16[8,64,384]{2,1,0:T(8,128)(2,1)}, u32[]{:S(2)}, u32[]{:S(2)}) collective-permute-start(bf16[8,64,384]{2,1,0:T(8,128)(2,1)} %all-to-all-done.2.refs_4_), channel_id=1, source_target_pairs={{0,4},{4,0},{8,12},{12,8},{16,20},{20,16},{24,28},{28,24},{1,5},{5... | collective-permute-start | bytes 1179656 | tf_op jit(solution)/shard_map/ppermute | solution.py:359
  146.2 8.8 %collective-permute-start.33 = (bf16[8,64,384]{2,1,0:T(8,128)(2,1)S(1)}, bf16[8,64,384]{2,1,0:T(8,128)(2,1)S(1)}, u32[]{:S(2)}, u32[]{:S(2)}) collective-permute-start(bf16[8,64,384]{2,1,0:T(8,128)(2,1)S(1)} %all-to-all-done.3.refs_6_), channel_id=1, source_target_pairs={{0,4},{4,0},{8,12},{12,8},{16,20},{20,16},{24,28},{28,24},{1,5},{5... | collective-permute-start | bytes 1179656 | tf_op jit(solution)/shard_map/ppermute | solution.py:359
  163.6 11.1 %all-to-all-start.5 = ((bf16[8,128,128]{2,1,0:T(8,128)(2,1)}), bf16[8,128,128]{2,1,0:T(8,128)(2,1)S(1)}, u32[]{:S(2)}, u32[]{:S(2)}) async-start(bf16[8,128,128]{2,1,0:T(8,128)(2,1)} %shard_map.78), calls=%async_computation.5 | async-start | bytes 524288 | tf_op jit(solution)/shard_map/all_to_all | solution.py:368
  174.7 48.0 %copy-start.5 = (bf16[8,128,128]{2,1,0:T(8,128)(2,1)}, bf16[8,128,128]{2,1,0:T(8,128)(2,1)S(1)}, u32[]{:S(2)}) copy-start(bf16[8,128,128]{2,1,0:T(8,128)(2,1)S(1)} %all-to-all-done.5.refs_2_) | copy-start | bytes 786436
  174.7 14.2 %all-to-all-start.4 = ((bf16[8,128,128]{2,1,0:T(8,128)(2,1)}), bf16[8,128,128]{2,1,0:T(8,128)(2,1)S(1)}, u32[]{:S(2)}, u32[]{:S(2)}) async-start(bf16[8,128,128]{2,1,0:T(8,128)(2,1)} %shard_map.77), calls=%async_computation.4 | async-start | bytes 524288 | tf_op jit(solution)/shard_map/all_to_all | solution.py:368
  178.9 17.0 %collective-permute-start.40 = (bf16[8,128,128]{2,1,0:T(8,128)(2,1)S(1)}, bf16[8,128,128]{2,1,0:T(8,128)(2,1)S(1)}, u32[]{:S(2)}, u32[]{:S(2)}) collective-permute-start(bf16[8,128,128]{2,1,0:T(8,128)(2,1)S(1)} %all-to-all-done.5.refs_2_), channel_id=1, source_target_pairs={{0,1},{1,2},{2,3},{4,5},{5,6},{6,7},{8,9},{9,10},{10,11},{12,13},{... | collective-permute-start | bytes 786440 | tf_op jit(solution)/shard_map/ppermute | solution.py:32
  187.6 10.4 %collective-permute-start.41 = (bf16[8,128,128]{2,1,0:T(8,128)(2,1)S(1)}, bf16[8,128,128]{2,1,0:T(8,128)(2,1)}, u32[]{:S(2)}, u32[]{:S(2)}) collective-permute-start(bf16[8,128,128]{2,1,0:T(8,128)(2,1)S(1)} %all-to-all-done.5.refs_2_), channel_id=1, source_target_pairs={{1,0},{2,1},{3,2},{5,4},{6,5},{7,6},{9,8},{10,9},{11,10},{13,12},{... | collective-permute-start | bytes 786440 | tf_op jit(solution)/shard_map/ppermute | solution.py:33
  188.9 39.1 %copy-start.6 = (bf16[8,128,128]{2,1,0:T(8,128)(2,1)}, bf16[8,128,128]{2,1,0:T(8,128)(2,1)S(1)}, u32[]{:S(2)}) copy-start(bf16[8,128,128]{2,1,0:T(8,128)(2,1)S(1)} %all-to-all-done.4.refs_2_) | copy-start | bytes 786436
  188.9 10.5 %collective-permute-start.34 = (bf16[8,128,128]{2,1,0:T(8,128)(2,1)S(1)}, bf16[8,128,128]{2,1,0:T(8,128)(2,1)S(1)}, u32[]{:S(2)}, u32[]{:S(2)}) collective-permute-start(bf16[8,128,128]{2,1,0:T(8,128)(2,1)S(1)} %all-to-all-done.4.refs_2_), channel_id=1, source_target_pairs={{0,1},{1,2},{2,3},{4,5},{5,6},{6,7},{8,9},{9,10},{10,11},{12,13},{... | collective-permute-start | bytes 786440 | tf_op jit(solution)/shard_map/ppermute | solution.py:32
  194.5 9.7 %collective-permute-start.35 = (bf16[8,128,128]{2,1,0:T(8,128)(2,1)S(1)}, bf16[8,128,128]{2,1,0:T(8,128)(2,1)S(1)}, u32[]{:S(2)}, u32[]{:S(2)}) collective-permute-start(bf16[8,128,128]{2,1,0:T(8,128)(2,1)S(1)} %all-to-all-done.4.refs_2_), channel_id=1, source_target_pairs={{1,0},{2,1},{3,2},{5,4},{6,5},{7,6},{9,8},{10,9},{11,10},{13,12},{... | collective-permute-start | bytes 786440 | tf_op jit(solution)/shard_map/ppermute | solution.py:33
  195.8 26.9 %copy-start.22 = (bf16[8,128,128]{2,1,0:T(8,128)(2,1)}, bf16[8,128,128]{2,1,0:T(8,128)(2,1)S(1)}, u32[]{:S(2)}) copy-start(bf16[8,128,128]{2,1,0:T(8,128)(2,1)S(1)} %collective-permute-done.40.refs_3_) | copy-start | bytes 786436
  195.9 9.7 %collective-permute-start.42 = (bf16[8,128,128]{2,1,0:T(8,128)(2,1)S(1)}, bf16[8,128,128]{2,1,0:T(8,128)(2,1)}, u32[]{:S(2)}, u32[]{:S(2)}) collective-permute-start(bf16[8,128,128]{2,1,0:T(8,128)(2,1)S(1)} %collective-permute-done.40.refs_3_), channel_id=1, source_target_pairs={{1,2},{2,3},{5,6},{6,7},{9,10},{10,11},{13,14},{14,15},{17,18},{18... | collective-permute-start | bytes 786440 | tf_op jit(solution)/shard_map/ppermute | solution.py:32
  198.0 11.2 %collective-permute-start.43 = (bf16[8,128,128]{2,1,0:T(8,128)(2,1)}, bf16[8,128,128]{2,1,0:T(8,128)(2,1)}, u32[]{:S(2)}, u32[]{:S(2)}) collective-permute-start(bf16[8,128,128]{2,1,0:T(8,128)(2,1)} %collective-permute-done.41.refs_4_), channel_id=1, source_target_pairs={{1,0},{2,1},{5,4},{6,5},{9,8},{10,9},{13,12},{14,13},{17,16},{18,1... | collective-permute-start | bytes 786440 | tf_op jit(solution)/shard_map/ppermute | solution.py:33
  199.4 28.6 %copy-start.21 = (bf16[8,128,128]{2,1,0:T(8,128)(2,1)}, bf16[8,128,128]{2,1,0:T(8,128)(2,1)S(1)}, u32[]{:S(2)}) copy-start(bf16[8,128,128]{2,1,0:T(8,128)(2,1)S(1)} %collective-permute-done.34.refs_3_) | copy-start | bytes 786436
  199.4 11.2 %collective-permute-start.36 = (bf16[8,128,128]{2,1,0:T(8,128)(2,1)S(1)}, bf16[8,128,128]{2,1,0:T(8,128)(2,1)}, u32[]{:S(2)}, u32[]{:S(2)}) collective-permute-start(bf16[8,128,128]{2,1,0:T(8,128)(2,1)S(1)} %collective-permute-done.34.refs_3_), channel_id=1, source_target_pairs={{1,2},{2,3},{5,6},{6,7},{9,10},{10,11},{13,14},{14,15},{17,18},{18... | collective-permute-start | bytes 786440 | tf_op jit(solution)/shard_map/ppermute | solution.py:32
  204.3 12.8 %collective-permute-start.37 = (bf16[8,128,128]{2,1,0:T(8,128)(2,1)S(1)}, bf16[8,128,128]{2,1,0:T(8,128)(2,1)}, u32[]{:S(2)}, u32[]{:S(2)}) collective-permute-start(bf16[8,128,128]{2,1,0:T(8,128)(2,1)S(1)} %collective-permute-done.35.refs_4_), channel_id=1, source_target_pairs={{1,0},{2,1},{5,4},{6,5},{9,8},{10,9},{13,12},{14,13},{17,16},{18,1... | collective-permute-start | bytes 786440 | tf_op jit(solution)/shard_map/ppermute | solution.py:33
  205.6 14.8 %collective-permute-start.44 = (bf16[8,128,128]{2,1,0:T(8,128)(2,1)}, bf16[8,128,128]{2,1,0:T(8,128)(2,1)}, u32[]{:S(2)}, u32[]{:S(2)}) collective-permute-start(bf16[8,128,128]{2,1,0:T(8,128)(2,1)} %collective-permute-done.42.refs_5_), channel_id=1, source_target_pairs={{2,3},{6,7},{10,11},{14,15},{18,19},{22,23},{26,27},{30,31}} | collective-permute-start | bytes 786440 | tf_op jit(solution)/shard_map/ppermute | solution.py:32
  209.3 13.4 %collective-permute-start.45 = (bf16[8,128,128]{2,1,0:T(8,128)(2,1)}, bf16[8,128,128]{2,1,0:T(8,128)(2,1)}, u32[]{:S(2)}, u32[]{:S(2)}) collective-permute-start(bf16[8,128,128]{2,1,0:T(8,128)(2,1)} %collective-permute-done.43.refs_6_), channel_id=1, source_target_pairs={{1,0},{5,4},{9,8},{13,12},{17,16},{21,20},{25,24},{29,28}} | collective-permute-start | bytes 786440 | tf_op jit(solution)/shard_map/ppermute | solution.py:33
  210.6 17.5 %collective-permute-start.38 = (bf16[8,128,128]{2,1,0:T(8,128)(2,1)}, bf16[8,128,128]{2,1,0:T(8,128)(2,1)}, u32[]{:S(2)}, u32[]{:S(2)}) collective-permute-start(bf16[8,128,128]{2,1,0:T(8,128)(2,1)} %collective-permute-done.36.refs_5_), channel_id=1, source_target_pairs={{2,3},{6,7},{10,11},{14,15},{18,19},{22,23},{26,27},{30,31}} | collective-permute-start | bytes 786440 | tf_op jit(solution)/shard_map/ppermute | solution.py:32
  217.1 11.0 %collective-permute-start.39 = (bf16[8,128,128]{2,1,0:T(8,128)(2,1)}, bf16[8,128,128]{2,1,0:T(8,128)(2,1)}, u32[]{:S(2)}, u32[]{:S(2)}) collective-permute-start(bf16[8,128,128]{2,1,0:T(8,128)(2,1)} %collective-permute-done.37.refs_6_), channel_id=1, source_target_pairs={{1,0},{5,4},{9,8},{13,12},{17,16},{21,20},{25,24},{29,28}} | collective-permute-start | bytes 786440 | tf_op jit(solution)/shard_map/ppermute | solution.py:33
  (15 other events, 147.1 us)

commit v3 on v2

v3 whole, which is shorter than its diff:
```python
import math
from functools import partial

import jax
import jax.numpy as jnp
from jax import lax
from jax.experimental import pallas as pl
from jax.experimental.pallas import tpu as pltpu
from jax.sharding import PartitionSpec as P

HEAD = 128
MASKED = -1e30
BACK = 2
LIMIT = 60 * 2**20


def sources(me, count):
    found = [(me, None)]
    for step in range(count - 1):
        found.append((me - 1 - step, me - 1 - step >= 0))
        found.append((me + 1 + step, me + 1 + step < count))
    return found


def line_gather(chunks, count, also=None):
    right = [(d, d + 1) for d in range(count - 1)]
    left = [(d + 1, d) for d in range(count - 1)]
    found = []
    for first in range(0, len(chunks), 2):
        pair = []
        for chunk in chunks[first : first + 2]:
            if first:
                chunk, _ = lax.optimization_barrier((chunk, (found[len(found) - 2 + len(pair)], also)))
            pair.append([chunk])
        last = [(chunk[0], chunk[0]) for chunk in pair]
        for step in range(count - 1):
            for at, (from_left, from_right) in enumerate(last):
                from_left = lax.ppermute(from_left, "tensor", right[step:])
                from_right = lax.ppermute(from_right, "tensor", left[: count - 1 - step])
                last[at] = (from_left, from_right)
                pair[at] += [from_left, from_right]
        found += pair
    return found


def project_kernel(group, count, me_ref, gain_ref, wq_ref, wk_ref, wv_ref, *refs):
    pieces = refs[:-3]
    out_ref, normed, sums = refs[-3:]
    step = pl.program_id(0)
    rows, width = pieces[0].shape

    @pl.when(step == 0)
    def _():
        for piece, (source, there) in zip(pieces, sources(me_ref[0], count)):
            def place(piece=piece, source=source):
                normed[source] = piece[...]

            if there is None:
                place()
            else:
                pl.when(there)(place)
        square = jnp.zeros((rows, 1), jnp.float32)
        for source in range(count):
            values = normed[source].astype(jnp.float32)
            square = square + jnp.sum(values * values, axis=1, keepdims=True)
        row_scale = lax.rsqrt(square / (count * width) + 1e-05)
        for source in range(count):
            values = normed[source].astype(jnp.float32)
            normed[source] = (values * row_scale * gain_ref[source : source + 1, :]).astype(
                jnp.bfloat16
            )

    x = normed[step]
    for which, weight in enumerate((wq_ref, wk_ref, wv_ref)):
        product = jnp.dot(x, weight[...], preferred_element_type=jnp.float32)

        @pl.when(step == 0)
        def _():
            sums[which] = product

        @pl.when(step > 0)
        def _():
            sums[which] += product

    @pl.when(step == count - 1)
    def _():
        part_rows = out_ref.shape[1]
        for which in range(3):
            total = sums[which].astype(jnp.bfloat16)
            for head in range(wq_ref.shape[1] // HEAD):
                for part in range(group):
                    out_ref[head * group + part, :, which * HEAD : (which + 1) * HEAD] = total[
                        part * part_rows : (part + 1) * part_rows, head * HEAD : (head + 1) * HEAD
                    ]


def project(me, pieces, gain, wq, wk, wv, seq_count, group):
    rows, columns = pieces[0].shape
    features, width = wq.shape
    count = features // columns
    part_rows = rows // group
    weight_spec = pl.BlockSpec((columns, width), lambda j: (j, 0))
    return pl.pallas_call(
        partial(project_kernel, group, count),
        grid=(count,),
        in_specs=[
            pl.BlockSpec(memory_space=pltpu.SMEM),
            pl.BlockSpec((count, columns), lambda j: (0, 0)),
            weight_spec,
            weight_spec,
            weight_spec,
        ]
        + [pl.BlockSpec((rows, columns), lambda j: (0, 0))] * len(pieces),
        out_specs=pl.BlockSpec((seq_count, part_rows, 3 * HEAD), lambda j: (0, 0, 0)),
        out_shape=jax.ShapeDtypeStruct((seq_count, part_rows, 3 * HEAD), jnp.bfloat16),
        scratch_shapes=[
            pltpu.VMEM((count, rows, columns), jnp.bfloat16),
            pltpu.VMEM((3, rows, width), jnp.float32),
        ],
        compiler_params=pltpu.CompilerParams(vmem_limit_bytes=LIMIT),
        cost_estimate=pl.CostEstimate(
            flops=6 * rows * features * width,
            bytes_accessed=6 * features * width + 2 * rows * (features + 3 * width),
            transcendentals=0,
        ),
    )(me, gain, wq, wk, wv, *pieces)


def attend_kernel(chunks, group, back, part_ref, bias_ref, *refs):
    pieces = refs[: chunks * group]
    outs = refs[chunks * group : chunks * group + back]
    keys, values = refs[-2:]
    mine = range(chunks)
    seq_count, part_rows, _ = pieces[0].shape
    rows = bias_ref.shape[1]
    chunk_rows = rows // chunks
    part = part_ref[0]

    def place(home, _):
        for chunk in range(chunks):
            for step in range(group):
                owner = lax.rem(part + step, group)
                at = pl.multiple_of(home * rows + chunk * chunk_rows + owner * part_rows, part_rows)
                piece = pieces[chunk * group + step]
                keys[pl.ds(at, part_rows), :] = piece[home, :, HEAD : 2 * HEAD]
                values[pl.ds(at, part_rows), :] = piece[home, :, 2 * HEAD :]
        return 0

    lax.fori_loop(0, seq_count, place, 0)
    scale = math.log2(math.e) / math.sqrt(HEAD)
    count = len(mine) * part_rows

    def store(home, rows_out):
        each = count // back
        for at, out in enumerate(outs):
            out[home] = rows_out[at * each : (at + 1) * each]

    def own_places():
        order = lax.broadcasted_iota(jnp.int32, (count, rows), 0)
        own = order % part_rows + part * part_rows
        for at_chunk, chunk in enumerate(mine):
            own = jnp.where(order // part_rows == at_chunk, own + chunk * chunk_rows, own)
        return own

    if seq_count <= 8:
        later = lax.broadcasted_iota(jnp.int32, (count, rows), 1) > own_places()
        for home in range(seq_count):
            queries = jnp.concatenate([pieces[c * group][home, :, :HEAD] for c in mine], axis=0)
            blocks = []
            for other in range(home + 1):
                scores = lax.dot_general(
                    queries,
                    keys[other * rows : (other + 1) * rows, :],
                    (((1,), (1,)), ((), ())),
                    preferred_element_type=jnp.float32,
                )
                scores = scores * scale + bias_ref[other : other + 1, :]
                if other == home:
                    scores = jnp.where(later, MASKED, scores)
                blocks.append(scores)
            scores = jnp.concatenate(blocks, axis=1)
            best = jnp.max(scores, axis=1, keepdims=True)
            weights = jnp.exp2(scores - best)
            total = jnp.sum(weights, axis=1, keepdims=True)
            summed = jnp.dot(
                weights.astype(jnp.bfloat16),
                values[: (home + 1) * rows, :],
                preferred_element_type=jnp.float32,
            )
            store(home, (summed / total).astype(jnp.bfloat16))
        return

    def one_home(home, _):
        queries = jnp.concatenate([pieces[c * group][home, :, :HEAD] for c in mine], axis=0)

        def fold(other, carry, diagonal):
            best, total, summed = carry
            at = pl.multiple_of(other * rows, rows)
            scores = lax.dot_general(
                queries,
                keys[pl.ds(at, rows), :],
                (((1,), (1,)), ((), ())),
                preferred_element_type=jnp.float32,
            )
            scores = scores * scale + bias_ref[pl.ds(other, 1), :]
            if diagonal:
                place_in = lax.broadcasted_iota(jnp.int32, (count, rows), 1)
                scores = jnp.where(place_in <= own_places(), scores, MASKED)
            newbest = jnp.maximum(best, jnp.max(scores, axis=1, keepdims=True))
            factor = jnp.exp2(best - newbest)
            weights = jnp.exp2(scores - newbest)
            total = total * factor + jnp.sum(weights, axis=1, keepdims=True)
            summed = summed * factor + jnp.dot(
                weights.astype(jnp.bfloat16),
                values[pl.ds(at, rows), :],
                preferred_element_type=jnp.float32,
            )
            return newbest, total, summed

        start = (
            jnp.full((count, 1), MASKED, jnp.float32),
            jnp.zeros((count, 1), jnp.float32),
            jnp.zeros((count, HEAD), jnp.float32),
        )
        carry = fold(home, start, True)
        carry = lax.fori_loop(0, home, lambda other, c: fold(other, c, False), carry)
        _, total, summed = carry
        store(home, (summed / total).astype(jnp.bfloat16))
        return 0

    lax.fori_loop(0, seq_count, one_home, 0)


def attend(part, bias, pieces, chunks, group, back):
    seq_count, part_rows, _ = pieces[0].shape
    rows = bias.shape[1]
    count = chunks * part_rows
    vmem = pl.BlockSpec(memory_space=pltpu.VMEM)
    pairs = seq_count * (seq_count + 1) // 2
    return pl.pallas_call(
        partial(attend_kernel, chunks, group, back),
        in_specs=[pl.BlockSpec(memory_space=pltpu.SMEM), vmem] + [vmem] * len(pieces),
        out_specs=[vmem] * back,
        out_shape=[jax.ShapeDtypeStruct((seq_count, count // back, HEAD), jnp.bfloat16)] * back,
        scratch_shapes=[
            pltpu.VMEM((seq_count * rows, HEAD), jnp.bfloat16),
            pltpu.VMEM((seq_count * rows, HEAD), jnp.bfloat16),
        ],
        compiler_params=pltpu.CompilerParams(vmem_limit_bytes=LIMIT),
        cost_estimate=pl.CostEstimate(
            flops=4 * pairs * count * rows * HEAD,
            bytes_accessed=8 * seq_count * rows * HEAD,
            transcendentals=pairs * count * rows,
        ),
    )(part, bias, *pieces)


def output_kernel(chunks, group, count, cuts, halves, me_ref, at_ref, hidden_ref, active_ref, *refs):
    weights = refs[:cuts]
    pieces = refs[cuts:-4]
    out_ref, rows_in, held, arrived = refs[-4:]
    copies = [
        pltpu.make_async_copy(weight, held.at[cut], arrived.at[cut])
        for cut, weight in enumerate(weights)
    ]
    for copy in copies:
        copy.start()
    seq_count, piece_rows, _ = pieces[0].shape
    heads = seq_count // group
    per_half = chunks // halves
    part_rows = piece_rows // per_half
    chunk_rows = part_rows * group
    width = weights[0].shape[1]
    found = sources(me_ref[0], count)

    for number, piece in enumerate(pieces):
        half, (source, there) = number // len(found), found[number % len(found)]

        def place(half=half, piece=piece, source=source):
            for head in range(heads):
                at = pl.multiple_of(at_ref[source * heads + head] * HEAD, HEAD)
                for part in range(group):
                    for chunk in range(per_half):
                        first = (half * per_half + chunk) * chunk_rows + part * part_rows
                        rows_in[first : first + part_rows, pl.ds(at, HEAD)] = piece[
                            head * group + part, chunk * part_rows : (chunk + 1) * part_rows, :
                        ]

        if there is None:
            place()
        else:
            pl.when(there)(place)

    for cut in range(cuts):
        copies[cut].wait()
        columns = pl.ds(pl.multiple_of(me_ref[1 + cut] * width, width), width)
        shares = jnp.dot(rows_in[...], held[cut], preferred_element_type=jnp.float32)
        hidden = hidden_ref[:, columns]
        renewed = (hidden.astype(jnp.float32) + shares).astype(jnp.bfloat16)
        out_ref[:, columns] = jnp.where(active_ref[...] > 0, renewed, hidden)


def output(scalars, at, pieces, weights, hidden, active, chunks, group, halves):
    rows, columns = hidden.shape
    depth, width = weights[0].shape
    smem = pl.BlockSpec(memory_space=pltpu.SMEM)
    vmem = pl.BlockSpec(memory_space=pltpu.VMEM)
    cuts = len(weights)
    count = (len(pieces) // halves + 1) // 2
    return pl.pallas_call(
        partial(output_kernel, chunks, group, count, cuts, halves),
        in_specs=[smem, smem, vmem, vmem]
        + [pl.BlockSpec(memory_space=pl.ANY)] * cuts
        + [vmem] * len(pieces),
        out_specs=vmem,
        out_shape=jax.ShapeDtypeStruct((rows, columns), jnp.bfloat16),
        scratch_shapes=[
            pltpu.VMEM((rows, depth), jnp.bfloat16),
            pltpu.VMEM((cuts, depth, width), jnp.bfloat16),
            pltpu.SemaphoreType.DMA((cuts,)),
        ],
        compiler_params=pltpu.CompilerParams(vmem_limit_bytes=LIMIT),
        cost_estimate=pl.CostEstimate(
            flops=2 * rows * depth * columns,
            bytes_accessed=2 * (rows * depth + depth * columns + 2 * rows * columns),
            transcendentals=0,
        ),
    )(scalars, at, hidden, active, *weights, *pieces)


def output_weight(w_out, seq_count, tensor_count, columns, after):
    heads = w_out.shape[0] // HEAD
    cuts = seq_count // heads
    width = columns // cuts
    row = jnp.arange(tensor_count * heads, dtype=jnp.int32)
    if width % HEAD:
        weight = lax.all_to_all(w_out, "tensor", split_axis=1, concat_axis=0, tiled=True)
        return [weight], [jnp.int32(0)], row
    seq_me = lax.axis_index("seq").astype(jnp.int32)
    me = lax.axis_index("tensor").astype(jnp.int32)
    head, cut = seq_me // cuts, seq_me % cuts

    def share(to):
        return lax.dynamic_slice(w_out, (head * HEAD, to * columns + cut * width), (HEAD, width))

    shares = [share((me + step) % tensor_count) for step in range(tensor_count)]
    shares, _ = lax.optimization_barrier((shares, after))
    for step in range(1, tensor_count):
        ring = [(d, (d + step) % tensor_count) for d in range(tensor_count)]
        shares[step] = lax.ppermute(shares[step], "tensor", ring)
    flips = []
    while cuts << len(flips) < seq_count:
        flips.append(cuts << len(flips))
    halves = 2 if width % (2 * HEAD) == 0 else 1
    each = width // halves
    weights, which = [], []
    for half in range(halves):
        held = {0: jnp.concatenate([s[:, half * each : (half + 1) * each] for s in shares], axis=0)}
        for flip in flips if half == 0 else flips[::-1]:
            pairs = [(d, d ^ flip) for d in range(seq_count)]
            sent = list(held)
            got = lax.ppermute(jnp.concatenate([held[k] for k in sent], axis=0), "seq", pairs)
            for k, block in zip(sent, jnp.split(got, len(sent))):
                held[k ^ flip] = block
        weights.append(jnp.concatenate([held[k] for k in sorted(held)], axis=0))
        which.append(cut * halves + half)
    for step in range(1, cuts):
        ring = [(d, d - d % cuts + (d - step) % cuts) for d in range(seq_count)]
        for half in range(halves):
            weights.append(lax.ppermute(weights[half], "seq", ring))
            which.append((cut + step) % cuts * halves + half)
    tensor, of = row // heads, row % heads
    at = (of ^ head) * tensor_count + (me - tensor) % tensor_count
    return weights, which, at


def shards(hidden, depth, norm_gain, w_query, w_key, w_value, w_out):
    rows, columns = hidden.shape
    seq_count = lax.axis_size("seq")
    tensor_count = lax.axis_size("tensor")
    heads = w_query.shape[1] // HEAD
    group = seq_count // heads
    chunks = min(4, rows // (16 * group))
    chunk_rows = rows // chunks
    back = min(BACK, chunks)
    part = (lax.axis_index("seq") % group).astype(jnp.int32).reshape(1)
    me = lax.axis_index("tensor").astype(jnp.int32)
    gain = norm_gain.reshape(tensor_count, columns)
    depths = lax.all_gather(depth, "seq", axis=0)
    bias = jnp.where(depths >= 2, 0.0, MASKED).astype(jnp.float32)
    active = (depth >= 2).astype(jnp.int32).reshape(rows, 1)

    gathered = line_gather(
        [hidden[c * chunk_rows : (c + 1) * chunk_rows] for c in range(chunks)], tensor_count, bias
    )
    pieces = []
    for found in gathered:
        sent = project(me.reshape(1), found, gain, w_query, w_key, w_value, seq_count, group)
        got = lax.all_to_all(sent, "seq", split_axis=0, concat_axis=0)
        pieces.append(got)
        for step in range(1, group):
            ring = [(d, d - d % group + (d - step) % group) for d in range(seq_count)]
            pieces.append(lax.ppermute(got, "seq", ring))

    weights, cut_of, at = output_weight(w_out, seq_count, tensor_count, columns, sent)
    scalars = jnp.stack([me, *cut_of])
    outs = attend(part, bias, pieces, chunks, group, back)
    homes = [lax.all_to_all(out, "seq", split_axis=0, concat_axis=0) for out in outs]
    found = sum(line_gather(homes, tensor_count), [])
    return output(scalars, at, found, weights, hidden, active, chunks, group, back)


def solution(mesh):
    return jax.shard_map(
        shards,
        mesh=mesh,
        in_specs=(
            P("seq", "tensor"),
            P("seq"),
            P(),
            P(None, "tensor"),
            P(None, "tensor"),
            P(None, "tensor"),
            P("tensor", None),
        ),
        out_specs=P("seq", "tensor"),
        check_vma=False,
    )
```

time: 235 us -> 248 us (1.055)
  local copies, waits for them, and re-layouts: 9.39 us -> 19.2 us
  waiting for transfers between devices: 54.4 us -> 60.4 us
  starting transfers between devices: 103 us -> 98.2 us
    ppermute x18, starting transfers between devices: 49.5 us -> 34.7 us  [line_gather(): from_left = lax.ppermute(from_left, 'tensor', right[step:])]
    all_to_all x2, waiting for transfers between devices: 0.01 us -> 9.12 us  [shards(): lax.all_to_all(out, 'seq', split_axis=0, concat_axis=0)]
    ppermute x6 -> x9, starting transfers between devices: 6.61 us -> 15.7 us  [the longest x3 9.85 us: output_weight(): shares[step] = lax.ppermute(shares[step], 'tensor', ring)]
    ppermute x18, waiting for transfers between devices: 46.3 us -> 38.2 us  [line_gather(): from_right = lax.ppermute(from_right, 'tensor', left[:count - 1 - step])]
    slice x0 -> x4, local copies, waits for them, and re-layouts: none -> 5.32 us  [output_weight(): s[:, half * each:(half + 1) * each]]
    ppermute x6 -> x9, waiting for transfers between devices: 0.06 us -> 4.13 us  [the longest x4 4.12 us: output_weight(): lax.ppermute(jnp.concatenate([held[k] for k in sent], axis=0), 'seq', pairs)]
    pallas_call x8 -> x6, Pallas kernels: 55.4 us -> 56.8 us  [the longest x4 36.6 us: project(): pl.pallas_call(partial(project_kernel, group, count), grid=(count,), in_s...]
  transfers between devices with their start and end apart: 52 -> 55, of which waited for: 14 -> 19; matrix products, arithmetic and copies ran while one was open for 2% -> 6% of each run, Pallas kernels for 21% -> 19%
where the time goes in v3:
time: 248 us; the launch traced here: 247 us
  starting transfers between devices  98.2 us (40%)
  waiting for transfers between devices  60.4 us (24%)
  Pallas kernels  56.8 us (23%)
  local copies, waits for them, and re-layouts  19.2 us (8%)
  blocking collectives  9.04 us (4%)
    ppermute x18, waiting for transfers between devices, line_gather(): from_right = lax.ppermute(from_right, 'tensor', left[:count - 1 - step])  38.2 us
    pallas_call x4, Pallas kernels, project(): pl.pallas_call(partial(project_kernel, group, count), grid=(count,), in_s...  36.6 us
    ppermute x18, starting transfers between devices, line_gather(): from_left = lax.ppermute(from_left, 'tensor', right[step:])  34.7 us
    ppermute x18, starting transfers between devices, line_gather(): from_right = lax.ppermute(from_right, 'tensor', left[:count - 1 - step])  23.1 us
    all_to_all x4, starting transfers between devices, shards(): got = lax.all_to_all(sent, 'seq', split_axis=0, concat_axis=0)  16 us
    pallas_call x1, Pallas kernels, attend(): pl.pallas_call(partial(attend_kernel, chunks, group, back), in_specs=[pl....  10.7 us
    ppermute x3, starting transfers between devices, output_weight(): shares[step] = lax.ppermute(shares[step], 'tensor', ring)  9.85 us
    pallas_call x1, Pallas kernels, output(): pl.pallas_call(partial(output_kernel, chunks, group, count, cuts, halves)...  9.55 us
  transfers between devices with their start and end apart: 55, of which 19 were waited for; matrix products, arithmetic and copies ran while one was open for 6% of the time, Pallas kernels for 19%

profile of v3, /device:TPU:0, one launch (start us, length us, event | category | flops | bytes accessed | tf_op | source)
XLA Modules:
  0.0 246.5 jit_solution(9857955829682652655)
XLA Ops:
  1.3 4.9 %collective-permute-start = (bf16[128,1024]{1,0:T(8,128)(2,1)S(1)}, bf16[128,1024]{1,0:T(8,128)(2,1)S(1)}, u32[]{:S(2)}, u32[]{:S(2)}) collective-permute-start(bf16[128,1024]{1,0:T(8,128)(2,1)S(1)} %get-tuple-element.27.refs_0_), channel_id=1, source_target_pairs={{0,1},{1,2},{2,3},{4,5},{5,6},{6,7},{8,9},{9,10},{10,11},{12,13},{... | collective-permute-start | bytes 786440 | tf_op jit(solution)/shard_map/ppermute | solution.py:38
  6.3 1.3 collective-permute-start.1
  7.6 4.6 %collective-permute-start.21 = (bf16[128,1024]{1,0:T(8,128)(2,1)S(1)}, bf16[128,1024]{1,0:T(8,128)(2,1)S(1)}, u32[]{:S(2)}, u32[]{:S(2)}) collective-permute-start(bf16[128,1024]{1,0:T(8,128)(2,1)S(1)} %get-tuple-element.26.refs_0_), channel_id=1, source_target_pairs={{0,1},{1,2},{2,3},{4,5},{5,6},{6,7},{8,9},{9,10},{10,11},{12,13},{... | collective-permute-start | bytes 786440 | tf_op jit(solution)/shard_map/ppermute | solution.py:38
  12.1 1.3 collective-permute-start.22
  14.1 2.0 collective-permute-done.1.refs_2_
  18.2 4.1 %collective-permute-done.22.refs_2_ = bf16[128,1024]{1,0:T(8,128)(2,1)S(1)} collective-permute-done((bf16[128,1024]{1,0:T(8,128)(2,1)S(1)}, bf16[128,1024]{1,0:T(8,128)(2,1)S(1)}, u32[]{:S(2)}, u32[]{:S(2)}) %collective-permute-start.22) | collective-permute-done | bytes 262176 | tf_op jit(solution)/shard_map/ppermute | solution.py:39
  24.2 3.9 %collective-permute-done.3.refs_4_ = bf16[128,1024]{1,0:T(8,128)(2,1)S(1)} collective-permute-done((bf16[128,1024]{1,0:T(8,128)(2,1)S(1)}, bf16[128,1024]{1,0:T(8,128)(2,1)S(1)}, u32[]{:S(2)}, u32[]{:S(2)}) %collective-permute-start.3) | collective-permute-done | bytes 262176 | tf_op jit(solution)/shard_map/ppermute | solution.py:39
  29.4 9.0 %all-gather.1 = s32[8,1,512]{2,1,0:T(1,128)S(1)} all-gather(s32[1,1,512]{2,1,0:T(1,128)} %bitcast.11), channel_id=2, replica_groups=mesh['seq'=8,'tensor'=4] {'seq'}, dimensions={0}, use_global_device_ids=true | all-gather | bytes 18432 | tf_op jit(solution)/shard_map/all_gather | solution.py:389
  39.1 1.3 collective-permute-start.26
  41.0 5.3 %collective-permute-start.6 = (bf16[128,1024]{1,0:T(8,128)(2,1)S(1)}, bf16[128,1024]{1,0:T(8,128)(2,1)}, u32[]{:S(2)}, u32[]{:S(2)}) collective-permute-start(bf16[128,1024]{1,0:T(8,128)(2,1)S(1)} %get-tuple-element.13.refs_0_), channel_id=1, source_target_pairs={{0,1},{1,2},{2,3},{4,5},{5,6},{6,7},{8,9},{9,10},{10,11},{12,13},{... | collective-permute-start | bytes 786440 | tf_op jit(solution)/shard_map/ppermute | solution.py:38
  47.7 2.2 collective-permute-done.26.refs_6_
  49.9 2.4 collective-permute-start.29
  52.3 1.3 collective-permute-start.30
  53.6 1.4 collective-permute-start.8
  54.9 1.9 collective-permute-done.7.refs_2_
  56.8 1.3 collective-permute-start.9
  58.2 1.3 reshape.17.gain_ref
  59.5 1.9 fusion.5
  61.4 1.4 collective-permute-start.31
  64.6 1.4 collective-permute-start.10
  66.0 1.9 collective-permute-done.9.refs_4_
  69.2 9.2 %shard_map.74 = bf16[8,64,384]{2,1,0:T(8,128)(2,1)} custom-call(s32[1]{0:T(128)} %bitcast.me_ref, f32[4,1024]{1,0:T(4,128)} %reshape.17.gain_ref, bf16[4096,512]{1,0:T(8,128)(2,1)} %wq_ref.7, bf16[4096,512]{1,0:T(8,128)(2,1)} %wk_ref.7, bf16[4096,512]{1,0:T(8,128)(2,1)} %wv_ref.7, bf16[128,1024]{1,0:T(8,128)(2,1)} %copy-done.5, ...), custom_call_target="tpu_custom_call" | custom-call | flops 1610612736 | bytes 14024704 | tf_op jit(solution)/shard_map/pallas_call | solution.py:103
  78.4 3.5 %all-to-all-start = ((bf16[8,64,384]{2,1,0:T(8,128)(2,1)}), bf16[8,64,384]{2,1,0:T(8,128)(2,1)S(1)}, u32[]{:S(2)}, u32[]{:S(2)}) async-start(bf16[8,64,384]{2,1,0:T(8,128)(2,1)} %shard_map.74), calls=%async_computation | async-start | bytes 786432 | tf_op jit(solution)/shard_map/all_to_all | solution.py:399
  81.9 9.1 %shard_map.75 = bf16[8,64,384]{2,1,0:T(8,128)(2,1)} custom-call(s32[1]{0:T(128)} %bitcast.me_ref, f32[4,1024]{1,0:T(4,128)} %reshape.17.gain_ref, bf16[4096,512]{1,0:T(8,128)(2,1)} %wq_ref.7, bf16[4096,512]{1,0:T(8,128)(2,1)} %wk_ref.7, bf16[4096,512]{1,0:T(8,128)(2,1)} %wv_ref.7, bf16[128,1024]{1,0:T(8,128)(2,1)} %copy-done.4, bf16[128,1024]{1,0:T(8,128)(2,1)} %copy-done.8, ...), custom_call_target="tpu_custom_call" | custom-call | flops 1610612736 | bytes 14024704 | tf_op jit(solution)/shard_map/pallas_call | solution.py:103
  91.7 1.3 collective-permute-start.34
  93.0 9.1 %shard_map.73 = bf16[8,64,384]{2,1,0:T(8,128)(2,1)} custom-call(s32[1]{0:T(128)} %bitcast.me_ref, f32[4,1024]{1,0:T(4,128)} %reshape.17.gain_ref, bf16[4096,512]{1,0:T(8,128)(2,1)} %wq_ref.7, bf16[4096,512]{1,0:T(8,128)(2,1)} %wk_ref.7, bf16[4096,512]{1,0:T(8,128)(2,1)} %wv_ref.7, bf16[128,1024]{1,0:T(8,128)(2,1)} %copy-done.3, ...), custom_call_target="tpu_custom_call" | custom-call | flops 1610612736 | bytes 14024704 | tf_op jit(solution)/shard_map/pallas_call | solution.py:103
  102.2 1.5 collective-permute-start.14
  103.7 6.4 %collective-permute-start.13 = (bf16[128,512]{1,0:T(8,128)(2,1)}, bf16[128,512]{1,0:T(8,128)(2,1)}, u32[]{:S(2)}, u32[]{:S(2)}) collective-permute-start(bf16[128,512]{1,0:T(8,128)(2,1)} %get-tuple-element.16), channel_id=1, source_target_pairs={{0,2},{1,3},{2,0},{3,1},{4,6},{5,7},{6,4},{7,5},{8,10},{9,11},{10,... | collective-permute-start | bytes 393224 | tf_op jit(solution)/shard_map/ppermute | solution.py:350
  110.1 2.0 collective-permute-start.12
  112.7 4.1 %all-to-all-start.1 = ((bf16[8,64,384]{2,1,0:T(8,128)(2,1)}), bf16[8,64,384]{2,1,0:T(8,128)(2,1)}, u32[]{:S(2)}, u32[]{:S(2)}) async-start(bf16[8,64,384]{2,1,0:T(8,128)(2,1)} %shard_map.75), calls=%async_computation.1 | async-start | bytes 786432 | tf_op jit(solution)/shard_map/all_to_all | solution.py:399
  118.3 9.1 %shard_map.76 = bf16[8,64,384]{2,1,0:T(8,128)(2,1)} custom-call(s32[1]{0:T(128)} %bitcast.me_ref, f32[4,1024]{1,0:T(4,128)} %reshape.17.gain_ref, bf16[4096,512]{1,0:T(8,128)(2,1)} %wq_ref.7, bf16[4096,512]{1,0:T(8,128)(2,1)} %wk_ref.7, bf16[4096,512]{1,0:T(8,128)(2,1)} %wv_ref.7, bf16[128,1024]{1,0:T(8,128)(2,1)} %copy-done.2, ...), custom_call_target="tpu_custom_call" | custom-call | flops 1610612736 | bytes 14024704 | tf_op jit(solution)/shard_map/pallas_call | solution.py:103
  128.0 1.5 fusion.8
  129.6 4.2 %all-to-all-start.2 = ((bf16[8,64,384]{2,1,0:T(8,128)(2,1)}), bf16[8,64,384]{2,1,0:T(8,128)(2,1)}, u32[]{:S(2)}, u32[]{:S(2)}) async-start(bf16[8,64,384]{2,1,0:T(8,128)(2,1)} %shard_map.76), calls=%async_computation.2 | async-start | bytes 786432 | tf_op jit(solution)/shard_map/all_to_all | solution.py:399
  133.8 1.6 fusion.9
  136.0 1.5 fusion.10
  137.5 4.7 %all-to-all-done.2.refs_4_ = bf16[8,64,384]{2,1,0:T(8,128)(2,1)} async-done(((bf16[8,64,384]{2,1,0:T(8,128)(2,1)}), bf16[8,64,384]{2,1,0:T(8,128)(2,1)}, u32[]{:S(2)}, u32[]{:S(2)}) %all-to-all-start.2) | async-done | bytes 393248 | tf_op jit(solution)/shard_map/all_to_all | solution.py:399
  142.2 4.3 %all-to-all-start.3 = ((bf16[8,64,384]{2,1,0:T(8,128)(2,1)}), bf16[8,64,384]{2,1,0:T(8,128)(2,1)}, u32[]{:S(2)}, u32[]{:S(2)}) async-start(bf16[8,64,384]{2,1,0:T(8,128)(2,1)} %shard_map.73), calls=%async_computation.3 | async-start | bytes 786432 | tf_op jit(solution)/shard_map/all_to_all | solution.py:399
  146.5 1.8 collective-permute-start.15
  149.1 1.5 collective-permute-start.17
  151.1 4.1 %all-to-all-done.3.refs_6_ = bf16[8,64,384]{2,1,0:T(8,128)(2,1)} async-done(((bf16[8,64,384]{2,1,0:T(8,128)(2,1)}), bf16[8,64,384]{2,1,0:T(8,128)(2,1)}, u32[]{:S(2)}, u32[]{:S(2)}) %all-to-all-start.3) | async-done | bytes 393248 | tf_op jit(solution)/shard_map/all_to_all | solution.py:399
  155.1 4.1 %collective-permute-done.15 = bf16[512,256]{1,0:T(8,128)(2,1)S(1)} collective-permute-done((bf16[512,256]{1,0:T(8,128)(2,1)S(1)}, bf16[512,256]{1,0:T(8,128)(2,1)S(1)}, u32[]{:S(2)}, u32[]{:S(2)}) %collective-permute-start.15) | collective-permute-done | bytes 262176 | tf_op jit(solution)/shard_map/ppermute | solution.py:362
  160.0 1.5 collective-permute-start.16
  163.5 10.7 %shard_map.77 = (bf16[8,128,128]{2,1,0:T(8,128)(2,1)}, bf16[8,128,128]{2,1,0:T(8,128)(2,1)}) custom-call(s32[1]{0:T(128)} %bitcast.8.part_ref, f32[8,512]{1,0:T(8,128)} %select_bitcast_fusion.bias_ref, bf16[8,64,384]{2,1,0:T(8,128)(2,1)} %copy-done.7, bf16[8,64,384]{2,1,0:T(8,128)(2,1)} %collective-permute-done.27.refs_1_, ...), custom_call_target="tpu_custom_call" | custom-call | flops 2415919104 | bytes 4194304 | tf_op jit(solution)/shard_map/pallas_call | solution.py:240
  174.2 4.1 %all-to-all-start.4 = ((bf16[8,128,128]{2,1,0:T(8,128)(2,1)}), bf16[8,128,128]{2,1,0:T(8,128)(2,1)}, u32[]{:S(2)}, u32[]{:S(2)}) async-start(bf16[8,128,128]{2,1,0:T(8,128)(2,1)} %get-tuple-element.19), calls=%async_computation.4 | async-start | bytes 524288 | tf_op jit(solution)/shard_map/all_to_all | solution.py:408
  178.8 6.4 %all-to-all-done.4.refs_4_ = bf16[8,128,128]{2,1,0:T(8,128)(2,1)} async-done(((bf16[8,128,128]{2,1,0:T(8,128)(2,1)}), bf16[8,128,128]{2,1,0:T(8,128)(2,1)}, u32[]{:S(2)}, u32[]{:S(2)}) %all-to-all-start.4) | async-done | bytes 262176 | tf_op jit(solution)/shard_map/all_to_all | solution.py:408
  185.2 4.1 %all-to-all-start.5 = ((bf16[8,128,128]{2,1,0:T(8,128)(2,1)}), bf16[8,128,128]{2,1,0:T(8,128)(2,1)}, u32[]{:S(2)}, u32[]{:S(2)}) async-start(bf16[8,128,128]{2,1,0:T(8,128)(2,1)} %get-tuple-element.20), calls=%async_computation.5 | async-start | bytes 524288 | tf_op jit(solution)/shard_map/all_to_all | solution.py:408
  190.3 2.0 collective-permute-start.37
  192.3 1.3 collective-permute-start.38
  193.6 2.7 %all-to-all-done.5.refs_11_ = bf16[8,128,128]{2,1,0:T(8,128)(2,1)} async-done(((bf16[8,128,128]{2,1,0:T(8,128)(2,1)}), bf16[8,128,128]{2,1,0:T(8,128)(2,1)}, u32[]{:S(2)}, u32[]{:S(2)}) %all-to-all-start.5) | async-done | bytes 262176 | tf_op jit(solution)/shard_map/all_to_all | solution.py:408
  196.2 2.6 %collective-permute-start.43 = (bf16[8,128,128]{2,1,0:T(8,128)(2,1)}, bf16[8,128,128]{2,1,0:T(8,128)(2,1)}, u32[]{:S(2)}, u32[]{:S(2)}) collective-permute-start(bf16[8,128,128]{2,1,0:T(8,128)(2,1)} %all-to-all-done.5.refs_11_), channel_id=1, source_target_pairs={{0,1},{1,2},{2,3},{4,5},{5,6},{6,7},{8,9},{9,10},{10,11},{12,13},{... | collective-permute-start | bytes 786440 | tf_op jit(solution)/shard_map/ppermute | solution.py:38
  199.9 1.3 collective-permute-start.44
  201.2 1.5 collective-permute-done.38.refs_6_
  202.8 1.4 collective-permute-start.39
  205.5 5.3 %collective-permute-done.44.refs_13_ = bf16[8,128,128]{2,1,0:T(8,128)(2,1)} collective-permute-done((bf16[8,128,128]{2,1,0:T(8,128)(2,1)}, bf16[8,128,128]{2,1,0:T(8,128)(2,1)}, u32[]{:S(2)}, u32[]{:S(2)}) %collective-permute-start.44) | collective-permute-done | bytes 262176 | tf_op jit(solution)/shard_map/ppermute | solution.py:39
  210.9 1.4 collective-permute-start.45
  212.3 1.3 collective-permute-start.46
  213.6 2.9 %collective-permute-done.40.refs_8_ = bf16[8,128,128]{2,1,0:T(8,128)(2,1)} collective-permute-done((bf16[8,128,128]{2,1,0:T(8,128)(2,1)}, bf16[8,128,128]{2,1,0:T(8,128)(2,1)}, u32[]{:S(2)}, u32[]{:S(2)}) %collective-permute-start.40) | collective-permute-done | bytes 262176 | tf_op jit(solution)/shard_map/ppermute | solution.py:39
  216.4 1.3 collective-permute-start.41
  217.8 1.3 collective-permute-start.42
  219.1 6.7 %collective-permute-done.46.refs_15_ = bf16[8,128,128]{2,1,0:T(8,128)(2,1)} collective-permute-done((bf16[8,128,128]{2,1,0:T(8,128)(2,1)}, bf16[8,128,128]{2,1,0:T(8,128)(2,1)}, u32[]{:S(2)}, u32[]{:S(2)}) %collective-permute-start.46) | collective-permute-done | bytes 262176 | tf_op jit(solution)/shard_map/ppermute | solution.py:39
  225.8 1.4 collective-permute-start.47
  227.2 1.3 collective-permute-start.48
  230.7 5.1 %collective-permute-done.48.refs_17_ = bf16[8,128,128]{2,1,0:T(8,128)(2,1)} collective-permute-done((bf16[8,128,128]{2,1,0:T(8,128)(2,1)}, bf16[8,128,128]{2,1,0:T(8,128)(2,1)}, u32[]{:S(2)}, u32[]{:S(2)}) %collective-permute-start.48) | collective-permute-done | bytes 262176 | tf_op jit(solution)/shard_map/ppermute | solution.py:39
  236.8 9.5 %shard_map.78 = bf16[512,1024]{1,0:T(8,128)(2,1)} custom-call(s32[5]{0:T(128)} %stack.23.me_ref, s32[16]{0:T(128)} %fusion.at_ref, bf16[512,1024]{1,0:T(8,128)(2,1)} %hidden_ref.1, s32[512,1]{1,0:T(8,128)} %copy.10.active_ref, bf16[2048,256]{1,0:T(8,128)(2,1)} %copy-done, bf16[2048,256]{1,0:T(8,128)(2,1)} %copy-done.1, bf16[2048,256]{1,0:T(8,128)(2,1)} %copy-done.6, ...), custom_call_target="tpu_custom_call" | custom-call | flops 2147483648 | bytes 8388608 | tf_op jit(solution)/shard_map/pallas_call | solution.py:310
  (129 shorter events, 28.0 us)
Async XLA Ops:
  1.3 67.9 %copy-start.5 = (bf16[128,1024]{1,0:T(8,128)(2,1)}, bf16[128,1024]{1,0:T(8,128)(2,1)S(1)}, u32[]{:S(2)}) copy-start(bf16[128,1024]{1,0:T(8,128)(2,1)S(1)} %get-tuple-element.26.refs_0_) | copy-start | bytes 786436
  1.3 77.1 %copy-start.2 = (bf16[128,1024]{1,0:T(8,128)(2,1)}, bf16[128,1024]{1,0:T(8,128)(2,1)S(1)}, u32[]{:S(2)}) copy-start(bf16[128,1024]{1,0:T(8,128)(2,1)S(1)} %get-tuple-element.18.refs_0_) | copy-start | bytes 786436
  1.3 77.1 %copy-start.3 = (bf16[128,1024]{1,0:T(8,128)(2,1)}, bf16[128,1024]{1,0:T(8,128)(2,1)S(1)}, u32[]{:S(2)}) copy-start(bf16[128,1024]{1,0:T(8,128)(2,1)S(1)} %get-tuple-element.13.refs_0_) | copy-start | bytes 786436
  1.3 77.1 %copy-start.4 = (bf16[128,1024]{1,0:T(8,128)(2,1)}, bf16[128,1024]{1,0:T(8,128)(2,1)S(1)}, u32[]{:S(2)}) copy-start(bf16[128,1024]{1,0:T(8,128)(2,1)S(1)} %get-tuple-element.27.refs_0_) | copy-start | bytes 786436
  1.3 12.1 %collective-permute-start = (bf16[128,1024]{1,0:T(8,128)(2,1)S(1)}, bf16[128,1024]{1,0:T(8,128)(2,1)S(1)}, u32[]{:S(2)}, u32[]{:S(2)}) collective-permute-start(bf16[128,1024]{1,0:T(8,128)(2,1)S(1)} %get-tuple-element.27.refs_0_), channel_id=1, source_target_pairs={{0,1},{1,2},{2,3},{4,5},{5,6},{6,7},{8,9},{9,10},{10,11},{12,13},{... | collective-permute-start | bytes 786440 | tf_op jit(solution)/shard_map/ppermute | solution.py:38
  6.3 9.9 %collective-permute-start.1 = (bf16[128,1024]{1,0:T(8,128)(2,1)S(1)}, bf16[128,1024]{1,0:T(8,128)(2,1)S(1)}, u32[]{:S(2)}, u32[]{:S(2)}) collective-permute-start(bf16[128,1024]{1,0:T(8,128)(2,1)S(1)} %get-tuple-element.27.refs_0_), channel_id=1, source_target_pairs={{1,0},{2,1},{3,2},{5,4},{6,5},{7,6},{9,8},{10,9},{11,10},{13,12},{... | collective-permute-start | bytes 786440 | tf_op jit(solution)/shard_map/ppermute | solution.py:39
  7.6 9.9 %collective-permute-start.21 = (bf16[128,1024]{1,0:T(8,128)(2,1)S(1)}, bf16[128,1024]{1,0:T(8,128)(2,1)S(1)}, u32[]{:S(2)}, u32[]{:S(2)}) collective-permute-start(bf16[128,1024]{1,0:T(8,128)(2,1)S(1)} %get-tuple-element.26.refs_0_), channel_id=1, source_target_pairs={{0,1},{1,2},{2,3},{4,5},{5,6},{6,7},{8,9},{9,10},{10,11},{12,13},{... | collective-permute-start | bytes 786440 | tf_op jit(solution)/shard_map/ppermute | solution.py:38
  12.1 10.1 %collective-permute-start.22 = (bf16[128,1024]{1,0:T(8,128)(2,1)S(1)}, bf16[128,1024]{1,0:T(8,128)(2,1)S(1)}, u32[]{:S(2)}, u32[]{:S(2)}) collective-permute-start(bf16[128,1024]{1,0:T(8,128)(2,1)S(1)} %get-tuple-element.26.refs_0_), channel_id=1, source_target_pairs={{1,0},{2,1},{3,2},{5,4},{6,5},{7,6},{9,8},{10,9},{11,10},{13,12},{... | collective-permute-start | bytes 786440 | tf_op jit(solution)/shard_map/ppermute | solution.py:39
  13.4 64.9 %copy-start.8 = (bf16[128,1024]{1,0:T(8,128)(2,1)}, bf16[128,1024]{1,0:T(8,128)(2,1)S(1)}, u32[]{:S(2)}) copy-start(bf16[128,1024]{1,0:T(8,128)(2,1)S(1)} %collective-permute-done.refs_1_) | copy-start | bytes 786436
  13.4 10.1 %collective-permute-start.2 = (bf16[128,1024]{1,0:T(8,128)(2,1)S(1)}, bf16[128,1024]{1,0:T(8,128)(2,1)S(1)}, u32[]{:S(2)}, u32[]{:S(2)}) collective-permute-start(bf16[128,1024]{1,0:T(8,128)(2,1)S(1)} %collective-permute-done.refs_1_), channel_id=1, source_target_pairs={{1,2},{2,3},{5,6},{6,7},{9,10},{10,11},{13,14},{14,15},{17,18},{18... | collective-permute-start | bytes 786440 | tf_op jit(solution)/shard_map/ppermute | solution.py:38
  16.2 62.2 %copy-start.9 = (bf16[128,1024]{1,0:T(8,128)(2,1)}, bf16[128,1024]{1,0:T(8,128)(2,1)S(1)}, u32[]{:S(2)}) copy-start(bf16[128,1024]{1,0:T(8,128)(2,1)S(1)} %collective-permute-done.1.refs_2_) | copy-start | bytes 786436
  16.2 11.9 %collective-permute-start.3 = (bf16[128,1024]{1,0:T(8,128)(2,1)S(1)}, bf16[128,1024]{1,0:T(8,128)(2,1)S(1)}, u32[]{:S(2)}, u32[]{:S(2)}) collective-permute-start(bf16[128,1024]{1,0:T(8,128)(2,1)S(1)} %collective-permute-done.1.refs_2_), channel_id=1, source_target_pairs={{1,0},{2,1},{5,4},{6,5},{9,8},{10,9},{13,12},{14,13},{17,16},{18,1... | collective-permute-start | bytes 786440 | tf_op jit(solution)/shard_map/ppermute | solution.py:39
  17.5 21.0 %collective-permute-start.23 = (bf16[128,1024]{1,0:T(8,128)(2,1)S(1)}, bf16[128,1024]{1,0:T(8,128)(2,1)S(1)}, u32[]{:S(2)}, u32[]{:S(2)}) collective-permute-start(bf16[128,1024]{1,0:T(8,128)(2,1)S(1)} %collective-permute-done.21.refs_1_), channel_id=1, source_target_pairs={{1,2},{2,3},{5,6},{6,7},{9,10},{10,11},{13,14},{14,15},{17,18},{18... | collective-permute-start | bytes 786440 | tf_op jit(solution)/shard_map/ppermute | solution.py:38
  22.2 16.9 %collective-permute-start.24 = (bf16[128,1024]{1,0:T(8,128)(2,1)S(1)}, bf16[128,1024]{1,0:T(8,128)(2,1)S(1)}, u32[]{:S(2)}, u32[]{:S(2)}) collective-permute-start(bf16[128,1024]{1,0:T(8,128)(2,1)S(1)} %collective-permute-done.22.refs_2_), channel_id=1, source_target_pairs={{1,0},{2,1},{5,4},{6,5},{9,8},{10,9},{13,12},{14,13},{17,16},{18,1... | collective-permute-start | bytes 786440 | tf_op jit(solution)/shard_map/ppermute | solution.py:39
  23.5 54.9 %copy-start.10 = (bf16[128,1024]{1,0:T(8,128)(2,1)}, bf16[128,1024]{1,0:T(8,128)(2,1)S(1)}, u32[]{:S(2)}) copy-start(bf16[128,1024]{1,0:T(8,128)(2,1)S(1)} %collective-permute-done.2.refs_3_) | copy-start | bytes 786436
  23.5 17.5 %collective-permute-start.4 = (bf16[128,1024]{1,0:T(8,128)(2,1)S(1)}, bf16[128,1024]{1,0:T(8,128)(2,1)S(1)}, u32[]{:S(2)}, u32[]{:S(2)}) collective-permute-start(bf16[128,1024]{1,0:T(8,128)(2,1)S(1)} %collective-permute-done.2.refs_3_), channel_id=1, source_target_pairs={{2,3},{6,7},{10,11},{14,15},{18,19},{22,23},{26,27},{30,31}} | collective-permute-start | bytes 786440 | tf_op jit(solution)/shard_map/ppermute | solution.py:38
  28.1 12.9 %collective-permute-start.5 = (bf16[128,1024]{1,0:T(8,128)(2,1)S(1)}, bf16[128,1024]{1,0:T(8,128)(2,1)S(1)}, u32[]{:S(2)}, u32[]{:S(2)}) collective-permute-start(bf16[128,1024]{1,0:T(8,128)(2,1)S(1)} %collective-permute-done.3.refs_4_), channel_id=1, source_target_pairs={{1,0},{5,4},{9,8},{13,12},{17,16},{21,20},{25,24},{29,28}} | collective-permute-start | bytes 786440 | tf_op jit(solution)/shard_map/ppermute | solution.py:39
  38.4 9.2 %collective-permute-start.25 = (bf16[128,1024]{1,0:T(8,128)(2,1)S(1)}, bf16[128,1024]{1,0:T(8,128)(2,1)S(1)}, u32[]{:S(2)}, u32[]{:S(2)}) collective-permute-start(bf16[128,1024]{1,0:T(8,128)(2,1)S(1)} %collective-permute-done.23.refs_3_), channel_id=1, source_target_pairs={{2,3},{6,7},{10,11},{14,15},{18,19},{22,23},{26,27},{30,31}} | collective-permute-start | bytes 786440 | tf_op jit(solution)/shard_map/ppermute | solution.py:38
  39.1 10.7 %collective-permute-start.26 = (bf16[128,1024]{1,0:T(8,128)(2,1)S(1)}, bf16[128,1024]{1,0:T(8,128)(2,1)S(1)}, u32[]{:S(2)}, u32[]{:S(2)}) collective-permute-start(bf16[128,1024]{1,0:T(8,128)(2,1)S(1)} %collective-permute-done.24.refs_4_), channel_id=1, source_target_pairs={{1,0},{5,4},{9,8},{13,12},{17,16},{21,20},{25,24},{29,28}} | collective-permute-start | bytes 786440 | tf_op jit(solution)/shard_map/ppermute | solution.py:39
  41.0 12.5 %collective-permute-start.6 = (bf16[128,1024]{1,0:T(8,128)(2,1)S(1)}, bf16[128,1024]{1,0:T(8,128)(2,1)}, u32[]{:S(2)}, u32[]{:S(2)}) collective-permute-start(bf16[128,1024]{1,0:T(8,128)(2,1)S(1)} %get-tuple-element.13.refs_0_), channel_id=1, source_target_pairs={{0,1},{1,2},{2,3},{4,5},{5,6},{6,7},{8,9},{9,10},{10,11},{12,13},{... | collective-permute-start | bytes 786440 | tf_op jit(solution)/shard_map/ppermute | solution.py:38
  46.4 10.5 %collective-permute-start.7 = (bf16[128,1024]{1,0:T(8,128)(2,1)S(1)}, bf16[128,1024]{1,0:T(8,128)(2,1)}, u32[]{:S(2)}, u32[]{:S(2)}) collective-permute-start(bf16[128,1024]{1,0:T(8,128)(2,1)S(1)} %get-tuple-element.13.refs_0_), channel_id=1, source_target_pairs={{1,0},{2,1},{3,2},{5,4},{6,5},{7,6},{9,8},{10,9},{11,10},{13,12},{... | collective-permute-start | bytes 786440 | tf_op jit(solution)/shard_map/ppermute | solution.py:39
  49.9 11.6 %collective-permute-start.29 = (bf16[128,1024]{1,0:T(8,128)(2,1)S(1)}, bf16[128,1024]{1,0:T(8,128)(2,1)S(1)}, u32[]{:S(2)}, u32[]{:S(2)}) collective-permute-start(bf16[128,1024]{1,0:T(8,128)(2,1)S(1)} %get-tuple-element.18.refs_0_), channel_id=1, source_target_pairs={{0,1},{1,2},{2,3},{4,5},{5,6},{6,7},{8,9},{9,10},{10,11},{12,13},{... | collective-permute-start | bytes 786440 | tf_op jit(solution)/shard_map/ppermute | solution.py:38
  52.3 11.0 %collective-permute-start.30 = (bf16[128,1024]{1,0:T(8,128)(2,1)S(1)}, bf16[128,1024]{1,0:T(8,128)(2,1)}, u32[]{:S(2)}, u32[]{:S(2)}) collective-permute-start(bf16[128,1024]{1,0:T(8,128)(2,1)S(1)} %get-tuple-element.18.refs_0_), channel_id=1, source_target_pairs={{1,0},{2,1},{3,2},{5,4},{6,5},{7,6},{9,8},{10,9},{11,10},{13,12},{... | collective-permute-start | bytes 786440 | tf_op jit(solution)/shard_map/ppermute | solution.py:39
  53.6 11.0 %collective-permute-start.8 = (bf16[128,1024]{1,0:T(8,128)(2,1)}, bf16[128,1024]{1,0:T(8,128)(2,1)}, u32[]{:S(2)}, u32[]{:S(2)}) collective-permute-start(bf16[128,1024]{1,0:T(8,128)(2,1)} %collective-permute-done.6.refs_1_), channel_id=1, source_target_pairs={{1,2},{2,3},{5,6},{6,7},{9,10},{10,11},{13,14},{14,15},{17,18},{18... | collective-permute-start | bytes 786440 | tf_op jit(solution)/shard_map/ppermute | solution.py:38
  56.8 11.0 %collective-permute-start.9 = (bf16[128,1024]{1,0:T(8,128)(2,1)}, bf16[128,1024]{1,0:T(8,128)(2,1)}, u32[]{:S(2)}, u32[]{:S(2)}) collective-permute-start(bf16[128,1024]{1,0:T(8,128)(2,1)} %collective-permute-done.7.refs_2_), channel_id=1, source_target_pairs={{1,0},{2,1},{5,4},{6,5},{9,8},{10,9},{13,12},{14,13},{17,16},{18,1... | collective-permute-start | bytes 786440 | tf_op jit(solution)/shard_map/ppermute | solution.py:39
  61.4 29.6 %collective-permute-start.31 = (bf16[128,1024]{1,0:T(8,128)(2,1)S(1)}, bf16[128,1024]{1,0:T(8,128)(2,1)}, u32[]{:S(2)}, u32[]{:S(2)}) collective-permute-start(bf16[128,1024]{1,0:T(8,128)(2,1)S(1)} %collective-permute-done.29.refs_1_), channel_id=1, source_target_pairs={{1,2},{2,3},{5,6},{6,7},{9,10},{10,11},{13,14},{14,15},{17,18},{18... | collective-permute-start | bytes 786440 | tf_op jit(solution)/shard_map/ppermute | solution.py:38
  63.3 28.4 %collective-permute-start.32 = (bf16[128,1024]{1,0:T(8,128)(2,1)}, bf16[128,1024]{1,0:T(8,128)(2,1)}, u32[]{:S(2)}, u32[]{:S(2)}) collective-permute-start(bf16[128,1024]{1,0:T(8,128)(2,1)} %collective-permute-done.30.refs_2_), channel_id=1, source_target_pairs={{1,0},{2,1},{5,4},{6,5},{9,8},{10,9},{13,12},{14,13},{17,16},{18,1... | collective-permute-start | bytes 786440 | tf_op jit(solution)/shard_map/ppermute | solution.py:39
  64.6 28.4 %collective-permute-start.10 = (bf16[128,1024]{1,0:T(8,128)(2,1)}, bf16[128,1024]{1,0:T(8,128)(2,1)}, u32[]{:S(2)}, u32[]{:S(2)}) collective-permute-start(bf16[128,1024]{1,0:T(8,128)(2,1)} %collective-permute-done.8.refs_3_), channel_id=1, source_target_pairs={{2,3},{6,7},{10,11},{14,15},{18,19},{22,23},{26,27},{30,31}} | collective-permute-start | bytes 786440 | tf_op jit(solution)/shard_map/ppermute | solution.py:38
  67.8 25.2 %collective-permute-start.11 = (bf16[128,1024]{1,0:T(8,128)(2,1)}, bf16[128,1024]{1,0:T(8,128)(2,1)}, u32[]{:S(2)}, u32[]{:S(2)}) collective-permute-start(bf16[128,1024]{1,0:T(8,128)(2,1)} %collective-permute-done.9.refs_4_), channel_id=1, source_target_pairs={{1,0},{5,4},{9,8},{13,12},{17,16},{21,20},{25,24},{29,28}} | collective-permute-start | bytes 786440 | tf_op jit(solution)/shard_map/ppermute | solution.py:39
  78.4 34.3 %all-to-all-start = ((bf16[8,64,384]{2,1,0:T(8,128)(2,1)}), bf16[8,64,384]{2,1,0:T(8,128)(2,1)S(1)}, u32[]{:S(2)}, u32[]{:S(2)}) async-start(bf16[8,64,384]{2,1,0:T(8,128)(2,1)} %shard_map.74), calls=%async_computation | async-start | bytes 786432 | tf_op jit(solution)/shard_map/all_to_all | solution.py:399
  91.0 25.8 %collective-permute-start.33 = (bf16[128,1024]{1,0:T(8,128)(2,1)}, bf16[128,1024]{1,0:T(8,128)(2,1)S(1)}, u32[]{:S(2)}, u32[]{:S(2)}) collective-permute-start(bf16[128,1024]{1,0:T(8,128)(2,1)} %collective-permute-done.31.refs_3_), channel_id=1, source_target_pairs={{2,3},{6,7},{10,11},{14,15},{18,19},{22,23},{26,27},{30,31}} | collective-permute-start | bytes 786440 | tf_op jit(solution)/shard_map/ppermute | solution.py:38
  91.7 25.1 %collective-permute-start.34 = (bf16[128,1024]{1,0:T(8,128)(2,1)}, bf16[128,1024]{1,0:T(8,128)(2,1)S(1)}, u32[]{:S(2)}, u32[]{:S(2)}) collective-permute-start(bf16[128,1024]{1,0:T(8,128)(2,1)} %collective-permute-done.32.refs_4_), channel_id=1, source_target_pairs={{1,0},{5,4},{9,8},{13,12},{17,16},{21,20},{25,24},{29,28}} | collective-permute-start | bytes 786440 | tf_op jit(solution)/shard_map/ppermute | solution.py:39
  102.2 33.2 %collective-permute-start.14 = (bf16[128,512]{1,0:T(8,128)(2,1)}, bf16[128,512]{1,0:T(8,128)(2,1)S(1)}, u32[]{:S(2)}, u32[]{:S(2)}) collective-permute-start(bf16[128,512]{1,0:T(8,128)(2,1)} %get-tuple-element.17), channel_id=1, source_target_pairs={{0,3},{1,0},{2,1},{3,2},{4,7},{5,4},{6,5},{7,6},{8,11},{9,8},{10,9... | collective-permute-start | bytes 393224 | tf_op jit(solution)/shard_map/ppermute | solution.py:350
  103.7 30.1 %collective-permute-start.13 = (bf16[128,512]{1,0:T(8,128)(2,1)}, bf16[128,512]{1,0:T(8,128)(2,1)}, u32[]{:S(2)}, u32[]{:S(2)}) collective-permute-start(bf16[128,512]{1,0:T(8,128)(2,1)} %get-tuple-element.16), channel_id=1, source_target_pairs={{0,2},{1,3},{2,0},{3,1},{4,6},{5,7},{6,4},{7,5},{8,10},{9,11},{10,... | collective-permute-start | bytes 393224 | tf_op jit(solution)/shard_map/ppermute | solution.py:350
  110.1 17.3 %collective-permute-start.12 = (bf16[128,512]{1,0:T(8,128)(2,1)}, bf16[128,512]{1,0:T(8,128)(2,1)S(1)}, u32[]{:S(2)}, u32[]{:S(2)}) collective-permute-start(bf16[128,512]{1,0:T(8,128)(2,1)} %get-tuple-element.15), channel_id=1, source_target_pairs={{0,1},{1,2},{2,3},{3,0},{4,5},{5,6},{6,7},{7,4},{8,9},{9,10},{10,1... | collective-permute-start | bytes 393224 | tf_op jit(solution)/shard_map/ppermute | solution.py:350
  112.7 16.9 %all-to-all-start.1 = ((bf16[8,64,384]{2,1,0:T(8,128)(2,1)}), bf16[8,64,384]{2,1,0:T(8,128)(2,1)}, u32[]{:S(2)}, u32[]{:S(2)}) async-start(bf16[8,64,384]{2,1,0:T(8,128)(2,1)} %shard_map.75), calls=%async_computation.1 | async-start | bytes 786432 | tf_op jit(solution)/shard_map/all_to_all | solution.py:399
  129.6 12.6 %all-to-all-start.2 = ((bf16[8,64,384]{2,1,0:T(8,128)(2,1)}), bf16[8,64,384]{2,1,0:T(8,128)(2,1)}, u32[]{:S(2)}, u32[]{:S(2)}) async-start(bf16[8,64,384]{2,1,0:T(8,128)(2,1)} %shard_map.76), calls=%async_computation.2 | async-start | bytes 786432 | tf_op jit(solution)/shard_map/all_to_all | solution.py:399
  142.2 12.9 %all-to-all-start.3 = ((bf16[8,64,384]{2,1,0:T(8,128)(2,1)}), bf16[8,64,384]{2,1,0:T(8,128)(2,1)}, u32[]{:S(2)}, u32[]{:S(2)}) async-start(bf16[8,64,384]{2,1,0:T(8,128)(2,1)} %shard_map.73), calls=%async_computation.3 | async-start | bytes 786432 | tf_op jit(solution)/shard_map/all_to_all | solution.py:399
  146.5 12.7 %collective-permute-start.15 = (bf16[512,256]{1,0:T(8,128)(2,1)S(1)}, bf16[512,256]{1,0:T(8,128)(2,1)S(1)}, u32[]{:S(2)}, u32[]{:S(2)}) collective-permute-start(bf16[512,256]{1,0:T(8,128)(2,1)S(1)} %pad_maximum_fusion), channel_id=1, source_target_pairs={{0,8},{4,12},{8,0},{12,4},{16,24},{20,28},{24,16},{28,20},{1,9},{5... | collective-permute-start | bytes 786440 | tf_op jit(solution)/shard_map/ppermute | solution.py:362
  148.3 13.9 %collective-permute-start.27 = (bf16[8,64,384]{2,1,0:T(8,128)(2,1)S(1)}, bf16[8,64,384]{2,1,0:T(8,128)(2,1)}, u32[]{:S(2)}, u32[]{:S(2)}) collective-permute-start(bf16[8,64,384]{2,1,0:T(8,128)(2,1)S(1)} %all-to-all-done.refs_0_), channel_id=1, source_target_pairs={{0,4},{4,0},{8,12},{12,8},{16,20},{20,16},{24,28},{28,24},{1,5},{5... | collective-permute-start | bytes 1179656 | tf_op jit(solution)/shard_map/ppermute | solution.py:403
  149.1 11.0 %collective-permute-start.17 = (bf16[512,256]{1,0:T(8,128)(2,1)}, bf16[512,256]{1,0:T(8,128)(2,1)S(1)}, u32[]{:S(2)}, u32[]{:S(2)}) collective-permute-start(bf16[512,256]{1,0:T(8,128)(2,1)} %pad_maximum_fusion.1), channel_id=1, source_target_pairs={{0,16},{4,20},{8,24},{12,28},{16,0},{20,4},{24,8},{28,12},{1,17},{... | collective-permute-start | bytes 786440 | tf_op jit(solution)/shard_map/ppermute | solution.py:362
  150.5 12.2 %collective-permute-start.28 = (bf16[8,64,384]{2,1,0:T(8,128)(2,1)}, bf16[8,64,384]{2,1,0:T(8,128)(2,1)}, u32[]{:S(2)}, u32[]{:S(2)}) collective-permute-start(bf16[8,64,384]{2,1,0:T(8,128)(2,1)} %all-to-all-done.1.refs_2_), channel_id=1, source_target_pairs={{0,4},{4,0},{8,12},{12,8},{16,20},{20,16},{24,28},{28,24},{1,5},{5... | collective-permute-start | bytes 1179656 | tf_op jit(solution)/shard_map/ppermute | solution.py:403
  150.8 12.0 %collective-permute-start.35 = (bf16[8,64,384]{2,1,0:T(8,128)(2,1)}, bf16[8,64,384]{2,1,0:T(8,128)(2,1)}, u32[]{:S(2)}, u32[]{:S(2)}) collective-permute-start(bf16[8,64,384]{2,1,0:T(8,128)(2,1)} %all-to-all-done.2.refs_4_), channel_id=1, source_target_pairs={{0,4},{4,0},{8,12},{12,8},{16,20},{20,16},{24,28},{28,24},{1,5},{5... | collective-permute-start | bytes 1179656 | tf_op jit(solution)/shard_map/ppermute | solution.py:403
  159.3 3.5 %collective-permute-start.36 = (bf16[8,64,384]{2,1,0:T(8,128)(2,1)}, bf16[8,64,384]{2,1,0:T(8,128)(2,1)S(1)}, u32[]{:S(2)}, u32[]{:S(2)}) collective-permute-start(bf16[8,64,384]{2,1,0:T(8,128)(2,1)} %all-to-all-done.3.refs_6_), channel_id=1, source_target_pairs={{0,4},{4,0},{8,12},{12,8},{16,20},{20,16},{24,28},{28,24},{1,5},{5... | collective-permute-start | bytes 1179656 | tf_op jit(solution)/shard_map/ppermute | solution.py:403
  160.0 18.3 %collective-permute-start.16 = (bf16[1024,256]{1,0:T(8,128)(2,1)}, bf16[1024,256]{1,0:T(8,128)(2,1)S(1)}, u32[]{:S(2)}, u32[]{:S(2)}) collective-permute-start(bf16[1024,256]{1,0:T(8,128)(2,1)} %get-tuple-element.29), channel_id=1, source_target_pairs={{0,16},{4,20},{8,24},{12,28},{16,0},{20,4},{24,8},{28,12},{1,17},{... | collective-permute-start | bytes 1572872 | tf_op jit(solution)/shard_map/ppermute | solution.py:362
  162.2 27.1 %collective-permute-start.18 = (bf16[1024,256]{1,0:T(8,128)(2,1)}, bf16[1024,256]{1,0:T(8,128)(2,1)}, u32[]{:S(2)}, u32[]{:S(2)}) collective-permute-start(bf16[1024,256]{1,0:T(8,128)(2,1)} %constant_dynamic-update-slice_fusion.11), channel_id=1, source_target_pairs={{0,8},{4,12},{8,0},{12,4},{16,24},{20,28},{24,16},{28,20},{1,9},{5... | collective-permute-start | bytes 1572872 | tf_op jit(solution)/shard_map/ppermute | solution.py:362
  163.5 65.0 %copy-start.26 = (s32[512]{0:T(512)S(1)}, s32[512]{0:T(512)}, u32[]{:S(2)}) copy-start(s32[512]{0:T(512)} %param.8) | copy-start | bytes 6148
  174.2 11.0 %all-to-all-start.4 = ((bf16[8,128,128]{2,1,0:T(8,128)(2,1)}), bf16[8,128,128]{2,1,0:T(8,128)(2,1)}, u32[]{:S(2)}, u32[]{:S(2)}) async-start(bf16[8,128,128]{2,1,0:T(8,128)(2,1)} %get-tuple-element.19), calls=%async_computation.4 | async-start | bytes 524288 | tf_op jit(solution)/shard_map/all_to_all | solution.py:408
  178.3 57.4 %copy-start = (bf16[2048,256]{1,0:T(8,128)(2,1)}, bf16[2048,256]{1,0:T(8,128)(2,1)S(1)}, u32[]{:S(2)}) copy-start(bf16[2048,256]{1,0:T(8,128)(2,1)S(1)} %constant_dynamic-update-slice_fusion.5.refs_0_) | copy-start | bytes 3145732
  178.4 57.4 %collective-permute-start.19 = (bf16[2048,256]{1,0:T(8,128)(2,1)S(1)}, bf16[2048,256]{1,0:T(8,128)(2,1)S(1)}, u32[]{:S(2)}, u32[]{:S(2)}) collective-permute-start(bf16[2048,256]{1,0:T(8,128)(2,1)S(1)} %constant_dynamic-update-slice_fusion.5.refs_0_), channel_id=1, source_target_pairs={{0,4},{4,0},{8,12},{12,8},{16,20},{20,16},{24,28},{28,24},{1,5},{5... | collective-permute-start | bytes 3145736 | tf_op jit(solution)/shard_map/ppermute | solution.py:370
  185.2 11.0 %all-to-all-start.5 = ((bf16[8,128,128]{2,1,0:T(8,128)(2,1)}), bf16[8,128,128]{2,1,0:T(8,128)(2,1)}, u32[]{:S(2)}, u32[]{:S(2)}) async-start(bf16[8,128,128]{2,1,0:T(8,128)(2,1)} %get-tuple-element.20), calls=%async_computation.5 | async-start | bytes 524288 | tf_op jit(solution)/shard_map/all_to_all | solution.py:408
  190.3 9.6 %collective-permute-start.37 = (bf16[8,128,128]{2,1,0:T(8,128)(2,1)}, bf16[8,128,128]{2,1,0:T(8,128)(2,1)S(1)}, u32[]{:S(2)}, u32[]{:S(2)}) collective-permute-start(bf16[8,128,128]{2,1,0:T(8,128)(2,1)} %all-to-all-done.4.refs_4_), channel_id=1, source_target_pairs={{0,1},{1,2},{2,3},{4,5},{5,6},{6,7},{8,9},{9,10},{10,11},{12,13},{... | collective-permute-start | bytes 786440 | tf_op jit(solution)/shard_map/ppermute | solution.py:38
  192.3 10.5 %collective-permute-start.38 = (bf16[8,128,128]{2,1,0:T(8,128)(2,1)}, bf16[8,128,128]{2,1,0:T(8,128)(2,1)}, u32[]{:S(2)}, u32[]{:S(2)}) collective-permute-start(bf16[8,128,128]{2,1,0:T(8,128)(2,1)} %all-to-all-done.4.refs_4_), channel_id=1, source_target_pairs={{1,0},{2,1},{3,2},{5,4},{6,5},{7,6},{9,8},{10,9},{11,10},{13,12},{... | collective-permute-start | bytes 786440 | tf_op jit(solution)/shard_map/ppermute | solution.py:39
  196.2 8.0 %collective-permute-start.43 = (bf16[8,128,128]{2,1,0:T(8,128)(2,1)}, bf16[8,128,128]{2,1,0:T(8,128)(2,1)}, u32[]{:S(2)}, u32[]{:S(2)}) collective-permute-start(bf16[8,128,128]{2,1,0:T(8,128)(2,1)} %all-to-all-done.5.refs_11_), channel_id=1, source_target_pairs={{0,1},{1,2},{2,3},{4,5},{5,6},{6,7},{8,9},{9,10},{10,11},{12,13},{... | collective-permute-start | bytes 786440 | tf_op jit(solution)/shard_map/ppermute | solution.py:38
  199.8 35.9 %collective-permute-start.20 = (bf16[2048,256]{1,0:T(8,128)(2,1)S(1)}, bf16[2048,256]{1,0:T(8,128)(2,1)}, u32[]{:S(2)}, u32[]{:S(2)}) collective-permute-start(bf16[2048,256]{1,0:T(8,128)(2,1)S(1)} %slice_dynamic-update-slice_fusion.refs_1_), channel_id=1, source_target_pairs={{0,4},{4,0},{8,12},{12,8},{16,20},{20,16},{24,28},{28,24},{1,5},{5... | collective-permute-start | bytes 3145736 | tf_op jit(solution)/shard_map/ppermute | solution.py:370
  199.9 10.9 %collective-permute-start.44 = (bf16[8,128,128]{2,1,0:T(8,128)(2,1)}, bf16[8,128,128]{2,1,0:T(8,128)(2,1)}, u32[]{:S(2)}, u32[]{:S(2)}) collective-permute-start(bf16[8,128,128]{2,1,0:T(8,128)(2,1)} %all-to-all-done.5.refs_11_), channel_id=1, source_target_pairs={{1,0},{2,1},{3,2},{5,4},{6,5},{7,6},{9,8},{10,9},{11,10},{13,12},{... | collective-permute-start | bytes 786440 | tf_op jit(solution)/shard_map/ppermute | solution.py:39
  202.8 9.5 %collective-permute-start.39 = (bf16[8,128,128]{2,1,0:T(8,128)(2,1)S(1)}, bf16[8,128,128]{2,1,0:T(8,128)(2,1)}, u32[]{:S(2)}, u32[]{:S(2)}) collective-permute-start(bf16[8,128,128]{2,1,0:T(8,128)(2,1)S(1)} %collective-permute-done.37.refs_5_), channel_id=1, source_target_pairs={{1,2},{2,3},{5,6},{6,7},{9,10},{10,11},{13,14},{14,15},{17,18},{18... | collective-permute-start | bytes 786440 | tf_op jit(solution)/shard_map/ppermute | solution.py:38
  204.2 12.2 %collective-permute-start.40 = (bf16[8,128,128]{2,1,0:T(8,128)(2,1)}, bf16[8,128,128]{2,1,0:T(8,128)(2,1)}, u32[]{:S(2)}, u32[]{:S(2)}) collective-permute-start(bf16[8,128,128]{2,1,0:T(8,128)(2,1)} %collective-permute-done.38.refs_6_), channel_id=1, source_target_pairs={{1,0},{2,1},{5,4},{6,5},{9,8},{10,9},{13,12},{14,13},{17,16},{18,1... | collective-permute-start | bytes 786440 | tf_op jit(solution)/shard_map/ppermute | solution.py:39
  210.9 6.9 %collective-permute-start.45 = (bf16[8,128,128]{2,1,0:T(8,128)(2,1)}, bf16[8,128,128]{2,1,0:T(8,128)(2,1)}, u32[]{:S(2)}, u32[]{:S(2)}) collective-permute-start(bf16[8,128,128]{2,1,0:T(8,128)(2,1)} %collective-permute-done.43.refs_12_), channel_id=1, source_target_pairs={{1,2},{2,3},{5,6},{6,7},{9,10},{10,11},{13,14},{14,15},{17,18},{18... | collective-permute-start | bytes 786440 | tf_op jit(solution)/shard_map/ppermute | solution.py:38
  212.3 13.5 %collective-permute-start.46 = (bf16[8,128,128]{2,1,0:T(8,128)(2,1)}, bf16[8,128,128]{2,1,0:T(8,128)(2,1)}, u32[]{:S(2)}, u32[]{:S(2)}) collective-permute-start(bf16[8,128,128]{2,1,0:T(8,128)(2,1)} %collective-permute-done.44.refs_13_), channel_id=1, source_target_pairs={{1,0},{2,1},{5,4},{6,5},{9,8},{10,9},{13,12},{14,13},{17,16},{18,1... | collective-permute-start | bytes 786440 | tf_op jit(solution)/shard_map/ppermute | solution.py:39
  216.4 10.7 %collective-permute-start.41 = (bf16[8,128,128]{2,1,0:T(8,128)(2,1)}, bf16[8,128,128]{2,1,0:T(8,128)(2,1)}, u32[]{:S(2)}, u32[]{:S(2)}) collective-permute-start(bf16[8,128,128]{2,1,0:T(8,128)(2,1)} %collective-permute-done.39.refs_7_), channel_id=1, source_target_pairs={{2,3},{6,7},{10,11},{14,15},{18,19},{22,23},{26,27},{30,31}} | collective-permute-start | bytes 786440 | tf_op jit(solution)/shard_map/ppermute | solution.py:38
  217.8 12.9 %collective-permute-start.42 = (bf16[8,128,128]{2,1,0:T(8,128)(2,1)}, bf16[8,128,128]{2,1,0:T(8,128)(2,1)}, u32[]{:S(2)}, u32[]{:S(2)}) collective-permute-start(bf16[8,128,128]{2,1,0:T(8,128)(2,1)} %collective-permute-done.40.refs_8_), channel_id=1, source_target_pairs={{1,0},{5,4},{9,8},{13,12},{17,16},{21,20},{25,24},{29,28}} | collective-permute-start | bytes 786440 | tf_op jit(solution)/shard_map/ppermute | solution.py:39
  225.8 4.9 %collective-permute-start.47 = (bf16[8,128,128]{2,1,0:T(8,128)(2,1)}, bf16[8,128,128]{2,1,0:T(8,128)(2,1)}, u32[]{:S(2)}, u32[]{:S(2)}) collective-permute-start(bf16[8,128,128]{2,1,0:T(8,128)(2,1)} %collective-permute-done.45.refs_14_), channel_id=1, source_target_pairs={{2,3},{6,7},{10,11},{14,15},{18,19},{22,23},{26,27},{30,31}} | collective-permute-start | bytes 786440 | tf_op jit(solution)/shard_map/ppermute | solution.py:38
  227.2 8.6 %collective-permute-start.48 = (bf16[8,128,128]{2,1,0:T(8,128)(2,1)}, bf16[8,128,128]{2,1,0:T(8,128)(2,1)}, u32[]{:S(2)}, u32[]{:S(2)}) collective-permute-start(bf16[8,128,128]{2,1,0:T(8,128)(2,1)} %collective-permute-done.46.refs_15_), channel_id=1, source_target_pairs={{1,0},{5,4},{9,8},{13,12},{17,16},{21,20},{25,24},{29,28}} | collective-permute-start | bytes 786440 | tf_op jit(solution)/shard_map/ppermute | solution.py:39
  (19 other events, 390.3 us)

commit v4 on v3

v4 whole, which is shorter than its diff:
```python
import math
from functools import partial

import jax
import jax.numpy as jnp
from jax import lax
from jax.experimental import pallas as pl
from jax.experimental.pallas import tpu as pltpu
from jax.sharding import PartitionSpec as P

HEAD = 128
MASKED = -1e30
ASIDE = 2.0**100
LIMIT = 60 * 2**20


def sources(me, count):
    found = [(me, None)]
    for step in range(count - 1):
        found.append((me - 1 - step, me - 1 - step >= 0))
        found.append((me + 1 + step, me + 1 + step < count))
    return found


def line_gather(chunks, count, between=None):
    right = [(d, d + 1) for d in range(count - 1)]
    left = [(d + 1, d) for d in range(count - 1)]
    found, made = [], None
    for first in range(0, len(chunks), 2):
        pair = []
        for chunk in chunks[first : first + 2]:
            if first:
                chunk, _ = lax.optimization_barrier((chunk, found[first - 2 + len(pair)]))
            pair.append([chunk])
        last = [(chunk[0], chunk[0]) for chunk in pair]
        for step in range(count - 1):
            for at in range(len(pair)):
                if step == 1 and at == 0 and made is not None:
                    last[at], _ = lax.optimization_barrier((last[at], made))
                from_left = lax.ppermute(last[at][0], "tensor", right[step:])
                from_right = lax.ppermute(last[at][1], "tensor", left[: count - 1 - step])
                last[at] = (from_left, from_right)
                pair[at] += [from_left, from_right]
        found += pair
        if between is not None and first + 2 < len(chunks):
            made = between(pair)
    return found


def project_kernel(group, count, me_ref, gain_ref, active_ref, *refs):
    matrices = refs[:3]
    pieces = refs[3:-4]
    out_ref, normed, held, arrived = refs[-4:]
    block = held.shape[3]
    blocks = matrices[0].shape[1] // block
    copies = [
        pltpu.make_async_copy(
            matrix.at[:, at * block : (at + 1) * block], held.at[at, which], arrived.at[at, which]
        )
        for at in range(blocks)
        for which, matrix in enumerate(matrices)
    ]
    for copy in copies:
        copy.start()
    found = sources(me_ref[0], count)
    chunk_rows, width = pieces[0].shape
    chunks = len(pieces) // len(found)
    rows = chunks * chunk_rows

    for number, piece in enumerate(pieces):
        first, (source, there) = number // len(found) * chunk_rows, found[number % len(found)]

        def place(first=first, piece=piece, source=source):
            normed[source, first : first + chunk_rows, :] = piece[...]

        if there is None:
            place()
        else:
            pl.when(there)(place)

    square = jnp.zeros((rows, 1), jnp.float32)
    for source in range(count):
        values = normed[source].astype(jnp.float32)
        square = square + jnp.sum(values * values, axis=1, keepdims=True)
    row_scale = lax.rsqrt(square / (count * width) + 1e-05)
    x = jnp.concatenate(
        [
            (normed[source].astype(jnp.float32) * row_scale * gain_ref[source : source + 1, :]).astype(
                jnp.bfloat16
            )
            for source in range(count)
        ],
        axis=1,
    )
    part_rows = chunk_rows // group
    for at in range(blocks):
        for which in range(3):
            copies[at * 3 + which].wait()
            total = jnp.dot(x, held[at, which], preferred_element_type=jnp.float32)
            if which == 0:
                total = jnp.where(active_ref[...] > 0, total, ASIDE)
            total = total.astype(jnp.bfloat16)
            for inner in range(block // HEAD):
                head = at * (block // HEAD) + inner
                for part in range(group):
                    for chunk in range(chunks):
                        first = chunk * chunk_rows + part * part_rows
                        out_ref[
                            head * group + part,
                            chunk * part_rows : (chunk + 1) * part_rows,
                            which * HEAD : (which + 1) * HEAD,
                        ] = total[first : first + part_rows, inner * HEAD : (inner + 1) * HEAD]


def project(me, pieces, active, gain, wq, wk, wv, seq_count, group):
    columns = pieces[0].shape[1]
    rows = active.shape[0]
    features, width = wq.shape
    count = features // columns
    block = min(256, width)
    vmem = pl.BlockSpec(memory_space=pltpu.VMEM)
    return pl.pallas_call(
        partial(project_kernel, group, count),
        in_specs=[pl.BlockSpec(memory_space=pltpu.SMEM), vmem, vmem]
        + [pl.BlockSpec(memory_space=pl.ANY)] * 3
        + [vmem] * len(pieces),
        out_specs=vmem,
        out_shape=jax.ShapeDtypeStruct((seq_count, rows // group, 3 * HEAD), jnp.bfloat16),
        scratch_shapes=[
            pltpu.VMEM((count, rows, columns), jnp.bfloat16),
            pltpu.VMEM((width // block, 3, features, block), jnp.bfloat16),
            pltpu.SemaphoreType.DMA((width // block, 3)),
        ],
        compiler_params=pltpu.CompilerParams(vmem_limit_bytes=LIMIT),
        cost_estimate=pl.CostEstimate(
            flops=6 * rows * features * width,
            bytes_accessed=6 * features * width + 2 * rows * (features + 3 * width),
            transcendentals=0,
        ),
    )(me, gain, active, wq, wk, wv, *pieces)


def attend_kernel(chunks, group, rows, part_ref, *refs):
    pieces = refs[:-3]
    out_ref, keys, values = refs[-3:]
    seq_count = pieces[0].shape[0]
    chunk_rows = rows // chunks
    part_rows = chunk_rows // group
    part = part_ref[0]

    def place(home, _):
        chunk = 0
        for number in range(0, len(pieces), group):
            inside = pieces[number].shape[1] // part_rows
            for step in range(group):
                owner = lax.rem(part + step, group)
                piece = pieces[number + step]
                for at_chunk in range(inside):
                    at = home * rows + (chunk + at_chunk) * chunk_rows + owner * part_rows
                    to = pl.ds(pl.multiple_of(at, part_rows), part_rows)
                    of = slice(at_chunk * part_rows, (at_chunk + 1) * part_rows)
                    aside = piece[home, of, :HEAD].astype(jnp.float32) >= ASIDE
                    keys[to, :HEAD] = piece[home, of, HEAD : 2 * HEAD]
                    keys[to, HEAD:] = jnp.where(aside, MASKED, 0.0).astype(jnp.bfloat16)
                    values[to, :] = piece[home, of, 2 * HEAD :]
            chunk += inside
        return 0

    lax.fori_loop(0, seq_count, place, 0)
    scale = math.log2(math.e) / math.sqrt(HEAD)
    count = chunks * part_rows
    first_lane = lax.broadcasted_iota(jnp.int32, (count, HEAD), 1) == 0
    mask_lane = jnp.where(first_lane, 1.0, 0.0).astype(jnp.bfloat16)
    order = lax.broadcasted_iota(jnp.int32, (count, rows), 0)
    own = order // part_rows * chunk_rows + part * part_rows + order % part_rows
    later = lax.broadcasted_iota(jnp.int32, (count, rows), 1) > own

    def queries_of(home):
        queries = jnp.concatenate(
            [pieces[number][home, :, :HEAD] for number in range(0, len(pieces), group)], axis=0
        )
        return jnp.concatenate([queries, mask_lane], axis=1)

    def scores_of(queries, at):
        return scale * lax.dot_general(
            queries,
            keys[at, :],
            (((1,), (1,)), ((), ())),
            preferred_element_type=jnp.float32,
        )

    if seq_count <= 8:
        for home in range(seq_count):
            queries = queries_of(home)
            blocks = []
            for other in range(home + 1):
                scores = scores_of(queries, slice(other * rows, (other + 1) * rows))
                if other == home:
                    scores = jnp.where(later, MASKED, scores)
                blocks.append(scores)
            scores = jnp.concatenate(blocks, axis=1)
            best = jnp.max(scores, axis=1, keepdims=True)
            weights = jnp.exp2(scores - best)
            total = jnp.sum(weights, axis=1, keepdims=True)
            summed = jnp.dot(
                weights.astype(jnp.bfloat16),
                values[: (home + 1) * rows, :],
                preferred_element_type=jnp.float32,
            )
            out_ref[home] = (summed / total).astype(jnp.bfloat16)
        return

    def one_home(home, _):
        queries = queries_of(home)

        def fold(other, carry, diagonal):
            best, total, summed = carry
            at = pl.ds(pl.multiple_of(other * rows, rows), rows)
            scores = scores_of(queries, at)
            if diagonal:
                scores = jnp.where(later, MASKED, scores)
            newbest = jnp.maximum(best, jnp.max(scores, axis=1, keepdims=True))
            factor = jnp.exp2(best - newbest)
            weights = jnp.exp2(scores - newbest)
            total = total * factor + jnp.sum(weights, axis=1, keepdims=True)
            summed = summed * factor + jnp.dot(
                weights.astype(jnp.bfloat16), values[at, :], preferred_element_type=jnp.float32
            )
            return newbest, total, summed

        start = (
            jnp.full((count, 1), MASKED, jnp.float32),
            jnp.zeros((count, 1), jnp.float32),
            jnp.zeros((count, HEAD), jnp.float32),
        )
        carry = fold(home, start, True)
        carry = lax.fori_loop(0, home, lambda other, c: fold(other, c, False), carry)
        _, total, summed = carry
        out_ref[home] = (summed / total).astype(jnp.bfloat16)
        return 0

    lax.fori_loop(0, seq_count, one_home, 0)


def attend(part, pieces, chunks, group, rows):
    seq_count = pieces[0].shape[0]
    count = rows // group
    vmem = pl.BlockSpec(memory_space=pltpu.VMEM)
    pairs = seq_count * (seq_count + 1) // 2
    return pl.pallas_call(
        partial(attend_kernel, chunks, group, rows),
        in_specs=[pl.BlockSpec(memory_space=pltpu.SMEM)] + [vmem] * len(pieces),
        out_specs=vmem,
        out_shape=jax.ShapeDtypeStruct((seq_count, count, HEAD), jnp.bfloat16),
        scratch_shapes=[
            pltpu.VMEM((seq_count * rows, 2 * HEAD), jnp.bfloat16),
            pltpu.VMEM((seq_count * rows, HEAD), jnp.bfloat16),
        ],
        compiler_params=pltpu.CompilerParams(vmem_limit_bytes=LIMIT),
        cost_estimate=pl.CostEstimate(
            flops=6 * pairs * count * rows * HEAD,
            bytes_accessed=8 * seq_count * rows * HEAD,
            transcendentals=pairs * count * rows,
        ),
    )(part, *pieces)


def output_kernel(chunks, group, count, cuts, halves, me_ref, at_ref, hidden_ref, active_ref, *refs):
    weights = refs[:cuts]
    pieces = refs[cuts:-4]
    out_ref, rows_in, held, arrived = refs[-4:]
    copies = [
        pltpu.make_async_copy(weight, held.at[cut], arrived.at[cut])
        for cut, weight in enumerate(weights)
    ]
    for copy in copies:
        copy.start()
    sent, piece_rows, _ = pieces[0].shape
    heads = sent // group
    part_rows = piece_rows // chunks
    chunk_rows = part_rows * group
    width = weights[0].shape[1]
    found = sources(me_ref[0], count)

    for number, piece in enumerate(pieces):
        half, (source, there) = number // len(found), found[number % len(found)]

        def place(half=half, piece=piece, source=source):
            for head in range(heads):
                at = pl.multiple_of(at_ref[(source * halves + half) * heads + head] * HEAD, HEAD)
                for part in range(group):
                    for chunk in range(chunks):
                        first = chunk * chunk_rows + part * part_rows
                        rows_in[first : first + part_rows, pl.ds(at, HEAD)] = piece[
                            head * group + part, chunk * part_rows : (chunk + 1) * part_rows, :
                        ]

        if there is None:
            place()
        else:
            pl.when(there)(place)

    for cut in range(cuts):
        copies[cut].wait()
        columns = pl.ds(pl.multiple_of(me_ref[1 + cut] * width, width), width)
        shares = jnp.dot(rows_in[...], held[cut], preferred_element_type=jnp.float32)
        hidden = hidden_ref[:, columns]
        renewed = (hidden.astype(jnp.float32) + shares).astype(jnp.bfloat16)
        out_ref[:, columns] = jnp.where(active_ref[...] > 0, renewed, hidden)


def output(scalars, at, pieces, weights, hidden, active, chunks, group, halves):
    rows, columns = hidden.shape
    depth, width = weights[0].shape
    smem = pl.BlockSpec(memory_space=pltpu.SMEM)
    vmem = pl.BlockSpec(memory_space=pltpu.VMEM)
    cuts = len(weights)
    count = (len(pieces) // halves + 1) // 2
    return pl.pallas_call(
        partial(output_kernel, chunks, group, count, cuts, halves),
        in_specs=[smem, smem, vmem, vmem]
        + [pl.BlockSpec(memory_space=pl.ANY)] * cuts
        + [vmem] * len(pieces),
        out_specs=vmem,
        out_shape=jax.ShapeDtypeStruct((rows, columns), jnp.bfloat16),
        scratch_shapes=[
            pltpu.VMEM((rows, depth), jnp.bfloat16),
            pltpu.VMEM((cuts, depth, width), jnp.bfloat16),
            pltpu.SemaphoreType.DMA((cuts,)),
        ],
        compiler_params=pltpu.CompilerParams(vmem_limit_bytes=LIMIT),
        cost_estimate=pl.CostEstimate(
            flops=2 * rows * depth * columns,
            bytes_accessed=2 * (rows * depth + depth * columns + 2 * rows * columns),
            transcendentals=0,
        ),
    )(scalars, at, hidden, active, *weights, *pieces)


def share_kernel(columns, place_ref, w_ref, *refs):
    shares, arrived = refs[:-1], refs[-1]
    copies = []
    for step, share in enumerate(shares):
        to = lax.rem(place_ref[2] + step, len(shares))
        for half in range(share.shape[0]):
            each = share.shape[2]
            first = pl.multiple_of(to * columns + place_ref[1] + half * each, each)
            rows = pl.ds(pl.multiple_of(place_ref[0], HEAD), HEAD)
            copies.append(
                pltpu.make_async_copy(
                    w_ref.at[rows, pl.ds(first, each)], share.at[half], arrived.at[step, half]
                )
            )
    for copy in copies:
        copy.start()
    for copy in copies:
        copy.wait()


def shares_of(w_out, place, count, halves, each):
    columns = w_out.shape[1] // count
    return pl.pallas_call(
        partial(share_kernel, columns),
        in_specs=[pl.BlockSpec(memory_space=pltpu.SMEM), pl.BlockSpec(memory_space=pl.ANY)],
        out_specs=[pl.BlockSpec(memory_space=pl.ANY)] * count,
        out_shape=[jax.ShapeDtypeStruct((halves, HEAD, each), w_out.dtype)] * count,
        scratch_shapes=[pltpu.SemaphoreType.DMA((count, halves))],
        compiler_params=pltpu.CompilerParams(vmem_limit_bytes=LIMIT),
    )(place, w_out)


def output_weight(w_out, seq_count, tensor_count, columns, after, last):
    heads = w_out.shape[0] // HEAD
    cuts = seq_count // heads
    width = columns // cuts
    row = jnp.arange(tensor_count * heads, dtype=jnp.int32)
    if width % HEAD:
        weight = lax.all_to_all(w_out, "tensor", split_axis=1, concat_axis=0, tiled=True)
        return [weight], [jnp.int32(0)], row
    seq_me = lax.axis_index("seq").astype(jnp.int32)
    me = lax.axis_index("tensor").astype(jnp.int32)
    head, cut = seq_me // cuts, seq_me % cuts

    halves = 2 if width % (2 * HEAD) == 0 else 1
    each = width // halves
    shares = shares_of(
        w_out, jnp.stack([head * HEAD, cut * width, me]), tensor_count, halves, each
    )
    shares, _ = lax.optimization_barrier((list(shares), after))
    for step in range(1, tensor_count):
        ring = [(d, (d + step) % tensor_count) for d in range(tensor_count)]
        shares[step] = lax.ppermute(shares[step], "tensor", ring)
    flips = []
    while cuts << len(flips) < seq_count:
        flips.append(cuts << len(flips))
    shares, _ = lax.optimization_barrier((shares, last))
    weights, which = [], []
    for half in range(halves):
        held = {0: jnp.concatenate([share[half] for share in shares], axis=0)}
        for flip in flips if half == 0 else flips[::-1]:
            pairs = [(d, d ^ flip) for d in range(seq_count)]
            sent = list(held)
            got = lax.ppermute(jnp.concatenate([held[k] for k in sent], axis=0), "seq", pairs)
            for k, block in zip(sent, jnp.split(got, len(sent))):
                held[k ^ flip] = block
        weights.append(jnp.concatenate([held[k] for k in sorted(held)], axis=0))
        which.append(cut * halves + half)
    for step in range(1, cuts):
        ring = [(d, d - d % cuts + (d - step) % cuts) for d in range(seq_count)]
        for half in range(halves):
            weights.append(lax.ppermute(weights[half], "seq", ring))
            which.append((cut + step) % cuts * halves + half)
    tensor, of = row // heads, row % heads
    at = (of ^ head) * tensor_count + (me - tensor) % tensor_count
    return weights, which, at


def shards(hidden, depth, norm_gain, w_query, w_key, w_value, w_out):
    rows, columns = hidden.shape
    seq_count = lax.axis_size("seq")
    tensor_count = lax.axis_size("tensor")
    heads = w_query.shape[1] // HEAD
    group = seq_count // heads
    chunks = min(4, rows // (16 * group))
    chunk_rows = rows // chunks
    part = (lax.axis_index("seq") % group).astype(jnp.int32).reshape(1)
    me = lax.axis_index("tensor").astype(jnp.int32)
    gain = norm_gain.reshape(tensor_count, columns)
    active = (depth >= 2).astype(jnp.int32).reshape(rows, 1)
    made = []

    def work(found):
        first = sum(count for count, _ in made)
        here = active[first * chunk_rows : (first + len(found)) * chunk_rows]
        sent = project(
            me.reshape(1), sum(found, []), here, gain, w_query, w_key, w_value, seq_count, group
        )
        made.append((len(found), sent))
        return sent

    gathered = line_gather(
        [hidden[c * chunk_rows : (c + 1) * chunk_rows] for c in range(chunks)], tensor_count, work
    )
    for found in gathered[sum(count for count, _ in made) :]:
        work([found])
    pieces = []
    for _, sent in made:
        got = lax.all_to_all(sent, "seq", split_axis=0, concat_axis=0)
        pieces.append(got)
        for step in range(1, group):
            ring = [(d, d - d % group + (d - step) % group) for d in range(seq_count)]
            pieces.append(lax.ppermute(got, "seq", ring))

    out = attend(part, pieces, chunks, group, rows)
    weights, cut_of, at = output_weight(w_out, seq_count, tensor_count, columns, made[-1][1], out)
    scalars = jnp.stack([me, *cut_of])
    home = lax.all_to_all(out, "seq", split_axis=0, concat_axis=0)
    found = sum(line_gather([home[: seq_count // 2], home[seq_count // 2 :]], tensor_count), [])
    return output(scalars, at, found, weights, hidden, active, chunks, group, 2)


def solution(mesh):
    return jax.shard_map(
        shards,
        mesh=mesh,
        in_specs=(
            P("seq", "tensor"),
            P("seq"),
            P(),
            P(None, "tensor"),
            P(None, "tensor"),
            P(None, "tensor"),
            P("tensor", None),
        ),
        out_specs=P("seq", "tensor"),
        check_vma=False,
    )
```

time: 248 us -> 248 us (level)
  waiting for transfers between devices: 60.4 us -> 74.5 us
  starting transfers between devices: 98.2 us -> 84.8 us
  Pallas kernels: 56.8 us -> 66.6 us
  blocking collectives: 9.04 us -> 0 us
    ppermute x36, waiting for transfers between devices: 38.4 us -> 55.4 us  [the longest x18 52.5 us: line_gather(): from_right = lax.ppermute(last[at][1], 'tensor', left[:count - 1 - step])]
    pallas_call x5, Pallas kernels: 47.2 us -> 57 us  [the longest x3 28 us: project(): pl.pallas_call(partial(project_kernel, group, count), in_specs=[pl.BlockS...]
    all_to_all x2 -> x1, waiting for transfers between devices: 9.12 us -> 0.01 us  [shards(): home = lax.all_to_all(out, 'seq', split_axis=0, concat_axis=0)]
    all_gather x1 -> x0, blocking collectives: 9.04 us -> none  [shards(): depths = lax.all_gather(depth, 'seq', axis=0)]
    ppermute x4, waiting for transfers between devices: 4.12 us -> 11.2 us  [output_weight(): lax.ppermute(jnp.concatenate([held[k] for k in sent], axis=0), 'seq', pairs)]
    ppermute x3, starting transfers between devices: 9.85 us -> 3.86 us  [output_weight(): shares[step] = lax.ppermute(shares[step], 'tensor', ring)]
    all_to_all x2 -> x1, starting transfers between devices: 8.11 us -> 3.71 us  [shards(): home = lax.all_to_all(out, 'seq', split_axis=0, concat_axis=0)]
    all_to_all x4 -> x3, starting transfers between devices: 16 us -> 11.9 us  [shards(): got = lax.all_to_all(sent, 'seq', split_axis=0, concat_axis=0)]
  transfers between devices with their start and end apart: 55 -> 52, of which waited for: 19 -> 18; matrix products, arithmetic and copies ran while one was open for 6% -> 6% of each run, Pallas kernels for 19% -> 23%
where the time goes in v4:
time: 248 us; the launch traced here: 246 us
  starting transfers between devices  84.8 us (34%)
  waiting for transfers between devices  74.5 us (30%)
  Pallas kernels  66.6 us (27%)
  local copies, waits for them, and re-layouts  17.5 us (7%)
    ppermute x18, waiting for transfers between devices, line_gather(): from_right = lax.ppermute(last[at][1], 'tensor', left[:count - 1 - step])  52.5 us
    ppermute x18, starting transfers between devices, line_gather(): from_left = lax.ppermute(last[at][0], 'tensor', right[step:])  35.7 us
    pallas_call x3, Pallas kernels, project(): pl.pallas_call(partial(project_kernel, group, count), in_specs=[pl.BlockS...  28 us
    ppermute x18, starting transfers between devices, line_gather(): from_right = lax.ppermute(last[at][1], 'tensor', left[:count - 1 - step])  23.1 us
    pallas_call x1, Pallas kernels, shares_of(): pl.pallas_call(partial(share_kernel, columns), in_specs=[pl.BlockSpec(mem...  17.7 us
    all_to_all x3, starting transfers between devices, shards(): got = lax.all_to_all(sent, 'seq', split_axis=0, concat_axis=0)  11.9 us
    pallas_call x1, Pallas kernels, attend(): pl.pallas_call(partial(attend_kernel, chunks, group, rows), in_specs=[pl....  11.3 us
    ppermute x4, waiting for transfers between devices, output_weight(): lax.ppermute(jnp.concatenate([held[k] for k in sent], axis=0), 'seq', pairs)  11.2 us
  transfers between devices with their start and end apart: 52, of which 18 were waited for; matrix products, arithmetic and copies ran while one was open for 6% of the time, Pallas kernels for 23%

profile of v4, /device:TPU:0, one launch (start us, length us, event | category | flops | bytes accessed | tf_op | source)
XLA Modules:
  0.0 246.3 jit_solution(14126660165812788218)
XLA Ops:
  0.0 1.3 fusion.5
  1.3 4.9 %collective-permute-start.15 = (bf16[128,1024]{1,0:T(8,128)(2,1)S(1)}, bf16[128,1024]{1,0:T(8,128)(2,1)S(1)}, u32[]{:S(2)}, u32[]{:S(2)}) collective-permute-start(bf16[128,1024]{1,0:T(8,128)(2,1)S(1)} %get-tuple-element.38.refs_3_), channel_id=1, source_target_pairs={{0,1},{1,2},{2,3},{4,5},{5,6},{6,7},{8,9},{9,10},{10,11},{12,13},{... | collective-permute-start | bytes 786440 | tf_op jit(solution)/shard_map/ppermute | solution.py:40
  6.3 1.3 collective-permute-start.16
  7.6 4.6 %collective-permute-start = (bf16[128,1024]{1,0:T(8,128)(2,1)S(1)}, bf16[128,1024]{1,0:T(8,128)(2,1)S(1)}, u32[]{:S(2)}, u32[]{:S(2)}) collective-permute-start(bf16[128,1024]{1,0:T(8,128)(2,1)S(1)} %get-tuple-element.39.refs_10_), channel_id=1, source_target_pairs={{0,1},{1,2},{2,3},{4,5},{5,6},{6,7},{8,9},{9,10},{10,11},{12,13},{... | collective-permute-start | bytes 786440 | tf_op jit(solution)/shard_map/ppermute | solution.py:40
  12.1 1.3 collective-permute-start.1
  14.1 2.0 collective-permute-done.16.refs_5_
  16.2 1.3 collective-permute-start.18
  18.1 4.1 %collective-permute-done.1.refs_12_ = bf16[128,1024]{1,0:T(8,128)(2,1)S(1)} collective-permute-done((bf16[128,1024]{1,0:T(8,128)(2,1)S(1)}, bf16[128,1024]{1,0:T(8,128)(2,1)S(1)}, u32[]{:S(2)}, u32[]{:S(2)}) %collective-permute-start.1) | collective-permute-done | bytes 262176 | tf_op jit(solution)/shard_map/ppermute | solution.py:41
  22.2 1.3 collective-permute-start.3
  24.2 3.9 %collective-permute-done.18.refs_7_ = bf16[128,1024]{1,0:T(8,128)(2,1)S(1)} collective-permute-done((bf16[128,1024]{1,0:T(8,128)(2,1)S(1)}, bf16[128,1024]{1,0:T(8,128)(2,1)S(1)}, u32[]{:S(2)}, u32[]{:S(2)}) %collective-permute-start.18) | collective-permute-done | bytes 262176 | tf_op jit(solution)/shard_map/ppermute | solution.py:41
  28.1 1.3 collective-permute-start.20
  29.4 1.4 collective-permute-start.4
  30.8 3.8 %collective-permute-done.3.refs_14_ = bf16[128,1024]{1,0:T(8,128)(2,1)S(1)} collective-permute-done((bf16[128,1024]{1,0:T(8,128)(2,1)S(1)}, bf16[128,1024]{1,0:T(8,128)(2,1)S(1)}, u32[]{:S(2)}, u32[]{:S(2)}) %collective-permute-start.3) | collective-permute-done | bytes 262176 | tf_op jit(solution)/shard_map/ppermute | solution.py:41
  34.6 1.3 collective-permute-start.5
  37.4 1.3 reshape.16.gain_ref
  38.8 1.6 collective-permute-done.20.refs_9_
  40.4 4.4 %collective-permute-start.22 = (bf16[128,1024]{1,0:T(8,128)(2,1)S(1)}, bf16[128,1024]{1,0:T(8,128)(2,1)}, u32[]{:S(2)}, u32[]{:S(2)}) collective-permute-start(bf16[128,1024]{1,0:T(8,128)(2,1)S(1)} %get-tuple-element.30.refs_3_), channel_id=1, source_target_pairs={{0,1},{1,2},{2,3},{4,5},{5,6},{6,7},{8,9},{9,10},{10,11},{12,13},{... | collective-permute-start | bytes 786440 | tf_op jit(solution)/shard_map/ppermute | solution.py:40
  44.7 1.3 collective-permute-start.23
  46.2 11.9 %shard_map.75 = bf16[8,128,384]{2,1,0:T(8,128)(2,1)} custom-call(s32[1]{0:T(128)} %bitcast.me_ref, f32[4,1024]{1,0:T(4,128)} %reshape.16.gain_ref, s32[256,1]{1,0:T(8,128)} %copy.11.active_ref, bf16[4096,512]{1,0:T(8,128)(2,1)} %refs_0_.5, bf16[4096,512]{1,0:T(8,128)(2,1)} %refs_1_.5, bf16[4096,512]{1,0:T(8,128)(2,1)} %refs_2_.5, ...), custom_call_target="tpu_custom_call" | custom-call | flops 3221225472 | bytes 15466496 | tf_op jit(solution)/shard_map/pallas_call | solution.py:122
  58.1 3.7 %all-to-all-start = ((bf16[8,128,384]{2,1,0:T(8,128)(2,1)}), bf16[8,128,384]{2,1,0:T(8,128)(2,1)S(1)}, u32[]{:S(2)}, u32[]{:S(2)}) async-start(bf16[8,128,384]{2,1,0:T(8,128)(2,1)} %shard_map.75), calls=%async_computation | async-start | bytes 1572864 | tf_op jit(solution)/shard_map/all_to_all | solution.py:448
  61.8 4.5 %collective-permute-start.6 = (bf16[128,1024]{1,0:T(8,128)(2,1)S(1)}, bf16[128,1024]{1,0:T(8,128)(2,1)S(1)}, u32[]{:S(2)}, u32[]{:S(2)}) collective-permute-start(bf16[128,1024]{1,0:T(8,128)(2,1)S(1)} %get-tuple-element.25.refs_3_), channel_id=1, source_target_pairs={{0,1},{1,2},{2,3},{4,5},{5,6},{6,7},{8,9},{9,10},{10,11},{12,13},{... | collective-permute-start | bytes 786440 | tf_op jit(solution)/shard_map/ppermute | solution.py:40
  66.4 1.3 collective-permute-start.7
  68.4 1.3 collective-permute-start.25
  69.7 2.9 %collective-permute-done.6.refs_4_ = bf16[128,1024]{1,0:T(8,128)(2,1)S(1)} collective-permute-done((bf16[128,1024]{1,0:T(8,128)(2,1)S(1)}, bf16[128,1024]{1,0:T(8,128)(2,1)S(1)}, u32[]{:S(2)}, u32[]{:S(2)}) %collective-permute-start.6) | collective-permute-done | bytes 262176 | tf_op jit(solution)/shard_map/ppermute | solution.py:40
  73.3 4.2 %collective-permute-done.7.refs_5_ = bf16[128,1024]{1,0:T(8,128)(2,1)S(1)} collective-permute-done((bf16[128,1024]{1,0:T(8,128)(2,1)S(1)}, bf16[128,1024]{1,0:T(8,128)(2,1)S(1)}, u32[]{:S(2)}, u32[]{:S(2)}) %collective-permute-start.7) | collective-permute-done | bytes 262176 | tf_op jit(solution)/shard_map/ppermute | solution.py:41
  77.4 1.3 collective-permute-start.9
  79.4 3.6 %collective-permute-done.25.refs_7_ = bf16[128,1024]{1,0:T(8,128)(2,1)S(1)} collective-permute-done((bf16[128,1024]{1,0:T(8,128)(2,1)}, bf16[128,1024]{1,0:T(8,128)(2,1)S(1)}, u32[]{:S(2)}, u32[]{:S(2)}) %collective-permute-start.25) | collective-permute-done | bytes 262176 | tf_op jit(solution)/shard_map/ppermute | solution.py:41
  83.1 1.3 collective-permute-start.27
  85.8 2.9 %collective-permute-done.9.refs_7_ = bf16[128,1024]{1,0:T(8,128)(2,1)S(1)} collective-permute-done((bf16[128,1024]{1,0:T(8,128)(2,1)S(1)}, bf16[128,1024]{1,0:T(8,128)(2,1)S(1)}, u32[]{:S(2)}, u32[]{:S(2)}) %collective-permute-start.9) | collective-permute-done | bytes 262176 | tf_op jit(solution)/shard_map/ppermute | solution.py:41
  88.7 1.3 collective-permute-start.11
  90.0 4.3 %collective-permute-done.27.refs_9_ = bf16[128,1024]{1,0:T(8,128)(2,1)S(1)} collective-permute-done((bf16[128,1024]{1,0:T(8,128)(2,1)S(1)}, bf16[128,1024]{1,0:T(8,128)(2,1)S(1)}, u32[]{:S(2)}, u32[]{:S(2)}) %collective-permute-start.27) | collective-permute-done | bytes 262176 | tf_op jit(solution)/shard_map/ppermute | solution.py:41
  95.0 8.0 %shard_map.76 = bf16[8,64,384]{2,1,0:T(8,128)(2,1)} custom-call(s32[1]{0:T(128)} %bitcast.me_ref, f32[4,1024]{1,0:T(4,128)} %reshape.16.gain_ref, s32[128,1]{1,0:T(8,128)} %copy.12.active_ref, bf16[4096,512]{1,0:T(8,128)(2,1)} %refs_0_.5, bf16[4096,512]{1,0:T(8,128)(2,1)} %refs_1_.5, bf16[4096,512]{1,0:T(8,128)(2,1)} %refs_2_.5, ...), custom_call_target="tpu_custom_call" | custom-call | flops 1610612736 | bytes 14024704 | tf_op jit(solution)/shard_map/pallas_call | solution.py:122
  103.1 4.3 %all-to-all-start.1 = ((bf16[8,64,384]{2,1,0:T(8,128)(2,1)}), bf16[8,64,384]{2,1,0:T(8,128)(2,1)S(1)}, u32[]{:S(2)}, u32[]{:S(2)}) async-start(bf16[8,64,384]{2,1,0:T(8,128)(2,1)} %shard_map.76), calls=%async_computation.1 | async-start | bytes 786432 | tf_op jit(solution)/shard_map/all_to_all | solution.py:448
  110.0 8.0 %shard_map.74 = bf16[8,64,384]{2,1,0:T(8,128)(2,1)} custom-call(s32[1]{0:T(128)} %bitcast.me_ref, f32[4,1024]{1,0:T(4,128)} %reshape.16.gain_ref, s32[128,1]{1,0:T(8,128)} %copy.10.active_ref, bf16[4096,512]{1,0:T(8,128)(2,1)} %refs_0_.5, bf16[4096,512]{1,0:T(8,128)(2,1)} %refs_1_.5, bf16[4096,512]{1,0:T(8,128)(2,1)} %refs_2_.5, ...), custom_call_target="tpu_custom_call" | custom-call | flops 1610612736 | bytes 14024704 | tf_op jit(solution)/shard_map/pallas_call | solution.py:122
  118.1 3.9 %all-to-all-start.2 = ((bf16[8,64,384]{2,1,0:T(8,128)(2,1)}), bf16[8,64,384]{2,1,0:T(8,128)(2,1)S(1)}, u32[]{:S(2)}, u32[]{:S(2)}) async-start(bf16[8,64,384]{2,1,0:T(8,128)(2,1)} %shard_map.74), calls=%async_computation.2 | async-start | bytes 786432 | tf_op jit(solution)/shard_map/all_to_all | solution.py:448
  122.4 7.8 %all-to-all-done.2.refs_4_ = bf16[8,64,384]{2,1,0:T(8,128)(2,1)S(1)} async-done(((bf16[8,64,384]{2,1,0:T(8,128)(2,1)}), bf16[8,64,384]{2,1,0:T(8,128)(2,1)S(1)}, u32[]{:S(2)}, u32[]{:S(2)}) %all-to-all-start.2) | async-done | bytes 393248 | tf_op jit(solution)/shard_map/all_to_all | solution.py:448
  130.9 17.7 %shard_map.73 = (bf16[2,128,256]{2,1,0:T(8,128)(2,1)}, bf16[2,128,256]{2,1,0:T(8,128)(2,1)}, bf16[2,128,256]{2,1,0:T(8,128)(2,1)}, bf16[2,128,256]{2,1,0:T(8,128)(2,1)}) custom-call(s32[3]{0:T(128)} %pad_add_fusion.place_ref, bf16[512,4096]{1,0:T(8,128)(2,1)} %w_ref.1), custom_call_target="tpu_custom_call" | custom-call | tf_op jit(solution)/shard_map/pallas_call | solution.py:362
  148.8 3.7 %collective-permute-start.14 = (bf16[2,128,256]{2,1,0:T(8,128)(2,1)}, bf16[2,128,256]{2,1,0:T(8,128)(2,1)S(1)}, u32[]{:S(2)}, u32[]{:S(2)}) collective-permute-start(bf16[2,128,256]{2,1,0:T(8,128)(2,1)} %get-tuple-element.29), channel_id=1, source_target_pairs={{0,3},{1,0},{2,1},{3,2},{4,7},{5,4},{6,5},{7,6},{8,11},{9,8},{10,9... | collective-permute-start | bytes 393224 | tf_op jit(solution)/shard_map/ppermute | solution.py:392
  153.4 11.3 %shard_map.77 = bf16[8,256,128]{2,1,0:T(8,128)(2,1)} custom-call(s32[1]{0:T(128)} %bitcast.9.part_ref, bf16[8,128,384]{2,1,0:T(8,128)(2,1)} %copy-done.8, bf16[8,128,384]{2,1,0:T(8,128)(2,1)} %collective-permute-done.21.refs_1_, bf16[8,64,384]{2,1,0:T(8,128)(2,1)} %copy-done.10, bf16[8,64,384]{2,1,0:T(8,128)(2,1)} %copy-done.37, ...), custom_call_target="tpu_custom_call" | custom-call | flops 3623878656 | bytes 4194304 | tf_op jit(solution)/shard_map/pallas_call | solution.py:250
  164.7 3.7 %all-to-all-start.3 = ((bf16[8,256,128]{2,1,0:T(8,128)(2,1)}), bf16[8,256,128]{2,1,0:T(8,128)(2,1)S(1)}, u32[]{:S(2)}, u32[]{:S(2)}) async-start(bf16[8,256,128]{2,1,0:T(8,128)(2,1)} %shard_map.77), calls=%async_computation.3 | async-start | bytes 1048576 | tf_op jit(solution)/shard_map/all_to_all | solution.py:457
  169.2 1.8 collective-permute-start.32
  171.0 1.5 collective-permute-start.30
  174.5 8.1 %collective-permute-done.32 = bf16[512,256]{1,0:T(8,128)(2,1)S(1)} collective-permute-done((bf16[512,256]{1,0:T(8,128)(2,1)S(1)}, bf16[512,256]{1,0:T(8,128)(2,1)S(1)}, u32[]{:S(2)}, u32[]{:S(2)}) %collective-permute-start.32) | collective-permute-done | bytes 262176 | tf_op jit(solution)/shard_map/ppermute | solution.py:403
  183.3 1.5 collective-permute-start.33
  185.9 2.5 %collective-permute-start.36 = (bf16[4,256,128]{2,1,0:T(8,128)(2,1)S(1)}, bf16[4,256,128]{2,1,0:T(8,128)(2,1)S(1)}, u32[]{:S(2)}, u32[]{:S(2)}) collective-permute-start(bf16[4,256,128]{2,1,0:T(8,128)(2,1)S(1)} %get-tuple-element.42.refs_4_), channel_id=1, source_target_pairs={{0,1},{1,2},{2,3},{4,5},{5,6},{6,7},{8,9},{9,10},{10,11},{12,13},{... | collective-permute-start | bytes 786440 | tf_op jit(solution)/shard_map/ppermute | solution.py:40
  188.4 1.3 collective-permute-start.37
  189.7 4.6 %collective-permute-start.42 = (bf16[4,256,128]{2,1,0:T(8,128)(2,1)S(1)}, bf16[4,256,128]{2,1,0:T(8,128)(2,1)S(1)}, u32[]{:S(2)}, u32[]{:S(2)}) collective-permute-start(bf16[4,256,128]{2,1,0:T(8,128)(2,1)S(1)} %get-tuple-element.41.refs_11_), channel_id=1, source_target_pairs={{0,1},{1,2},{2,3},{4,5},{5,6},{6,7},{8,9},{9,10},{10,11},{12,13},{... | collective-permute-start | bytes 786440 | tf_op jit(solution)/shard_map/ppermute | solution.py:40
  194.3 2.9 %collective-permute-done.33 = bf16[1024,256]{1,0:T(8,128)(2,1)} collective-permute-done((bf16[1024,256]{1,0:T(8,128)(2,1)}, bf16[1024,256]{1,0:T(8,128)(2,1)}, u32[]{:S(2)}, u32[]{:S(2)}) %collective-permute-start.33) | collective-permute-done | bytes 524320 | tf_op jit(solution)/shard_map/ppermute | solution.py:403
  197.2 1.0 slice_dynamic-update-slice_fusion.1
  198.2 1.0 slice_dynamic-update-slice_fusion.refs_1_
  199.5 1.2 constant_dynamic-update-slice_fusion.5.refs_0_
  201.0 1.3 collective-permute-start.43
  203.0 1.3 collective-permute-start.39
  204.3 7.7 %collective-permute-done.43.refs_13_ = bf16[4,256,128]{2,1,0:T(8,128)(2,1)S(1)} collective-permute-done((bf16[4,256,128]{2,1,0:T(8,128)(2,1)S(1)}, bf16[4,256,128]{2,1,0:T(8,128)(2,1)S(1)}, u32[]{:S(2)}, u32[]{:S(2)}) %collective-permute-start.43) | collective-permute-done | bytes 262176 | tf_op jit(solution)/shard_map/ppermute | solution.py:41
  212.0 1.4 collective-permute-start.44
  213.4 1.3 collective-permute-start.45
  214.7 2.4 collective-permute-done.39.refs_8_
  217.8 1.3 collective-permute-start.41
  219.1 6.7 %collective-permute-done.45.refs_15_ = bf16[4,256,128]{2,1,0:T(8,128)(2,1)} collective-permute-done((bf16[4,256,128]{2,1,0:T(8,128)(2,1)S(1)}, bf16[4,256,128]{2,1,0:T(8,128)(2,1)}, u32[]{:S(2)}, u32[]{:S(2)}) %collective-permute-start.45) | collective-permute-done | bytes 262176 | tf_op jit(solution)/shard_map/ppermute | solution.py:41
  225.8 1.4 collective-permute-start.46
  227.9 1.3 collective-permute-start.47
  229.2 0.9 copy.13.active_ref
  231.3 5.2 %collective-permute-done.47.refs_17_ = bf16[4,256,128]{2,1,0:T(8,128)(2,1)} collective-permute-done((bf16[4,256,128]{2,1,0:T(8,128)(2,1)}, bf16[4,256,128]{2,1,0:T(8,128)(2,1)}, u32[]{:S(2)}, u32[]{:S(2)}) %collective-permute-start.47) | collective-permute-done | bytes 262176 | tf_op jit(solution)/shard_map/ppermute | solution.py:41
  236.5 9.6 %shard_map.78 = bf16[512,1024]{1,0:T(8,128)(2,1)} custom-call(s32[5]{0:T(128)} %stack.33.me_ref, s32[16]{0:T(128)} %fusion.at_ref, bf16[512,1024]{1,0:T(8,128)(2,1)} %hidden_ref.1, s32[512,1]{1,0:T(8,128)} %copy.13.active_ref, bf16[2048,256]{1,0:T(8,128)(2,1)} %copy-done.1, bf16[2048,256]{1,0:T(8,128)(2,1)} %copy-done, ...), custom_call_target="tpu_custom_call" | custom-call | flops 2147483648 | bytes 8388608 | tf_op jit(solution)/shard_map/pallas_call | solution.py:319
  (151 shorter events, 20.9 us)
Async XLA Ops:
  1.3 44.8 %copy-start.2 = (bf16[128,1024]{1,0:T(8,128)(2,1)}, bf16[128,1024]{1,0:T(8,128)(2,1)S(1)}, u32[]{:S(2)}) copy-start(bf16[128,1024]{1,0:T(8,128)(2,1)S(1)} %get-tuple-element.38.refs_3_) | copy-start | bytes 786436
  1.3 44.8 %copy-start.3 = (bf16[128,1024]{1,0:T(8,128)(2,1)}, bf16[128,1024]{1,0:T(8,128)(2,1)S(1)}, u32[]{:S(2)}) copy-start(bf16[128,1024]{1,0:T(8,128)(2,1)S(1)} %get-tuple-element.39.refs_10_) | copy-start | bytes 786436
  1.3 56.8 %copy-start.7 = (bf16[128,1024]{1,0:T(8,128)(2,1)}, bf16[128,1024]{1,0:T(8,128)(2,1)S(1)}, u32[]{:S(2)}) copy-start(bf16[128,1024]{1,0:T(8,128)(2,1)S(1)} %get-tuple-element.30.refs_3_) | copy-start | bytes 786436
  1.3 65.1 %copy-start.6 = (bf16[128,1024]{1,0:T(8,128)(2,1)}, bf16[128,1024]{1,0:T(8,128)(2,1)S(1)}, u32[]{:S(2)}) copy-start(bf16[128,1024]{1,0:T(8,128)(2,1)S(1)} %get-tuple-element.25.refs_3_) | copy-start | bytes 786436
  1.3 12.1 %collective-permute-start.15 = (bf16[128,1024]{1,0:T(8,128)(2,1)S(1)}, bf16[128,1024]{1,0:T(8,128)(2,1)S(1)}, u32[]{:S(2)}, u32[]{:S(2)}) collective-permute-start(bf16[128,1024]{1,0:T(8,128)(2,1)S(1)} %get-tuple-element.38.refs_3_), channel_id=1, source_target_pairs={{0,1},{1,2},{2,3},{4,5},{5,6},{6,7},{8,9},{9,10},{10,11},{12,13},{... | collective-permute-start | bytes 786440 | tf_op jit(solution)/shard_map/ppermute | solution.py:40
  6.3 9.9 %collective-permute-start.16 = (bf16[128,1024]{1,0:T(8,128)(2,1)S(1)}, bf16[128,1024]{1,0:T(8,128)(2,1)S(1)}, u32[]{:S(2)}, u32[]{:S(2)}) collective-permute-start(bf16[128,1024]{1,0:T(8,128)(2,1)S(1)} %get-tuple-element.38.refs_3_), channel_id=1, source_target_pairs={{1,0},{2,1},{3,2},{5,4},{6,5},{7,6},{9,8},{10,9},{11,10},{13,12},{... | collective-permute-start | bytes 786440 | tf_op jit(solution)/shard_map/ppermute | solution.py:41
  7.6 9.9 %collective-permute-start = (bf16[128,1024]{1,0:T(8,128)(2,1)S(1)}, bf16[128,1024]{1,0:T(8,128)(2,1)S(1)}, u32[]{:S(2)}, u32[]{:S(2)}) collective-permute-start(bf16[128,1024]{1,0:T(8,128)(2,1)S(1)} %get-tuple-element.39.refs_10_), channel_id=1, source_target_pairs={{0,1},{1,2},{2,3},{4,5},{5,6},{6,7},{8,9},{9,10},{10,11},{12,13},{... | collective-permute-start | bytes 786440 | tf_op jit(solution)/shard_map/ppermute | solution.py:40
  12.1 10.1 %collective-permute-start.1 = (bf16[128,1024]{1,0:T(8,128)(2,1)S(1)}, bf16[128,1024]{1,0:T(8,128)(2,1)S(1)}, u32[]{:S(2)}, u32[]{:S(2)}) collective-permute-start(bf16[128,1024]{1,0:T(8,128)(2,1)S(1)} %get-tuple-element.39.refs_10_), channel_id=1, source_target_pairs={{1,0},{2,1},{3,2},{5,4},{6,5},{7,6},{9,8},{10,9},{11,10},{13,12},{... | collective-permute-start | bytes 786440 | tf_op jit(solution)/shard_map/ppermute | solution.py:41
  13.4 32.6 %copy-start.12 = (bf16[128,1024]{1,0:T(8,128)(2,1)}, bf16[128,1024]{1,0:T(8,128)(2,1)S(1)}, u32[]{:S(2)}) copy-start(bf16[128,1024]{1,0:T(8,128)(2,1)S(1)} %collective-permute-done.15.refs_4_) | copy-start | bytes 786436
  13.4 10.1 %collective-permute-start.17 = (bf16[128,1024]{1,0:T(8,128)(2,1)S(1)}, bf16[128,1024]{1,0:T(8,128)(2,1)S(1)}, u32[]{:S(2)}, u32[]{:S(2)}) collective-permute-start(bf16[128,1024]{1,0:T(8,128)(2,1)S(1)} %collective-permute-done.15.refs_4_), channel_id=1, source_target_pairs={{1,2},{2,3},{5,6},{6,7},{9,10},{10,11},{13,14},{14,15},{17,18},{18... | collective-permute-start | bytes 786440 | tf_op jit(solution)/shard_map/ppermute | solution.py:40
  16.2 11.9 %collective-permute-start.18 = (bf16[128,1024]{1,0:T(8,128)(2,1)S(1)}, bf16[128,1024]{1,0:T(8,128)(2,1)S(1)}, u32[]{:S(2)}, u32[]{:S(2)}) collective-permute-start(bf16[128,1024]{1,0:T(8,128)(2,1)S(1)} %collective-permute-done.16.refs_5_), channel_id=1, source_target_pairs={{1,0},{2,1},{5,4},{6,5},{9,8},{10,9},{13,12},{14,13},{17,16},{18,1... | collective-permute-start | bytes 786440 | tf_op jit(solution)/shard_map/ppermute | solution.py:41
  17.5 11.9 %collective-permute-start.2 = (bf16[128,1024]{1,0:T(8,128)(2,1)S(1)}, bf16[128,1024]{1,0:T(8,128)(2,1)S(1)}, u32[]{:S(2)}, u32[]{:S(2)}) collective-permute-start(bf16[128,1024]{1,0:T(8,128)(2,1)S(1)} %collective-permute-done.refs_11_), channel_id=1, source_target_pairs={{1,2},{2,3},{5,6},{6,7},{9,10},{10,11},{13,14},{14,15},{17,18},{18... | collective-permute-start | bytes 786440 | tf_op jit(solution)/shard_map/ppermute | solution.py:40
  22.2 12.4 %collective-permute-start.3 = (bf16[128,1024]{1,0:T(8,128)(2,1)S(1)}, bf16[128,1024]{1,0:T(8,128)(2,1)S(1)}, u32[]{:S(2)}, u32[]{:S(2)}) collective-permute-start(bf16[128,1024]{1,0:T(8,128)(2,1)S(1)} %collective-permute-done.1.refs_12_), channel_id=1, source_target_pairs={{1,0},{2,1},{5,4},{6,5},{9,8},{10,9},{13,12},{14,13},{17,16},{18,1... | collective-permute-start | bytes 786440 | tf_op jit(solution)/shard_map/ppermute | solution.py:41
  23.5 15.2 %collective-permute-start.19 = (bf16[128,1024]{1,0:T(8,128)(2,1)S(1)}, bf16[128,1024]{1,0:T(8,128)(2,1)S(1)}, u32[]{:S(2)}, u32[]{:S(2)}) collective-permute-start(bf16[128,1024]{1,0:T(8,128)(2,1)S(1)} %collective-permute-done.17.refs_6_), channel_id=1, source_target_pairs={{2,3},{6,7},{10,11},{14,15},{18,19},{22,23},{26,27},{30,31}} | collective-permute-start | bytes 786440 | tf_op jit(solution)/shard_map/ppermute | solution.py:40
  28.1 12.3 %collective-permute-start.20 = (bf16[128,1024]{1,0:T(8,128)(2,1)S(1)}, bf16[128,1024]{1,0:T(8,128)(2,1)}, u32[]{:S(2)}, u32[]{:S(2)}) collective-permute-start(bf16[128,1024]{1,0:T(8,128)(2,1)S(1)} %collective-permute-done.18.refs_7_), channel_id=1, source_target_pairs={{1,0},{5,4},{9,8},{13,12},{17,16},{21,20},{25,24},{29,28}} | collective-permute-start | bytes 786440 | tf_op jit(solution)/shard_map/ppermute | solution.py:41
  29.4 16.6 %collective-permute-start.4 = (bf16[128,1024]{1,0:T(8,128)(2,1)S(1)}, bf16[128,1024]{1,0:T(8,128)(2,1)}, u32[]{:S(2)}, u32[]{:S(2)}) collective-permute-start(bf16[128,1024]{1,0:T(8,128)(2,1)S(1)} %collective-permute-done.2.refs_13_), channel_id=1, source_target_pairs={{2,3},{6,7},{10,11},{14,15},{18,19},{22,23},{26,27},{30,31}} | collective-permute-start | bytes 786440 | tf_op jit(solution)/shard_map/ppermute | solution.py:40
  34.6 11.4 %collective-permute-start.5 = (bf16[128,1024]{1,0:T(8,128)(2,1)S(1)}, bf16[128,1024]{1,0:T(8,128)(2,1)}, u32[]{:S(2)}, u32[]{:S(2)}) collective-permute-start(bf16[128,1024]{1,0:T(8,128)(2,1)S(1)} %collective-permute-done.3.refs_14_), channel_id=1, source_target_pairs={{1,0},{5,4},{9,8},{13,12},{17,16},{21,20},{25,24},{29,28}} | collective-permute-start | bytes 786440 | tf_op jit(solution)/shard_map/ppermute | solution.py:41
  40.4 27.4 %collective-permute-start.22 = (bf16[128,1024]{1,0:T(8,128)(2,1)S(1)}, bf16[128,1024]{1,0:T(8,128)(2,1)}, u32[]{:S(2)}, u32[]{:S(2)}) collective-permute-start(bf16[128,1024]{1,0:T(8,128)(2,1)S(1)} %get-tuple-element.30.refs_3_), channel_id=1, source_target_pairs={{0,1},{1,2},{2,3},{4,5},{5,6},{6,7},{8,9},{9,10},{10,11},{12,13},{... | collective-permute-start | bytes 786440 | tf_op jit(solution)/shard_map/ppermute | solution.py:40
  44.7 23.0 %collective-permute-start.23 = (bf16[128,1024]{1,0:T(8,128)(2,1)S(1)}, bf16[128,1024]{1,0:T(8,128)(2,1)}, u32[]{:S(2)}, u32[]{:S(2)}) collective-permute-start(bf16[128,1024]{1,0:T(8,128)(2,1)S(1)} %get-tuple-element.30.refs_3_), channel_id=1, source_target_pairs={{1,0},{2,1},{3,2},{5,4},{6,5},{7,6},{9,8},{10,9},{11,10},{13,12},{... | collective-permute-start | bytes 786440 | tf_op jit(solution)/shard_map/ppermute | solution.py:41
  58.1 45.0 %all-to-all-start = ((bf16[8,128,384]{2,1,0:T(8,128)(2,1)}), bf16[8,128,384]{2,1,0:T(8,128)(2,1)S(1)}, u32[]{:S(2)}, u32[]{:S(2)}) async-start(bf16[8,128,384]{2,1,0:T(8,128)(2,1)} %shard_map.75), calls=%async_computation | async-start | bytes 1572864 | tf_op jit(solution)/shard_map/all_to_all | solution.py:448
  61.8 10.8 %collective-permute-start.6 = (bf16[128,1024]{1,0:T(8,128)(2,1)S(1)}, bf16[128,1024]{1,0:T(8,128)(2,1)S(1)}, u32[]{:S(2)}, u32[]{:S(2)}) collective-permute-start(bf16[128,1024]{1,0:T(8,128)(2,1)S(1)} %get-tuple-element.25.refs_3_), channel_id=1, source_target_pairs={{0,1},{1,2},{2,3},{4,5},{5,6},{6,7},{8,9},{9,10},{10,11},{12,13},{... | collective-permute-start | bytes 786440 | tf_op jit(solution)/shard_map/ppermute | solution.py:40
  66.4 11.0 %collective-permute-start.7 = (bf16[128,1024]{1,0:T(8,128)(2,1)S(1)}, bf16[128,1024]{1,0:T(8,128)(2,1)S(1)}, u32[]{:S(2)}, u32[]{:S(2)}) collective-permute-start(bf16[128,1024]{1,0:T(8,128)(2,1)S(1)} %get-tuple-element.25.refs_3_), channel_id=1, source_target_pairs={{1,0},{2,1},{3,2},{5,4},{6,5},{7,6},{9,8},{10,9},{11,10},{13,12},{... | collective-permute-start | bytes 786440 | tf_op jit(solution)/shard_map/ppermute | solution.py:41
  67.7 11.0 %collective-permute-start.24 = (bf16[128,1024]{1,0:T(8,128)(2,1)}, bf16[128,1024]{1,0:T(8,128)(2,1)S(1)}, u32[]{:S(2)}, u32[]{:S(2)}) collective-permute-start(bf16[128,1024]{1,0:T(8,128)(2,1)} %collective-permute-done.22.refs_4_), channel_id=1, source_target_pairs={{1,2},{2,3},{5,6},{6,7},{9,10},{10,11},{13,14},{14,15},{17,18},{18... | collective-permute-start | bytes 786440 | tf_op jit(solution)/shard_map/ppermute | solution.py:40
  68.4 14.6 %collective-permute-start.25 = (bf16[128,1024]{1,0:T(8,128)(2,1)}, bf16[128,1024]{1,0:T(8,128)(2,1)S(1)}, u32[]{:S(2)}, u32[]{:S(2)}) collective-permute-start(bf16[128,1024]{1,0:T(8,128)(2,1)} %collective-permute-done.23.refs_5_), channel_id=1, source_target_pairs={{1,0},{2,1},{5,4},{6,5},{9,8},{10,9},{13,12},{14,13},{17,16},{18,1... | collective-permute-start | bytes 786440 | tf_op jit(solution)/shard_map/ppermute | solution.py:41
  72.6 12.5 %collective-permute-start.8 = (bf16[128,1024]{1,0:T(8,128)(2,1)S(1)}, bf16[128,1024]{1,0:T(8,128)(2,1)S(1)}, u32[]{:S(2)}, u32[]{:S(2)}) collective-permute-start(bf16[128,1024]{1,0:T(8,128)(2,1)S(1)} %collective-permute-done.6.refs_4_), channel_id=1, source_target_pairs={{1,2},{2,3},{5,6},{6,7},{9,10},{10,11},{13,14},{14,15},{17,18},{18... | collective-permute-start | bytes 786440 | tf_op jit(solution)/shard_map/ppermute | solution.py:40
  77.4 11.2 %collective-permute-start.9 = (bf16[128,1024]{1,0:T(8,128)(2,1)S(1)}, bf16[128,1024]{1,0:T(8,128)(2,1)S(1)}, u32[]{:S(2)}, u32[]{:S(2)}) collective-permute-start(bf16[128,1024]{1,0:T(8,128)(2,1)S(1)} %collective-permute-done.7.refs_5_), channel_id=1, source_target_pairs={{1,0},{2,1},{5,4},{6,5},{9,8},{10,9},{13,12},{14,13},{17,16},{18,1... | collective-permute-start | bytes 786440 | tf_op jit(solution)/shard_map/ppermute | solution.py:41
  78.8 11.2 %collective-permute-start.26 = (bf16[128,1024]{1,0:T(8,128)(2,1)S(1)}, bf16[128,1024]{1,0:T(8,128)(2,1)S(1)}, u32[]{:S(2)}, u32[]{:S(2)}) collective-permute-start(bf16[128,1024]{1,0:T(8,128)(2,1)S(1)} %collective-permute-done.24.refs_6_), channel_id=1, source_target_pairs={{2,3},{6,7},{10,11},{14,15},{18,19},{22,23},{26,27},{30,31}} | collective-permute-start | bytes 786440 | tf_op jit(solution)/shard_map/ppermute | solution.py:40
  83.1 11.2 %collective-permute-start.27 = (bf16[128,1024]{1,0:T(8,128)(2,1)S(1)}, bf16[128,1024]{1,0:T(8,128)(2,1)S(1)}, u32[]{:S(2)}, u32[]{:S(2)}) collective-permute-start(bf16[128,1024]{1,0:T(8,128)(2,1)S(1)} %collective-permute-done.25.refs_7_), channel_id=1, source_target_pairs={{1,0},{5,4},{9,8},{13,12},{17,16},{21,20},{25,24},{29,28}} | collective-permute-start | bytes 786440 | tf_op jit(solution)/shard_map/ppermute | solution.py:41
  85.1 23.5 %collective-permute-start.10 = (bf16[128,1024]{1,0:T(8,128)(2,1)S(1)}, bf16[128,1024]{1,0:T(8,128)(2,1)S(1)}, u32[]{:S(2)}, u32[]{:S(2)}) collective-permute-start(bf16[128,1024]{1,0:T(8,128)(2,1)S(1)} %collective-permute-done.8.refs_6_), channel_id=1, source_target_pairs={{2,3},{6,7},{10,11},{14,15},{18,19},{22,23},{26,27},{30,31}} | collective-permute-start | bytes 786440 | tf_op jit(solution)/shard_map/ppermute | solution.py:40
  88.7 19.9 %collective-permute-start.11 = (bf16[128,1024]{1,0:T(8,128)(2,1)S(1)}, bf16[128,1024]{1,0:T(8,128)(2,1)S(1)}, u32[]{:S(2)}, u32[]{:S(2)}) collective-permute-start(bf16[128,1024]{1,0:T(8,128)(2,1)S(1)} %collective-permute-done.9.refs_7_), channel_id=1, source_target_pairs={{1,0},{5,4},{9,8},{13,12},{17,16},{21,20},{25,24},{29,28}} | collective-permute-start | bytes 786440 | tf_op jit(solution)/shard_map/ppermute | solution.py:41
  103.1 15.0 %all-to-all-start.1 = ((bf16[8,64,384]{2,1,0:T(8,128)(2,1)}), bf16[8,64,384]{2,1,0:T(8,128)(2,1)S(1)}, u32[]{:S(2)}, u32[]{:S(2)}) async-start(bf16[8,64,384]{2,1,0:T(8,128)(2,1)} %shard_map.76), calls=%async_computation.1 | async-start | bytes 786432 | tf_op jit(solution)/shard_map/all_to_all | solution.py:448
  108.1 40.7 %collective-permute-start.21 = (bf16[8,128,384]{2,1,0:T(8,128)(2,1)S(1)}, bf16[8,128,384]{2,1,0:T(8,128)(2,1)}, u32[]{:S(2)}, u32[]{:S(2)}) collective-permute-start(bf16[8,128,384]{2,1,0:T(8,128)(2,1)S(1)} %all-to-all-done.refs_0_), channel_id=1, source_target_pairs={{0,4},{4,0},{8,12},{12,8},{16,20},{20,16},{24,28},{28,24},{1,5},{5... | collective-permute-start | bytes 2359304 | tf_op jit(solution)/shard_map/ppermute | solution.py:452
  118.1 34.5 %copy-start.10 = (bf16[8,64,384]{2,1,0:T(8,128)(2,1)}, bf16[8,64,384]{2,1,0:T(8,128)(2,1)S(1)}, u32[]{:S(2)}) copy-start(bf16[8,64,384]{2,1,0:T(8,128)(2,1)S(1)} %all-to-all-done.1.refs_2_) | copy-start | bytes 1179652
  118.1 12.2 %all-to-all-start.2 = ((bf16[8,64,384]{2,1,0:T(8,128)(2,1)}), bf16[8,64,384]{2,1,0:T(8,128)(2,1)S(1)}, u32[]{:S(2)}, u32[]{:S(2)}) async-start(bf16[8,64,384]{2,1,0:T(8,128)(2,1)} %shard_map.74), calls=%async_computation.2 | async-start | bytes 786432 | tf_op jit(solution)/shard_map/all_to_all | solution.py:448
  121.9 30.6 %collective-permute-start.28 = (bf16[8,64,384]{2,1,0:T(8,128)(2,1)S(1)}, bf16[8,64,384]{2,1,0:T(8,128)(2,1)S(1)}, u32[]{:S(2)}, u32[]{:S(2)}) collective-permute-start(bf16[8,64,384]{2,1,0:T(8,128)(2,1)S(1)} %all-to-all-done.1.refs_2_), channel_id=1, source_target_pairs={{0,4},{4,0},{8,12},{12,8},{16,20},{20,16},{24,28},{28,24},{1,5},{5... | collective-permute-start | bytes 1179656 | tf_op jit(solution)/shard_map/ppermute | solution.py:452
  130.3 22.2 %collective-permute-start.29 = (bf16[8,64,384]{2,1,0:T(8,128)(2,1)S(1)}, bf16[8,64,384]{2,1,0:T(8,128)(2,1)S(1)}, u32[]{:S(2)}, u32[]{:S(2)}) collective-permute-start(bf16[8,64,384]{2,1,0:T(8,128)(2,1)S(1)} %all-to-all-done.2.refs_4_), channel_id=1, source_target_pairs={{0,4},{4,0},{8,12},{12,8},{16,20},{20,16},{24,28},{28,24},{1,5},{5... | collective-permute-start | bytes 1179656 | tf_op jit(solution)/shard_map/ppermute | solution.py:452
  148.6 19.8 %collective-permute-start.12 = (bf16[2,128,256]{2,1,0:T(8,128)(2,1)}, bf16[2,128,256]{2,1,0:T(8,128)(2,1)S(1)}, u32[]{:S(2)}, u32[]{:S(2)}) collective-permute-start(bf16[2,128,256]{2,1,0:T(8,128)(2,1)} %get-tuple-element.27), channel_id=1, source_target_pairs={{0,1},{1,2},{2,3},{3,0},{4,5},{5,6},{6,7},{7,4},{8,9},{9,10},{10,1... | collective-permute-start | bytes 393224 | tf_op jit(solution)/shard_map/ppermute | solution.py:392
  148.7 19.7 %collective-permute-start.13 = (bf16[2,128,256]{2,1,0:T(8,128)(2,1)}, bf16[2,128,256]{2,1,0:T(8,128)(2,1)S(1)}, u32[]{:S(2)}, u32[]{:S(2)}) collective-permute-start(bf16[2,128,256]{2,1,0:T(8,128)(2,1)} %get-tuple-element.28), channel_id=1, source_target_pairs={{0,2},{1,3},{2,0},{3,1},{4,6},{5,7},{6,4},{7,5},{8,10},{9,11},{10,... | collective-permute-start | bytes 393224 | tf_op jit(solution)/shard_map/ppermute | solution.py:392
  148.8 19.7 %collective-permute-start.14 = (bf16[2,128,256]{2,1,0:T(8,128)(2,1)}, bf16[2,128,256]{2,1,0:T(8,128)(2,1)S(1)}, u32[]{:S(2)}, u32[]{:S(2)}) collective-permute-start(bf16[2,128,256]{2,1,0:T(8,128)(2,1)} %get-tuple-element.29), channel_id=1, source_target_pairs={{0,3},{1,0},{2,1},{3,2},{4,7},{5,4},{6,5},{7,6},{8,11},{9,8},{10,9... | collective-permute-start | bytes 393224 | tf_op jit(solution)/shard_map/ppermute | solution.py:392
  164.7 21.2 %all-to-all-start.3 = ((bf16[8,256,128]{2,1,0:T(8,128)(2,1)}), bf16[8,256,128]{2,1,0:T(8,128)(2,1)S(1)}, u32[]{:S(2)}, u32[]{:S(2)}) async-start(bf16[8,256,128]{2,1,0:T(8,128)(2,1)} %shard_map.77), calls=%async_computation.3 | async-start | bytes 1048576 | tf_op jit(solution)/shard_map/all_to_all | solution.py:457
  169.2 13.4 %collective-permute-start.32 = (bf16[512,256]{1,0:T(8,128)(2,1)S(1)}, bf16[512,256]{1,0:T(8,128)(2,1)S(1)}, u32[]{:S(2)}, u32[]{:S(2)}) collective-permute-start(bf16[512,256]{1,0:T(8,128)(2,1)S(1)} %pad_maximum_fusion.1), channel_id=1, source_target_pairs={{0,16},{4,20},{8,24},{12,28},{16,0},{20,4},{24,8},{28,12},{1,17},{... | collective-permute-start | bytes 786440 | tf_op jit(solution)/shard_map/ppermute | solution.py:403
  171.0 13.8 %collective-permute-start.30 = (bf16[512,256]{1,0:T(8,128)(2,1)S(1)}, bf16[512,256]{1,0:T(8,128)(2,1)S(1)}, u32[]{:S(2)}, u32[]{:S(2)}) collective-permute-start(bf16[512,256]{1,0:T(8,128)(2,1)S(1)} %pad_maximum_fusion), channel_id=1, source_target_pairs={{0,8},{4,12},{8,0},{12,4},{16,24},{20,28},{24,16},{28,20},{1,9},{5... | collective-permute-start | bytes 786440 | tf_op jit(solution)/shard_map/ppermute | solution.py:403
  183.3 13.9 %collective-permute-start.33 = (bf16[1024,256]{1,0:T(8,128)(2,1)}, bf16[1024,256]{1,0:T(8,128)(2,1)}, u32[]{:S(2)}, u32[]{:S(2)}) collective-permute-start(bf16[1024,256]{1,0:T(8,128)(2,1)} %constant_dynamic-update-slice_fusion.11), channel_id=1, source_target_pairs={{0,8},{4,12},{8,0},{12,4},{16,24},{20,28},{24,16},{28,20},{1,9},{5... | collective-permute-start | bytes 1572872 | tf_op jit(solution)/shard_map/ppermute | solution.py:403
  185.5 13.9 %collective-permute-start.31 = (bf16[1024,256]{1,0:T(8,128)(2,1)}, bf16[1024,256]{1,0:T(8,128)(2,1)}, u32[]{:S(2)}, u32[]{:S(2)}) collective-permute-start(bf16[1024,256]{1,0:T(8,128)(2,1)} %get-tuple-element.43), channel_id=1, source_target_pairs={{0,16},{4,20},{8,24},{12,28},{16,0},{20,4},{24,8},{28,12},{1,17},{... | collective-permute-start | bytes 1572872 | tf_op jit(solution)/shard_map/ppermute | solution.py:403
  185.9 50.6 %copy-start.4 = (bf16[4,256,128]{2,1,0:T(8,128)(2,1)}, bf16[4,256,128]{2,1,0:T(8,128)(2,1)S(1)}, u32[]{:S(2)}) copy-start(bf16[4,256,128]{2,1,0:T(8,128)(2,1)S(1)} %get-tuple-element.41.refs_11_) | copy-start | bytes 786436
  185.9 50.6 %copy-start.5 = (bf16[4,256,128]{2,1,0:T(8,128)(2,1)}, bf16[4,256,128]{2,1,0:T(8,128)(2,1)S(1)}, u32[]{:S(2)}) copy-start(bf16[4,256,128]{2,1,0:T(8,128)(2,1)S(1)} %get-tuple-element.42.refs_4_) | copy-start | bytes 786436
  185.9 15.0 %collective-permute-start.36 = (bf16[4,256,128]{2,1,0:T(8,128)(2,1)S(1)}, bf16[4,256,128]{2,1,0:T(8,128)(2,1)S(1)}, u32[]{:S(2)}, u32[]{:S(2)}) collective-permute-start(bf16[4,256,128]{2,1,0:T(8,128)(2,1)S(1)} %get-tuple-element.42.refs_4_), channel_id=1, source_target_pairs={{0,1},{1,2},{2,3},{4,5},{5,6},{6,7},{8,9},{9,10},{10,11},{12,13},{... | collective-permute-start | bytes 786440 | tf_op jit(solution)/shard_map/ppermute | solution.py:40
  188.4 13.8 %collective-permute-start.37 = (bf16[4,256,128]{2,1,0:T(8,128)(2,1)S(1)}, bf16[4,256,128]{2,1,0:T(8,128)(2,1)S(1)}, u32[]{:S(2)}, u32[]{:S(2)}) collective-permute-start(bf16[4,256,128]{2,1,0:T(8,128)(2,1)S(1)} %get-tuple-element.42.refs_4_), channel_id=1, source_target_pairs={{1,0},{2,1},{3,2},{5,4},{6,5},{7,6},{9,8},{10,9},{11,10},{13,12},{... | collective-permute-start | bytes 786440 | tf_op jit(solution)/shard_map/ppermute | solution.py:41
  189.7 13.2 %collective-permute-start.42 = (bf16[4,256,128]{2,1,0:T(8,128)(2,1)S(1)}, bf16[4,256,128]{2,1,0:T(8,128)(2,1)S(1)}, u32[]{:S(2)}, u32[]{:S(2)}) collective-permute-start(bf16[4,256,128]{2,1,0:T(8,128)(2,1)S(1)} %get-tuple-element.41.refs_11_), channel_id=1, source_target_pairs={{0,1},{1,2},{2,3},{4,5},{5,6},{6,7},{8,9},{9,10},{10,11},{12,13},{... | collective-permute-start | bytes 786440 | tf_op jit(solution)/shard_map/ppermute | solution.py:40
  199.2 37.3 %copy-start = (bf16[2048,256]{1,0:T(8,128)(2,1)}, bf16[2048,256]{1,0:T(8,128)(2,1)S(1)}, u32[]{:S(2)}) copy-start(bf16[2048,256]{1,0:T(8,128)(2,1)S(1)} %slice_dynamic-update-slice_fusion.refs_1_) | copy-start | bytes 3145732
  199.2 37.2 %collective-permute-start.35 = (bf16[2048,256]{1,0:T(8,128)(2,1)S(1)}, bf16[2048,256]{1,0:T(8,128)(2,1)}, u32[]{:S(2)}, u32[]{:S(2)}) collective-permute-start(bf16[2048,256]{1,0:T(8,128)(2,1)S(1)} %slice_dynamic-update-slice_fusion.refs_1_), channel_id=1, source_target_pairs={{0,4},{4,0},{8,12},{12,8},{16,20},{20,16},{24,28},{28,24},{1,5},{5... | collective-permute-start | bytes 3145736 | tf_op jit(solution)/shard_map/ppermute | solution.py:411
  200.7 35.8 %copy-start.1 = (bf16[2048,256]{1,0:T(8,128)(2,1)}, bf16[2048,256]{1,0:T(8,128)(2,1)S(1)}, u32[]{:S(2)}) copy-start(bf16[2048,256]{1,0:T(8,128)(2,1)S(1)} %constant_dynamic-update-slice_fusion.5.refs_0_) | copy-start | bytes 3145732
  200.7 35.8 %collective-permute-start.34 = (bf16[2048,256]{1,0:T(8,128)(2,1)S(1)}, bf16[2048,256]{1,0:T(8,128)(2,1)}, u32[]{:S(2)}, u32[]{:S(2)}) collective-permute-start(bf16[2048,256]{1,0:T(8,128)(2,1)S(1)} %constant_dynamic-update-slice_fusion.5.refs_0_), channel_id=1, source_target_pairs={{0,4},{4,0},{8,12},{12,8},{16,20},{20,16},{24,28},{28,24},{1,5},{5... | collective-permute-start | bytes 3145736 | tf_op jit(solution)/shard_map/ppermute | solution.py:411
  201.0 35.5 %copy-start.21 = (bf16[4,256,128]{2,1,0:T(8,128)(2,1)}, bf16[4,256,128]{2,1,0:T(8,128)(2,1)S(1)}, u32[]{:S(2)}) copy-start(bf16[4,256,128]{2,1,0:T(8,128)(2,1)S(1)} %collective-permute-done.36.refs_5_) | copy-start | bytes 786436
  201.0 11.0 %collective-permute-start.43 = (bf16[4,256,128]{2,1,0:T(8,128)(2,1)S(1)}, bf16[4,256,128]{2,1,0:T(8,128)(2,1)S(1)}, u32[]{:S(2)}, u32[]{:S(2)}) collective-permute-start(bf16[4,256,128]{2,1,0:T(8,128)(2,1)S(1)} %get-tuple-element.41.refs_11_), channel_id=1, source_target_pairs={{1,0},{2,1},{3,2},{5,4},{6,5},{7,6},{9,8},{10,9},{11,10},{13,12},{... | collective-permute-start | bytes 786440 | tf_op jit(solution)/shard_map/ppermute | solution.py:41
  202.3 34.3 %copy-start.22 = (bf16[4,256,128]{2,1,0:T(8,128)(2,1)}, bf16[4,256,128]{2,1,0:T(8,128)(2,1)S(1)}, u32[]{:S(2)}) copy-start(bf16[4,256,128]{2,1,0:T(8,128)(2,1)S(1)} %collective-permute-done.37.refs_6_) | copy-start | bytes 786436
  202.3 11.1 %collective-permute-start.38 = (bf16[4,256,128]{2,1,0:T(8,128)(2,1)S(1)}, bf16[4,256,128]{2,1,0:T(8,128)(2,1)S(1)}, u32[]{:S(2)}, u32[]{:S(2)}) collective-permute-start(bf16[4,256,128]{2,1,0:T(8,128)(2,1)S(1)} %collective-permute-done.36.refs_5_), channel_id=1, source_target_pairs={{1,2},{2,3},{5,6},{6,7},{9,10},{10,11},{13,14},{14,15},{17,18},{18... | collective-permute-start | bytes 786440 | tf_op jit(solution)/shard_map/ppermute | solution.py:40
  203.0 14.1 %collective-permute-start.39 = (bf16[4,256,128]{2,1,0:T(8,128)(2,1)S(1)}, bf16[4,256,128]{2,1,0:T(8,128)(2,1)}, u32[]{:S(2)}, u32[]{:S(2)}) collective-permute-start(bf16[4,256,128]{2,1,0:T(8,128)(2,1)S(1)} %collective-permute-done.37.refs_6_), channel_id=1, source_target_pairs={{1,0},{2,1},{5,4},{6,5},{9,8},{10,9},{13,12},{14,13},{17,16},{18,1... | collective-permute-start | bytes 786440 | tf_op jit(solution)/shard_map/ppermute | solution.py:41
  212.0 5.8 %collective-permute-start.44 = (bf16[4,256,128]{2,1,0:T(8,128)(2,1)S(1)}, bf16[4,256,128]{2,1,0:T(8,128)(2,1)}, u32[]{:S(2)}, u32[]{:S(2)}) collective-permute-start(bf16[4,256,128]{2,1,0:T(8,128)(2,1)S(1)} %collective-permute-done.42.refs_12_), channel_id=1, source_target_pairs={{1,2},{2,3},{5,6},{6,7},{9,10},{10,11},{13,14},{14,15},{17,18},{18... | collective-permute-start | bytes 786440 | tf_op jit(solution)/shard_map/ppermute | solution.py:40
  213.4 12.4 %collective-permute-start.45 = (bf16[4,256,128]{2,1,0:T(8,128)(2,1)S(1)}, bf16[4,256,128]{2,1,0:T(8,128)(2,1)}, u32[]{:S(2)}, u32[]{:S(2)}) collective-permute-start(bf16[4,256,128]{2,1,0:T(8,128)(2,1)S(1)} %collective-permute-done.43.refs_13_), channel_id=1, source_target_pairs={{1,0},{2,1},{5,4},{6,5},{9,8},{10,9},{13,12},{14,13},{17,16},{18,1... | collective-permute-start | bytes 786440 | tf_op jit(solution)/shard_map/ppermute | solution.py:41
  217.1 10.1 %collective-permute-start.40 = (bf16[4,256,128]{2,1,0:T(8,128)(2,1)S(1)}, bf16[4,256,128]{2,1,0:T(8,128)(2,1)S(1)}, u32[]{:S(2)}, u32[]{:S(2)}) collective-permute-start(bf16[4,256,128]{2,1,0:T(8,128)(2,1)S(1)} %collective-permute-done.38.refs_7_), channel_id=1, source_target_pairs={{2,3},{6,7},{10,11},{14,15},{18,19},{22,23},{26,27},{30,31}} | collective-permute-start | bytes 786440 | tf_op jit(solution)/shard_map/ppermute | solution.py:40
  217.8 13.5 %collective-permute-start.41 = (bf16[4,256,128]{2,1,0:T(8,128)(2,1)}, bf16[4,256,128]{2,1,0:T(8,128)(2,1)}, u32[]{:S(2)}, u32[]{:S(2)}) collective-permute-start(bf16[4,256,128]{2,1,0:T(8,128)(2,1)} %collective-permute-done.39.refs_8_), channel_id=1, source_target_pairs={{1,0},{5,4},{9,8},{13,12},{17,16},{21,20},{25,24},{29,28}} | collective-permute-start | bytes 786440 | tf_op jit(solution)/shard_map/ppermute | solution.py:41
  225.8 5.4 %collective-permute-start.46 = (bf16[4,256,128]{2,1,0:T(8,128)(2,1)}, bf16[4,256,128]{2,1,0:T(8,128)(2,1)}, u32[]{:S(2)}, u32[]{:S(2)}) collective-permute-start(bf16[4,256,128]{2,1,0:T(8,128)(2,1)} %collective-permute-done.44.refs_14_), channel_id=1, source_target_pairs={{2,3},{6,7},{10,11},{14,15},{18,19},{22,23},{26,27},{30,31}} | collective-permute-start | bytes 786440 | tf_op jit(solution)/shard_map/ppermute | solution.py:40
  227.9 8.6 %collective-permute-start.47 = (bf16[4,256,128]{2,1,0:T(8,128)(2,1)}, bf16[4,256,128]{2,1,0:T(8,128)(2,1)}, u32[]{:S(2)}, u32[]{:S(2)}) collective-permute-start(bf16[4,256,128]{2,1,0:T(8,128)(2,1)} %collective-permute-done.45.refs_15_), channel_id=1, source_target_pairs={{1,0},{5,4},{9,8},{13,12},{17,16},{21,20},{25,24},{29,28}} | collective-permute-start | bytes 786440 | tf_op jit(solution)/shard_map/ppermute | solution.py:41
  (27 other events, 386.0 us)

commit v5 on v4

--- a/solution.py
+++ b/solution.py
@@ -20,6 +20,13 @@
         found.append((me - 1 - step, me - 1 - step >= 0))
         found.append((me + 1 + step, me + 1 + step < count))
     return found
+
+
+def when(there, act):
+    if there is None:
+        act()
+    else:
+        pl.when(there)(act)
 
 
 def line_gather(chunks, count, between=None):
@@ -30,7 +37,7 @@
         pair = []
         for chunk in chunks[first : first + 2]:
             if first:
-                chunk, _ = lax.optimization_barrier((chunk, found[first - 2 + len(pair)]))
+                chunk, _ = lax.optimization_barrier((chunk, found[first - 2]))
             pair.append([chunk])
         last = [(chunk[0], chunk[0]) for chunk in pair]
         for step in range(count - 1):
@@ -49,67 +56,69 @@
 
 def project_kernel(group, count, me_ref, gain_ref, active_ref, *refs):
     matrices = refs[:3]
-    pieces = refs[3:-4]
-    out_ref, normed, held, arrived = refs[-4:]
-    block = held.shape[3]
-    blocks = matrices[0].shape[1] // block
-    copies = [
-        pltpu.make_async_copy(
-            matrix.at[:, at * block : (at + 1) * block], held.at[at, which], arrived.at[at, which]
-        )
-        for at in range(blocks)
-        for which, matrix in enumerate(matrices)
-    ]
-    for copy in copies:
-        copy.start()
+    pieces = refs[3:-5]
+    out_ref, normed, held, piece_in, weight_in = refs[-5:]
     found = sources(me_ref[0], count)
     chunk_rows, width = pieces[0].shape
     chunks = len(pieces) // len(found)
     rows = chunks * chunk_rows
 
-    for number, piece in enumerate(pieces):
-        first, (source, there) = number // len(found) * chunk_rows, found[number % len(found)]
-
-        def place(first=first, piece=piece, source=source):
-            normed[source, first : first + chunk_rows, :] = piece[...]
-
-        if there is None:
-            place()
-        else:
-            pl.when(there)(place)
+    def copy_of(number):
+        chunk, (source, there) = number // len(found), found[number % len(found)]
+        to = normed.at[source, chunk * chunk_rows : (chunk + 1) * chunk_rows, :]
+        return there, lambda: pltpu.make_async_copy(
+            pieces[number], to, piece_in.at[chunk, source]
+        )
+
+    for number in range(len(pieces)):
+        there, copy = copy_of(number)
+        when(there, lambda: copy().start())
+    copies = [
+        [
+            pltpu.make_async_copy(
+                matrix.at[step * width : (step + 1) * width, :],
+                held.at[step, which],
+                weight_in.at[step, which],
+            )
+            for which, matrix in enumerate(matrices)
+        ]
+        for step in range(count)
+    ]
+    for step in range(count):
+        for copy in copies[step]:
+            copy.start()
+    for number in range(len(pieces)):
+        there, copy = copy_of(number)
+        when(there, lambda: copy().wait())
 
     square = jnp.zeros((rows, 1), jnp.float32)
     for source in range(count):
         values = normed[source].astype(jnp.float32)
         square = square + jnp.sum(values * values, axis=1, keepdims=True)
     row_scale = lax.rsqrt(square / (count * width) + 1e-05)
-    x = jnp.concatenate(
-        [
-            (normed[source].astype(jnp.float32) * row_scale * gain_ref[source : source + 1, :]).astype(
-                jnp.bfloat16
-            )
-            for source in range(count)
-        ],
-        axis=1,
-    )
+    for source in range(count):
+        values = normed[source].astype(jnp.float32) * row_scale * gain_ref[source : source + 1, :]
+        normed[source] = values.astype(jnp.bfloat16)
     part_rows = chunk_rows // group
-    for at in range(blocks):
+    totals = [None] * 3
+    for step in range(count):
         for which in range(3):
-            copies[at * 3 + which].wait()
-            total = jnp.dot(x, held[at, which], preferred_element_type=jnp.float32)
-            if which == 0:
-                total = jnp.where(active_ref[...] > 0, total, ASIDE)
-            total = total.astype(jnp.bfloat16)
-            for inner in range(block // HEAD):
-                head = at * (block // HEAD) + inner
-                for part in range(group):
-                    for chunk in range(chunks):
-                        first = chunk * chunk_rows + part * part_rows
-                        out_ref[
-                            head * group + part,
-                            chunk * part_rows : (chunk + 1) * part_rows,
-                            which * HEAD : (which + 1) * HEAD,
-                        ] = total[first : first + part_rows, inner * HEAD : (inner + 1) * HEAD]
+            copies[step][which].wait()
+            product = jnp.dot(normed[step], held[step, which], preferred_element_type=jnp.float32)
+            totals[which] = product if step == 0 else totals[which] + product
+    for which, total in enumerate(totals):
+        if which == 0:
+            total = jnp.where(active_ref[...] > 0, total, ASIDE)
+        total = total.astype(jnp.bfloat16)
+        for head in range(total.shape[1] // HEAD):
+            for part in range(group):
+                for chunk in range(chunks):
+                    first = chunk * chunk_rows + part * part_rows
+                    out_ref[
+                        head * group + part,
+                        chunk * part_rows : (chunk + 1) * part_rows,
+                        which * HEAD : (which + 1) * HEAD,
+                    ] = total[first : first + part_rows, head * HEAD : (head + 1) * HEAD]
 
 
 def project(me, pieces, active, gain, wq, wk, wv, seq_count, group):
@@ -117,19 +126,18 @@
     rows = active.shape[0]
     features, width = wq.shape
     count = features // columns
-    block = min(256, width)
     vmem = pl.BlockSpec(memory_space=pltpu.VMEM)
     return pl.pallas_call(
         partial(project_kernel, group, count),
         in_specs=[pl.BlockSpec(memory_space=pltpu.SMEM), vmem, vmem]
-        + [pl.BlockSpec(memory_space=pl.ANY)] * 3
-        + [vmem] * len(pieces),
+        + [pl.BlockSpec(memory_space=pl.ANY)] * (3 + len(pieces)),
         out_specs=vmem,
         out_shape=jax.ShapeDtypeStruct((seq_count, rows // group, 3 * HEAD), jnp.bfloat16),
         scratch_shapes=[
             pltpu.VMEM((count, rows, columns), jnp.bfloat16),
-            pltpu.VMEM((width // block, 3, features, block), jnp.bfloat16),
-            pltpu.SemaphoreType.DMA((width // block, 3)),
+            pltpu.VMEM((count, 3, columns, width), jnp.bfloat16),
+            pltpu.SemaphoreType.DMA((rows // pieces[0].shape[0], count)),
+            pltpu.SemaphoreType.DMA((count, 3)),
         ],
         compiler_params=pltpu.CompilerParams(vmem_limit_bytes=LIMIT),
         cost_estimate=pl.CostEstimate(
@@ -265,46 +273,55 @@
     )(part, *pieces)
 
 
-def output_kernel(chunks, group, count, cuts, halves, me_ref, at_ref, hidden_ref, active_ref, *refs):
+def output_kernel(group, count, cuts, halves, me_ref, at_ref, active_ref, hidden_ref, *refs):
     weights = refs[:cuts]
-    pieces = refs[cuts:-4]
-    out_ref, rows_in, held, arrived = refs[-4:]
-    copies = [
-        pltpu.make_async_copy(weight, held.at[cut], arrived.at[cut])
+    pieces = refs[cuts:-7]
+    out_ref, rows_in, held, own, piece_in, weight_in, own_in = refs[-7:]
+    heads = pieces[0].shape[0] // group
+    found = sources(me_ref[0], count)
+    own_copy = pltpu.make_async_copy(hidden_ref, own, own_in)
+    weight_copies = [
+        pltpu.make_async_copy(weight, held.at[cut], weight_in.at[cut])
         for cut, weight in enumerate(weights)
     ]
-    for copy in copies:
-        copy.start()
-    sent, piece_rows, _ = pieces[0].shape
-    heads = sent // group
-    part_rows = piece_rows // chunks
-    chunk_rows = part_rows * group
-    width = weights[0].shape[1]
-    found = sources(me_ref[0], count)
-
-    for number, piece in enumerate(pieces):
+
+    def copies_of(number):
         half, (source, there) = number // len(found), found[number % len(found)]
 
-        def place(half=half, piece=piece, source=source):
+        def each(act):
             for head in range(heads):
                 at = pl.multiple_of(at_ref[(source * halves + half) * heads + head] * HEAD, HEAD)
                 for part in range(group):
-                    for chunk in range(chunks):
-                        first = chunk * chunk_rows + part * part_rows
-                        rows_in[first : first + part_rows, pl.ds(at, HEAD)] = piece[
-                            head * group + part, chunk * part_rows : (chunk + 1) * part_rows, :
-                        ]
-
-        if there is None:
-            place()
-        else:
-            pl.when(there)(place)
-
+                    act(
+                        pltpu.make_async_copy(
+                            pieces[number].at[head * group + part],
+                            rows_in.at[:, part, :, pl.ds(at, HEAD)],
+                            piece_in.at[half, source, head, part],
+                        )
+                    )
+
+        return there, each
+
+    for number in range(len(pieces)):
+        there, each = copies_of(number)
+        when(there, lambda: each(lambda copy: copy.start()))
+    weight_copies[0].start()
+    own_copy.start()
+    for copy in weight_copies[1:]:
+        copy.start()
+    for number in range(len(pieces)):
+        there, each = copies_of(number)
+        when(there, lambda: each(lambda copy: copy.wait()))
+
+    rows, width = own.shape[0], held.shape[2]
+    x = rows_in[...].reshape(rows, -1)
     for cut in range(cuts):
-        copies[cut].wait()
+        weight_copies[cut].wait()
         columns = pl.ds(pl.multiple_of(me_ref[1 + cut] * width, width), width)
-        shares = jnp.dot(rows_in[...], held[cut], preferred_element_type=jnp.float32)
-        hidden = hidden_ref[:, columns]
+        shares = jnp.dot(x, held[cut], preferred_element_type=jnp.float32)
+        if cut == 0:
+            own_copy.wait()
+        hidden = own[:, columns]
         renewed = (hidden.astype(jnp.float32) + shares).astype(jnp.bfloat16)
         out_ref[:, columns] = jnp.where(active_ref[...] > 0, renewed, hidden)
 
@@ -312,21 +329,25 @@
 def output(scalars, at, pieces, weights, hidden, active, chunks, group, halves):
     rows, columns = hidden.shape
     depth, width = weights[0].shape
+    cuts = len(weights)
+    count = (len(pieces) // halves + 1) // 2
+    part_rows = rows // chunks // group
+    pieces = [piece.reshape(-1, chunks, part_rows, HEAD) for piece in pieces]
     smem = pl.BlockSpec(memory_space=pltpu.SMEM)
     vmem = pl.BlockSpec(memory_space=pltpu.VMEM)
-    cuts = len(weights)
-    count = (len(pieces) // halves + 1) // 2
     return pl.pallas_call(
-        partial(output_kernel, chunks, group, count, cuts, halves),
-        in_specs=[smem, smem, vmem, vmem]
-        + [pl.BlockSpec(memory_space=pl.ANY)] * cuts
-        + [vmem] * len(pieces),
+        partial(output_kernel, group, count, cuts, halves),
+        in_specs=[smem, smem, vmem]
+        + [pl.BlockSpec(memory_space=pl.ANY)] * (1 + cuts + len(pieces)),
         out_specs=vmem,
         out_shape=jax.ShapeDtypeStruct((rows, columns), jnp.bfloat16),
         scratch_shapes=[
-            pltpu.VMEM((rows, depth), jnp.bfloat16),
+            pltpu.VMEM((chunks, group, part_rows, depth), jnp.bfloat16),
             pltpu.VMEM((cuts, depth, width), jnp.bfloat16),
+            pltpu.VMEM((rows, columns), jnp.bfloat16),
+            pltpu.SemaphoreType.DMA((halves, count, pieces[0].shape[0] // group, group)),
             pltpu.SemaphoreType.DMA((cuts,)),
+            pltpu.SemaphoreType.DMA,
         ],
         compiler_params=pltpu.CompilerParams(vmem_limit_bytes=LIMIT),
         cost_estimate=pl.CostEstimate(
@@ -334,66 +355,81 @@
             bytes_accessed=2 * (rows * depth + depth * columns + 2 * rows * columns),
             transcendentals=0,
         ),
-    )(scalars, at, hidden, active, *weights, *pieces)
-
-
-def share_kernel(columns, place_ref, w_ref, *refs):
-    shares, arrived = refs[:-1], refs[-1]
-    copies = []
+    )(scalars, at, active, hidden, *weights, *pieces)
+
+
+def share_kernel(place_ref, w_ref, *shares):
     for step, share in enumerate(shares):
-        to = lax.rem(place_ref[2] + step, len(shares))
-        for half in range(share.shape[0]):
+
+        @pl.when(pl.program_id(0) == step)
+        def _():
             each = share.shape[2]
-            first = pl.multiple_of(to * columns + place_ref[1] + half * each, each)
-            rows = pl.ds(pl.multiple_of(place_ref[0], HEAD), HEAD)
-            copies.append(
-                pltpu.make_async_copy(
-                    w_ref.at[rows, pl.ds(first, each)], share.at[half], arrived.at[step, half]
+            for half in range(share.shape[0]):
+                share[half] = w_ref[:, half * each : (half + 1) * each]
+
+
+def shares_of(w_out, place, count, halves, each):
+    width = halves * each
+    cuts = w_out.shape[1] // count // width
+    return pl.pallas_call(
+        share_kernel,
+        grid_spec=pltpu.PrefetchScalarGridSpec(
+            num_scalar_prefetch=1,
+            grid=(count,),
+            in_specs=[
+                pl.BlockSpec(
+                    (HEAD, width),
+                    lambda j, place: (place[0], lax.rem(place[2] + j, count) * cuts + place[1]),
                 )
-            )
-    for copy in copies:
-        copy.start()
-    for copy in copies:
-        copy.wait()
-
-
-def shares_of(w_out, place, count, halves, each):
-    columns = w_out.shape[1] // count
-    return pl.pallas_call(
-        partial(share_kernel, columns),
-        in_specs=[pl.BlockSpec(memory_space=pltpu.SMEM), pl.BlockSpec(memory_space=pl.ANY)],
-        out_specs=[pl.BlockSpec(memory_space=pl.ANY)] * count,
+            ],
+            out_specs=[pl.BlockSpec((halves, HEAD, each), lambda j, place: (0, 0, 0))] * count,
+        ),
         out_shape=[jax.ShapeDtypeStruct((halves, HEAD, each), w_out.dtype)] * count,
-        scratch_shapes=[pltpu.SemaphoreType.DMA((count, halves))],
         compiler_params=pltpu.CompilerParams(vmem_limit_bytes=LIMIT),
     )(place, w_out)
 
 
-def output_weight(w_out, seq_count, tensor_count, columns, after, last):
+def weight_cuts(w_out, seq_count, columns):
     heads = w_out.shape[0] // HEAD
     cuts = seq_count // heads
     width = columns // cuts
+    halves = 2 if width % (2 * HEAD) == 0 else 1
+    return heads, cuts, halves, width // halves
+
+
+def weight_shares(w_out, seq_count, tensor_count, columns):
+    heads, cuts, halves, each = weight_cuts(w_out, seq_count, columns)
+    if each % HEAD:
+        return None
+    seq_me = lax.axis_index("seq").astype(jnp.int32)
+    me = lax.axis_index("tensor").astype(jnp.int32)
+    place = jnp.stack([seq_me // cuts, seq_me % cuts, me])
+    return list(shares_of(w_out, place, tensor_count, halves, each))
+
+
+def send_shares(shares, tensor_count, after):
+    if shares is None:
+        return None
+    shares, _ = lax.optimization_barrier((list(shares), after))
+    for step in range(1, tensor_count):
+        ring = [(d, (d + step) % tensor_count) for d in range(tensor_count)]
+        shares[step] = lax.ppermute(shares[step], "tensor", ring)
+    return shares
+
+
+def output_weight(w_out, shares, seq_count, tensor_count, columns, after):
+    heads, cuts, halves, each = weight_cuts(w_out, seq_count, columns)
     row = jnp.arange(tensor_count * heads, dtype=jnp.int32)
-    if width % HEAD:
+    if shares is None:
         weight = lax.all_to_all(w_out, "tensor", split_axis=1, concat_axis=0, tiled=True)
         return [weight], [jnp.int32(0)], row
     seq_me = lax.axis_index("seq").astype(jnp.int32)
     me = lax.axis_index("tensor").astype(jnp.int32)
     head, cut = seq_me // cuts, seq_me % cuts
-
-    halves = 2 if width % (2 * HEAD) == 0 else 1
-    each = width // halves
-    shares = shares_of(
-        w_out, jnp.stack([head * HEAD, cut * width, me]), tensor_count, halves, each
-    )
-    shares, _ = lax.optimization_barrier((list(shares), after))
-    for step in range(1, tensor_count):
-        ring = [(d, (d + step) % tensor_count) for d in range(tensor_count)]
-        shares[step] = lax.ppermute(shares[step], "tensor", ring)
     flips = []
     while cuts << len(flips) < seq_count:
         flips.append(cuts << len(flips))
-    shares, _ = lax.optimization_barrier((shares, last))
+    shares, _ = lax.optimization_barrier((shares, after))
     weights, which = [], []
     for half in range(halves):
         held = {0: jnp.concatenate([share[half] for share in shares], axis=0)}
@@ -428,6 +464,7 @@
     gain = norm_gain.reshape(tensor_count, columns)
     active = (depth >= 2).astype(jnp.int32).reshape(rows, 1)
     made = []
+    shares = weight_shares(w_out, seq_count, tensor_count, columns)
 
     def work(found):
         first = sum(count for count, _ in made)
@@ -436,13 +473,14 @@
             me.reshape(1), sum(found, []), here, gain, w_query, w_key, w_value, seq_count, group
         )
         made.append((len(found), sent))
-        return sent
+        return sent, shares
 
     gathered = line_gather(
         [hidden[c * chunk_rows : (c + 1) * chunk_rows] for c in range(chunks)], tensor_count, work
     )
-    for found in gathered[sum(count for count, _ in made) :]:
-        work([found])
+    rest = gathered[sum(count for count, _ in made) :]
+    sending = send_shares(shares, tensor_count, rest[-1])
+    work(rest)
     pieces = []
     for _, sent in made:
         got = lax.all_to_all(sent, "seq", split_axis=0, concat_axis=0)
@@ -451,12 +489,15 @@
             ring = [(d, d - d % group + (d - step) % group) for d in range(seq_count)]
             pieces.append(lax.ppermute(got, "seq", ring))
 
+    pieces[-1], sending = lax.optimization_barrier((pieces[-1], sending))
     out = attend(part, pieces, chunks, group, rows)
-    weights, cut_of, at = output_weight(w_out, seq_count, tensor_count, columns, made[-1][1], out)
+    home = lax.all_to_all(out, "seq", split_axis=0, concat_axis=0)
+    found = line_gather([home[: seq_count // 2], home[seq_count // 2 :]], tensor_count)
+    weights, cut_of, at = output_weight(
+        w_out, sending, seq_count, tensor_count, columns, [pieces[1:3] for pieces in found]
+    )
     scalars = jnp.stack([me, *cut_of])
-    home = lax.all_to_all(out, "seq", split_axis=0, concat_axis=0)
-    found = sum(line_gather([home[: seq_count // 2], home[seq_count // 2 :]], tensor_count), [])
-    return output(scalars, at, found, weights, hidden, active, chunks, group, 2)
+    return output(scalars, at, sum(found, []), weights, hidden, active, chunks, group, 2)
 
 
 def solution(mesh):

time: 248 us -> 276 us (1.11)
  waiting for transfers between devices: 74.5 us -> 109 us
  blocking collectives: 0 us -> 29.4 us
  Pallas kernels: 66.6 us -> 48.9 us
  starting transfers between devices: 84.8 us -> 73.2 us
  local copies, waits for them, and re-layouts: 17.5 us -> 10.9 us
    all_to_all x0 -> x2, blocking collectives: none -> 29.4 us  [the longest x1 16.3 us: shards(): got = lax.all_to_all(sent, 'seq', split_axis=0, concat_axis=0)]
    ppermute x4, waiting for transfers between devices: 11.2 us -> 30.5 us  [output_weight(): lax.ppermute(jnp.concatenate([held[k] for k in sent], axis=0), 'seq', pairs)]
    pallas_call x2, Pallas kernels: 27.3 us -> 12.8 us  [the longest x1 9.4 us: output(): pl.pallas_call(partial(output_kernel, group, count, cuts, halves), in_spe...]
    ppermute x3, waiting for transfers between devices: 0.01 us -> 9.31 us  [send_shares(): shares[step] = lax.ppermute(shares[step], 'tensor', ring)]
    all_to_all x3 -> x1, starting transfers between devices: 11.9 us -> 3.55 us  [shards(): got = lax.all_to_all(sent, 'seq', split_axis=0, concat_axis=0)]
    all_to_all x3 -> x1, waiting for transfers between devices: 7.84 us -> 12.1 us  [shards(): got = lax.all_to_all(sent, 'seq', split_axis=0, concat_axis=0)]
    all_to_all x1 -> x0, starting transfers between devices: 3.71 us -> none  [shards(): home = lax.all_to_all(out, 'seq', split_axis=0, concat_axis=0)]
    ppermute x18, waiting for transfers between devices: 52.5 us -> 56.1 us  [line_gather(): from_right = lax.ppermute(last[at][1], 'tensor', left[:count - 1 - step])]
  transfers between devices with their start and end apart: 52 -> 48, of which waited for: 18 -> 20; matrix products, arithmetic and copies ran while one was open for 6% -> 2% of each run, Pallas kernels for 23% -> 6%
where the time goes in v5:
time: 276 us; the launch traced here: 275 us
  waiting for transfers between devices  109 us (39%)
  starting transfers between devices  73.2 us (27%)
  Pallas kernels  48.9 us (18%)
  blocking collectives  29.4 us (11%)
  local copies, waits for them, and re-layouts  10.9 us (4%)
    ppermute x18, waiting for transfers between devices, line_gather(): from_right = lax.ppermute(last[at][1], 'tensor', left[:count - 1 - step])  56.1 us
    ppermute x18, starting transfers between devices, line_gather(): from_left = lax.ppermute(last[at][0], 'tensor', right[step:])  38.9 us
    ppermute x4, waiting for transfers between devices, output_weight(): lax.ppermute(jnp.concatenate([held[k] for k in sent], axis=0), 'seq', pairs)  30.5 us
    pallas_call x2, Pallas kernels, project(): pl.pallas_call(partial(project_kernel, group, count), in_specs=[pl.BlockS...  24.8 us
    ppermute x18, starting transfers between devices, line_gather(): from_right = lax.ppermute(last[at][1], 'tensor', left[:count - 1 - step])  23.4 us
    all_to_all x1, blocking collectives, shards(): got = lax.all_to_all(sent, 'seq', split_axis=0, concat_axis=0)  16.3 us
    all_to_all x1, blocking collectives, shards(): home = lax.all_to_all(out, 'seq', split_axis=0, concat_axis=0)  13.1 us
    all_to_all x1, waiting for transfers between devices, shards(): got = lax.all_to_all(sent, 'seq', split_axis=0, concat_axis=0)  12.1 us
  transfers between devices with their start and end apart: 48, of which 20 were waited for; matrix products, arithmetic and copies ran while one was open for 2% of the time, Pallas kernels for 6%

profile of v5, /device:TPU:0, one launch (start us, length us, event | category | flops | bytes accessed | tf_op | source)
XLA Modules:
  0.0 274.7 jit_solution(18032280814643699580)
XLA Ops:
  0.0 1.3 fusion.5
  1.3 4.9 %collective-permute-start = (bf16[128,1024]{1,0:T(8,128)(2,1)S(1)}, bf16[128,1024]{1,0:T(8,128)(2,1)S(1)}, u32[]{:S(2)}, u32[]{:S(2)}) collective-permute-start(bf16[128,1024]{1,0:T(8,128)(2,1)S(1)} %get-tuple-element.49.refs_3_), channel_id=1, source_target_pairs={{0,1},{1,2},{2,3},{4,5},{5,6},{6,7},{8,9},{9,10},{10,11},{12,13},{... | collective-permute-start | bytes 786440 | tf_op jit(solution)/shard_map/ppermute | solution.py:47
  6.3 1.3 collective-permute-start.1
  7.6 4.6 %collective-permute-start.8 = (bf16[128,1024]{1,0:T(8,128)(2,1)S(1)}, bf16[128,1024]{1,0:T(8,128)(2,1)S(1)}, u32[]{:S(2)}, u32[]{:S(2)}) collective-permute-start(bf16[128,1024]{1,0:T(8,128)(2,1)S(1)} %get-tuple-element.48.refs_10_), channel_id=1, source_target_pairs={{0,1},{1,2},{2,3},{4,5},{5,6},{6,7},{8,9},{9,10},{10,11},{12,13},{... | collective-permute-start | bytes 786440 | tf_op jit(solution)/shard_map/ppermute | solution.py:47
  12.1 1.3 collective-permute-start.9
  14.1 2.0 collective-permute-done.1.refs_5_
  16.2 1.3 collective-permute-start.3
  18.1 4.1 %collective-permute-done.9.refs_12_ = bf16[128,1024]{1,0:T(8,128)(2,1)S(1)} collective-permute-done((bf16[128,1024]{1,0:T(8,128)(2,1)S(1)}, bf16[128,1024]{1,0:T(8,128)(2,1)S(1)}, u32[]{:S(2)}, u32[]{:S(2)}) %collective-permute-start.9) | collective-permute-done | bytes 262176 | tf_op jit(solution)/shard_map/ppermute | solution.py:48
  22.2 1.3 collective-permute-start.11
  24.9 3.2 %collective-permute-done.3.refs_7_ = bf16[128,1024]{1,0:T(8,128)(2,1)S(1)} collective-permute-done((bf16[128,1024]{1,0:T(8,128)(2,1)S(1)}, bf16[128,1024]{1,0:T(8,128)(2,1)S(1)}, u32[]{:S(2)}, u32[]{:S(2)}) %collective-permute-start.3) | collective-permute-done | bytes 262176 | tf_op jit(solution)/shard_map/ppermute | solution.py:48
  28.1 1.3 collective-permute-start.5
  29.4 1.4 collective-permute-start.12
  30.8 3.9 %collective-permute-done.11.refs_14_ = bf16[128,1024]{1,0:T(8,128)(2,1)S(1)} collective-permute-done((bf16[128,1024]{1,0:T(8,128)(2,1)S(1)}, bf16[128,1024]{1,0:T(8,128)(2,1)S(1)}, u32[]{:S(2)}, u32[]{:S(2)}) %collective-permute-start.11) | collective-permute-done | bytes 262176 | tf_op jit(solution)/shard_map/ppermute | solution.py:48
  34.6 1.3 collective-permute-start.13
  35.9 0.8 copy.8.active_ref
  36.7 1.3 reshape.54.gain_ref
  38.6 3.4 %shard_map.74 = (bf16[2,128,256]{2,1,0:T(8,128)(2,1)}, bf16[2,128,256]{2,1,0:T(8,128)(2,1)}, bf16[2,128,256]{2,1,0:T(8,128)(2,1)}, bf16[2,128,256]{2,1,0:T(8,128)(2,1)}) custom-call(s32[3]{0:T(128)} %pad_add_fusion.place_ref, bf16[512,4096]{1,0:T(8,128)(2,1)} %w_ref.1), custom_call_target="tpu_custom_call" | custom-call | tf_op jit(solution)/shard_map/pallas_call | solution.py:374
  42.8 5.2 %collective-permute-start.18 = (bf16[128,1024]{1,0:T(8,128)(2,1)S(1)}, bf16[128,1024]{1,0:T(8,128)(2,1)S(1)}, u32[]{:S(2)}, u32[]{:S(2)}) collective-permute-start(bf16[128,1024]{1,0:T(8,128)(2,1)S(1)} %get-tuple-element.33.refs_10_), channel_id=1, source_target_pairs={{0,1},{1,2},{2,3},{4,5},{5,6},{6,7},{8,9},{9,10},{10,11},{12,13},{... | collective-permute-start | bytes 786440 | tf_op jit(solution)/shard_map/ppermute | solution.py:47
  48.1 1.3 collective-permute-start.19
  49.4 4.6 %collective-permute-start.6 = (bf16[128,1024]{1,0:T(8,128)(2,1)S(1)}, bf16[128,1024]{1,0:T(8,128)(2,1)S(1)}, u32[]{:S(2)}, u32[]{:S(2)}) collective-permute-start(bf16[128,1024]{1,0:T(8,128)(2,1)S(1)} %get-tuple-element.26.refs_3_), channel_id=1, source_target_pairs={{0,1},{1,2},{2,3},{4,5},{5,6},{6,7},{8,9},{9,10},{10,11},{12,13},{... | collective-permute-start | bytes 786440 | tf_op jit(solution)/shard_map/ppermute | solution.py:47
  53.9 1.3 collective-permute-start.7
  55.3 12.4 %shard_map.73 = bf16[8,128,384]{2,1,0:T(8,128)(2,1)} custom-call(s32[1]{0:T(128)} %bitcast.me_ref, f32[4,1024]{1,0:T(4,128)} %reshape.54.gain_ref, s32[256,1]{1,0:T(8,128)} %copy.8.active_ref, bf16[4096,512]{1,0:T(8,128)(2,1)} %refs_0_.3, bf16[4096,512]{1,0:T(8,128)(2,1)} %refs_1_.3, bf16[4096,512]{1,0:T(8,128)(2,1)} %refs_2_.3, ...), custom_call_target="tpu_custom_call" | custom-call | flops 3221225472 | bytes 15466496 | tf_op jit(solution)/shard_map/pallas_call | solution.py:130
  68.5 1.3 collective-permute-start.21
  70.5 1.3 collective-permute-start.15
  72.5 8.4 %collective-permute-done.21.refs_14_ = bf16[128,1024]{1,0:T(8,128)(2,1)S(1)} collective-permute-done((bf16[128,1024]{1,0:T(8,128)(2,1)S(1)}, bf16[128,1024]{1,0:T(8,128)(2,1)S(1)}, u32[]{:S(2)}, u32[]{:S(2)}) %collective-permute-start.21) | collective-permute-done | bytes 262176 | tf_op jit(solution)/shard_map/ppermute | solution.py:48
  81.0 1.3 collective-permute-start.23
  83.0 4.2 %collective-permute-done.15.refs_7_ = bf16[128,1024]{1,0:T(8,128)(2,1)S(1)} collective-permute-done((bf16[128,1024]{1,0:T(8,128)(2,1)}, bf16[128,1024]{1,0:T(8,128)(2,1)S(1)}, u32[]{:S(2)}, u32[]{:S(2)}) %collective-permute-start.15) | collective-permute-done | bytes 262176 | tf_op jit(solution)/shard_map/ppermute | solution.py:48
  87.1 1.3 collective-permute-start.17
  89.2 2.8 %collective-permute-done.23.refs_16_ = bf16[128,1024]{1,0:T(8,128)(2,1)S(1)} collective-permute-done((bf16[128,1024]{1,0:T(8,128)(2,1)S(1)}, bf16[128,1024]{1,0:T(8,128)(2,1)S(1)}, u32[]{:S(2)}, u32[]{:S(2)}) %collective-permute-start.23) | collective-permute-done | bytes 262176 | tf_op jit(solution)/shard_map/ppermute | solution.py:48
  92.0 3.3 %collective-permute-done.17.refs_9_ = bf16[128,1024]{1,0:T(8,128)(2,1)S(1)} collective-permute-done((bf16[128,1024]{1,0:T(8,128)(2,1)S(1)}, bf16[128,1024]{1,0:T(8,128)(2,1)S(1)}, u32[]{:S(2)}, u32[]{:S(2)}) %collective-permute-start.17) | collective-permute-done | bytes 262176 | tf_op jit(solution)/shard_map/ppermute | solution.py:48
  96.1 12.4 %shard_map.75 = bf16[8,128,384]{2,1,0:T(8,128)(2,1)} custom-call(s32[1]{0:T(128)} %bitcast.me_ref, f32[4,1024]{1,0:T(4,128)} %reshape.54.gain_ref, s32[256,1]{1,0:T(8,128)} %copy.9.active_ref, bf16[4096,512]{1,0:T(8,128)(2,1)} %refs_0_.3, bf16[4096,512]{1,0:T(8,128)(2,1)} %refs_1_.3, bf16[4096,512]{1,0:T(8,128)(2,1)} %refs_2_.3, ...), custom_call_target="tpu_custom_call" | custom-call | flops 3221225472 | bytes 15466496 | tf_op jit(solution)/shard_map/pallas_call | solution.py:130
  108.5 16.3 %all_to_all.15.refs_2_ = bf16[8,128,384]{2,1,0:T(8,128)(2,1)S(1)} all-to-all(bf16[8,128,384]{2,1,0:T(8,128)(2,1)} %shard_map.75), channel_id=1, replica_groups=mesh['seq'=8,'tensor'=4] {'seq'}, dimensions={0} | all-to-all | bytes 1572864 | tf_op jit(solution)/shard_map/all_to_all | solution.py:486
  124.8 3.5 %all-to-all-start.1 = ((bf16[8,128,384]{2,1,0:T(8,128)(2,1)}), bf16[8,128,384]{2,1,0:T(8,128)(2,1)S(1)}, u32[]{:S(2)}, u32[]{:S(2)}) async-start(bf16[8,128,384]{2,1,0:T(8,128)(2,1)} %shard_map.73), calls=%async_computation.1 | async-start | bytes 1572864 | tf_op jit(solution)/shard_map/all_to_all | solution.py:486
  128.8 12.1 %all-to-all-done.1.refs_0_ = bf16[8,128,384]{2,1,0:T(8,128)(2,1)S(1)} async-done(((bf16[8,128,384]{2,1,0:T(8,128)(2,1)}), bf16[8,128,384]{2,1,0:T(8,128)(2,1)S(1)}, u32[]{:S(2)}, u32[]{:S(2)}) %all-to-all-start.1) | async-done | bytes 786464 | tf_op jit(solution)/shard_map/all_to_all | solution.py:486
  141.0 3.7 %collective-permute-start.27 = (bf16[2,128,256]{2,1,0:T(8,128)(2,1)S(1)}, bf16[2,128,256]{2,1,0:T(8,128)(2,1)S(1)}, u32[]{:S(2)}, u32[]{:S(2)}) collective-permute-start(bf16[2,128,256]{2,1,0:T(8,128)(2,1)S(1)} %copy-done.40), channel_id=1, source_target_pairs={{0,3},{1,0},{2,1},{3,2},{4,7},{5,4},{6,5},{7,6},{8,11},{9,8},{10,9... | collective-permute-start | bytes 393224 | tf_op jit(solution)/shard_map/ppermute | solution.py:416
  144.8 4.6 %collective-permute-done.25 = bf16[2,128,256]{2,1,0:T(8,128)(2,1)S(1)} collective-permute-done((bf16[2,128,256]{2,1,0:T(8,128)(2,1)}, bf16[2,128,256]{2,1,0:T(8,128)(2,1)S(1)}, u32[]{:S(2)}, u32[]{:S(2)}) %collective-permute-start.25) | collective-permute-done | bytes 131104 | tf_op jit(solution)/shard_map/ppermute | solution.py:416
  149.4 4.7 %collective-permute-done.26 = bf16[2,128,256]{2,1,0:T(8,128)(2,1)S(1)} collective-permute-done((bf16[2,128,256]{2,1,0:T(8,128)(2,1)}, bf16[2,128,256]{2,1,0:T(8,128)(2,1)S(1)}, u32[]{:S(2)}, u32[]{:S(2)}) %collective-permute-start.26) | collective-permute-done | bytes 131104 | tf_op jit(solution)/shard_map/ppermute | solution.py:416
  154.1 0.8 copy-done.38
  155.0 0.9 copy-done.39
  155.8 11.3 %shard_map.76 = bf16[8,256,128]{2,1,0:T(8,128)(2,1)} custom-call(s32[1]{0:T(128)} %bitcast.9.part_ref, bf16[8,128,384]{2,1,0:T(8,128)(2,1)} %copy-done.10, bf16[8,128,384]{2,1,0:T(8,128)(2,1)} %copy-done.39, bf16[8,128,384]{2,1,0:T(8,128)(2,1)} %copy-done.9, bf16[8,128,384]{2,1,0:T(8,128)(2,1)} %copy-done.38), custom_call_target="tpu_custom_call" | custom-call | flops 3623878656 | bytes 4194304 | tf_op jit(solution)/shard_map/pallas_call | solution.py:258
  167.1 13.1 %all_to_all.16 = bf16[8,256,128]{2,1,0:T(8,128)(2,1)S(1)} all-to-all(bf16[8,256,128]{2,1,0:T(8,128)(2,1)} %shard_map.76), channel_id=1, replica_groups=mesh['seq'=8,'tensor'=4] {'seq'}, dimensions={0} | all-to-all | bytes 1048576 | tf_op jit(solution)/shard_map/all_to_all | solution.py:494
  180.3 4.8 %collective-permute-start.29 = (bf16[4,256,128]{2,1,0:T(8,128)(2,1)S(1)}, bf16[4,256,128]{2,1,0:T(8,128)(2,1)S(1)}, u32[]{:S(2)}, u32[]{:S(2)}) collective-permute-start(bf16[4,256,128]{2,1,0:T(8,128)(2,1)S(1)} %get-tuple-element.52), channel_id=1, source_target_pairs={{0,1},{1,2},{2,3},{4,5},{5,6},{6,7},{8,9},{9,10},{10,11},{12,13},{... | collective-permute-start | bytes 786440 | tf_op jit(solution)/shard_map/ppermute | solution.py:47
  185.1 1.3 collective-permute-start.30
  186.4 4.6 %collective-permute-start.31 = (bf16[4,256,128]{2,1,0:T(8,128)(2,1)S(1)}, bf16[4,256,128]{2,1,0:T(8,128)(2,1)S(1)}, u32[]{:S(2)}, u32[]{:S(2)}) collective-permute-start(bf16[4,256,128]{2,1,0:T(8,128)(2,1)S(1)} %get-tuple-element.51), channel_id=1, source_target_pairs={{0,1},{1,2},{2,3},{4,5},{5,6},{6,7},{8,9},{9,10},{10,11},{12,13},{... | collective-permute-start | bytes 786440 | tf_op jit(solution)/shard_map/ppermute | solution.py:47
  191.0 1.3 collective-permute-start.32
  192.3 2.1 collective-permute-done.30
  194.4 1.2 collective-permute-done.31
  195.6 4.1 %collective-permute-done.32 = bf16[4,256,128]{2,1,0:T(8,128)(2,1)S(1)} collective-permute-done((bf16[4,256,128]{2,1,0:T(8,128)(2,1)S(1)}, bf16[4,256,128]{2,1,0:T(8,128)(2,1)S(1)}, u32[]{:S(2)}, u32[]{:S(2)}) %collective-permute-start.32) | collective-permute-done | bytes 262176 | tf_op jit(solution)/shard_map/ppermute | solution.py:48
  200.6 5.7 %collective-permute-done.35 = bf16[512,256]{1,0:T(8,128)(2,1)S(1)} collective-permute-done((bf16[512,256]{1,0:T(8,128)(2,1)S(1)}, bf16[512,256]{1,0:T(8,128)(2,1)S(1)}, u32[]{:S(2)}, u32[]{:S(2)}) %collective-permute-start.35) | collective-permute-done | bytes 262176 | tf_op jit(solution)/shard_map/ppermute | solution.py:439
  206.3 1.7 collective-permute-start.36
  208.5 14.7 %collective-permute-done.33 = bf16[512,256]{1,0:T(8,128)(2,1)S(1)} collective-permute-done((bf16[512,256]{1,0:T(8,128)(2,1)S(1)}, bf16[512,256]{1,0:T(8,128)(2,1)S(1)}, u32[]{:S(2)}, u32[]{:S(2)}) %collective-permute-start.33) | collective-permute-done | bytes 262176 | tf_op jit(solution)/shard_map/ppermute | solution.py:439
  223.7 10.0 %collective-permute-done.34 = bf16[1024,256]{1,0:T(8,128)(2,1)S(1)} collective-permute-done((bf16[1024,256]{1,0:T(8,128)(2,1)S(1)}, bf16[1024,256]{1,0:T(8,128)(2,1)S(1)}, u32[]{:S(2)}, u32[]{:S(2)}) %collective-permute-start.34) | collective-permute-done | bytes 524320 | tf_op jit(solution)/shard_map/ppermute | solution.py:439
  234.5 1.3 collective-permute-start.40
  235.8 1.4 collective-permute-start.43
  237.2 1.3 collective-permute-start.44
  238.5 7.2 %collective-permute-done.40 = bf16[4,256,128]{2,1,0:T(8,128)(2,1)} collective-permute-done((bf16[4,256,128]{2,1,0:T(8,128)(2,1)S(1)}, bf16[4,256,128]{2,1,0:T(8,128)(2,1)}, u32[]{:S(2)}, u32[]{:S(2)}) %collective-permute-start.40) | collective-permute-done | bytes 262176 | tf_op jit(solution)/shard_map/ppermute | solution.py:48
  246.4 1.3 collective-permute-start.42
  247.7 5.8 %collective-permute-done.44 = bf16[4,256,128]{2,1,0:T(8,128)(2,1)} collective-permute-done((bf16[4,256,128]{2,1,0:T(8,128)(2,1)S(1)}, bf16[4,256,128]{2,1,0:T(8,128)(2,1)}, u32[]{:S(2)}, u32[]{:S(2)}) %collective-permute-start.44) | collective-permute-done | bytes 262176 | tf_op jit(solution)/shard_map/ppermute | solution.py:48
  253.4 1.4 collective-permute-start.45
  255.5 1.5 collective-permute-start.46
  257.0 0.9 copy.10.active_ref
  259.0 5.1 %collective-permute-done.46 = bf16[4,256,128]{2,1,0:T(8,128)(2,1)} collective-permute-done((bf16[4,256,128]{2,1,0:T(8,128)(2,1)}, bf16[4,256,128]{2,1,0:T(8,128)(2,1)}, u32[]{:S(2)}, u32[]{:S(2)}) %collective-permute-start.46) | collective-permute-done | bytes 262176 | tf_op jit(solution)/shard_map/ppermute | solution.py:48
  264.1 1.0 copy-done.6
  265.1 9.4 %shard_map.77 = bf16[512,1024]{1,0:T(8,128)(2,1)} custom-call(s32[5]{0:T(128)} %stack.33.me_ref, s32[16]{0:T(128)} %fusion.at_ref, s32[512,1]{1,0:T(8,128)} %copy.10.active_ref, bf16[512,1024]{1,0:T(8,128)(2,1)} %hidden_ref.1, bf16[2048,256]{1,0:T(8,128)(2,1)} %copy-done.1, bf16[2048,256]{1,0:T(8,128)(2,1)} %copy-done, ...), custom_call_target="tpu_custom_call" | custom-call | flops 2147483648 | bytes 8388608 | tf_op jit(solution)/shard_map/pallas_call | solution.py:338
  (146 shorter events, 13.9 us)
Async XLA Ops:
  1.3 54.0 %copy-start.4 = (bf16[128,1024]{1,0:T(8,128)(2,1)}, bf16[128,1024]{1,0:T(8,128)(2,1)S(1)}, u32[]{:S(2)}) copy-start(bf16[128,1024]{1,0:T(8,128)(2,1)S(1)} %get-tuple-element.48.refs_10_) | copy-start | bytes 786436
  1.3 54.0 %copy-start.5 = (bf16[128,1024]{1,0:T(8,128)(2,1)}, bf16[128,1024]{1,0:T(8,128)(2,1)S(1)}, u32[]{:S(2)}) copy-start(bf16[128,1024]{1,0:T(8,128)(2,1)S(1)} %get-tuple-element.49.refs_3_) | copy-start | bytes 786436
  1.3 66.5 %copy-start.2 = (bf16[128,1024]{1,0:T(8,128)(2,1)}, bf16[128,1024]{1,0:T(8,128)(2,1)S(1)}, u32[]{:S(2)}) copy-start(bf16[128,1024]{1,0:T(8,128)(2,1)S(1)} %get-tuple-element.33.refs_10_) | copy-start | bytes 786436
  1.3 66.5 %copy-start.3 = (bf16[128,1024]{1,0:T(8,128)(2,1)}, bf16[128,1024]{1,0:T(8,128)(2,1)S(1)}, u32[]{:S(2)}) copy-start(bf16[128,1024]{1,0:T(8,128)(2,1)S(1)} %get-tuple-element.26.refs_3_) | copy-start | bytes 786436
  1.3 12.1 %collective-permute-start = (bf16[128,1024]{1,0:T(8,128)(2,1)S(1)}, bf16[128,1024]{1,0:T(8,128)(2,1)S(1)}, u32[]{:S(2)}, u32[]{:S(2)}) collective-permute-start(bf16[128,1024]{1,0:T(8,128)(2,1)S(1)} %get-tuple-element.49.refs_3_), channel_id=1, source_target_pairs={{0,1},{1,2},{2,3},{4,5},{5,6},{6,7},{8,9},{9,10},{10,11},{12,13},{... | collective-permute-start | bytes 786440 | tf_op jit(solution)/shard_map/ppermute | solution.py:47
  6.3 9.9 %collective-permute-start.1 = (bf16[128,1024]{1,0:T(8,128)(2,1)S(1)}, bf16[128,1024]{1,0:T(8,128)(2,1)S(1)}, u32[]{:S(2)}, u32[]{:S(2)}) collective-permute-start(bf16[128,1024]{1,0:T(8,128)(2,1)S(1)} %get-tuple-element.49.refs_3_), channel_id=1, source_target_pairs={{1,0},{2,1},{3,2},{5,4},{6,5},{7,6},{9,8},{10,9},{11,10},{13,12},{... | collective-permute-start | bytes 786440 | tf_op jit(solution)/shard_map/ppermute | solution.py:48
  7.6 9.9 %collective-permute-start.8 = (bf16[128,1024]{1,0:T(8,128)(2,1)S(1)}, bf16[128,1024]{1,0:T(8,128)(2,1)S(1)}, u32[]{:S(2)}, u32[]{:S(2)}) collective-permute-start(bf16[128,1024]{1,0:T(8,128)(2,1)S(1)} %get-tuple-element.48.refs_10_), channel_id=1, source_target_pairs={{0,1},{1,2},{2,3},{4,5},{5,6},{6,7},{8,9},{9,10},{10,11},{12,13},{... | collective-permute-start | bytes 786440 | tf_op jit(solution)/shard_map/ppermute | solution.py:47
  12.1 10.1 %collective-permute-start.9 = (bf16[128,1024]{1,0:T(8,128)(2,1)S(1)}, bf16[128,1024]{1,0:T(8,128)(2,1)S(1)}, u32[]{:S(2)}, u32[]{:S(2)}) collective-permute-start(bf16[128,1024]{1,0:T(8,128)(2,1)S(1)} %get-tuple-element.48.refs_10_), channel_id=1, source_target_pairs={{1,0},{2,1},{3,2},{5,4},{6,5},{7,6},{9,8},{10,9},{11,10},{13,12},{... | collective-permute-start | bytes 786440 | tf_op jit(solution)/shard_map/ppermute | solution.py:48
  13.4 41.8 %copy-start.12 = (bf16[128,1024]{1,0:T(8,128)(2,1)}, bf16[128,1024]{1,0:T(8,128)(2,1)S(1)}, u32[]{:S(2)}) copy-start(bf16[128,1024]{1,0:T(8,128)(2,1)S(1)} %collective-permute-done.refs_4_) | copy-start | bytes 786436
  13.4 10.8 %collective-permute-start.2 = (bf16[128,1024]{1,0:T(8,128)(2,1)S(1)}, bf16[128,1024]{1,0:T(8,128)(2,1)S(1)}, u32[]{:S(2)}, u32[]{:S(2)}) collective-permute-start(bf16[128,1024]{1,0:T(8,128)(2,1)S(1)} %collective-permute-done.refs_4_), channel_id=1, source_target_pairs={{1,2},{2,3},{5,6},{6,7},{9,10},{10,11},{13,14},{14,15},{17,18},{18... | collective-permute-start | bytes 786440 | tf_op jit(solution)/shard_map/ppermute | solution.py:47
  16.2 39.1 %copy-start.13 = (bf16[128,1024]{1,0:T(8,128)(2,1)}, bf16[128,1024]{1,0:T(8,128)(2,1)S(1)}, u32[]{:S(2)}) copy-start(bf16[128,1024]{1,0:T(8,128)(2,1)S(1)} %collective-permute-done.1.refs_5_) | copy-start | bytes 786436
  16.2 11.9 %collective-permute-start.3 = (bf16[128,1024]{1,0:T(8,128)(2,1)S(1)}, bf16[128,1024]{1,0:T(8,128)(2,1)S(1)}, u32[]{:S(2)}, u32[]{:S(2)}) collective-permute-start(bf16[128,1024]{1,0:T(8,128)(2,1)S(1)} %collective-permute-done.1.refs_5_), channel_id=1, source_target_pairs={{1,0},{2,1},{5,4},{6,5},{9,8},{10,9},{13,12},{14,13},{17,16},{18,1... | collective-permute-start | bytes 786440 | tf_op jit(solution)/shard_map/ppermute | solution.py:48
  17.5 37.8 %copy-start.14 = (bf16[128,1024]{1,0:T(8,128)(2,1)}, bf16[128,1024]{1,0:T(8,128)(2,1)S(1)}, u32[]{:S(2)}) copy-start(bf16[128,1024]{1,0:T(8,128)(2,1)S(1)} %collective-permute-done.8.refs_11_) | copy-start | bytes 786436
  17.5 11.9 %collective-permute-start.10 = (bf16[128,1024]{1,0:T(8,128)(2,1)S(1)}, bf16[128,1024]{1,0:T(8,128)(2,1)S(1)}, u32[]{:S(2)}, u32[]{:S(2)}) collective-permute-start(bf16[128,1024]{1,0:T(8,128)(2,1)S(1)} %collective-permute-done.8.refs_11_), channel_id=1, source_target_pairs={{1,2},{2,3},{5,6},{6,7},{9,10},{10,11},{13,14},{14,15},{17,18},{18... | collective-permute-start | bytes 786440 | tf_op jit(solution)/shard_map/ppermute | solution.py:47
  22.2 12.4 %collective-permute-start.11 = (bf16[128,1024]{1,0:T(8,128)(2,1)S(1)}, bf16[128,1024]{1,0:T(8,128)(2,1)S(1)}, u32[]{:S(2)}, u32[]{:S(2)}) collective-permute-start(bf16[128,1024]{1,0:T(8,128)(2,1)S(1)} %collective-permute-done.9.refs_12_), channel_id=1, source_target_pairs={{1,0},{2,1},{5,4},{6,5},{9,8},{10,9},{13,12},{14,13},{17,16},{18,1... | collective-permute-start | bytes 786440 | tf_op jit(solution)/shard_map/ppermute | solution.py:48
  24.2 17.9 %collective-permute-start.4 = (bf16[128,1024]{1,0:T(8,128)(2,1)S(1)}, bf16[128,1024]{1,0:T(8,128)(2,1)S(1)}, u32[]{:S(2)}, u32[]{:S(2)}) collective-permute-start(bf16[128,1024]{1,0:T(8,128)(2,1)S(1)} %collective-permute-done.2.refs_6_), channel_id=1, source_target_pairs={{2,3},{6,7},{10,11},{14,15},{18,19},{22,23},{26,27},{30,31}} | collective-permute-start | bytes 786440 | tf_op jit(solution)/shard_map/ppermute | solution.py:47
  28.1 14.0 %collective-permute-start.5 = (bf16[128,1024]{1,0:T(8,128)(2,1)S(1)}, bf16[128,1024]{1,0:T(8,128)(2,1)}, u32[]{:S(2)}, u32[]{:S(2)}) collective-permute-start(bf16[128,1024]{1,0:T(8,128)(2,1)S(1)} %collective-permute-done.3.refs_7_), channel_id=1, source_target_pairs={{1,0},{5,4},{9,8},{13,12},{17,16},{21,20},{25,24},{29,28}} | collective-permute-start | bytes 786440 | tf_op jit(solution)/shard_map/ppermute | solution.py:48
  29.4 24.5 %collective-permute-start.12 = (bf16[128,1024]{1,0:T(8,128)(2,1)S(1)}, bf16[128,1024]{1,0:T(8,128)(2,1)}, u32[]{:S(2)}, u32[]{:S(2)}) collective-permute-start(bf16[128,1024]{1,0:T(8,128)(2,1)S(1)} %collective-permute-done.10.refs_13_), channel_id=1, source_target_pairs={{2,3},{6,7},{10,11},{14,15},{18,19},{22,23},{26,27},{30,31}} | collective-permute-start | bytes 786440 | tf_op jit(solution)/shard_map/ppermute | solution.py:47
  34.6 20.6 %collective-permute-start.13 = (bf16[128,1024]{1,0:T(8,128)(2,1)S(1)}, bf16[128,1024]{1,0:T(8,128)(2,1)}, u32[]{:S(2)}, u32[]{:S(2)}) collective-permute-start(bf16[128,1024]{1,0:T(8,128)(2,1)S(1)} %collective-permute-done.11.refs_14_), channel_id=1, source_target_pairs={{1,0},{5,4},{9,8},{13,12},{17,16},{21,20},{25,24},{29,28}} | collective-permute-start | bytes 786440 | tf_op jit(solution)/shard_map/ppermute | solution.py:48
  42.8 25.0 %collective-permute-start.18 = (bf16[128,1024]{1,0:T(8,128)(2,1)S(1)}, bf16[128,1024]{1,0:T(8,128)(2,1)S(1)}, u32[]{:S(2)}, u32[]{:S(2)}) collective-permute-start(bf16[128,1024]{1,0:T(8,128)(2,1)S(1)} %get-tuple-element.33.refs_10_), channel_id=1, source_target_pairs={{0,1},{1,2},{2,3},{4,5},{5,6},{6,7},{8,9},{9,10},{10,11},{12,13},{... | collective-permute-start | bytes 786440 | tf_op jit(solution)/shard_map/ppermute | solution.py:47
  48.1 20.5 %collective-permute-start.19 = (bf16[128,1024]{1,0:T(8,128)(2,1)S(1)}, bf16[128,1024]{1,0:T(8,128)(2,1)S(1)}, u32[]{:S(2)}, u32[]{:S(2)}) collective-permute-start(bf16[128,1024]{1,0:T(8,128)(2,1)S(1)} %get-tuple-element.33.refs_10_), channel_id=1, source_target_pairs={{1,0},{2,1},{3,2},{5,4},{6,5},{7,6},{9,8},{10,9},{11,10},{13,12},{... | collective-permute-start | bytes 786440 | tf_op jit(solution)/shard_map/ppermute | solution.py:48
  49.4 18.4 %collective-permute-start.6 = (bf16[128,1024]{1,0:T(8,128)(2,1)S(1)}, bf16[128,1024]{1,0:T(8,128)(2,1)S(1)}, u32[]{:S(2)}, u32[]{:S(2)}) collective-permute-start(bf16[128,1024]{1,0:T(8,128)(2,1)S(1)} %get-tuple-element.26.refs_3_), channel_id=1, source_target_pairs={{0,1},{1,2},{2,3},{4,5},{5,6},{6,7},{8,9},{9,10},{10,11},{12,13},{... | collective-permute-start | bytes 786440 | tf_op jit(solution)/shard_map/ppermute | solution.py:47
  53.9 13.9 %collective-permute-start.7 = (bf16[128,1024]{1,0:T(8,128)(2,1)S(1)}, bf16[128,1024]{1,0:T(8,128)(2,1)}, u32[]{:S(2)}, u32[]{:S(2)}) collective-permute-start(bf16[128,1024]{1,0:T(8,128)(2,1)S(1)} %get-tuple-element.26.refs_3_), channel_id=1, source_target_pairs={{1,0},{2,1},{3,2},{5,4},{6,5},{7,6},{9,8},{10,9},{11,10},{13,12},{... | collective-permute-start | bytes 786440 | tf_op jit(solution)/shard_map/ppermute | solution.py:48
  67.8 4.0 %collective-permute-start.20 = (bf16[128,1024]{1,0:T(8,128)(2,1)S(1)}, bf16[128,1024]{1,0:T(8,128)(2,1)S(1)}, u32[]{:S(2)}, u32[]{:S(2)}) collective-permute-start(bf16[128,1024]{1,0:T(8,128)(2,1)S(1)} %collective-permute-done.18.refs_11_), channel_id=1, source_target_pairs={{1,2},{2,3},{5,6},{6,7},{9,10},{10,11},{13,14},{14,15},{17,18},{18... | collective-permute-start | bytes 786440 | tf_op jit(solution)/shard_map/ppermute | solution.py:47
  68.5 12.4 %collective-permute-start.21 = (bf16[128,1024]{1,0:T(8,128)(2,1)S(1)}, bf16[128,1024]{1,0:T(8,128)(2,1)S(1)}, u32[]{:S(2)}, u32[]{:S(2)}) collective-permute-start(bf16[128,1024]{1,0:T(8,128)(2,1)S(1)} %collective-permute-done.19.refs_12_), channel_id=1, source_target_pairs={{1,0},{2,1},{5,4},{6,5},{9,8},{10,9},{13,12},{14,13},{17,16},{18,1... | collective-permute-start | bytes 786440 | tf_op jit(solution)/shard_map/ppermute | solution.py:48
  69.8 12.4 %collective-permute-start.14 = (bf16[128,1024]{1,0:T(8,128)(2,1)S(1)}, bf16[128,1024]{1,0:T(8,128)(2,1)S(1)}, u32[]{:S(2)}, u32[]{:S(2)}) collective-permute-start(bf16[128,1024]{1,0:T(8,128)(2,1)S(1)} %collective-permute-done.6.refs_4_), channel_id=1, source_target_pairs={{1,2},{2,3},{5,6},{6,7},{9,10},{10,11},{13,14},{14,15},{17,18},{18... | collective-permute-start | bytes 786440 | tf_op jit(solution)/shard_map/ppermute | solution.py:47
  70.5 16.6 %collective-permute-start.15 = (bf16[128,1024]{1,0:T(8,128)(2,1)}, bf16[128,1024]{1,0:T(8,128)(2,1)S(1)}, u32[]{:S(2)}, u32[]{:S(2)}) collective-permute-start(bf16[128,1024]{1,0:T(8,128)(2,1)} %collective-permute-done.7.refs_5_), channel_id=1, source_target_pairs={{1,0},{2,1},{5,4},{6,5},{9,8},{10,9},{13,12},{14,13},{17,16},{18,1... | collective-permute-start | bytes 786440 | tf_op jit(solution)/shard_map/ppermute | solution.py:48
  71.8 17.4 %collective-permute-start.22 = (bf16[128,1024]{1,0:T(8,128)(2,1)S(1)}, bf16[128,1024]{1,0:T(8,128)(2,1)S(1)}, u32[]{:S(2)}, u32[]{:S(2)}) collective-permute-start(bf16[128,1024]{1,0:T(8,128)(2,1)S(1)} %collective-permute-done.20.refs_13_), channel_id=1, source_target_pairs={{2,3},{6,7},{10,11},{14,15},{18,19},{22,23},{26,27},{30,31}} | collective-permute-start | bytes 786440 | tf_op jit(solution)/shard_map/ppermute | solution.py:47
  81.0 11.1 %collective-permute-start.23 = (bf16[128,1024]{1,0:T(8,128)(2,1)S(1)}, bf16[128,1024]{1,0:T(8,128)(2,1)S(1)}, u32[]{:S(2)}, u32[]{:S(2)}) collective-permute-start(bf16[128,1024]{1,0:T(8,128)(2,1)S(1)} %collective-permute-done.21.refs_14_), channel_id=1, source_target_pairs={{1,0},{5,4},{9,8},{13,12},{17,16},{21,20},{25,24},{29,28}} | collective-permute-start | bytes 786440 | tf_op jit(solution)/shard_map/ppermute | solution.py:48
  82.3 9.8 %collective-permute-start.16 = (bf16[128,1024]{1,0:T(8,128)(2,1)S(1)}, bf16[128,1024]{1,0:T(8,128)(2,1)S(1)}, u32[]{:S(2)}, u32[]{:S(2)}) collective-permute-start(bf16[128,1024]{1,0:T(8,128)(2,1)S(1)} %collective-permute-done.14.refs_6_), channel_id=1, source_target_pairs={{2,3},{6,7},{10,11},{14,15},{18,19},{22,23},{26,27},{30,31}} | collective-permute-start | bytes 786440 | tf_op jit(solution)/shard_map/ppermute | solution.py:47
  87.1 8.3 %collective-permute-start.17 = (bf16[128,1024]{1,0:T(8,128)(2,1)S(1)}, bf16[128,1024]{1,0:T(8,128)(2,1)S(1)}, u32[]{:S(2)}, u32[]{:S(2)}) collective-permute-start(bf16[128,1024]{1,0:T(8,128)(2,1)S(1)} %collective-permute-done.15.refs_7_), channel_id=1, source_target_pairs={{1,0},{5,4},{9,8},{13,12},{17,16},{21,20},{25,24},{29,28}} | collective-permute-start | bytes 786440 | tf_op jit(solution)/shard_map/ppermute | solution.py:48
  89.2 51.8 %copy-start.40 = (bf16[2,128,256]{2,1,0:T(8,128)(2,1)S(1)}, bf16[2,128,256]{2,1,0:T(8,128)(2,1)}, u32[]{:S(2)}) copy-start(bf16[2,128,256]{2,1,0:T(8,128)(2,1)} %get-tuple-element.37) | copy-start | bytes 393220
  124.8 16.1 %all-to-all-start.1 = ((bf16[8,128,384]{2,1,0:T(8,128)(2,1)}), bf16[8,128,384]{2,1,0:T(8,128)(2,1)S(1)}, u32[]{:S(2)}, u32[]{:S(2)}) async-start(bf16[8,128,384]{2,1,0:T(8,128)(2,1)} %shard_map.73), calls=%async_computation.1 | async-start | bytes 1572864 | tf_op jit(solution)/shard_map/all_to_all | solution.py:486
  128.4 71.4 %copy-start.11 = (bf16[2,128,256]{2,1,0:T(8,128)(2,1)S(1)}, bf16[2,128,256]{2,1,0:T(8,128)(2,1)}, u32[]{:S(2)}) copy-start(bf16[2,128,256]{2,1,0:T(8,128)(2,1)} %get-tuple-element.43) | copy-start | bytes 393220
  128.4 25.7 %collective-permute-start.24 = (bf16[8,128,384]{2,1,0:T(8,128)(2,1)S(1)}, bf16[8,128,384]{2,1,0:T(8,128)(2,1)S(1)}, u32[]{:S(2)}, u32[]{:S(2)}) collective-permute-start(bf16[8,128,384]{2,1,0:T(8,128)(2,1)S(1)} %all_to_all.15.refs_2_), channel_id=1, source_target_pairs={{0,4},{4,0},{8,12},{12,8},{16,20},{20,16},{24,28},{28,24},{1,5},{5... | collective-permute-start | bytes 2359304 | tf_op jit(solution)/shard_map/ppermute | solution.py:490
  140.9 13.2 %collective-permute-start.28 = (bf16[8,128,384]{2,1,0:T(8,128)(2,1)S(1)}, bf16[8,128,384]{2,1,0:T(8,128)(2,1)S(1)}, u32[]{:S(2)}, u32[]{:S(2)}) collective-permute-start(bf16[8,128,384]{2,1,0:T(8,128)(2,1)S(1)} %all-to-all-done.1.refs_0_), channel_id=1, source_target_pairs={{0,4},{4,0},{8,12},{12,8},{16,20},{20,16},{24,28},{28,24},{1,5},{5... | collective-permute-start | bytes 2359304 | tf_op jit(solution)/shard_map/ppermute | solution.py:490
  140.9 8.4 %collective-permute-start.25 = (bf16[2,128,256]{2,1,0:T(8,128)(2,1)}, bf16[2,128,256]{2,1,0:T(8,128)(2,1)S(1)}, u32[]{:S(2)}, u32[]{:S(2)}) collective-permute-start(bf16[2,128,256]{2,1,0:T(8,128)(2,1)} %get-tuple-element.35), channel_id=1, source_target_pairs={{0,1},{1,2},{2,3},{3,0},{4,5},{5,6},{6,7},{7,4},{8,9},{9,10},{10,1... | collective-permute-start | bytes 393224 | tf_op jit(solution)/shard_map/ppermute | solution.py:416
  140.9 13.1 %collective-permute-start.26 = (bf16[2,128,256]{2,1,0:T(8,128)(2,1)}, bf16[2,128,256]{2,1,0:T(8,128)(2,1)S(1)}, u32[]{:S(2)}, u32[]{:S(2)}) collective-permute-start(bf16[2,128,256]{2,1,0:T(8,128)(2,1)} %get-tuple-element.36), channel_id=1, source_target_pairs={{0,2},{1,3},{2,0},{3,1},{4,6},{5,7},{6,4},{7,5},{8,10},{9,11},{10,... | collective-permute-start | bytes 393224 | tf_op jit(solution)/shard_map/ppermute | solution.py:416
  141.0 13.1 %collective-permute-start.27 = (bf16[2,128,256]{2,1,0:T(8,128)(2,1)S(1)}, bf16[2,128,256]{2,1,0:T(8,128)(2,1)S(1)}, u32[]{:S(2)}, u32[]{:S(2)}) collective-permute-start(bf16[2,128,256]{2,1,0:T(8,128)(2,1)S(1)} %copy-done.40), channel_id=1, source_target_pairs={{0,3},{1,0},{2,1},{3,2},{4,7},{5,4},{6,5},{7,6},{8,11},{9,8},{10,9... | collective-permute-start | bytes 393224 | tf_op jit(solution)/shard_map/ppermute | solution.py:416
  180.3 53.4 %copy-start.8 = (bf16[4,256,128]{2,1,0:T(8,128)(2,1)}, bf16[4,256,128]{2,1,0:T(8,128)(2,1)S(1)}, u32[]{:S(2)}) copy-start(bf16[4,256,128]{2,1,0:T(8,128)(2,1)S(1)} %get-tuple-element.52) | copy-start | bytes 786436
  180.3 83.8 %copy-start.7 = (bf16[4,256,128]{2,1,0:T(8,128)(2,1)}, bf16[4,256,128]{2,1,0:T(8,128)(2,1)S(1)}, u32[]{:S(2)}) copy-start(bf16[4,256,128]{2,1,0:T(8,128)(2,1)S(1)} %get-tuple-element.51) | copy-start | bytes 786436
  180.3 12.0 %collective-permute-start.29 = (bf16[4,256,128]{2,1,0:T(8,128)(2,1)S(1)}, bf16[4,256,128]{2,1,0:T(8,128)(2,1)S(1)}, u32[]{:S(2)}, u32[]{:S(2)}) collective-permute-start(bf16[4,256,128]{2,1,0:T(8,128)(2,1)S(1)} %get-tuple-element.52), channel_id=1, source_target_pairs={{0,1},{1,2},{2,3},{4,5},{5,6},{6,7},{8,9},{9,10},{10,11},{12,13},{... | collective-permute-start | bytes 786440 | tf_op jit(solution)/shard_map/ppermute | solution.py:47
  185.1 9.2 %collective-permute-start.30 = (bf16[4,256,128]{2,1,0:T(8,128)(2,1)S(1)}, bf16[4,256,128]{2,1,0:T(8,128)(2,1)S(1)}, u32[]{:S(2)}, u32[]{:S(2)}) collective-permute-start(bf16[4,256,128]{2,1,0:T(8,128)(2,1)S(1)} %get-tuple-element.52), channel_id=1, source_target_pairs={{1,0},{2,1},{3,2},{5,4},{6,5},{7,6},{9,8},{10,9},{11,10},{13,12},{... | collective-permute-start | bytes 786440 | tf_op jit(solution)/shard_map/ppermute | solution.py:48
  186.4 9.2 %collective-permute-start.31 = (bf16[4,256,128]{2,1,0:T(8,128)(2,1)S(1)}, bf16[4,256,128]{2,1,0:T(8,128)(2,1)S(1)}, u32[]{:S(2)}, u32[]{:S(2)}) collective-permute-start(bf16[4,256,128]{2,1,0:T(8,128)(2,1)S(1)} %get-tuple-element.51), channel_id=1, source_target_pairs={{0,1},{1,2},{2,3},{4,5},{5,6},{6,7},{8,9},{9,10},{10,11},{12,13},{... | collective-permute-start | bytes 786440 | tf_op jit(solution)/shard_map/ppermute | solution.py:47
  191.0 8.8 %collective-permute-start.32 = (bf16[4,256,128]{2,1,0:T(8,128)(2,1)S(1)}, bf16[4,256,128]{2,1,0:T(8,128)(2,1)S(1)}, u32[]{:S(2)}, u32[]{:S(2)}) collective-permute-start(bf16[4,256,128]{2,1,0:T(8,128)(2,1)S(1)} %get-tuple-element.51), channel_id=1, source_target_pairs={{1,0},{2,1},{3,2},{5,4},{6,5},{7,6},{9,8},{10,9},{11,10},{13,12},{... | collective-permute-start | bytes 786440 | tf_op jit(solution)/shard_map/ppermute | solution.py:48
  192.3 41.5 %copy-start.32 = (bf16[4,256,128]{2,1,0:T(8,128)(2,1)}, bf16[4,256,128]{2,1,0:T(8,128)(2,1)S(1)}, u32[]{:S(2)}) copy-start(bf16[4,256,128]{2,1,0:T(8,128)(2,1)S(1)} %collective-permute-done.29) | copy-start | bytes 786436
  194.4 42.8 %copy-start.33 = (bf16[4,256,128]{2,1,0:T(8,128)(2,1)}, bf16[4,256,128]{2,1,0:T(8,128)(2,1)S(1)}, u32[]{:S(2)}) copy-start(bf16[4,256,128]{2,1,0:T(8,128)(2,1)S(1)} %collective-permute-done.30) | copy-start | bytes 786436
  195.6 50.0 %copy-start.34 = (bf16[4,256,128]{2,1,0:T(8,128)(2,1)}, bf16[4,256,128]{2,1,0:T(8,128)(2,1)S(1)}, u32[]{:S(2)}) copy-start(bf16[4,256,128]{2,1,0:T(8,128)(2,1)S(1)} %collective-permute-done.31) | copy-start | bytes 786436
  199.8 46.6 %copy-start.35 = (bf16[4,256,128]{2,1,0:T(8,128)(2,1)}, bf16[4,256,128]{2,1,0:T(8,128)(2,1)S(1)}, u32[]{:S(2)}) copy-start(bf16[4,256,128]{2,1,0:T(8,128)(2,1)S(1)} %collective-permute-done.32) | copy-start | bytes 786436
  199.9 6.4 %collective-permute-start.35 = (bf16[512,256]{1,0:T(8,128)(2,1)S(1)}, bf16[512,256]{1,0:T(8,128)(2,1)S(1)}, u32[]{:S(2)}, u32[]{:S(2)}) collective-permute-start(bf16[512,256]{1,0:T(8,128)(2,1)S(1)} %pad_maximum_fusion.1), channel_id=1, source_target_pairs={{0,16},{4,20},{8,24},{12,28},{16,0},{20,4},{24,8},{28,12},{1,17},{... | collective-permute-start | bytes 786440 | tf_op jit(solution)/shard_map/ppermute | solution.py:439
  206.3 17.2 %collective-permute-start.36 = (bf16[1024,256]{1,0:T(8,128)(2,1)S(1)}, bf16[1024,256]{1,0:T(8,128)(2,1)S(1)}, u32[]{:S(2)}, u32[]{:S(2)}) collective-permute-start(bf16[1024,256]{1,0:T(8,128)(2,1)S(1)} %constant_dynamic-update-slice_fusion.11), channel_id=1, source_target_pairs={{0,8},{4,12},{8,0},{12,4},{16,24},{20,28},{24,16},{28,20},{1,9},{5... | collective-permute-start | bytes 1572872 | tf_op jit(solution)/shard_map/ppermute | solution.py:439
  208.0 15.2 %collective-permute-start.33 = (bf16[512,256]{1,0:T(8,128)(2,1)S(1)}, bf16[512,256]{1,0:T(8,128)(2,1)S(1)}, u32[]{:S(2)}, u32[]{:S(2)}) collective-permute-start(bf16[512,256]{1,0:T(8,128)(2,1)S(1)} %pad_maximum_fusion), channel_id=1, source_target_pairs={{0,8},{4,12},{8,0},{12,4},{16,24},{20,28},{24,16},{28,20},{1,9},{5... | collective-permute-start | bytes 786440 | tf_op jit(solution)/shard_map/ppermute | solution.py:439
  223.3 10.4 %collective-permute-start.34 = (bf16[1024,256]{1,0:T(8,128)(2,1)S(1)}, bf16[1024,256]{1,0:T(8,128)(2,1)S(1)}, u32[]{:S(2)}, u32[]{:S(2)}) collective-permute-start(bf16[1024,256]{1,0:T(8,128)(2,1)S(1)} %get-tuple-element.53), channel_id=1, source_target_pairs={{0,16},{4,20},{8,24},{12,28},{16,0},{20,4},{24,8},{28,12},{1,17},{... | collective-permute-start | bytes 1572872 | tf_op jit(solution)/shard_map/ppermute | solution.py:439
  223.6 40.5 %copy-start = (bf16[2048,256]{1,0:T(8,128)(2,1)}, bf16[2048,256]{1,0:T(8,128)(2,1)S(1)}, u32[]{:S(2)}) copy-start(bf16[2048,256]{1,0:T(8,128)(2,1)S(1)} %slice_dynamic-update-slice_fusion.refs_1_) | copy-start | bytes 3145732
  223.6 40.5 %collective-permute-start.38 = (bf16[2048,256]{1,0:T(8,128)(2,1)S(1)}, bf16[2048,256]{1,0:T(8,128)(2,1)S(1)}, u32[]{:S(2)}, u32[]{:S(2)}) collective-permute-start(bf16[2048,256]{1,0:T(8,128)(2,1)S(1)} %slice_dynamic-update-slice_fusion.refs_1_), channel_id=1, source_target_pairs={{0,4},{4,0},{8,12},{12,8},{16,20},{20,16},{24,28},{28,24},{1,5},{5... | collective-permute-start | bytes 3145736 | tf_op jit(solution)/shard_map/ppermute | solution.py:447
  233.7 30.4 %collective-permute-start.37 = (bf16[2048,256]{1,0:T(8,128)(2,1)S(1)}, bf16[2048,256]{1,0:T(8,128)(2,1)}, u32[]{:S(2)}, u32[]{:S(2)}) collective-permute-start(bf16[2048,256]{1,0:T(8,128)(2,1)S(1)} %constant_dynamic-update-slice_fusion.5.refs_0_), channel_id=1, source_target_pairs={{0,4},{4,0},{8,12},{12,8},{16,20},{20,16},{24,28},{28,24},{1,5},{5... | collective-permute-start | bytes 3145736 | tf_op jit(solution)/shard_map/ppermute | solution.py:447
  233.8 3.4 %collective-permute-start.39 = (bf16[4,256,128]{2,1,0:T(8,128)(2,1)S(1)}, bf16[4,256,128]{2,1,0:T(8,128)(2,1)S(1)}, u32[]{:S(2)}, u32[]{:S(2)}) collective-permute-start(bf16[4,256,128]{2,1,0:T(8,128)(2,1)S(1)} %collective-permute-done.29), channel_id=1, source_target_pairs={{1,2},{2,3},{5,6},{6,7},{9,10},{10,11},{13,14},{14,15},{17,18},{18... | collective-permute-start | bytes 786440 | tf_op jit(solution)/shard_map/ppermute | solution.py:47
  234.5 11.2 %collective-permute-start.40 = (bf16[4,256,128]{2,1,0:T(8,128)(2,1)S(1)}, bf16[4,256,128]{2,1,0:T(8,128)(2,1)}, u32[]{:S(2)}, u32[]{:S(2)}) collective-permute-start(bf16[4,256,128]{2,1,0:T(8,128)(2,1)S(1)} %collective-permute-done.30), channel_id=1, source_target_pairs={{1,0},{2,1},{5,4},{6,5},{9,8},{10,9},{13,12},{14,13},{17,16},{18,1... | collective-permute-start | bytes 786440 | tf_op jit(solution)/shard_map/ppermute | solution.py:48
  235.8 10.5 %collective-permute-start.43 = (bf16[4,256,128]{2,1,0:T(8,128)(2,1)S(1)}, bf16[4,256,128]{2,1,0:T(8,128)(2,1)}, u32[]{:S(2)}, u32[]{:S(2)}) collective-permute-start(bf16[4,256,128]{2,1,0:T(8,128)(2,1)S(1)} %collective-permute-done.31), channel_id=1, source_target_pairs={{1,2},{2,3},{5,6},{6,7},{9,10},{10,11},{13,14},{14,15},{17,18},{18... | collective-permute-start | bytes 786440 | tf_op jit(solution)/shard_map/ppermute | solution.py:47
  237.2 16.2 %collective-permute-start.44 = (bf16[4,256,128]{2,1,0:T(8,128)(2,1)S(1)}, bf16[4,256,128]{2,1,0:T(8,128)(2,1)}, u32[]{:S(2)}, u32[]{:S(2)}) collective-permute-start(bf16[4,256,128]{2,1,0:T(8,128)(2,1)S(1)} %collective-permute-done.32), channel_id=1, source_target_pairs={{1,0},{2,1},{5,4},{6,5},{9,8},{10,9},{13,12},{14,13},{17,16},{18,1... | collective-permute-start | bytes 786440 | tf_op jit(solution)/shard_map/ppermute | solution.py:48
  245.7 9.1 %collective-permute-start.41 = (bf16[4,256,128]{2,1,0:T(8,128)(2,1)S(1)}, bf16[4,256,128]{2,1,0:T(8,128)(2,1)S(1)}, u32[]{:S(2)}, u32[]{:S(2)}) collective-permute-start(bf16[4,256,128]{2,1,0:T(8,128)(2,1)S(1)} %collective-permute-done.39), channel_id=1, source_target_pairs={{2,3},{6,7},{10,11},{14,15},{18,19},{22,23},{26,27},{30,31}} | collective-permute-start | bytes 786440 | tf_op jit(solution)/shard_map/ppermute | solution.py:47
  246.4 12.7 %collective-permute-start.42 = (bf16[4,256,128]{2,1,0:T(8,128)(2,1)}, bf16[4,256,128]{2,1,0:T(8,128)(2,1)}, u32[]{:S(2)}, u32[]{:S(2)}) collective-permute-start(bf16[4,256,128]{2,1,0:T(8,128)(2,1)} %collective-permute-done.40), channel_id=1, source_target_pairs={{1,0},{5,4},{9,8},{13,12},{17,16},{21,20},{25,24},{29,28}} | collective-permute-start | bytes 786440 | tf_op jit(solution)/shard_map/ppermute | solution.py:48
  253.4 5.6 %collective-permute-start.45 = (bf16[4,256,128]{2,1,0:T(8,128)(2,1)}, bf16[4,256,128]{2,1,0:T(8,128)(2,1)}, u32[]{:S(2)}, u32[]{:S(2)}) collective-permute-start(bf16[4,256,128]{2,1,0:T(8,128)(2,1)} %collective-permute-done.43), channel_id=1, source_target_pairs={{2,3},{6,7},{10,11},{14,15},{18,19},{22,23},{26,27},{30,31}} | collective-permute-start | bytes 786440 | tf_op jit(solution)/shard_map/ppermute | solution.py:47
  255.5 8.6 %collective-permute-start.46 = (bf16[4,256,128]{2,1,0:T(8,128)(2,1)}, bf16[4,256,128]{2,1,0:T(8,128)(2,1)}, u32[]{:S(2)}, u32[]{:S(2)}) collective-permute-start(bf16[4,256,128]{2,1,0:T(8,128)(2,1)} %collective-permute-done.44), channel_id=1, source_target_pairs={{1,0},{5,4},{9,8},{13,12},{17,16},{21,20},{25,24},{29,28}} | collective-permute-start | bytes 786440 | tf_op jit(solution)/shard_map/ppermute | solution.py:48
  (25 other events, 348.4 us)

commit v6 on v5

--- a/solution.py
+++ b/solution.py
@@ -29,10 +29,10 @@
         pl.when(there)(act)
 
 
-def line_gather(chunks, count, between=None):
+def line_gather(chunks, count, join=None):
     right = [(d, d + 1) for d in range(count - 1)]
     left = [(d + 1, d) for d in range(count - 1)]
-    found, made = [], None
+    found = []
     for first in range(0, len(chunks), 2):
         pair = []
         for chunk in chunks[first : first + 2]:
@@ -41,16 +41,14 @@
             pair.append([chunk])
         last = [(chunk[0], chunk[0]) for chunk in pair]
         for step in range(count - 1):
+            if join is not None:
+                last = join(first, step, last, found)
             for at in range(len(pair)):
-                if step == 1 and at == 0 and made is not None:
-                    last[at], _ = lax.optimization_barrier((last[at], made))
                 from_left = lax.ppermute(last[at][0], "tensor", right[step:])
                 from_right = lax.ppermute(last[at][1], "tensor", left[: count - 1 - step])
                 last[at] = (from_left, from_right)
                 pair[at] += [from_left, from_right]
         found += pair
-        if between is not None and first + 2 < len(chunks):
-            made = between(pair)
     return found
 
 
@@ -417,38 +415,33 @@
     return shares
 
 
-def output_weight(w_out, shares, seq_count, tensor_count, columns, after):
+def swap(held, flips):
+    grown = []
+    for blocks, flip in zip(held, flips):
+        pairs = [(d, d ^ flip) for d in range(lax.axis_size("seq"))]
+        sent = list(blocks)
+        whole = [blocks[k] for k in sent]
+        got = lax.ppermute(
+            jnp.concatenate(whole, axis=0) if len(whole) > 1 else whole[0], "seq", pairs
+        )
+        grown.append(dict(blocks))
+        for k, block in zip(sent, jnp.split(got, len(sent))):
+            grown[-1][k ^ flip] = block
+    return grown
+
+
+def output_order(w_out, seq_count, tensor_count, columns):
     heads, cuts, halves, each = weight_cuts(w_out, seq_count, columns)
     row = jnp.arange(tensor_count * heads, dtype=jnp.int32)
-    if shares is None:
-        weight = lax.all_to_all(w_out, "tensor", split_axis=1, concat_axis=0, tiled=True)
-        return [weight], [jnp.int32(0)], row
+    if each % HEAD:
+        return [jnp.int32(0)], row
     seq_me = lax.axis_index("seq").astype(jnp.int32)
     me = lax.axis_index("tensor").astype(jnp.int32)
-    head, cut = seq_me // cuts, seq_me % cuts
-    flips = []
-    while cuts << len(flips) < seq_count:
-        flips.append(cuts << len(flips))
-    shares, _ = lax.optimization_barrier((shares, after))
-    weights, which = [], []
-    for half in range(halves):
-        held = {0: jnp.concatenate([share[half] for share in shares], axis=0)}
-        for flip in flips if half == 0 else flips[::-1]:
-            pairs = [(d, d ^ flip) for d in range(seq_count)]
-            sent = list(held)
-            got = lax.ppermute(jnp.concatenate([held[k] for k in sent], axis=0), "seq", pairs)
-            for k, block in zip(sent, jnp.split(got, len(sent))):
-                held[k ^ flip] = block
-        weights.append(jnp.concatenate([held[k] for k in sorted(held)], axis=0))
-        which.append(cut * halves + half)
-    for step in range(1, cuts):
-        ring = [(d, d - d % cuts + (d - step) % cuts) for d in range(seq_count)]
-        for half in range(halves):
-            weights.append(lax.ppermute(weights[half], "seq", ring))
-            which.append((cut + step) % cuts * halves + half)
+    which = [
+        (seq_me % cuts + step) % cuts * halves + half for step in range(cuts) for half in range(halves)
+    ]
     tensor, of = row // heads, row % heads
-    at = (of ^ head) * tensor_count + (me - tensor) % tensor_count
-    return weights, which, at
+    return which, (of ^ (seq_me // cuts)) * tensor_count + (me - tensor) % tensor_count
 
 
 def shards(hidden, depth, norm_gain, w_query, w_key, w_value, w_out):
@@ -467,35 +460,73 @@
     shares = weight_shares(w_out, seq_count, tensor_count, columns)
 
     def work(found):
-        first = sum(count for count, _ in made)
+        first = chunks - len(found) if made else 0
         here = active[first * chunk_rows : (first + len(found)) * chunk_rows]
-        sent = project(
+        return project(
             me.reshape(1), sum(found, []), here, gain, w_query, w_key, w_value, seq_count, group
         )
-        made.append((len(found), sent))
-        return sent, shares
+
+    def to_heads(sent):
+        return lax.all_to_all(sent, "seq", split_axis=0, concat_axis=0)
+
+    def to_parts(got):
+        rings = [
+            [(d, d - d % group + (d - step) % group) for d in range(seq_count)]
+            for step in range(1, group)
+        ]
+        return [got] + [lax.ppermute(got, "seq", ring) for ring in rings]
+
+    def first_pair(first, step, last, found):
+        if first == 2 and step == 1:
+            last, sent, _ = lax.optimization_barrier((last, work(found[:2]), shares))
+            made.append(to_heads(sent))
+        if first == 2 and step == 2:
+            got, last = lax.optimization_barrier((made.pop(), last))
+            made.extend(to_parts(got))
+        return last
 
     gathered = line_gather(
-        [hidden[c * chunk_rows : (c + 1) * chunk_rows] for c in range(chunks)], tensor_count, work
+        [hidden[c * chunk_rows : (c + 1) * chunk_rows] for c in range(chunks)],
+        tensor_count,
+        first_pair,
     )
-    rest = gathered[sum(count for count, _ in made) :]
+    rest = gathered[-2:]
     sending = send_shares(shares, tensor_count, rest[-1])
-    work(rest)
-    pieces = []
-    for _, sent in made:
-        got = lax.all_to_all(sent, "seq", split_axis=0, concat_axis=0)
-        pieces.append(got)
-        for step in range(1, group):
-            ring = [(d, d - d % group + (d - step) % group) for d in range(seq_count)]
-            pieces.append(lax.ppermute(got, "seq", ring))
-
-    pieces[-1], sending = lax.optimization_barrier((pieces[-1], sending))
+    sent = work(rest)
+    sent, sending, made = lax.optimization_barrier((sent, sending, made))
+    pieces = list(made) + to_parts(to_heads(sent))
+
+    heads, cuts, halves, _ = weight_cuts(w_out, seq_count, columns)
+    held, flips = [], []
+    if sending is not None:
+        held = [
+            {0: jnp.concatenate([share[half] for share in sending], axis=0)}
+            for half in range(halves)
+        ]
+        while cuts << len(flips) < seq_count:
+            flips.append(cuts << len(flips))
+        held = swap(held, [flips[0], flips[-1]])
     out = attend(part, pieces, chunks, group, rows)
+    out, held = lax.optimization_barrier((out, held))
     home = lax.all_to_all(out, "seq", split_axis=0, concat_axis=0)
-    found = line_gather([home[: seq_count // 2], home[seq_count // 2 :]], tensor_count)
-    weights, cut_of, at = output_weight(
-        w_out, sending, seq_count, tensor_count, columns, [pieces[1:3] for pieces in found]
-    )
+    home, held = lax.optimization_barrier((home, held))
+
+    def spread(first, step, last, found):
+        nonlocal held
+        if held and 0 < step < len(flips):
+            last, held = lax.optimization_barrier(
+                (last, swap(held, [flips[step], flips[-1 - step]]))
+            )
+        return last
+
+    found = line_gather([home[: seq_count // 2], home[seq_count // 2 :]], tensor_count, spread)
+    weights = [jnp.concatenate([blocks[k] for k in sorted(blocks)], axis=0) for blocks in held]
+    for turn in range(1, cuts):
+        ring = [(d, d - d % cuts + (d - turn) % cuts) for d in range(seq_count)]
+        weights += [lax.ppermute(weights[half], "seq", ring) for half in range(len(held))]
+    if not held:
+        weights = [lax.all_to_all(w_out, "tensor", split_axis=1, concat_axis=0, tiled=True)]
+    cut_of, at = output_order(w_out, seq_count, tensor_count, columns)
     scalars = jnp.stack([me, *cut_of])
     return output(scalars, at, sum(found, []), weights, hidden, active, chunks, group, 2)
 

time: 276 us -> 233 us (0.84)
  waiting for transfers between devices: 109 us -> 66.8 us
    ppermute x8, waiting for transfers between devices: 30.5 us -> 5.49 us  [the longest x4 4.57 us: swap(): lax.ppermute(jnp.concatenate(whole, axis=0) if len(whole) > 1 else whole[...]
    all_to_all x1, waiting for transfers between devices: 12.1 us -> 0.01 us  [to_heads(): return lax.all_to_all(sent, 'seq', split_axis=0, concat_axis=0)]
    ppermute x3, waiting for transfers between devices: 9.31 us -> 0.01 us  [send_shares(): shares[step] = lax.ppermute(shares[step], 'tensor', ring)]
    ppermute x18, waiting for transfers between devices: 56.1 us -> 58.9 us  [line_gather(): from_right = lax.ppermute(last[at][1], 'tensor', left[:count - 1 - step])]
  transfers between devices with their start and end apart: 48 -> 48, of which waited for: 20 -> 15; matrix products, arithmetic and copies ran while one was open for 2% -> 3% of each run, Pallas kernels for 6% -> 17%
where the time goes in v6:
time: 233 us; the launch traced here: 231 us
  starting transfers between devices  71.3 us (31%)
  waiting for transfers between devices  66.8 us (29%)
  Pallas kernels  48.8 us (21%)
  blocking collectives  29.6 us (13%)
  local copies, waits for them, and re-layouts  11.6 us (5%)
    ppermute x18, waiting for transfers between devices, line_gather(): from_right = lax.ppermute(last[at][1], 'tensor', left[:count - 1 - step])  58.9 us
    ppermute x18, starting transfers between devices, line_gather(): from_left = lax.ppermute(last[at][0], 'tensor', right[step:])  36.3 us
    pallas_call x2, Pallas kernels, project(): pl.pallas_call(partial(project_kernel, group, count), in_specs=[pl.BlockS...  24.8 us
    ppermute x18, starting transfers between devices, line_gather(): from_right = lax.ppermute(last[at][1], 'tensor', left[:count - 1 - step])  23.5 us
    all_to_all x1, blocking collectives, to_heads(): return lax.all_to_all(sent, 'seq', split_axis=0, concat_axis=0)  16.4 us
    all_to_all x1, blocking collectives, shards(): home = lax.all_to_all(out, 'seq', split_axis=0, concat_axis=0)  13.1 us
    pallas_call x1, Pallas kernels, attend(): pl.pallas_call(partial(attend_kernel, chunks, group, rows), in_specs=[pl....  11.3 us
    pallas_call x1, Pallas kernels, output(): pl.pallas_call(partial(output_kernel, group, count, cuts, halves), in_spe...  9.39 us
  transfers between devices with their start and end apart: 48, of which 15 were waited for; matrix products, arithmetic and copies ran while one was open for 3% of the time, Pallas kernels for 17%

profile of v6, /device:TPU:0, one launch (start us, length us, event | category | flops | bytes accessed | tf_op | source)
XLA Modules:
  0.0 231.3 jit_solution(2326474843781651829)
XLA Ops:
  0.0 1.3 fusion.5
  1.3 1.3 collective-permute-start.11
  2.6 5.6 %collective-permute-start.10 = (bf16[128,1024]{1,0:T(8,128)(2,1)S(1)}, bf16[128,1024]{1,0:T(8,128)(2,1)S(1)}, u32[]{:S(2)}, u32[]{:S(2)}) collective-permute-start(bf16[128,1024]{1,0:T(8,128)(2,1)S(1)} %get-tuple-element.103.refs_10_), channel_id=1, source_target_pairs={{0,1},{1,2},{2,3},{4,5},{5,6},{6,7},{8,9},{9,10},{10,11},{12,13},{... | collective-permute-start | bytes 786440 | tf_op jit(solution)/shard_map/ppermute | solution.py:47
  8.2 1.3 collective-permute-start.1
  9.5 4.6 %collective-permute-start = (bf16[128,1024]{1,0:T(8,128)(2,1)S(1)}, bf16[128,1024]{1,0:T(8,128)(2,1)S(1)}, u32[]{:S(2)}, u32[]{:S(2)}) collective-permute-start(bf16[128,1024]{1,0:T(8,128)(2,1)S(1)} %get-tuple-element.105.refs_3_), channel_id=1, source_target_pairs={{0,1},{1,2},{2,3},{4,5},{5,6},{6,7},{8,9},{9,10},{10,11},{12,13},{... | collective-permute-start | bytes 786440 | tf_op jit(solution)/shard_map/ppermute | solution.py:47
  14.1 1.3 collective-permute-start.13
  16.1 2.6 %collective-permute-done.1.refs_5_ = bf16[128,1024]{1,0:T(8,128)(2,1)S(1)} collective-permute-done((bf16[128,1024]{1,0:T(8,128)(2,1)S(1)}, bf16[128,1024]{1,0:T(8,128)(2,1)S(1)}, u32[]{:S(2)}, u32[]{:S(2)}) %collective-permute-start.1) | collective-permute-done | bytes 262176 | tf_op jit(solution)/shard_map/ppermute | solution.py:48
  18.7 1.3 collective-permute-start.3
  20.7 1.3 reshape.57.gain_ref
  22.7 1.9 collective-permute-done.13.refs_14_
  24.6 1.3 collective-permute-start.15
  25.9 1.4 collective-permute-start.14
  27.3 2.1 collective-permute-done.3.refs_7_
  29.4 1.3 collective-permute-start.5
  30.7 1.4 collective-permute-start.4
  32.1 0.8 copy.8.active_ref
  33.5 3.4 %shard_map.74 = (bf16[2,128,256]{2,1,0:T(8,128)(2,1)}, bf16[2,128,256]{2,1,0:T(8,128)(2,1)}, bf16[2,128,256]{2,1,0:T(8,128)(2,1)}, bf16[2,128,256]{2,1,0:T(8,128)(2,1)}) custom-call(s32[3]{0:T(128)} %pad_add_fusion.place_ref, bf16[512,4096]{1,0:T(8,128)(2,1)} %w_ref.1), custom_call_target="tpu_custom_call" | custom-call | tf_op jit(solution)/shard_map/pallas_call | solution.py:372
  36.9 4.3 %collective-permute-done.5.refs_9_ = bf16[128,1024]{1,0:T(8,128)(2,1)S(1)} collective-permute-done((bf16[128,1024]{1,0:T(8,128)(2,1)S(1)}, bf16[128,1024]{1,0:T(8,128)(2,1)S(1)}, u32[]{:S(2)}, u32[]{:S(2)}) %collective-permute-start.5) | collective-permute-done | bytes 262176 | tf_op jit(solution)/shard_map/ppermute | solution.py:48
  41.2 0.7 copy-done.27
  41.9 1.3 collective-permute-start.7
  43.2 4.6 %collective-permute-start.6 = (bf16[128,1024]{1,0:T(8,128)(2,1)S(1)}, bf16[128,1024]{1,0:T(8,128)(2,1)S(1)}, u32[]{:S(2)}, u32[]{:S(2)}) collective-permute-start(bf16[128,1024]{1,0:T(8,128)(2,1)S(1)} %get-tuple-element.54.refs_3_), channel_id=1, source_target_pairs={{0,1},{1,2},{2,3},{4,5},{5,6},{6,7},{8,9},{9,10},{10,11},{12,13},{... | collective-permute-start | bytes 786440 | tf_op jit(solution)/shard_map/ppermute | solution.py:47
  47.7 1.4 collective-permute-start.9
  49.2 4.9 %collective-permute-start.8 = (bf16[128,1024]{1,0:T(8,128)(2,1)S(1)}, bf16[128,1024]{1,0:T(8,128)(2,1)S(1)}, u32[]{:S(2)}, u32[]{:S(2)}) collective-permute-start(bf16[128,1024]{1,0:T(8,128)(2,1)S(1)} %get-tuple-element.55.refs_10_), channel_id=1, source_target_pairs={{0,1},{1,2},{2,3},{4,5},{5,6},{6,7},{8,9},{9,10},{10,11},{12,13},{... | collective-permute-start | bytes 786440 | tf_op jit(solution)/shard_map/ppermute | solution.py:47
  54.2 12.4 %shard_map.73 = bf16[8,128,384]{2,1,0:T(8,128)(2,1)} custom-call(s32[1]{0:T(128)} %bitcast.me_ref, f32[4,1024]{1,0:T(4,128)} %reshape.57.gain_ref, s32[256,1]{1,0:T(8,128)} %copy.8.active_ref, bf16[4096,512]{1,0:T(8,128)(2,1)} %refs_0_.3, bf16[4096,512]{1,0:T(8,128)(2,1)} %refs_1_.3, bf16[4096,512]{1,0:T(8,128)(2,1)} %refs_2_.3, ...), custom_call_target="tpu_custom_call" | custom-call | flops 3221225472 | bytes 15466496 | tf_op jit(solution)/shard_map/pallas_call | solution.py:128
  66.7 0.8 copy-done.21
  67.4 0.7 copy-done.22
  68.1 3.7 %all-to-all-start = ((bf16[8,128,384]{2,1,0:T(8,128)(2,1)}), bf16[8,128,384]{2,1,0:T(8,128)(2,1)S(1)}, u32[]{:S(2)}, u32[]{:S(2)}) async-start(bf16[8,128,384]{2,1,0:T(8,128)(2,1)} %shard_map.73), calls=%async_computation | async-start | bytes 1572864 | tf_op jit(solution)/shard_map/all_to_all | solution.py:470
  72.5 1.3 collective-permute-start.17
  74.5 1.3 collective-permute-start.19
  75.8 9.4 %collective-permute-done.17.refs_7_ = bf16[128,1024]{1,0:T(8,128)(2,1)S(1)} collective-permute-done((bf16[128,1024]{1,0:T(8,128)(2,1)S(1)}, bf16[128,1024]{1,0:T(8,128)(2,1)S(1)}, u32[]{:S(2)}, u32[]{:S(2)}) %collective-permute-start.17) | collective-permute-done | bytes 262176 | tf_op jit(solution)/shard_map/ppermute | solution.py:48
  85.2 5.6 %collective-permute-done.19.refs_14_ = bf16[128,1024]{1,0:T(8,128)(2,1)S(1)} collective-permute-done((bf16[128,1024]{1,0:T(8,128)(2,1)}, bf16[128,1024]{1,0:T(8,128)(2,1)S(1)}, u32[]{:S(2)}, u32[]{:S(2)}) %collective-permute-start.19) | collective-permute-done | bytes 262176 | tf_op jit(solution)/shard_map/ppermute | solution.py:48
  91.6 1.3 collective-permute-start.23
  93.6 1.3 collective-permute-start.21
  94.9 0.8 copy.9.active_ref
  95.7 6.9 %collective-permute-done.23.refs_16_ = bf16[128,1024]{1,0:T(8,128)(2,1)S(1)} collective-permute-done((bf16[128,1024]{1,0:T(8,128)(2,1)S(1)}, bf16[128,1024]{1,0:T(8,128)(2,1)S(1)}, u32[]{:S(2)}, u32[]{:S(2)}) %collective-permute-start.23) | collective-permute-done | bytes 262176 | tf_op jit(solution)/shard_map/ppermute | solution.py:48
  102.6 4.5 %collective-permute-start.26 = (bf16[2,128,256]{2,1,0:T(8,128)(2,1)S(1)}, bf16[2,128,256]{2,1,0:T(8,128)(2,1)S(1)}, u32[]{:S(2)}, u32[]{:S(2)}) collective-permute-start(bf16[2,128,256]{2,1,0:T(8,128)(2,1)S(1)} %copy-done.40), channel_id=1, source_target_pairs={{0,3},{1,0},{2,1},{3,2},{4,7},{5,4},{6,5},{7,6},{8,11},{9,8},{10,9... | collective-permute-start | bytes 393224 | tf_op jit(solution)/shard_map/ppermute | solution.py:414
  107.2 5.8 %collective-permute-done.21.refs_9_ = bf16[128,1024]{1,0:T(8,128)(2,1)S(1)} collective-permute-done((bf16[128,1024]{1,0:T(8,128)(2,1)S(1)}, bf16[128,1024]{1,0:T(8,128)(2,1)S(1)}, u32[]{:S(2)}, u32[]{:S(2)}) %collective-permute-start.21) | collective-permute-done | bytes 262176 | tf_op jit(solution)/shard_map/ppermute | solution.py:48
  113.0 0.7 copy-done.31
  113.7 12.4 %shard_map.75 = bf16[8,128,384]{2,1,0:T(8,128)(2,1)} custom-call(s32[1]{0:T(128)} %bitcast.me_ref, f32[4,1024]{1,0:T(4,128)} %reshape.57.gain_ref, s32[256,1]{1,0:T(8,128)} %copy.9.active_ref, bf16[4096,512]{1,0:T(8,128)(2,1)} %refs_0_.3, bf16[4096,512]{1,0:T(8,128)(2,1)} %refs_1_.3, bf16[4096,512]{1,0:T(8,128)(2,1)} %refs_2_.3, ...), custom_call_target="tpu_custom_call" | custom-call | flops 3221225472 | bytes 15466496 | tf_op jit(solution)/shard_map/pallas_call | solution.py:128
  126.2 16.4 %all_to_all.15.refs_2_ = bf16[8,128,384]{2,1,0:T(8,128)(2,1)S(1)} all-to-all(bf16[8,128,384]{2,1,0:T(8,128)(2,1)} %shard_map.75), channel_id=1, replica_groups=mesh['seq'=8,'tensor'=4] {'seq'}, dimensions={0} | all-to-all | bytes 1572864 | tf_op jit(solution)/shard_map/all_to_all | solution.py:470
  144.0 0.9 collective-permute-done.28.refs_3_
  144.9 0.9 copy-done.39
  145.8 11.3 %shard_map.76 = bf16[8,256,128]{2,1,0:T(8,128)(2,1)} custom-call(s32[1]{0:T(128)} %bitcast.6.part_ref, bf16[8,128,384]{2,1,0:T(8,128)(2,1)} %copy-done.9, bf16[8,128,384]{2,1,0:T(8,128)(2,1)} %collective-permute-done.27.refs_1_, bf16[8,128,384]{2,1,0:T(8,128)(2,1)} %copy-done.10, bf16[8,128,384]{2,1,0:T(8,128)(2,1)} %copy-done.39), custom_call_target="tpu_custom_call" | custom-call | flops 3623878656 | bytes 4194304 | tf_op jit(solution)/shard_map/pallas_call | solution.py:256
  157.0 13.1 %all_to_all.16 = bf16[8,256,128]{2,1,0:T(8,128)(2,1)S(1)} all-to-all(bf16[8,256,128]{2,1,0:T(8,128)(2,1)} %shard_map.76), channel_id=1, replica_groups=mesh['seq'=8,'tensor'=4] {'seq'}, dimensions={0} | all-to-all | bytes 1048576 | tf_op jit(solution)/shard_map/all_to_all | solution.py:511
  171.6 1.3 collective-permute-start.34
  172.9 4.6 %collective-permute-start.33 = (bf16[4,256,128]{2,1,0:T(8,128)(2,1)S(1)}, bf16[4,256,128]{2,1,0:T(8,128)(2,1)S(1)}, u32[]{:S(2)}, u32[]{:S(2)}) collective-permute-start(bf16[4,256,128]{2,1,0:T(8,128)(2,1)S(1)} %get-tuple-element.111), channel_id=1, source_target_pairs={{0,1},{1,2},{2,3},{4,5},{5,6},{6,7},{8,9},{9,10},{10,11},{12,13},{... | collective-permute-start | bytes 786440 | tf_op jit(solution)/shard_map/ppermute | solution.py:47
  177.4 1.3 collective-permute-start.32
  178.7 4.6 %collective-permute-done.36 = bf16[1024,256]{1,0:T(8,128)(2,1)S(1)} collective-permute-done((bf16[1024,256]{1,0:T(8,128)(2,1)S(1)}, bf16[1024,256]{1,0:T(8,128)(2,1)S(1)}, u32[]{:S(2)}, u32[]{:S(2)}) %collective-permute-start.36) | collective-permute-done | bytes 524320 | tf_op jit(solution)/shard_map/ppermute | solution.py:424
  183.3 1.3 collective-permute-start.31
  184.7 1.8 collective-permute-done.32
  186.5 2.3 %collective-permute-done.31 = bf16[4,256,128]{2,1,0:T(8,128)(2,1)S(1)} collective-permute-done((bf16[4,256,128]{2,1,0:T(8,128)(2,1)S(1)}, bf16[4,256,128]{2,1,0:T(8,128)(2,1)S(1)}, u32[]{:S(2)}, u32[]{:S(2)}) %collective-permute-start.31) | collective-permute-done | bytes 262176 | tf_op jit(solution)/shard_map/ppermute | solution.py:47
  190.4 1.3 collective-permute-start.40
  191.7 1.4 collective-permute-start.43
  193.1 1.3 collective-permute-start.44
  194.4 7.6 %collective-permute-done.40 = bf16[4,256,128]{2,1,0:T(8,128)(2,1)} collective-permute-done((bf16[4,256,128]{2,1,0:T(8,128)(2,1)S(1)}, bf16[4,256,128]{2,1,0:T(8,128)(2,1)}, u32[]{:S(2)}, u32[]{:S(2)}) %collective-permute-start.40) | collective-permute-done | bytes 262176 | tf_op jit(solution)/shard_map/ppermute | solution.py:48
  202.7 1.3 collective-permute-start.42
  204.0 6.0 %collective-permute-done.44 = bf16[4,256,128]{2,1,0:T(8,128)(2,1)} collective-permute-done((bf16[4,256,128]{2,1,0:T(8,128)(2,1)S(1)}, bf16[4,256,128]{2,1,0:T(8,128)(2,1)}, u32[]{:S(2)}, u32[]{:S(2)}) %collective-permute-start.44) | collective-permute-done | bytes 262176 | tf_op jit(solution)/shard_map/ppermute | solution.py:48
  210.0 1.4 collective-permute-start.45
  211.4 0.7 copy-done.37
  212.1 1.5 collective-permute-start.46
  213.6 0.9 copy.10.active_ref
  215.7 5.0 %collective-permute-done.46 = bf16[4,256,128]{2,1,0:T(8,128)(2,1)} collective-permute-done((bf16[4,256,128]{2,1,0:T(8,128)(2,1)}, bf16[4,256,128]{2,1,0:T(8,128)(2,1)}, u32[]{:S(2)}, u32[]{:S(2)}) %collective-permute-start.46) | collective-permute-done | bytes 262176 | tf_op jit(solution)/shard_map/ppermute | solution.py:48
  220.7 1.0 copy-done.6
  221.7 9.4 %shard_map.77 = bf16[512,1024]{1,0:T(8,128)(2,1)} custom-call(s32[5]{0:T(128)} %stack.31.me_ref, s32[16]{0:T(128)} %fusion.at_ref, s32[512,1]{1,0:T(8,128)} %copy.10.active_ref, bf16[512,1024]{1,0:T(8,128)(2,1)} %hidden_ref.1, bf16[2048,256]{1,0:T(8,128)(2,1)} %copy-done, bf16[2048,256]{1,0:T(8,128)(2,1)} %copy-done.1, ...), custom_call_target="tpu_custom_call" | custom-call | flops 2147483648 | bytes 8388608 | tf_op jit(solution)/shard_map/pallas_call | solution.py:336
  (148 shorter events, 11.7 us)
Async XLA Ops:
  1.3 52.8 %copy-start.4 = (bf16[128,1024]{1,0:T(8,128)(2,1)}, bf16[128,1024]{1,0:T(8,128)(2,1)S(1)}, u32[]{:S(2)}) copy-start(bf16[128,1024]{1,0:T(8,128)(2,1)S(1)} %get-tuple-element.103.refs_10_) | copy-start | bytes 786436
  1.3 52.8 %copy-start.5 = (bf16[128,1024]{1,0:T(8,128)(2,1)}, bf16[128,1024]{1,0:T(8,128)(2,1)S(1)}, u32[]{:S(2)}) copy-start(bf16[128,1024]{1,0:T(8,128)(2,1)S(1)} %get-tuple-element.105.refs_3_) | copy-start | bytes 786436
  1.3 65.3 %copy-start.2 = (bf16[128,1024]{1,0:T(8,128)(2,1)}, bf16[128,1024]{1,0:T(8,128)(2,1)S(1)}, u32[]{:S(2)}) copy-start(bf16[128,1024]{1,0:T(8,128)(2,1)S(1)} %get-tuple-element.55.refs_10_) | copy-start | bytes 786436
  1.3 65.3 %copy-start.3 = (bf16[128,1024]{1,0:T(8,128)(2,1)}, bf16[128,1024]{1,0:T(8,128)(2,1)S(1)}, u32[]{:S(2)}) copy-start(bf16[128,1024]{1,0:T(8,128)(2,1)S(1)} %get-tuple-element.54.refs_3_) | copy-start | bytes 786436
  1.3 12.8 %collective-permute-start.11 = (bf16[128,1024]{1,0:T(8,128)(2,1)S(1)}, bf16[128,1024]{1,0:T(8,128)(2,1)S(1)}, u32[]{:S(2)}, u32[]{:S(2)}) collective-permute-start(bf16[128,1024]{1,0:T(8,128)(2,1)S(1)} %get-tuple-element.103.refs_10_), channel_id=1, source_target_pairs={{1,0},{2,1},{3,2},{5,4},{6,5},{7,6},{9,8},{10,9},{11,10},{13,12},{... | collective-permute-start | bytes 786440 | tf_op jit(solution)/shard_map/ppermute | solution.py:48
  2.6 12.8 %collective-permute-start.10 = (bf16[128,1024]{1,0:T(8,128)(2,1)S(1)}, bf16[128,1024]{1,0:T(8,128)(2,1)S(1)}, u32[]{:S(2)}, u32[]{:S(2)}) collective-permute-start(bf16[128,1024]{1,0:T(8,128)(2,1)S(1)} %get-tuple-element.103.refs_10_), channel_id=1, source_target_pairs={{0,1},{1,2},{2,3},{4,5},{5,6},{6,7},{8,9},{9,10},{10,11},{12,13},{... | collective-permute-start | bytes 786440 | tf_op jit(solution)/shard_map/ppermute | solution.py:47
  8.2 10.5 %collective-permute-start.1 = (bf16[128,1024]{1,0:T(8,128)(2,1)S(1)}, bf16[128,1024]{1,0:T(8,128)(2,1)S(1)}, u32[]{:S(2)}, u32[]{:S(2)}) collective-permute-start(bf16[128,1024]{1,0:T(8,128)(2,1)S(1)} %get-tuple-element.105.refs_3_), channel_id=1, source_target_pairs={{1,0},{2,1},{3,2},{5,4},{6,5},{7,6},{9,8},{10,9},{11,10},{13,12},{... | collective-permute-start | bytes 786440 | tf_op jit(solution)/shard_map/ppermute | solution.py:48
  9.5 10.5 %collective-permute-start = (bf16[128,1024]{1,0:T(8,128)(2,1)S(1)}, bf16[128,1024]{1,0:T(8,128)(2,1)S(1)}, u32[]{:S(2)}, u32[]{:S(2)}) collective-permute-start(bf16[128,1024]{1,0:T(8,128)(2,1)S(1)} %get-tuple-element.105.refs_3_), channel_id=1, source_target_pairs={{0,1},{1,2},{2,3},{4,5},{5,6},{6,7},{8,9},{9,10},{10,11},{12,13},{... | collective-permute-start | bytes 786440 | tf_op jit(solution)/shard_map/ppermute | solution.py:47
  14.1 40.0 %copy-start.11 = (bf16[128,1024]{1,0:T(8,128)(2,1)}, bf16[128,1024]{1,0:T(8,128)(2,1)S(1)}, u32[]{:S(2)}) copy-start(bf16[128,1024]{1,0:T(8,128)(2,1)S(1)} %collective-permute-done.11.refs_12_) | copy-start | bytes 786436
  14.1 10.5 %collective-permute-start.13 = (bf16[128,1024]{1,0:T(8,128)(2,1)S(1)}, bf16[128,1024]{1,0:T(8,128)(2,1)S(1)}, u32[]{:S(2)}, u32[]{:S(2)}) collective-permute-start(bf16[128,1024]{1,0:T(8,128)(2,1)S(1)} %collective-permute-done.11.refs_12_), channel_id=1, source_target_pairs={{1,0},{2,1},{5,4},{6,5},{9,8},{10,9},{13,12},{14,13},{17,16},{18,1... | collective-permute-start | bytes 786440 | tf_op jit(solution)/shard_map/ppermute | solution.py:48
  15.4 38.7 %copy-start.12 = (bf16[128,1024]{1,0:T(8,128)(2,1)}, bf16[128,1024]{1,0:T(8,128)(2,1)S(1)}, u32[]{:S(2)}) copy-start(bf16[128,1024]{1,0:T(8,128)(2,1)S(1)} %collective-permute-done.10.refs_11_) | copy-start | bytes 786436
  15.4 10.5 %collective-permute-start.12 = (bf16[128,1024]{1,0:T(8,128)(2,1)S(1)}, bf16[128,1024]{1,0:T(8,128)(2,1)S(1)}, u32[]{:S(2)}, u32[]{:S(2)}) collective-permute-start(bf16[128,1024]{1,0:T(8,128)(2,1)S(1)} %collective-permute-done.10.refs_11_), channel_id=1, source_target_pairs={{1,2},{2,3},{5,6},{6,7},{9,10},{10,11},{13,14},{14,15},{17,18},{18... | collective-permute-start | bytes 786440 | tf_op jit(solution)/shard_map/ppermute | solution.py:47
  18.7 35.4 %copy-start.13 = (bf16[128,1024]{1,0:T(8,128)(2,1)}, bf16[128,1024]{1,0:T(8,128)(2,1)S(1)}, u32[]{:S(2)}) copy-start(bf16[128,1024]{1,0:T(8,128)(2,1)S(1)} %collective-permute-done.1.refs_5_) | copy-start | bytes 786436
  18.7 10.7 %collective-permute-start.3 = (bf16[128,1024]{1,0:T(8,128)(2,1)S(1)}, bf16[128,1024]{1,0:T(8,128)(2,1)S(1)}, u32[]{:S(2)}, u32[]{:S(2)}) collective-permute-start(bf16[128,1024]{1,0:T(8,128)(2,1)S(1)} %collective-permute-done.1.refs_5_), channel_id=1, source_target_pairs={{1,0},{2,1},{5,4},{6,5},{9,8},{10,9},{13,12},{14,13},{17,16},{18,1... | collective-permute-start | bytes 786440 | tf_op jit(solution)/shard_map/ppermute | solution.py:48
  20.0 34.1 %copy-start.14 = (bf16[128,1024]{1,0:T(8,128)(2,1)}, bf16[128,1024]{1,0:T(8,128)(2,1)S(1)}, u32[]{:S(2)}) copy-start(bf16[128,1024]{1,0:T(8,128)(2,1)S(1)} %collective-permute-done.refs_4_) | copy-start | bytes 786436
  20.0 10.7 %collective-permute-start.2 = (bf16[128,1024]{1,0:T(8,128)(2,1)S(1)}, bf16[128,1024]{1,0:T(8,128)(2,1)S(1)}, u32[]{:S(2)}, u32[]{:S(2)}) collective-permute-start(bf16[128,1024]{1,0:T(8,128)(2,1)S(1)} %collective-permute-done.refs_4_), channel_id=1, source_target_pairs={{1,2},{2,3},{5,6},{6,7},{9,10},{10,11},{13,14},{14,15},{17,18},{18... | collective-permute-start | bytes 786440 | tf_op jit(solution)/shard_map/ppermute | solution.py:47
  24.6 24.6 %collective-permute-start.15 = (bf16[128,1024]{1,0:T(8,128)(2,1)S(1)}, bf16[128,1024]{1,0:T(8,128)(2,1)}, u32[]{:S(2)}, u32[]{:S(2)}) collective-permute-start(bf16[128,1024]{1,0:T(8,128)(2,1)S(1)} %collective-permute-done.13.refs_14_), channel_id=1, source_target_pairs={{1,0},{5,4},{9,8},{13,12},{17,16},{21,20},{25,24},{29,28}} | collective-permute-start | bytes 786440 | tf_op jit(solution)/shard_map/ppermute | solution.py:48
  25.9 28.2 %collective-permute-start.14 = (bf16[128,1024]{1,0:T(8,128)(2,1)S(1)}, bf16[128,1024]{1,0:T(8,128)(2,1)}, u32[]{:S(2)}, u32[]{:S(2)}) collective-permute-start(bf16[128,1024]{1,0:T(8,128)(2,1)S(1)} %collective-permute-done.12.refs_13_), channel_id=1, source_target_pairs={{2,3},{6,7},{10,11},{14,15},{18,19},{22,23},{26,27},{30,31}} | collective-permute-start | bytes 786440 | tf_op jit(solution)/shard_map/ppermute | solution.py:47
  29.4 11.8 %collective-permute-start.5 = (bf16[128,1024]{1,0:T(8,128)(2,1)S(1)}, bf16[128,1024]{1,0:T(8,128)(2,1)S(1)}, u32[]{:S(2)}, u32[]{:S(2)}) collective-permute-start(bf16[128,1024]{1,0:T(8,128)(2,1)S(1)} %collective-permute-done.3.refs_7_), channel_id=1, source_target_pairs={{1,0},{5,4},{9,8},{13,12},{17,16},{21,20},{25,24},{29,28}} | collective-permute-start | bytes 786440 | tf_op jit(solution)/shard_map/ppermute | solution.py:48
  30.7 10.5 %collective-permute-start.4 = (bf16[128,1024]{1,0:T(8,128)(2,1)S(1)}, bf16[128,1024]{1,0:T(8,128)(2,1)}, u32[]{:S(2)}, u32[]{:S(2)}) collective-permute-start(bf16[128,1024]{1,0:T(8,128)(2,1)S(1)} %collective-permute-done.2.refs_6_), channel_id=1, source_target_pairs={{2,3},{6,7},{10,11},{14,15},{18,19},{22,23},{26,27},{30,31}} | collective-permute-start | bytes 786440 | tf_op jit(solution)/shard_map/ppermute | solution.py:47
  41.9 24.7 %collective-permute-start.7 = (bf16[128,1024]{1,0:T(8,128)(2,1)S(1)}, bf16[128,1024]{1,0:T(8,128)(2,1)S(1)}, u32[]{:S(2)}, u32[]{:S(2)}) collective-permute-start(bf16[128,1024]{1,0:T(8,128)(2,1)S(1)} %get-tuple-element.54.refs_3_), channel_id=1, source_target_pairs={{1,0},{2,1},{3,2},{5,4},{6,5},{7,6},{9,8},{10,9},{11,10},{13,12},{... | collective-permute-start | bytes 786440 | tf_op jit(solution)/shard_map/ppermute | solution.py:48
  43.2 23.4 %collective-permute-start.6 = (bf16[128,1024]{1,0:T(8,128)(2,1)S(1)}, bf16[128,1024]{1,0:T(8,128)(2,1)S(1)}, u32[]{:S(2)}, u32[]{:S(2)}) collective-permute-start(bf16[128,1024]{1,0:T(8,128)(2,1)S(1)} %get-tuple-element.54.refs_3_), channel_id=1, source_target_pairs={{0,1},{1,2},{2,3},{4,5},{5,6},{6,7},{8,9},{9,10},{10,11},{12,13},{... | collective-permute-start | bytes 786440 | tf_op jit(solution)/shard_map/ppermute | solution.py:47
  47.7 54.9 %copy-start.40 = (bf16[2,128,256]{2,1,0:T(8,128)(2,1)S(1)}, bf16[2,128,256]{2,1,0:T(8,128)(2,1)}, u32[]{:S(2)}) copy-start(bf16[2,128,256]{2,1,0:T(8,128)(2,1)} %get-tuple-element.72) | copy-start | bytes 393220
  47.7 18.9 %collective-permute-start.9 = (bf16[128,1024]{1,0:T(8,128)(2,1)S(1)}, bf16[128,1024]{1,0:T(8,128)(2,1)S(1)}, u32[]{:S(2)}, u32[]{:S(2)}) collective-permute-start(bf16[128,1024]{1,0:T(8,128)(2,1)S(1)} %get-tuple-element.55.refs_10_), channel_id=1, source_target_pairs={{1,0},{2,1},{3,2},{5,4},{6,5},{7,6},{9,8},{10,9},{11,10},{13,12},{... | collective-permute-start | bytes 786440 | tf_op jit(solution)/shard_map/ppermute | solution.py:48
  49.2 17.5 %collective-permute-start.8 = (bf16[128,1024]{1,0:T(8,128)(2,1)S(1)}, bf16[128,1024]{1,0:T(8,128)(2,1)S(1)}, u32[]{:S(2)}, u32[]{:S(2)}) collective-permute-start(bf16[128,1024]{1,0:T(8,128)(2,1)S(1)} %get-tuple-element.55.refs_10_), channel_id=1, source_target_pairs={{0,1},{1,2},{2,3},{4,5},{5,6},{6,7},{8,9},{9,10},{10,11},{12,13},{... | collective-permute-start | bytes 786440 | tf_op jit(solution)/shard_map/ppermute | solution.py:47
  66.6 46.4 %copy-start.18 = (bf16[128,1024]{1,0:T(8,128)(2,1)}, bf16[128,1024]{1,0:T(8,128)(2,1)S(1)}, u32[]{:S(2)}) copy-start(bf16[128,1024]{1,0:T(8,128)(2,1)S(1)} %collective-permute-done.7.refs_5_) | copy-start | bytes 786436
  66.6 46.4 %copy-start.19 = (bf16[128,1024]{1,0:T(8,128)(2,1)}, bf16[128,1024]{1,0:T(8,128)(2,1)S(1)}, u32[]{:S(2)}) copy-start(bf16[128,1024]{1,0:T(8,128)(2,1)S(1)} %collective-permute-done.6.refs_4_) | copy-start | bytes 786436
  68.1 22.7 %all-to-all-start = ((bf16[8,128,384]{2,1,0:T(8,128)(2,1)}), bf16[8,128,384]{2,1,0:T(8,128)(2,1)S(1)}, u32[]{:S(2)}, u32[]{:S(2)}) async-start(bf16[8,128,384]{2,1,0:T(8,128)(2,1)} %shard_map.73), calls=%async_computation | async-start | bytes 1572864 | tf_op jit(solution)/shard_map/all_to_all | solution.py:470
  71.8 4.0 %collective-permute-start.16 = (bf16[128,1024]{1,0:T(8,128)(2,1)S(1)}, bf16[128,1024]{1,0:T(8,128)(2,1)S(1)}, u32[]{:S(2)}, u32[]{:S(2)}) collective-permute-start(bf16[128,1024]{1,0:T(8,128)(2,1)S(1)} %collective-permute-done.6.refs_4_), channel_id=1, source_target_pairs={{1,2},{2,3},{5,6},{6,7},{9,10},{10,11},{13,14},{14,15},{17,18},{18... | collective-permute-start | bytes 786440 | tf_op jit(solution)/shard_map/ppermute | solution.py:47
  72.5 12.7 %collective-permute-start.17 = (bf16[128,1024]{1,0:T(8,128)(2,1)S(1)}, bf16[128,1024]{1,0:T(8,128)(2,1)S(1)}, u32[]{:S(2)}, u32[]{:S(2)}) collective-permute-start(bf16[128,1024]{1,0:T(8,128)(2,1)S(1)} %collective-permute-done.7.refs_5_), channel_id=1, source_target_pairs={{1,0},{2,1},{5,4},{6,5},{9,8},{10,9},{13,12},{14,13},{17,16},{18,1... | collective-permute-start | bytes 786440 | tf_op jit(solution)/shard_map/ppermute | solution.py:48
  73.8 11.4 %collective-permute-start.18 = (bf16[128,1024]{1,0:T(8,128)(2,1)}, bf16[128,1024]{1,0:T(8,128)(2,1)S(1)}, u32[]{:S(2)}, u32[]{:S(2)}) collective-permute-start(bf16[128,1024]{1,0:T(8,128)(2,1)} %copy-done.22), channel_id=1, source_target_pairs={{1,2},{2,3},{5,6},{6,7},{9,10},{10,11},{13,14},{14,15},{17,18},{18... | collective-permute-start | bytes 786440 | tf_op jit(solution)/shard_map/ppermute | solution.py:47
  74.5 16.3 %collective-permute-start.19 = (bf16[128,1024]{1,0:T(8,128)(2,1)}, bf16[128,1024]{1,0:T(8,128)(2,1)S(1)}, u32[]{:S(2)}, u32[]{:S(2)}) collective-permute-start(bf16[128,1024]{1,0:T(8,128)(2,1)} %copy-done.21), channel_id=1, source_target_pairs={{1,0},{2,1},{5,4},{6,5},{9,8},{10,9},{13,12},{14,13},{17,16},{18,1... | collective-permute-start | bytes 786440 | tf_op jit(solution)/shard_map/ppermute | solution.py:48
  75.8 37.2 %copy-start.23 = (bf16[128,1024]{1,0:T(8,128)(2,1)}, bf16[128,1024]{1,0:T(8,128)(2,1)S(1)}, u32[]{:S(2)}) copy-start(bf16[128,1024]{1,0:T(8,128)(2,1)S(1)} %collective-permute-done.16.refs_6_) | copy-start | bytes 786436
  90.8 35.3 %copy-start.9 = (bf16[8,128,384]{2,1,0:T(8,128)(2,1)}, bf16[8,128,384]{2,1,0:T(8,128)(2,1)S(1)}, u32[]{:S(2)}) copy-start(bf16[8,128,384]{2,1,0:T(8,128)(2,1)S(1)} %all-to-all-done.refs_0_) | copy-start | bytes 2359300
  90.8 35.3 %collective-permute-start.27 = (bf16[8,128,384]{2,1,0:T(8,128)(2,1)S(1)}, bf16[8,128,384]{2,1,0:T(8,128)(2,1)}, u32[]{:S(2)}, u32[]{:S(2)}) collective-permute-start(bf16[8,128,384]{2,1,0:T(8,128)(2,1)S(1)} %all-to-all-done.refs_0_), channel_id=1, source_target_pairs={{0,4},{4,0},{8,12},{12,8},{16,20},{20,16},{24,28},{28,24},{1,5},{5... | collective-permute-start | bytes 2359304 | tf_op jit(solution)/shard_map/ppermute | solution.py:477
  90.9 4.8 %collective-permute-start.22 = (bf16[128,1024]{1,0:T(8,128)(2,1)S(1)}, bf16[128,1024]{1,0:T(8,128)(2,1)S(1)}, u32[]{:S(2)}, u32[]{:S(2)}) collective-permute-start(bf16[128,1024]{1,0:T(8,128)(2,1)S(1)} %collective-permute-done.18.refs_13_), channel_id=1, source_target_pairs={{2,3},{6,7},{10,11},{14,15},{18,19},{22,23},{26,27},{30,31}} | collective-permute-start | bytes 786440 | tf_op jit(solution)/shard_map/ppermute | solution.py:47
  91.6 11.0 %collective-permute-start.23 = (bf16[128,1024]{1,0:T(8,128)(2,1)S(1)}, bf16[128,1024]{1,0:T(8,128)(2,1)S(1)}, u32[]{:S(2)}, u32[]{:S(2)}) collective-permute-start(bf16[128,1024]{1,0:T(8,128)(2,1)S(1)} %collective-permute-done.19.refs_14_), channel_id=1, source_target_pairs={{1,0},{5,4},{9,8},{13,12},{17,16},{21,20},{25,24},{29,28}} | collective-permute-start | bytes 786440 | tf_op jit(solution)/shard_map/ppermute | solution.py:48
  92.9 9.7 %collective-permute-start.20 = (bf16[128,1024]{1,0:T(8,128)(2,1)S(1)}, bf16[128,1024]{1,0:T(8,128)(2,1)S(1)}, u32[]{:S(2)}, u32[]{:S(2)}) collective-permute-start(bf16[128,1024]{1,0:T(8,128)(2,1)S(1)} %collective-permute-done.16.refs_6_), channel_id=1, source_target_pairs={{2,3},{6,7},{10,11},{14,15},{18,19},{22,23},{26,27},{30,31}} | collective-permute-start | bytes 786440 | tf_op jit(solution)/shard_map/ppermute | solution.py:47
  93.6 19.4 %collective-permute-start.21 = (bf16[128,1024]{1,0:T(8,128)(2,1)S(1)}, bf16[128,1024]{1,0:T(8,128)(2,1)S(1)}, u32[]{:S(2)}, u32[]{:S(2)}) collective-permute-start(bf16[128,1024]{1,0:T(8,128)(2,1)S(1)} %collective-permute-done.17.refs_7_), channel_id=1, source_target_pairs={{1,0},{5,4},{9,8},{13,12},{17,16},{21,20},{25,24},{29,28}} | collective-permute-start | bytes 786440 | tf_op jit(solution)/shard_map/ppermute | solution.py:48
  95.7 46.9 %copy-start.38 = (bf16[2,128,256]{2,1,0:T(8,128)(2,1)S(1)}, bf16[2,128,256]{2,1,0:T(8,128)(2,1)}, u32[]{:S(2)}) copy-start(bf16[2,128,256]{2,1,0:T(8,128)(2,1)} %get-tuple-element.77) | copy-start | bytes 393220
  102.6 23.6 %collective-permute-start.24 = (bf16[2,128,256]{2,1,0:T(8,128)(2,1)}, bf16[2,128,256]{2,1,0:T(8,128)(2,1)S(1)}, u32[]{:S(2)}, u32[]{:S(2)}) collective-permute-start(bf16[2,128,256]{2,1,0:T(8,128)(2,1)} %get-tuple-element.70), channel_id=1, source_target_pairs={{0,1},{1,2},{2,3},{3,0},{4,5},{5,6},{6,7},{7,4},{8,9},{9,10},{10,1... | collective-permute-start | bytes 393224 | tf_op jit(solution)/shard_map/ppermute | solution.py:414
  102.6 23.6 %collective-permute-start.25 = (bf16[2,128,256]{2,1,0:T(8,128)(2,1)}, bf16[2,128,256]{2,1,0:T(8,128)(2,1)S(1)}, u32[]{:S(2)}, u32[]{:S(2)}) collective-permute-start(bf16[2,128,256]{2,1,0:T(8,128)(2,1)} %get-tuple-element.71), channel_id=1, source_target_pairs={{0,2},{1,3},{2,0},{3,1},{4,6},{5,7},{6,4},{7,5},{8,10},{9,11},{10,... | collective-permute-start | bytes 393224 | tf_op jit(solution)/shard_map/ppermute | solution.py:414
  102.6 23.5 %collective-permute-start.26 = (bf16[2,128,256]{2,1,0:T(8,128)(2,1)S(1)}, bf16[2,128,256]{2,1,0:T(8,128)(2,1)S(1)}, u32[]{:S(2)}, u32[]{:S(2)}) collective-permute-start(bf16[2,128,256]{2,1,0:T(8,128)(2,1)S(1)} %copy-done.40), channel_id=1, source_target_pairs={{0,3},{1,0},{2,1},{3,2},{4,7},{5,4},{6,5},{7,6},{8,11},{9,8},{10,9... | collective-permute-start | bytes 393224 | tf_op jit(solution)/shard_map/ppermute | solution.py:414
  142.6 2.3 collective-permute-start.28
  142.7 14.3 %collective-permute-start.29 = (bf16[512,256]{1,0:T(8,128)(2,1)S(1)}, bf16[512,256]{1,0:T(8,128)(2,1)S(1)}, u32[]{:S(2)}, u32[]{:S(2)}) collective-permute-start(bf16[512,256]{1,0:T(8,128)(2,1)S(1)} %pad_maximum_fusion.2), channel_id=1, source_target_pairs={{0,8},{4,12},{8,0},{12,4},{16,24},{20,28},{24,16},{28,20},{1,9},{5... | collective-permute-start | bytes 786440 | tf_op jit(solution)/shard_map/ppermute | solution.py:424
  143.3 13.7 %collective-permute-start.30 = (bf16[512,256]{1,0:T(8,128)(2,1)S(1)}, bf16[512,256]{1,0:T(8,128)(2,1)S(1)}, u32[]{:S(2)}, u32[]{:S(2)}) collective-permute-start(bf16[512,256]{1,0:T(8,128)(2,1)S(1)} %pad_maximum_fusion.3), channel_id=1, source_target_pairs={{0,16},{4,20},{8,24},{12,28},{16,0},{20,4},{24,8},{28,12},{1,17},{... | collective-permute-start | bytes 786440 | tf_op jit(solution)/shard_map/ppermute | solution.py:424
  170.2 13.1 %collective-permute-start.36 = (bf16[1024,256]{1,0:T(8,128)(2,1)S(1)}, bf16[1024,256]{1,0:T(8,128)(2,1)S(1)}, u32[]{:S(2)}, u32[]{:S(2)}) collective-permute-start(bf16[1024,256]{1,0:T(8,128)(2,1)S(1)} %pad_maximum_fusion.1), channel_id=1, source_target_pairs={{0,8},{4,12},{8,0},{12,4},{16,24},{20,28},{24,16},{28,20},{1,9},{5... | collective-permute-start | bytes 1572872 | tf_op jit(solution)/shard_map/ppermute | solution.py:424
  170.9 13.8 %collective-permute-start.35 = (bf16[1024,256]{1,0:T(8,128)(2,1)S(1)}, bf16[1024,256]{1,0:T(8,128)(2,1)S(1)}, u32[]{:S(2)}, u32[]{:S(2)}) collective-permute-start(bf16[1024,256]{1,0:T(8,128)(2,1)S(1)} %pad_maximum_fusion), channel_id=1, source_target_pairs={{0,16},{4,20},{8,24},{12,28},{16,0},{20,4},{24,8},{28,12},{1,17},{... | collective-permute-start | bytes 1572872 | tf_op jit(solution)/shard_map/ppermute | solution.py:424
  171.6 13.1 %collective-permute-start.34 = (bf16[4,256,128]{2,1,0:T(8,128)(2,1)S(1)}, bf16[4,256,128]{2,1,0:T(8,128)(2,1)S(1)}, u32[]{:S(2)}, u32[]{:S(2)}) collective-permute-start(bf16[4,256,128]{2,1,0:T(8,128)(2,1)S(1)} %get-tuple-element.111), channel_id=1, source_target_pairs={{1,0},{2,1},{3,2},{5,4},{6,5},{7,6},{9,8},{10,9},{11,10},{13,12},{... | collective-permute-start | bytes 786440 | tf_op jit(solution)/shard_map/ppermute | solution.py:48
  172.9 11.9 %collective-permute-start.33 = (bf16[4,256,128]{2,1,0:T(8,128)(2,1)S(1)}, bf16[4,256,128]{2,1,0:T(8,128)(2,1)S(1)}, u32[]{:S(2)}, u32[]{:S(2)}) collective-permute-start(bf16[4,256,128]{2,1,0:T(8,128)(2,1)S(1)} %get-tuple-element.111), channel_id=1, source_target_pairs={{0,1},{1,2},{2,3},{4,5},{5,6},{6,7},{8,9},{9,10},{10,11},{12,13},{... | collective-permute-start | bytes 786440 | tf_op jit(solution)/shard_map/ppermute | solution.py:47
  177.4 9.1 %collective-permute-start.32 = (bf16[4,256,128]{2,1,0:T(8,128)(2,1)S(1)}, bf16[4,256,128]{2,1,0:T(8,128)(2,1)S(1)}, u32[]{:S(2)}, u32[]{:S(2)}) collective-permute-start(bf16[4,256,128]{2,1,0:T(8,128)(2,1)S(1)} %get-tuple-element.112), channel_id=1, source_target_pairs={{1,0},{2,1},{3,2},{5,4},{6,5},{7,6},{9,8},{10,9},{11,10},{13,12},{... | collective-permute-start | bytes 786440 | tf_op jit(solution)/shard_map/ppermute | solution.py:48
  183.3 5.5 %collective-permute-start.31 = (bf16[4,256,128]{2,1,0:T(8,128)(2,1)S(1)}, bf16[4,256,128]{2,1,0:T(8,128)(2,1)S(1)}, u32[]{:S(2)}, u32[]{:S(2)}) collective-permute-start(bf16[4,256,128]{2,1,0:T(8,128)(2,1)S(1)} %get-tuple-element.112), channel_id=1, source_target_pairs={{0,1},{1,2},{2,3},{4,5},{5,6},{6,7},{8,9},{9,10},{10,11},{12,13},{... | collective-permute-start | bytes 786440 | tf_op jit(solution)/shard_map/ppermute | solution.py:47
  184.7 36.0 %copy-start.32 = (bf16[4,256,128]{2,1,0:T(8,128)(2,1)}, bf16[4,256,128]{2,1,0:T(8,128)(2,1)S(1)}, u32[]{:S(2)}) copy-start(bf16[4,256,128]{2,1,0:T(8,128)(2,1)S(1)} %collective-permute-done.34) | copy-start | bytes 786436
  189.0 31.7 %copy-start.1 = (bf16[2048,256]{1,0:T(8,128)(2,1)}, bf16[2048,256]{1,0:T(8,128)(2,1)S(1)}, u32[]{:S(2)}) copy-start(bf16[2048,256]{1,0:T(8,128)(2,1)S(1)} %constant_dynamic-update-slice_fusion.4.refs_1_) | copy-start | bytes 3145732
  189.0 31.7 %collective-permute-start.38 = (bf16[2048,256]{1,0:T(8,128)(2,1)S(1)}, bf16[2048,256]{1,0:T(8,128)(2,1)S(1)}, u32[]{:S(2)}, u32[]{:S(2)}) collective-permute-start(bf16[2048,256]{1,0:T(8,128)(2,1)S(1)} %constant_dynamic-update-slice_fusion.4.refs_1_), channel_id=1, source_target_pairs={{0,4},{4,0},{8,12},{12,8},{16,20},{20,16},{24,28},{28,24},{1,5},{5... | collective-permute-start | bytes 3145736 | tf_op jit(solution)/shard_map/ppermute | solution.py:526
  189.2 31.5 %collective-permute-start.37 = (bf16[2048,256]{1,0:T(8,128)(2,1)S(1)}, bf16[2048,256]{1,0:T(8,128)(2,1)}, u32[]{:S(2)}, u32[]{:S(2)}) collective-permute-start(bf16[2048,256]{1,0:T(8,128)(2,1)S(1)} %constant_dynamic-update-slice_fusion.refs_0_), channel_id=1, source_target_pairs={{0,4},{4,0},{8,12},{12,8},{16,20},{20,16},{24,28},{28,24},{1,5},{5... | collective-permute-start | bytes 3145736 | tf_op jit(solution)/shard_map/ppermute | solution.py:526
  189.7 3.4 %collective-permute-start.39 = (bf16[4,256,128]{2,1,0:T(8,128)(2,1)S(1)}, bf16[4,256,128]{2,1,0:T(8,128)(2,1)S(1)}, u32[]{:S(2)}, u32[]{:S(2)}) collective-permute-start(bf16[4,256,128]{2,1,0:T(8,128)(2,1)S(1)} %collective-permute-done.31), channel_id=1, source_target_pairs={{1,2},{2,3},{5,6},{6,7},{9,10},{10,11},{13,14},{14,15},{17,18},{18... | collective-permute-start | bytes 786440 | tf_op jit(solution)/shard_map/ppermute | solution.py:47
  190.4 11.6 %collective-permute-start.40 = (bf16[4,256,128]{2,1,0:T(8,128)(2,1)S(1)}, bf16[4,256,128]{2,1,0:T(8,128)(2,1)}, u32[]{:S(2)}, u32[]{:S(2)}) collective-permute-start(bf16[4,256,128]{2,1,0:T(8,128)(2,1)S(1)} %collective-permute-done.32), channel_id=1, source_target_pairs={{1,0},{2,1},{5,4},{6,5},{9,8},{10,9},{13,12},{14,13},{17,16},{18,1... | collective-permute-start | bytes 786440 | tf_op jit(solution)/shard_map/ppermute | solution.py:48
  191.7 11.0 %collective-permute-start.43 = (bf16[4,256,128]{2,1,0:T(8,128)(2,1)S(1)}, bf16[4,256,128]{2,1,0:T(8,128)(2,1)}, u32[]{:S(2)}, u32[]{:S(2)}) collective-permute-start(bf16[4,256,128]{2,1,0:T(8,128)(2,1)S(1)} %collective-permute-done.33), channel_id=1, source_target_pairs={{1,2},{2,3},{5,6},{6,7},{9,10},{10,11},{13,14},{14,15},{17,18},{18... | collective-permute-start | bytes 786440 | tf_op jit(solution)/shard_map/ppermute | solution.py:47
  193.1 16.9 %collective-permute-start.44 = (bf16[4,256,128]{2,1,0:T(8,128)(2,1)S(1)}, bf16[4,256,128]{2,1,0:T(8,128)(2,1)}, u32[]{:S(2)}, u32[]{:S(2)}) collective-permute-start(bf16[4,256,128]{2,1,0:T(8,128)(2,1)S(1)} %collective-permute-done.34), channel_id=1, source_target_pairs={{1,0},{2,1},{5,4},{6,5},{9,8},{10,9},{13,12},{14,13},{17,16},{18,1... | collective-permute-start | bytes 786440 | tf_op jit(solution)/shard_map/ppermute | solution.py:48
  202.0 9.3 %collective-permute-start.41 = (bf16[4,256,128]{2,1,0:T(8,128)(2,1)S(1)}, bf16[4,256,128]{2,1,0:T(8,128)(2,1)S(1)}, u32[]{:S(2)}, u32[]{:S(2)}) collective-permute-start(bf16[4,256,128]{2,1,0:T(8,128)(2,1)S(1)} %collective-permute-done.39), channel_id=1, source_target_pairs={{2,3},{6,7},{10,11},{14,15},{18,19},{22,23},{26,27},{30,31}} | collective-permute-start | bytes 786440 | tf_op jit(solution)/shard_map/ppermute | solution.py:47
  202.7 13.0 %collective-permute-start.42 = (bf16[4,256,128]{2,1,0:T(8,128)(2,1)}, bf16[4,256,128]{2,1,0:T(8,128)(2,1)}, u32[]{:S(2)}, u32[]{:S(2)}) collective-permute-start(bf16[4,256,128]{2,1,0:T(8,128)(2,1)} %collective-permute-done.40), channel_id=1, source_target_pairs={{1,0},{5,4},{9,8},{13,12},{17,16},{21,20},{25,24},{29,28}} | collective-permute-start | bytes 786440 | tf_op jit(solution)/shard_map/ppermute | solution.py:48
  210.0 5.7 %collective-permute-start.45 = (bf16[4,256,128]{2,1,0:T(8,128)(2,1)}, bf16[4,256,128]{2,1,0:T(8,128)(2,1)}, u32[]{:S(2)}, u32[]{:S(2)}) collective-permute-start(bf16[4,256,128]{2,1,0:T(8,128)(2,1)} %collective-permute-done.43), channel_id=1, source_target_pairs={{2,3},{6,7},{10,11},{14,15},{18,19},{22,23},{26,27},{30,31}} | collective-permute-start | bytes 786440 | tf_op jit(solution)/shard_map/ppermute | solution.py:47
  212.1 8.6 %collective-permute-start.46 = (bf16[4,256,128]{2,1,0:T(8,128)(2,1)}, bf16[4,256,128]{2,1,0:T(8,128)(2,1)}, u32[]{:S(2)}, u32[]{:S(2)}) collective-permute-start(bf16[4,256,128]{2,1,0:T(8,128)(2,1)} %collective-permute-done.44), channel_id=1, source_target_pairs={{1,0},{5,4},{9,8},{13,12},{17,16},{21,20},{25,24},{29,28}} | collective-permute-start | bytes 786440 | tf_op jit(solution)/shard_map/ppermute | solution.py:48
  (25 other events, 374.9 us)

commit v7 on v6

--- a/solution.py
+++ b/solution.py
@@ -11,7 +11,7 @@
 HEAD = 128
 MASKED = -1e30
 ASIDE = 2.0**100
-LIMIT = 60 * 2**20
+LIMIT = 63 * 2**20
 
 
 def sources(me, count):
@@ -477,12 +477,9 @@
         return [got] + [lax.ppermute(got, "seq", ring) for ring in rings]
 
     def first_pair(first, step, last, found):
-        if first == 2 and step == 1:
-            last, sent, _ = lax.optimization_barrier((last, work(found[:2]), shares))
-            made.append(to_heads(sent))
         if first == 2 and step == 2:
-            got, last = lax.optimization_barrier((made.pop(), last))
-            made.extend(to_parts(got))
+            last, pair, mine = lax.optimization_barrier((last, found[:2], shares))
+            made.append((work(pair), mine))
         return last
 
     gathered = line_gather(
@@ -491,10 +488,14 @@
         first_pair,
     )
     rest = gathered[-2:]
+    got = []
+    if made:
+        (early, shares), rest = lax.optimization_barrier((made[0], rest))
+        got = [to_heads(early)]
     sending = send_shares(shares, tensor_count, rest[-1])
     sent = work(rest)
-    sent, sending, made = lax.optimization_barrier((sent, sending, made))
-    pieces = list(made) + to_parts(to_heads(sent))
+    sent, sending, got = lax.optimization_barrier((sent, sending, got))
+    pieces = sum([to_parts(each) for each in got + [to_heads(sent)]], [])
 
     heads, cuts, halves, _ = weight_cuts(w_out, seq_count, columns)
     held, flips = [], []

time: 233 us -> 222 us (0.953)
  starting transfers between devices: 71.3 us -> 88.7 us
  blocking collectives: 29.6 us -> 13.1 us
  waiting for transfers between devices: 66.8 us -> 56.2 us
    ppermute x18, waiting for transfers between devices: 58.9 us -> 35.8 us  [line_gather(): from_right = lax.ppermute(last[at][1], 'tensor', left[:count - 1 - step])]
    all_to_all x1 -> x0, blocking collectives: 16.4 us -> none  [to_heads(): return lax.all_to_all(sent, 'seq', split_axis=0, concat_axis=0)]
    all_to_all x1 -> x2, waiting for transfers between devices: 0.01 us -> 12.1 us  [to_heads(): return lax.all_to_all(sent, 'seq', split_axis=0, concat_axis=0)]
    ppermute x18, starting transfers between devices: 36.3 us -> 43.4 us  [line_gather(): from_left = lax.ppermute(last[at][0], 'tensor', right[step:])]
    ppermute x3, starting transfers between devices: 4.56 us -> 10.2 us  [send_shares(): shares[step] = lax.ppermute(shares[step], 'tensor', ring)]
    all_to_all x1 -> x2, starting transfers between devices: 3.72 us -> 8.33 us  [to_heads(): return lax.all_to_all(sent, 'seq', split_axis=0, concat_axis=0)]
    unnamed x88 -> x62, local copies, waits for them, and re-layouts: 5.7 us -> 4.13 us
  transfers between devices with their start and end apart: 48 -> 49, of which waited for: 15 -> 14; matrix products, arithmetic and copies ran while one was open for 3% -> 3% of each run, Pallas kernels for 17% -> 18%
where the time goes in v7:
time: 222 us; the launch traced here: 221 us
  starting transfers between devices  88.7 us (40%)
  waiting for transfers between devices  56.2 us (25%)
  Pallas kernels  48.9 us (22%)
  blocking collectives  13.1 us (6%)
  local copies, waits for them, and re-layouts  10.1 us (5%)
  other arithmetic  2.86 us (1%)
    ppermute x18, starting transfers between devices, line_gather(): from_left = lax.ppermute(last[at][0], 'tensor', right[step:])  43.4 us
    ppermute x18, waiting for transfers between devices, line_gather(): from_right = lax.ppermute(last[at][1], 'tensor', left[:count - 1 - step])  35.8 us
    pallas_call x2, Pallas kernels, project(): pl.pallas_call(partial(project_kernel, group, count), in_specs=[pl.BlockS...  24.8 us
    ppermute x18, starting transfers between devices, line_gather(): from_right = lax.ppermute(last[at][1], 'tensor', left[:count - 1 - step])  23.4 us
    all_to_all x1, blocking collectives, shards(): home = lax.all_to_all(out, 'seq', split_axis=0, concat_axis=0)  13.1 us
    all_to_all x2, waiting for transfers between devices, to_heads(): return lax.all_to_all(sent, 'seq', split_axis=0, concat_axis=0)  12.1 us
    pallas_call x1, Pallas kernels, attend(): pl.pallas_call(partial(attend_kernel, chunks, group, rows), in_specs=[pl....  11.3 us
    ppermute x3, starting transfers between devices, send_shares(): shares[step] = lax.ppermute(shares[step], 'tensor', ring)  10.2 us
  transfers between devices with their start and end apart: 49, of which 14 were waited for; matrix products, arithmetic and copies ran while one was open for 3% of the time, Pallas kernels for 18%

profile of v7, /device:TPU:0, one launch (start us, length us, event | category | flops | bytes accessed | tf_op | source)
XLA Modules:
  0.0 220.8 jit_solution(7370651758085545028)
XLA Ops:
  0.0 1.3 fusion.5
  1.3 1.3 collective-permute-start.1
  2.6 5.6 %collective-permute-start = (bf16[128,1024]{1,0:T(8,128)(2,1)S(1)}, bf16[128,1024]{1,0:T(8,128)(2,1)S(1)}, u32[]{:S(2)}, u32[]{:S(2)}) collective-permute-start(bf16[128,1024]{1,0:T(8,128)(2,1)S(1)} %get-tuple-element.90.refs_3_), channel_id=1, source_target_pairs={{0,1},{1,2},{2,3},{4,5},{5,6},{6,7},{8,9},{9,10},{10,11},{12,13},{... | collective-permute-start | bytes 786440 | tf_op jit(solution)/shard_map/ppermute | solution.py:47
  8.2 1.3 collective-permute-start.15
  9.5 3.3 %collective-permute-done.1.refs_5_ = bf16[128,1024]{1,0:T(8,128)(2,1)S(1)} collective-permute-done((bf16[128,1024]{1,0:T(8,128)(2,1)S(1)}, bf16[128,1024]{1,0:T(8,128)(2,1)S(1)}, u32[]{:S(2)}, u32[]{:S(2)}) %collective-permute-start.1) | collective-permute-done | bytes 262176 | tf_op jit(solution)/shard_map/ppermute | solution.py:48
  12.8 1.3 collective-permute-start.3
  14.8 7.6 %collective-permute-start.14 = (bf16[128,1024]{1,0:T(8,128)(2,1)S(1)}, bf16[128,1024]{1,0:T(8,128)(2,1)S(1)}, u32[]{:S(2)}, u32[]{:S(2)}) collective-permute-start(bf16[128,1024]{1,0:T(8,128)(2,1)S(1)} %get-tuple-element.97.refs_10_), channel_id=1, source_target_pairs={{0,1},{1,2},{2,3},{4,5},{5,6},{6,7},{8,9},{9,10},{10,11},{12,13},{... | collective-permute-start | bytes 786440 | tf_op jit(solution)/shard_map/ppermute | solution.py:47
  22.4 1.3 collective-permute-start.17
  23.8 1.3 collective-permute-start.5
  26.2 1.4 collective-permute-start.16
  27.6 5.6 %collective-permute-done.17.refs_14_ = bf16[128,1024]{1,0:T(8,128)(2,1)S(1)} collective-permute-done((bf16[128,1024]{1,0:T(8,128)(2,1)S(1)}, bf16[128,1024]{1,0:T(8,128)(2,1)S(1)}, u32[]{:S(2)}, u32[]{:S(2)}) %collective-permute-start.17) | collective-permute-done | bytes 262176 | tf_op jit(solution)/shard_map/ppermute | solution.py:48
  33.1 1.3 collective-permute-start.19
  34.4 2.8 %collective-permute-done.5.refs_9_ = bf16[128,1024]{1,0:T(8,128)(2,1)S(1)} collective-permute-done((bf16[128,1024]{1,0:T(8,128)(2,1)S(1)}, bf16[128,1024]{1,0:T(8,128)(2,1)S(1)}, u32[]{:S(2)}, u32[]{:S(2)}) %collective-permute-start.5) | collective-permute-done | bytes 262176 | tf_op jit(solution)/shard_map/ppermute | solution.py:48
  37.2 1.3 collective-permute-start.8
  38.5 5.2 %collective-permute-start.6 = (bf16[128,1024]{1,0:T(8,128)(2,1)S(1)}, bf16[128,1024]{1,0:T(8,128)(2,1)}, u32[]{:S(2)}, u32[]{:S(2)}) collective-permute-start(bf16[128,1024]{1,0:T(8,128)(2,1)S(1)} %get-tuple-element.112.refs_3_), channel_id=1, source_target_pairs={{0,1},{1,2},{2,3},{4,5},{5,6},{6,7},{8,9},{9,10},{10,11},{12,13},{... | collective-permute-start | bytes 786440 | tf_op jit(solution)/shard_map/ppermute | solution.py:47
  43.8 1.3 collective-permute-start.12
  45.1 5.2 %collective-permute-start.10 = (bf16[128,1024]{1,0:T(8,128)(2,1)S(1)}, bf16[128,1024]{1,0:T(8,128)(2,1)}, u32[]{:S(2)}, u32[]{:S(2)}) collective-permute-start(bf16[128,1024]{1,0:T(8,128)(2,1)S(1)} %get-tuple-element.119.refs_10_), channel_id=1, source_target_pairs={{0,1},{1,2},{2,3},{4,5},{5,6},{6,7},{8,9},{9,10},{10,11},{12,13},{... | collective-permute-start | bytes 786440 | tf_op jit(solution)/shard_map/ppermute | solution.py:47
  50.4 1.3 reshape.57.gain_ref
  52.4 1.4 collective-permute-start.18
  53.8 1.3 collective-permute-start.9
  55.1 1.4 collective-permute-start.7
  56.5 1.3 collective-permute-start.13
  57.8 1.4 collective-permute-start.11
  59.2 0.8 copy.8.active_ref
  60.6 3.5 %shard_map.73 = (bf16[2,128,256]{2,1,0:T(8,128)(2,1)}, bf16[2,128,256]{2,1,0:T(8,128)(2,1)}, bf16[2,128,256]{2,1,0:T(8,128)(2,1)}, bf16[2,128,256]{2,1,0:T(8,128)(2,1)}) custom-call(s32[3]{0:T(128)} %pad_add_fusion.place_ref, bf16[512,4096]{1,0:T(8,128)(2,1)} %w_ref.1), custom_call_target="tpu_custom_call" | custom-call | tf_op jit(solution)/shard_map/pallas_call | solution.py:372
  64.1 3.8 %collective-permute-done.13.refs_14_ = bf16[128,1024]{1,0:T(8,128)(2,1)} collective-permute-done((bf16[128,1024]{1,0:T(8,128)(2,1)}, bf16[128,1024]{1,0:T(8,128)(2,1)}, u32[]{:S(2)}, u32[]{:S(2)}) %collective-permute-start.13) | collective-permute-done | bytes 262176 | tf_op jit(solution)/shard_map/ppermute | solution.py:48
  67.8 1.5 collective-permute-start.20
  69.3 1.3 collective-permute-start.21
  70.6 1.4 collective-permute-start.22
  72.0 1.3 collective-permute-start.23
  73.3 12.4 %shard_map.74 = bf16[8,128,384]{2,1,0:T(8,128)(2,1)} custom-call(s32[1]{0:T(128)} %bitcast.me_ref, f32[4,1024]{1,0:T(4,128)} %reshape.57.gain_ref, s32[256,1]{1,0:T(8,128)} %copy.8.active_ref, bf16[4096,512]{1,0:T(8,128)(2,1)} %refs_0_.3, bf16[4096,512]{1,0:T(8,128)(2,1)} %refs_1_.3, bf16[4096,512]{1,0:T(8,128)(2,1)} %refs_2_.3, ...), custom_call_target="tpu_custom_call" | custom-call | flops 3221225472 | bytes 15466496 | tf_op jit(solution)/shard_map/pallas_call | solution.py:128
  85.8 4.2 %all-to-all-start = ((bf16[8,128,384]{2,1,0:T(8,128)(2,1)}), bf16[8,128,384]{2,1,0:T(8,128)(2,1)}, u32[]{:S(2)}, u32[]{:S(2)}) async-start(bf16[8,128,384]{2,1,0:T(8,128)(2,1)} %shard_map.74), calls=%async_computation | async-start | bytes 1572864 | tf_op jit(solution)/shard_map/all_to_all | solution.py:470
  90.0 0.8 copy.9.active_ref
  90.8 6.4 %collective-permute-start.24 = (bf16[2,128,256]{2,1,0:T(8,128)(2,1)}, bf16[2,128,256]{2,1,0:T(8,128)(2,1)S(1)}, u32[]{:S(2)}, u32[]{:S(2)}) collective-permute-start(bf16[2,128,256]{2,1,0:T(8,128)(2,1)} %get-tuple-element.131), channel_id=1, source_target_pairs={{0,1},{1,2},{2,3},{3,0},{4,5},{5,6},{6,7},{7,4},{8,9},{9,10},{10,1... | collective-permute-start | bytes 393224 | tf_op jit(solution)/shard_map/ppermute | solution.py:414
  97.2 0.9 collective-permute-start.25
  98.1 2.9 %collective-permute-start.26 = (bf16[2,128,256]{2,1,0:T(8,128)(2,1)S(1)}, bf16[2,128,256]{2,1,0:T(8,128)(2,1)S(1)}, u32[]{:S(2)}, u32[]{:S(2)}) collective-permute-start(bf16[2,128,256]{2,1,0:T(8,128)(2,1)S(1)} %copy-done.27), channel_id=1, source_target_pairs={{0,3},{1,0},{2,1},{3,2},{4,7},{5,4},{6,5},{7,6},{8,11},{9,8},{10,9... | collective-permute-start | bytes 393224 | tf_op jit(solution)/shard_map/ppermute | solution.py:414
  101.0 12.4 %shard_map.75 = bf16[8,128,384]{2,1,0:T(8,128)(2,1)} custom-call(s32[1]{0:T(128)} %bitcast.me_ref, f32[4,1024]{1,0:T(4,128)} %reshape.57.gain_ref, s32[256,1]{1,0:T(8,128)} %copy.9.active_ref, bf16[4096,512]{1,0:T(8,128)(2,1)} %refs_0_.3, bf16[4096,512]{1,0:T(8,128)(2,1)} %refs_1_.3, bf16[4096,512]{1,0:T(8,128)(2,1)} %refs_2_.3, ...), custom_call_target="tpu_custom_call" | custom-call | flops 3221225472 | bytes 15466496 | tf_op jit(solution)/shard_map/pallas_call | solution.py:128
  113.4 4.1 %all-to-all-start.1 = ((bf16[8,128,384]{2,1,0:T(8,128)(2,1)}), bf16[8,128,384]{2,1,0:T(8,128)(2,1)S(1)}, u32[]{:S(2)}, u32[]{:S(2)}) async-start(bf16[8,128,384]{2,1,0:T(8,128)(2,1)} %shard_map.75), calls=%async_computation.1 | async-start | bytes 1572864 | tf_op jit(solution)/shard_map/all_to_all | solution.py:470
  118.0 12.1 %all-to-all-done.1.refs_2_ = bf16[8,128,384]{2,1,0:T(8,128)(2,1)S(1)} async-done(((bf16[8,128,384]{2,1,0:T(8,128)(2,1)}), bf16[8,128,384]{2,1,0:T(8,128)(2,1)S(1)}, u32[]{:S(2)}, u32[]{:S(2)}) %all-to-all-start.1) | async-done | bytes 786464 | tf_op jit(solution)/shard_map/all_to_all | solution.py:470
  131.7 0.9 collective-permute-done.28.refs_3_
  132.6 11.3 %shard_map.76 = bf16[8,256,128]{2,1,0:T(8,128)(2,1)} custom-call(s32[1]{0:T(128)} %bitcast.6.part_ref, bf16[8,128,384]{2,1,0:T(8,128)(2,1)} %all-to-all-done.refs_0_, bf16[8,128,384]{2,1,0:T(8,128)(2,1)} %collective-permute-done.27.refs_1_, bf16[8,128,384]{2,1,0:T(8,128)(2,1)} %copy-done.9, bf16[8,128,384]{2,1,0:T(8,128)(2,1)} %collective-permute-done.28.refs_3_), custom_call_target="tpu_custom_call" | custom-call | flops 3623878656 | bytes 4194304 | tf_op jit(solution)/shard_map/pallas_call | solution.py:256
  143.8 13.1 %all_to_all.15 = bf16[8,256,128]{2,1,0:T(8,128)(2,1)S(1)} all-to-all(bf16[8,256,128]{2,1,0:T(8,128)(2,1)} %shard_map.76), channel_id=1, replica_groups=mesh['seq'=8,'tensor'=4] {'seq'}, dimensions={0} | all-to-all | bytes 1048576 | tf_op jit(solution)/shard_map/all_to_all | solution.py:512
  157.0 1.0 pad_maximum_fusion.1
  159.3 1.3 collective-permute-start.34
  160.6 4.6 %collective-permute-start.33 = (bf16[4,256,128]{2,1,0:T(8,128)(2,1)S(1)}, bf16[4,256,128]{2,1,0:T(8,128)(2,1)S(1)}, u32[]{:S(2)}, u32[]{:S(2)}) collective-permute-start(bf16[4,256,128]{2,1,0:T(8,128)(2,1)S(1)} %get-tuple-element.171), channel_id=1, source_target_pairs={{0,1},{1,2},{2,3},{4,5},{5,6},{6,7},{8,9},{9,10},{10,11},{12,13},{... | collective-permute-start | bytes 786440 | tf_op jit(solution)/shard_map/ppermute | solution.py:47
  165.2 1.3 collective-permute-start.32
  166.5 4.6 %collective-permute-done.36 = bf16[1024,256]{1,0:T(8,128)(2,1)S(1)} collective-permute-done((bf16[1024,256]{1,0:T(8,128)(2,1)S(1)}, bf16[1024,256]{1,0:T(8,128)(2,1)S(1)}, u32[]{:S(2)}, u32[]{:S(2)}) %collective-permute-start.36) | collective-permute-done | bytes 524320 | tf_op jit(solution)/shard_map/ppermute | solution.py:424
  171.0 1.3 collective-permute-start.31
  172.5 1.8 collective-permute-done.32
  174.3 2.3 %collective-permute-done.31 = bf16[4,256,128]{2,1,0:T(8,128)(2,1)S(1)} collective-permute-done((bf16[4,256,128]{2,1,0:T(8,128)(2,1)S(1)}, bf16[4,256,128]{2,1,0:T(8,128)(2,1)S(1)}, u32[]{:S(2)}, u32[]{:S(2)}) %collective-permute-start.31) | collective-permute-done | bytes 262176 | tf_op jit(solution)/shard_map/ppermute | solution.py:47
  176.7 1.0 constant_dynamic-update-slice_fusion.5
  177.9 1.1 copy-done
  180.0 1.3 collective-permute-start.40
  181.3 1.4 collective-permute-start.43
  182.7 1.3 collective-permute-start.44
  184.0 7.7 %collective-permute-done.40 = bf16[4,256,128]{2,1,0:T(8,128)(2,1)} collective-permute-done((bf16[4,256,128]{2,1,0:T(8,128)(2,1)S(1)}, bf16[4,256,128]{2,1,0:T(8,128)(2,1)}, u32[]{:S(2)}, u32[]{:S(2)}) %collective-permute-start.40) | collective-permute-done | bytes 262176 | tf_op jit(solution)/shard_map/ppermute | solution.py:48
  192.5 1.3 collective-permute-start.42
  193.8 5.8 %collective-permute-done.44 = bf16[4,256,128]{2,1,0:T(8,128)(2,1)} collective-permute-done((bf16[4,256,128]{2,1,0:T(8,128)(2,1)S(1)}, bf16[4,256,128]{2,1,0:T(8,128)(2,1)}, u32[]{:S(2)}, u32[]{:S(2)}) %collective-permute-start.44) | collective-permute-done | bytes 262176 | tf_op jit(solution)/shard_map/ppermute | solution.py:48
  199.6 1.4 collective-permute-start.45
  201.7 1.5 collective-permute-start.46
  203.2 0.9 copy.10.active_ref
  205.3 5.0 %collective-permute-done.46 = bf16[4,256,128]{2,1,0:T(8,128)(2,1)} collective-permute-done((bf16[4,256,128]{2,1,0:T(8,128)(2,1)}, bf16[4,256,128]{2,1,0:T(8,128)(2,1)}, u32[]{:S(2)}, u32[]{:S(2)}) %collective-permute-start.46) | collective-permute-done | bytes 262176 | tf_op jit(solution)/shard_map/ppermute | solution.py:48
  210.2 1.0 copy-done.6
  211.2 9.4 %shard_map.77 = bf16[512,1024]{1,0:T(8,128)(2,1)} custom-call(s32[5]{0:T(128)} %stack.31.me_ref, s32[16]{0:T(128)} %fusion.at_ref, s32[512,1]{1,0:T(8,128)} %copy.10.active_ref, bf16[512,1024]{1,0:T(8,128)(2,1)} %hidden_ref.1, bf16[2048,256]{1,0:T(8,128)(2,1)} %copy-done, bf16[2048,256]{1,0:T(8,128)(2,1)} %copy-done.1, bf16[2048,256]{1,0:T(8,128)(2,1)} %copy-done.6, ...), custom_call_target="tpu_custom_call" | custom-call | flops 2147483648 | bytes 8388608 | tf_op jit(solution)/shard_map/pallas_call | solution.py:336
  (123 shorter events, 10.5 us)
Async XLA Ops:
  1.3 43.8 %copy-start.5 = (bf16[128,1024]{1,0:T(8,128)(2,1)}, bf16[128,1024]{1,0:T(8,128)(2,1)S(1)}, u32[]{:S(2)}) copy-start(bf16[128,1024]{1,0:T(8,128)(2,1)S(1)} %get-tuple-element.90.refs_3_) | copy-start | bytes 786436
  1.3 72.0 %copy-start.4 = (bf16[128,1024]{1,0:T(8,128)(2,1)}, bf16[128,1024]{1,0:T(8,128)(2,1)S(1)}, u32[]{:S(2)}) copy-start(bf16[128,1024]{1,0:T(8,128)(2,1)S(1)} %get-tuple-element.97.refs_10_) | copy-start | bytes 786436
  1.3 84.4 %copy-start.2 = (bf16[128,1024]{1,0:T(8,128)(2,1)}, bf16[128,1024]{1,0:T(8,128)(2,1)S(1)}, u32[]{:S(2)}) copy-start(bf16[128,1024]{1,0:T(8,128)(2,1)S(1)} %get-tuple-element.119.refs_10_) | copy-start | bytes 786436
  1.3 84.4 %copy-start.3 = (bf16[128,1024]{1,0:T(8,128)(2,1)}, bf16[128,1024]{1,0:T(8,128)(2,1)S(1)}, u32[]{:S(2)}) copy-start(bf16[128,1024]{1,0:T(8,128)(2,1)S(1)} %get-tuple-element.112.refs_3_) | copy-start | bytes 786436
  1.3 11.5 %collective-permute-start.1 = (bf16[128,1024]{1,0:T(8,128)(2,1)S(1)}, bf16[128,1024]{1,0:T(8,128)(2,1)S(1)}, u32[]{:S(2)}, u32[]{:S(2)}) collective-permute-start(bf16[128,1024]{1,0:T(8,128)(2,1)S(1)} %get-tuple-element.90.refs_3_), channel_id=1, source_target_pairs={{1,0},{2,1},{3,2},{5,4},{6,5},{7,6},{9,8},{10,9},{11,10},{13,12},{... | collective-permute-start | bytes 786440 | tf_op jit(solution)/shard_map/ppermute | solution.py:48
  2.6 11.5 %collective-permute-start = (bf16[128,1024]{1,0:T(8,128)(2,1)S(1)}, bf16[128,1024]{1,0:T(8,128)(2,1)S(1)}, u32[]{:S(2)}, u32[]{:S(2)}) collective-permute-start(bf16[128,1024]{1,0:T(8,128)(2,1)S(1)} %get-tuple-element.90.refs_3_), channel_id=1, source_target_pairs={{0,1},{1,2},{2,3},{4,5},{5,6},{6,7},{8,9},{9,10},{10,11},{12,13},{... | collective-permute-start | bytes 786440 | tf_op jit(solution)/shard_map/ppermute | solution.py:47
  8.2 14.2 %collective-permute-start.15 = (bf16[128,1024]{1,0:T(8,128)(2,1)S(1)}, bf16[128,1024]{1,0:T(8,128)(2,1)S(1)}, u32[]{:S(2)}, u32[]{:S(2)}) collective-permute-start(bf16[128,1024]{1,0:T(8,128)(2,1)S(1)} %get-tuple-element.97.refs_10_), channel_id=1, source_target_pairs={{1,0},{2,1},{3,2},{5,4},{6,5},{7,6},{9,8},{10,9},{11,10},{13,12},{... | collective-permute-start | bytes 786440 | tf_op jit(solution)/shard_map/ppermute | solution.py:48
  12.8 32.3 %copy-start.10 = (bf16[128,1024]{1,0:T(8,128)(2,1)}, bf16[128,1024]{1,0:T(8,128)(2,1)S(1)}, u32[]{:S(2)}) copy-start(bf16[128,1024]{1,0:T(8,128)(2,1)S(1)} %collective-permute-done.1.refs_5_) | copy-start | bytes 786436
  12.8 11.0 %collective-permute-start.3 = (bf16[128,1024]{1,0:T(8,128)(2,1)S(1)}, bf16[128,1024]{1,0:T(8,128)(2,1)S(1)}, u32[]{:S(2)}, u32[]{:S(2)}) collective-permute-start(bf16[128,1024]{1,0:T(8,128)(2,1)S(1)} %collective-permute-done.1.refs_5_), channel_id=1, source_target_pairs={{1,0},{2,1},{5,4},{6,5},{9,8},{10,9},{13,12},{14,13},{17,16},{18,1... | collective-permute-start | bytes 786440 | tf_op jit(solution)/shard_map/ppermute | solution.py:48
  14.1 36.3 %copy-start.11 = (bf16[128,1024]{1,0:T(8,128)(2,1)}, bf16[128,1024]{1,0:T(8,128)(2,1)S(1)}, u32[]{:S(2)}) copy-start(bf16[128,1024]{1,0:T(8,128)(2,1)S(1)} %collective-permute-done.refs_4_) | copy-start | bytes 786436
  14.1 11.0 %collective-permute-start.2 = (bf16[128,1024]{1,0:T(8,128)(2,1)S(1)}, bf16[128,1024]{1,0:T(8,128)(2,1)S(1)}, u32[]{:S(2)}, u32[]{:S(2)}) collective-permute-start(bf16[128,1024]{1,0:T(8,128)(2,1)S(1)} %collective-permute-done.refs_4_), channel_id=1, source_target_pairs={{1,2},{2,3},{5,6},{6,7},{9,10},{10,11},{13,14},{14,15},{17,18},{18... | collective-permute-start | bytes 786440 | tf_op jit(solution)/shard_map/ppermute | solution.py:47
  14.8 11.4 %collective-permute-start.14 = (bf16[128,1024]{1,0:T(8,128)(2,1)S(1)}, bf16[128,1024]{1,0:T(8,128)(2,1)S(1)}, u32[]{:S(2)}, u32[]{:S(2)}) collective-permute-start(bf16[128,1024]{1,0:T(8,128)(2,1)S(1)} %get-tuple-element.97.refs_10_), channel_id=1, source_target_pairs={{0,1},{1,2},{2,3},{4,5},{5,6},{6,7},{8,9},{9,10},{10,11},{12,13},{... | collective-permute-start | bytes 786440 | tf_op jit(solution)/shard_map/ppermute | solution.py:47
  22.3 28.0 %copy-start.12 = (bf16[128,1024]{1,0:T(8,128)(2,1)}, bf16[128,1024]{1,0:T(8,128)(2,1)S(1)}, u32[]{:S(2)}) copy-start(bf16[128,1024]{1,0:T(8,128)(2,1)S(1)} %collective-permute-done.15.refs_12_) | copy-start | bytes 786436
  22.4 10.8 %collective-permute-start.17 = (bf16[128,1024]{1,0:T(8,128)(2,1)S(1)}, bf16[128,1024]{1,0:T(8,128)(2,1)S(1)}, u32[]{:S(2)}, u32[]{:S(2)}) collective-permute-start(bf16[128,1024]{1,0:T(8,128)(2,1)S(1)} %collective-permute-done.15.refs_12_), channel_id=1, source_target_pairs={{1,0},{2,1},{5,4},{6,5},{9,8},{10,9},{13,12},{14,13},{17,16},{18,1... | collective-permute-start | bytes 786440 | tf_op jit(solution)/shard_map/ppermute | solution.py:48
  23.8 26.6 %copy-start.13 = (bf16[128,1024]{1,0:T(8,128)(2,1)}, bf16[128,1024]{1,0:T(8,128)(2,1)S(1)}, u32[]{:S(2)}) copy-start(bf16[128,1024]{1,0:T(8,128)(2,1)S(1)} %collective-permute-done.3.refs_7_) | copy-start | bytes 786436
  23.8 13.5 %collective-permute-start.5 = (bf16[128,1024]{1,0:T(8,128)(2,1)S(1)}, bf16[128,1024]{1,0:T(8,128)(2,1)S(1)}, u32[]{:S(2)}, u32[]{:S(2)}) collective-permute-start(bf16[128,1024]{1,0:T(8,128)(2,1)S(1)} %collective-permute-done.3.refs_7_), channel_id=1, source_target_pairs={{1,0},{5,4},{9,8},{13,12},{17,16},{21,20},{25,24},{29,28}} | collective-permute-start | bytes 786440 | tf_op jit(solution)/shard_map/ppermute | solution.py:48
  25.1 25.3 %copy-start.14 = (bf16[128,1024]{1,0:T(8,128)(2,1)}, bf16[128,1024]{1,0:T(8,128)(2,1)S(1)}, u32[]{:S(2)}) copy-start(bf16[128,1024]{1,0:T(8,128)(2,1)S(1)} %collective-permute-done.2.refs_6_) | copy-start | bytes 786436
  25.1 12.1 %collective-permute-start.4 = (bf16[128,1024]{1,0:T(8,128)(2,1)S(1)}, bf16[128,1024]{1,0:T(8,128)(2,1)S(1)}, u32[]{:S(2)}, u32[]{:S(2)}) collective-permute-start(bf16[128,1024]{1,0:T(8,128)(2,1)S(1)} %collective-permute-done.2.refs_6_), channel_id=1, source_target_pairs={{2,3},{6,7},{10,11},{14,15},{18,19},{22,23},{26,27},{30,31}} | collective-permute-start | bytes 786440 | tf_op jit(solution)/shard_map/ppermute | solution.py:47
  26.2 18.9 %collective-permute-start.16 = (bf16[128,1024]{1,0:T(8,128)(2,1)S(1)}, bf16[128,1024]{1,0:T(8,128)(2,1)}, u32[]{:S(2)}, u32[]{:S(2)}) collective-permute-start(bf16[128,1024]{1,0:T(8,128)(2,1)S(1)} %collective-permute-done.14.refs_11_), channel_id=1, source_target_pairs={{1,2},{2,3},{5,6},{6,7},{9,10},{10,11},{13,14},{14,15},{17,18},{18... | collective-permute-start | bytes 786440 | tf_op jit(solution)/shard_map/ppermute | solution.py:47
  33.1 19.2 %collective-permute-start.19 = (bf16[128,1024]{1,0:T(8,128)(2,1)S(1)}, bf16[128,1024]{1,0:T(8,128)(2,1)S(1)}, u32[]{:S(2)}, u32[]{:S(2)}) collective-permute-start(bf16[128,1024]{1,0:T(8,128)(2,1)S(1)} %collective-permute-done.17.refs_14_), channel_id=1, source_target_pairs={{1,0},{5,4},{9,8},{13,12},{17,16},{21,20},{25,24},{29,28}} | collective-permute-start | bytes 786440 | tf_op jit(solution)/shard_map/ppermute | solution.py:48
  37.2 16.6 %collective-permute-start.8 = (bf16[128,1024]{1,0:T(8,128)(2,1)S(1)}, bf16[128,1024]{1,0:T(8,128)(2,1)}, u32[]{:S(2)}, u32[]{:S(2)}) collective-permute-start(bf16[128,1024]{1,0:T(8,128)(2,1)S(1)} %get-tuple-element.112.refs_3_), channel_id=1, source_target_pairs={{1,0},{2,1},{3,2},{5,4},{6,5},{7,6},{9,8},{10,9},{11,10},{13,12},{... | collective-permute-start | bytes 786440 | tf_op jit(solution)/shard_map/ppermute | solution.py:48
  38.5 16.6 %collective-permute-start.6 = (bf16[128,1024]{1,0:T(8,128)(2,1)S(1)}, bf16[128,1024]{1,0:T(8,128)(2,1)}, u32[]{:S(2)}, u32[]{:S(2)}) collective-permute-start(bf16[128,1024]{1,0:T(8,128)(2,1)S(1)} %get-tuple-element.112.refs_3_), channel_id=1, source_target_pairs={{0,1},{1,2},{2,3},{4,5},{5,6},{6,7},{8,9},{9,10},{10,11},{12,13},{... | collective-permute-start | bytes 786440 | tf_op jit(solution)/shard_map/ppermute | solution.py:47
  43.8 12.7 %collective-permute-start.12 = (bf16[128,1024]{1,0:T(8,128)(2,1)S(1)}, bf16[128,1024]{1,0:T(8,128)(2,1)}, u32[]{:S(2)}, u32[]{:S(2)}) collective-permute-start(bf16[128,1024]{1,0:T(8,128)(2,1)S(1)} %get-tuple-element.119.refs_10_), channel_id=1, source_target_pairs={{1,0},{2,1},{3,2},{5,4},{6,5},{7,6},{9,8},{10,9},{11,10},{13,12},{... | collective-permute-start | bytes 786440 | tf_op jit(solution)/shard_map/ppermute | solution.py:48
  45.1 12.7 %collective-permute-start.10 = (bf16[128,1024]{1,0:T(8,128)(2,1)S(1)}, bf16[128,1024]{1,0:T(8,128)(2,1)}, u32[]{:S(2)}, u32[]{:S(2)}) collective-permute-start(bf16[128,1024]{1,0:T(8,128)(2,1)S(1)} %get-tuple-element.119.refs_10_), channel_id=1, source_target_pairs={{0,1},{1,2},{2,3},{4,5},{5,6},{6,7},{8,9},{9,10},{10,11},{12,13},{... | collective-permute-start | bytes 786440 | tf_op jit(solution)/shard_map/ppermute | solution.py:47
  52.4 11.7 %collective-permute-start.18 = (bf16[128,1024]{1,0:T(8,128)(2,1)}, bf16[128,1024]{1,0:T(8,128)(2,1)}, u32[]{:S(2)}, u32[]{:S(2)}) collective-permute-start(bf16[128,1024]{1,0:T(8,128)(2,1)} %collective-permute-done.16.refs_13_), channel_id=1, source_target_pairs={{2,3},{6,7},{10,11},{14,15},{18,19},{22,23},{26,27},{30,31}} | collective-permute-start | bytes 786440 | tf_op jit(solution)/shard_map/ppermute | solution.py:47
  53.8 10.3 %collective-permute-start.9 = (bf16[128,1024]{1,0:T(8,128)(2,1)}, bf16[128,1024]{1,0:T(8,128)(2,1)}, u32[]{:S(2)}, u32[]{:S(2)}) collective-permute-start(bf16[128,1024]{1,0:T(8,128)(2,1)} %collective-permute-done.8.refs_5_), channel_id=1, source_target_pairs={{1,0},{2,1},{5,4},{6,5},{9,8},{10,9},{13,12},{14,13},{17,16},{18,1... | collective-permute-start | bytes 786440 | tf_op jit(solution)/shard_map/ppermute | solution.py:48
  55.1 9.0 %collective-permute-start.7 = (bf16[128,1024]{1,0:T(8,128)(2,1)}, bf16[128,1024]{1,0:T(8,128)(2,1)}, u32[]{:S(2)}, u32[]{:S(2)}) collective-permute-start(bf16[128,1024]{1,0:T(8,128)(2,1)} %collective-permute-done.6.refs_4_), channel_id=1, source_target_pairs={{1,2},{2,3},{5,6},{6,7},{9,10},{10,11},{13,14},{14,15},{17,18},{18... | collective-permute-start | bytes 786440 | tf_op jit(solution)/shard_map/ppermute | solution.py:47
  56.5 11.3 %collective-permute-start.13 = (bf16[128,1024]{1,0:T(8,128)(2,1)}, bf16[128,1024]{1,0:T(8,128)(2,1)}, u32[]{:S(2)}, u32[]{:S(2)}) collective-permute-start(bf16[128,1024]{1,0:T(8,128)(2,1)} %collective-permute-done.12.refs_12_), channel_id=1, source_target_pairs={{1,0},{2,1},{5,4},{6,5},{9,8},{10,9},{13,12},{14,13},{17,16},{18,1... | collective-permute-start | bytes 786440 | tf_op jit(solution)/shard_map/ppermute | solution.py:48
  57.8 10.0 %collective-permute-start.11 = (bf16[128,1024]{1,0:T(8,128)(2,1)}, bf16[128,1024]{1,0:T(8,128)(2,1)}, u32[]{:S(2)}, u32[]{:S(2)}) collective-permute-start(bf16[128,1024]{1,0:T(8,128)(2,1)} %collective-permute-done.10.refs_11_), channel_id=1, source_target_pairs={{1,2},{2,3},{5,6},{6,7},{9,10},{10,11},{13,14},{14,15},{17,18},{18... | collective-permute-start | bytes 786440 | tf_op jit(solution)/shard_map/ppermute | solution.py:47
  67.8 30.2 %copy-start.27 = (bf16[2,128,256]{2,1,0:T(8,128)(2,1)S(1)}, bf16[2,128,256]{2,1,0:T(8,128)(2,1)}, u32[]{:S(2)}) copy-start(bf16[2,128,256]{2,1,0:T(8,128)(2,1)} %get-tuple-element.133) | copy-start | bytes 393220
  67.8 17.9 %collective-permute-start.20 = (bf16[128,1024]{1,0:T(8,128)(2,1)}, bf16[128,1024]{1,0:T(8,128)(2,1)}, u32[]{:S(2)}, u32[]{:S(2)}) collective-permute-start(bf16[128,1024]{1,0:T(8,128)(2,1)} %collective-permute-done.7.refs_6_), channel_id=1, source_target_pairs={{2,3},{6,7},{10,11},{14,15},{18,19},{22,23},{26,27},{30,31}} | collective-permute-start | bytes 786440 | tf_op jit(solution)/shard_map/ppermute | solution.py:47
  69.3 16.4 %collective-permute-start.21 = (bf16[128,1024]{1,0:T(8,128)(2,1)}, bf16[128,1024]{1,0:T(8,128)(2,1)}, u32[]{:S(2)}, u32[]{:S(2)}) collective-permute-start(bf16[128,1024]{1,0:T(8,128)(2,1)} %collective-permute-done.9.refs_7_), channel_id=1, source_target_pairs={{1,0},{5,4},{9,8},{13,12},{17,16},{21,20},{25,24},{29,28}} | collective-permute-start | bytes 786440 | tf_op jit(solution)/shard_map/ppermute | solution.py:48
  70.6 15.1 %collective-permute-start.22 = (bf16[128,1024]{1,0:T(8,128)(2,1)}, bf16[128,1024]{1,0:T(8,128)(2,1)}, u32[]{:S(2)}, u32[]{:S(2)}) collective-permute-start(bf16[128,1024]{1,0:T(8,128)(2,1)} %collective-permute-done.11.refs_13_), channel_id=1, source_target_pairs={{2,3},{6,7},{10,11},{14,15},{18,19},{22,23},{26,27},{30,31}} | collective-permute-start | bytes 786440 | tf_op jit(solution)/shard_map/ppermute | solution.py:47
  72.0 13.8 %collective-permute-start.23 = (bf16[128,1024]{1,0:T(8,128)(2,1)}, bf16[128,1024]{1,0:T(8,128)(2,1)}, u32[]{:S(2)}, u32[]{:S(2)}) collective-permute-start(bf16[128,1024]{1,0:T(8,128)(2,1)} %collective-permute-done.13.refs_14_), channel_id=1, source_target_pairs={{1,0},{5,4},{9,8},{13,12},{17,16},{21,20},{25,24},{29,28}} | collective-permute-start | bytes 786440 | tf_op jit(solution)/shard_map/ppermute | solution.py:48
  85.8 27.7 %all-to-all-start = ((bf16[8,128,384]{2,1,0:T(8,128)(2,1)}), bf16[8,128,384]{2,1,0:T(8,128)(2,1)}, u32[]{:S(2)}, u32[]{:S(2)}) async-start(bf16[8,128,384]{2,1,0:T(8,128)(2,1)} %shard_map.74), calls=%async_computation | async-start | bytes 1572864 | tf_op jit(solution)/shard_map/all_to_all | solution.py:470
  90.8 39.3 %copy-start.26 = (bf16[2,128,256]{2,1,0:T(8,128)(2,1)S(1)}, bf16[2,128,256]{2,1,0:T(8,128)(2,1)}, u32[]{:S(2)}) copy-start(bf16[2,128,256]{2,1,0:T(8,128)(2,1)} %get-tuple-element.137) | copy-start | bytes 393220
  90.8 22.6 %collective-permute-start.24 = (bf16[2,128,256]{2,1,0:T(8,128)(2,1)}, bf16[2,128,256]{2,1,0:T(8,128)(2,1)S(1)}, u32[]{:S(2)}, u32[]{:S(2)}) collective-permute-start(bf16[2,128,256]{2,1,0:T(8,128)(2,1)} %get-tuple-element.131), channel_id=1, source_target_pairs={{0,1},{1,2},{2,3},{3,0},{4,5},{5,6},{6,7},{7,4},{8,9},{9,10},{10,1... | collective-permute-start | bytes 393224 | tf_op jit(solution)/shard_map/ppermute | solution.py:414
  97.2 16.2 %collective-permute-start.25 = (bf16[2,128,256]{2,1,0:T(8,128)(2,1)}, bf16[2,128,256]{2,1,0:T(8,128)(2,1)S(1)}, u32[]{:S(2)}, u32[]{:S(2)}) collective-permute-start(bf16[2,128,256]{2,1,0:T(8,128)(2,1)} %get-tuple-element.132), channel_id=1, source_target_pairs={{0,2},{1,3},{2,0},{3,1},{4,6},{5,7},{6,4},{7,5},{8,10},{9,11},{10,... | collective-permute-start | bytes 393224 | tf_op jit(solution)/shard_map/ppermute | solution.py:414
  98.1 15.3 %collective-permute-start.26 = (bf16[2,128,256]{2,1,0:T(8,128)(2,1)S(1)}, bf16[2,128,256]{2,1,0:T(8,128)(2,1)S(1)}, u32[]{:S(2)}, u32[]{:S(2)}) collective-permute-start(bf16[2,128,256]{2,1,0:T(8,128)(2,1)S(1)} %copy-done.27), channel_id=1, source_target_pairs={{0,3},{1,0},{2,1},{3,2},{4,7},{5,4},{6,5},{7,6},{8,11},{9,8},{10,9... | collective-permute-start | bytes 393224 | tf_op jit(solution)/shard_map/ppermute | solution.py:414
  113.4 16.7 %all-to-all-start.1 = ((bf16[8,128,384]{2,1,0:T(8,128)(2,1)}), bf16[8,128,384]{2,1,0:T(8,128)(2,1)S(1)}, u32[]{:S(2)}, u32[]{:S(2)}) async-start(bf16[8,128,384]{2,1,0:T(8,128)(2,1)} %shard_map.75), calls=%async_computation.1 | async-start | bytes 1572864 | tf_op jit(solution)/shard_map/all_to_all | solution.py:470
  117.5 14.1 %collective-permute-start.27 = (bf16[8,128,384]{2,1,0:T(8,128)(2,1)}, bf16[8,128,384]{2,1,0:T(8,128)(2,1)}, u32[]{:S(2)}, u32[]{:S(2)}) collective-permute-start(bf16[8,128,384]{2,1,0:T(8,128)(2,1)} %all-to-all-done.refs_0_), channel_id=1, source_target_pairs={{0,4},{4,0},{8,12},{12,8},{16,20},{20,16},{24,28},{28,24},{1,5},{5... | collective-permute-start | bytes 2359304 | tf_op jit(solution)/shard_map/ppermute | solution.py:477
  130.1 2.4 %collective-permute-start.28 = (bf16[8,128,384]{2,1,0:T(8,128)(2,1)S(1)}, bf16[8,128,384]{2,1,0:T(8,128)(2,1)}, u32[]{:S(2)}, u32[]{:S(2)}) collective-permute-start(bf16[8,128,384]{2,1,0:T(8,128)(2,1)S(1)} %all-to-all-done.1.refs_2_), channel_id=1, source_target_pairs={{0,4},{4,0},{8,12},{12,8},{16,20},{20,16},{24,28},{28,24},{1,5},{5... | collective-permute-start | bytes 2359304 | tf_op jit(solution)/shard_map/ppermute | solution.py:477
  130.2 13.6 %collective-permute-start.29 = (bf16[512,256]{1,0:T(8,128)(2,1)S(1)}, bf16[512,256]{1,0:T(8,128)(2,1)S(1)}, u32[]{:S(2)}, u32[]{:S(2)}) collective-permute-start(bf16[512,256]{1,0:T(8,128)(2,1)S(1)} %pad_maximum_fusion.2), channel_id=1, source_target_pairs={{0,8},{4,12},{8,0},{12,4},{16,24},{20,28},{24,16},{28,20},{1,9},{5... | collective-permute-start | bytes 786440 | tf_op jit(solution)/shard_map/ppermute | solution.py:424
  131.0 12.8 %collective-permute-start.30 = (bf16[512,256]{1,0:T(8,128)(2,1)S(1)}, bf16[512,256]{1,0:T(8,128)(2,1)}, u32[]{:S(2)}, u32[]{:S(2)}) collective-permute-start(bf16[512,256]{1,0:T(8,128)(2,1)S(1)} %pad_maximum_fusion.3), channel_id=1, source_target_pairs={{0,16},{4,20},{8,24},{12,28},{16,0},{20,4},{24,8},{28,12},{1,17},{... | collective-permute-start | bytes 786440 | tf_op jit(solution)/shard_map/ppermute | solution.py:424
  158.0 13.1 %collective-permute-start.36 = (bf16[1024,256]{1,0:T(8,128)(2,1)S(1)}, bf16[1024,256]{1,0:T(8,128)(2,1)S(1)}, u32[]{:S(2)}, u32[]{:S(2)}) collective-permute-start(bf16[1024,256]{1,0:T(8,128)(2,1)S(1)} %pad_maximum_fusion.1), channel_id=1, source_target_pairs={{0,8},{4,12},{8,0},{12,4},{16,24},{20,28},{24,16},{28,20},{1,9},{5... | collective-permute-start | bytes 1572872 | tf_op jit(solution)/shard_map/ppermute | solution.py:424
  158.6 13.8 %collective-permute-start.35 = (bf16[1024,256]{1,0:T(8,128)(2,1)S(1)}, bf16[1024,256]{1,0:T(8,128)(2,1)S(1)}, u32[]{:S(2)}, u32[]{:S(2)}) collective-permute-start(bf16[1024,256]{1,0:T(8,128)(2,1)S(1)} %pad_maximum_fusion), channel_id=1, source_target_pairs={{0,16},{4,20},{8,24},{12,28},{16,0},{20,4},{24,8},{28,12},{1,17},{... | collective-permute-start | bytes 1572872 | tf_op jit(solution)/shard_map/ppermute | solution.py:424
  159.3 13.1 %collective-permute-start.34 = (bf16[4,256,128]{2,1,0:T(8,128)(2,1)S(1)}, bf16[4,256,128]{2,1,0:T(8,128)(2,1)S(1)}, u32[]{:S(2)}, u32[]{:S(2)}) collective-permute-start(bf16[4,256,128]{2,1,0:T(8,128)(2,1)S(1)} %get-tuple-element.171), channel_id=1, source_target_pairs={{1,0},{2,1},{3,2},{5,4},{6,5},{7,6},{9,8},{10,9},{11,10},{13,12},{... | collective-permute-start | bytes 786440 | tf_op jit(solution)/shard_map/ppermute | solution.py:48
  160.6 11.9 %collective-permute-start.33 = (bf16[4,256,128]{2,1,0:T(8,128)(2,1)S(1)}, bf16[4,256,128]{2,1,0:T(8,128)(2,1)S(1)}, u32[]{:S(2)}, u32[]{:S(2)}) collective-permute-start(bf16[4,256,128]{2,1,0:T(8,128)(2,1)S(1)} %get-tuple-element.171), channel_id=1, source_target_pairs={{0,1},{1,2},{2,3},{4,5},{5,6},{6,7},{8,9},{9,10},{10,11},{12,13},{... | collective-permute-start | bytes 786440 | tf_op jit(solution)/shard_map/ppermute | solution.py:47
  165.2 9.1 %collective-permute-start.32 = (bf16[4,256,128]{2,1,0:T(8,128)(2,1)S(1)}, bf16[4,256,128]{2,1,0:T(8,128)(2,1)S(1)}, u32[]{:S(2)}, u32[]{:S(2)}) collective-permute-start(bf16[4,256,128]{2,1,0:T(8,128)(2,1)S(1)} %get-tuple-element.172), channel_id=1, source_target_pairs={{1,0},{2,1},{3,2},{5,4},{6,5},{7,6},{9,8},{10,9},{11,10},{13,12},{... | collective-permute-start | bytes 786440 | tf_op jit(solution)/shard_map/ppermute | solution.py:48
  171.0 5.5 %collective-permute-start.31 = (bf16[4,256,128]{2,1,0:T(8,128)(2,1)S(1)}, bf16[4,256,128]{2,1,0:T(8,128)(2,1)S(1)}, u32[]{:S(2)}, u32[]{:S(2)}) collective-permute-start(bf16[4,256,128]{2,1,0:T(8,128)(2,1)S(1)} %get-tuple-element.172), channel_id=1, source_target_pairs={{0,1},{1,2},{2,3},{4,5},{5,6},{6,7},{8,9},{9,10},{10,11},{12,13},{... | collective-permute-start | bytes 786440 | tf_op jit(solution)/shard_map/ppermute | solution.py:47
  172.5 27.1 %copy-start.21 = (bf16[4,256,128]{2,1,0:T(8,128)(2,1)}, bf16[4,256,128]{2,1,0:T(8,128)(2,1)S(1)}, u32[]{:S(2)}) copy-start(bf16[4,256,128]{2,1,0:T(8,128)(2,1)S(1)} %collective-permute-done.33) | copy-start | bytes 786436
  174.3 26.7 %copy-start.22 = (bf16[4,256,128]{2,1,0:T(8,128)(2,1)}, bf16[4,256,128]{2,1,0:T(8,128)(2,1)S(1)}, u32[]{:S(2)}) copy-start(bf16[4,256,128]{2,1,0:T(8,128)(2,1)S(1)} %collective-permute-done.32) | copy-start | bytes 786436
  177.7 32.5 %copy-start.1 = (bf16[2048,256]{1,0:T(8,128)(2,1)}, bf16[2048,256]{1,0:T(8,128)(2,1)S(1)}, u32[]{:S(2)}) copy-start(bf16[2048,256]{1,0:T(8,128)(2,1)S(1)} %constant_dynamic-update-slice_fusion.4.refs_1_) | copy-start | bytes 3145732
  177.7 32.5 %collective-permute-start.38 = (bf16[2048,256]{1,0:T(8,128)(2,1)S(1)}, bf16[2048,256]{1,0:T(8,128)(2,1)}, u32[]{:S(2)}, u32[]{:S(2)}) collective-permute-start(bf16[2048,256]{1,0:T(8,128)(2,1)S(1)} %constant_dynamic-update-slice_fusion.4.refs_1_), channel_id=1, source_target_pairs={{0,4},{4,0},{8,12},{12,8},{16,20},{20,16},{24,28},{28,24},{1,5},{5... | collective-permute-start | bytes 3145736 | tf_op jit(solution)/shard_map/ppermute | solution.py:527
  179.0 31.2 %collective-permute-start.37 = (bf16[2048,256]{1,0:T(8,128)(2,1)S(1)}, bf16[2048,256]{1,0:T(8,128)(2,1)S(1)}, u32[]{:S(2)}, u32[]{:S(2)}) collective-permute-start(bf16[2048,256]{1,0:T(8,128)(2,1)S(1)} %constant_dynamic-update-slice_fusion.refs_0_), channel_id=1, source_target_pairs={{0,4},{4,0},{8,12},{12,8},{16,20},{20,16},{24,28},{28,24},{1,5},{5... | collective-permute-start | bytes 3145736 | tf_op jit(solution)/shard_map/ppermute | solution.py:527
  179.3 3.4 %collective-permute-start.39 = (bf16[4,256,128]{2,1,0:T(8,128)(2,1)S(1)}, bf16[4,256,128]{2,1,0:T(8,128)(2,1)S(1)}, u32[]{:S(2)}, u32[]{:S(2)}) collective-permute-start(bf16[4,256,128]{2,1,0:T(8,128)(2,1)S(1)} %collective-permute-done.31), channel_id=1, source_target_pairs={{1,2},{2,3},{5,6},{6,7},{9,10},{10,11},{13,14},{14,15},{17,18},{18... | collective-permute-start | bytes 786440 | tf_op jit(solution)/shard_map/ppermute | solution.py:47
  180.0 11.8 %collective-permute-start.40 = (bf16[4,256,128]{2,1,0:T(8,128)(2,1)S(1)}, bf16[4,256,128]{2,1,0:T(8,128)(2,1)}, u32[]{:S(2)}, u32[]{:S(2)}) collective-permute-start(bf16[4,256,128]{2,1,0:T(8,128)(2,1)S(1)} %collective-permute-done.32), channel_id=1, source_target_pairs={{1,0},{2,1},{5,4},{6,5},{9,8},{10,9},{13,12},{14,13},{17,16},{18,1... | collective-permute-start | bytes 786440 | tf_op jit(solution)/shard_map/ppermute | solution.py:48
  181.3 11.1 %collective-permute-start.43 = (bf16[4,256,128]{2,1,0:T(8,128)(2,1)S(1)}, bf16[4,256,128]{2,1,0:T(8,128)(2,1)}, u32[]{:S(2)}, u32[]{:S(2)}) collective-permute-start(bf16[4,256,128]{2,1,0:T(8,128)(2,1)S(1)} %collective-permute-done.33), channel_id=1, source_target_pairs={{1,2},{2,3},{5,6},{6,7},{9,10},{10,11},{13,14},{14,15},{17,18},{18... | collective-permute-start | bytes 786440 | tf_op jit(solution)/shard_map/ppermute | solution.py:47
  182.7 28.5 %copy-start.24 = (bf16[4,256,128]{2,1,0:T(8,128)(2,1)}, bf16[4,256,128]{2,1,0:T(8,128)(2,1)S(1)}, u32[]{:S(2)}) copy-start(bf16[4,256,128]{2,1,0:T(8,128)(2,1)S(1)} %collective-permute-done.39) | copy-start | bytes 786436
  182.7 16.8 %collective-permute-start.44 = (bf16[4,256,128]{2,1,0:T(8,128)(2,1)S(1)}, bf16[4,256,128]{2,1,0:T(8,128)(2,1)}, u32[]{:S(2)}, u32[]{:S(2)}) collective-permute-start(bf16[4,256,128]{2,1,0:T(8,128)(2,1)S(1)} %collective-permute-done.34), channel_id=1, source_target_pairs={{1,0},{2,1},{5,4},{6,5},{9,8},{10,9},{13,12},{14,13},{17,16},{18,1... | collective-permute-start | bytes 786440 | tf_op jit(solution)/shard_map/ppermute | solution.py:48
  191.8 9.2 %collective-permute-start.41 = (bf16[4,256,128]{2,1,0:T(8,128)(2,1)S(1)}, bf16[4,256,128]{2,1,0:T(8,128)(2,1)S(1)}, u32[]{:S(2)}, u32[]{:S(2)}) collective-permute-start(bf16[4,256,128]{2,1,0:T(8,128)(2,1)S(1)} %collective-permute-done.39), channel_id=1, source_target_pairs={{2,3},{6,7},{10,11},{14,15},{18,19},{22,23},{26,27},{30,31}} | collective-permute-start | bytes 786440 | tf_op jit(solution)/shard_map/ppermute | solution.py:47
  192.5 12.8 %collective-permute-start.42 = (bf16[4,256,128]{2,1,0:T(8,128)(2,1)}, bf16[4,256,128]{2,1,0:T(8,128)(2,1)}, u32[]{:S(2)}, u32[]{:S(2)}) collective-permute-start(bf16[4,256,128]{2,1,0:T(8,128)(2,1)} %collective-permute-done.40), channel_id=1, source_target_pairs={{1,0},{5,4},{9,8},{13,12},{17,16},{21,20},{25,24},{29,28}} | collective-permute-start | bytes 786440 | tf_op jit(solution)/shard_map/ppermute | solution.py:48
  199.6 5.7 %collective-permute-start.45 = (bf16[4,256,128]{2,1,0:T(8,128)(2,1)}, bf16[4,256,128]{2,1,0:T(8,128)(2,1)}, u32[]{:S(2)}, u32[]{:S(2)}) collective-permute-start(bf16[4,256,128]{2,1,0:T(8,128)(2,1)} %collective-permute-done.43), channel_id=1, source_target_pairs={{2,3},{6,7},{10,11},{14,15},{18,19},{22,23},{26,27},{30,31}} | collective-permute-start | bytes 786440 | tf_op jit(solution)/shard_map/ppermute | solution.py:47
  201.7 8.6 %collective-permute-start.46 = (bf16[4,256,128]{2,1,0:T(8,128)(2,1)}, bf16[4,256,128]{2,1,0:T(8,128)(2,1)}, u32[]{:S(2)}, u32[]{:S(2)}) collective-permute-start(bf16[4,256,128]{2,1,0:T(8,128)(2,1)} %collective-permute-done.44), channel_id=1, source_target_pairs={{1,0},{5,4},{9,8},{13,12},{17,16},{21,20},{25,24},{29,28}} | collective-permute-start | bytes 786440 | tf_op jit(solution)/shard_map/ppermute | solution.py:48
  (13 other events, 178.7 us)

commit v8 on v7

--- a/solution.py
+++ b/solution.py
@@ -405,10 +405,10 @@
     return list(shares_of(w_out, place, tensor_count, halves, each))
 
 
-def send_shares(shares, tensor_count, after):
+def send_shares(shares, tensor_count):
     if shares is None:
         return None
-    shares, _ = lax.optimization_barrier((list(shares), after))
+    shares = list(shares)
     for step in range(1, tensor_count):
         ring = [(d, (d + step) % tensor_count) for d in range(tensor_count)]
         shares[step] = lax.ppermute(shares[step], "tensor", ring)
@@ -492,10 +492,10 @@
     if made:
         (early, shares), rest = lax.optimization_barrier((made[0], rest))
         got = [to_heads(early)]
-    sending = send_shares(shares, tensor_count, rest[-1])
-    sent = work(rest)
-    sent, sending, got = lax.optimization_barrier((sent, sending, got))
-    pieces = sum([to_parts(each) for each in got + [to_heads(sent)]], [])
+    sent, got, shares = lax.optimization_barrier((work(rest), got, shares))
+    sending = send_shares(shares, tensor_count)
+    late, sending = lax.optimization_barrier((to_heads(sent), sending))
+    pieces = sum([to_parts(each) for each in got + [late]], [])
 
     heads, cuts, halves, _ = weight_cuts(w_out, seq_count, columns)
     held, flips = [], []
@@ -514,10 +514,10 @@
 
     def spread(first, step, last, found):
         nonlocal held
-        if held and 0 < step < len(flips):
-            last, held = lax.optimization_barrier(
-                (last, swap(held, [flips[step], flips[-1 - step]]))
-            )
+        if held and step == 2:
+            for stage in range(1, len(flips)):
+                held = swap(held, [flips[stage], flips[-1 - stage]])
+            last, held = lax.optimization_barrier((last, held))
         return last
 
     found = line_gather([home[: seq_count // 2], home[seq_count // 2 :]], tensor_count, spread)

time: 222 us -> 215 us (0.968)
  waiting for transfers between devices: 56.2 us -> 45 us
  starting transfers between devices: 88.7 us -> 93.1 us
    all_to_all x2, waiting for transfers between devices: 12.1 us -> 0.01 us  [to_heads(): return lax.all_to_all(sent, 'seq', split_axis=0, concat_axis=0)]
    ppermute x3, waiting for transfers between devices: 0.01 us -> 6.41 us  [send_shares(): shares[step] = lax.ppermute(shares[step], 'tensor', ring)]
    ppermute x4, waiting for transfers between devices: 4.57 us -> 0.01 us  [swap(): lax.ppermute(jnp.concatenate(whole, axis=0) if len(whole) > 1 else whole[...]
    ppermute x18, starting transfers between devices: 43.4 us -> 47.3 us  [line_gather(): from_left = lax.ppermute(last[at][0], 'tensor', right[step:])]
    ppermute x18, waiting for transfers between devices: 2.8 us -> 0.48 us  [line_gather(): from_left = lax.ppermute(last[at][0], 'tensor', right[step:])]
    ppermute x18, waiting for transfers between devices: 35.8 us -> 38.1 us  [line_gather(): from_right = lax.ppermute(last[at][1], 'tensor', left[:count - 1 - step])]
  transfers between devices with their start and end apart: 49 -> 49, of which waited for: 14 -> 14; matrix products, arithmetic and copies ran while one was open for 3% -> 4% of each run, Pallas kernels for 18% -> 19%
where the time goes in v8:
time: 215 us; the launch traced here: 213 us
  starting transfers between devices  93.1 us (43%)
  Pallas kernels  49 us (23%)
  waiting for transfers between devices  45 us (21%)
  blocking collectives  13.1 us (6%)
  local copies, waits for them, and re-layouts  9.19 us (4%)
  other arithmetic  2.92 us (1%)
    ppermute x18, starting transfers between devices, line_gather(): from_left = lax.ppermute(last[at][0], 'tensor', right[step:])  47.3 us
    ppermute x18, waiting for transfers between devices, line_gather(): from_right = lax.ppermute(last[at][1], 'tensor', left[:count - 1 - step])  38.1 us
    pallas_call x2, Pallas kernels, project(): pl.pallas_call(partial(project_kernel, group, count), in_specs=[pl.BlockS...  24.9 us
    ppermute x18, starting transfers between devices, line_gather(): from_right = lax.ppermute(last[at][1], 'tensor', left[:count - 1 - step])  23.4 us
    all_to_all x1, blocking collectives, shards(): home = lax.all_to_all(out, 'seq', split_axis=0, concat_axis=0)  13.1 us
    pallas_call x1, Pallas kernels, attend(): pl.pallas_call(partial(attend_kernel, chunks, group, rows), in_specs=[pl....  11.3 us
    pallas_call x1, Pallas kernels, output(): pl.pallas_call(partial(output_kernel, group, count, cuts, halves), in_spe...  9.39 us
    ppermute x3, starting transfers between devices, send_shares(): shares[step] = lax.ppermute(shares[step], 'tensor', ring)  9.04 us
  transfers between devices with their start and end apart: 49, of which 14 were waited for; matrix products, arithmetic and copies ran while one was open for 4% of the time, Pallas kernels for 19%

profile of v8, /device:TPU:0, one launch (start us, length us, event | category | flops | bytes accessed | tf_op | source)
XLA Modules:
  0.0 213.3 jit_solution(16220651550491601917)
XLA Ops:
  0.0 1.3 fusion.5
  1.3 1.3 collective-permute-start.1
  2.6 5.6 %collective-permute-start = (bf16[128,1024]{1,0:T(8,128)(2,1)S(1)}, bf16[128,1024]{1,0:T(8,128)(2,1)S(1)}, u32[]{:S(2)}, u32[]{:S(2)}) collective-permute-start(bf16[128,1024]{1,0:T(8,128)(2,1)S(1)} %get-tuple-element.91.refs_3_), channel_id=1, source_target_pairs={{0,1},{1,2},{2,3},{4,5},{5,6},{6,7},{8,9},{9,10},{10,11},{12,13},{... | collective-permute-start | bytes 786440 | tf_op jit(solution)/shard_map/ppermute | solution.py:47
  8.2 1.3 collective-permute-start.15
  9.5 3.3 %collective-permute-done.1.refs_5_ = bf16[128,1024]{1,0:T(8,128)(2,1)S(1)} collective-permute-done((bf16[128,1024]{1,0:T(8,128)(2,1)S(1)}, bf16[128,1024]{1,0:T(8,128)(2,1)S(1)}, u32[]{:S(2)}, u32[]{:S(2)}) %collective-permute-start.1) | collective-permute-done | bytes 262176 | tf_op jit(solution)/shard_map/ppermute | solution.py:48
  12.8 1.3 collective-permute-start.3
  14.8 7.6 %collective-permute-start.14 = (bf16[128,1024]{1,0:T(8,128)(2,1)S(1)}, bf16[128,1024]{1,0:T(8,128)(2,1)S(1)}, u32[]{:S(2)}, u32[]{:S(2)}) collective-permute-start(bf16[128,1024]{1,0:T(8,128)(2,1)S(1)} %get-tuple-element.98.refs_10_), channel_id=1, source_target_pairs={{0,1},{1,2},{2,3},{4,5},{5,6},{6,7},{8,9},{9,10},{10,11},{12,13},{... | collective-permute-start | bytes 786440 | tf_op jit(solution)/shard_map/ppermute | solution.py:47
  22.4 1.3 collective-permute-start.17
  23.8 1.3 collective-permute-start.5
  26.2 1.4 collective-permute-start.16
  27.6 5.6 %collective-permute-done.17.refs_14_ = bf16[128,1024]{1,0:T(8,128)(2,1)S(1)} collective-permute-done((bf16[128,1024]{1,0:T(8,128)(2,1)S(1)}, bf16[128,1024]{1,0:T(8,128)(2,1)S(1)}, u32[]{:S(2)}, u32[]{:S(2)}) %collective-permute-start.17) | collective-permute-done | bytes 262176 | tf_op jit(solution)/shard_map/ppermute | solution.py:48
  33.1 1.3 collective-permute-start.19
  34.4 2.8 %collective-permute-done.5.refs_9_ = bf16[128,1024]{1,0:T(8,128)(2,1)S(1)} collective-permute-done((bf16[128,1024]{1,0:T(8,128)(2,1)S(1)}, bf16[128,1024]{1,0:T(8,128)(2,1)S(1)}, u32[]{:S(2)}, u32[]{:S(2)}) %collective-permute-start.5) | collective-permute-done | bytes 262176 | tf_op jit(solution)/shard_map/ppermute | solution.py:48
  37.2 1.3 collective-permute-start.8
  38.5 5.3 %collective-permute-start.6 = (bf16[128,1024]{1,0:T(8,128)(2,1)S(1)}, bf16[128,1024]{1,0:T(8,128)(2,1)}, u32[]{:S(2)}, u32[]{:S(2)}) collective-permute-start(bf16[128,1024]{1,0:T(8,128)(2,1)S(1)} %get-tuple-element.113.refs_3_), channel_id=1, source_target_pairs={{0,1},{1,2},{2,3},{4,5},{5,6},{6,7},{8,9},{9,10},{10,11},{12,13},{... | collective-permute-start | bytes 786440 | tf_op jit(solution)/shard_map/ppermute | solution.py:47
  43.8 1.3 collective-permute-start.12
  45.1 5.3 %collective-permute-start.10 = (bf16[128,1024]{1,0:T(8,128)(2,1)S(1)}, bf16[128,1024]{1,0:T(8,128)(2,1)}, u32[]{:S(2)}, u32[]{:S(2)}) collective-permute-start(bf16[128,1024]{1,0:T(8,128)(2,1)S(1)} %get-tuple-element.120.refs_10_), channel_id=1, source_target_pairs={{0,1},{1,2},{2,3},{4,5},{5,6},{6,7},{8,9},{9,10},{10,11},{12,13},{... | collective-permute-start | bytes 786440 | tf_op jit(solution)/shard_map/ppermute | solution.py:47
  50.4 1.3 reshape.57.gain_ref
  51.7 0.7 compare_convert_fusion
  52.4 1.4 collective-permute-start.18
  53.9 1.3 collective-permute-start.9
  55.2 1.4 collective-permute-start.7
  56.6 1.3 collective-permute-start.13
  57.9 1.4 collective-permute-start.11
  59.3 0.8 copy.8.active_ref
  60.6 3.5 %shard_map.73 = (bf16[2,128,256]{2,1,0:T(8,128)(2,1)}, bf16[2,128,256]{2,1,0:T(8,128)(2,1)}, bf16[2,128,256]{2,1,0:T(8,128)(2,1)}, bf16[2,128,256]{2,1,0:T(8,128)(2,1)}) custom-call(s32[3]{0:T(128)} %pad_add_fusion.place_ref, bf16[512,4096]{1,0:T(8,128)(2,1)} %w_ref.1), custom_call_target="tpu_custom_call" | custom-call | tf_op jit(solution)/shard_map/pallas_call | solution.py:372
  64.1 3.7 %collective-permute-done.13.refs_14_ = bf16[128,1024]{1,0:T(8,128)(2,1)} collective-permute-done((bf16[128,1024]{1,0:T(8,128)(2,1)}, bf16[128,1024]{1,0:T(8,128)(2,1)}, u32[]{:S(2)}, u32[]{:S(2)}) %collective-permute-start.13) | collective-permute-done | bytes 262176 | tf_op jit(solution)/shard_map/ppermute | solution.py:48
  67.8 1.4 collective-permute-start.20
  69.2 1.3 collective-permute-start.21
  70.5 1.4 collective-permute-start.22
  71.9 1.3 collective-permute-start.23
  73.2 12.4 %shard_map.74 = bf16[8,128,384]{2,1,0:T(8,128)(2,1)} custom-call(s32[1]{0:T(128)} %bitcast.me_ref, f32[4,1024]{1,0:T(4,128)} %reshape.57.gain_ref, s32[256,1]{1,0:T(8,128)} %copy.8.active_ref, bf16[4096,512]{1,0:T(8,128)(2,1)} %refs_0_.3, bf16[4096,512]{1,0:T(8,128)(2,1)} %refs_1_.3, bf16[4096,512]{1,0:T(8,128)(2,1)} %refs_2_.3, ...), custom_call_target="tpu_custom_call" | custom-call | flops 3221225472 | bytes 15466496 | tf_op jit(solution)/shard_map/pallas_call | solution.py:128
  85.6 4.2 %all-to-all-start = ((bf16[8,128,384]{2,1,0:T(8,128)(2,1)}), bf16[8,128,384]{2,1,0:T(8,128)(2,1)}, u32[]{:S(2)}, u32[]{:S(2)}) async-start(bf16[8,128,384]{2,1,0:T(8,128)(2,1)} %shard_map.74), calls=%async_computation | async-start | bytes 1572864 | tf_op jit(solution)/shard_map/all_to_all | solution.py:470
  89.9 0.8 copy.9.active_ref
  90.7 12.5 %shard_map.75 = bf16[8,128,384]{2,1,0:T(8,128)(2,1)} custom-call(s32[1]{0:T(128)} %bitcast.me_ref, f32[4,1024]{1,0:T(4,128)} %reshape.57.gain_ref, s32[256,1]{1,0:T(8,128)} %copy.9.active_ref, bf16[4096,512]{1,0:T(8,128)(2,1)} %refs_0_.3, bf16[4096,512]{1,0:T(8,128)(2,1)} %refs_1_.3, bf16[4096,512]{1,0:T(8,128)(2,1)} %refs_2_.3, ...), custom_call_target="tpu_custom_call" | custom-call | flops 3221225472 | bytes 15466496 | tf_op jit(solution)/shard_map/pallas_call | solution.py:128
  103.2 4.1 %all-to-all-start.1 = ((bf16[8,128,384]{2,1,0:T(8,128)(2,1)}), bf16[8,128,384]{2,1,0:T(8,128)(2,1)S(1)}, u32[]{:S(2)}, u32[]{:S(2)}) async-start(bf16[8,128,384]{2,1,0:T(8,128)(2,1)} %shard_map.75), calls=%async_computation.1 | async-start | bytes 1572864 | tf_op jit(solution)/shard_map/all_to_all | solution.py:470
  107.3 5.9 %collective-permute-start.25 = (bf16[2,128,256]{2,1,0:T(8,128)(2,1)S(1)}, bf16[2,128,256]{2,1,0:T(8,128)(2,1)S(1)}, u32[]{:S(2)}, u32[]{:S(2)}) collective-permute-start(bf16[2,128,256]{2,1,0:T(8,128)(2,1)S(1)} %copy-done.29), channel_id=1, source_target_pairs={{0,1},{1,2},{2,3},{3,0},{4,5},{5,6},{6,7},{7,4},{8,9},{9,10},{10,1... | collective-permute-start | bytes 393224 | tf_op jit(solution)/shard_map/ppermute | solution.py:414
  113.5 2.8 %collective-permute-start.27 = (bf16[2,128,256]{2,1,0:T(8,128)(2,1)S(1)}, bf16[2,128,256]{2,1,0:T(8,128)(2,1)S(1)}, u32[]{:S(2)}, u32[]{:S(2)}) collective-permute-start(bf16[2,128,256]{2,1,0:T(8,128)(2,1)S(1)} %copy-done.27), channel_id=1, source_target_pairs={{0,3},{1,0},{2,1},{3,2},{4,7},{5,4},{6,5},{7,6},{8,11},{9,8},{10,9... | collective-permute-start | bytes 393224 | tf_op jit(solution)/shard_map/ppermute | solution.py:414
  117.0 5.8 %collective-permute-done.26 = bf16[2,128,256]{2,1,0:T(8,128)(2,1)S(1)} collective-permute-done((bf16[2,128,256]{2,1,0:T(8,128)(2,1)S(1)}, bf16[2,128,256]{2,1,0:T(8,128)(2,1)S(1)}, u32[]{:S(2)}, u32[]{:S(2)}) %collective-permute-start.26) | collective-permute-done | bytes 131104 | tf_op jit(solution)/shard_map/ppermute | solution.py:414
  123.0 1.8 collective-permute-start.29
  124.8 1.5 collective-permute-start.30
  126.3 11.3 %shard_map.76 = bf16[8,256,128]{2,1,0:T(8,128)(2,1)} custom-call(s32[1]{0:T(128)} %bitcast.6.part_ref, bf16[8,128,384]{2,1,0:T(8,128)(2,1)} %all-to-all-done.refs_0_, bf16[8,128,384]{2,1,0:T(8,128)(2,1)} %collective-permute-done.24.refs_1_, bf16[8,128,384]{2,1,0:T(8,128)(2,1)} %copy-done.9, bf16[8,128,384]{2,1,0:T(8,128)(2,1)} %collective-permute-done.28.refs_3_), custom_call_target="tpu_custom_call" | custom-call | flops 3623878656 | bytes 4194304 | tf_op jit(solution)/shard_map/pallas_call | solution.py:256
  137.6 13.1 %all_to_all.15 = bf16[8,256,128]{2,1,0:T(8,128)(2,1)S(1)} all-to-all(bf16[8,256,128]{2,1,0:T(8,128)(2,1)} %shard_map.76), channel_id=1, replica_groups=mesh['seq'=8,'tensor'=4] {'seq'}, dimensions={0} | all-to-all | bytes 1048576 | tf_op jit(solution)/shard_map/all_to_all | solution.py:512
  150.8 1.3 collective-permute-start.37
  152.1 1.0 pad_maximum_fusion.1
  154.4 5.5 %collective-permute-start.35 = (bf16[4,256,128]{2,1,0:T(8,128)(2,1)S(1)}, bf16[4,256,128]{2,1,0:T(8,128)(2,1)S(1)}, u32[]{:S(2)}, u32[]{:S(2)}) collective-permute-start(bf16[4,256,128]{2,1,0:T(8,128)(2,1)S(1)} %get-tuple-element.173), channel_id=1, source_target_pairs={{0,1},{1,2},{2,3},{4,5},{5,6},{6,7},{8,9},{9,10},{10,11},{12,13},{... | collective-permute-start | bytes 786440 | tf_op jit(solution)/shard_map/ppermute | solution.py:47
  159.9 1.3 collective-permute-start.33
  161.3 4.5 %collective-permute-start.31 = (bf16[4,256,128]{2,1,0:T(8,128)(2,1)S(1)}, bf16[4,256,128]{2,1,0:T(8,128)(2,1)S(1)}, u32[]{:S(2)}, u32[]{:S(2)}) collective-permute-start(bf16[4,256,128]{2,1,0:T(8,128)(2,1)S(1)} %get-tuple-element.174), channel_id=1, source_target_pairs={{0,1},{1,2},{2,3},{4,5},{5,6},{6,7},{8,9},{9,10},{10,11},{12,13},{... | collective-permute-start | bytes 786440 | tf_op jit(solution)/shard_map/ppermute | solution.py:47
  165.8 1.3 collective-permute-start.38
  167.1 2.0 collective-permute-done.33
  169.1 1.4 collective-permute-start.36
  170.5 1.3 collective-permute-start.34
  172.5 2.1 collective-permute-done.38
  174.6 6.7 %collective-permute-done.34 = bf16[4,256,128]{2,1,0:T(8,128)(2,1)} collective-permute-done((bf16[4,256,128]{2,1,0:T(8,128)(2,1)S(1)}, bf16[4,256,128]{2,1,0:T(8,128)(2,1)}, u32[]{:S(2)}, u32[]{:S(2)}) %collective-permute-start.34) | collective-permute-done | bytes 262176 | tf_op jit(solution)/shard_map/ppermute | solution.py:48
  181.4 1.0 constant_dynamic-update-slice_fusion.5
  182.7 1.1 copy-done
  184.8 1.3 collective-permute-start.44
  186.1 1.4 collective-permute-start.45
  187.5 1.5 collective-permute-start.46
  189.1 0.9 copy.10.active_ref
  191.1 6.4 %collective-permute-done.44 = bf16[4,256,128]{2,1,0:T(8,128)(2,1)} collective-permute-done((bf16[4,256,128]{2,1,0:T(8,128)(2,1)}, bf16[4,256,128]{2,1,0:T(8,128)(2,1)}, u32[]{:S(2)}, u32[]{:S(2)}) %collective-permute-start.44) | collective-permute-done | bytes 262176 | tf_op jit(solution)/shard_map/ppermute | solution.py:48
  197.5 5.2 %collective-permute-done.46 = bf16[4,256,128]{2,1,0:T(8,128)(2,1)} collective-permute-done((bf16[4,256,128]{2,1,0:T(8,128)(2,1)}, bf16[4,256,128]{2,1,0:T(8,128)(2,1)}, u32[]{:S(2)}, u32[]{:S(2)}) %collective-permute-start.46) | collective-permute-done | bytes 262176 | tf_op jit(solution)/shard_map/ppermute | solution.py:48
  202.7 1.0 copy-done.6
  203.7 9.4 %shard_map.77 = bf16[512,1024]{1,0:T(8,128)(2,1)} custom-call(s32[5]{0:T(128)} %stack.31.me_ref, s32[16]{0:T(128)} %fusion.at_ref, s32[512,1]{1,0:T(8,128)} %copy.10.active_ref, bf16[512,1024]{1,0:T(8,128)(2,1)} %hidden_ref.1, bf16[2048,256]{1,0:T(8,128)(2,1)} %copy-done, bf16[2048,256]{1,0:T(8,128)(2,1)} %copy-done.1, bf16[2048,256]{1,0:T(8,128)(2,1)} %copy-done.6, ...), custom_call_target="tpu_custom_call" | custom-call | flops 2147483648 | bytes 8388608 | tf_op jit(solution)/shard_map/pallas_call | solution.py:336
  (127 shorter events, 8.4 us)
Async XLA Ops:
  1.3 43.8 %copy-start.5 = (bf16[128,1024]{1,0:T(8,128)(2,1)}, bf16[128,1024]{1,0:T(8,128)(2,1)S(1)}, u32[]{:S(2)}) copy-start(bf16[128,1024]{1,0:T(8,128)(2,1)S(1)} %get-tuple-element.91.refs_3_) | copy-start | bytes 786436
  1.3 71.9 %copy-start.4 = (bf16[128,1024]{1,0:T(8,128)(2,1)}, bf16[128,1024]{1,0:T(8,128)(2,1)S(1)}, u32[]{:S(2)}) copy-start(bf16[128,1024]{1,0:T(8,128)(2,1)S(1)} %get-tuple-element.98.refs_10_) | copy-start | bytes 786436
  1.3 84.3 %copy-start.2 = (bf16[128,1024]{1,0:T(8,128)(2,1)}, bf16[128,1024]{1,0:T(8,128)(2,1)S(1)}, u32[]{:S(2)}) copy-start(bf16[128,1024]{1,0:T(8,128)(2,1)S(1)} %get-tuple-element.120.refs_10_) | copy-start | bytes 786436
  1.3 84.3 %copy-start.3 = (bf16[128,1024]{1,0:T(8,128)(2,1)}, bf16[128,1024]{1,0:T(8,128)(2,1)S(1)}, u32[]{:S(2)}) copy-start(bf16[128,1024]{1,0:T(8,128)(2,1)S(1)} %get-tuple-element.113.refs_3_) | copy-start | bytes 786436
  1.3 11.5 %collective-permute-start.1 = (bf16[128,1024]{1,0:T(8,128)(2,1)S(1)}, bf16[128,1024]{1,0:T(8,128)(2,1)S(1)}, u32[]{:S(2)}, u32[]{:S(2)}) collective-permute-start(bf16[128,1024]{1,0:T(8,128)(2,1)S(1)} %get-tuple-element.91.refs_3_), channel_id=1, source_target_pairs={{1,0},{2,1},{3,2},{5,4},{6,5},{7,6},{9,8},{10,9},{11,10},{13,12},{... | collective-permute-start | bytes 786440 | tf_op jit(solution)/shard_map/ppermute | solution.py:48
  2.6 11.5 %collective-permute-start = (bf16[128,1024]{1,0:T(8,128)(2,1)S(1)}, bf16[128,1024]{1,0:T(8,128)(2,1)S(1)}, u32[]{:S(2)}, u32[]{:S(2)}) collective-permute-start(bf16[128,1024]{1,0:T(8,128)(2,1)S(1)} %get-tuple-element.91.refs_3_), channel_id=1, source_target_pairs={{0,1},{1,2},{2,3},{4,5},{5,6},{6,7},{8,9},{9,10},{10,11},{12,13},{... | collective-permute-start | bytes 786440 | tf_op jit(solution)/shard_map/ppermute | solution.py:47
  8.2 14.2 %collective-permute-start.15 = (bf16[128,1024]{1,0:T(8,128)(2,1)S(1)}, bf16[128,1024]{1,0:T(8,128)(2,1)S(1)}, u32[]{:S(2)}, u32[]{:S(2)}) collective-permute-start(bf16[128,1024]{1,0:T(8,128)(2,1)S(1)} %get-tuple-element.98.refs_10_), channel_id=1, source_target_pairs={{1,0},{2,1},{3,2},{5,4},{6,5},{7,6},{9,8},{10,9},{11,10},{13,12},{... | collective-permute-start | bytes 786440 | tf_op jit(solution)/shard_map/ppermute | solution.py:48
  12.8 32.3 %copy-start.10 = (bf16[128,1024]{1,0:T(8,128)(2,1)}, bf16[128,1024]{1,0:T(8,128)(2,1)S(1)}, u32[]{:S(2)}) copy-start(bf16[128,1024]{1,0:T(8,128)(2,1)S(1)} %collective-permute-done.1.refs_5_) | copy-start | bytes 786436
  12.8 11.0 %collective-permute-start.3 = (bf16[128,1024]{1,0:T(8,128)(2,1)S(1)}, bf16[128,1024]{1,0:T(8,128)(2,1)S(1)}, u32[]{:S(2)}, u32[]{:S(2)}) collective-permute-start(bf16[128,1024]{1,0:T(8,128)(2,1)S(1)} %collective-permute-done.1.refs_5_), channel_id=1, source_target_pairs={{1,0},{2,1},{5,4},{6,5},{9,8},{10,9},{13,12},{14,13},{17,16},{18,1... | collective-permute-start | bytes 786440 | tf_op jit(solution)/shard_map/ppermute | solution.py:48
  14.1 36.3 %copy-start.11 = (bf16[128,1024]{1,0:T(8,128)(2,1)}, bf16[128,1024]{1,0:T(8,128)(2,1)S(1)}, u32[]{:S(2)}) copy-start(bf16[128,1024]{1,0:T(8,128)(2,1)S(1)} %collective-permute-done.refs_4_) | copy-start | bytes 786436
  14.1 11.0 %collective-permute-start.2 = (bf16[128,1024]{1,0:T(8,128)(2,1)S(1)}, bf16[128,1024]{1,0:T(8,128)(2,1)S(1)}, u32[]{:S(2)}, u32[]{:S(2)}) collective-permute-start(bf16[128,1024]{1,0:T(8,128)(2,1)S(1)} %collective-permute-done.refs_4_), channel_id=1, source_target_pairs={{1,2},{2,3},{5,6},{6,7},{9,10},{10,11},{13,14},{14,15},{17,18},{18... | collective-permute-start | bytes 786440 | tf_op jit(solution)/shard_map/ppermute | solution.py:47
  14.8 11.4 %collective-permute-start.14 = (bf16[128,1024]{1,0:T(8,128)(2,1)S(1)}, bf16[128,1024]{1,0:T(8,128)(2,1)S(1)}, u32[]{:S(2)}, u32[]{:S(2)}) collective-permute-start(bf16[128,1024]{1,0:T(8,128)(2,1)S(1)} %get-tuple-element.98.refs_10_), channel_id=1, source_target_pairs={{0,1},{1,2},{2,3},{4,5},{5,6},{6,7},{8,9},{9,10},{10,11},{12,13},{... | collective-permute-start | bytes 786440 | tf_op jit(solution)/shard_map/ppermute | solution.py:47
  22.3 28.0 %copy-start.12 = (bf16[128,1024]{1,0:T(8,128)(2,1)}, bf16[128,1024]{1,0:T(8,128)(2,1)S(1)}, u32[]{:S(2)}) copy-start(bf16[128,1024]{1,0:T(8,128)(2,1)S(1)} %collective-permute-done.15.refs_12_) | copy-start | bytes 786436
  22.4 10.8 %collective-permute-start.17 = (bf16[128,1024]{1,0:T(8,128)(2,1)S(1)}, bf16[128,1024]{1,0:T(8,128)(2,1)S(1)}, u32[]{:S(2)}, u32[]{:S(2)}) collective-permute-start(bf16[128,1024]{1,0:T(8,128)(2,1)S(1)} %collective-permute-done.15.refs_12_), channel_id=1, source_target_pairs={{1,0},{2,1},{5,4},{6,5},{9,8},{10,9},{13,12},{14,13},{17,16},{18,1... | collective-permute-start | bytes 786440 | tf_op jit(solution)/shard_map/ppermute | solution.py:48
  23.8 26.6 %copy-start.13 = (bf16[128,1024]{1,0:T(8,128)(2,1)}, bf16[128,1024]{1,0:T(8,128)(2,1)S(1)}, u32[]{:S(2)}) copy-start(bf16[128,1024]{1,0:T(8,128)(2,1)S(1)} %collective-permute-done.3.refs_7_) | copy-start | bytes 786436
  23.8 13.5 %collective-permute-start.5 = (bf16[128,1024]{1,0:T(8,128)(2,1)S(1)}, bf16[128,1024]{1,0:T(8,128)(2,1)S(1)}, u32[]{:S(2)}, u32[]{:S(2)}) collective-permute-start(bf16[128,1024]{1,0:T(8,128)(2,1)S(1)} %collective-permute-done.3.refs_7_), channel_id=1, source_target_pairs={{1,0},{5,4},{9,8},{13,12},{17,16},{21,20},{25,24},{29,28}} | collective-permute-start | bytes 786440 | tf_op jit(solution)/shard_map/ppermute | solution.py:48
  25.1 25.3 %copy-start.14 = (bf16[128,1024]{1,0:T(8,128)(2,1)}, bf16[128,1024]{1,0:T(8,128)(2,1)S(1)}, u32[]{:S(2)}) copy-start(bf16[128,1024]{1,0:T(8,128)(2,1)S(1)} %collective-permute-done.2.refs_6_) | copy-start | bytes 786436
  25.1 12.2 %collective-permute-start.4 = (bf16[128,1024]{1,0:T(8,128)(2,1)S(1)}, bf16[128,1024]{1,0:T(8,128)(2,1)S(1)}, u32[]{:S(2)}, u32[]{:S(2)}) collective-permute-start(bf16[128,1024]{1,0:T(8,128)(2,1)S(1)} %collective-permute-done.2.refs_6_), channel_id=1, source_target_pairs={{2,3},{6,7},{10,11},{14,15},{18,19},{22,23},{26,27},{30,31}} | collective-permute-start | bytes 786440 | tf_op jit(solution)/shard_map/ppermute | solution.py:47
  26.2 24.2 %copy-start.15 = (bf16[128,1024]{1,0:T(8,128)(2,1)}, bf16[128,1024]{1,0:T(8,128)(2,1)S(1)}, u32[]{:S(2)}) copy-start(bf16[128,1024]{1,0:T(8,128)(2,1)S(1)} %collective-permute-done.14.refs_11_) | copy-start | bytes 786436
  26.2 18.9 %collective-permute-start.16 = (bf16[128,1024]{1,0:T(8,128)(2,1)S(1)}, bf16[128,1024]{1,0:T(8,128)(2,1)}, u32[]{:S(2)}, u32[]{:S(2)}) collective-permute-start(bf16[128,1024]{1,0:T(8,128)(2,1)S(1)} %collective-permute-done.14.refs_11_), channel_id=1, source_target_pairs={{1,2},{2,3},{5,6},{6,7},{9,10},{10,11},{13,14},{14,15},{17,18},{18... | collective-permute-start | bytes 786440 | tf_op jit(solution)/shard_map/ppermute | solution.py:47
  33.1 24.7 %copy-start.16 = (bf16[128,1024]{1,0:T(8,128)(2,1)}, bf16[128,1024]{1,0:T(8,128)(2,1)S(1)}, u32[]{:S(2)}) copy-start(bf16[128,1024]{1,0:T(8,128)(2,1)S(1)} %collective-permute-done.17.refs_14_) | copy-start | bytes 786436
  33.1 19.3 %collective-permute-start.19 = (bf16[128,1024]{1,0:T(8,128)(2,1)S(1)}, bf16[128,1024]{1,0:T(8,128)(2,1)S(1)}, u32[]{:S(2)}, u32[]{:S(2)}) collective-permute-start(bf16[128,1024]{1,0:T(8,128)(2,1)S(1)} %collective-permute-done.17.refs_14_), channel_id=1, source_target_pairs={{1,0},{5,4},{9,8},{13,12},{17,16},{21,20},{25,24},{29,28}} | collective-permute-start | bytes 786440 | tf_op jit(solution)/shard_map/ppermute | solution.py:48
  37.2 16.6 %collective-permute-start.8 = (bf16[128,1024]{1,0:T(8,128)(2,1)S(1)}, bf16[128,1024]{1,0:T(8,128)(2,1)}, u32[]{:S(2)}, u32[]{:S(2)}) collective-permute-start(bf16[128,1024]{1,0:T(8,128)(2,1)S(1)} %get-tuple-element.113.refs_3_), channel_id=1, source_target_pairs={{1,0},{2,1},{3,2},{5,4},{6,5},{7,6},{9,8},{10,9},{11,10},{13,12},{... | collective-permute-start | bytes 786440 | tf_op jit(solution)/shard_map/ppermute | solution.py:48
  38.5 16.6 %collective-permute-start.6 = (bf16[128,1024]{1,0:T(8,128)(2,1)S(1)}, bf16[128,1024]{1,0:T(8,128)(2,1)}, u32[]{:S(2)}, u32[]{:S(2)}) collective-permute-start(bf16[128,1024]{1,0:T(8,128)(2,1)S(1)} %get-tuple-element.113.refs_3_), channel_id=1, source_target_pairs={{0,1},{1,2},{2,3},{4,5},{5,6},{6,7},{8,9},{9,10},{10,11},{12,13},{... | collective-permute-start | bytes 786440 | tf_op jit(solution)/shard_map/ppermute | solution.py:47
  43.8 12.8 %collective-permute-start.12 = (bf16[128,1024]{1,0:T(8,128)(2,1)S(1)}, bf16[128,1024]{1,0:T(8,128)(2,1)}, u32[]{:S(2)}, u32[]{:S(2)}) collective-permute-start(bf16[128,1024]{1,0:T(8,128)(2,1)S(1)} %get-tuple-element.120.refs_10_), channel_id=1, source_target_pairs={{1,0},{2,1},{3,2},{5,4},{6,5},{7,6},{9,8},{10,9},{11,10},{13,12},{... | collective-permute-start | bytes 786440 | tf_op jit(solution)/shard_map/ppermute | solution.py:48
  45.1 12.7 %collective-permute-start.10 = (bf16[128,1024]{1,0:T(8,128)(2,1)S(1)}, bf16[128,1024]{1,0:T(8,128)(2,1)}, u32[]{:S(2)}, u32[]{:S(2)}) collective-permute-start(bf16[128,1024]{1,0:T(8,128)(2,1)S(1)} %get-tuple-element.120.refs_10_), channel_id=1, source_target_pairs={{0,1},{1,2},{2,3},{4,5},{5,6},{6,7},{8,9},{9,10},{10,11},{12,13},{... | collective-permute-start | bytes 786440 | tf_op jit(solution)/shard_map/ppermute | solution.py:47
  52.4 11.7 %collective-permute-start.18 = (bf16[128,1024]{1,0:T(8,128)(2,1)}, bf16[128,1024]{1,0:T(8,128)(2,1)}, u32[]{:S(2)}, u32[]{:S(2)}) collective-permute-start(bf16[128,1024]{1,0:T(8,128)(2,1)} %collective-permute-done.16.refs_13_), channel_id=1, source_target_pairs={{2,3},{6,7},{10,11},{14,15},{18,19},{22,23},{26,27},{30,31}} | collective-permute-start | bytes 786440 | tf_op jit(solution)/shard_map/ppermute | solution.py:47
  53.9 10.3 %collective-permute-start.9 = (bf16[128,1024]{1,0:T(8,128)(2,1)}, bf16[128,1024]{1,0:T(8,128)(2,1)}, u32[]{:S(2)}, u32[]{:S(2)}) collective-permute-start(bf16[128,1024]{1,0:T(8,128)(2,1)} %collective-permute-done.8.refs_5_), channel_id=1, source_target_pairs={{1,0},{2,1},{5,4},{6,5},{9,8},{10,9},{13,12},{14,13},{17,16},{18,1... | collective-permute-start | bytes 786440 | tf_op jit(solution)/shard_map/ppermute | solution.py:48
  55.2 9.0 %collective-permute-start.7 = (bf16[128,1024]{1,0:T(8,128)(2,1)}, bf16[128,1024]{1,0:T(8,128)(2,1)}, u32[]{:S(2)}, u32[]{:S(2)}) collective-permute-start(bf16[128,1024]{1,0:T(8,128)(2,1)} %collective-permute-done.6.refs_4_), channel_id=1, source_target_pairs={{1,2},{2,3},{5,6},{6,7},{9,10},{10,11},{13,14},{14,15},{17,18},{18... | collective-permute-start | bytes 786440 | tf_op jit(solution)/shard_map/ppermute | solution.py:47
  56.6 11.3 %collective-permute-start.13 = (bf16[128,1024]{1,0:T(8,128)(2,1)}, bf16[128,1024]{1,0:T(8,128)(2,1)}, u32[]{:S(2)}, u32[]{:S(2)}) collective-permute-start(bf16[128,1024]{1,0:T(8,128)(2,1)} %collective-permute-done.12.refs_12_), channel_id=1, source_target_pairs={{1,0},{2,1},{5,4},{6,5},{9,8},{10,9},{13,12},{14,13},{17,16},{18,1... | collective-permute-start | bytes 786440 | tf_op jit(solution)/shard_map/ppermute | solution.py:48
  57.9 10.0 %collective-permute-start.11 = (bf16[128,1024]{1,0:T(8,128)(2,1)}, bf16[128,1024]{1,0:T(8,128)(2,1)}, u32[]{:S(2)}, u32[]{:S(2)}) collective-permute-start(bf16[128,1024]{1,0:T(8,128)(2,1)} %collective-permute-done.10.refs_11_), channel_id=1, source_target_pairs={{1,2},{2,3},{5,6},{6,7},{9,10},{10,11},{13,14},{14,15},{17,18},{18... | collective-permute-start | bytes 786440 | tf_op jit(solution)/shard_map/ppermute | solution.py:47
  67.8 17.8 %collective-permute-start.20 = (bf16[128,1024]{1,0:T(8,128)(2,1)}, bf16[128,1024]{1,0:T(8,128)(2,1)}, u32[]{:S(2)}, u32[]{:S(2)}) collective-permute-start(bf16[128,1024]{1,0:T(8,128)(2,1)} %collective-permute-done.7.refs_6_), channel_id=1, source_target_pairs={{2,3},{6,7},{10,11},{14,15},{18,19},{22,23},{26,27},{30,31}} | collective-permute-start | bytes 786440 | tf_op jit(solution)/shard_map/ppermute | solution.py:47
  69.2 16.4 %collective-permute-start.21 = (bf16[128,1024]{1,0:T(8,128)(2,1)}, bf16[128,1024]{1,0:T(8,128)(2,1)}, u32[]{:S(2)}, u32[]{:S(2)}) collective-permute-start(bf16[128,1024]{1,0:T(8,128)(2,1)} %collective-permute-done.9.refs_7_), channel_id=1, source_target_pairs={{1,0},{5,4},{9,8},{13,12},{17,16},{21,20},{25,24},{29,28}} | collective-permute-start | bytes 786440 | tf_op jit(solution)/shard_map/ppermute | solution.py:48
  70.5 15.1 %collective-permute-start.22 = (bf16[128,1024]{1,0:T(8,128)(2,1)}, bf16[128,1024]{1,0:T(8,128)(2,1)}, u32[]{:S(2)}, u32[]{:S(2)}) collective-permute-start(bf16[128,1024]{1,0:T(8,128)(2,1)} %collective-permute-done.11.refs_13_), channel_id=1, source_target_pairs={{2,3},{6,7},{10,11},{14,15},{18,19},{22,23},{26,27},{30,31}} | collective-permute-start | bytes 786440 | tf_op jit(solution)/shard_map/ppermute | solution.py:47
  71.9 13.8 %collective-permute-start.23 = (bf16[128,1024]{1,0:T(8,128)(2,1)}, bf16[128,1024]{1,0:T(8,128)(2,1)}, u32[]{:S(2)}, u32[]{:S(2)}) collective-permute-start(bf16[128,1024]{1,0:T(8,128)(2,1)} %collective-permute-done.13.refs_14_), channel_id=1, source_target_pairs={{1,0},{5,4},{9,8},{13,12},{17,16},{21,20},{25,24},{29,28}} | collective-permute-start | bytes 786440 | tf_op jit(solution)/shard_map/ppermute | solution.py:48
  85.6 17.6 %all-to-all-start = ((bf16[8,128,384]{2,1,0:T(8,128)(2,1)}), bf16[8,128,384]{2,1,0:T(8,128)(2,1)}, u32[]{:S(2)}, u32[]{:S(2)}) async-start(bf16[8,128,384]{2,1,0:T(8,128)(2,1)} %shard_map.74), calls=%async_computation | async-start | bytes 1572864 | tf_op jit(solution)/shard_map/all_to_all | solution.py:470
  90.7 32.2 %copy-start.26 = (bf16[2,128,256]{2,1,0:T(8,128)(2,1)S(1)}, bf16[2,128,256]{2,1,0:T(8,128)(2,1)}, u32[]{:S(2)}) copy-start(bf16[2,128,256]{2,1,0:T(8,128)(2,1)} %get-tuple-element.139) | copy-start | bytes 393220
  103.2 19.6 %all-to-all-start.1 = ((bf16[8,128,384]{2,1,0:T(8,128)(2,1)}), bf16[8,128,384]{2,1,0:T(8,128)(2,1)S(1)}, u32[]{:S(2)}, u32[]{:S(2)}) async-start(bf16[8,128,384]{2,1,0:T(8,128)(2,1)} %shard_map.75), calls=%async_computation.1 | async-start | bytes 1572864 | tf_op jit(solution)/shard_map/all_to_all | solution.py:470
  107.3 9.7 %collective-permute-start.25 = (bf16[2,128,256]{2,1,0:T(8,128)(2,1)S(1)}, bf16[2,128,256]{2,1,0:T(8,128)(2,1)S(1)}, u32[]{:S(2)}, u32[]{:S(2)}) collective-permute-start(bf16[2,128,256]{2,1,0:T(8,128)(2,1)S(1)} %copy-done.29), channel_id=1, source_target_pairs={{0,1},{1,2},{2,3},{3,0},{4,5},{5,6},{6,7},{7,4},{8,9},{9,10},{10,1... | collective-permute-start | bytes 393224 | tf_op jit(solution)/shard_map/ppermute | solution.py:414
  113.2 9.6 %collective-permute-start.26 = (bf16[2,128,256]{2,1,0:T(8,128)(2,1)S(1)}, bf16[2,128,256]{2,1,0:T(8,128)(2,1)S(1)}, u32[]{:S(2)}, u32[]{:S(2)}) collective-permute-start(bf16[2,128,256]{2,1,0:T(8,128)(2,1)S(1)} %copy-done.28), channel_id=1, source_target_pairs={{0,2},{1,3},{2,0},{3,1},{4,6},{5,7},{6,4},{7,5},{8,10},{9,11},{10,... | collective-permute-start | bytes 393224 | tf_op jit(solution)/shard_map/ppermute | solution.py:414
  113.5 9.3 %collective-permute-start.27 = (bf16[2,128,256]{2,1,0:T(8,128)(2,1)S(1)}, bf16[2,128,256]{2,1,0:T(8,128)(2,1)S(1)}, u32[]{:S(2)}, u32[]{:S(2)}) collective-permute-start(bf16[2,128,256]{2,1,0:T(8,128)(2,1)S(1)} %copy-done.27), channel_id=1, source_target_pairs={{0,3},{1,0},{2,1},{3,2},{4,7},{5,4},{6,5},{7,6},{8,11},{9,8},{10,9... | collective-permute-start | bytes 393224 | tf_op jit(solution)/shard_map/ppermute | solution.py:414
  116.4 9.9 %collective-permute-start.24 = (bf16[8,128,384]{2,1,0:T(8,128)(2,1)}, bf16[8,128,384]{2,1,0:T(8,128)(2,1)}, u32[]{:S(2)}, u32[]{:S(2)}) collective-permute-start(bf16[8,128,384]{2,1,0:T(8,128)(2,1)} %all-to-all-done.refs_0_), channel_id=1, source_target_pairs={{0,4},{4,0},{8,12},{12,8},{16,20},{20,16},{24,28},{28,24},{1,5},{5... | collective-permute-start | bytes 2359304 | tf_op jit(solution)/shard_map/ppermute | solution.py:477
  122.8 3.5 %collective-permute-start.28 = (bf16[8,128,384]{2,1,0:T(8,128)(2,1)S(1)}, bf16[8,128,384]{2,1,0:T(8,128)(2,1)}, u32[]{:S(2)}, u32[]{:S(2)}) collective-permute-start(bf16[8,128,384]{2,1,0:T(8,128)(2,1)S(1)} %all-to-all-done.1.refs_2_), channel_id=1, source_target_pairs={{0,4},{4,0},{8,12},{12,8},{16,20},{20,16},{24,28},{28,24},{1,5},{5... | collective-permute-start | bytes 2359304 | tf_op jit(solution)/shard_map/ppermute | solution.py:477
  123.0 14.6 %collective-permute-start.29 = (bf16[512,256]{1,0:T(8,128)(2,1)S(1)}, bf16[512,256]{1,0:T(8,128)(2,1)S(1)}, u32[]{:S(2)}, u32[]{:S(2)}) collective-permute-start(bf16[512,256]{1,0:T(8,128)(2,1)S(1)} %pad_maximum_fusion.2), channel_id=1, source_target_pairs={{0,8},{4,12},{8,0},{12,4},{16,24},{20,28},{24,16},{28,20},{1,9},{5... | collective-permute-start | bytes 786440 | tf_op jit(solution)/shard_map/ppermute | solution.py:424
  124.8 12.8 %collective-permute-start.30 = (bf16[512,256]{1,0:T(8,128)(2,1)S(1)}, bf16[512,256]{1,0:T(8,128)(2,1)}, u32[]{:S(2)}, u32[]{:S(2)}) collective-permute-start(bf16[512,256]{1,0:T(8,128)(2,1)S(1)} %pad_maximum_fusion.3), channel_id=1, source_target_pairs={{0,16},{4,20},{8,24},{12,28},{16,0},{20,4},{24,8},{28,12},{1,17},{... | collective-permute-start | bytes 786440 | tf_op jit(solution)/shard_map/ppermute | solution.py:424
  150.8 31.9 %copy-start.7 = (bf16[4,256,128]{2,1,0:T(8,128)(2,1)}, bf16[4,256,128]{2,1,0:T(8,128)(2,1)S(1)}, u32[]{:S(2)}) copy-start(bf16[4,256,128]{2,1,0:T(8,128)(2,1)S(1)} %get-tuple-element.173) | copy-start | bytes 786436
  150.8 31.9 %copy-start.8 = (bf16[4,256,128]{2,1,0:T(8,128)(2,1)}, bf16[4,256,128]{2,1,0:T(8,128)(2,1)S(1)}, u32[]{:S(2)}) copy-start(bf16[4,256,128]{2,1,0:T(8,128)(2,1)S(1)} %get-tuple-element.174) | copy-start | bytes 786436
  150.8 10.5 %collective-permute-start.37 = (bf16[4,256,128]{2,1,0:T(8,128)(2,1)S(1)}, bf16[4,256,128]{2,1,0:T(8,128)(2,1)S(1)}, u32[]{:S(2)}, u32[]{:S(2)}) collective-permute-start(bf16[4,256,128]{2,1,0:T(8,128)(2,1)S(1)} %get-tuple-element.173), channel_id=1, source_target_pairs={{1,0},{2,1},{3,2},{5,4},{6,5},{7,6},{9,8},{10,9},{11,10},{13,12},{... | collective-permute-start | bytes 786440 | tf_op jit(solution)/shard_map/ppermute | solution.py:48
  153.1 18.7 %collective-permute-start.40 = (bf16[1024,256]{1,0:T(8,128)(2,1)S(1)}, bf16[1024,256]{1,0:T(8,128)(2,1)S(1)}, u32[]{:S(2)}, u32[]{:S(2)}) collective-permute-start(bf16[1024,256]{1,0:T(8,128)(2,1)S(1)} %pad_maximum_fusion.1), channel_id=1, source_target_pairs={{0,8},{4,12},{8,0},{12,4},{16,24},{20,28},{24,16},{28,20},{1,9},{5... | collective-permute-start | bytes 1572872 | tf_op jit(solution)/shard_map/ppermute | solution.py:424
  153.7 18.8 %collective-permute-start.39 = (bf16[1024,256]{1,0:T(8,128)(2,1)S(1)}, bf16[1024,256]{1,0:T(8,128)(2,1)S(1)}, u32[]{:S(2)}, u32[]{:S(2)}) collective-permute-start(bf16[1024,256]{1,0:T(8,128)(2,1)S(1)} %pad_maximum_fusion), channel_id=1, source_target_pairs={{0,16},{4,20},{8,24},{12,28},{16,0},{20,4},{24,8},{28,12},{1,17},{... | collective-permute-start | bytes 1572872 | tf_op jit(solution)/shard_map/ppermute | solution.py:424
  154.4 11.4 %collective-permute-start.35 = (bf16[4,256,128]{2,1,0:T(8,128)(2,1)S(1)}, bf16[4,256,128]{2,1,0:T(8,128)(2,1)S(1)}, u32[]{:S(2)}, u32[]{:S(2)}) collective-permute-start(bf16[4,256,128]{2,1,0:T(8,128)(2,1)S(1)} %get-tuple-element.173), channel_id=1, source_target_pairs={{0,1},{1,2},{2,3},{4,5},{5,6},{6,7},{8,9},{9,10},{10,11},{12,13},{... | collective-permute-start | bytes 786440 | tf_op jit(solution)/shard_map/ppermute | solution.py:47
  159.9 9.2 %collective-permute-start.33 = (bf16[4,256,128]{2,1,0:T(8,128)(2,1)S(1)}, bf16[4,256,128]{2,1,0:T(8,128)(2,1)S(1)}, u32[]{:S(2)}, u32[]{:S(2)}) collective-permute-start(bf16[4,256,128]{2,1,0:T(8,128)(2,1)S(1)} %get-tuple-element.174), channel_id=1, source_target_pairs={{1,0},{2,1},{3,2},{5,4},{6,5},{7,6},{9,8},{10,9},{11,10},{13,12},{... | collective-permute-start | bytes 786440 | tf_op jit(solution)/shard_map/ppermute | solution.py:48
  161.3 22.8 %copy-start.20 = (bf16[4,256,128]{2,1,0:T(8,128)(2,1)}, bf16[4,256,128]{2,1,0:T(8,128)(2,1)S(1)}, u32[]{:S(2)}) copy-start(bf16[4,256,128]{2,1,0:T(8,128)(2,1)S(1)} %collective-permute-done.37) | copy-start | bytes 786436
  161.3 9.2 %collective-permute-start.31 = (bf16[4,256,128]{2,1,0:T(8,128)(2,1)S(1)}, bf16[4,256,128]{2,1,0:T(8,128)(2,1)S(1)}, u32[]{:S(2)}, u32[]{:S(2)}) collective-permute-start(bf16[4,256,128]{2,1,0:T(8,128)(2,1)S(1)} %get-tuple-element.174), channel_id=1, source_target_pairs={{0,1},{1,2},{2,3},{4,5},{5,6},{6,7},{8,9},{9,10},{10,11},{12,13},{... | collective-permute-start | bytes 786440 | tf_op jit(solution)/shard_map/ppermute | solution.py:47
  165.8 8.8 %collective-permute-start.38 = (bf16[4,256,128]{2,1,0:T(8,128)(2,1)S(1)}, bf16[4,256,128]{2,1,0:T(8,128)(2,1)}, u32[]{:S(2)}, u32[]{:S(2)}) collective-permute-start(bf16[4,256,128]{2,1,0:T(8,128)(2,1)S(1)} %collective-permute-done.37), channel_id=1, source_target_pairs={{1,0},{2,1},{5,4},{6,5},{9,8},{10,9},{13,12},{14,13},{17,16},{18,1... | collective-permute-start | bytes 786440 | tf_op jit(solution)/shard_map/ppermute | solution.py:48
  169.1 5.5 %collective-permute-start.36 = (bf16[4,256,128]{2,1,0:T(8,128)(2,1)S(1)}, bf16[4,256,128]{2,1,0:T(8,128)(2,1)}, u32[]{:S(2)}, u32[]{:S(2)}) collective-permute-start(bf16[4,256,128]{2,1,0:T(8,128)(2,1)S(1)} %collective-permute-done.35), channel_id=1, source_target_pairs={{1,2},{2,3},{5,6},{6,7},{9,10},{10,11},{13,14},{14,15},{17,18},{18... | collective-permute-start | bytes 786440 | tf_op jit(solution)/shard_map/ppermute | solution.py:47
  170.5 10.9 %collective-permute-start.34 = (bf16[4,256,128]{2,1,0:T(8,128)(2,1)S(1)}, bf16[4,256,128]{2,1,0:T(8,128)(2,1)}, u32[]{:S(2)}, u32[]{:S(2)}) collective-permute-start(bf16[4,256,128]{2,1,0:T(8,128)(2,1)S(1)} %collective-permute-done.33), channel_id=1, source_target_pairs={{1,0},{2,1},{5,4},{6,5},{9,8},{10,9},{13,12},{14,13},{17,16},{18,1... | collective-permute-start | bytes 786440 | tf_op jit(solution)/shard_map/ppermute | solution.py:48
  171.8 9.6 %collective-permute-start.32 = (bf16[4,256,128]{2,1,0:T(8,128)(2,1)S(1)}, bf16[4,256,128]{2,1,0:T(8,128)(2,1)S(1)}, u32[]{:S(2)}, u32[]{:S(2)}) collective-permute-start(bf16[4,256,128]{2,1,0:T(8,128)(2,1)S(1)} %collective-permute-done.31), channel_id=1, source_target_pairs={{1,2},{2,3},{5,6},{6,7},{9,10},{10,11},{13,14},{14,15},{17,18},{18... | collective-permute-start | bytes 786440 | tf_op jit(solution)/shard_map/ppermute | solution.py:47
  182.5 20.2 %collective-permute-start.42 = (bf16[2048,256]{1,0:T(8,128)(2,1)S(1)}, bf16[2048,256]{1,0:T(8,128)(2,1)}, u32[]{:S(2)}, u32[]{:S(2)}) collective-permute-start(bf16[2048,256]{1,0:T(8,128)(2,1)S(1)} %constant_dynamic-update-slice_fusion.4.refs_1_), channel_id=1, source_target_pairs={{0,4},{4,0},{8,12},{12,8},{16,20},{20,16},{24,28},{28,24},{1,5},{5... | collective-permute-start | bytes 3145736 | tf_op jit(solution)/shard_map/ppermute | solution.py:527
  183.8 18.9 %collective-permute-start.41 = (bf16[2048,256]{1,0:T(8,128)(2,1)S(1)}, bf16[2048,256]{1,0:T(8,128)(2,1)S(1)}, u32[]{:S(2)}, u32[]{:S(2)}) collective-permute-start(bf16[2048,256]{1,0:T(8,128)(2,1)S(1)} %constant_dynamic-update-slice_fusion.refs_0_), channel_id=1, source_target_pairs={{0,4},{4,0},{8,12},{12,8},{16,20},{20,16},{24,28},{28,24},{1,5},{5... | collective-permute-start | bytes 3145736 | tf_op jit(solution)/shard_map/ppermute | solution.py:527
  184.1 3.4 %collective-permute-start.43 = (bf16[4,256,128]{2,1,0:T(8,128)(2,1)S(1)}, bf16[4,256,128]{2,1,0:T(8,128)(2,1)S(1)}, u32[]{:S(2)}, u32[]{:S(2)}) collective-permute-start(bf16[4,256,128]{2,1,0:T(8,128)(2,1)S(1)} %collective-permute-done.32), channel_id=1, source_target_pairs={{2,3},{6,7},{10,11},{14,15},{18,19},{22,23},{26,27},{30,31}} | collective-permute-start | bytes 786440 | tf_op jit(solution)/shard_map/ppermute | solution.py:47
  184.8 12.7 %collective-permute-start.44 = (bf16[4,256,128]{2,1,0:T(8,128)(2,1)}, bf16[4,256,128]{2,1,0:T(8,128)(2,1)}, u32[]{:S(2)}, u32[]{:S(2)}) collective-permute-start(bf16[4,256,128]{2,1,0:T(8,128)(2,1)} %collective-permute-done.34), channel_id=1, source_target_pairs={{1,0},{5,4},{9,8},{13,12},{17,16},{21,20},{25,24},{29,28}} | collective-permute-start | bytes 786440 | tf_op jit(solution)/shard_map/ppermute | solution.py:48
  186.1 11.4 %collective-permute-start.45 = (bf16[4,256,128]{2,1,0:T(8,128)(2,1)}, bf16[4,256,128]{2,1,0:T(8,128)(2,1)}, u32[]{:S(2)}, u32[]{:S(2)}) collective-permute-start(bf16[4,256,128]{2,1,0:T(8,128)(2,1)} %collective-permute-done.36), channel_id=1, source_target_pairs={{2,3},{6,7},{10,11},{14,15},{18,19},{22,23},{26,27},{30,31}} | collective-permute-start | bytes 786440 | tf_op jit(solution)/shard_map/ppermute | solution.py:47
  187.5 15.2 %collective-permute-start.46 = (bf16[4,256,128]{2,1,0:T(8,128)(2,1)}, bf16[4,256,128]{2,1,0:T(8,128)(2,1)}, u32[]{:S(2)}, u32[]{:S(2)}) collective-permute-start(bf16[4,256,128]{2,1,0:T(8,128)(2,1)} %collective-permute-done.38), channel_id=1, source_target_pairs={{1,0},{5,4},{9,8},{13,12},{17,16},{21,20},{25,24},{29,28}} | collective-permute-start | bytes 786440 | tf_op jit(solution)/shard_map/ppermute | solution.py:48
  (15 other events, 212.5 us)

commit v9 on v8

--- a/solution.py
+++ b/solution.py
@@ -29,26 +29,18 @@
         pl.when(there)(act)
 
 
-def line_gather(chunks, count, join=None):
+def line_gather(chunks, count, join):
     right = [(d, d + 1) for d in range(count - 1)]
     left = [(d + 1, d) for d in range(count - 1)]
-    found = []
-    for first in range(0, len(chunks), 2):
-        pair = []
-        for chunk in chunks[first : first + 2]:
-            if first:
-                chunk, _ = lax.optimization_barrier((chunk, found[first - 2]))
-            pair.append([chunk])
-        last = [(chunk[0], chunk[0]) for chunk in pair]
-        for step in range(count - 1):
-            if join is not None:
-                last = join(first, step, last, found)
-            for at in range(len(pair)):
-                from_left = lax.ppermute(last[at][0], "tensor", right[step:])
-                from_right = lax.ppermute(last[at][1], "tensor", left[: count - 1 - step])
-                last[at] = (from_left, from_right)
-                pair[at] += [from_left, from_right]
-        found += pair
+    found = [[chunk] for chunk in chunks]
+    last = [(chunk, chunk) for chunk in chunks]
+    for step in range(count - 1):
+        last = join(step, last)
+        for at in range(len(chunks)):
+            from_left = lax.ppermute(last[at][0], "tensor", right[step:])
+            from_right = lax.ppermute(last[at][1], "tensor", left[: count - 1 - step])
+            last[at] = (from_left, from_right)
+            found[at] += [from_left, from_right]
     return found
 
 
@@ -450,20 +442,18 @@
     tensor_count = lax.axis_size("tensor")
     heads = w_query.shape[1] // HEAD
     group = seq_count // heads
-    chunks = min(4, rows // (16 * group))
+    chunks = 2
     chunk_rows = rows // chunks
     part = (lax.axis_index("seq") % group).astype(jnp.int32).reshape(1)
     me = lax.axis_index("tensor").astype(jnp.int32)
     gain = norm_gain.reshape(tensor_count, columns)
     active = (depth >= 2).astype(jnp.int32).reshape(rows, 1)
-    made = []
     shares = weight_shares(w_out, seq_count, tensor_count, columns)
 
-    def work(found):
-        first = chunks - len(found) if made else 0
-        here = active[first * chunk_rows : (first + len(found)) * chunk_rows]
+    def work(found, chunk):
+        here = active[chunk * chunk_rows : (chunk + 1) * chunk_rows]
         return project(
-            me.reshape(1), sum(found, []), here, gain, w_query, w_key, w_value, seq_count, group
+            me.reshape(1), found, here, gain, w_query, w_key, w_value, seq_count, group
         )
 
     def to_heads(sent):
@@ -476,26 +466,20 @@
         ]
         return [got] + [lax.ppermute(got, "seq", ring) for ring in rings]
 
-    def first_pair(first, step, last, found):
-        if first == 2 and step == 2:
-            last, pair, mine = lax.optimization_barrier((last, found[:2], shares))
-            made.append((work(pair), mine))
+    def cut_weight(step, last):
+        nonlocal shares
+        if step == 1:
+            last[1], shares = lax.optimization_barrier((last[1], shares))
         return last
 
-    gathered = line_gather(
-        [hidden[c * chunk_rows : (c + 1) * chunk_rows] for c in range(chunks)],
-        tensor_count,
-        first_pair,
+    first, second = line_gather(
+        [hidden[:chunk_rows], hidden[chunk_rows:]], tensor_count, cut_weight
     )
-    rest = gathered[-2:]
-    got = []
-    if made:
-        (early, shares), rest = lax.optimization_barrier((made[0], rest))
-        got = [to_heads(early)]
-    sent, got, shares = lax.optimization_barrier((work(rest), got, shares))
+    early, second = lax.optimization_barrier((work(first, 0), second))
+    sent, early, shares = lax.optimization_barrier((work(second, 1), to_heads(early), shares))
     sending = send_shares(shares, tensor_count)
     late, sending = lax.optimization_barrier((to_heads(sent), sending))
-    pieces = sum([to_parts(each) for each in got + [late]], [])
+    pieces = to_parts(early) + to_parts(late)
 
     heads, cuts, halves, _ = weight_cuts(w_out, seq_count, columns)
     held, flips = [], []
@@ -512,7 +496,7 @@
     home = lax.all_to_all(out, "seq", split_axis=0, concat_axis=0)
     home, held = lax.optimization_barrier((home, held))
 
-    def spread(first, step, last, found):
+    def spread(step, last):
         nonlocal held
         if held and step == 2:
             for stage in range(1, len(flips)):

time: 215 us -> 208 us (0.967)
  starting transfers between devices: 93.1 us -> 63.1 us
  waiting for transfers between devices: 45 us -> 70.8 us
    ppermute x18 -> x12, waiting for transfers between devices: 38.1 us -> 58 us  [line_gather(): from_right = lax.ppermute(last[at][1], 'tensor', left[:count - 1 - step])]
    ppermute x18 -> x12, starting transfers between devices: 47.3 us -> 30 us  [line_gather(): from_left = lax.ppermute(last[at][0], 'tensor', right[step:])]
    ppermute x18 -> x12, starting transfers between devices: 23.4 us -> 15.6 us  [line_gather(): from_right = lax.ppermute(last[at][1], 'tensor', left[:count - 1 - step])]
    ppermute x3, starting transfers between devices: 9.04 us -> 4.09 us  [send_shares(): shares[step] = lax.ppermute(shares[step], 'tensor', ring)]
    ppermute x18 -> x12, waiting for transfers between devices: 0.48 us -> 3.89 us  [line_gather(): from_left = lax.ppermute(last[at][0], 'tensor', right[step:])]
    ppermute x3, waiting for transfers between devices: 6.41 us -> 8.88 us  [send_shares(): shares[step] = lax.ppermute(shares[step], 'tensor', ring)]
  transfers between devices with their start and end apart: 49 -> 37, of which waited for: 14 -> 15; matrix products, arithmetic and copies ran while one was open for 4% -> 3% of each run, Pallas kernels for 19% -> 19%
where the time goes in v9:
time: 208 us; the launch traced here: 207 us
  waiting for transfers between devices  70.8 us (34%)
  starting transfers between devices  63.1 us (30%)
  Pallas kernels  48.3 us (23%)
  blocking collectives  13.1 us (6%)
  local copies, waits for them, and re-layouts  8.16 us (4%)
  other arithmetic  2.25 us (1%)
    ppermute x12, waiting for transfers between devices, line_gather(): from_right = lax.ppermute(last[at][1], 'tensor', left[:count - 1 - step])  58 us
    ppermute x12, starting transfers between devices, line_gather(): from_left = lax.ppermute(last[at][0], 'tensor', right[step:])  30 us
    pallas_call x2, Pallas kernels, project(): pl.pallas_call(partial(project_kernel, group, count), in_specs=[pl.BlockS...  24.2 us
    ppermute x12, starting transfers between devices, line_gather(): from_right = lax.ppermute(last[at][1], 'tensor', left[:count - 1 - step])  15.6 us
    all_to_all x1, blocking collectives, shards(): home = lax.all_to_all(out, 'seq', split_axis=0, concat_axis=0)  13.1 us
    pallas_call x1, Pallas kernels, attend(): pl.pallas_call(partial(attend_kernel, chunks, group, rows), in_specs=[pl....  11.3 us
    pallas_call x1, Pallas kernels, output(): pl.pallas_call(partial(output_kernel, group, count, cuts, halves), in_spe...  9.39 us
    ppermute x3, waiting for transfers between devices, send_shares(): shares[step] = lax.ppermute(shares[step], 'tensor', ring)  8.88 us
  transfers between devices with their start and end apart: 37, of which 15 were waited for; matrix products, arithmetic and copies ran while one was open for 3% of the time, Pallas kernels for 19%

profile of v9, /device:TPU:0, one launch (start us, length us, event | category | flops | bytes accessed | tf_op | source)
XLA Modules:
  0.0 206.5 jit_solution(15287113386252556186)
XLA Ops:
  0.0 1.3 fusion.5
  1.3 5.7 %collective-permute-start = (bf16[256,1024]{1,0:T(8,128)(2,1)S(1)}, bf16[256,1024]{1,0:T(8,128)(2,1)}, u32[]{:S(2)}, u32[]{:S(2)}) collective-permute-start(bf16[256,1024]{1,0:T(8,128)(2,1)S(1)} %get-tuple-element.108.refs_3_), channel_id=1, source_target_pairs={{0,1},{1,2},{2,3},{4,5},{5,6},{6,7},{8,9},{9,10},{10,11},{12,13},{... | collective-permute-start | bytes 1572872 | tf_op jit(solution)/shard_map/ppermute | solution.py:40
  7.1 1.3 collective-permute-start.1
  8.4 5.3 %collective-permute-start.6 = (bf16[256,1024]{1,0:T(8,128)(2,1)S(1)}, bf16[256,1024]{1,0:T(8,128)(2,1)}, u32[]{:S(2)}, u32[]{:S(2)}) collective-permute-start(bf16[256,1024]{1,0:T(8,128)(2,1)S(1)} %get-tuple-element.62.refs_3_), channel_id=1, source_target_pairs={{0,1},{1,2},{2,3},{4,5},{5,6},{6,7},{8,9},{9,10},{10,11},{12,13},{... | collective-permute-start | bytes 1572872 | tf_op jit(solution)/shard_map/ppermute | solution.py:40
  13.7 1.3 collective-permute-start.7
  15.0 3.6 %collective-permute-done.refs_4_ = bf16[256,1024]{1,0:T(8,128)(2,1)} collective-permute-done((bf16[256,1024]{1,0:T(8,128)(2,1)S(1)}, bf16[256,1024]{1,0:T(8,128)(2,1)}, u32[]{:S(2)}, u32[]{:S(2)}) %collective-permute-start) | collective-permute-done | bytes 524320 | tf_op jit(solution)/shard_map/ppermute | solution.py:40
  18.6 1.5 collective-permute-start.2
  20.0 3.8 %collective-permute-done.1.refs_5_ = bf16[256,1024]{1,0:T(8,128)(2,1)} collective-permute-done((bf16[256,1024]{1,0:T(8,128)(2,1)S(1)}, bf16[256,1024]{1,0:T(8,128)(2,1)}, u32[]{:S(2)}, u32[]{:S(2)}) %collective-permute-start.1) | collective-permute-done | bytes 524320 | tf_op jit(solution)/shard_map/ppermute | solution.py:41
  23.9 1.3 collective-permute-start.3
  25.2 0.6 pad_add_fusion.place_ref
  25.8 3.5 %shard_map.74 = (bf16[2,128,256]{2,1,0:T(8,128)(2,1)}, bf16[2,128,256]{2,1,0:T(8,128)(2,1)}, bf16[2,128,256]{2,1,0:T(8,128)(2,1)}, bf16[2,128,256]{2,1,0:T(8,128)(2,1)}) custom-call(s32[3]{0:T(128)} %pad_add_fusion.place_ref, bf16[512,4096]{1,0:T(8,128)(2,1)} %w_ref.1), custom_call_target="tpu_custom_call" | custom-call | tf_op jit(solution)/shard_map/pallas_call | solution.py:364
  29.3 5.9 %collective-permute-done.7.refs_5_ = bf16[256,1024]{1,0:T(8,128)(2,1)} collective-permute-done((bf16[256,1024]{1,0:T(8,128)(2,1)S(1)}, bf16[256,1024]{1,0:T(8,128)(2,1)}, u32[]{:S(2)}, u32[]{:S(2)}) %collective-permute-start.7) | collective-permute-done | bytes 524320 | tf_op jit(solution)/shard_map/ppermute | solution.py:41
  35.1 1.4 collective-permute-start.8
  36.6 1.3 collective-permute-start.9
  37.9 1.5 collective-permute-start.4
  39.3 7.0 %collective-permute-done.3.refs_7_ = bf16[256,1024]{1,0:T(8,128)(2,1)} collective-permute-done((bf16[256,1024]{1,0:T(8,128)(2,1)}, bf16[256,1024]{1,0:T(8,128)(2,1)}, u32[]{:S(2)}, u32[]{:S(2)}) %collective-permute-start.3) | collective-permute-done | bytes 524320 | tf_op jit(solution)/shard_map/ppermute | solution.py:41
  46.4 1.3 collective-permute-start.5
  47.7 1.5 collective-permute-start.10
  49.2 8.4 %collective-permute-done.9.refs_7_ = bf16[256,1024]{1,0:T(8,128)(2,1)} collective-permute-done((bf16[256,1024]{1,0:T(8,128)(2,1)}, bf16[256,1024]{1,0:T(8,128)(2,1)}, u32[]{:S(2)}, u32[]{:S(2)}) %collective-permute-start.9) | collective-permute-done | bytes 524320 | tf_op jit(solution)/shard_map/ppermute | solution.py:41
  57.6 1.3 collective-permute-start.11
  58.9 0.8 copy.8.active_ref
  59.7 0.6 reshape.57.gain_ref
  60.3 8.5 %collective-permute-done.5.refs_9_ = bf16[256,1024]{1,0:T(8,128)(2,1)} collective-permute-done((bf16[256,1024]{1,0:T(8,128)(2,1)}, bf16[256,1024]{1,0:T(8,128)(2,1)}, u32[]{:S(2)}, u32[]{:S(2)}) %collective-permute-start.5) | collective-permute-done | bytes 524320 | tf_op jit(solution)/shard_map/ppermute | solution.py:41
  68.8 12.1 %shard_map.73 = bf16[8,128,384]{2,1,0:T(8,128)(2,1)} custom-call(s32[1]{0:T(128)} %bitcast.me_ref, f32[4,1024]{1,0:T(4,128)} %reshape.57.gain_ref, s32[256,1]{1,0:T(8,128)} %copy.8.active_ref, bf16[4096,512]{1,0:T(8,128)(2,1)} %refs_0_.3, bf16[4096,512]{1,0:T(8,128)(2,1)} %refs_1_.3, bf16[4096,512]{1,0:T(8,128)(2,1)} %refs_2_.3, ...), custom_call_target="tpu_custom_call" | custom-call | flops 3221225472 | bytes 15466496 | tf_op jit(solution)/shard_map/pallas_call | solution.py:120
  80.9 4.2 %all-to-all-start = ((bf16[8,128,384]{2,1,0:T(8,128)(2,1)}), bf16[8,128,384]{2,1,0:T(8,128)(2,1)}, u32[]{:S(2)}, u32[]{:S(2)}) async-start(bf16[8,128,384]{2,1,0:T(8,128)(2,1)} %shard_map.73), calls=%async_computation | async-start | bytes 1572864 | tf_op jit(solution)/shard_map/all_to_all | solution.py:460
  85.2 0.8 copy.9.active_ref
  86.0 12.1 %shard_map.75 = bf16[8,128,384]{2,1,0:T(8,128)(2,1)} custom-call(s32[1]{0:T(128)} %bitcast.me_ref, f32[4,1024]{1,0:T(4,128)} %reshape.57.gain_ref, s32[256,1]{1,0:T(8,128)} %copy.9.active_ref, bf16[4096,512]{1,0:T(8,128)(2,1)} %refs_0_.3, bf16[4096,512]{1,0:T(8,128)(2,1)} %refs_1_.3, bf16[4096,512]{1,0:T(8,128)(2,1)} %refs_2_.3, bf16[256,1024]{1,0:T(8,128)(2,1)} %copy-done, ...), custom_call_target="tpu_custom_call" | custom-call | flops 3221225472 | bytes 15466496 | tf_op jit(solution)/shard_map/pallas_call | solution.py:120
  98.1 4.1 %all-to-all-start.1 = ((bf16[8,128,384]{2,1,0:T(8,128)(2,1)}), bf16[8,128,384]{2,1,0:T(8,128)(2,1)S(1)}, u32[]{:S(2)}, u32[]{:S(2)}) async-start(bf16[8,128,384]{2,1,0:T(8,128)(2,1)} %shard_map.75), calls=%async_computation.1 | async-start | bytes 1572864 | tf_op jit(solution)/shard_map/all_to_all | solution.py:460
  102.4 4.0 %collective-permute-start.15 = (bf16[2,128,256]{2,1,0:T(8,128)(2,1)S(1)}, bf16[2,128,256]{2,1,0:T(8,128)(2,1)S(1)}, u32[]{:S(2)}, u32[]{:S(2)}) collective-permute-start(bf16[2,128,256]{2,1,0:T(8,128)(2,1)S(1)} %copy-done.17), channel_id=1, source_target_pairs={{0,3},{1,0},{2,1},{3,2},{4,7},{5,4},{6,5},{7,6},{8,11},{9,8},{10,9... | collective-permute-start | bytes 393224 | tf_op jit(solution)/shard_map/ppermute | solution.py:406
  106.4 4.2 %collective-permute-done.13 = bf16[2,128,256]{2,1,0:T(8,128)(2,1)S(1)} collective-permute-done((bf16[2,128,256]{2,1,0:T(8,128)(2,1)S(1)}, bf16[2,128,256]{2,1,0:T(8,128)(2,1)S(1)}, u32[]{:S(2)}, u32[]{:S(2)}) %collective-permute-start.13) | collective-permute-done | bytes 131104 | tf_op jit(solution)/shard_map/ppermute | solution.py:406
  110.5 4.7 %collective-permute-done.14 = bf16[2,128,256]{2,1,0:T(8,128)(2,1)S(1)} collective-permute-done((bf16[2,128,256]{2,1,0:T(8,128)(2,1)S(1)}, bf16[2,128,256]{2,1,0:T(8,128)(2,1)S(1)}, u32[]{:S(2)}, u32[]{:S(2)}) %collective-permute-start.14) | collective-permute-done | bytes 131104 | tf_op jit(solution)/shard_map/ppermute | solution.py:406
  115.4 2.1 collective-permute-start.18
  117.5 1.5 collective-permute-start.17
  119.0 11.3 %shard_map.76 = bf16[8,256,128]{2,1,0:T(8,128)(2,1)} custom-call(s32[1]{0:T(128)} %bitcast.6.part_ref, bf16[8,128,384]{2,1,0:T(8,128)(2,1)} %all-to-all-done.refs_0_, bf16[8,128,384]{2,1,0:T(8,128)(2,1)} %collective-permute-done.12.refs_1_, bf16[8,128,384]{2,1,0:T(8,128)(2,1)} %copy-done.7, bf16[8,128,384]{2,1,0:T(8,128)(2,1)} %collective-permute-done.16.refs_3_), custom_call_target="tpu_custom_call" | custom-call | flops 3623878656 | bytes 4194304 | tf_op jit(solution)/shard_map/pallas_call | solution.py:248
  130.3 13.1 %all_to_all.15 = bf16[8,256,128]{2,1,0:T(8,128)(2,1)S(1)} all-to-all(bf16[8,256,128]{2,1,0:T(8,128)(2,1)} %shard_map.76), channel_id=1, replica_groups=mesh['seq'=8,'tensor'=4] {'seq'}, dimensions={0} | all-to-all | bytes 1048576 | tf_op jit(solution)/shard_map/all_to_all | solution.py:496
  143.5 4.4 %collective-permute-start.19 = (bf16[4,256,128]{2,1,0:T(8,128)(2,1)S(1)}, bf16[4,256,128]{2,1,0:T(8,128)(2,1)S(1)}, u32[]{:S(2)}, u32[]{:S(2)}) collective-permute-start(bf16[4,256,128]{2,1,0:T(8,128)(2,1)S(1)} %get-tuple-element.114), channel_id=1, source_target_pairs={{0,1},{1,2},{2,3},{4,5},{5,6},{6,7},{8,9},{9,10},{10,11},{12,13},{... | collective-permute-start | bytes 786440 | tf_op jit(solution)/shard_map/ppermute | solution.py:40
  147.9 1.0 pad_maximum_fusion.1
  148.9 0.6 collective-permute-start.28
  149.6 0.6 collective-permute-start.27
  150.2 1.3 collective-permute-start.21
  151.5 4.6 %collective-permute-start.23 = (bf16[4,256,128]{2,1,0:T(8,128)(2,1)S(1)}, bf16[4,256,128]{2,1,0:T(8,128)(2,1)S(1)}, u32[]{:S(2)}, u32[]{:S(2)}) collective-permute-start(bf16[4,256,128]{2,1,0:T(8,128)(2,1)S(1)} %get-tuple-element.113), channel_id=1, source_target_pairs={{0,1},{1,2},{2,3},{4,5},{5,6},{6,7},{8,9},{9,10},{10,11},{12,13},{... | collective-permute-start | bytes 786440 | tf_op jit(solution)/shard_map/ppermute | solution.py:40
  156.1 1.3 collective-permute-start.25
  157.4 2.1 %collective-permute-done.21 = bf16[4,256,128]{2,1,0:T(8,128)(2,1)S(1)} collective-permute-done((bf16[4,256,128]{2,1,0:T(8,128)(2,1)S(1)}, bf16[4,256,128]{2,1,0:T(8,128)(2,1)S(1)}, u32[]{:S(2)}, u32[]{:S(2)}) %collective-permute-start.21) | collective-permute-done | bytes 262176 | tf_op jit(solution)/shard_map/ppermute | solution.py:41
  159.5 0.7 collective-permute-start.20
  160.1 0.3 collective-permute-done.23
  160.4 1.3 collective-permute-start.22
  161.7 4.6 %collective-permute-done.25 = bf16[4,256,128]{2,1,0:T(8,128)(2,1)S(1)} collective-permute-done((bf16[4,256,128]{2,1,0:T(8,128)(2,1)S(1)}, bf16[4,256,128]{2,1,0:T(8,128)(2,1)S(1)}, u32[]{:S(2)}, u32[]{:S(2)}) %collective-permute-start.25) | collective-permute-done | bytes 262176 | tf_op jit(solution)/shard_map/ppermute | solution.py:41
  166.3 1.4 collective-permute-start.24
  167.6 1.3 collective-permute-start.26
  169.1 1.9 collective-permute-done.22
  170.9 5.6 %collective-permute-done.26 = bf16[4,256,128]{2,1,0:T(8,128)(2,1)} collective-permute-done((bf16[4,256,128]{2,1,0:T(8,128)(2,1)S(1)}, bf16[4,256,128]{2,1,0:T(8,128)(2,1)}, u32[]{:S(2)}, u32[]{:S(2)}) %collective-permute-start.26) | collective-permute-done | bytes 262176 | tf_op jit(solution)/shard_map/ppermute | solution.py:41
  176.6 1.0 constant_dynamic-update-slice_fusion.5
  177.7 0.9 copy-done.2
  178.8 0.7 collective-permute-start.31
  179.5 1.3 collective-permute-start.32
  180.8 1.4 collective-permute-start.33
  182.2 1.5 collective-permute-start.34
  183.7 0.9 copy.10.active_ref
  184.6 0.6 stack.31.me_ref
  185.2 0.6 fusion.at_ref
  185.8 5.0 %collective-permute-done.32 = bf16[4,256,128]{2,1,0:T(8,128)(2,1)} collective-permute-done((bf16[4,256,128]{2,1,0:T(8,128)(2,1)}, bf16[4,256,128]{2,1,0:T(8,128)(2,1)}, u32[]{:S(2)}, u32[]{:S(2)}) %collective-permute-start.32) | collective-permute-done | bytes 262176 | tf_op jit(solution)/shard_map/ppermute | solution.py:41
  190.8 5.2 %collective-permute-done.34 = bf16[4,256,128]{2,1,0:T(8,128)(2,1)} collective-permute-done((bf16[4,256,128]{2,1,0:T(8,128)(2,1)}, bf16[4,256,128]{2,1,0:T(8,128)(2,1)}, u32[]{:S(2)}, u32[]{:S(2)}) %collective-permute-start.34) | collective-permute-done | bytes 262176 | tf_op jit(solution)/shard_map/ppermute | solution.py:41
  196.0 1.0 copy-done.4
  197.0 9.4 %shard_map.77 = bf16[512,1024]{1,0:T(8,128)(2,1)} custom-call(s32[5]{0:T(128)} %stack.31.me_ref, s32[16]{0:T(128)} %fusion.at_ref, s32[512,1]{1,0:T(8,128)} %copy.10.active_ref, bf16[512,1024]{1,0:T(8,128)(2,1)} %hidden_ref.1, bf16[2048,256]{1,0:T(8,128)(2,1)} %copy-done.3, bf16[2048,256]{1,0:T(8,128)(2,1)} %copy-done.2, bf16[2048,256]{1,0:T(8,128)(2,1)} %copy-done.4, ...), custom_call_target="tpu_custom_call" | custom-call | flops 2147483648 | bytes 8388608 | tf_op jit(solution)/shard_map/pallas_call | solution.py:328
  (83 shorter events, 0.8 us)
Async XLA Ops:
  0.0 47.7 %copy-start.16 = (s32[512]{0:T(512)S(1)}, s32[512]{0:T(512)}, u32[]{:S(2)}) copy-start(s32[512]{0:T(512)} %param.8) | copy-start | bytes 6148
  0.0 59.7 %copy-start.15 = (f32[4096]{0:T(1024)S(1)}, f32[4096]{0:T(1024)}, u32[]{:S(2)}) copy-start(f32[4096]{0:T(1024)} %param.9) | copy-start | bytes 49156
  1.3 7.0 %copy-start.1 = (bf16[256,1024]{1,0:T(8,128)(2,1)}, bf16[256,1024]{1,0:T(8,128)(2,1)S(1)}, u32[]{:S(2)}) copy-start(bf16[256,1024]{1,0:T(8,128)(2,1)S(1)} %get-tuple-element.108.refs_3_) | copy-start | bytes 1572868
  1.3 79.6 %copy-start = (bf16[256,1024]{1,0:T(8,128)(2,1)}, bf16[256,1024]{1,0:T(8,128)(2,1)S(1)}, u32[]{:S(2)}) copy-start(bf16[256,1024]{1,0:T(8,128)(2,1)S(1)} %get-tuple-element.62.refs_3_) | copy-start | bytes 1572868
  1.3 17.2 %collective-permute-start = (bf16[256,1024]{1,0:T(8,128)(2,1)S(1)}, bf16[256,1024]{1,0:T(8,128)(2,1)}, u32[]{:S(2)}, u32[]{:S(2)}) collective-permute-start(bf16[256,1024]{1,0:T(8,128)(2,1)S(1)} %get-tuple-element.108.refs_3_), channel_id=1, source_target_pairs={{0,1},{1,2},{2,3},{4,5},{5,6},{6,7},{8,9},{9,10},{10,11},{12,13},{... | collective-permute-start | bytes 1572872 | tf_op jit(solution)/shard_map/ppermute | solution.py:40
  7.1 16.8 %collective-permute-start.1 = (bf16[256,1024]{1,0:T(8,128)(2,1)S(1)}, bf16[256,1024]{1,0:T(8,128)(2,1)}, u32[]{:S(2)}, u32[]{:S(2)}) collective-permute-start(bf16[256,1024]{1,0:T(8,128)(2,1)S(1)} %get-tuple-element.108.refs_3_), channel_id=1, source_target_pairs={{1,0},{2,1},{3,2},{5,4},{6,5},{7,6},{9,8},{10,9},{11,10},{13,12},{... | collective-permute-start | bytes 1572872 | tf_op jit(solution)/shard_map/ppermute | solution.py:41
  8.4 20.9 %collective-permute-start.6 = (bf16[256,1024]{1,0:T(8,128)(2,1)S(1)}, bf16[256,1024]{1,0:T(8,128)(2,1)}, u32[]{:S(2)}, u32[]{:S(2)}) collective-permute-start(bf16[256,1024]{1,0:T(8,128)(2,1)S(1)} %get-tuple-element.62.refs_3_), channel_id=1, source_target_pairs={{0,1},{1,2},{2,3},{4,5},{5,6},{6,7},{8,9},{9,10},{10,11},{12,13},{... | collective-permute-start | bytes 1572872 | tf_op jit(solution)/shard_map/ppermute | solution.py:40
  13.7 21.4 %collective-permute-start.7 = (bf16[256,1024]{1,0:T(8,128)(2,1)S(1)}, bf16[256,1024]{1,0:T(8,128)(2,1)}, u32[]{:S(2)}, u32[]{:S(2)}) collective-permute-start(bf16[256,1024]{1,0:T(8,128)(2,1)S(1)} %get-tuple-element.62.refs_3_), channel_id=1, source_target_pairs={{1,0},{2,1},{3,2},{5,4},{6,5},{7,6},{9,8},{10,9},{11,10},{13,12},{... | collective-permute-start | bytes 1572872 | tf_op jit(solution)/shard_map/ppermute | solution.py:41
  18.6 19.3 %collective-permute-start.2 = (bf16[256,1024]{1,0:T(8,128)(2,1)}, bf16[256,1024]{1,0:T(8,128)(2,1)}, u32[]{:S(2)}, u32[]{:S(2)}) collective-permute-start(bf16[256,1024]{1,0:T(8,128)(2,1)} %collective-permute-done.refs_4_), channel_id=1, source_target_pairs={{1,2},{2,3},{5,6},{6,7},{9,10},{10,11},{13,14},{14,15},{17,18},{18... | collective-permute-start | bytes 1572872 | tf_op jit(solution)/shard_map/ppermute | solution.py:40
  23.9 22.5 %collective-permute-start.3 = (bf16[256,1024]{1,0:T(8,128)(2,1)}, bf16[256,1024]{1,0:T(8,128)(2,1)}, u32[]{:S(2)}, u32[]{:S(2)}) collective-permute-start(bf16[256,1024]{1,0:T(8,128)(2,1)} %collective-permute-done.1.refs_5_), channel_id=1, source_target_pairs={{1,0},{2,1},{5,4},{6,5},{9,8},{10,9},{13,12},{14,13},{17,16},{18,1... | collective-permute-start | bytes 1572872 | tf_op jit(solution)/shard_map/ppermute | solution.py:41
  35.1 12.5 %collective-permute-start.8 = (bf16[256,1024]{1,0:T(8,128)(2,1)}, bf16[256,1024]{1,0:T(8,128)(2,1)}, u32[]{:S(2)}, u32[]{:S(2)}) collective-permute-start(bf16[256,1024]{1,0:T(8,128)(2,1)} %collective-permute-done.6.refs_4_), channel_id=1, source_target_pairs={{1,2},{2,3},{5,6},{6,7},{9,10},{10,11},{13,14},{14,15},{17,18},{18... | collective-permute-start | bytes 1572872 | tf_op jit(solution)/shard_map/ppermute | solution.py:40
  36.6 21.0 %collective-permute-start.9 = (bf16[256,1024]{1,0:T(8,128)(2,1)}, bf16[256,1024]{1,0:T(8,128)(2,1)}, u32[]{:S(2)}, u32[]{:S(2)}) collective-permute-start(bf16[256,1024]{1,0:T(8,128)(2,1)} %collective-permute-done.7.refs_5_), channel_id=1, source_target_pairs={{1,0},{2,1},{5,4},{6,5},{9,8},{10,9},{13,12},{14,13},{17,16},{18,1... | collective-permute-start | bytes 1572872 | tf_op jit(solution)/shard_map/ppermute | solution.py:41
  37.9 22.4 %collective-permute-start.4 = (bf16[256,1024]{1,0:T(8,128)(2,1)}, bf16[256,1024]{1,0:T(8,128)(2,1)}, u32[]{:S(2)}, u32[]{:S(2)}) collective-permute-start(bf16[256,1024]{1,0:T(8,128)(2,1)} %collective-permute-done.2.refs_6_), channel_id=1, source_target_pairs={{2,3},{6,7},{10,11},{14,15},{18,19},{22,23},{26,27},{30,31}} | collective-permute-start | bytes 1572872 | tf_op jit(solution)/shard_map/ppermute | solution.py:40
  46.4 22.5 %collective-permute-start.5 = (bf16[256,1024]{1,0:T(8,128)(2,1)}, bf16[256,1024]{1,0:T(8,128)(2,1)}, u32[]{:S(2)}, u32[]{:S(2)}) collective-permute-start(bf16[256,1024]{1,0:T(8,128)(2,1)} %collective-permute-done.3.refs_7_), channel_id=1, source_target_pairs={{1,0},{5,4},{9,8},{13,12},{17,16},{21,20},{25,24},{29,28}} | collective-permute-start | bytes 1572872 | tf_op jit(solution)/shard_map/ppermute | solution.py:41
  47.7 33.2 %collective-permute-start.10 = (bf16[256,1024]{1,0:T(8,128)(2,1)}, bf16[256,1024]{1,0:T(8,128)(2,1)}, u32[]{:S(2)}, u32[]{:S(2)}) collective-permute-start(bf16[256,1024]{1,0:T(8,128)(2,1)} %collective-permute-done.8.refs_6_), channel_id=1, source_target_pairs={{2,3},{6,7},{10,11},{14,15},{18,19},{22,23},{26,27},{30,31}} | collective-permute-start | bytes 1572872 | tf_op jit(solution)/shard_map/ppermute | solution.py:40
  57.6 23.3 %collective-permute-start.11 = (bf16[256,1024]{1,0:T(8,128)(2,1)}, bf16[256,1024]{1,0:T(8,128)(2,1)}, u32[]{:S(2)}, u32[]{:S(2)}) collective-permute-start(bf16[256,1024]{1,0:T(8,128)(2,1)} %collective-permute-done.9.refs_7_), channel_id=1, source_target_pairs={{1,0},{5,4},{9,8},{13,12},{17,16},{21,20},{25,24},{29,28}} | collective-permute-start | bytes 1572872 | tf_op jit(solution)/shard_map/ppermute | solution.py:41
  80.9 17.2 %all-to-all-start = ((bf16[8,128,384]{2,1,0:T(8,128)(2,1)}), bf16[8,128,384]{2,1,0:T(8,128)(2,1)}, u32[]{:S(2)}, u32[]{:S(2)}) async-start(bf16[8,128,384]{2,1,0:T(8,128)(2,1)} %shard_map.73), calls=%async_computation | async-start | bytes 1572864 | tf_op jit(solution)/shard_map/all_to_all | solution.py:460
  86.0 16.3 %copy-start.19 = (bf16[2,128,256]{2,1,0:T(8,128)(2,1)S(1)}, bf16[2,128,256]{2,1,0:T(8,128)(2,1)}, u32[]{:S(2)}) copy-start(bf16[2,128,256]{2,1,0:T(8,128)(2,1)} %get-tuple-element.77) | copy-start | bytes 393220
  86.0 16.3 %copy-start.18 = (bf16[2,128,256]{2,1,0:T(8,128)(2,1)S(1)}, bf16[2,128,256]{2,1,0:T(8,128)(2,1)}, u32[]{:S(2)}) copy-start(bf16[2,128,256]{2,1,0:T(8,128)(2,1)} %get-tuple-element.78) | copy-start | bytes 393220
  86.0 16.4 %copy-start.17 = (bf16[2,128,256]{2,1,0:T(8,128)(2,1)S(1)}, bf16[2,128,256]{2,1,0:T(8,128)(2,1)}, u32[]{:S(2)}) copy-start(bf16[2,128,256]{2,1,0:T(8,128)(2,1)} %get-tuple-element.79) | copy-start | bytes 393220
  86.0 29.4 %copy-start.14 = (bf16[2,128,256]{2,1,0:T(8,128)(2,1)S(1)}, bf16[2,128,256]{2,1,0:T(8,128)(2,1)}, u32[]{:S(2)}) copy-start(bf16[2,128,256]{2,1,0:T(8,128)(2,1)} %get-tuple-element.81) | copy-start | bytes 393220
  98.1 17.1 %all-to-all-start.1 = ((bf16[8,128,384]{2,1,0:T(8,128)(2,1)}), bf16[8,128,384]{2,1,0:T(8,128)(2,1)S(1)}, u32[]{:S(2)}, u32[]{:S(2)}) async-start(bf16[8,128,384]{2,1,0:T(8,128)(2,1)} %shard_map.75), calls=%async_computation.1 | async-start | bytes 1572864 | tf_op jit(solution)/shard_map/all_to_all | solution.py:460
  102.2 8.3 %collective-permute-start.13 = (bf16[2,128,256]{2,1,0:T(8,128)(2,1)S(1)}, bf16[2,128,256]{2,1,0:T(8,128)(2,1)S(1)}, u32[]{:S(2)}, u32[]{:S(2)}) collective-permute-start(bf16[2,128,256]{2,1,0:T(8,128)(2,1)S(1)} %copy-done.19), channel_id=1, source_target_pairs={{0,1},{1,2},{2,3},{3,0},{4,5},{5,6},{6,7},{7,4},{8,9},{9,10},{10,1... | collective-permute-start | bytes 393224 | tf_op jit(solution)/shard_map/ppermute | solution.py:406
  102.3 12.9 %collective-permute-start.14 = (bf16[2,128,256]{2,1,0:T(8,128)(2,1)S(1)}, bf16[2,128,256]{2,1,0:T(8,128)(2,1)S(1)}, u32[]{:S(2)}, u32[]{:S(2)}) collective-permute-start(bf16[2,128,256]{2,1,0:T(8,128)(2,1)S(1)} %copy-done.18), channel_id=1, source_target_pairs={{0,2},{1,3},{2,0},{3,1},{4,6},{5,7},{6,4},{7,5},{8,10},{9,11},{10,... | collective-permute-start | bytes 393224 | tf_op jit(solution)/shard_map/ppermute | solution.py:406
  102.4 12.8 %collective-permute-start.15 = (bf16[2,128,256]{2,1,0:T(8,128)(2,1)S(1)}, bf16[2,128,256]{2,1,0:T(8,128)(2,1)S(1)}, u32[]{:S(2)}, u32[]{:S(2)}) collective-permute-start(bf16[2,128,256]{2,1,0:T(8,128)(2,1)S(1)} %copy-done.17), channel_id=1, source_target_pairs={{0,3},{1,0},{2,1},{3,2},{4,7},{5,4},{6,5},{7,6},{8,11},{9,8},{10,9... | collective-permute-start | bytes 393224 | tf_op jit(solution)/shard_map/ppermute | solution.py:406
  106.4 12.7 %collective-permute-start.12 = (bf16[8,128,384]{2,1,0:T(8,128)(2,1)}, bf16[8,128,384]{2,1,0:T(8,128)(2,1)}, u32[]{:S(2)}, u32[]{:S(2)}) collective-permute-start(bf16[8,128,384]{2,1,0:T(8,128)(2,1)} %all-to-all-done.refs_0_), channel_id=1, source_target_pairs={{0,4},{4,0},{8,12},{12,8},{16,20},{20,16},{24,28},{28,24},{1,5},{5... | collective-permute-start | bytes 2359304 | tf_op jit(solution)/shard_map/ppermute | solution.py:467
  115.3 2.2 %copy-start.7 = (bf16[8,128,384]{2,1,0:T(8,128)(2,1)}, bf16[8,128,384]{2,1,0:T(8,128)(2,1)S(1)}, u32[]{:S(2)}) copy-start(bf16[8,128,384]{2,1,0:T(8,128)(2,1)S(1)} %all-to-all-done.1.refs_2_) | copy-start | bytes 2359300
  115.3 3.8 %collective-permute-start.16 = (bf16[8,128,384]{2,1,0:T(8,128)(2,1)S(1)}, bf16[8,128,384]{2,1,0:T(8,128)(2,1)}, u32[]{:S(2)}, u32[]{:S(2)}) collective-permute-start(bf16[8,128,384]{2,1,0:T(8,128)(2,1)S(1)} %all-to-all-done.1.refs_2_), channel_id=1, source_target_pairs={{0,4},{4,0},{8,12},{12,8},{16,20},{20,16},{24,28},{28,24},{1,5},{5... | collective-permute-start | bytes 2359304 | tf_op jit(solution)/shard_map/ppermute | solution.py:467
  115.4 14.9 %collective-permute-start.18 = (bf16[512,256]{1,0:T(8,128)(2,1)S(1)}, bf16[512,256]{1,0:T(8,128)(2,1)}, u32[]{:S(2)}, u32[]{:S(2)}) collective-permute-start(bf16[512,256]{1,0:T(8,128)(2,1)S(1)} %pad_maximum_fusion.3), channel_id=1, source_target_pairs={{0,16},{4,20},{8,24},{12,28},{16,0},{20,4},{24,8},{28,12},{1,17},{... | collective-permute-start | bytes 786440 | tf_op jit(solution)/shard_map/ppermute | solution.py:416
  117.5 12.8 %collective-permute-start.17 = (bf16[512,256]{1,0:T(8,128)(2,1)S(1)}, bf16[512,256]{1,0:T(8,128)(2,1)S(1)}, u32[]{:S(2)}, u32[]{:S(2)}) collective-permute-start(bf16[512,256]{1,0:T(8,128)(2,1)S(1)} %pad_maximum_fusion.2), channel_id=1, source_target_pairs={{0,8},{4,12},{8,0},{12,4},{16,24},{20,28},{24,16},{28,20},{1,9},{5... | collective-permute-start | bytes 786440 | tf_op jit(solution)/shard_map/ppermute | solution.py:416
  143.5 35.2 %copy-start.5 = (bf16[4,256,128]{2,1,0:T(8,128)(2,1)}, bf16[4,256,128]{2,1,0:T(8,128)(2,1)S(1)}, u32[]{:S(2)}) copy-start(bf16[4,256,128]{2,1,0:T(8,128)(2,1)S(1)} %get-tuple-element.113) | copy-start | bytes 786436
  143.5 35.2 %copy-start.6 = (bf16[4,256,128]{2,1,0:T(8,128)(2,1)}, bf16[4,256,128]{2,1,0:T(8,128)(2,1)S(1)}, u32[]{:S(2)}) copy-start(bf16[4,256,128]{2,1,0:T(8,128)(2,1)S(1)} %get-tuple-element.114) | copy-start | bytes 786436
  143.5 12.6 %collective-permute-start.19 = (bf16[4,256,128]{2,1,0:T(8,128)(2,1)S(1)}, bf16[4,256,128]{2,1,0:T(8,128)(2,1)S(1)}, u32[]{:S(2)}, u32[]{:S(2)}) collective-permute-start(bf16[4,256,128]{2,1,0:T(8,128)(2,1)S(1)} %get-tuple-element.114), channel_id=1, source_target_pairs={{0,1},{1,2},{2,3},{4,5},{5,6},{6,7},{8,9},{9,10},{10,11},{12,13},{... | collective-permute-start | bytes 786440 | tf_op jit(solution)/shard_map/ppermute | solution.py:40
  148.9 18.7 %collective-permute-start.28 = (bf16[1024,256]{1,0:T(8,128)(2,1)S(1)}, bf16[1024,256]{1,0:T(8,128)(2,1)S(1)}, u32[]{:S(2)}, u32[]{:S(2)}) collective-permute-start(bf16[1024,256]{1,0:T(8,128)(2,1)S(1)} %pad_maximum_fusion.1), channel_id=1, source_target_pairs={{0,8},{4,12},{8,0},{12,4},{16,24},{20,28},{24,16},{28,20},{1,9},{5... | collective-permute-start | bytes 1572872 | tf_op jit(solution)/shard_map/ppermute | solution.py:416
  149.6 19.4 %collective-permute-start.27 = (bf16[1024,256]{1,0:T(8,128)(2,1)S(1)}, bf16[1024,256]{1,0:T(8,128)(2,1)S(1)}, u32[]{:S(2)}, u32[]{:S(2)}) collective-permute-start(bf16[1024,256]{1,0:T(8,128)(2,1)S(1)} %pad_maximum_fusion), channel_id=1, source_target_pairs={{0,16},{4,20},{8,24},{12,28},{16,0},{20,4},{24,8},{28,12},{1,17},{... | collective-permute-start | bytes 1572872 | tf_op jit(solution)/shard_map/ppermute | solution.py:416
  150.2 9.2 %collective-permute-start.21 = (bf16[4,256,128]{2,1,0:T(8,128)(2,1)S(1)}, bf16[4,256,128]{2,1,0:T(8,128)(2,1)S(1)}, u32[]{:S(2)}, u32[]{:S(2)}) collective-permute-start(bf16[4,256,128]{2,1,0:T(8,128)(2,1)S(1)} %get-tuple-element.114), channel_id=1, source_target_pairs={{1,0},{2,1},{3,2},{5,4},{6,5},{7,6},{9,8},{10,9},{11,10},{13,12},{... | collective-permute-start | bytes 786440 | tf_op jit(solution)/shard_map/ppermute | solution.py:41
  151.5 8.9 %collective-permute-start.23 = (bf16[4,256,128]{2,1,0:T(8,128)(2,1)S(1)}, bf16[4,256,128]{2,1,0:T(8,128)(2,1)S(1)}, u32[]{:S(2)}, u32[]{:S(2)}) collective-permute-start(bf16[4,256,128]{2,1,0:T(8,128)(2,1)S(1)} %get-tuple-element.113), channel_id=1, source_target_pairs={{0,1},{1,2},{2,3},{4,5},{5,6},{6,7},{8,9},{9,10},{10,11},{12,13},{... | collective-permute-start | bytes 786440 | tf_op jit(solution)/shard_map/ppermute | solution.py:40
  156.1 22.7 %copy-start.8 = (bf16[4,256,128]{2,1,0:T(8,128)(2,1)}, bf16[4,256,128]{2,1,0:T(8,128)(2,1)S(1)}, u32[]{:S(2)}) copy-start(bf16[4,256,128]{2,1,0:T(8,128)(2,1)S(1)} %collective-permute-done.19) | copy-start | bytes 786436
  156.1 10.2 %collective-permute-start.25 = (bf16[4,256,128]{2,1,0:T(8,128)(2,1)S(1)}, bf16[4,256,128]{2,1,0:T(8,128)(2,1)S(1)}, u32[]{:S(2)}, u32[]{:S(2)}) collective-permute-start(bf16[4,256,128]{2,1,0:T(8,128)(2,1)S(1)} %get-tuple-element.113), channel_id=1, source_target_pairs={{1,0},{2,1},{3,2},{5,4},{6,5},{7,6},{9,8},{10,9},{11,10},{13,12},{... | collective-permute-start | bytes 786440 | tf_op jit(solution)/shard_map/ppermute | solution.py:41
  159.5 20.0 %copy-start.9 = (bf16[4,256,128]{2,1,0:T(8,128)(2,1)}, bf16[4,256,128]{2,1,0:T(8,128)(2,1)S(1)}, u32[]{:S(2)}) copy-start(bf16[4,256,128]{2,1,0:T(8,128)(2,1)S(1)} %collective-permute-done.21) | copy-start | bytes 786436
  159.5 9.6 %collective-permute-start.20 = (bf16[4,256,128]{2,1,0:T(8,128)(2,1)S(1)}, bf16[4,256,128]{2,1,0:T(8,128)(2,1)S(1)}, u32[]{:S(2)}, u32[]{:S(2)}) collective-permute-start(bf16[4,256,128]{2,1,0:T(8,128)(2,1)S(1)} %collective-permute-done.19), channel_id=1, source_target_pairs={{1,2},{2,3},{5,6},{6,7},{9,10},{10,11},{13,14},{14,15},{17,18},{18... | collective-permute-start | bytes 786440 | tf_op jit(solution)/shard_map/ppermute | solution.py:40
  160.4 20.3 %copy-start.10 = (bf16[4,256,128]{2,1,0:T(8,128)(2,1)}, bf16[4,256,128]{2,1,0:T(8,128)(2,1)S(1)}, u32[]{:S(2)}) copy-start(bf16[4,256,128]{2,1,0:T(8,128)(2,1)S(1)} %collective-permute-done.23) | copy-start | bytes 786436
  160.4 10.5 %collective-permute-start.22 = (bf16[4,256,128]{2,1,0:T(8,128)(2,1)S(1)}, bf16[4,256,128]{2,1,0:T(8,128)(2,1)}, u32[]{:S(2)}, u32[]{:S(2)}) collective-permute-start(bf16[4,256,128]{2,1,0:T(8,128)(2,1)S(1)} %collective-permute-done.21), channel_id=1, source_target_pairs={{1,0},{2,1},{5,4},{6,5},{9,8},{10,9},{13,12},{14,13},{17,16},{18,1... | collective-permute-start | bytes 786440 | tf_op jit(solution)/shard_map/ppermute | solution.py:41
  166.3 15.9 %copy-start.11 = (bf16[4,256,128]{2,1,0:T(8,128)(2,1)}, bf16[4,256,128]{2,1,0:T(8,128)(2,1)S(1)}, u32[]{:S(2)}) copy-start(bf16[4,256,128]{2,1,0:T(8,128)(2,1)S(1)} %collective-permute-done.25) | copy-start | bytes 786436
  166.3 4.7 %collective-permute-start.24 = (bf16[4,256,128]{2,1,0:T(8,128)(2,1)S(1)}, bf16[4,256,128]{2,1,0:T(8,128)(2,1)}, u32[]{:S(2)}, u32[]{:S(2)}) collective-permute-start(bf16[4,256,128]{2,1,0:T(8,128)(2,1)S(1)} %collective-permute-done.23), channel_id=1, source_target_pairs={{1,2},{2,3},{5,6},{6,7},{9,10},{10,11},{13,14},{14,15},{17,18},{18... | collective-permute-start | bytes 786440 | tf_op jit(solution)/shard_map/ppermute | solution.py:40
  167.6 8.9 %collective-permute-start.26 = (bf16[4,256,128]{2,1,0:T(8,128)(2,1)S(1)}, bf16[4,256,128]{2,1,0:T(8,128)(2,1)}, u32[]{:S(2)}, u32[]{:S(2)}) collective-permute-start(bf16[4,256,128]{2,1,0:T(8,128)(2,1)S(1)} %collective-permute-done.25), channel_id=1, source_target_pairs={{1,0},{2,1},{5,4},{6,5},{9,8},{10,9},{13,12},{14,13},{17,16},{18,1... | collective-permute-start | bytes 786440 | tf_op jit(solution)/shard_map/ppermute | solution.py:41
  169.0 13.1 %copy-start.12 = (bf16[4,256,128]{2,1,0:T(8,128)(2,1)}, bf16[4,256,128]{2,1,0:T(8,128)(2,1)S(1)}, u32[]{:S(2)}) copy-start(bf16[4,256,128]{2,1,0:T(8,128)(2,1)S(1)} %collective-permute-done.20) | copy-start | bytes 786436
  177.6 1.0 copy-start.2
  177.6 18.4 %collective-permute-start.30 = (bf16[2048,256]{1,0:T(8,128)(2,1)S(1)}, bf16[2048,256]{1,0:T(8,128)(2,1)}, u32[]{:S(2)}, u32[]{:S(2)}) collective-permute-start(bf16[2048,256]{1,0:T(8,128)(2,1)S(1)} %constant_dynamic-update-slice_fusion.4.refs_1_), channel_id=1, source_target_pairs={{0,4},{4,0},{8,12},{12,8},{16,20},{20,16},{24,28},{28,24},{1,5},{5... | collective-permute-start | bytes 3145736 | tf_op jit(solution)/shard_map/ppermute | solution.py:511
  178.7 17.3 %copy-start.3 = (bf16[2048,256]{1,0:T(8,128)(2,1)}, bf16[2048,256]{1,0:T(8,128)(2,1)S(1)}, u32[]{:S(2)}) copy-start(bf16[2048,256]{1,0:T(8,128)(2,1)S(1)} %constant_dynamic-update-slice_fusion.refs_0_) | copy-start | bytes 3145732
  178.7 17.3 %collective-permute-start.29 = (bf16[2048,256]{1,0:T(8,128)(2,1)S(1)}, bf16[2048,256]{1,0:T(8,128)(2,1)S(1)}, u32[]{:S(2)}, u32[]{:S(2)}) collective-permute-start(bf16[2048,256]{1,0:T(8,128)(2,1)S(1)} %constant_dynamic-update-slice_fusion.refs_0_), channel_id=1, source_target_pairs={{0,4},{4,0},{8,12},{12,8},{16,20},{20,16},{24,28},{28,24},{1,5},{5... | collective-permute-start | bytes 3145736 | tf_op jit(solution)/shard_map/ppermute | solution.py:511
  178.8 3.4 %collective-permute-start.31 = (bf16[4,256,128]{2,1,0:T(8,128)(2,1)S(1)}, bf16[4,256,128]{2,1,0:T(8,128)(2,1)S(1)}, u32[]{:S(2)}, u32[]{:S(2)}) collective-permute-start(bf16[4,256,128]{2,1,0:T(8,128)(2,1)S(1)} %collective-permute-done.20), channel_id=1, source_target_pairs={{2,3},{6,7},{10,11},{14,15},{18,19},{22,23},{26,27},{30,31}} | collective-permute-start | bytes 786440 | tf_op jit(solution)/shard_map/ppermute | solution.py:40
  179.5 11.3 %collective-permute-start.32 = (bf16[4,256,128]{2,1,0:T(8,128)(2,1)}, bf16[4,256,128]{2,1,0:T(8,128)(2,1)}, u32[]{:S(2)}, u32[]{:S(2)}) collective-permute-start(bf16[4,256,128]{2,1,0:T(8,128)(2,1)} %collective-permute-done.22), channel_id=1, source_target_pairs={{1,0},{5,4},{9,8},{13,12},{17,16},{21,20},{25,24},{29,28}} | collective-permute-start | bytes 786440 | tf_op jit(solution)/shard_map/ppermute | solution.py:41
  180.8 10.0 %collective-permute-start.33 = (bf16[4,256,128]{2,1,0:T(8,128)(2,1)}, bf16[4,256,128]{2,1,0:T(8,128)(2,1)}, u32[]{:S(2)}, u32[]{:S(2)}) collective-permute-start(bf16[4,256,128]{2,1,0:T(8,128)(2,1)} %collective-permute-done.24), channel_id=1, source_target_pairs={{2,3},{6,7},{10,11},{14,15},{18,19},{22,23},{26,27},{30,31}} | collective-permute-start | bytes 786440 | tf_op jit(solution)/shard_map/ppermute | solution.py:40
  182.2 14.8 %copy-start.13 = (bf16[4,256,128]{2,1,0:T(8,128)(2,1)}, bf16[4,256,128]{2,1,0:T(8,128)(2,1)S(1)}, u32[]{:S(2)}) copy-start(bf16[4,256,128]{2,1,0:T(8,128)(2,1)S(1)} %collective-permute-done.31) | copy-start | bytes 786436
  182.2 13.8 %collective-permute-start.34 = (bf16[4,256,128]{2,1,0:T(8,128)(2,1)}, bf16[4,256,128]{2,1,0:T(8,128)(2,1)}, u32[]{:S(2)}, u32[]{:S(2)}) collective-permute-start(bf16[4,256,128]{2,1,0:T(8,128)(2,1)} %collective-permute-done.26), channel_id=1, source_target_pairs={{1,0},{5,4},{9,8},{13,12},{17,16},{21,20},{25,24},{29,28}} | collective-permute-start | bytes 786440 | tf_op jit(solution)/shard_map/ppermute | solution.py:41
  196.0 1.0 copy-start.4

commit v10 on v9

--- a/solution.py
+++ b/solution.py
@@ -495,25 +495,30 @@
     out, held = lax.optimization_barrier((out, held))
     home = lax.all_to_all(out, "seq", split_axis=0, concat_axis=0)
     home, held = lax.optimization_barrier((home, held))
+    weights = []
 
     def spread(step, last):
-        nonlocal held
-        if held and step == 2:
+        nonlocal held, weights
+        if held and step == 1:
             for stage in range(1, len(flips)):
                 held = swap(held, [flips[stage], flips[-1 - stage]])
             last, held = lax.optimization_barrier((last, held))
+        if held and step == 2:
+            weights = [
+                jnp.concatenate([blocks[k] for k in sorted(blocks)], axis=0) for blocks in held
+            ]
+            for turn in range(1, cuts):
+                ring = [(d, d - d % cuts + (d - turn) % cuts) for d in range(seq_count)]
+                weights += [lax.ppermute(weights[half], "seq", ring) for half in range(halves)]
+            last, weights = lax.optimization_barrier((last, weights))
         return last
 
-    found = line_gather([home[: seq_count // 2], home[seq_count // 2 :]], tensor_count, spread)
-    weights = [jnp.concatenate([blocks[k] for k in sorted(blocks)], axis=0) for blocks in held]
-    for turn in range(1, cuts):
-        ring = [(d, d - d % cuts + (d - turn) % cuts) for d in range(seq_count)]
-        weights += [lax.ppermute(weights[half], "seq", ring) for half in range(len(held))]
+    (found,) = line_gather([home], tensor_count, spread)
     if not held:
         weights = [lax.all_to_all(w_out, "tensor", split_axis=1, concat_axis=0, tiled=True)]
     cut_of, at = output_order(w_out, seq_count, tensor_count, columns)
     scalars = jnp.stack([me, *cut_of])
-    return output(scalars, at, sum(found, []), weights, hidden, active, chunks, group, 2)
+    return output(scalars, at, found, weights, hidden, active, chunks, group, 1)
 
 
 def solution(mesh):

time: 208 us -> 211 us (1.014)
  waiting for transfers between devices: 70.8 us -> 85.4 us
  starting transfers between devices: 63.1 us -> 52.5 us
    ppermute x12 -> x9, starting transfers between devices: 30 us -> 22.7 us  [line_gather(): from_left = lax.ppermute(last[at][0], 'tensor', right[step:])]
    ppermute x4, waiting for transfers between devices: 0.01 us -> 7.14 us  [swap(): lax.ppermute(jnp.concatenate(whole, axis=0) if len(whole) > 1 else whole[...]
    ppermute x12 -> x9, waiting for transfers between devices: 58 us -> 63.8 us  [line_gather(): from_right = lax.ppermute(last[at][1], 'tensor', left[:count - 1 - step])]
    ppermute x12 -> x9, starting transfers between devices: 15.6 us -> 11.8 us  [line_gather(): from_right = lax.ppermute(last[at][1], 'tensor', left[:count - 1 - step])]
    ppermute x12 -> x9, waiting for transfers between devices: 3.89 us -> 5.57 us  [line_gather(): from_left = lax.ppermute(last[at][0], 'tensor', right[step:])]
  transfers between devices with their start and end apart: 37 -> 31, of which waited for: 15 -> 14; matrix products, arithmetic and copies ran while one was open for 3% -> 2% of each run, Pallas kernels for 19% -> 19%
where the time goes in v10:
time: 211 us; the launch traced here: 210 us
  waiting for transfers between devices  85.4 us (40%)
  starting transfers between devices  52.5 us (25%)
  Pallas kernels  48.3 us (23%)
  blocking collectives  13.1 us (6%)
  local copies, waits for them, and re-layouts  7.91 us (4%)
  other arithmetic  2.3 us (1%)
    ppermute x9, waiting for transfers between devices, line_gather(): from_right = lax.ppermute(last[at][1], 'tensor', left[:count - 1 - step])  63.8 us
    pallas_call x2, Pallas kernels, project(): pl.pallas_call(partial(project_kernel, group, count), in_specs=[pl.BlockS...  24.2 us
    ppermute x9, starting transfers between devices, line_gather(): from_left = lax.ppermute(last[at][0], 'tensor', right[step:])  22.7 us
    all_to_all x1, blocking collectives, shards(): home = lax.all_to_all(out, 'seq', split_axis=0, concat_axis=0)  13.1 us
    ppermute x9, starting transfers between devices, line_gather(): from_right = lax.ppermute(last[at][1], 'tensor', left[:count - 1 - step])  11.8 us
    pallas_call x1, Pallas kernels, attend(): pl.pallas_call(partial(attend_kernel, chunks, group, rows), in_specs=[pl....  11.3 us
    pallas_call x1, Pallas kernels, output(): pl.pallas_call(partial(output_kernel, group, count, cuts, halves), in_spe...  9.39 us
    ppermute x3, waiting for transfers between devices, send_shares(): shares[step] = lax.ppermute(shares[step], 'tensor', ring)  8.88 us
  transfers between devices with their start and end apart: 31, of which 14 were waited for; matrix products, arithmetic and copies ran while one was open for 2% of the time, Pallas kernels for 19%

profile of v10, /device:TPU:0, one launch (start us, length us, event | category | flops | bytes accessed | tf_op | source)
XLA Modules:
  0.0 210.3 jit_solution(7520695995939354038)
XLA Ops:
  0.0 1.3 fusion.5
  1.3 5.8 %collective-permute-start = (bf16[256,1024]{1,0:T(8,128)(2,1)S(1)}, bf16[256,1024]{1,0:T(8,128)(2,1)}, u32[]{:S(2)}, u32[]{:S(2)}) collective-permute-start(bf16[256,1024]{1,0:T(8,128)(2,1)S(1)} %get-tuple-element.116.refs_3_), channel_id=1, source_target_pairs={{0,1},{1,2},{2,3},{4,5},{5,6},{6,7},{8,9},{9,10},{10,11},{12,13},{... | collective-permute-start | bytes 1572872 | tf_op jit(solution)/shard_map/ppermute | solution.py:40
  7.1 1.3 collective-permute-start.1
  8.4 5.4 %collective-permute-start.6 = (bf16[256,1024]{1,0:T(8,128)(2,1)S(1)}, bf16[256,1024]{1,0:T(8,128)(2,1)}, u32[]{:S(2)}, u32[]{:S(2)}) collective-permute-start(bf16[256,1024]{1,0:T(8,128)(2,1)S(1)} %get-tuple-element.66.refs_3_), channel_id=1, source_target_pairs={{0,1},{1,2},{2,3},{4,5},{5,6},{6,7},{8,9},{9,10},{10,11},{12,13},{... | collective-permute-start | bytes 1572872 | tf_op jit(solution)/shard_map/ppermute | solution.py:40
  13.7 1.3 collective-permute-start.7
  15.0 3.6 %collective-permute-done.refs_4_ = bf16[256,1024]{1,0:T(8,128)(2,1)} collective-permute-done((bf16[256,1024]{1,0:T(8,128)(2,1)S(1)}, bf16[256,1024]{1,0:T(8,128)(2,1)}, u32[]{:S(2)}, u32[]{:S(2)}) %collective-permute-start) | collective-permute-done | bytes 524320 | tf_op jit(solution)/shard_map/ppermute | solution.py:40
  18.6 1.5 collective-permute-start.2
  20.0 3.9 %collective-permute-done.1.refs_5_ = bf16[256,1024]{1,0:T(8,128)(2,1)} collective-permute-done((bf16[256,1024]{1,0:T(8,128)(2,1)S(1)}, bf16[256,1024]{1,0:T(8,128)(2,1)}, u32[]{:S(2)}, u32[]{:S(2)}) %collective-permute-start.1) | collective-permute-done | bytes 524320 | tf_op jit(solution)/shard_map/ppermute | solution.py:41
  23.9 1.3 collective-permute-start.3
  25.2 0.6 pad_add_fusion.place_ref
  25.8 3.5 %shard_map.74 = (bf16[2,128,256]{2,1,0:T(8,128)(2,1)}, bf16[2,128,256]{2,1,0:T(8,128)(2,1)}, bf16[2,128,256]{2,1,0:T(8,128)(2,1)}, bf16[2,128,256]{2,1,0:T(8,128)(2,1)}) custom-call(s32[3]{0:T(128)} %pad_add_fusion.place_ref, bf16[512,4096]{1,0:T(8,128)(2,1)} %w_ref.1), custom_call_target="tpu_custom_call" | custom-call | tf_op jit(solution)/shard_map/pallas_call | solution.py:364
  29.3 0.0 collective-permute-done.6.refs_4_
  29.3 5.9 %collective-permute-done.7.refs_5_ = bf16[256,1024]{1,0:T(8,128)(2,1)} collective-permute-done((bf16[256,1024]{1,0:T(8,128)(2,1)S(1)}, bf16[256,1024]{1,0:T(8,128)(2,1)}, u32[]{:S(2)}, u32[]{:S(2)}) %collective-permute-start.7) | collective-permute-done | bytes 524320 | tf_op jit(solution)/shard_map/ppermute | solution.py:41
  35.1 1.4 collective-permute-start.8
  36.6 1.3 collective-permute-start.9
  37.9 1.5 collective-permute-start.4
  39.3 7.0 %collective-permute-done.3.refs_7_ = bf16[256,1024]{1,0:T(8,128)(2,1)} collective-permute-done((bf16[256,1024]{1,0:T(8,128)(2,1)}, bf16[256,1024]{1,0:T(8,128)(2,1)}, u32[]{:S(2)}, u32[]{:S(2)}) %collective-permute-start.3) | collective-permute-done | bytes 524320 | tf_op jit(solution)/shard_map/ppermute | solution.py:41
  46.4 1.3 collective-permute-start.5
  47.7 1.5 collective-permute-start.10
  49.2 8.4 %collective-permute-done.9.refs_7_ = bf16[256,1024]{1,0:T(8,128)(2,1)} collective-permute-done((bf16[256,1024]{1,0:T(8,128)(2,1)}, bf16[256,1024]{1,0:T(8,128)(2,1)}, u32[]{:S(2)}, u32[]{:S(2)}) %collective-permute-start.9) | collective-permute-done | bytes 524320 | tf_op jit(solution)/shard_map/ppermute | solution.py:41
  57.6 1.3 collective-permute-start.11
  58.9 0.8 copy.8.active_ref
  59.7 0.6 reshape.36.gain_ref
  60.3 8.5 %collective-permute-done.5.refs_9_ = bf16[256,1024]{1,0:T(8,128)(2,1)} collective-permute-done((bf16[256,1024]{1,0:T(8,128)(2,1)}, bf16[256,1024]{1,0:T(8,128)(2,1)}, u32[]{:S(2)}, u32[]{:S(2)}) %collective-permute-start.5) | collective-permute-done | bytes 524320 | tf_op jit(solution)/shard_map/ppermute | solution.py:41
  68.9 12.1 %shard_map.73 = bf16[8,128,384]{2,1,0:T(8,128)(2,1)} custom-call(s32[1]{0:T(128)} %bitcast.me_ref, f32[4,1024]{1,0:T(4,128)} %reshape.36.gain_ref, s32[256,1]{1,0:T(8,128)} %copy.8.active_ref, bf16[4096,512]{1,0:T(8,128)(2,1)} %refs_0_.3, bf16[4096,512]{1,0:T(8,128)(2,1)} %refs_1_.3, bf16[4096,512]{1,0:T(8,128)(2,1)} %refs_2_.3, ...), custom_call_target="tpu_custom_call" | custom-call | flops 3221225472 | bytes 15466496 | tf_op jit(solution)/shard_map/pallas_call | solution.py:120
  81.0 4.2 %all-to-all-start = ((bf16[8,128,384]{2,1,0:T(8,128)(2,1)}), bf16[8,128,384]{2,1,0:T(8,128)(2,1)}, u32[]{:S(2)}, u32[]{:S(2)}) async-start(bf16[8,128,384]{2,1,0:T(8,128)(2,1)} %shard_map.73), calls=%async_computation | async-start | bytes 1572864 | tf_op jit(solution)/shard_map/all_to_all | solution.py:460
  85.2 0.8 copy.9.active_ref
  86.0 12.1 %shard_map.75 = bf16[8,128,384]{2,1,0:T(8,128)(2,1)} custom-call(s32[1]{0:T(128)} %bitcast.me_ref, f32[4,1024]{1,0:T(4,128)} %reshape.36.gain_ref, s32[256,1]{1,0:T(8,128)} %copy.9.active_ref, bf16[4096,512]{1,0:T(8,128)(2,1)} %refs_0_.3, bf16[4096,512]{1,0:T(8,128)(2,1)} %refs_1_.3, bf16[4096,512]{1,0:T(8,128)(2,1)} %refs_2_.3, bf16[256,1024]{1,0:T(8,128)(2,1)} %copy-done, ...), custom_call_target="tpu_custom_call" | custom-call | flops 3221225472 | bytes 15466496 | tf_op jit(solution)/shard_map/pallas_call | solution.py:120
  98.1 4.1 %all-to-all-start.1 = ((bf16[8,128,384]{2,1,0:T(8,128)(2,1)}), bf16[8,128,384]{2,1,0:T(8,128)(2,1)S(1)}, u32[]{:S(2)}, u32[]{:S(2)}) async-start(bf16[8,128,384]{2,1,0:T(8,128)(2,1)} %shard_map.75), calls=%async_computation.1 | async-start | bytes 1572864 | tf_op jit(solution)/shard_map/all_to_all | solution.py:460
  102.3 0.1 collective-permute-start.13
  102.3 0.1 collective-permute-start.14
  102.4 4.0 %collective-permute-start.15 = (bf16[2,128,256]{2,1,0:T(8,128)(2,1)S(1)}, bf16[2,128,256]{2,1,0:T(8,128)(2,1)S(1)}, u32[]{:S(2)}, u32[]{:S(2)}) collective-permute-start(bf16[2,128,256]{2,1,0:T(8,128)(2,1)S(1)} %copy-done.16), channel_id=1, source_target_pairs={{0,3},{1,0},{2,1},{3,2},{4,7},{5,4},{6,5},{7,6},{8,11},{9,8},{10,9... | collective-permute-start | bytes 393224 | tf_op jit(solution)/shard_map/ppermute | solution.py:406
  106.4 4.2 %collective-permute-done.13 = bf16[2,128,256]{2,1,0:T(8,128)(2,1)S(1)} collective-permute-done((bf16[2,128,256]{2,1,0:T(8,128)(2,1)S(1)}, bf16[2,128,256]{2,1,0:T(8,128)(2,1)S(1)}, u32[]{:S(2)}, u32[]{:S(2)}) %collective-permute-start.13) | collective-permute-done | bytes 131104 | tf_op jit(solution)/shard_map/ppermute | solution.py:406
  110.6 4.7 %collective-permute-done.14 = bf16[2,128,256]{2,1,0:T(8,128)(2,1)S(1)} collective-permute-done((bf16[2,128,256]{2,1,0:T(8,128)(2,1)S(1)}, bf16[2,128,256]{2,1,0:T(8,128)(2,1)S(1)}, u32[]{:S(2)}, u32[]{:S(2)}) %collective-permute-start.14) | collective-permute-done | bytes 131104 | tf_op jit(solution)/shard_map/ppermute | solution.py:406
  115.3 0.1 collective-permute-start.16
  115.5 2.1 collective-permute-start.18
  117.5 1.5 collective-permute-start.17
  119.1 11.3 %shard_map.76 = bf16[8,256,128]{2,1,0:T(8,128)(2,1)} custom-call(s32[1]{0:T(128)} %bitcast.6.part_ref, bf16[8,128,384]{2,1,0:T(8,128)(2,1)} %all-to-all-done.refs_0_, bf16[8,128,384]{2,1,0:T(8,128)(2,1)} %collective-permute-done.12.refs_1_, bf16[8,128,384]{2,1,0:T(8,128)(2,1)} %copy-done.7, bf16[8,128,384]{2,1,0:T(8,128)(2,1)} %collective-permute-done.16.refs_3_), custom_call_target="tpu_custom_call" | custom-call | flops 3623878656 | bytes 4194304 | tf_op jit(solution)/shard_map/pallas_call | solution.py:248
  130.3 13.1 %all_to_all.15 = bf16[8,256,128]{2,1,0:T(8,128)(2,1)S(1)} all-to-all(bf16[8,256,128]{2,1,0:T(8,128)(2,1)} %shard_map.76), channel_id=1, replica_groups=mesh['seq'=8,'tensor'=4] {'seq'}, dimensions={0} | all-to-all | bytes 1048576 | tf_op jit(solution)/shard_map/all_to_all | solution.py:496
  143.5 1.2 pad_maximum_fusion.1
  144.7 0.6 collective-permute-start.22
  145.3 0.6 collective-permute-start.21
  145.9 4.4 %collective-permute-start.19 = (bf16[8,256,128]{2,1,0:T(8,128)(2,1)S(1)}, bf16[8,256,128]{2,1,0:T(8,128)(2,1)S(1)}, u32[]{:S(2)}, u32[]{:S(2)}) collective-permute-start(bf16[8,256,128]{2,1,0:T(8,128)(2,1)S(1)} %all_to_all.15), channel_id=1, source_target_pairs={{0,1},{1,2},{2,3},{4,5},{5,6},{6,7},{8,9},{9,10},{10,11},{12,13},{... | collective-permute-start | bytes 1572872 | tf_op jit(solution)/shard_map/ppermute | solution.py:40
  150.4 1.3 collective-permute-start.20
  151.7 6.1 %collective-permute-done.22 = bf16[1024,256]{1,0:T(8,128)(2,1)S(1)} collective-permute-done((bf16[1024,256]{1,0:T(8,128)(2,1)S(1)}, bf16[1024,256]{1,0:T(8,128)(2,1)S(1)}, u32[]{:S(2)}, u32[]{:S(2)}) %collective-permute-start.22) | collective-permute-done | bytes 524320 | tf_op jit(solution)/shard_map/ppermute | solution.py:416
  157.8 1.1 collective-permute-done.21
  158.9 2.0 collective-permute-done.19
  160.9 4.1 %collective-permute-done.20 = bf16[8,256,128]{2,1,0:T(8,128)(2,1)S(1)} collective-permute-done((bf16[8,256,128]{2,1,0:T(8,128)(2,1)S(1)}, bf16[8,256,128]{2,1,0:T(8,128)(2,1)S(1)}, u32[]{:S(2)}, u32[]{:S(2)}) %collective-permute-start.20) | collective-permute-done | bytes 524320 | tf_op jit(solution)/shard_map/ppermute | solution.py:41
  165.1 1.1 constant_dynamic-update-slice_fusion.5
  166.2 0.1 collective-permute-start.26
  166.5 0.6 collective-permute-start.25
  167.0 0.2 copy-done.3
  167.2 0.7 collective-permute-start.23
  167.9 1.3 collective-permute-start.24
  169.2 14.7 %collective-permute-done.24 = bf16[8,256,128]{2,1,0:T(8,128)(2,1)S(1)} collective-permute-done((bf16[8,256,128]{2,1,0:T(8,128)(2,1)S(1)}, bf16[8,256,128]{2,1,0:T(8,128)(2,1)S(1)}, u32[]{:S(2)}, u32[]{:S(2)}) %collective-permute-start.24) | collective-permute-done | bytes 524320 | tf_op jit(solution)/shard_map/ppermute | solution.py:41
  183.9 1.0 copy-done.5
  184.9 0.7 collective-permute-start.27
  185.6 0.3 copy-done.6
  185.9 1.5 collective-permute-start.28
  187.5 0.9 copy.10.active_ref
  188.3 0.6 stack.31.me_ref
  189.0 0.5 fusion.at_ref
  189.5 11.2 %collective-permute-done.28 = bf16[8,256,128]{2,1,0:T(8,128)(2,1)} collective-permute-done((bf16[8,256,128]{2,1,0:T(8,128)(2,1)S(1)}, bf16[8,256,128]{2,1,0:T(8,128)(2,1)}, u32[]{:S(2)}, u32[]{:S(2)}) %collective-permute-start.28) | collective-permute-done | bytes 524320 | tf_op jit(solution)/shard_map/ppermute | solution.py:41
  200.7 9.4 %shard_map.77 = bf16[512,1024]{1,0:T(8,128)(2,1)} custom-call(s32[5]{0:T(128)} %stack.31.me_ref, s32[16]{0:T(128)} %fusion.at_ref, s32[512,1]{1,0:T(8,128)} %copy.10.active_ref, bf16[512,1024]{1,0:T(8,128)(2,1)} %hidden_ref.1, bf16[2048,256]{1,0:T(8,128)(2,1)} %copy-done.4, bf16[2048,256]{1,0:T(8,128)(2,1)} %copy-done.3, bf16[2048,256]{1,0:T(8,128)(2,1)} %copy-done.6, ...), custom_call_target="tpu_custom_call" | custom-call | flops 2147483648 | bytes 8388608 | tf_op jit(solution)/shard_map/pallas_call | solution.py:328
  (68 shorter events, 0.4 us)
Async XLA Ops:
  0.0 47.7 %copy-start.15 = (s32[512]{0:T(512)S(1)}, s32[512]{0:T(512)}, u32[]{:S(2)}) copy-start(s32[512]{0:T(512)} %param.8) | copy-start | bytes 6148
  0.0 59.7 %copy-start.14 = (f32[4096]{0:T(1024)S(1)}, f32[4096]{0:T(1024)}, u32[]{:S(2)}) copy-start(f32[4096]{0:T(1024)} %param.9) | copy-start | bytes 49156
  1.3 7.1 %copy-start.1 = (bf16[256,1024]{1,0:T(8,128)(2,1)}, bf16[256,1024]{1,0:T(8,128)(2,1)S(1)}, u32[]{:S(2)}) copy-start(bf16[256,1024]{1,0:T(8,128)(2,1)S(1)} %get-tuple-element.116.refs_3_) | copy-start | bytes 1572868
  1.3 79.6 %copy-start = (bf16[256,1024]{1,0:T(8,128)(2,1)}, bf16[256,1024]{1,0:T(8,128)(2,1)S(1)}, u32[]{:S(2)}) copy-start(bf16[256,1024]{1,0:T(8,128)(2,1)S(1)} %get-tuple-element.66.refs_3_) | copy-start | bytes 1572868
  1.3 17.2 %collective-permute-start = (bf16[256,1024]{1,0:T(8,128)(2,1)S(1)}, bf16[256,1024]{1,0:T(8,128)(2,1)}, u32[]{:S(2)}, u32[]{:S(2)}) collective-permute-start(bf16[256,1024]{1,0:T(8,128)(2,1)S(1)} %get-tuple-element.116.refs_3_), channel_id=1, source_target_pairs={{0,1},{1,2},{2,3},{4,5},{5,6},{6,7},{8,9},{9,10},{10,11},{12,13},{... | collective-permute-start | bytes 1572872 | tf_op jit(solution)/shard_map/ppermute | solution.py:40
  7.1 16.8 %collective-permute-start.1 = (bf16[256,1024]{1,0:T(8,128)(2,1)S(1)}, bf16[256,1024]{1,0:T(8,128)(2,1)}, u32[]{:S(2)}, u32[]{:S(2)}) collective-permute-start(bf16[256,1024]{1,0:T(8,128)(2,1)S(1)} %get-tuple-element.116.refs_3_), channel_id=1, source_target_pairs={{1,0},{2,1},{3,2},{5,4},{6,5},{7,6},{9,8},{10,9},{11,10},{13,12},{... | collective-permute-start | bytes 1572872 | tf_op jit(solution)/shard_map/ppermute | solution.py:41
  8.4 20.9 %collective-permute-start.6 = (bf16[256,1024]{1,0:T(8,128)(2,1)S(1)}, bf16[256,1024]{1,0:T(8,128)(2,1)}, u32[]{:S(2)}, u32[]{:S(2)}) collective-permute-start(bf16[256,1024]{1,0:T(8,128)(2,1)S(1)} %get-tuple-element.66.refs_3_), channel_id=1, source_target_pairs={{0,1},{1,2},{2,3},{4,5},{5,6},{6,7},{8,9},{9,10},{10,11},{12,13},{... | collective-permute-start | bytes 1572872 | tf_op jit(solution)/shard_map/ppermute | solution.py:40
  13.7 21.4 %collective-permute-start.7 = (bf16[256,1024]{1,0:T(8,128)(2,1)S(1)}, bf16[256,1024]{1,0:T(8,128)(2,1)}, u32[]{:S(2)}, u32[]{:S(2)}) collective-permute-start(bf16[256,1024]{1,0:T(8,128)(2,1)S(1)} %get-tuple-element.66.refs_3_), channel_id=1, source_target_pairs={{1,0},{2,1},{3,2},{5,4},{6,5},{7,6},{9,8},{10,9},{11,10},{13,12},{... | collective-permute-start | bytes 1572872 | tf_op jit(solution)/shard_map/ppermute | solution.py:41
  18.6 19.3 %collective-permute-start.2 = (bf16[256,1024]{1,0:T(8,128)(2,1)}, bf16[256,1024]{1,0:T(8,128)(2,1)}, u32[]{:S(2)}, u32[]{:S(2)}) collective-permute-start(bf16[256,1024]{1,0:T(8,128)(2,1)} %collective-permute-done.refs_4_), channel_id=1, source_target_pairs={{1,2},{2,3},{5,6},{6,7},{9,10},{10,11},{13,14},{14,15},{17,18},{18... | collective-permute-start | bytes 1572872 | tf_op jit(solution)/shard_map/ppermute | solution.py:40
  23.9 22.5 %collective-permute-start.3 = (bf16[256,1024]{1,0:T(8,128)(2,1)}, bf16[256,1024]{1,0:T(8,128)(2,1)}, u32[]{:S(2)}, u32[]{:S(2)}) collective-permute-start(bf16[256,1024]{1,0:T(8,128)(2,1)} %collective-permute-done.1.refs_5_), channel_id=1, source_target_pairs={{1,0},{2,1},{5,4},{6,5},{9,8},{10,9},{13,12},{14,13},{17,16},{18,1... | collective-permute-start | bytes 1572872 | tf_op jit(solution)/shard_map/ppermute | solution.py:41
  35.1 12.5 %collective-permute-start.8 = (bf16[256,1024]{1,0:T(8,128)(2,1)}, bf16[256,1024]{1,0:T(8,128)(2,1)}, u32[]{:S(2)}, u32[]{:S(2)}) collective-permute-start(bf16[256,1024]{1,0:T(8,128)(2,1)} %collective-permute-done.6.refs_4_), channel_id=1, source_target_pairs={{1,2},{2,3},{5,6},{6,7},{9,10},{10,11},{13,14},{14,15},{17,18},{18... | collective-permute-start | bytes 1572872 | tf_op jit(solution)/shard_map/ppermute | solution.py:40
  36.6 21.0 %collective-permute-start.9 = (bf16[256,1024]{1,0:T(8,128)(2,1)}, bf16[256,1024]{1,0:T(8,128)(2,1)}, u32[]{:S(2)}, u32[]{:S(2)}) collective-permute-start(bf16[256,1024]{1,0:T(8,128)(2,1)} %collective-permute-done.7.refs_5_), channel_id=1, source_target_pairs={{1,0},{2,1},{5,4},{6,5},{9,8},{10,9},{13,12},{14,13},{17,16},{18,1... | collective-permute-start | bytes 1572872 | tf_op jit(solution)/shard_map/ppermute | solution.py:41
  37.9 22.5 %collective-permute-start.4 = (bf16[256,1024]{1,0:T(8,128)(2,1)}, bf16[256,1024]{1,0:T(8,128)(2,1)}, u32[]{:S(2)}, u32[]{:S(2)}) collective-permute-start(bf16[256,1024]{1,0:T(8,128)(2,1)} %collective-permute-done.2.refs_6_), channel_id=1, source_target_pairs={{2,3},{6,7},{10,11},{14,15},{18,19},{22,23},{26,27},{30,31}} | collective-permute-start | bytes 1572872 | tf_op jit(solution)/shard_map/ppermute | solution.py:40
  46.4 22.5 %collective-permute-start.5 = (bf16[256,1024]{1,0:T(8,128)(2,1)}, bf16[256,1024]{1,0:T(8,128)(2,1)}, u32[]{:S(2)}, u32[]{:S(2)}) collective-permute-start(bf16[256,1024]{1,0:T(8,128)(2,1)} %collective-permute-done.3.refs_7_), channel_id=1, source_target_pairs={{1,0},{5,4},{9,8},{13,12},{17,16},{21,20},{25,24},{29,28}} | collective-permute-start | bytes 1572872 | tf_op jit(solution)/shard_map/ppermute | solution.py:41
  47.7 33.2 %collective-permute-start.10 = (bf16[256,1024]{1,0:T(8,128)(2,1)}, bf16[256,1024]{1,0:T(8,128)(2,1)}, u32[]{:S(2)}, u32[]{:S(2)}) collective-permute-start(bf16[256,1024]{1,0:T(8,128)(2,1)} %collective-permute-done.8.refs_6_), channel_id=1, source_target_pairs={{2,3},{6,7},{10,11},{14,15},{18,19},{22,23},{26,27},{30,31}} | collective-permute-start | bytes 1572872 | tf_op jit(solution)/shard_map/ppermute | solution.py:40
  57.6 23.3 %collective-permute-start.11 = (bf16[256,1024]{1,0:T(8,128)(2,1)}, bf16[256,1024]{1,0:T(8,128)(2,1)}, u32[]{:S(2)}, u32[]{:S(2)}) collective-permute-start(bf16[256,1024]{1,0:T(8,128)(2,1)} %collective-permute-done.9.refs_7_), channel_id=1, source_target_pairs={{1,0},{5,4},{9,8},{13,12},{17,16},{21,20},{25,24},{29,28}} | collective-permute-start | bytes 1572872 | tf_op jit(solution)/shard_map/ppermute | solution.py:41
  81.0 17.2 %all-to-all-start = ((bf16[8,128,384]{2,1,0:T(8,128)(2,1)}), bf16[8,128,384]{2,1,0:T(8,128)(2,1)}, u32[]{:S(2)}, u32[]{:S(2)}) async-start(bf16[8,128,384]{2,1,0:T(8,128)(2,1)} %shard_map.73), calls=%async_computation | async-start | bytes 1572864 | tf_op jit(solution)/shard_map/all_to_all | solution.py:460
  86.0 16.3 %copy-start.18 = (bf16[2,128,256]{2,1,0:T(8,128)(2,1)S(1)}, bf16[2,128,256]{2,1,0:T(8,128)(2,1)}, u32[]{:S(2)}) copy-start(bf16[2,128,256]{2,1,0:T(8,128)(2,1)} %get-tuple-element.81) | copy-start | bytes 393220
  86.0 16.3 %copy-start.17 = (bf16[2,128,256]{2,1,0:T(8,128)(2,1)S(1)}, bf16[2,128,256]{2,1,0:T(8,128)(2,1)}, u32[]{:S(2)}) copy-start(bf16[2,128,256]{2,1,0:T(8,128)(2,1)} %get-tuple-element.82) | copy-start | bytes 393220
  86.0 16.4 %copy-start.16 = (bf16[2,128,256]{2,1,0:T(8,128)(2,1)S(1)}, bf16[2,128,256]{2,1,0:T(8,128)(2,1)}, u32[]{:S(2)}) copy-start(bf16[2,128,256]{2,1,0:T(8,128)(2,1)} %get-tuple-element.83) | copy-start | bytes 393220
  86.0 29.4 %copy-start.13 = (bf16[2,128,256]{2,1,0:T(8,128)(2,1)S(1)}, bf16[2,128,256]{2,1,0:T(8,128)(2,1)}, u32[]{:S(2)}) copy-start(bf16[2,128,256]{2,1,0:T(8,128)(2,1)} %get-tuple-element.85) | copy-start | bytes 393220
  98.1 17.1 %all-to-all-start.1 = ((bf16[8,128,384]{2,1,0:T(8,128)(2,1)}), bf16[8,128,384]{2,1,0:T(8,128)(2,1)S(1)}, u32[]{:S(2)}, u32[]{:S(2)}) async-start(bf16[8,128,384]{2,1,0:T(8,128)(2,1)} %shard_map.75), calls=%async_computation.1 | async-start | bytes 1572864 | tf_op jit(solution)/shard_map/all_to_all | solution.py:460
  102.3 8.3 %collective-permute-start.13 = (bf16[2,128,256]{2,1,0:T(8,128)(2,1)S(1)}, bf16[2,128,256]{2,1,0:T(8,128)(2,1)S(1)}, u32[]{:S(2)}, u32[]{:S(2)}) collective-permute-start(bf16[2,128,256]{2,1,0:T(8,128)(2,1)S(1)} %copy-done.18), channel_id=1, source_target_pairs={{0,1},{1,2},{2,3},{3,0},{4,5},{5,6},{6,7},{7,4},{8,9},{9,10},{10,1... | collective-permute-start | bytes 393224 | tf_op jit(solution)/shard_map/ppermute | solution.py:406
  102.3 12.9 %collective-permute-start.14 = (bf16[2,128,256]{2,1,0:T(8,128)(2,1)S(1)}, bf16[2,128,256]{2,1,0:T(8,128)(2,1)S(1)}, u32[]{:S(2)}, u32[]{:S(2)}) collective-permute-start(bf16[2,128,256]{2,1,0:T(8,128)(2,1)S(1)} %copy-done.17), channel_id=1, source_target_pairs={{0,2},{1,3},{2,0},{3,1},{4,6},{5,7},{6,4},{7,5},{8,10},{9,11},{10,... | collective-permute-start | bytes 393224 | tf_op jit(solution)/shard_map/ppermute | solution.py:406
  102.4 12.8 %collective-permute-start.15 = (bf16[2,128,256]{2,1,0:T(8,128)(2,1)S(1)}, bf16[2,128,256]{2,1,0:T(8,128)(2,1)S(1)}, u32[]{:S(2)}, u32[]{:S(2)}) collective-permute-start(bf16[2,128,256]{2,1,0:T(8,128)(2,1)S(1)} %copy-done.16), channel_id=1, source_target_pairs={{0,3},{1,0},{2,1},{3,2},{4,7},{5,4},{6,5},{7,6},{8,11},{9,8},{10,9... | collective-permute-start | bytes 393224 | tf_op jit(solution)/shard_map/ppermute | solution.py:406
  106.4 12.7 %collective-permute-start.12 = (bf16[8,128,384]{2,1,0:T(8,128)(2,1)}, bf16[8,128,384]{2,1,0:T(8,128)(2,1)}, u32[]{:S(2)}, u32[]{:S(2)}) collective-permute-start(bf16[8,128,384]{2,1,0:T(8,128)(2,1)} %all-to-all-done.refs_0_), channel_id=1, source_target_pairs={{0,4},{4,0},{8,12},{12,8},{16,20},{20,16},{24,28},{28,24},{1,5},{5... | collective-permute-start | bytes 2359304 | tf_op jit(solution)/shard_map/ppermute | solution.py:467
  115.3 2.2 %copy-start.7 = (bf16[8,128,384]{2,1,0:T(8,128)(2,1)}, bf16[8,128,384]{2,1,0:T(8,128)(2,1)S(1)}, u32[]{:S(2)}) copy-start(bf16[8,128,384]{2,1,0:T(8,128)(2,1)S(1)} %all-to-all-done.1.refs_2_) | copy-start | bytes 2359300
  115.3 3.8 %collective-permute-start.16 = (bf16[8,128,384]{2,1,0:T(8,128)(2,1)S(1)}, bf16[8,128,384]{2,1,0:T(8,128)(2,1)}, u32[]{:S(2)}, u32[]{:S(2)}) collective-permute-start(bf16[8,128,384]{2,1,0:T(8,128)(2,1)S(1)} %all-to-all-done.1.refs_2_), channel_id=1, source_target_pairs={{0,4},{4,0},{8,12},{12,8},{16,20},{20,16},{24,28},{28,24},{1,5},{5... | collective-permute-start | bytes 2359304 | tf_op jit(solution)/shard_map/ppermute | solution.py:467
  115.5 14.9 %collective-permute-start.18 = (bf16[512,256]{1,0:T(8,128)(2,1)S(1)}, bf16[512,256]{1,0:T(8,128)(2,1)}, u32[]{:S(2)}, u32[]{:S(2)}) collective-permute-start(bf16[512,256]{1,0:T(8,128)(2,1)S(1)} %pad_maximum_fusion.3), channel_id=1, source_target_pairs={{0,16},{4,20},{8,24},{12,28},{16,0},{20,4},{24,8},{28,12},{1,17},{... | collective-permute-start | bytes 786440 | tf_op jit(solution)/shard_map/ppermute | solution.py:416
  117.5 12.8 %collective-permute-start.17 = (bf16[512,256]{1,0:T(8,128)(2,1)S(1)}, bf16[512,256]{1,0:T(8,128)(2,1)S(1)}, u32[]{:S(2)}, u32[]{:S(2)}) collective-permute-start(bf16[512,256]{1,0:T(8,128)(2,1)S(1)} %pad_maximum_fusion.2), channel_id=1, source_target_pairs={{0,8},{4,12},{8,0},{12,4},{16,24},{20,28},{24,16},{28,20},{1,9},{5... | collective-permute-start | bytes 786440 | tf_op jit(solution)/shard_map/ppermute | solution.py:416
  143.5 22.9 %copy-start.2 = (bf16[8,256,128]{2,1,0:T(8,128)(2,1)}, bf16[8,256,128]{2,1,0:T(8,128)(2,1)S(1)}, u32[]{:S(2)}) copy-start(bf16[8,256,128]{2,1,0:T(8,128)(2,1)S(1)} %all_to_all.15) | copy-start | bytes 1572868
  144.7 13.1 %collective-permute-start.22 = (bf16[1024,256]{1,0:T(8,128)(2,1)S(1)}, bf16[1024,256]{1,0:T(8,128)(2,1)S(1)}, u32[]{:S(2)}, u32[]{:S(2)}) collective-permute-start(bf16[1024,256]{1,0:T(8,128)(2,1)S(1)} %pad_maximum_fusion.1), channel_id=1, source_target_pairs={{0,8},{4,12},{8,0},{12,4},{16,24},{20,28},{24,16},{28,20},{1,9},{5... | collective-permute-start | bytes 1572872 | tf_op jit(solution)/shard_map/ppermute | solution.py:416
  145.3 13.5 %collective-permute-start.21 = (bf16[1024,256]{1,0:T(8,128)(2,1)S(1)}, bf16[1024,256]{1,0:T(8,128)(2,1)S(1)}, u32[]{:S(2)}, u32[]{:S(2)}) collective-permute-start(bf16[1024,256]{1,0:T(8,128)(2,1)S(1)} %pad_maximum_fusion), channel_id=1, source_target_pairs={{0,16},{4,20},{8,24},{12,28},{16,0},{20,4},{24,8},{28,12},{1,17},{... | collective-permute-start | bytes 1572872 | tf_op jit(solution)/shard_map/ppermute | solution.py:416
  145.9 14.9 %collective-permute-start.19 = (bf16[8,256,128]{2,1,0:T(8,128)(2,1)S(1)}, bf16[8,256,128]{2,1,0:T(8,128)(2,1)S(1)}, u32[]{:S(2)}, u32[]{:S(2)}) collective-permute-start(bf16[8,256,128]{2,1,0:T(8,128)(2,1)S(1)} %all_to_all.15), channel_id=1, source_target_pairs={{0,1},{1,2},{2,3},{4,5},{5,6},{6,7},{8,9},{9,10},{10,11},{12,13},{... | collective-permute-start | bytes 1572872 | tf_op jit(solution)/shard_map/ppermute | solution.py:40
  150.4 14.7 %collective-permute-start.20 = (bf16[8,256,128]{2,1,0:T(8,128)(2,1)S(1)}, bf16[8,256,128]{2,1,0:T(8,128)(2,1)S(1)}, u32[]{:S(2)}, u32[]{:S(2)}) collective-permute-start(bf16[8,256,128]{2,1,0:T(8,128)(2,1)S(1)} %all_to_all.15), channel_id=1, source_target_pairs={{1,0},{2,1},{3,2},{5,4},{6,5},{7,6},{9,8},{10,9},{11,10},{13,12},{... | collective-permute-start | bytes 1572872 | tf_op jit(solution)/shard_map/ppermute | solution.py:41
  160.9 26.5 %copy-start.8 = (bf16[8,256,128]{2,1,0:T(8,128)(2,1)}, bf16[8,256,128]{2,1,0:T(8,128)(2,1)S(1)}, u32[]{:S(2)}) copy-start(bf16[8,256,128]{2,1,0:T(8,128)(2,1)S(1)} %collective-permute-done.19) | copy-start | bytes 1572868
  165.0 22.4 %copy-start.9 = (bf16[8,256,128]{2,1,0:T(8,128)(2,1)}, bf16[8,256,128]{2,1,0:T(8,128)(2,1)S(1)}, u32[]{:S(2)}) copy-start(bf16[8,256,128]{2,1,0:T(8,128)(2,1)S(1)} %collective-permute-done.20) | copy-start | bytes 1572868
  166.2 1.0 copy-start.3
  166.2 17.7 %collective-permute-start.26 = (bf16[2048,256]{1,0:T(8,128)(2,1)S(1)}, bf16[2048,256]{1,0:T(8,128)(2,1)S(1)}, u32[]{:S(2)}, u32[]{:S(2)}) collective-permute-start(bf16[2048,256]{1,0:T(8,128)(2,1)S(1)} %constant_dynamic-update-slice_fusion.4.refs_1_), channel_id=1, source_target_pairs={{0,4},{4,0},{8,12},{12,8},{16,20},{20,16},{24,28},{28,24},{1,5},{5... | collective-permute-start | bytes 3145736 | tf_op jit(solution)/shard_map/ppermute | solution.py:512
  166.4 17.5 %copy-start.4 = (bf16[2048,256]{1,0:T(8,128)(2,1)}, bf16[2048,256]{1,0:T(8,128)(2,1)S(1)}, u32[]{:S(2)}) copy-start(bf16[2048,256]{1,0:T(8,128)(2,1)S(1)} %constant_dynamic-update-slice_fusion.refs_0_) | copy-start | bytes 3145732
  166.5 17.5 %collective-permute-start.25 = (bf16[2048,256]{1,0:T(8,128)(2,1)S(1)}, bf16[2048,256]{1,0:T(8,128)(2,1)S(1)}, u32[]{:S(2)}, u32[]{:S(2)}) collective-permute-start(bf16[2048,256]{1,0:T(8,128)(2,1)S(1)} %constant_dynamic-update-slice_fusion.refs_0_), channel_id=1, source_target_pairs={{0,4},{4,0},{8,12},{12,8},{16,20},{20,16},{24,28},{28,24},{1,5},{5... | collective-permute-start | bytes 3145736 | tf_op jit(solution)/shard_map/ppermute | solution.py:512
  167.2 2.0 collective-permute-start.23
  167.9 16.0 %collective-permute-start.24 = (bf16[8,256,128]{2,1,0:T(8,128)(2,1)S(1)}, bf16[8,256,128]{2,1,0:T(8,128)(2,1)S(1)}, u32[]{:S(2)}, u32[]{:S(2)}) collective-permute-start(bf16[8,256,128]{2,1,0:T(8,128)(2,1)S(1)} %collective-permute-done.20), channel_id=1, source_target_pairs={{1,0},{2,1},{5,4},{6,5},{9,8},{10,9},{13,12},{14,13},{17,16},{18,1... | collective-permute-start | bytes 1572872 | tf_op jit(solution)/shard_map/ppermute | solution.py:41
  169.2 31.5 %copy-start.10 = (bf16[8,256,128]{2,1,0:T(8,128)(2,1)}, bf16[8,256,128]{2,1,0:T(8,128)(2,1)S(1)}, u32[]{:S(2)}) copy-start(bf16[8,256,128]{2,1,0:T(8,128)(2,1)S(1)} %collective-permute-done.23) | copy-start | bytes 1572868
  183.9 5.6 %copy-start.11 = (bf16[8,256,128]{2,1,0:T(8,128)(2,1)}, bf16[8,256,128]{2,1,0:T(8,128)(2,1)S(1)}, u32[]{:S(2)}) copy-start(bf16[8,256,128]{2,1,0:T(8,128)(2,1)S(1)} %collective-permute-done.24) | copy-start | bytes 1572868
  183.9 1.0 copy-start.5
  184.9 1.0 copy-start.6
  184.9 4.5 %collective-permute-start.27 = (bf16[8,256,128]{2,1,0:T(8,128)(2,1)S(1)}, bf16[8,256,128]{2,1,0:T(8,128)(2,1)S(1)}, u32[]{:S(2)}, u32[]{:S(2)}) collective-permute-start(bf16[8,256,128]{2,1,0:T(8,128)(2,1)S(1)} %collective-permute-done.23), channel_id=1, source_target_pairs={{2,3},{6,7},{10,11},{14,15},{18,19},{22,23},{26,27},{30,31}} | collective-permute-start | bytes 1572872 | tf_op jit(solution)/shard_map/ppermute | solution.py:40
  185.9 14.8 %collective-permute-start.28 = (bf16[8,256,128]{2,1,0:T(8,128)(2,1)S(1)}, bf16[8,256,128]{2,1,0:T(8,128)(2,1)}, u32[]{:S(2)}, u32[]{:S(2)}) collective-permute-start(bf16[8,256,128]{2,1,0:T(8,128)(2,1)S(1)} %collective-permute-done.24), channel_id=1, source_target_pairs={{1,0},{5,4},{9,8},{13,12},{17,16},{21,20},{25,24},{29,28}} | collective-permute-start | bytes 1572872 | tf_op jit(solution)/shard_map/ppermute | solution.py:41
  189.5 11.2 %copy-start.12 = (bf16[8,256,128]{2,1,0:T(8,128)(2,1)}, bf16[8,256,128]{2,1,0:T(8,128)(2,1)S(1)}, u32[]{:S(2)}) copy-start(bf16[8,256,128]{2,1,0:T(8,128)(2,1)S(1)} %collective-permute-done.27) | copy-start | bytes 1572868

commit v11 on v9

--- a/solution.py
+++ b/solution.py
@@ -494,17 +494,12 @@
     out = attend(part, pieces, chunks, group, rows)
     out, held = lax.optimization_barrier((out, held))
     home = lax.all_to_all(out, "seq", split_axis=0, concat_axis=0)
+    for stage in range(1, len(flips)):
+        held = swap(held, [flips[stage], flips[-1 - stage]])
     home, held = lax.optimization_barrier((home, held))
-
-    def spread(step, last):
-        nonlocal held
-        if held and step == 2:
-            for stage in range(1, len(flips)):
-                held = swap(held, [flips[stage], flips[-1 - stage]])
-            last, held = lax.optimization_barrier((last, held))
-        return last
-
-    found = line_gather([home[: seq_count // 2], home[seq_count // 2 :]], tensor_count, spread)
+    found = line_gather(
+        [home[: seq_count // 2], home[seq_count // 2 :]], tensor_count, lambda step, last: last
+    )
     weights = [jnp.concatenate([blocks[k] for k in sorted(blocks)], axis=0) for blocks in held]
     for turn in range(1, cuts):
         ring = [(d, d - d % cuts + (d - turn) % cuts) for d in range(seq_count)]

time: 208 us -> 211 us (1.014)
  blocking collectives: 13.1 us -> 0 us
  waiting for transfers between devices: 70.8 us -> 80.2 us
  starting transfers between devices: 63.1 us -> 67.8 us
    all_to_all x1 -> x0, blocking collectives: 13.1 us -> none  [shards(): home = lax.all_to_all(out, 'seq', split_axis=0, concat_axis=0)]
    ppermute x4, waiting for transfers between devices: 0.01 us -> 11.9 us  [swap(): lax.ppermute(jnp.concatenate(whole, axis=0) if len(whole) > 1 else whole[...]
    ppermute x12, waiting for transfers between devices: 58 us -> 51.1 us  [line_gather(): from_right = lax.ppermute(last[at][1], 'tensor', left[:count - 1 - step])]
    all_to_all x0 -> x1, starting transfers between devices: none -> 3.49 us  [shards(): home = lax.all_to_all(out, 'seq', split_axis=0, concat_axis=0)]
    ppermute x12, waiting for transfers between devices: 3.89 us -> 6.46 us  [line_gather(): from_left = lax.ppermute(last[at][0], 'tensor', right[step:])]
  transfers between devices with their start and end apart: 37 -> 38, of which waited for: 15 -> 16; matrix products, arithmetic and copies ran while one was open for 3% -> 4% of each run, Pallas kernels for 19% -> 19%
where the time goes in v11:
time: 211 us; the launch traced here: 210 us
  waiting for transfers between devices  80.2 us (38%)
  starting transfers between devices  67.8 us (32%)
  Pallas kernels  48.3 us (23%)
  local copies, waits for them, and re-layouts  9.75 us (5%)
  other arithmetic  2.97 us (1%)
    ppermute x12, waiting for transfers between devices, line_gather(): from_right = lax.ppermute(last[at][1], 'tensor', left[:count - 1 - step])  51.1 us
    ppermute x12, starting transfers between devices, line_gather(): from_left = lax.ppermute(last[at][0], 'tensor', right[step:])  30.1 us
    pallas_call x2, Pallas kernels, project(): pl.pallas_call(partial(project_kernel, group, count), in_specs=[pl.BlockS...  24.2 us
    ppermute x12, starting transfers between devices, line_gather(): from_right = lax.ppermute(last[at][1], 'tensor', left[:count - 1 - step])  15.6 us
    ppermute x4, waiting for transfers between devices, swap(): lax.ppermute(jnp.concatenate(whole, axis=0) if len(whole) > 1 else whole[...  11.9 us
    pallas_call x1, Pallas kernels, attend(): pl.pallas_call(partial(attend_kernel, chunks, group, rows), in_specs=[pl....  11.2 us
    pallas_call x1, Pallas kernels, output(): pl.pallas_call(partial(output_kernel, group, count, cuts, halves), in_spe...  9.39 us
    ppermute x3, waiting for transfers between devices, send_shares(): shares[step] = lax.ppermute(shares[step], 'tensor', ring)  8.88 us
  transfers between devices with their start and end apart: 38, of which 16 were waited for; matrix products, arithmetic and copies ran while one was open for 4% of the time, Pallas kernels for 19%

profile of v11, /device:TPU:0, one launch (start us, length us, event | category | flops | bytes accessed | tf_op | source)
XLA Modules:
  0.0 209.8 jit_solution(11787526591678621861)
XLA Ops:
  0.0 1.3 fusion.5
  1.3 5.7 %collective-permute-start = (bf16[256,1024]{1,0:T(8,128)(2,1)S(1)}, bf16[256,1024]{1,0:T(8,128)(2,1)}, u32[]{:S(2)}, u32[]{:S(2)}) collective-permute-start(bf16[256,1024]{1,0:T(8,128)(2,1)S(1)} %get-tuple-element.92.refs_3_), channel_id=1, source_target_pairs={{0,1},{1,2},{2,3},{4,5},{5,6},{6,7},{8,9},{9,10},{10,11},{12,13},{... | collective-permute-start | bytes 1572872 | tf_op jit(solution)/shard_map/ppermute | solution.py:40
  7.0 1.3 collective-permute-start.1
  8.3 5.4 %collective-permute-start.6 = (bf16[256,1024]{1,0:T(8,128)(2,1)S(1)}, bf16[256,1024]{1,0:T(8,128)(2,1)}, u32[]{:S(2)}, u32[]{:S(2)}) collective-permute-start(bf16[256,1024]{1,0:T(8,128)(2,1)S(1)} %get-tuple-element.54.refs_3_), channel_id=1, source_target_pairs={{0,1},{1,2},{2,3},{4,5},{5,6},{6,7},{8,9},{9,10},{10,11},{12,13},{... | collective-permute-start | bytes 1572872 | tf_op jit(solution)/shard_map/ppermute | solution.py:40
  13.7 1.3 collective-permute-start.7
  15.0 3.6 %collective-permute-done.refs_4_ = bf16[256,1024]{1,0:T(8,128)(2,1)} collective-permute-done((bf16[256,1024]{1,0:T(8,128)(2,1)S(1)}, bf16[256,1024]{1,0:T(8,128)(2,1)}, u32[]{:S(2)}, u32[]{:S(2)}) %collective-permute-start) | collective-permute-done | bytes 524320 | tf_op jit(solution)/shard_map/ppermute | solution.py:40
  18.6 1.5 collective-permute-start.2
  20.0 3.8 %collective-permute-done.1.refs_5_ = bf16[256,1024]{1,0:T(8,128)(2,1)} collective-permute-done((bf16[256,1024]{1,0:T(8,128)(2,1)S(1)}, bf16[256,1024]{1,0:T(8,128)(2,1)}, u32[]{:S(2)}, u32[]{:S(2)}) %collective-permute-start.1) | collective-permute-done | bytes 524320 | tf_op jit(solution)/shard_map/ppermute | solution.py:41
  23.9 1.3 collective-permute-start.3
  25.8 3.4 %shard_map.74 = (bf16[2,128,256]{2,1,0:T(8,128)(2,1)}, bf16[2,128,256]{2,1,0:T(8,128)(2,1)}, bf16[2,128,256]{2,1,0:T(8,128)(2,1)}, bf16[2,128,256]{2,1,0:T(8,128)(2,1)}) custom-call(s32[3]{0:T(128)} %pad_add_fusion.place_ref, bf16[512,4096]{1,0:T(8,128)(2,1)} %w_ref.1), custom_call_target="tpu_custom_call" | custom-call | tf_op jit(solution)/shard_map/pallas_call | solution.py:364
  29.2 5.9 %collective-permute-done.7.refs_5_ = bf16[256,1024]{1,0:T(8,128)(2,1)} collective-permute-done((bf16[256,1024]{1,0:T(8,128)(2,1)S(1)}, bf16[256,1024]{1,0:T(8,128)(2,1)}, u32[]{:S(2)}, u32[]{:S(2)}) %collective-permute-start.7) | collective-permute-done | bytes 524320 | tf_op jit(solution)/shard_map/ppermute | solution.py:41
  35.1 1.5 collective-permute-start.8
  36.6 1.3 collective-permute-start.9
  37.9 1.4 collective-permute-start.4
  39.3 7.0 %collective-permute-done.3.refs_7_ = bf16[256,1024]{1,0:T(8,128)(2,1)} collective-permute-done((bf16[256,1024]{1,0:T(8,128)(2,1)}, bf16[256,1024]{1,0:T(8,128)(2,1)}, u32[]{:S(2)}, u32[]{:S(2)}) %collective-permute-start.3) | collective-permute-done | bytes 524320 | tf_op jit(solution)/shard_map/ppermute | solution.py:41
  46.4 1.3 collective-permute-start.5
  47.7 1.5 collective-permute-start.10
  49.1 8.4 %collective-permute-done.9.refs_7_ = bf16[256,1024]{1,0:T(8,128)(2,1)} collective-permute-done((bf16[256,1024]{1,0:T(8,128)(2,1)}, bf16[256,1024]{1,0:T(8,128)(2,1)}, u32[]{:S(2)}, u32[]{:S(2)}) %collective-permute-start.9) | collective-permute-done | bytes 524320 | tf_op jit(solution)/shard_map/ppermute | solution.py:41
  57.6 1.3 collective-permute-start.11
  58.9 0.8 copy.8.active_ref
  60.3 8.5 %collective-permute-done.5.refs_9_ = bf16[256,1024]{1,0:T(8,128)(2,1)} collective-permute-done((bf16[256,1024]{1,0:T(8,128)(2,1)}, bf16[256,1024]{1,0:T(8,128)(2,1)}, u32[]{:S(2)}, u32[]{:S(2)}) %collective-permute-start.5) | collective-permute-done | bytes 524320 | tf_op jit(solution)/shard_map/ppermute | solution.py:41
  68.8 12.1 %shard_map.73 = bf16[8,128,384]{2,1,0:T(8,128)(2,1)} custom-call(s32[1]{0:T(128)} %bitcast.me_ref, f32[4,1024]{1,0:T(4,128)} %reshape.57.gain_ref, s32[256,1]{1,0:T(8,128)} %copy.8.active_ref, bf16[4096,512]{1,0:T(8,128)(2,1)} %refs_0_.3, bf16[4096,512]{1,0:T(8,128)(2,1)} %refs_1_.3, bf16[4096,512]{1,0:T(8,128)(2,1)} %refs_2_.3, ...), custom_call_target="tpu_custom_call" | custom-call | flops 3221225472 | bytes 15466496 | tf_op jit(solution)/shard_map/pallas_call | solution.py:120
  80.9 4.2 %all-to-all-start = ((bf16[8,128,384]{2,1,0:T(8,128)(2,1)}), bf16[8,128,384]{2,1,0:T(8,128)(2,1)}, u32[]{:S(2)}, u32[]{:S(2)}) async-start(bf16[8,128,384]{2,1,0:T(8,128)(2,1)} %shard_map.73), calls=%async_computation | async-start | bytes 1572864 | tf_op jit(solution)/shard_map/all_to_all | solution.py:460
  85.2 0.8 copy.9.active_ref
  86.0 12.1 %shard_map.75 = bf16[8,128,384]{2,1,0:T(8,128)(2,1)} custom-call(s32[1]{0:T(128)} %bitcast.me_ref, f32[4,1024]{1,0:T(4,128)} %reshape.57.gain_ref, s32[256,1]{1,0:T(8,128)} %copy.9.active_ref, bf16[4096,512]{1,0:T(8,128)(2,1)} %refs_0_.3, bf16[4096,512]{1,0:T(8,128)(2,1)} %refs_1_.3, bf16[4096,512]{1,0:T(8,128)(2,1)} %refs_2_.3, bf16[256,1024]{1,0:T(8,128)(2,1)} %copy-done, ...), custom_call_target="tpu_custom_call" | custom-call | flops 3221225472 | bytes 15466496 | tf_op jit(solution)/shard_map/pallas_call | solution.py:120
  98.1 4.1 %all-to-all-start.1 = ((bf16[8,128,384]{2,1,0:T(8,128)(2,1)}), bf16[8,128,384]{2,1,0:T(8,128)(2,1)S(1)}, u32[]{:S(2)}, u32[]{:S(2)}) async-start(bf16[8,128,384]{2,1,0:T(8,128)(2,1)} %shard_map.75), calls=%async_computation.1 | async-start | bytes 1572864 | tf_op jit(solution)/shard_map/all_to_all | solution.py:460
  102.4 4.0 %collective-permute-start.15 = (bf16[2,128,256]{2,1,0:T(8,128)(2,1)S(1)}, bf16[2,128,256]{2,1,0:T(8,128)(2,1)S(1)}, u32[]{:S(2)}, u32[]{:S(2)}) collective-permute-start(bf16[2,128,256]{2,1,0:T(8,128)(2,1)S(1)} %copy-done.18), channel_id=1, source_target_pairs={{0,3},{1,0},{2,1},{3,2},{4,7},{5,4},{6,5},{7,6},{8,11},{9,8},{10,9... | collective-permute-start | bytes 393224 | tf_op jit(solution)/shard_map/ppermute | solution.py:406
  106.3 4.2 %collective-permute-done.13 = bf16[2,128,256]{2,1,0:T(8,128)(2,1)S(1)} collective-permute-done((bf16[2,128,256]{2,1,0:T(8,128)(2,1)S(1)}, bf16[2,128,256]{2,1,0:T(8,128)(2,1)S(1)}, u32[]{:S(2)}, u32[]{:S(2)}) %collective-permute-start.13) | collective-permute-done | bytes 131104 | tf_op jit(solution)/shard_map/ppermute | solution.py:406
  110.5 4.7 %collective-permute-done.14 = bf16[2,128,256]{2,1,0:T(8,128)(2,1)S(1)} collective-permute-done((bf16[2,128,256]{2,1,0:T(8,128)(2,1)S(1)}, bf16[2,128,256]{2,1,0:T(8,128)(2,1)S(1)}, u32[]{:S(2)}, u32[]{:S(2)}) %collective-permute-start.14) | collective-permute-done | bytes 131104 | tf_op jit(solution)/shard_map/ppermute | solution.py:406
  115.4 2.1 collective-permute-start.18
  117.5 1.5 collective-permute-start.17
  119.0 11.2 %shard_map.76 = bf16[8,256,128]{2,1,0:T(8,128)(2,1)} custom-call(s32[1]{0:T(128)} %bitcast.6.part_ref, bf16[8,128,384]{2,1,0:T(8,128)(2,1)} %all-to-all-done.refs_0_, bf16[8,128,384]{2,1,0:T(8,128)(2,1)} %collective-permute-done.12.refs_1_, bf16[8,128,384]{2,1,0:T(8,128)(2,1)} %copy-done.8, bf16[8,128,384]{2,1,0:T(8,128)(2,1)} %collective-permute-done.16.refs_3_), custom_call_target="tpu_custom_call" | custom-call | flops 3623878656 | bytes 4194304 | tf_op jit(solution)/shard_map/pallas_call | solution.py:248
  130.3 1.0 pad_maximum_fusion.1
  131.3 0.7 collective-permute-start.20
  132.0 0.8 pad_maximum_fusion
  132.8 1.5 collective-permute-start.19
  134.3 3.5 %all-to-all-start.2 = ((bf16[8,256,128]{2,1,0:T(8,128)(2,1)}), bf16[8,256,128]{2,1,0:T(8,128)(2,1)S(1)}, u32[]{:S(2)}, u32[]{:S(2)}) async-start(bf16[8,256,128]{2,1,0:T(8,128)(2,1)} %shard_map.76), calls=%async_computation.2 | async-start | bytes 1048576 | tf_op jit(solution)/shard_map/all_to_all | solution.py:496
  137.8 8.3 %collective-permute-done.20 = bf16[1024,256]{1,0:T(8,128)(2,1)S(1)} collective-permute-done((bf16[1024,256]{1,0:T(8,128)(2,1)S(1)}, bf16[1024,256]{1,0:T(8,128)(2,1)S(1)}, u32[]{:S(2)}, u32[]{:S(2)}) %collective-permute-start.20) | collective-permute-done | bytes 524320 | tf_op jit(solution)/shard_map/ppermute | solution.py:416
  146.2 3.5 %collective-permute-done.19 = bf16[1024,256]{1,0:T(8,128)(2,1)S(1)} collective-permute-done((bf16[1024,256]{1,0:T(8,128)(2,1)}, bf16[1024,256]{1,0:T(8,128)(2,1)S(1)}, u32[]{:S(2)}, u32[]{:S(2)}) %collective-permute-start.19) | collective-permute-done | bytes 524320 | tf_op jit(solution)/shard_map/ppermute | solution.py:416
  149.7 0.7 fusion.8
  150.4 1.9 all-to-all-done.2
  152.4 4.6 %collective-permute-start.23 = (bf16[4,256,128]{2,1,0:T(8,128)(2,1)S(1)}, bf16[4,256,128]{2,1,0:T(8,128)(2,1)S(1)}, u32[]{:S(2)}, u32[]{:S(2)}) collective-permute-start(bf16[4,256,128]{2,1,0:T(8,128)(2,1)S(1)} %get-tuple-element.94), channel_id=1, source_target_pairs={{0,1},{1,2},{2,3},{4,5},{5,6},{6,7},{8,9},{9,10},{10,11},{12,13},{... | collective-permute-start | bytes 786440 | tf_op jit(solution)/shard_map/ppermute | solution.py:40
  157.0 1.3 collective-permute-start.24
  158.3 1.0 constant_dynamic-update-slice_fusion.5
  159.4 4.6 %collective-permute-start.29 = (bf16[4,256,128]{2,1,0:T(8,128)(2,1)S(1)}, bf16[4,256,128]{2,1,0:T(8,128)(2,1)S(1)}, u32[]{:S(2)}, u32[]{:S(2)}) collective-permute-start(bf16[4,256,128]{2,1,0:T(8,128)(2,1)S(1)} %get-tuple-element.93), channel_id=1, source_target_pairs={{0,1},{1,2},{2,3},{4,5},{5,6},{6,7},{8,9},{9,10},{10,11},{12,13},{... | collective-permute-start | bytes 786440 | tf_op jit(solution)/shard_map/ppermute | solution.py:40
  164.1 1.0 copy-done.2
  165.4 1.3 collective-permute-start.30
  166.7 0.7 collective-permute-start.25
  167.4 2.9 %collective-permute-done.29 = bf16[4,256,128]{2,1,0:T(8,128)(2,1)S(1)} collective-permute-done((bf16[4,256,128]{2,1,0:T(8,128)(2,1)S(1)}, bf16[4,256,128]{2,1,0:T(8,128)(2,1)S(1)}, u32[]{:S(2)}, u32[]{:S(2)}) %collective-permute-start.29) | collective-permute-done | bytes 262176 | tf_op jit(solution)/shard_map/ppermute | solution.py:40
  170.2 1.3 collective-permute-start.26
  171.5 4.8 %collective-permute-done.30 = bf16[4,256,128]{2,1,0:T(8,128)(2,1)S(1)} collective-permute-done((bf16[4,256,128]{2,1,0:T(8,128)(2,1)S(1)}, bf16[4,256,128]{2,1,0:T(8,128)(2,1)S(1)}, u32[]{:S(2)}, u32[]{:S(2)}) %collective-permute-start.30) | collective-permute-done | bytes 262176 | tf_op jit(solution)/shard_map/ppermute | solution.py:41
  176.3 1.4 collective-permute-start.31
  177.7 1.3 collective-permute-start.32
  179.0 2.5 %collective-permute-done.26 = bf16[4,256,128]{2,1,0:T(8,128)(2,1)} collective-permute-done((bf16[4,256,128]{2,1,0:T(8,128)(2,1)S(1)}, bf16[4,256,128]{2,1,0:T(8,128)(2,1)}, u32[]{:S(2)}, u32[]{:S(2)}) %collective-permute-start.26) | collective-permute-done | bytes 262176 | tf_op jit(solution)/shard_map/ppermute | solution.py:41
  181.5 0.7 collective-permute-start.27
  182.2 1.3 collective-permute-start.28
  183.5 5.1 %collective-permute-done.32 = bf16[4,256,128]{2,1,0:T(8,128)(2,1)} collective-permute-done((bf16[4,256,128]{2,1,0:T(8,128)(2,1)S(1)}, bf16[4,256,128]{2,1,0:T(8,128)(2,1)}, u32[]{:S(2)}, u32[]{:S(2)}) %collective-permute-start.32) | collective-permute-done | bytes 262176 | tf_op jit(solution)/shard_map/ppermute | solution.py:41
  188.6 1.4 collective-permute-start.33
  189.9 0.7 copy-done.14
  190.7 1.5 collective-permute-start.34
  192.2 0.9 copy.10.active_ref
  194.3 5.0 %collective-permute-done.34 = bf16[4,256,128]{2,1,0:T(8,128)(2,1)} collective-permute-done((bf16[4,256,128]{2,1,0:T(8,128)(2,1)}, bf16[4,256,128]{2,1,0:T(8,128)(2,1)}, u32[]{:S(2)}, u32[]{:S(2)}) %collective-permute-start.34) | collective-permute-done | bytes 262176 | tf_op jit(solution)/shard_map/ppermute | solution.py:41
  199.2 1.0 copy-done.5
  200.2 9.4 %shard_map.77 = bf16[512,1024]{1,0:T(8,128)(2,1)} custom-call(s32[5]{0:T(128)} %stack.31.me_ref, s32[16]{0:T(128)} %fusion.at_ref, s32[512,1]{1,0:T(8,128)} %copy.10.active_ref, bf16[512,1024]{1,0:T(8,128)(2,1)} %hidden_ref.1, bf16[2048,256]{1,0:T(8,128)(2,1)} %copy-done.2, bf16[2048,256]{1,0:T(8,128)(2,1)} %copy-done.3, bf16[2048,256]{1,0:T(8,128)(2,1)} %copy-done.5, ...), custom_call_target="tpu_custom_call" | custom-call | flops 2147483648 | bytes 8388608 | tf_op jit(solution)/shard_map/pallas_call | solution.py:328
  (86 shorter events, 3.3 us)
Async XLA Ops:
  0.0 47.6 %copy-start.17 = (s32[512]{0:T(512)S(1)}, s32[512]{0:T(512)}, u32[]{:S(2)}) copy-start(s32[512]{0:T(512)} %param.8) | copy-start | bytes 6148
  0.0 59.7 %copy-start.16 = (f32[4096]{0:T(1024)S(1)}, f32[4096]{0:T(1024)}, u32[]{:S(2)}) copy-start(f32[4096]{0:T(1024)} %param.9) | copy-start | bytes 49156
  1.3 7.0 %copy-start.1 = (bf16[256,1024]{1,0:T(8,128)(2,1)}, bf16[256,1024]{1,0:T(8,128)(2,1)S(1)}, u32[]{:S(2)}) copy-start(bf16[256,1024]{1,0:T(8,128)(2,1)S(1)} %get-tuple-element.92.refs_3_) | copy-start | bytes 1572868
  1.3 79.6 %copy-start = (bf16[256,1024]{1,0:T(8,128)(2,1)}, bf16[256,1024]{1,0:T(8,128)(2,1)S(1)}, u32[]{:S(2)}) copy-start(bf16[256,1024]{1,0:T(8,128)(2,1)S(1)} %get-tuple-element.54.refs_3_) | copy-start | bytes 1572868
  1.3 17.2 %collective-permute-start = (bf16[256,1024]{1,0:T(8,128)(2,1)S(1)}, bf16[256,1024]{1,0:T(8,128)(2,1)}, u32[]{:S(2)}, u32[]{:S(2)}) collective-permute-start(bf16[256,1024]{1,0:T(8,128)(2,1)S(1)} %get-tuple-element.92.refs_3_), channel_id=1, source_target_pairs={{0,1},{1,2},{2,3},{4,5},{5,6},{6,7},{8,9},{9,10},{10,11},{12,13},{... | collective-permute-start | bytes 1572872 | tf_op jit(solution)/shard_map/ppermute | solution.py:40
  7.0 16.8 %collective-permute-start.1 = (bf16[256,1024]{1,0:T(8,128)(2,1)S(1)}, bf16[256,1024]{1,0:T(8,128)(2,1)}, u32[]{:S(2)}, u32[]{:S(2)}) collective-permute-start(bf16[256,1024]{1,0:T(8,128)(2,1)S(1)} %get-tuple-element.92.refs_3_), channel_id=1, source_target_pairs={{1,0},{2,1},{3,2},{5,4},{6,5},{7,6},{9,8},{10,9},{11,10},{13,12},{... | collective-permute-start | bytes 1572872 | tf_op jit(solution)/shard_map/ppermute | solution.py:41
  8.3 20.9 %collective-permute-start.6 = (bf16[256,1024]{1,0:T(8,128)(2,1)S(1)}, bf16[256,1024]{1,0:T(8,128)(2,1)}, u32[]{:S(2)}, u32[]{:S(2)}) collective-permute-start(bf16[256,1024]{1,0:T(8,128)(2,1)S(1)} %get-tuple-element.54.refs_3_), channel_id=1, source_target_pairs={{0,1},{1,2},{2,3},{4,5},{5,6},{6,7},{8,9},{9,10},{10,11},{12,13},{... | collective-permute-start | bytes 1572872 | tf_op jit(solution)/shard_map/ppermute | solution.py:40
  13.7 21.4 %collective-permute-start.7 = (bf16[256,1024]{1,0:T(8,128)(2,1)S(1)}, bf16[256,1024]{1,0:T(8,128)(2,1)}, u32[]{:S(2)}, u32[]{:S(2)}) collective-permute-start(bf16[256,1024]{1,0:T(8,128)(2,1)S(1)} %get-tuple-element.54.refs_3_), channel_id=1, source_target_pairs={{1,0},{2,1},{3,2},{5,4},{6,5},{7,6},{9,8},{10,9},{11,10},{13,12},{... | collective-permute-start | bytes 1572872 | tf_op jit(solution)/shard_map/ppermute | solution.py:41
  18.6 19.3 %collective-permute-start.2 = (bf16[256,1024]{1,0:T(8,128)(2,1)}, bf16[256,1024]{1,0:T(8,128)(2,1)}, u32[]{:S(2)}, u32[]{:S(2)}) collective-permute-start(bf16[256,1024]{1,0:T(8,128)(2,1)} %collective-permute-done.refs_4_), channel_id=1, source_target_pairs={{1,2},{2,3},{5,6},{6,7},{9,10},{10,11},{13,14},{14,15},{17,18},{18... | collective-permute-start | bytes 1572872 | tf_op jit(solution)/shard_map/ppermute | solution.py:40
  23.9 22.5 %collective-permute-start.3 = (bf16[256,1024]{1,0:T(8,128)(2,1)}, bf16[256,1024]{1,0:T(8,128)(2,1)}, u32[]{:S(2)}, u32[]{:S(2)}) collective-permute-start(bf16[256,1024]{1,0:T(8,128)(2,1)} %collective-permute-done.1.refs_5_), channel_id=1, source_target_pairs={{1,0},{2,1},{5,4},{6,5},{9,8},{10,9},{13,12},{14,13},{17,16},{18,1... | collective-permute-start | bytes 1572872 | tf_op jit(solution)/shard_map/ppermute | solution.py:41
  35.1 12.5 %collective-permute-start.8 = (bf16[256,1024]{1,0:T(8,128)(2,1)}, bf16[256,1024]{1,0:T(8,128)(2,1)}, u32[]{:S(2)}, u32[]{:S(2)}) collective-permute-start(bf16[256,1024]{1,0:T(8,128)(2,1)} %collective-permute-done.6.refs_4_), channel_id=1, source_target_pairs={{1,2},{2,3},{5,6},{6,7},{9,10},{10,11},{13,14},{14,15},{17,18},{18... | collective-permute-start | bytes 1572872 | tf_op jit(solution)/shard_map/ppermute | solution.py:40
  36.6 21.0 %collective-permute-start.9 = (bf16[256,1024]{1,0:T(8,128)(2,1)}, bf16[256,1024]{1,0:T(8,128)(2,1)}, u32[]{:S(2)}, u32[]{:S(2)}) collective-permute-start(bf16[256,1024]{1,0:T(8,128)(2,1)} %collective-permute-done.7.refs_5_), channel_id=1, source_target_pairs={{1,0},{2,1},{5,4},{6,5},{9,8},{10,9},{13,12},{14,13},{17,16},{18,1... | collective-permute-start | bytes 1572872 | tf_op jit(solution)/shard_map/ppermute | solution.py:41
  37.9 22.4 %collective-permute-start.4 = (bf16[256,1024]{1,0:T(8,128)(2,1)}, bf16[256,1024]{1,0:T(8,128)(2,1)}, u32[]{:S(2)}, u32[]{:S(2)}) collective-permute-start(bf16[256,1024]{1,0:T(8,128)(2,1)} %collective-permute-done.2.refs_6_), channel_id=1, source_target_pairs={{2,3},{6,7},{10,11},{14,15},{18,19},{22,23},{26,27},{30,31}} | collective-permute-start | bytes 1572872 | tf_op jit(solution)/shard_map/ppermute | solution.py:40
  46.4 22.5 %collective-permute-start.5 = (bf16[256,1024]{1,0:T(8,128)(2,1)}, bf16[256,1024]{1,0:T(8,128)(2,1)}, u32[]{:S(2)}, u32[]{:S(2)}) collective-permute-start(bf16[256,1024]{1,0:T(8,128)(2,1)} %collective-permute-done.3.refs_7_), channel_id=1, source_target_pairs={{1,0},{5,4},{9,8},{13,12},{17,16},{21,20},{25,24},{29,28}} | collective-permute-start | bytes 1572872 | tf_op jit(solution)/shard_map/ppermute | solution.py:41
  47.7 33.2 %collective-permute-start.10 = (bf16[256,1024]{1,0:T(8,128)(2,1)}, bf16[256,1024]{1,0:T(8,128)(2,1)}, u32[]{:S(2)}, u32[]{:S(2)}) collective-permute-start(bf16[256,1024]{1,0:T(8,128)(2,1)} %collective-permute-done.8.refs_6_), channel_id=1, source_target_pairs={{2,3},{6,7},{10,11},{14,15},{18,19},{22,23},{26,27},{30,31}} | collective-permute-start | bytes 1572872 | tf_op jit(solution)/shard_map/ppermute | solution.py:40
  57.6 23.3 %collective-permute-start.11 = (bf16[256,1024]{1,0:T(8,128)(2,1)}, bf16[256,1024]{1,0:T(8,128)(2,1)}, u32[]{:S(2)}, u32[]{:S(2)}) collective-permute-start(bf16[256,1024]{1,0:T(8,128)(2,1)} %collective-permute-done.9.refs_7_), channel_id=1, source_target_pairs={{1,0},{5,4},{9,8},{13,12},{17,16},{21,20},{25,24},{29,28}} | collective-permute-start | bytes 1572872 | tf_op jit(solution)/shard_map/ppermute | solution.py:41
  80.9 17.2 %all-to-all-start = ((bf16[8,128,384]{2,1,0:T(8,128)(2,1)}), bf16[8,128,384]{2,1,0:T(8,128)(2,1)}, u32[]{:S(2)}, u32[]{:S(2)}) async-start(bf16[8,128,384]{2,1,0:T(8,128)(2,1)} %shard_map.73), calls=%async_computation | async-start | bytes 1572864 | tf_op jit(solution)/shard_map/all_to_all | solution.py:460
  85.9 16.3 %copy-start.20 = (bf16[2,128,256]{2,1,0:T(8,128)(2,1)S(1)}, bf16[2,128,256]{2,1,0:T(8,128)(2,1)}, u32[]{:S(2)}) copy-start(bf16[2,128,256]{2,1,0:T(8,128)(2,1)} %get-tuple-element.69) | copy-start | bytes 393220
  85.9 16.3 %copy-start.19 = (bf16[2,128,256]{2,1,0:T(8,128)(2,1)S(1)}, bf16[2,128,256]{2,1,0:T(8,128)(2,1)}, u32[]{:S(2)}) copy-start(bf16[2,128,256]{2,1,0:T(8,128)(2,1)} %get-tuple-element.70) | copy-start | bytes 393220
  86.0 16.4 %copy-start.18 = (bf16[2,128,256]{2,1,0:T(8,128)(2,1)S(1)}, bf16[2,128,256]{2,1,0:T(8,128)(2,1)}, u32[]{:S(2)}) copy-start(bf16[2,128,256]{2,1,0:T(8,128)(2,1)} %get-tuple-element.71) | copy-start | bytes 393220
  86.0 29.4 %copy-start.15 = (bf16[2,128,256]{2,1,0:T(8,128)(2,1)S(1)}, bf16[2,128,256]{2,1,0:T(8,128)(2,1)}, u32[]{:S(2)}) copy-start(bf16[2,128,256]{2,1,0:T(8,128)(2,1)} %get-tuple-element.73) | copy-start | bytes 393220
  98.1 17.1 %all-to-all-start.1 = ((bf16[8,128,384]{2,1,0:T(8,128)(2,1)}), bf16[8,128,384]{2,1,0:T(8,128)(2,1)S(1)}, u32[]{:S(2)}, u32[]{:S(2)}) async-start(bf16[8,128,384]{2,1,0:T(8,128)(2,1)} %shard_map.75), calls=%async_computation.1 | async-start | bytes 1572864 | tf_op jit(solution)/shard_map/all_to_all | solution.py:460
  102.2 8.3 %collective-permute-start.13 = (bf16[2,128,256]{2,1,0:T(8,128)(2,1)S(1)}, bf16[2,128,256]{2,1,0:T(8,128)(2,1)S(1)}, u32[]{:S(2)}, u32[]{:S(2)}) collective-permute-start(bf16[2,128,256]{2,1,0:T(8,128)(2,1)S(1)} %copy-done.20), channel_id=1, source_target_pairs={{0,1},{1,2},{2,3},{3,0},{4,5},{5,6},{6,7},{7,4},{8,9},{9,10},{10,1... | collective-permute-start | bytes 393224 | tf_op jit(solution)/shard_map/ppermute | solution.py:406
  102.3 12.9 %collective-permute-start.14 = (bf16[2,128,256]{2,1,0:T(8,128)(2,1)S(1)}, bf16[2,128,256]{2,1,0:T(8,128)(2,1)S(1)}, u32[]{:S(2)}, u32[]{:S(2)}) collective-permute-start(bf16[2,128,256]{2,1,0:T(8,128)(2,1)S(1)} %copy-done.19), channel_id=1, source_target_pairs={{0,2},{1,3},{2,0},{3,1},{4,6},{5,7},{6,4},{7,5},{8,10},{9,11},{10,... | collective-permute-start | bytes 393224 | tf_op jit(solution)/shard_map/ppermute | solution.py:406
  102.4 12.8 %collective-permute-start.15 = (bf16[2,128,256]{2,1,0:T(8,128)(2,1)S(1)}, bf16[2,128,256]{2,1,0:T(8,128)(2,1)S(1)}, u32[]{:S(2)}, u32[]{:S(2)}) collective-permute-start(bf16[2,128,256]{2,1,0:T(8,128)(2,1)S(1)} %copy-done.18), channel_id=1, source_target_pairs={{0,3},{1,0},{2,1},{3,2},{4,7},{5,4},{6,5},{7,6},{8,11},{9,8},{10,9... | collective-permute-start | bytes 393224 | tf_op jit(solution)/shard_map/ppermute | solution.py:406
  106.3 12.7 %collective-permute-start.12 = (bf16[8,128,384]{2,1,0:T(8,128)(2,1)}, bf16[8,128,384]{2,1,0:T(8,128)(2,1)}, u32[]{:S(2)}, u32[]{:S(2)}) collective-permute-start(bf16[8,128,384]{2,1,0:T(8,128)(2,1)} %all-to-all-done.refs_0_), channel_id=1, source_target_pairs={{0,4},{4,0},{8,12},{12,8},{16,20},{20,16},{24,28},{28,24},{1,5},{5... | collective-permute-start | bytes 2359304 | tf_op jit(solution)/shard_map/ppermute | solution.py:467
  115.2 2.2 %copy-start.8 = (bf16[8,128,384]{2,1,0:T(8,128)(2,1)}, bf16[8,128,384]{2,1,0:T(8,128)(2,1)S(1)}, u32[]{:S(2)}) copy-start(bf16[8,128,384]{2,1,0:T(8,128)(2,1)S(1)} %all-to-all-done.1.refs_2_) | copy-start | bytes 2359300
  115.2 3.8 %collective-permute-start.16 = (bf16[8,128,384]{2,1,0:T(8,128)(2,1)S(1)}, bf16[8,128,384]{2,1,0:T(8,128)(2,1)}, u32[]{:S(2)}, u32[]{:S(2)}) collective-permute-start(bf16[8,128,384]{2,1,0:T(8,128)(2,1)S(1)} %all-to-all-done.1.refs_2_), channel_id=1, source_target_pairs={{0,4},{4,0},{8,12},{12,8},{16,20},{20,16},{24,28},{28,24},{1,5},{5... | collective-permute-start | bytes 2359304 | tf_op jit(solution)/shard_map/ppermute | solution.py:467
  115.4 14.9 %collective-permute-start.18 = (bf16[512,256]{1,0:T(8,128)(2,1)S(1)}, bf16[512,256]{1,0:T(8,128)(2,1)}, u32[]{:S(2)}, u32[]{:S(2)}) collective-permute-start(bf16[512,256]{1,0:T(8,128)(2,1)S(1)} %pad_maximum_fusion.3), channel_id=1, source_target_pairs={{0,16},{4,20},{8,24},{12,28},{16,0},{20,4},{24,8},{28,12},{1,17},{... | collective-permute-start | bytes 786440 | tf_op jit(solution)/shard_map/ppermute | solution.py:416
  117.5 12.8 %collective-permute-start.17 = (bf16[512,256]{1,0:T(8,128)(2,1)S(1)}, bf16[512,256]{1,0:T(8,128)(2,1)S(1)}, u32[]{:S(2)}, u32[]{:S(2)}) collective-permute-start(bf16[512,256]{1,0:T(8,128)(2,1)S(1)} %pad_maximum_fusion.2), channel_id=1, source_target_pairs={{0,8},{4,12},{8,0},{12,4},{16,24},{20,28},{24,16},{28,20},{1,9},{5... | collective-permute-start | bytes 786440 | tf_op jit(solution)/shard_map/ppermute | solution.py:416
  131.3 14.9 %collective-permute-start.20 = (bf16[1024,256]{1,0:T(8,128)(2,1)S(1)}, bf16[1024,256]{1,0:T(8,128)(2,1)S(1)}, u32[]{:S(2)}, u32[]{:S(2)}) collective-permute-start(bf16[1024,256]{1,0:T(8,128)(2,1)S(1)} %pad_maximum_fusion.1), channel_id=1, source_target_pairs={{0,8},{4,12},{8,0},{12,4},{16,24},{20,28},{24,16},{28,20},{1,9},{5... | collective-permute-start | bytes 1572872 | tf_op jit(solution)/shard_map/ppermute | solution.py:416
  132.8 16.9 %collective-permute-start.19 = (bf16[1024,256]{1,0:T(8,128)(2,1)}, bf16[1024,256]{1,0:T(8,128)(2,1)S(1)}, u32[]{:S(2)}, u32[]{:S(2)}) collective-permute-start(bf16[1024,256]{1,0:T(8,128)(2,1)} %pad_maximum_fusion), channel_id=1, source_target_pairs={{0,16},{4,20},{8,24},{12,28},{16,0},{20,4},{24,8},{28,12},{1,17},{... | collective-permute-start | bytes 1572872 | tf_op jit(solution)/shard_map/ppermute | solution.py:416
  134.3 18.0 %all-to-all-start.2 = ((bf16[8,256,128]{2,1,0:T(8,128)(2,1)}), bf16[8,256,128]{2,1,0:T(8,128)(2,1)S(1)}, u32[]{:S(2)}, u32[]{:S(2)}) async-start(bf16[8,256,128]{2,1,0:T(8,128)(2,1)} %shard_map.76), calls=%async_computation.2 | async-start | bytes 1048576 | tf_op jit(solution)/shard_map/all_to_all | solution.py:496
  152.3 11.7 %copy-start.4 = (bf16[512,256]{1,0:T(8,128)(2,1)S(1)}, bf16[512,256]{1,0:T(8,128)(2,1)}, u32[]{:S(2)}) copy-start(bf16[512,256]{1,0:T(8,128)(2,1)} %get-tuple-element.84) | copy-start | bytes 786436
  152.4 13.0 %copy-start.6 = (bf16[4,256,128]{2,1,0:T(8,128)(2,1)}, bf16[4,256,128]{2,1,0:T(8,128)(2,1)S(1)}, u32[]{:S(2)}) copy-start(bf16[4,256,128]{2,1,0:T(8,128)(2,1)S(1)} %get-tuple-element.93) | copy-start | bytes 786436
  152.4 23.9 %copy-start.7 = (bf16[4,256,128]{2,1,0:T(8,128)(2,1)}, bf16[4,256,128]{2,1,0:T(8,128)(2,1)S(1)}, u32[]{:S(2)}) copy-start(bf16[4,256,128]{2,1,0:T(8,128)(2,1)S(1)} %get-tuple-element.94) | copy-start | bytes 786436
  152.4 12.9 %collective-permute-start.23 = (bf16[4,256,128]{2,1,0:T(8,128)(2,1)S(1)}, bf16[4,256,128]{2,1,0:T(8,128)(2,1)S(1)}, u32[]{:S(2)}, u32[]{:S(2)}) collective-permute-start(bf16[4,256,128]{2,1,0:T(8,128)(2,1)S(1)} %get-tuple-element.94), channel_id=1, source_target_pairs={{0,1},{1,2},{2,3},{4,5},{5,6},{6,7},{8,9},{9,10},{10,11},{12,13},{... | collective-permute-start | bytes 786440 | tf_op jit(solution)/shard_map/ppermute | solution.py:40
  157.0 9.7 %collective-permute-start.24 = (bf16[4,256,128]{2,1,0:T(8,128)(2,1)S(1)}, bf16[4,256,128]{2,1,0:T(8,128)(2,1)S(1)}, u32[]{:S(2)}, u32[]{:S(2)}) collective-permute-start(bf16[4,256,128]{2,1,0:T(8,128)(2,1)S(1)} %get-tuple-element.94), channel_id=1, source_target_pairs={{1,0},{2,1},{3,2},{5,4},{6,5},{7,6},{9,8},{10,9},{11,10},{13,12},{... | collective-permute-start | bytes 786440 | tf_op jit(solution)/shard_map/ppermute | solution.py:41
  159.3 39.9 %copy-start.3 = (bf16[2048,256]{1,0:T(8,128)(2,1)}, bf16[2048,256]{1,0:T(8,128)(2,1)S(1)}, u32[]{:S(2)}) copy-start(bf16[2048,256]{1,0:T(8,128)(2,1)S(1)} %constant_dynamic-update-slice_fusion.4.refs_1_) | copy-start | bytes 3145732
  159.3 39.9 %collective-permute-start.22 = (bf16[2048,256]{1,0:T(8,128)(2,1)S(1)}, bf16[2048,256]{1,0:T(8,128)(2,1)}, u32[]{:S(2)}, u32[]{:S(2)}) collective-permute-start(bf16[2048,256]{1,0:T(8,128)(2,1)S(1)} %constant_dynamic-update-slice_fusion.4.refs_1_), channel_id=1, source_target_pairs={{0,4},{4,0},{8,12},{12,8},{16,20},{20,16},{24,28},{28,24},{1,5},{5... | collective-permute-start | bytes 3145736 | tf_op jit(solution)/shard_map/ppermute | solution.py:506
  159.4 10.8 %collective-permute-start.29 = (bf16[4,256,128]{2,1,0:T(8,128)(2,1)S(1)}, bf16[4,256,128]{2,1,0:T(8,128)(2,1)S(1)}, u32[]{:S(2)}, u32[]{:S(2)}) collective-permute-start(bf16[4,256,128]{2,1,0:T(8,128)(2,1)S(1)} %get-tuple-element.93), channel_id=1, source_target_pairs={{0,1},{1,2},{2,3},{4,5},{5,6},{6,7},{8,9},{9,10},{10,11},{12,13},{... | collective-permute-start | bytes 786440 | tf_op jit(solution)/shard_map/ppermute | solution.py:40
  164.1 1.0 copy-start.2
  165.1 34.1 %collective-permute-start.21 = (bf16[2048,256]{1,0:T(8,128)(2,1)S(1)}, bf16[2048,256]{1,0:T(8,128)(2,1)S(1)}, u32[]{:S(2)}, u32[]{:S(2)}) collective-permute-start(bf16[2048,256]{1,0:T(8,128)(2,1)S(1)} %constant_dynamic-update-slice_fusion.refs_0_), channel_id=1, source_target_pairs={{0,4},{4,0},{8,12},{12,8},{16,20},{20,16},{24,28},{28,24},{1,5},{5... | collective-permute-start | bytes 3145736 | tf_op jit(solution)/shard_map/ppermute | solution.py:506
  165.4 12.3 %copy-start.9 = (bf16[4,256,128]{2,1,0:T(8,128)(2,1)}, bf16[4,256,128]{2,1,0:T(8,128)(2,1)S(1)}, u32[]{:S(2)}) copy-start(bf16[4,256,128]{2,1,0:T(8,128)(2,1)S(1)} %collective-permute-done.23) | copy-start | bytes 786436
  165.4 10.9 %collective-permute-start.30 = (bf16[4,256,128]{2,1,0:T(8,128)(2,1)S(1)}, bf16[4,256,128]{2,1,0:T(8,128)(2,1)S(1)}, u32[]{:S(2)}, u32[]{:S(2)}) collective-permute-start(bf16[4,256,128]{2,1,0:T(8,128)(2,1)S(1)} %get-tuple-element.93), channel_id=1, source_target_pairs={{1,0},{2,1},{3,2},{5,4},{6,5},{7,6},{9,8},{10,9},{11,10},{13,12},{... | collective-permute-start | bytes 786440 | tf_op jit(solution)/shard_map/ppermute | solution.py:41
  166.7 11.0 %copy-start.10 = (bf16[4,256,128]{2,1,0:T(8,128)(2,1)}, bf16[4,256,128]{2,1,0:T(8,128)(2,1)S(1)}, u32[]{:S(2)}) copy-start(bf16[4,256,128]{2,1,0:T(8,128)(2,1)S(1)} %collective-permute-done.24) | copy-start | bytes 786436
  166.7 11.0 %collective-permute-start.25 = (bf16[4,256,128]{2,1,0:T(8,128)(2,1)S(1)}, bf16[4,256,128]{2,1,0:T(8,128)(2,1)S(1)}, u32[]{:S(2)}, u32[]{:S(2)}) collective-permute-start(bf16[4,256,128]{2,1,0:T(8,128)(2,1)S(1)} %collective-permute-done.23), channel_id=1, source_target_pairs={{1,2},{2,3},{5,6},{6,7},{9,10},{10,11},{13,14},{14,15},{17,18},{18... | collective-permute-start | bytes 786440 | tf_op jit(solution)/shard_map/ppermute | solution.py:40
  170.2 30.0 %copy-start.11 = (bf16[4,256,128]{2,1,0:T(8,128)(2,1)}, bf16[4,256,128]{2,1,0:T(8,128)(2,1)S(1)}, u32[]{:S(2)}) copy-start(bf16[4,256,128]{2,1,0:T(8,128)(2,1)S(1)} %collective-permute-done.29) | copy-start | bytes 786436
  170.2 11.3 %collective-permute-start.26 = (bf16[4,256,128]{2,1,0:T(8,128)(2,1)S(1)}, bf16[4,256,128]{2,1,0:T(8,128)(2,1)}, u32[]{:S(2)}, u32[]{:S(2)}) collective-permute-start(bf16[4,256,128]{2,1,0:T(8,128)(2,1)S(1)} %collective-permute-done.24), channel_id=1, source_target_pairs={{1,0},{2,1},{5,4},{6,5},{9,8},{10,9},{13,12},{14,13},{17,16},{18,1... | collective-permute-start | bytes 786440 | tf_op jit(solution)/shard_map/ppermute | solution.py:41
  176.3 5.9 %copy-start.12 = (bf16[4,256,128]{2,1,0:T(8,128)(2,1)}, bf16[4,256,128]{2,1,0:T(8,128)(2,1)S(1)}, u32[]{:S(2)}) copy-start(bf16[4,256,128]{2,1,0:T(8,128)(2,1)S(1)} %collective-permute-done.30) | copy-start | bytes 786436
  176.3 5.9 %collective-permute-start.31 = (bf16[4,256,128]{2,1,0:T(8,128)(2,1)S(1)}, bf16[4,256,128]{2,1,0:T(8,128)(2,1)}, u32[]{:S(2)}, u32[]{:S(2)}) collective-permute-start(bf16[4,256,128]{2,1,0:T(8,128)(2,1)S(1)} %collective-permute-done.29), channel_id=1, source_target_pairs={{1,2},{2,3},{5,6},{6,7},{9,10},{10,11},{13,14},{14,15},{17,18},{18... | collective-permute-start | bytes 786440 | tf_op jit(solution)/shard_map/ppermute | solution.py:40
  177.7 10.9 %copy-start.13 = (bf16[4,256,128]{2,1,0:T(8,128)(2,1)}, bf16[4,256,128]{2,1,0:T(8,128)(2,1)S(1)}, u32[]{:S(2)}) copy-start(bf16[4,256,128]{2,1,0:T(8,128)(2,1)S(1)} %collective-permute-done.25) | copy-start | bytes 786436
  177.7 10.9 %collective-permute-start.32 = (bf16[4,256,128]{2,1,0:T(8,128)(2,1)S(1)}, bf16[4,256,128]{2,1,0:T(8,128)(2,1)}, u32[]{:S(2)}, u32[]{:S(2)}) collective-permute-start(bf16[4,256,128]{2,1,0:T(8,128)(2,1)S(1)} %collective-permute-done.30), channel_id=1, source_target_pairs={{1,0},{2,1},{5,4},{6,5},{9,8},{10,9},{13,12},{14,13},{17,16},{18,1... | collective-permute-start | bytes 786440 | tf_op jit(solution)/shard_map/ppermute | solution.py:41
  181.5 8.5 %collective-permute-start.27 = (bf16[4,256,128]{2,1,0:T(8,128)(2,1)S(1)}, bf16[4,256,128]{2,1,0:T(8,128)(2,1)S(1)}, u32[]{:S(2)}, u32[]{:S(2)}) collective-permute-start(bf16[4,256,128]{2,1,0:T(8,128)(2,1)S(1)} %collective-permute-done.25), channel_id=1, source_target_pairs={{2,3},{6,7},{10,11},{14,15},{18,19},{22,23},{26,27},{30,31}} | collective-permute-start | bytes 786440 | tf_op jit(solution)/shard_map/ppermute | solution.py:40
  182.2 12.1 %collective-permute-start.28 = (bf16[4,256,128]{2,1,0:T(8,128)(2,1)}, bf16[4,256,128]{2,1,0:T(8,128)(2,1)}, u32[]{:S(2)}, u32[]{:S(2)}) collective-permute-start(bf16[4,256,128]{2,1,0:T(8,128)(2,1)} %collective-permute-done.26), channel_id=1, source_target_pairs={{1,0},{5,4},{9,8},{13,12},{17,16},{21,20},{25,24},{29,28}} | collective-permute-start | bytes 786440 | tf_op jit(solution)/shard_map/ppermute | solution.py:41
  188.6 5.7 %collective-permute-start.33 = (bf16[4,256,128]{2,1,0:T(8,128)(2,1)}, bf16[4,256,128]{2,1,0:T(8,128)(2,1)}, u32[]{:S(2)}, u32[]{:S(2)}) collective-permute-start(bf16[4,256,128]{2,1,0:T(8,128)(2,1)} %collective-permute-done.31), channel_id=1, source_target_pairs={{2,3},{6,7},{10,11},{14,15},{18,19},{22,23},{26,27},{30,31}} | collective-permute-start | bytes 786440 | tf_op jit(solution)/shard_map/ppermute | solution.py:40
  189.9 0.7 copy-start.14
  190.7 8.6 %collective-permute-start.34 = (bf16[4,256,128]{2,1,0:T(8,128)(2,1)}, bf16[4,256,128]{2,1,0:T(8,128)(2,1)}, u32[]{:S(2)}, u32[]{:S(2)}) collective-permute-start(bf16[4,256,128]{2,1,0:T(8,128)(2,1)} %collective-permute-done.32), channel_id=1, source_target_pairs={{1,0},{5,4},{9,8},{13,12},{17,16},{21,20},{25,24},{29,28}} | collective-permute-start | bytes 786440 | tf_op jit(solution)/shard_map/ppermute | solution.py:41
  199.2 1.0 copy-start.5

commit v12 on v11

--- a/solution.py
+++ b/solution.py
@@ -263,16 +263,21 @@
     )(part, *pieces)
 
 
-def output_kernel(group, count, cuts, halves, me_ref, at_ref, active_ref, hidden_ref, *refs):
-    weights = refs[:cuts]
-    pieces = refs[cuts:-7]
+def output_kernel(group, count, cuts, blocks, halves, me_ref, at_ref, active_ref, hidden_ref, *refs):
+    weights = refs[: cuts * blocks]
+    pieces = refs[cuts * blocks : -7]
     out_ref, rows_in, held, own, piece_in, weight_in, own_in = refs[-7:]
     heads = pieces[0].shape[0] // group
     found = sources(me_ref[0], count)
     own_copy = pltpu.make_async_copy(hidden_ref, own, own_in)
+    depth = weights[0].shape[0]
     weight_copies = [
-        pltpu.make_async_copy(weight, held.at[cut], weight_in.at[cut])
-        for cut, weight in enumerate(weights)
+        pltpu.make_async_copy(
+            weight,
+            held.at[number // blocks, number % blocks * depth : (number % blocks + 1) * depth, :],
+            weight_in.at[number],
+        )
+        for number, weight in enumerate(weights)
     ]
 
     def copies_of(number):
@@ -295,9 +300,7 @@
     for number in range(len(pieces)):
         there, each = copies_of(number)
         when(there, lambda: each(lambda copy: copy.start()))
-    weight_copies[0].start()
-    own_copy.start()
-    for copy in weight_copies[1:]:
+    for copy in weight_copies[:blocks] + [own_copy] + weight_copies[blocks:]:
         copy.start()
     for number in range(len(pieces)):
         there, each = copies_of(number)
@@ -306,7 +309,8 @@
     rows, width = own.shape[0], held.shape[2]
     x = rows_in[...].reshape(rows, -1)
     for cut in range(cuts):
-        weight_copies[cut].wait()
+        for copy in weight_copies[cut * blocks : (cut + 1) * blocks]:
+            copy.wait()
         columns = pl.ds(pl.multiple_of(me_ref[1 + cut] * width, width), width)
         shares = jnp.dot(x, held[cut], preferred_element_type=jnp.float32)
         if cut == 0:
@@ -318,17 +322,19 @@
 
 def output(scalars, at, pieces, weights, hidden, active, chunks, group, halves):
     rows, columns = hidden.shape
-    depth, width = weights[0].shape
-    cuts = len(weights)
+    width = weights[0].shape[1]
+    cuts = columns // width
+    blocks = len(weights) // cuts
+    depth = weights[0].shape[0] * blocks
     count = (len(pieces) // halves + 1) // 2
     part_rows = rows // chunks // group
     pieces = [piece.reshape(-1, chunks, part_rows, HEAD) for piece in pieces]
     smem = pl.BlockSpec(memory_space=pltpu.SMEM)
     vmem = pl.BlockSpec(memory_space=pltpu.VMEM)
     return pl.pallas_call(
-        partial(output_kernel, group, count, cuts, halves),
+        partial(output_kernel, group, count, cuts, blocks, halves),
         in_specs=[smem, smem, vmem]
-        + [pl.BlockSpec(memory_space=pl.ANY)] * (1 + cuts + len(pieces)),
+        + [pl.BlockSpec(memory_space=pl.ANY)] * (1 + len(weights) + len(pieces)),
         out_specs=vmem,
         out_shape=jax.ShapeDtypeStruct((rows, columns), jnp.bfloat16),
         scratch_shapes=[
@@ -336,7 +342,7 @@
             pltpu.VMEM((cuts, depth, width), jnp.bfloat16),
             pltpu.VMEM((rows, columns), jnp.bfloat16),
             pltpu.SemaphoreType.DMA((halves, count, pieces[0].shape[0] // group, group)),
-            pltpu.SemaphoreType.DMA((cuts,)),
+            pltpu.SemaphoreType.DMA((cuts * blocks,)),
             pltpu.SemaphoreType.DMA,
         ],
         compiler_params=pltpu.CompilerParams(vmem_limit_bytes=LIMIT),
@@ -353,87 +359,54 @@
 
         @pl.when(pl.program_id(0) == step)
         def _():
-            each = share.shape[2]
-            for half in range(share.shape[0]):
-                share[half] = w_ref[:, half * each : (half + 1) * each]
-
-
-def shares_of(w_out, place, count, halves, each):
-    width = halves * each
-    cuts = w_out.shape[1] // count // width
-    return pl.pallas_call(
-        share_kernel,
-        grid_spec=pltpu.PrefetchScalarGridSpec(
-            num_scalar_prefetch=1,
-            grid=(count,),
-            in_specs=[
-                pl.BlockSpec(
-                    (HEAD, width),
-                    lambda j, place: (place[0], lax.rem(place[2] + j, count) * cuts + place[1]),
-                )
-            ],
-            out_specs=[pl.BlockSpec((halves, HEAD, each), lambda j, place: (0, 0, 0))] * count,
-        ),
-        out_shape=[jax.ShapeDtypeStruct((halves, HEAD, each), w_out.dtype)] * count,
-        compiler_params=pltpu.CompilerParams(vmem_limit_bytes=LIMIT),
-    )(place, w_out)
-
-
-def weight_cuts(w_out, seq_count, columns):
+            share[...] = w_ref[...]
+
+
+def weight_shares(w_out, seq_count, tensor_count, columns):
+    depth = w_out.shape[0]
+    cuts = seq_count // (depth // HEAD)
+    width = columns // cuts
+    if width % HEAD:
+        return None
+    cut = lax.axis_index("seq").astype(jnp.int32) % cuts
+    place = jnp.stack([lax.axis_index("tensor").astype(jnp.int32), cut])
+    return list(
+        pl.pallas_call(
+            share_kernel,
+            grid_spec=pltpu.PrefetchScalarGridSpec(
+                num_scalar_prefetch=1,
+                grid=(tensor_count,),
+                in_specs=[
+                    pl.BlockSpec(
+                        (depth, width),
+                        lambda j, place: (0, lax.rem(place[0] + j, tensor_count) * cuts + place[1]),
+                    )
+                ],
+                out_specs=[pl.BlockSpec((depth, width), lambda j, place: (0, 0))] * tensor_count,
+            ),
+            out_shape=[jax.ShapeDtypeStruct((depth, width), w_out.dtype)] * tensor_count,
+            compiler_params=pltpu.CompilerParams(vmem_limit_bytes=LIMIT),
+        )(place, w_out)
+    )
+
+
+def send_share(shares, step):
+    if shares is None:
+        return None
+    count = len(shares)
+    return lax.ppermute(shares[step], "tensor", [(d, (d + step) % count) for d in range(count)])
+
+
+def output_order(w_out, seq_count, tensor_count, whole):
     heads = w_out.shape[0] // HEAD
     cuts = seq_count // heads
-    width = columns // cuts
-    halves = 2 if width % (2 * HEAD) == 0 else 1
-    return heads, cuts, halves, width // halves
-
-
-def weight_shares(w_out, seq_count, tensor_count, columns):
-    heads, cuts, halves, each = weight_cuts(w_out, seq_count, columns)
-    if each % HEAD:
-        return None
-    seq_me = lax.axis_index("seq").astype(jnp.int32)
-    me = lax.axis_index("tensor").astype(jnp.int32)
-    place = jnp.stack([seq_me // cuts, seq_me % cuts, me])
-    return list(shares_of(w_out, place, tensor_count, halves, each))
-
-
-def send_shares(shares, tensor_count):
-    if shares is None:
-        return None
-    shares = list(shares)
-    for step in range(1, tensor_count):
-        ring = [(d, (d + step) % tensor_count) for d in range(tensor_count)]
-        shares[step] = lax.ppermute(shares[step], "tensor", ring)
-    return shares
-
-
-def swap(held, flips):
-    grown = []
-    for blocks, flip in zip(held, flips):
-        pairs = [(d, d ^ flip) for d in range(lax.axis_size("seq"))]
-        sent = list(blocks)
-        whole = [blocks[k] for k in sent]
-        got = lax.ppermute(
-            jnp.concatenate(whole, axis=0) if len(whole) > 1 else whole[0], "seq", pairs
-        )
-        grown.append(dict(blocks))
-        for k, block in zip(sent, jnp.split(got, len(sent))):
-            grown[-1][k ^ flip] = block
-    return grown
-
-
-def output_order(w_out, seq_count, tensor_count, columns):
-    heads, cuts, halves, each = weight_cuts(w_out, seq_count, columns)
     row = jnp.arange(tensor_count * heads, dtype=jnp.int32)
-    if each % HEAD:
+    if whole:
         return [jnp.int32(0)], row
     seq_me = lax.axis_index("seq").astype(jnp.int32)
     me = lax.axis_index("tensor").astype(jnp.int32)
-    which = [
-        (seq_me % cuts + step) % cuts * halves + half for step in range(cuts) for half in range(halves)
-    ]
-    tensor, of = row // heads, row % heads
-    return which, (of ^ (seq_me // cuts)) * tensor_count + (me - tensor) % tensor_count
+    which = [(seq_me % cuts + step) % cuts for step in range(cuts)]
+    return which, (me - row // heads) % tensor_count * heads + row % heads
 
 
 def shards(hidden, depth, norm_gain, w_query, w_key, w_value, w_out):
@@ -477,36 +450,26 @@
     )
     early, second = lax.optimization_barrier((work(first, 0), second))
     sent, early, shares = lax.optimization_barrier((work(second, 1), to_heads(early), shares))
-    sending = send_shares(shares, tensor_count)
-    late, sending = lax.optimization_barrier((to_heads(sent), sending))
+    late, far = lax.optimization_barrier((to_heads(sent), send_share(shares, 2)))
     pieces = to_parts(early) + to_parts(late)
-
-    heads, cuts, halves, _ = weight_cuts(w_out, seq_count, columns)
-    held, flips = [], []
-    if sending is not None:
-        held = [
-            {0: jnp.concatenate([share[half] for share in sending], axis=0)}
-            for half in range(halves)
-        ]
-        while cuts << len(flips) < seq_count:
-            flips.append(cuts << len(flips))
-        held = swap(held, [flips[0], flips[-1]])
-    out = attend(part, pieces, chunks, group, rows)
-    out, held = lax.optimization_barrier((out, held))
+    out, near = lax.optimization_barrier(
+        (attend(part, pieces, chunks, group, rows), send_share(shares, 1))
+    )
     home = lax.all_to_all(out, "seq", split_axis=0, concat_axis=0)
-    for stage in range(1, len(flips)):
-        held = swap(held, [flips[stage], flips[-1 - stage]])
-    home, held = lax.optimization_barrier((home, held))
+    if shares is None:
+        weights = [lax.all_to_all(w_out, "tensor", split_axis=1, concat_axis=0, tiled=True)]
+    else:
+        _, rest = lax.optimization_barrier((near, shares))
+        others = [send_share(rest, step) for step in range(3, tensor_count)]
+        home, others = lax.optimization_barrier((home, others))
+        weights = [shares[0], near, far, *others]
+        for step in range(1, group):
+            ring = [(d, d - d % group + (d - step) % group) for d in range(seq_count)]
+            weights += [lax.ppermute(weight, "seq", ring) for weight in weights[:tensor_count]]
     found = line_gather(
         [home[: seq_count // 2], home[seq_count // 2 :]], tensor_count, lambda step, last: last
     )
-    weights = [jnp.concatenate([blocks[k] for k in sorted(blocks)], axis=0) for blocks in held]
-    for turn in range(1, cuts):
-        ring = [(d, d - d % cuts + (d - turn) % cuts) for d in range(seq_count)]
-        weights += [lax.ppermute(weights[half], "seq", ring) for half in range(len(held))]
-    if not held:
-        weights = [lax.all_to_all(w_out, "tensor", split_axis=1, concat_axis=0, tiled=True)]
-    cut_of, at = output_order(w_out, seq_count, tensor_count, columns)
+    cut_of, at = output_order(w_out, seq_count, tensor_count, shares is None)
     scalars = jnp.stack([me, *cut_of])
     return output(scalars, at, sum(found, []), weights, hidden, active, chunks, group, 2)
 

time: 211 us -> 205 us (0.972)
  local copies, waits for them, and re-layouts: 9.75 us -> 5.8 us
  waiting for transfers between devices: 80.2 us -> 83.9 us
  starting transfers between devices: 67.8 us -> 65.1 us
    all_to_all x1, waiting for transfers between devices: 1.91 us -> 8.73 us  [shards(): home = lax.all_to_all(out, 'seq', split_axis=0, concat_axis=0)]
    ppermute x9 -> x7, waiting for transfers between devices: 20.8 us -> 27 us  [the longest x3 27 us: send_share(): lax.ppermute(shares[step], 'tensor', [(d, (d + step) % count) for d in ra...]
    ppermute x12, waiting for transfers between devices: 6.46 us -> 0.38 us  [line_gather(): from_left = lax.ppermute(last[at][0], 'tensor', right[step:])]
    ppermute x9 -> x7, starting transfers between devices: 10.2 us -> 5.29 us  [the longest x3 4.2 us: send_share(): lax.ppermute(shares[step], 'tensor', [(d, (d + step) % count) for d in ra...]
    ppermute x12, waiting for transfers between devices: 51.1 us -> 47.3 us  [line_gather(): from_right = lax.ppermute(last[at][1], 'tensor', left[:count - 1 - step])]
    unnamed x48 -> x36, local copies, waits for them, and re-layouts: 3.82 us -> 1.41 us
    ppermute x12, starting transfers between devices: 30.1 us -> 32.3 us  [line_gather(): from_left = lax.ppermute(last[at][0], 'tensor', right[step:])]
  transfers between devices with their start and end apart: 38 -> 36, of which waited for: 16 -> 15; matrix products, arithmetic and copies ran while one was open for 4% -> 2% of each run, Pallas kernels for 19% -> 20%
where the time goes in v12:
time: 205 us; the launch traced here: 204 us
  waiting for transfers between devices  83.9 us (41%)
  starting transfers between devices  65.1 us (32%)
  Pallas kernels  47.2 us (23%)
  local copies, waits for them, and re-layouts  5.8 us (3%)
    ppermute x12, waiting for transfers between devices, line_gather(): from_right = lax.ppermute(last[at][1], 'tensor', left[:count - 1 - step])  47.3 us
    ppermute x12, starting transfers between devices, line_gather(): from_left = lax.ppermute(last[at][0], 'tensor', right[step:])  32.3 us
    ppermute x3, waiting for transfers between devices, send_share(): lax.ppermute(shares[step], 'tensor', [(d, (d + step) % count) for d in ra...  27 us
    pallas_call x2, Pallas kernels, project(): pl.pallas_call(partial(project_kernel, group, count), in_specs=[pl.BlockS...  24.1 us
    ppermute x12, starting transfers between devices, line_gather(): from_right = lax.ppermute(last[at][1], 'tensor', left[:count - 1 - step])  15.4 us
    pallas_call x1, Pallas kernels, attend(): pl.pallas_call(partial(attend_kernel, chunks, group, rows), in_specs=[pl....  11.3 us
    all_to_all x1, waiting for transfers between devices, shards(): home = lax.all_to_all(out, 'seq', split_axis=0, concat_axis=0)  8.73 us
    all_to_all x2, starting transfers between devices, to_heads(): return lax.all_to_all(sent, 'seq', split_axis=0, concat_axis=0)  7.94 us
  transfers between devices with their start and end apart: 36, of which 15 were waited for; matrix products, arithmetic and copies ran while one was open for 2% of the time, Pallas kernels for 20%

profile of v12, /device:TPU:0, one launch (start us, length us, event | category | flops | bytes accessed | tf_op | source)
XLA Modules:
  0.0 204.2 jit_solution(17109460563227067238)
XLA Ops:
  0.0 1.3 fusion.4
  1.3 1.3 collective-permute-start.1
  2.6 6.4 %collective-permute-start = (bf16[256,1024]{1,0:T(8,128)(2,1)S(1)}, bf16[256,1024]{1,0:T(8,128)(2,1)}, u32[]{:S(2)}, u32[]{:S(2)}) collective-permute-start(bf16[256,1024]{1,0:T(8,128)(2,1)S(1)} %get-tuple-element.68.refs_3_), channel_id=1, source_target_pairs={{0,1},{1,2},{2,3},{4,5},{5,6},{6,7},{8,9},{9,10},{10,11},{12,13},{... | collective-permute-start | bytes 1572872 | tf_op jit(solution)/shard_map/ppermute | solution.py:40
  9.0 1.3 collective-permute-start.7
  10.3 5.4 %collective-permute-start.6 = (bf16[256,1024]{1,0:T(8,128)(2,1)S(1)}, bf16[256,1024]{1,0:T(8,128)(2,1)}, u32[]{:S(2)}, u32[]{:S(2)}) collective-permute-start(bf16[256,1024]{1,0:T(8,128)(2,1)S(1)} %get-tuple-element.42.refs_3_), channel_id=1, source_target_pairs={{0,1},{1,2},{2,3},{4,5},{5,6},{6,7},{8,9},{9,10},{10,11},{12,13},{... | collective-permute-start | bytes 1572872 | tf_op jit(solution)/shard_map/ppermute | solution.py:40
  15.7 3.4 %collective-permute-done.1.refs_5_ = bf16[256,1024]{1,0:T(8,128)(2,1)} collective-permute-done((bf16[256,1024]{1,0:T(8,128)(2,1)S(1)}, bf16[256,1024]{1,0:T(8,128)(2,1)}, u32[]{:S(2)}, u32[]{:S(2)}) %collective-permute-start.1) | collective-permute-done | bytes 524320 | tf_op jit(solution)/shard_map/ppermute | solution.py:41
  19.1 1.3 collective-permute-start.3
  20.4 0.1 collective-permute-done.refs_4_
  20.5 1.5 collective-permute-start.2
  22.0 0.6 pad_add_fusion.1.place_ref
  22.5 4.4 %shard_map.74 = (bf16[512,512]{1,0:T(8,128)(2,1)}, bf16[512,512]{1,0:T(8,128)(2,1)}, bf16[512,512]{1,0:T(8,128)(2,1)}, bf16[512,512]{1,0:T(8,128)(2,1)}) custom-call(s32[2]{0:T(128)} %pad_add_fusion.1.place_ref, bf16[512,4096]{1,0:T(8,128)(2,1)} %w_ref.1), custom_call_target="tpu_custom_call" | custom-call | tf_op jit(solution)/shard_map/pallas_call | solution.py:374
  27.0 3.4 %collective-permute-done.7.refs_5_ = bf16[256,1024]{1,0:T(8,128)(2,1)} collective-permute-done((bf16[256,1024]{1,0:T(8,128)(2,1)S(1)}, bf16[256,1024]{1,0:T(8,128)(2,1)}, u32[]{:S(2)}, u32[]{:S(2)}) %collective-permute-start.7) | collective-permute-done | bytes 524320 | tf_op jit(solution)/shard_map/ppermute | solution.py:41
  30.3 0.2 collective-permute-done.6.refs_4_
  30.6 1.5 collective-permute-start.8
  32.1 1.3 collective-permute-start.9
  33.3 8.2 %collective-permute-done.3.refs_7_ = bf16[256,1024]{1,0:T(8,128)(2,1)} collective-permute-done((bf16[256,1024]{1,0:T(8,128)(2,1)}, bf16[256,1024]{1,0:T(8,128)(2,1)}, u32[]{:S(2)}, u32[]{:S(2)}) %collective-permute-start.3) | collective-permute-done | bytes 524320 | tf_op jit(solution)/shard_map/ppermute | solution.py:41
  41.6 1.3 collective-permute-start.5
  42.9 1.5 collective-permute-start.4
  44.3 0.6 reshape.54.gain_ref
  45.0 1.5 collective-permute-start.10
  46.5 7.6 %collective-permute-done.9.refs_7_ = bf16[256,1024]{1,0:T(8,128)(2,1)} collective-permute-done((bf16[256,1024]{1,0:T(8,128)(2,1)}, bf16[256,1024]{1,0:T(8,128)(2,1)}, u32[]{:S(2)}, u32[]{:S(2)}) %collective-permute-start.9) | collective-permute-done | bytes 524320 | tf_op jit(solution)/shard_map/ppermute | solution.py:41
  54.1 1.3 collective-permute-start.11
  55.4 0.8 copy.8.active_ref
  56.2 9.1 %collective-permute-done.5.refs_9_ = bf16[256,1024]{1,0:T(8,128)(2,1)} collective-permute-done((bf16[256,1024]{1,0:T(8,128)(2,1)}, bf16[256,1024]{1,0:T(8,128)(2,1)}, u32[]{:S(2)}, u32[]{:S(2)}) %collective-permute-start.5) | collective-permute-done | bytes 524320 | tf_op jit(solution)/shard_map/ppermute | solution.py:41
  65.4 12.1 %shard_map.73 = bf16[8,128,384]{2,1,0:T(8,128)(2,1)} custom-call(s32[1]{0:T(128)} %bitcast.me_ref, f32[4,1024]{1,0:T(4,128)} %reshape.54.gain_ref, s32[256,1]{1,0:T(8,128)} %copy.8.active_ref, bf16[4096,512]{1,0:T(8,128)(2,1)} %refs_0_.3, bf16[4096,512]{1,0:T(8,128)(2,1)} %refs_1_.3, bf16[4096,512]{1,0:T(8,128)(2,1)} %refs_2_.3, ...), custom_call_target="tpu_custom_call" | custom-call | flops 3221225472 | bytes 15466496 | tf_op jit(solution)/shard_map/pallas_call | solution.py:120
  77.5 3.7 %all-to-all-start = ((bf16[8,128,384]{2,1,0:T(8,128)(2,1)}), bf16[8,128,384]{2,1,0:T(8,128)(2,1)S(1)}, u32[]{:S(2)}, u32[]{:S(2)}) async-start(bf16[8,128,384]{2,1,0:T(8,128)(2,1)} %shard_map.73), calls=%async_computation | async-start | bytes 1572864 | tf_op jit(solution)/shard_map/all_to_all | solution.py:433
  81.2 0.8 copy.9.active_ref
  82.0 12.1 %shard_map.75 = bf16[8,128,384]{2,1,0:T(8,128)(2,1)} custom-call(s32[1]{0:T(128)} %bitcast.me_ref, f32[4,1024]{1,0:T(4,128)} %reshape.54.gain_ref, s32[256,1]{1,0:T(8,128)} %copy.9.active_ref, bf16[4096,512]{1,0:T(8,128)(2,1)} %refs_0_.3, bf16[4096,512]{1,0:T(8,128)(2,1)} %refs_1_.3, bf16[4096,512]{1,0:T(8,128)(2,1)} %refs_2_.3, bf16[256,1024]{1,0:T(8,128)(2,1)} %copy-done, ...), custom_call_target="tpu_custom_call" | custom-call | flops 3221225472 | bytes 15466496 | tf_op jit(solution)/shard_map/pallas_call | solution.py:120
  94.1 4.2 %all-to-all-start.1 = ((bf16[8,128,384]{2,1,0:T(8,128)(2,1)}), bf16[8,128,384]{2,1,0:T(8,128)(2,1)S(1)}, u32[]{:S(2)}, u32[]{:S(2)}) async-start(bf16[8,128,384]{2,1,0:T(8,128)(2,1)} %shard_map.75), calls=%async_computation.1 | async-start | bytes 1572864 | tf_op jit(solution)/shard_map/all_to_all | solution.py:433
  98.3 2.3 %collective-permute-start.13 = (bf16[512,512]{1,0:T(8,128)(2,1)}, bf16[512,512]{1,0:T(8,128)(2,1)S(1)}, u32[]{:S(2)}, u32[]{:S(2)}) collective-permute-start(bf16[512,512]{1,0:T(8,128)(2,1)} %get-tuple-element.57), channel_id=1, source_target_pairs={{0,2},{1,3},{2,0},{3,1},{4,6},{5,7},{6,4},{7,5},{8,10},{9,11},{10,... | collective-permute-start | bytes 1572872 | tf_op jit(solution)/shard_map/ppermute | solution.py:397
  100.6 0.2 collective-permute-start.12
  100.8 24.2 %collective-permute-done.13.refs_2_ = bf16[512,512]{1,0:T(8,128)(2,1)S(1)} collective-permute-done((bf16[512,512]{1,0:T(8,128)(2,1)}, bf16[512,512]{1,0:T(8,128)(2,1)S(1)}, u32[]{:S(2)}, u32[]{:S(2)}) %collective-permute-start.13) | collective-permute-done | bytes 524320 | tf_op jit(solution)/shard_map/ppermute | solution.py:397
  125.1 0.6 collective-permute-start.15
  125.7 0.1 copy-done.6
  125.8 0.3 copy-done.5
  126.1 0.9 copy-done.17
  127.0 0.5 collective-permute-done.14.refs_3_
  127.5 11.3 %shard_map.76 = bf16[8,256,128]{2,1,0:T(8,128)(2,1)} custom-call(s32[1]{0:T(128)} %bitcast.6.part_ref, bf16[8,128,384]{2,1,0:T(8,128)(2,1)} %copy-done.4, bf16[8,128,384]{2,1,0:T(8,128)(2,1)} %copy-done.17, bf16[8,128,384]{2,1,0:T(8,128)(2,1)} %copy-done.5, bf16[8,128,384]{2,1,0:T(8,128)(2,1)} %collective-permute-done.14.refs_3_), custom_call_target="tpu_custom_call" | custom-call | flops 3623878656 | bytes 4194304 | tf_op jit(solution)/shard_map/pallas_call | solution.py:248
  138.7 2.8 %collective-permute-done.15.refs_1_ = bf16[512,512]{1,0:T(8,128)(2,1)} collective-permute-done((bf16[512,512]{1,0:T(8,128)(2,1)}, bf16[512,512]{1,0:T(8,128)(2,1)}, u32[]{:S(2)}, u32[]{:S(2)}) %collective-permute-start.15) | collective-permute-done | bytes 524320 | tf_op jit(solution)/shard_map/ppermute | solution.py:397
  141.5 1.3 collective-permute-start.16
  142.8 3.8 %all-to-all-start.2 = ((bf16[8,256,128]{2,1,0:T(8,128)(2,1)}), bf16[8,256,128]{2,1,0:T(8,128)(2,1)S(1)}, u32[]{:S(2)}, u32[]{:S(2)}) async-start(bf16[8,256,128]{2,1,0:T(8,128)(2,1)} %shard_map.76), calls=%async_computation.2 | async-start | bytes 1048576 | tf_op jit(solution)/shard_map/all_to_all | solution.py:458
  146.7 0.5 collective-permute-start.17
  147.2 0.5 collective-permute-start.18
  147.7 8.7 %all-to-all-done.2 = bf16[8,256,128]{2,1,0:T(8,128)(2,1)S(1)} async-done(((bf16[8,256,128]{2,1,0:T(8,128)(2,1)}), bf16[8,256,128]{2,1,0:T(8,128)(2,1)S(1)}, u32[]{:S(2)}, u32[]{:S(2)}) %all-to-all-start.2) | async-done | bytes 524320 | tf_op jit(solution)/shard_map/all_to_all | solution.py:458
  156.5 1.3 collective-permute-start.28
  157.8 4.6 %collective-permute-start.27 = (bf16[4,256,128]{2,1,0:T(8,128)(2,1)S(1)}, bf16[4,256,128]{2,1,0:T(8,128)(2,1)S(1)}, u32[]{:S(2)}, u32[]{:S(2)}) collective-permute-start(bf16[4,256,128]{2,1,0:T(8,128)(2,1)S(1)} %get-tuple-element.69), channel_id=1, source_target_pairs={{0,1},{1,2},{2,3},{4,5},{5,6},{6,7},{8,9},{9,10},{10,11},{12,13},{... | collective-permute-start | bytes 786440 | tf_op jit(solution)/shard_map/ppermute | solution.py:40
  162.4 1.3 collective-permute-start.22
  163.7 4.6 %collective-permute-start.21 = (bf16[4,256,128]{2,1,0:T(8,128)(2,1)S(1)}, bf16[4,256,128]{2,1,0:T(8,128)(2,1)S(1)}, u32[]{:S(2)}, u32[]{:S(2)}) collective-permute-start(bf16[4,256,128]{2,1,0:T(8,128)(2,1)S(1)} %get-tuple-element.70), channel_id=1, source_target_pairs={{0,1},{1,2},{2,3},{4,5},{5,6},{6,7},{8,9},{9,10},{10,11},{12,13},{... | collective-permute-start | bytes 786440 | tf_op jit(solution)/shard_map/ppermute | solution.py:40
  168.4 1.3 collective-permute-start.30
  169.7 1.4 collective-permute-start.29
  171.1 1.3 collective-permute-start.24
  172.4 1.4 collective-permute-start.23
  173.8 5.3 %collective-permute-done.30 = bf16[4,256,128]{2,1,0:T(8,128)(2,1)} collective-permute-done((bf16[4,256,128]{2,1,0:T(8,128)(2,1)S(1)}, bf16[4,256,128]{2,1,0:T(8,128)(2,1)}, u32[]{:S(2)}, u32[]{:S(2)}) %collective-permute-start.30) | collective-permute-done | bytes 262176 | tf_op jit(solution)/shard_map/ppermute | solution.py:41
  179.1 1.3 collective-permute-start.32
  180.4 1.4 collective-permute-start.31
  181.7 3.0 %collective-permute-done.24 = bf16[4,256,128]{2,1,0:T(8,128)(2,1)} collective-permute-done((bf16[4,256,128]{2,1,0:T(8,128)(2,1)S(1)}, bf16[4,256,128]{2,1,0:T(8,128)(2,1)}, u32[]{:S(2)}, u32[]{:S(2)}) %collective-permute-start.24) | collective-permute-done | bytes 262176 | tf_op jit(solution)/shard_map/ppermute | solution.py:41
  184.7 1.3 collective-permute-start.26
  186.0 1.4 collective-permute-start.25
  187.4 0.9 copy.10.active_ref
  188.3 0.5 fusion.at_ref
  188.8 0.6 pad_add_fusion.me_ref
  189.4 3.0 %collective-permute-done.32 = bf16[4,256,128]{2,1,0:T(8,128)(2,1)} collective-permute-done((bf16[4,256,128]{2,1,0:T(8,128)(2,1)}, bf16[4,256,128]{2,1,0:T(8,128)(2,1)}, u32[]{:S(2)}, u32[]{:S(2)}) %collective-permute-start.32) | collective-permute-done | bytes 262176 | tf_op jit(solution)/shard_map/ppermute | solution.py:41
  192.4 4.2 %collective-permute-done.26 = bf16[4,256,128]{2,1,0:T(8,128)(2,1)} collective-permute-done((bf16[4,256,128]{2,1,0:T(8,128)(2,1)}, bf16[4,256,128]{2,1,0:T(8,128)(2,1)}, u32[]{:S(2)}, u32[]{:S(2)}) %collective-permute-start.26) | collective-permute-done | bytes 262176 | tf_op jit(solution)/shard_map/ppermute | solution.py:41
  196.7 7.4 %shard_map.77 = bf16[512,1024]{1,0:T(8,128)(2,1)} custom-call(s32[3]{0:T(128)} %pad_add_fusion.me_ref, s32[16]{0:T(128)} %fusion.at_ref, s32[512,1]{1,0:T(8,128)} %copy.10.active_ref, bf16[512,1024]{1,0:T(8,128)(2,1)} %hidden_ref.1, bf16[512,512]{1,0:T(8,128)(2,1)} %get-tuple-element.54.refs_0_, bf16[512,512]{1,0:T(8,128)(2,1)} %collective-permute-done.15.refs_1_, ...), custom_call_target="tpu_custom_call" | custom-call | flops 2147483648 | bytes 8388608 | tf_op jit(solution)/shard_map/pallas_call | solution.py:334
  (60 shorter events, 0.3 us)
Async XLA Ops:
  0.0 44.3 %copy-start.15 = (f32[4096]{0:T(1024)S(1)}, f32[4096]{0:T(1024)}, u32[]{:S(2)}) copy-start(f32[4096]{0:T(1024)} %param.9) | copy-start | bytes 49156
  0.0 44.9 %copy-start.16 = (s32[512]{0:T(512)S(1)}, s32[512]{0:T(512)}, u32[]{:S(2)}) copy-start(s32[512]{0:T(512)} %param.8) | copy-start | bytes 6148
  1.3 7.7 %copy-start.1 = (bf16[256,1024]{1,0:T(8,128)(2,1)}, bf16[256,1024]{1,0:T(8,128)(2,1)S(1)}, u32[]{:S(2)}) copy-start(bf16[256,1024]{1,0:T(8,128)(2,1)S(1)} %get-tuple-element.68.refs_3_) | copy-start | bytes 1572868
  1.3 76.1 %copy-start = (bf16[256,1024]{1,0:T(8,128)(2,1)}, bf16[256,1024]{1,0:T(8,128)(2,1)S(1)}, u32[]{:S(2)}) copy-start(bf16[256,1024]{1,0:T(8,128)(2,1)S(1)} %get-tuple-element.42.refs_3_) | copy-start | bytes 1572868
  1.3 17.8 %collective-permute-start.1 = (bf16[256,1024]{1,0:T(8,128)(2,1)S(1)}, bf16[256,1024]{1,0:T(8,128)(2,1)}, u32[]{:S(2)}, u32[]{:S(2)}) collective-permute-start(bf16[256,1024]{1,0:T(8,128)(2,1)S(1)} %get-tuple-element.68.refs_3_), channel_id=1, source_target_pairs={{1,0},{2,1},{3,2},{5,4},{6,5},{7,6},{9,8},{10,9},{11,10},{13,12},{... | collective-permute-start | bytes 1572872 | tf_op jit(solution)/shard_map/ppermute | solution.py:41
  2.6 17.9 %collective-permute-start = (bf16[256,1024]{1,0:T(8,128)(2,1)S(1)}, bf16[256,1024]{1,0:T(8,128)(2,1)}, u32[]{:S(2)}, u32[]{:S(2)}) collective-permute-start(bf16[256,1024]{1,0:T(8,128)(2,1)S(1)} %get-tuple-element.68.refs_3_), channel_id=1, source_target_pairs={{0,1},{1,2},{2,3},{4,5},{5,6},{6,7},{8,9},{9,10},{10,11},{12,13},{... | collective-permute-start | bytes 1572872 | tf_op jit(solution)/shard_map/ppermute | solution.py:40
  9.0 21.3 %collective-permute-start.7 = (bf16[256,1024]{1,0:T(8,128)(2,1)S(1)}, bf16[256,1024]{1,0:T(8,128)(2,1)}, u32[]{:S(2)}, u32[]{:S(2)}) collective-permute-start(bf16[256,1024]{1,0:T(8,128)(2,1)S(1)} %get-tuple-element.42.refs_3_), channel_id=1, source_target_pairs={{1,0},{2,1},{3,2},{5,4},{6,5},{7,6},{9,8},{10,9},{11,10},{13,12},{... | collective-permute-start | bytes 1572872 | tf_op jit(solution)/shard_map/ppermute | solution.py:41
  10.3 20.3 %collective-permute-start.6 = (bf16[256,1024]{1,0:T(8,128)(2,1)S(1)}, bf16[256,1024]{1,0:T(8,128)(2,1)}, u32[]{:S(2)}, u32[]{:S(2)}) collective-permute-start(bf16[256,1024]{1,0:T(8,128)(2,1)S(1)} %get-tuple-element.42.refs_3_), channel_id=1, source_target_pairs={{0,1},{1,2},{2,3},{4,5},{5,6},{6,7},{8,9},{9,10},{10,11},{12,13},{... | collective-permute-start | bytes 1572872 | tf_op jit(solution)/shard_map/ppermute | solution.py:40
  19.1 22.5 %collective-permute-start.3 = (bf16[256,1024]{1,0:T(8,128)(2,1)}, bf16[256,1024]{1,0:T(8,128)(2,1)}, u32[]{:S(2)}, u32[]{:S(2)}) collective-permute-start(bf16[256,1024]{1,0:T(8,128)(2,1)} %collective-permute-done.1.refs_5_), channel_id=1, source_target_pairs={{1,0},{2,1},{5,4},{6,5},{9,8},{10,9},{13,12},{14,13},{17,16},{18,1... | collective-permute-start | bytes 1572872 | tf_op jit(solution)/shard_map/ppermute | solution.py:41
  20.5 22.4 %collective-permute-start.2 = (bf16[256,1024]{1,0:T(8,128)(2,1)}, bf16[256,1024]{1,0:T(8,128)(2,1)}, u32[]{:S(2)}, u32[]{:S(2)}) collective-permute-start(bf16[256,1024]{1,0:T(8,128)(2,1)} %collective-permute-done.refs_4_), channel_id=1, source_target_pairs={{1,2},{2,3},{5,6},{6,7},{9,10},{10,11},{13,14},{14,15},{17,18},{18... | collective-permute-start | bytes 1572872 | tf_op jit(solution)/shard_map/ppermute | solution.py:40
  30.6 14.4 %collective-permute-start.8 = (bf16[256,1024]{1,0:T(8,128)(2,1)}, bf16[256,1024]{1,0:T(8,128)(2,1)}, u32[]{:S(2)}, u32[]{:S(2)}) collective-permute-start(bf16[256,1024]{1,0:T(8,128)(2,1)} %collective-permute-done.6.refs_4_), channel_id=1, source_target_pairs={{1,2},{2,3},{5,6},{6,7},{9,10},{10,11},{13,14},{14,15},{17,18},{18... | collective-permute-start | bytes 1572872 | tf_op jit(solution)/shard_map/ppermute | solution.py:40
  32.1 22.1 %collective-permute-start.9 = (bf16[256,1024]{1,0:T(8,128)(2,1)}, bf16[256,1024]{1,0:T(8,128)(2,1)}, u32[]{:S(2)}, u32[]{:S(2)}) collective-permute-start(bf16[256,1024]{1,0:T(8,128)(2,1)} %collective-permute-done.7.refs_5_), channel_id=1, source_target_pairs={{1,0},{2,1},{5,4},{6,5},{9,8},{10,9},{13,12},{14,13},{17,16},{18,1... | collective-permute-start | bytes 1572872 | tf_op jit(solution)/shard_map/ppermute | solution.py:41
  41.6 23.8 %collective-permute-start.5 = (bf16[256,1024]{1,0:T(8,128)(2,1)}, bf16[256,1024]{1,0:T(8,128)(2,1)}, u32[]{:S(2)}, u32[]{:S(2)}) collective-permute-start(bf16[256,1024]{1,0:T(8,128)(2,1)} %collective-permute-done.3.refs_7_), channel_id=1, source_target_pairs={{1,0},{5,4},{9,8},{13,12},{17,16},{21,20},{25,24},{29,28}} | collective-permute-start | bytes 1572872 | tf_op jit(solution)/shard_map/ppermute | solution.py:41
  42.9 22.5 %collective-permute-start.4 = (bf16[256,1024]{1,0:T(8,128)(2,1)}, bf16[256,1024]{1,0:T(8,128)(2,1)}, u32[]{:S(2)}, u32[]{:S(2)}) collective-permute-start(bf16[256,1024]{1,0:T(8,128)(2,1)} %collective-permute-done.2.refs_6_), channel_id=1, source_target_pairs={{2,3},{6,7},{10,11},{14,15},{18,19},{22,23},{26,27},{30,31}} | collective-permute-start | bytes 1572872 | tf_op jit(solution)/shard_map/ppermute | solution.py:40
  45.0 32.5 %collective-permute-start.10 = (bf16[256,1024]{1,0:T(8,128)(2,1)}, bf16[256,1024]{1,0:T(8,128)(2,1)}, u32[]{:S(2)}, u32[]{:S(2)}) collective-permute-start(bf16[256,1024]{1,0:T(8,128)(2,1)} %collective-permute-done.8.refs_6_), channel_id=1, source_target_pairs={{2,3},{6,7},{10,11},{14,15},{18,19},{22,23},{26,27},{30,31}} | collective-permute-start | bytes 1572872 | tf_op jit(solution)/shard_map/ppermute | solution.py:40
  54.1 23.3 %collective-permute-start.11 = (bf16[256,1024]{1,0:T(8,128)(2,1)}, bf16[256,1024]{1,0:T(8,128)(2,1)}, u32[]{:S(2)}, u32[]{:S(2)}) collective-permute-start(bf16[256,1024]{1,0:T(8,128)(2,1)} %collective-permute-done.9.refs_7_), channel_id=1, source_target_pairs={{1,0},{5,4},{9,8},{13,12},{17,16},{21,20},{25,24},{29,28}} | collective-permute-start | bytes 1572872 | tf_op jit(solution)/shard_map/ppermute | solution.py:41
  77.5 16.6 %all-to-all-start = ((bf16[8,128,384]{2,1,0:T(8,128)(2,1)}), bf16[8,128,384]{2,1,0:T(8,128)(2,1)S(1)}, u32[]{:S(2)}, u32[]{:S(2)}) async-start(bf16[8,128,384]{2,1,0:T(8,128)(2,1)} %shard_map.73), calls=%async_computation | async-start | bytes 1572864 | tf_op jit(solution)/shard_map/all_to_all | solution.py:433
  94.1 33.4 %copy-start.4 = (bf16[8,128,384]{2,1,0:T(8,128)(2,1)}, bf16[8,128,384]{2,1,0:T(8,128)(2,1)S(1)}, u32[]{:S(2)}) copy-start(bf16[8,128,384]{2,1,0:T(8,128)(2,1)S(1)} %all-to-all-done.refs_0_) | copy-start | bytes 2359300
  94.1 30.9 %all-to-all-start.1 = ((bf16[8,128,384]{2,1,0:T(8,128)(2,1)}), bf16[8,128,384]{2,1,0:T(8,128)(2,1)S(1)}, u32[]{:S(2)}, u32[]{:S(2)}) async-start(bf16[8,128,384]{2,1,0:T(8,128)(2,1)} %shard_map.75), calls=%async_computation.1 | async-start | bytes 1572864 | tf_op jit(solution)/shard_map/all_to_all | solution.py:433
  98.3 26.7 %collective-permute-start.13 = (bf16[512,512]{1,0:T(8,128)(2,1)}, bf16[512,512]{1,0:T(8,128)(2,1)S(1)}, u32[]{:S(2)}, u32[]{:S(2)}) collective-permute-start(bf16[512,512]{1,0:T(8,128)(2,1)} %get-tuple-element.57), channel_id=1, source_target_pairs={{0,2},{1,3},{2,0},{3,1},{4,6},{5,7},{6,4},{7,5},{8,10},{9,11},{10,... | collective-permute-start | bytes 1572872 | tf_op jit(solution)/shard_map/ppermute | solution.py:397
  100.6 25.1 %collective-permute-start.12 = (bf16[8,128,384]{2,1,0:T(8,128)(2,1)S(1)}, bf16[8,128,384]{2,1,0:T(8,128)(2,1)S(1)}, u32[]{:S(2)}, u32[]{:S(2)}) collective-permute-start(bf16[8,128,384]{2,1,0:T(8,128)(2,1)S(1)} %all-to-all-done.refs_0_), channel_id=1, source_target_pairs={{0,4},{4,0},{8,12},{12,8},{16,20},{20,16},{24,28},{28,24},{1,5},{5... | collective-permute-start | bytes 2359304 | tf_op jit(solution)/shard_map/ppermute | solution.py:440
  125.0 0.8 copy-start.6
  125.0 1.1 copy-start.5
  125.0 2.5 %collective-permute-start.14 = (bf16[8,128,384]{2,1,0:T(8,128)(2,1)S(1)}, bf16[8,128,384]{2,1,0:T(8,128)(2,1)}, u32[]{:S(2)}, u32[]{:S(2)}) collective-permute-start(bf16[8,128,384]{2,1,0:T(8,128)(2,1)S(1)} %all-to-all-done.1.refs_2_), channel_id=1, source_target_pairs={{0,4},{4,0},{8,12},{12,8},{16,20},{20,16},{24,28},{28,24},{1,5},{5... | collective-permute-start | bytes 2359304 | tf_op jit(solution)/shard_map/ppermute | solution.py:440
  125.1 16.4 %collective-permute-start.15 = (bf16[512,512]{1,0:T(8,128)(2,1)}, bf16[512,512]{1,0:T(8,128)(2,1)}, u32[]{:S(2)}, u32[]{:S(2)}) collective-permute-start(bf16[512,512]{1,0:T(8,128)(2,1)} %get-tuple-element.59), channel_id=1, source_target_pairs={{0,1},{1,2},{2,3},{3,0},{4,5},{5,6},{6,7},{7,4},{8,9},{9,10},{10,1... | collective-permute-start | bytes 1572872 | tf_op jit(solution)/shard_map/ppermute | solution.py:397
  126.1 0.9 copy-start.17
  141.5 14.9 %collective-permute-start.16 = (bf16[512,512]{1,0:T(8,128)(2,1)}, bf16[512,512]{1,0:T(8,128)(2,1)S(1)}, u32[]{:S(2)}, u32[]{:S(2)}) collective-permute-start(bf16[512,512]{1,0:T(8,128)(2,1)} %get-tuple-element.64), channel_id=1, source_target_pairs={{0,3},{1,0},{2,1},{3,2},{4,7},{5,4},{6,5},{7,6},{8,11},{9,8},{10,9... | collective-permute-start | bytes 1572872 | tf_op jit(solution)/shard_map/ppermute | solution.py:397
  142.8 13.6 %all-to-all-start.2 = ((bf16[8,256,128]{2,1,0:T(8,128)(2,1)}), bf16[8,256,128]{2,1,0:T(8,128)(2,1)S(1)}, u32[]{:S(2)}, u32[]{:S(2)}) async-start(bf16[8,256,128]{2,1,0:T(8,128)(2,1)} %shard_map.76), calls=%async_computation.2 | async-start | bytes 1048576 | tf_op jit(solution)/shard_map/all_to_all | solution.py:458
  146.7 15.7 %collective-permute-start.17 = (bf16[512,512]{1,0:T(8,128)(2,1)}, bf16[512,512]{1,0:T(8,128)(2,1)S(1)}, u32[]{:S(2)}, u32[]{:S(2)}) collective-permute-start(bf16[512,512]{1,0:T(8,128)(2,1)} %get-tuple-element.54.refs_0_), channel_id=1, source_target_pairs={{0,4},{4,0},{8,12},{12,8},{16,20},{20,16},{24,28},{28,24},{1,5},{5... | collective-permute-start | bytes 1572872 | tf_op jit(solution)/shard_map/ppermute | solution.py:468
  147.2 16.5 %collective-permute-start.19 = (bf16[512,512]{1,0:T(8,128)(2,1)}, bf16[512,512]{1,0:T(8,128)(2,1)S(1)}, u32[]{:S(2)}, u32[]{:S(2)}) collective-permute-start(bf16[512,512]{1,0:T(8,128)(2,1)} %copy-done.6), channel_id=1, source_target_pairs={{0,4},{4,0},{8,12},{12,8},{16,20},{20,16},{24,28},{28,24},{1,5},{5... | collective-permute-start | bytes 1572872 | tf_op jit(solution)/shard_map/ppermute | solution.py:468
  147.2 21.1 %collective-permute-start.18 = (bf16[512,512]{1,0:T(8,128)(2,1)}, bf16[512,512]{1,0:T(8,128)(2,1)}, u32[]{:S(2)}, u32[]{:S(2)}) collective-permute-start(bf16[512,512]{1,0:T(8,128)(2,1)} %collective-permute-done.15.refs_1_), channel_id=1, source_target_pairs={{0,4},{4,0},{8,12},{12,8},{16,20},{20,16},{24,28},{28,24},{1,5},{5... | collective-permute-start | bytes 1572872 | tf_op jit(solution)/shard_map/ppermute | solution.py:468
  156.4 16.0 %copy-start.7 = (bf16[512,512]{1,0:T(8,128)(2,1)}, bf16[512,512]{1,0:T(8,128)(2,1)S(1)}, u32[]{:S(2)}) copy-start(bf16[512,512]{1,0:T(8,128)(2,1)S(1)} %collective-permute-done.16.refs_3_) | copy-start | bytes 1572868
  156.5 40.2 %copy-start.2 = (bf16[4,256,128]{2,1,0:T(8,128)(2,1)}, bf16[4,256,128]{2,1,0:T(8,128)(2,1)S(1)}, u32[]{:S(2)}) copy-start(bf16[4,256,128]{2,1,0:T(8,128)(2,1)S(1)} %get-tuple-element.69) | copy-start | bytes 786436
  156.5 40.2 %copy-start.3 = (bf16[4,256,128]{2,1,0:T(8,128)(2,1)}, bf16[4,256,128]{2,1,0:T(8,128)(2,1)S(1)}, u32[]{:S(2)}) copy-start(bf16[4,256,128]{2,1,0:T(8,128)(2,1)S(1)} %get-tuple-element.70) | copy-start | bytes 786436
  156.5 11.9 %collective-permute-start.28 = (bf16[4,256,128]{2,1,0:T(8,128)(2,1)S(1)}, bf16[4,256,128]{2,1,0:T(8,128)(2,1)S(1)}, u32[]{:S(2)}, u32[]{:S(2)}) collective-permute-start(bf16[4,256,128]{2,1,0:T(8,128)(2,1)S(1)} %get-tuple-element.69), channel_id=1, source_target_pairs={{1,0},{2,1},{3,2},{5,4},{6,5},{7,6},{9,8},{10,9},{11,10},{13,12},{... | collective-permute-start | bytes 786440 | tf_op jit(solution)/shard_map/ppermute | solution.py:41
  157.8 11.9 %collective-permute-start.27 = (bf16[4,256,128]{2,1,0:T(8,128)(2,1)S(1)}, bf16[4,256,128]{2,1,0:T(8,128)(2,1)S(1)}, u32[]{:S(2)}, u32[]{:S(2)}) collective-permute-start(bf16[4,256,128]{2,1,0:T(8,128)(2,1)S(1)} %get-tuple-element.69), channel_id=1, source_target_pairs={{0,1},{1,2},{2,3},{4,5},{5,6},{6,7},{8,9},{9,10},{10,11},{12,13},{... | collective-permute-start | bytes 786440 | tf_op jit(solution)/shard_map/ppermute | solution.py:40
  162.4 27.0 %copy-start.8 = (bf16[512,512]{1,0:T(8,128)(2,1)}, bf16[512,512]{1,0:T(8,128)(2,1)S(1)}, u32[]{:S(2)}) copy-start(bf16[512,512]{1,0:T(8,128)(2,1)S(1)} %collective-permute-done.17.refs_4_) | copy-start | bytes 1572868
  162.4 8.7 %collective-permute-start.22 = (bf16[4,256,128]{2,1,0:T(8,128)(2,1)S(1)}, bf16[4,256,128]{2,1,0:T(8,128)(2,1)S(1)}, u32[]{:S(2)}, u32[]{:S(2)}) collective-permute-start(bf16[4,256,128]{2,1,0:T(8,128)(2,1)S(1)} %get-tuple-element.70), channel_id=1, source_target_pairs={{1,0},{2,1},{3,2},{5,4},{6,5},{7,6},{9,8},{10,9},{11,10},{13,12},{... | collective-permute-start | bytes 786440 | tf_op jit(solution)/shard_map/ppermute | solution.py:41
  163.7 28.7 %copy-start.9 = (bf16[512,512]{1,0:T(8,128)(2,1)}, bf16[512,512]{1,0:T(8,128)(2,1)S(1)}, u32[]{:S(2)}) copy-start(bf16[512,512]{1,0:T(8,128)(2,1)S(1)} %collective-permute-done.19.refs_6_) | copy-start | bytes 1572868
  163.7 8.7 %collective-permute-start.21 = (bf16[4,256,128]{2,1,0:T(8,128)(2,1)S(1)}, bf16[4,256,128]{2,1,0:T(8,128)(2,1)S(1)}, u32[]{:S(2)}, u32[]{:S(2)}) collective-permute-start(bf16[4,256,128]{2,1,0:T(8,128)(2,1)S(1)} %get-tuple-element.70), channel_id=1, source_target_pairs={{0,1},{1,2},{2,3},{4,5},{5,6},{6,7},{8,9},{9,10},{10,11},{12,13},{... | collective-permute-start | bytes 786440 | tf_op jit(solution)/shard_map/ppermute | solution.py:40
  168.3 21.1 %collective-permute-start.20 = (bf16[512,512]{1,0:T(8,128)(2,1)S(1)}, bf16[512,512]{1,0:T(8,128)(2,1)S(1)}, u32[]{:S(2)}, u32[]{:S(2)}) collective-permute-start(bf16[512,512]{1,0:T(8,128)(2,1)S(1)} %collective-permute-done.16.refs_3_), channel_id=1, source_target_pairs={{0,4},{4,0},{8,12},{12,8},{16,20},{20,16},{24,28},{28,24},{1,5},{5... | collective-permute-start | bytes 1572872 | tf_op jit(solution)/shard_map/ppermute | solution.py:468
  168.4 28.3 %copy-start.11 = (bf16[4,256,128]{2,1,0:T(8,128)(2,1)}, bf16[4,256,128]{2,1,0:T(8,128)(2,1)S(1)}, u32[]{:S(2)}) copy-start(bf16[4,256,128]{2,1,0:T(8,128)(2,1)S(1)} %collective-permute-done.28) | copy-start | bytes 786436
  168.4 10.7 %collective-permute-start.30 = (bf16[4,256,128]{2,1,0:T(8,128)(2,1)S(1)}, bf16[4,256,128]{2,1,0:T(8,128)(2,1)}, u32[]{:S(2)}, u32[]{:S(2)}) collective-permute-start(bf16[4,256,128]{2,1,0:T(8,128)(2,1)S(1)} %collective-permute-done.28), channel_id=1, source_target_pairs={{1,0},{2,1},{5,4},{6,5},{9,8},{10,9},{13,12},{14,13},{17,16},{18,1... | collective-permute-start | bytes 786440 | tf_op jit(solution)/shard_map/ppermute | solution.py:41
  169.7 26.9 %copy-start.12 = (bf16[4,256,128]{2,1,0:T(8,128)(2,1)}, bf16[4,256,128]{2,1,0:T(8,128)(2,1)S(1)}, u32[]{:S(2)}) copy-start(bf16[4,256,128]{2,1,0:T(8,128)(2,1)S(1)} %collective-permute-done.27) | copy-start | bytes 786436
  169.7 10.7 %collective-permute-start.29 = (bf16[4,256,128]{2,1,0:T(8,128)(2,1)S(1)}, bf16[4,256,128]{2,1,0:T(8,128)(2,1)}, u32[]{:S(2)}, u32[]{:S(2)}) collective-permute-start(bf16[4,256,128]{2,1,0:T(8,128)(2,1)S(1)} %collective-permute-done.27), channel_id=1, source_target_pairs={{1,2},{2,3},{5,6},{6,7},{9,10},{10,11},{13,14},{14,15},{17,18},{18... | collective-permute-start | bytes 786440 | tf_op jit(solution)/shard_map/ppermute | solution.py:40
  171.1 9.3 %copy-start.13 = (bf16[4,256,128]{2,1,0:T(8,128)(2,1)}, bf16[4,256,128]{2,1,0:T(8,128)(2,1)S(1)}, u32[]{:S(2)}) copy-start(bf16[4,256,128]{2,1,0:T(8,128)(2,1)S(1)} %collective-permute-done.22) | copy-start | bytes 786436
  171.1 13.6 %collective-permute-start.24 = (bf16[4,256,128]{2,1,0:T(8,128)(2,1)S(1)}, bf16[4,256,128]{2,1,0:T(8,128)(2,1)}, u32[]{:S(2)}, u32[]{:S(2)}) collective-permute-start(bf16[4,256,128]{2,1,0:T(8,128)(2,1)S(1)} %collective-permute-done.22), channel_id=1, source_target_pairs={{1,0},{2,1},{5,4},{6,5},{9,8},{10,9},{13,12},{14,13},{17,16},{18,1... | collective-permute-start | bytes 786440 | tf_op jit(solution)/shard_map/ppermute | solution.py:41
  172.4 12.3 %copy-start.14 = (bf16[4,256,128]{2,1,0:T(8,128)(2,1)}, bf16[4,256,128]{2,1,0:T(8,128)(2,1)S(1)}, u32[]{:S(2)}) copy-start(bf16[4,256,128]{2,1,0:T(8,128)(2,1)S(1)} %collective-permute-done.21) | copy-start | bytes 786436
  172.4 13.6 %collective-permute-start.23 = (bf16[4,256,128]{2,1,0:T(8,128)(2,1)S(1)}, bf16[4,256,128]{2,1,0:T(8,128)(2,1)}, u32[]{:S(2)}, u32[]{:S(2)}) collective-permute-start(bf16[4,256,128]{2,1,0:T(8,128)(2,1)S(1)} %collective-permute-done.21), channel_id=1, source_target_pairs={{1,2},{2,3},{5,6},{6,7},{9,10},{10,11},{13,14},{14,15},{17,18},{18... | collective-permute-start | bytes 786440 | tf_op jit(solution)/shard_map/ppermute | solution.py:40
  179.1 13.3 %collective-permute-start.32 = (bf16[4,256,128]{2,1,0:T(8,128)(2,1)}, bf16[4,256,128]{2,1,0:T(8,128)(2,1)}, u32[]{:S(2)}, u32[]{:S(2)}) collective-permute-start(bf16[4,256,128]{2,1,0:T(8,128)(2,1)} %collective-permute-done.30), channel_id=1, source_target_pairs={{1,0},{5,4},{9,8},{13,12},{17,16},{21,20},{25,24},{29,28}} | collective-permute-start | bytes 786440 | tf_op jit(solution)/shard_map/ppermute | solution.py:41
  180.4 12.0 %collective-permute-start.31 = (bf16[4,256,128]{2,1,0:T(8,128)(2,1)}, bf16[4,256,128]{2,1,0:T(8,128)(2,1)}, u32[]{:S(2)}, u32[]{:S(2)}) collective-permute-start(bf16[4,256,128]{2,1,0:T(8,128)(2,1)} %collective-permute-done.29), channel_id=1, source_target_pairs={{2,3},{6,7},{10,11},{14,15},{18,19},{22,23},{26,27},{30,31}} | collective-permute-start | bytes 786440 | tf_op jit(solution)/shard_map/ppermute | solution.py:40
  184.7 11.9 %collective-permute-start.26 = (bf16[4,256,128]{2,1,0:T(8,128)(2,1)}, bf16[4,256,128]{2,1,0:T(8,128)(2,1)}, u32[]{:S(2)}, u32[]{:S(2)}) collective-permute-start(bf16[4,256,128]{2,1,0:T(8,128)(2,1)} %collective-permute-done.24), channel_id=1, source_target_pairs={{1,0},{5,4},{9,8},{13,12},{17,16},{21,20},{25,24},{29,28}} | collective-permute-start | bytes 786440 | tf_op jit(solution)/shard_map/ppermute | solution.py:41
  186.0 10.6 %collective-permute-start.25 = (bf16[4,256,128]{2,1,0:T(8,128)(2,1)}, bf16[4,256,128]{2,1,0:T(8,128)(2,1)}, u32[]{:S(2)}, u32[]{:S(2)}) collective-permute-start(bf16[4,256,128]{2,1,0:T(8,128)(2,1)} %collective-permute-done.23), channel_id=1, source_target_pairs={{2,3},{6,7},{10,11},{14,15},{18,19},{22,23},{26,27},{30,31}} | collective-permute-start | bytes 786440 | tf_op jit(solution)/shard_map/ppermute | solution.py:40
  189.4 3.0 %copy-start.10 = (bf16[512,512]{1,0:T(8,128)(2,1)}, bf16[512,512]{1,0:T(8,128)(2,1)S(1)}, u32[]{:S(2)}) copy-start(bf16[512,512]{1,0:T(8,128)(2,1)S(1)} %collective-permute-done.20.refs_7_) | copy-start | bytes 1572868

commit v13 on v12

--- a/solution.py
+++ b/solution.py
@@ -390,11 +390,12 @@
     )
 
 
-def send_share(shares, step):
+def send_share(shares, step, rows=slice(None)):
     if shares is None:
         return None
     count = len(shares)
-    return lax.ppermute(shares[step], "tensor", [(d, (d + step) % count) for d in range(count)])
+    ring = [(d, (d + step) % count) for d in range(count)]
+    return lax.ppermute(shares[step][rows], "tensor", ring)
 
 
 def output_order(w_out, seq_count, tensor_count, whole):
@@ -448,9 +449,14 @@
     first, second = line_gather(
         [hidden[:chunk_rows], hidden[chunk_rows:]], tensor_count, cut_weight
     )
-    early, second = lax.optimization_barrier((work(first, 0), second))
-    sent, early, shares = lax.optimization_barrier((work(second, 1), to_heads(early), shares))
-    late, far = lax.optimization_barrier((to_heads(sent), send_share(shares, 2)))
+    early, second, shares = lax.optimization_barrier((work(first, 0), second, shares))
+    middle = w_out.shape[0] // 2
+    sent, early, far, shares = lax.optimization_barrier(
+        (work(second, 1), to_heads(early), send_share(shares, 2, slice(0, middle)), shares)
+    )
+    late, rest = lax.optimization_barrier(
+        (to_heads(sent), send_share(shares, 2, slice(middle, None)))
+    )
     pieces = to_parts(early) + to_parts(late)
     out, near = lax.optimization_barrier(
         (attend(part, pieces, chunks, group, rows), send_share(shares, 1))
@@ -459,10 +465,10 @@
     if shares is None:
         weights = [lax.all_to_all(w_out, "tensor", split_axis=1, concat_axis=0, tiled=True)]
     else:
-        _, rest = lax.optimization_barrier((near, shares))
-        others = [send_share(rest, step) for step in range(3, tensor_count)]
+        _, last = lax.optimization_barrier((near, shares))
+        others = [send_share(last, step) for step in range(3, tensor_count)]
         home, others = lax.optimization_barrier((home, others))
-        weights = [shares[0], near, far, *others]
+        weights = [shares[0], near, jnp.concatenate([far, rest], axis=0), *others]
         for step in range(1, group):
             ring = [(d, d - d % group + (d - step) % group) for d in range(seq_count)]
             weights += [lax.ppermute(weight, "seq", ring) for weight in weights[:tensor_count]]

time: 205 us -> 200 us (0.976)
  waiting for transfers between devices: 83.9 us -> 75 us
  local copies, waits for them, and re-layouts: 5.8 us -> 10.6 us
    ppermute x3 -> x4, waiting for transfers between devices: 27 us -> 18.2 us  [send_share(): return lax.ppermute(shares[step][rows], 'tensor', ring)]
    slice x0 -> x2, local copies, waits for them, and re-layouts: none -> 2.64 us  [send_share(): return lax.ppermute(shares[step][rows], 'tensor', ring)]
    ppermute x3 -> x4, starting transfers between devices: 4.2 us -> 3.41 us  [send_share(): return lax.ppermute(shares[step][rows], 'tensor', ring)]
  transfers between devices with their start and end apart: 36 -> 37, of which waited for: 15 -> 16; matrix products, arithmetic and copies ran while one was open for 2% -> 5% of each run, Pallas kernels for 20% -> 20%
where the time goes in v13:
time: 200 us; the launch traced here: 199 us
  waiting for transfers between devices  75 us (38%)
  starting transfers between devices  64 us (32%)
  Pallas kernels  47.2 us (24%)
  local copies, waits for them, and re-layouts  10.6 us (5%)
    ppermute x12, waiting for transfers between devices, line_gather(): from_right = lax.ppermute(last[at][1], 'tensor', left[:count - 1 - step])  48.7 us
    ppermute x12, starting transfers between devices, line_gather(): from_left = lax.ppermute(last[at][0], 'tensor', right[step:])  32.3 us
    pallas_call x2, Pallas kernels, project(): pl.pallas_call(partial(project_kernel, group, count), in_specs=[pl.BlockS...  24.2 us
    ppermute x4, waiting for transfers between devices, send_share(): return lax.ppermute(shares[step][rows], 'tensor', ring)  18.2 us
    ppermute x12, starting transfers between devices, line_gather(): from_right = lax.ppermute(last[at][1], 'tensor', left[:count - 1 - step])  15.4 us
    pallas_call x1, Pallas kernels, attend(): pl.pallas_call(partial(attend_kernel, chunks, group, rows), in_specs=[pl....  11.3 us
    all_to_all x2, starting transfers between devices, to_heads(): return lax.all_to_all(sent, 'seq', split_axis=0, concat_axis=0)  7.58 us
    pallas_call x1, Pallas kernels, output(): pl.pallas_call(partial(output_kernel, group, count, cuts, blocks, halves)...  7.37 us
  transfers between devices with their start and end apart: 37, of which 16 were waited for; matrix products, arithmetic and copies ran while one was open for 5% of the time, Pallas kernels for 20%

profile of v13, /device:TPU:0, one launch (start us, length us, event | category | flops | bytes accessed | tf_op | source)
XLA Modules:
  0.0 199.1 jit_solution(3809041459986181935)
XLA Ops:
  0.0 1.3 fusion.4
  1.3 1.3 collective-permute-start.1
  2.6 6.4 %collective-permute-start = (bf16[256,1024]{1,0:T(8,128)(2,1)S(1)}, bf16[256,1024]{1,0:T(8,128)(2,1)}, u32[]{:S(2)}, u32[]{:S(2)}) collective-permute-start(bf16[256,1024]{1,0:T(8,128)(2,1)S(1)} %get-tuple-element.78.refs_3_), channel_id=1, source_target_pairs={{0,1},{1,2},{2,3},{4,5},{5,6},{6,7},{8,9},{9,10},{10,11},{12,13},{... | collective-permute-start | bytes 1572872 | tf_op jit(solution)/shard_map/ppermute | solution.py:40
  9.0 1.3 collective-permute-start.7
  10.3 5.4 %collective-permute-start.6 = (bf16[256,1024]{1,0:T(8,128)(2,1)S(1)}, bf16[256,1024]{1,0:T(8,128)(2,1)}, u32[]{:S(2)}, u32[]{:S(2)}) collective-permute-start(bf16[256,1024]{1,0:T(8,128)(2,1)S(1)} %get-tuple-element.51.refs_3_), channel_id=1, source_target_pairs={{0,1},{1,2},{2,3},{4,5},{5,6},{6,7},{8,9},{9,10},{10,11},{12,13},{... | collective-permute-start | bytes 1572872 | tf_op jit(solution)/shard_map/ppermute | solution.py:40
  15.6 3.5 %collective-permute-done.1.refs_5_ = bf16[256,1024]{1,0:T(8,128)(2,1)} collective-permute-done((bf16[256,1024]{1,0:T(8,128)(2,1)S(1)}, bf16[256,1024]{1,0:T(8,128)(2,1)}, u32[]{:S(2)}, u32[]{:S(2)}) %collective-permute-start.1) | collective-permute-done | bytes 524320 | tf_op jit(solution)/shard_map/ppermute | solution.py:41
  19.1 1.3 collective-permute-start.3
  20.5 1.5 collective-permute-start.2
  22.0 0.6 pad_add_fusion.1.place_ref
  22.6 4.4 %shard_map.74 = (bf16[512,512]{1,0:T(8,128)(2,1)}, bf16[512,512]{1,0:T(8,128)(2,1)}, bf16[512,512]{1,0:T(8,128)(2,1)}, bf16[512,512]{1,0:T(8,128)(2,1)}) custom-call(s32[2]{0:T(128)} %pad_add_fusion.1.place_ref, bf16[512,4096]{1,0:T(8,128)(2,1)} %w_ref.1), custom_call_target="tpu_custom_call" | custom-call | tf_op jit(solution)/shard_map/pallas_call | solution.py:374
  26.9 3.4 %collective-permute-done.7.refs_5_ = bf16[256,1024]{1,0:T(8,128)(2,1)} collective-permute-done((bf16[256,1024]{1,0:T(8,128)(2,1)S(1)}, bf16[256,1024]{1,0:T(8,128)(2,1)}, u32[]{:S(2)}, u32[]{:S(2)}) %collective-permute-start.7) | collective-permute-done | bytes 524320 | tf_op jit(solution)/shard_map/ppermute | solution.py:41
  30.6 1.5 collective-permute-start.8
  32.1 1.3 collective-permute-start.9
  33.4 8.2 %collective-permute-done.3.refs_7_ = bf16[256,1024]{1,0:T(8,128)(2,1)} collective-permute-done((bf16[256,1024]{1,0:T(8,128)(2,1)}, bf16[256,1024]{1,0:T(8,128)(2,1)}, u32[]{:S(2)}, u32[]{:S(2)}) %collective-permute-start.3) | collective-permute-done | bytes 524320 | tf_op jit(solution)/shard_map/ppermute | solution.py:41
  41.6 1.3 collective-permute-start.5
  42.9 1.5 collective-permute-start.4
  44.3 0.6 reshape.54.gain_ref
  45.0 1.5 collective-permute-start.10
  46.4 7.7 %collective-permute-done.9.refs_7_ = bf16[256,1024]{1,0:T(8,128)(2,1)} collective-permute-done((bf16[256,1024]{1,0:T(8,128)(2,1)}, bf16[256,1024]{1,0:T(8,128)(2,1)}, u32[]{:S(2)}, u32[]{:S(2)}) %collective-permute-start.9) | collective-permute-done | bytes 524320 | tf_op jit(solution)/shard_map/ppermute | solution.py:41
  54.2 1.3 collective-permute-start.11
  55.5 0.8 copy.8.active_ref
  56.3 9.1 %collective-permute-done.5.refs_9_ = bf16[256,1024]{1,0:T(8,128)(2,1)} collective-permute-done((bf16[256,1024]{1,0:T(8,128)(2,1)}, bf16[256,1024]{1,0:T(8,128)(2,1)}, u32[]{:S(2)}, u32[]{:S(2)}) %collective-permute-start.5) | collective-permute-done | bytes 524320 | tf_op jit(solution)/shard_map/ppermute | solution.py:41
  65.4 12.1 %shard_map.73 = bf16[8,128,384]{2,1,0:T(8,128)(2,1)} custom-call(s32[1]{0:T(128)} %bitcast.me_ref, f32[4,1024]{1,0:T(4,128)} %reshape.54.gain_ref, s32[256,1]{1,0:T(8,128)} %copy.8.active_ref, bf16[4096,512]{1,0:T(8,128)(2,1)} %refs_0_.3, bf16[4096,512]{1,0:T(8,128)(2,1)} %refs_1_.3, bf16[4096,512]{1,0:T(8,128)(2,1)} %refs_2_.3, ...), custom_call_target="tpu_custom_call" | custom-call | flops 3221225472 | bytes 15466496 | tf_op jit(solution)/shard_map/pallas_call | solution.py:120
  77.5 3.7 %all-to-all-start = ((bf16[8,128,384]{2,1,0:T(8,128)(2,1)}), bf16[8,128,384]{2,1,0:T(8,128)(2,1)S(1)}, u32[]{:S(2)}, u32[]{:S(2)}) async-start(bf16[8,128,384]{2,1,0:T(8,128)(2,1)} %shard_map.73), calls=%async_computation | async-start | bytes 1572864 | tf_op jit(solution)/shard_map/all_to_all | solution.py:434
  81.2 0.8 copy.9.active_ref
  82.0 1.7 slice.36
  83.7 3.1 %collective-permute-start.12 = (bf16[256,512]{1,0:T(8,128)(2,1)}, bf16[256,512]{1,0:T(8,128)(2,1)}, u32[]{:S(2)}, u32[]{:S(2)}) collective-permute-start(bf16[256,512]{1,0:T(8,128)(2,1)} %slice.36), channel_id=1, source_target_pairs={{0,2},{1,3},{2,0},{3,1},{4,6},{5,7},{6,4},{7,5},{8,10},{9,11},{10,... | collective-permute-start | bytes 786440 | tf_op jit(solution)/shard_map/ppermute | solution.py:398
  86.8 12.1 %shard_map.75 = bf16[8,128,384]{2,1,0:T(8,128)(2,1)} custom-call(s32[1]{0:T(128)} %bitcast.me_ref, f32[4,1024]{1,0:T(4,128)} %reshape.54.gain_ref, s32[256,1]{1,0:T(8,128)} %copy.9.active_ref, bf16[4096,512]{1,0:T(8,128)(2,1)} %refs_0_.3, bf16[4096,512]{1,0:T(8,128)(2,1)} %refs_1_.3, bf16[4096,512]{1,0:T(8,128)(2,1)} %refs_2_.3, bf16[256,1024]{1,0:T(8,128)(2,1)} %copy-done, ...), custom_call_target="tpu_custom_call" | custom-call | flops 3221225472 | bytes 15466496 | tf_op jit(solution)/shard_map/pallas_call | solution.py:120
  98.9 0.8 collective-permute-done.12
  99.7 3.8 %all-to-all-start.1 = ((bf16[8,128,384]{2,1,0:T(8,128)(2,1)}), bf16[8,128,384]{2,1,0:T(8,128)(2,1)S(1)}, u32[]{:S(2)}, u32[]{:S(2)}) async-start(bf16[8,128,384]{2,1,0:T(8,128)(2,1)} %shard_map.75), calls=%async_computation.1 | async-start | bytes 1572864 | tf_op jit(solution)/shard_map/all_to_all | solution.py:434
  103.5 1.0 slice.37
  104.6 0.6 collective-permute-start.13
  105.2 14.6 %collective-permute-done.14 = bf16[256,512]{1,0:T(8,128)(2,1)S(1)} collective-permute-done((bf16[256,512]{1,0:T(8,128)(2,1)S(1)}, bf16[256,512]{1,0:T(8,128)(2,1)S(1)}, u32[]{:S(2)}, u32[]{:S(2)}) %collective-permute-start.14) | collective-permute-done | bytes 262176 | tf_op jit(solution)/shard_map/ppermute | solution.py:398
  120.2 0.4 copy-done.11
  120.5 0.3 copy-done.6
  120.8 0.9 copy-done.18
  121.7 0.6 collective-permute-done.15.refs_3_
  122.3 11.3 %shard_map.76 = bf16[8,256,128]{2,1,0:T(8,128)(2,1)} custom-call(s32[1]{0:T(128)} %bitcast.6.part_ref, bf16[8,128,384]{2,1,0:T(8,128)(2,1)} %copy-done.5, bf16[8,128,384]{2,1,0:T(8,128)(2,1)} %copy-done.18, bf16[8,128,384]{2,1,0:T(8,128)(2,1)} %copy-done.6, bf16[8,128,384]{2,1,0:T(8,128)(2,1)} %collective-permute-done.15.refs_3_), custom_call_target="tpu_custom_call" | custom-call | flops 3623878656 | bytes 4194304 | tf_op jit(solution)/shard_map/pallas_call | solution.py:248
  133.6 2.7 %collective-permute-done.16.refs_1_ = bf16[512,512]{1,0:T(8,128)(2,1)} collective-permute-done((bf16[512,512]{1,0:T(8,128)(2,1)}, bf16[512,512]{1,0:T(8,128)(2,1)}, u32[]{:S(2)}, u32[]{:S(2)}) %collective-permute-start.16) | collective-permute-done | bytes 524320 | tf_op jit(solution)/shard_map/ppermute | solution.py:398
  136.3 4.0 %all-to-all-start.2 = ((bf16[8,256,128]{2,1,0:T(8,128)(2,1)}), bf16[8,256,128]{2,1,0:T(8,128)(2,1)S(1)}, u32[]{:S(2)}, u32[]{:S(2)}) async-start(bf16[8,256,128]{2,1,0:T(8,128)(2,1)} %shard_map.76), calls=%async_computation.2 | async-start | bytes 1048576 | tf_op jit(solution)/shard_map/all_to_all | solution.py:464
  140.3 1.0 constant_dynamic-update-slice_fusion.1
  141.3 1.0 constant_dynamic-update-slice_fusion.refs_2_
  142.3 0.6 collective-permute-start.20
  142.9 7.1 %all-to-all-done.2 = bf16[8,256,128]{2,1,0:T(8,128)(2,1)S(1)} async-done(((bf16[8,256,128]{2,1,0:T(8,128)(2,1)}), bf16[8,256,128]{2,1,0:T(8,128)(2,1)S(1)}, u32[]{:S(2)}, u32[]{:S(2)}) %all-to-all-start.2) | async-done | bytes 524320 | tf_op jit(solution)/shard_map/all_to_all | solution.py:464
  150.1 1.3 collective-permute-start.29
  151.4 4.6 %collective-permute-start.28 = (bf16[4,256,128]{2,1,0:T(8,128)(2,1)S(1)}, bf16[4,256,128]{2,1,0:T(8,128)(2,1)S(1)}, u32[]{:S(2)}, u32[]{:S(2)}) collective-permute-start(bf16[4,256,128]{2,1,0:T(8,128)(2,1)S(1)} %get-tuple-element.79), channel_id=1, source_target_pairs={{0,1},{1,2},{2,3},{4,5},{5,6},{6,7},{8,9},{9,10},{10,11},{12,13},{... | collective-permute-start | bytes 786440 | tf_op jit(solution)/shard_map/ppermute | solution.py:40
  156.0 1.3 collective-permute-start.23
  157.3 4.6 %collective-permute-start.22 = (bf16[4,256,128]{2,1,0:T(8,128)(2,1)S(1)}, bf16[4,256,128]{2,1,0:T(8,128)(2,1)S(1)}, u32[]{:S(2)}, u32[]{:S(2)}) collective-permute-start(bf16[4,256,128]{2,1,0:T(8,128)(2,1)S(1)} %get-tuple-element.80), channel_id=1, source_target_pairs={{0,1},{1,2},{2,3},{4,5},{5,6},{6,7},{8,9},{9,10},{10,11},{12,13},{... | collective-permute-start | bytes 786440 | tf_op jit(solution)/shard_map/ppermute | solution.py:40
  162.0 1.3 collective-permute-start.31
  163.3 1.4 collective-permute-start.30
  164.7 1.3 collective-permute-start.25
  166.0 1.4 collective-permute-start.24
  167.4 5.5 %collective-permute-done.31 = bf16[4,256,128]{2,1,0:T(8,128)(2,1)} collective-permute-done((bf16[4,256,128]{2,1,0:T(8,128)(2,1)S(1)}, bf16[4,256,128]{2,1,0:T(8,128)(2,1)}, u32[]{:S(2)}, u32[]{:S(2)}) %collective-permute-start.31) | collective-permute-done | bytes 262176 | tf_op jit(solution)/shard_map/ppermute | solution.py:41
  172.9 1.3 collective-permute-start.33
  174.3 1.4 collective-permute-start.32
  175.6 4.0 %collective-permute-done.25 = bf16[4,256,128]{2,1,0:T(8,128)(2,1)} collective-permute-done((bf16[4,256,128]{2,1,0:T(8,128)(2,1)S(1)}, bf16[4,256,128]{2,1,0:T(8,128)(2,1)}, u32[]{:S(2)}, u32[]{:S(2)}) %collective-permute-start.25) | collective-permute-done | bytes 262176 | tf_op jit(solution)/shard_map/ppermute | solution.py:41
  179.7 1.3 collective-permute-start.27
  181.0 1.4 collective-permute-start.26
  182.3 0.9 copy.10.active_ref
  183.2 0.5 fusion.at_ref
  183.7 0.6 pad_add_fusion.me_ref
  184.3 3.0 %collective-permute-done.33 = bf16[4,256,128]{2,1,0:T(8,128)(2,1)} collective-permute-done((bf16[4,256,128]{2,1,0:T(8,128)(2,1)}, bf16[4,256,128]{2,1,0:T(8,128)(2,1)}, u32[]{:S(2)}, u32[]{:S(2)}) %collective-permute-start.33) | collective-permute-done | bytes 262176 | tf_op jit(solution)/shard_map/ppermute | solution.py:41
  187.3 4.2 %collective-permute-done.27 = bf16[4,256,128]{2,1,0:T(8,128)(2,1)} collective-permute-done((bf16[4,256,128]{2,1,0:T(8,128)(2,1)}, bf16[4,256,128]{2,1,0:T(8,128)(2,1)}, u32[]{:S(2)}, u32[]{:S(2)}) %collective-permute-start.27) | collective-permute-done | bytes 262176 | tf_op jit(solution)/shard_map/ppermute | solution.py:41
  191.6 7.4 %shard_map.77 = bf16[512,1024]{1,0:T(8,128)(2,1)} custom-call(s32[3]{0:T(128)} %pad_add_fusion.me_ref, s32[16]{0:T(128)} %fusion.at_ref, s32[512,1]{1,0:T(8,128)} %copy.10.active_ref, bf16[512,1024]{1,0:T(8,128)(2,1)} %hidden_ref.1, bf16[512,512]{1,0:T(8,128)(2,1)} %get-tuple-element.63.refs_0_, bf16[512,512]{1,0:T(8,128)(2,1)} %collective-permute-done.16.refs_1_, ...), custom_call_target="tpu_custom_call" | custom-call | flops 2147483648 | bytes 8388608 | tf_op jit(solution)/shard_map/pallas_call | solution.py:334
  (68 shorter events, 1.1 us)
Async XLA Ops:
  0.0 44.3 %copy-start.16 = (f32[4096]{0:T(1024)S(1)}, f32[4096]{0:T(1024)}, u32[]{:S(2)}) copy-start(f32[4096]{0:T(1024)} %param.9) | copy-start | bytes 49156
  0.0 45.0 %copy-start.17 = (s32[512]{0:T(512)S(1)}, s32[512]{0:T(512)}, u32[]{:S(2)}) copy-start(s32[512]{0:T(512)} %param.8) | copy-start | bytes 6148
  1.3 7.7 %copy-start.1 = (bf16[256,1024]{1,0:T(8,128)(2,1)}, bf16[256,1024]{1,0:T(8,128)(2,1)S(1)}, u32[]{:S(2)}) copy-start(bf16[256,1024]{1,0:T(8,128)(2,1)S(1)} %get-tuple-element.78.refs_3_) | copy-start | bytes 1572868
  1.3 76.2 %copy-start = (bf16[256,1024]{1,0:T(8,128)(2,1)}, bf16[256,1024]{1,0:T(8,128)(2,1)S(1)}, u32[]{:S(2)}) copy-start(bf16[256,1024]{1,0:T(8,128)(2,1)S(1)} %get-tuple-element.51.refs_3_) | copy-start | bytes 1572868
  1.3 17.8 %collective-permute-start.1 = (bf16[256,1024]{1,0:T(8,128)(2,1)S(1)}, bf16[256,1024]{1,0:T(8,128)(2,1)}, u32[]{:S(2)}, u32[]{:S(2)}) collective-permute-start(bf16[256,1024]{1,0:T(8,128)(2,1)S(1)} %get-tuple-element.78.refs_3_), channel_id=1, source_target_pairs={{1,0},{2,1},{3,2},{5,4},{6,5},{7,6},{9,8},{10,9},{11,10},{13,12},{... | collective-permute-start | bytes 1572872 | tf_op jit(solution)/shard_map/ppermute | solution.py:41
  2.6 17.9 %collective-permute-start = (bf16[256,1024]{1,0:T(8,128)(2,1)S(1)}, bf16[256,1024]{1,0:T(8,128)(2,1)}, u32[]{:S(2)}, u32[]{:S(2)}) collective-permute-start(bf16[256,1024]{1,0:T(8,128)(2,1)S(1)} %get-tuple-element.78.refs_3_), channel_id=1, source_target_pairs={{0,1},{1,2},{2,3},{4,5},{5,6},{6,7},{8,9},{9,10},{10,11},{12,13},{... | collective-permute-start | bytes 1572872 | tf_op jit(solution)/shard_map/ppermute | solution.py:40
  9.0 21.3 %collective-permute-start.7 = (bf16[256,1024]{1,0:T(8,128)(2,1)S(1)}, bf16[256,1024]{1,0:T(8,128)(2,1)}, u32[]{:S(2)}, u32[]{:S(2)}) collective-permute-start(bf16[256,1024]{1,0:T(8,128)(2,1)S(1)} %get-tuple-element.51.refs_3_), channel_id=1, source_target_pairs={{1,0},{2,1},{3,2},{5,4},{6,5},{7,6},{9,8},{10,9},{11,10},{13,12},{... | collective-permute-start | bytes 1572872 | tf_op jit(solution)/shard_map/ppermute | solution.py:41
  10.3 20.3 %collective-permute-start.6 = (bf16[256,1024]{1,0:T(8,128)(2,1)S(1)}, bf16[256,1024]{1,0:T(8,128)(2,1)}, u32[]{:S(2)}, u32[]{:S(2)}) collective-permute-start(bf16[256,1024]{1,0:T(8,128)(2,1)S(1)} %get-tuple-element.51.refs_3_), channel_id=1, source_target_pairs={{0,1},{1,2},{2,3},{4,5},{5,6},{6,7},{8,9},{9,10},{10,11},{12,13},{... | collective-permute-start | bytes 1572872 | tf_op jit(solution)/shard_map/ppermute | solution.py:40
  19.1 22.5 %collective-permute-start.3 = (bf16[256,1024]{1,0:T(8,128)(2,1)}, bf16[256,1024]{1,0:T(8,128)(2,1)}, u32[]{:S(2)}, u32[]{:S(2)}) collective-permute-start(bf16[256,1024]{1,0:T(8,128)(2,1)} %collective-permute-done.1.refs_5_), channel_id=1, source_target_pairs={{1,0},{2,1},{5,4},{6,5},{9,8},{10,9},{13,12},{14,13},{17,16},{18,1... | collective-permute-start | bytes 1572872 | tf_op jit(solution)/shard_map/ppermute | solution.py:41
  20.5 22.4 %collective-permute-start.2 = (bf16[256,1024]{1,0:T(8,128)(2,1)}, bf16[256,1024]{1,0:T(8,128)(2,1)}, u32[]{:S(2)}, u32[]{:S(2)}) collective-permute-start(bf16[256,1024]{1,0:T(8,128)(2,1)} %collective-permute-done.refs_4_), channel_id=1, source_target_pairs={{1,2},{2,3},{5,6},{6,7},{9,10},{10,11},{13,14},{14,15},{17,18},{18... | collective-permute-start | bytes 1572872 | tf_op jit(solution)/shard_map/ppermute | solution.py:40
  30.6 14.4 %collective-permute-start.8 = (bf16[256,1024]{1,0:T(8,128)(2,1)}, bf16[256,1024]{1,0:T(8,128)(2,1)}, u32[]{:S(2)}, u32[]{:S(2)}) collective-permute-start(bf16[256,1024]{1,0:T(8,128)(2,1)} %collective-permute-done.6.refs_4_), channel_id=1, source_target_pairs={{1,2},{2,3},{5,6},{6,7},{9,10},{10,11},{13,14},{14,15},{17,18},{18... | collective-permute-start | bytes 1572872 | tf_op jit(solution)/shard_map/ppermute | solution.py:40
  32.1 22.1 %collective-permute-start.9 = (bf16[256,1024]{1,0:T(8,128)(2,1)}, bf16[256,1024]{1,0:T(8,128)(2,1)}, u32[]{:S(2)}, u32[]{:S(2)}) collective-permute-start(bf16[256,1024]{1,0:T(8,128)(2,1)} %collective-permute-done.7.refs_5_), channel_id=1, source_target_pairs={{1,0},{2,1},{5,4},{6,5},{9,8},{10,9},{13,12},{14,13},{17,16},{18,1... | collective-permute-start | bytes 1572872 | tf_op jit(solution)/shard_map/ppermute | solution.py:41
  41.6 23.8 %collective-permute-start.5 = (bf16[256,1024]{1,0:T(8,128)(2,1)}, bf16[256,1024]{1,0:T(8,128)(2,1)}, u32[]{:S(2)}, u32[]{:S(2)}) collective-permute-start(bf16[256,1024]{1,0:T(8,128)(2,1)} %collective-permute-done.3.refs_7_), channel_id=1, source_target_pairs={{1,0},{5,4},{9,8},{13,12},{17,16},{21,20},{25,24},{29,28}} | collective-permute-start | bytes 1572872 | tf_op jit(solution)/shard_map/ppermute | solution.py:41
  42.9 22.5 %collective-permute-start.4 = (bf16[256,1024]{1,0:T(8,128)(2,1)}, bf16[256,1024]{1,0:T(8,128)(2,1)}, u32[]{:S(2)}, u32[]{:S(2)}) collective-permute-start(bf16[256,1024]{1,0:T(8,128)(2,1)} %collective-permute-done.2.refs_6_), channel_id=1, source_target_pairs={{2,3},{6,7},{10,11},{14,15},{18,19},{22,23},{26,27},{30,31}} | collective-permute-start | bytes 1572872 | tf_op jit(solution)/shard_map/ppermute | solution.py:40
  45.0 32.5 %collective-permute-start.10 = (bf16[256,1024]{1,0:T(8,128)(2,1)}, bf16[256,1024]{1,0:T(8,128)(2,1)}, u32[]{:S(2)}, u32[]{:S(2)}) collective-permute-start(bf16[256,1024]{1,0:T(8,128)(2,1)} %collective-permute-done.8.refs_6_), channel_id=1, source_target_pairs={{2,3},{6,7},{10,11},{14,15},{18,19},{22,23},{26,27},{30,31}} | collective-permute-start | bytes 1572872 | tf_op jit(solution)/shard_map/ppermute | solution.py:40
  54.2 23.3 %collective-permute-start.11 = (bf16[256,1024]{1,0:T(8,128)(2,1)}, bf16[256,1024]{1,0:T(8,128)(2,1)}, u32[]{:S(2)}, u32[]{:S(2)}) collective-permute-start(bf16[256,1024]{1,0:T(8,128)(2,1)} %collective-permute-done.9.refs_7_), channel_id=1, source_target_pairs={{1,0},{5,4},{9,8},{13,12},{17,16},{21,20},{25,24},{29,28}} | collective-permute-start | bytes 1572872 | tf_op jit(solution)/shard_map/ppermute | solution.py:41
  77.5 22.2 %all-to-all-start = ((bf16[8,128,384]{2,1,0:T(8,128)(2,1)}), bf16[8,128,384]{2,1,0:T(8,128)(2,1)S(1)}, u32[]{:S(2)}, u32[]{:S(2)}) async-start(bf16[8,128,384]{2,1,0:T(8,128)(2,1)} %shard_map.73), calls=%async_computation | async-start | bytes 1572864 | tf_op jit(solution)/shard_map/all_to_all | solution.py:434
  83.7 16.0 %collective-permute-start.12 = (bf16[256,512]{1,0:T(8,128)(2,1)}, bf16[256,512]{1,0:T(8,128)(2,1)}, u32[]{:S(2)}, u32[]{:S(2)}) collective-permute-start(bf16[256,512]{1,0:T(8,128)(2,1)} %slice.36), channel_id=1, source_target_pairs={{0,2},{1,3},{2,0},{3,1},{4,6},{5,7},{6,4},{7,5},{8,10},{9,11},{10,... | collective-permute-start | bytes 786440 | tf_op jit(solution)/shard_map/ppermute | solution.py:398
  99.7 22.6 %copy-start.5 = (bf16[8,128,384]{2,1,0:T(8,128)(2,1)}, bf16[8,128,384]{2,1,0:T(8,128)(2,1)S(1)}, u32[]{:S(2)}) copy-start(bf16[8,128,384]{2,1,0:T(8,128)(2,1)S(1)} %all-to-all-done.refs_0_) | copy-start | bytes 2359300
  99.7 20.1 %all-to-all-start.1 = ((bf16[8,128,384]{2,1,0:T(8,128)(2,1)}), bf16[8,128,384]{2,1,0:T(8,128)(2,1)S(1)}, u32[]{:S(2)}, u32[]{:S(2)}) async-start(bf16[8,128,384]{2,1,0:T(8,128)(2,1)} %shard_map.75), calls=%async_computation.1 | async-start | bytes 1572864 | tf_op jit(solution)/shard_map/all_to_all | solution.py:434
  104.5 15.3 %collective-permute-start.14 = (bf16[256,512]{1,0:T(8,128)(2,1)S(1)}, bf16[256,512]{1,0:T(8,128)(2,1)S(1)}, u32[]{:S(2)}, u32[]{:S(2)}) collective-permute-start(bf16[256,512]{1,0:T(8,128)(2,1)S(1)} %slice.37), channel_id=1, source_target_pairs={{0,2},{1,3},{2,0},{3,1},{4,6},{5,7},{6,4},{7,5},{8,10},{9,11},{10,... | collective-permute-start | bytes 786440 | tf_op jit(solution)/shard_map/ppermute | solution.py:398
  104.6 15.6 %collective-permute-start.13 = (bf16[8,128,384]{2,1,0:T(8,128)(2,1)S(1)}, bf16[8,128,384]{2,1,0:T(8,128)(2,1)S(1)}, u32[]{:S(2)}, u32[]{:S(2)}) collective-permute-start(bf16[8,128,384]{2,1,0:T(8,128)(2,1)S(1)} %all-to-all-done.refs_0_), channel_id=1, source_target_pairs={{0,4},{4,0},{8,12},{12,8},{16,20},{20,16},{24,28},{28,24},{1,5},{5... | collective-permute-start | bytes 2359304 | tf_op jit(solution)/shard_map/ppermute | solution.py:441
  119.8 0.7 copy-start.11
  119.8 1.0 copy-start.6
  119.8 2.5 %collective-permute-start.15 = (bf16[8,128,384]{2,1,0:T(8,128)(2,1)S(1)}, bf16[8,128,384]{2,1,0:T(8,128)(2,1)}, u32[]{:S(2)}, u32[]{:S(2)}) collective-permute-start(bf16[8,128,384]{2,1,0:T(8,128)(2,1)S(1)} %all-to-all-done.1.refs_2_), channel_id=1, source_target_pairs={{0,4},{4,0},{8,12},{12,8},{16,20},{20,16},{24,28},{28,24},{1,5},{5... | collective-permute-start | bytes 2359304 | tf_op jit(solution)/shard_map/ppermute | solution.py:441
  119.9 16.4 %collective-permute-start.16 = (bf16[512,512]{1,0:T(8,128)(2,1)}, bf16[512,512]{1,0:T(8,128)(2,1)}, u32[]{:S(2)}, u32[]{:S(2)}) collective-permute-start(bf16[512,512]{1,0:T(8,128)(2,1)} %get-tuple-element.68), channel_id=1, source_target_pairs={{0,1},{1,2},{2,3},{3,0},{4,5},{5,6},{6,7},{7,4},{8,9},{9,10},{10,1... | collective-permute-start | bytes 1572872 | tf_op jit(solution)/shard_map/ppermute | solution.py:398
  120.8 0.9 copy-start.18
  136.3 13.7 %collective-permute-start.17 = (bf16[512,512]{1,0:T(8,128)(2,1)}, bf16[512,512]{1,0:T(8,128)(2,1)S(1)}, u32[]{:S(2)}, u32[]{:S(2)}) collective-permute-start(bf16[512,512]{1,0:T(8,128)(2,1)} %get-tuple-element.74), channel_id=1, source_target_pairs={{0,3},{1,0},{2,1},{3,2},{4,7},{5,4},{6,5},{7,6},{8,11},{9,8},{10,9... | collective-permute-start | bytes 1572872 | tf_op jit(solution)/shard_map/ppermute | solution.py:398
  136.3 19.7 %collective-permute-start.18 = (bf16[512,512]{1,0:T(8,128)(2,1)}, bf16[512,512]{1,0:T(8,128)(2,1)S(1)}, u32[]{:S(2)}, u32[]{:S(2)}) collective-permute-start(bf16[512,512]{1,0:T(8,128)(2,1)} %get-tuple-element.63.refs_0_), channel_id=1, source_target_pairs={{0,4},{4,0},{8,12},{12,8},{16,20},{20,16},{24,28},{28,24},{1,5},{5... | collective-permute-start | bytes 1572872 | tf_op jit(solution)/shard_map/ppermute | solution.py:474
  136.3 13.7 %all-to-all-start.2 = ((bf16[8,256,128]{2,1,0:T(8,128)(2,1)}), bf16[8,256,128]{2,1,0:T(8,128)(2,1)S(1)}, u32[]{:S(2)}, u32[]{:S(2)}) async-start(bf16[8,256,128]{2,1,0:T(8,128)(2,1)} %shard_map.76), calls=%async_computation.2 | async-start | bytes 1048576 | tf_op jit(solution)/shard_map/all_to_all | solution.py:464
  142.2 49.3 %copy-start.2 = (bf16[512,512]{1,0:T(8,128)(2,1)}, bf16[512,512]{1,0:T(8,128)(2,1)S(1)}, u32[]{:S(2)}) copy-start(bf16[512,512]{1,0:T(8,128)(2,1)S(1)} %constant_dynamic-update-slice_fusion.refs_2_) | copy-start | bytes 1572868
  142.3 15.1 %collective-permute-start.20 = (bf16[512,512]{1,0:T(8,128)(2,1)S(1)}, bf16[512,512]{1,0:T(8,128)(2,1)S(1)}, u32[]{:S(2)}, u32[]{:S(2)}) collective-permute-start(bf16[512,512]{1,0:T(8,128)(2,1)S(1)} %constant_dynamic-update-slice_fusion.refs_2_), channel_id=1, source_target_pairs={{0,4},{4,0},{8,12},{12,8},{16,20},{20,16},{24,28},{28,24},{1,5},{5... | collective-permute-start | bytes 1572872 | tf_op jit(solution)/shard_map/ppermute | solution.py:474
  142.8 19.1 %collective-permute-start.19 = (bf16[512,512]{1,0:T(8,128)(2,1)}, bf16[512,512]{1,0:T(8,128)(2,1)}, u32[]{:S(2)}, u32[]{:S(2)}) collective-permute-start(bf16[512,512]{1,0:T(8,128)(2,1)} %collective-permute-done.16.refs_1_), channel_id=1, source_target_pairs={{0,4},{4,0},{8,12},{12,8},{16,20},{20,16},{24,28},{28,24},{1,5},{5... | collective-permute-start | bytes 1572872 | tf_op jit(solution)/shard_map/ppermute | solution.py:474
  150.0 16.0 %copy-start.7 = (bf16[512,512]{1,0:T(8,128)(2,1)}, bf16[512,512]{1,0:T(8,128)(2,1)S(1)}, u32[]{:S(2)}) copy-start(bf16[512,512]{1,0:T(8,128)(2,1)S(1)} %collective-permute-done.17.refs_3_) | copy-start | bytes 1572868
  150.1 13.2 %copy-start.4 = (bf16[4,256,128]{2,1,0:T(8,128)(2,1)}, bf16[4,256,128]{2,1,0:T(8,128)(2,1)S(1)}, u32[]{:S(2)}) copy-start(bf16[4,256,128]{2,1,0:T(8,128)(2,1)S(1)} %get-tuple-element.80) | copy-start | bytes 786436
  150.1 41.5 %copy-start.3 = (bf16[4,256,128]{2,1,0:T(8,128)(2,1)}, bf16[4,256,128]{2,1,0:T(8,128)(2,1)S(1)}, u32[]{:S(2)}) copy-start(bf16[4,256,128]{2,1,0:T(8,128)(2,1)S(1)} %get-tuple-element.79) | copy-start | bytes 786436
  150.1 11.9 %collective-permute-start.29 = (bf16[4,256,128]{2,1,0:T(8,128)(2,1)S(1)}, bf16[4,256,128]{2,1,0:T(8,128)(2,1)S(1)}, u32[]{:S(2)}, u32[]{:S(2)}) collective-permute-start(bf16[4,256,128]{2,1,0:T(8,128)(2,1)S(1)} %get-tuple-element.79), channel_id=1, source_target_pairs={{1,0},{2,1},{3,2},{5,4},{6,5},{7,6},{9,8},{10,9},{11,10},{13,12},{... | collective-permute-start | bytes 786440 | tf_op jit(solution)/shard_map/ppermute | solution.py:41
  151.4 11.9 %collective-permute-start.28 = (bf16[4,256,128]{2,1,0:T(8,128)(2,1)S(1)}, bf16[4,256,128]{2,1,0:T(8,128)(2,1)S(1)}, u32[]{:S(2)}, u32[]{:S(2)}) collective-permute-start(bf16[4,256,128]{2,1,0:T(8,128)(2,1)S(1)} %get-tuple-element.79), channel_id=1, source_target_pairs={{0,1},{1,2},{2,3},{4,5},{5,6},{6,7},{8,9},{9,10},{10,11},{12,13},{... | collective-permute-start | bytes 786440 | tf_op jit(solution)/shard_map/ppermute | solution.py:40
  156.0 28.3 %copy-start.8 = (bf16[512,512]{1,0:T(8,128)(2,1)}, bf16[512,512]{1,0:T(8,128)(2,1)S(1)}, u32[]{:S(2)}) copy-start(bf16[512,512]{1,0:T(8,128)(2,1)S(1)} %collective-permute-done.18.refs_4_) | copy-start | bytes 1572868
  156.0 8.7 %collective-permute-start.23 = (bf16[4,256,128]{2,1,0:T(8,128)(2,1)S(1)}, bf16[4,256,128]{2,1,0:T(8,128)(2,1)S(1)}, u32[]{:S(2)}, u32[]{:S(2)}) collective-permute-start(bf16[4,256,128]{2,1,0:T(8,128)(2,1)S(1)} %get-tuple-element.80), channel_id=1, source_target_pairs={{1,0},{2,1},{3,2},{5,4},{6,5},{7,6},{9,8},{10,9},{11,10},{13,12},{... | collective-permute-start | bytes 786440 | tf_op jit(solution)/shard_map/ppermute | solution.py:41
  157.3 30.0 %copy-start.9 = (bf16[512,512]{1,0:T(8,128)(2,1)}, bf16[512,512]{1,0:T(8,128)(2,1)S(1)}, u32[]{:S(2)}) copy-start(bf16[512,512]{1,0:T(8,128)(2,1)S(1)} %collective-permute-done.20.refs_6_) | copy-start | bytes 1572868
  157.3 8.7 %collective-permute-start.22 = (bf16[4,256,128]{2,1,0:T(8,128)(2,1)S(1)}, bf16[4,256,128]{2,1,0:T(8,128)(2,1)S(1)}, u32[]{:S(2)}, u32[]{:S(2)}) collective-permute-start(bf16[4,256,128]{2,1,0:T(8,128)(2,1)S(1)} %get-tuple-element.80), channel_id=1, source_target_pairs={{0,1},{1,2},{2,3},{4,5},{5,6},{6,7},{8,9},{9,10},{10,11},{12,13},{... | collective-permute-start | bytes 786440 | tf_op jit(solution)/shard_map/ppermute | solution.py:40
  161.9 22.4 %collective-permute-start.21 = (bf16[512,512]{1,0:T(8,128)(2,1)S(1)}, bf16[512,512]{1,0:T(8,128)(2,1)S(1)}, u32[]{:S(2)}, u32[]{:S(2)}) collective-permute-start(bf16[512,512]{1,0:T(8,128)(2,1)S(1)} %collective-permute-done.17.refs_3_), channel_id=1, source_target_pairs={{0,4},{4,0},{8,12},{12,8},{16,20},{20,16},{24,28},{28,24},{1,5},{5... | collective-permute-start | bytes 1572872 | tf_op jit(solution)/shard_map/ppermute | solution.py:474
  162.0 29.6 %copy-start.12 = (bf16[4,256,128]{2,1,0:T(8,128)(2,1)}, bf16[4,256,128]{2,1,0:T(8,128)(2,1)S(1)}, u32[]{:S(2)}) copy-start(bf16[4,256,128]{2,1,0:T(8,128)(2,1)S(1)} %collective-permute-done.29) | copy-start | bytes 786436
  162.0 10.9 %collective-permute-start.31 = (bf16[4,256,128]{2,1,0:T(8,128)(2,1)S(1)}, bf16[4,256,128]{2,1,0:T(8,128)(2,1)}, u32[]{:S(2)}, u32[]{:S(2)}) collective-permute-start(bf16[4,256,128]{2,1,0:T(8,128)(2,1)S(1)} %collective-permute-done.29), channel_id=1, source_target_pairs={{1,0},{2,1},{5,4},{6,5},{9,8},{10,9},{13,12},{14,13},{17,16},{18,1... | collective-permute-start | bytes 786440 | tf_op jit(solution)/shard_map/ppermute | solution.py:41
  163.3 9.6 %copy-start.13 = (bf16[4,256,128]{2,1,0:T(8,128)(2,1)}, bf16[4,256,128]{2,1,0:T(8,128)(2,1)S(1)}, u32[]{:S(2)}) copy-start(bf16[4,256,128]{2,1,0:T(8,128)(2,1)S(1)} %collective-permute-done.28) | copy-start | bytes 786436
  163.3 10.9 %collective-permute-start.30 = (bf16[4,256,128]{2,1,0:T(8,128)(2,1)S(1)}, bf16[4,256,128]{2,1,0:T(8,128)(2,1)}, u32[]{:S(2)}, u32[]{:S(2)}) collective-permute-start(bf16[4,256,128]{2,1,0:T(8,128)(2,1)S(1)} %collective-permute-done.28), channel_id=1, source_target_pairs={{1,2},{2,3},{5,6},{6,7},{9,10},{10,11},{13,14},{14,15},{17,18},{18... | collective-permute-start | bytes 786440 | tf_op jit(solution)/shard_map/ppermute | solution.py:40
  164.7 9.5 %copy-start.14 = (bf16[4,256,128]{2,1,0:T(8,128)(2,1)}, bf16[4,256,128]{2,1,0:T(8,128)(2,1)S(1)}, u32[]{:S(2)}) copy-start(bf16[4,256,128]{2,1,0:T(8,128)(2,1)S(1)} %collective-permute-done.23) | copy-start | bytes 786436
  164.7 14.9 %collective-permute-start.25 = (bf16[4,256,128]{2,1,0:T(8,128)(2,1)S(1)}, bf16[4,256,128]{2,1,0:T(8,128)(2,1)}, u32[]{:S(2)}, u32[]{:S(2)}) collective-permute-start(bf16[4,256,128]{2,1,0:T(8,128)(2,1)S(1)} %collective-permute-done.23), channel_id=1, source_target_pairs={{1,0},{2,1},{5,4},{6,5},{9,8},{10,9},{13,12},{14,13},{17,16},{18,1... | collective-permute-start | bytes 786440 | tf_op jit(solution)/shard_map/ppermute | solution.py:41
  166.0 13.6 %copy-start.15 = (bf16[4,256,128]{2,1,0:T(8,128)(2,1)}, bf16[4,256,128]{2,1,0:T(8,128)(2,1)S(1)}, u32[]{:S(2)}) copy-start(bf16[4,256,128]{2,1,0:T(8,128)(2,1)S(1)} %collective-permute-done.22) | copy-start | bytes 786436
  166.0 14.9 %collective-permute-start.24 = (bf16[4,256,128]{2,1,0:T(8,128)(2,1)S(1)}, bf16[4,256,128]{2,1,0:T(8,128)(2,1)}, u32[]{:S(2)}, u32[]{:S(2)}) collective-permute-start(bf16[4,256,128]{2,1,0:T(8,128)(2,1)S(1)} %collective-permute-done.22), channel_id=1, source_target_pairs={{1,2},{2,3},{5,6},{6,7},{9,10},{10,11},{13,14},{14,15},{17,18},{18... | collective-permute-start | bytes 786440 | tf_op jit(solution)/shard_map/ppermute | solution.py:40
  172.9 14.4 %collective-permute-start.33 = (bf16[4,256,128]{2,1,0:T(8,128)(2,1)}, bf16[4,256,128]{2,1,0:T(8,128)(2,1)}, u32[]{:S(2)}, u32[]{:S(2)}) collective-permute-start(bf16[4,256,128]{2,1,0:T(8,128)(2,1)} %collective-permute-done.31), channel_id=1, source_target_pairs={{1,0},{5,4},{9,8},{13,12},{17,16},{21,20},{25,24},{29,28}} | collective-permute-start | bytes 786440 | tf_op jit(solution)/shard_map/ppermute | solution.py:41
  174.3 13.1 %collective-permute-start.32 = (bf16[4,256,128]{2,1,0:T(8,128)(2,1)}, bf16[4,256,128]{2,1,0:T(8,128)(2,1)}, u32[]{:S(2)}, u32[]{:S(2)}) collective-permute-start(bf16[4,256,128]{2,1,0:T(8,128)(2,1)} %collective-permute-done.30), channel_id=1, source_target_pairs={{2,3},{6,7},{10,11},{14,15},{18,19},{22,23},{26,27},{30,31}} | collective-permute-start | bytes 786440 | tf_op jit(solution)/shard_map/ppermute | solution.py:40
  179.7 11.9 %collective-permute-start.27 = (bf16[4,256,128]{2,1,0:T(8,128)(2,1)}, bf16[4,256,128]{2,1,0:T(8,128)(2,1)}, u32[]{:S(2)}, u32[]{:S(2)}) collective-permute-start(bf16[4,256,128]{2,1,0:T(8,128)(2,1)} %collective-permute-done.25), channel_id=1, source_target_pairs={{1,0},{5,4},{9,8},{13,12},{17,16},{21,20},{25,24},{29,28}} | collective-permute-start | bytes 786440 | tf_op jit(solution)/shard_map/ppermute | solution.py:41
  181.0 10.6 %collective-permute-start.26 = (bf16[4,256,128]{2,1,0:T(8,128)(2,1)}, bf16[4,256,128]{2,1,0:T(8,128)(2,1)}, u32[]{:S(2)}, u32[]{:S(2)}) collective-permute-start(bf16[4,256,128]{2,1,0:T(8,128)(2,1)} %collective-permute-done.24), channel_id=1, source_target_pairs={{2,3},{6,7},{10,11},{14,15},{18,19},{22,23},{26,27},{30,31}} | collective-permute-start | bytes 786440 | tf_op jit(solution)/shard_map/ppermute | solution.py:40
  184.3 3.0 %copy-start.10 = (bf16[512,512]{1,0:T(8,128)(2,1)}, bf16[512,512]{1,0:T(8,128)(2,1)S(1)}, u32[]{:S(2)}) copy-start(bf16[512,512]{1,0:T(8,128)(2,1)S(1)} %collective-permute-done.21.refs_7_) | copy-start | bytes 1572868

commit v14 on v13

--- a/solution.py
+++ b/solution.py
@@ -355,11 +355,13 @@
 
 
 def share_kernel(place_ref, w_ref, *shares):
-    for step, share in enumerate(shares):
+    for number, share in enumerate(shares):
+        step = number if number < 3 else number - 1
+        first = w_ref.shape[0] // 2 if number == 3 else 0
 
         @pl.when(pl.program_id(0) == step)
         def _():
-            share[...] = w_ref[...]
+            share[...] = w_ref[first : first + share.shape[0], :]
 
 
 def weight_shares(w_out, seq_count, tensor_count, columns):
@@ -369,6 +371,7 @@
     if width % HEAD:
         return None
     cut = lax.axis_index("seq").astype(jnp.int32) % cuts
+    sizes = [depth, depth, depth // 2, depth // 2] + [depth] * (tensor_count - 3)
     place = jnp.stack([lax.axis_index("tensor").astype(jnp.int32), cut])
     return list(
         pl.pallas_call(
@@ -382,20 +385,21 @@
                         lambda j, place: (0, lax.rem(place[0] + j, tensor_count) * cuts + place[1]),
                     )
                 ],
-                out_specs=[pl.BlockSpec((depth, width), lambda j, place: (0, 0))] * tensor_count,
+                out_specs=[pl.BlockSpec((size, width), lambda j, place: (0, 0)) for size in sizes],
             ),
-            out_shape=[jax.ShapeDtypeStruct((depth, width), w_out.dtype)] * tensor_count,
+            out_shape=[jax.ShapeDtypeStruct((size, width), w_out.dtype) for size in sizes],
             compiler_params=pltpu.CompilerParams(vmem_limit_bytes=LIMIT),
         )(place, w_out)
     )
 
 
-def send_share(shares, step, rows=slice(None)):
+def send_share(shares, number):
     if shares is None:
         return None
-    count = len(shares)
+    step = number if number < 3 else number - 1
+    count = len(shares) - 1
     ring = [(d, (d + step) % count) for d in range(count)]
-    return lax.ppermute(shares[step][rows], "tensor", ring)
+    return lax.ppermute(shares[number], "tensor", ring)
 
 
 def output_order(w_out, seq_count, tensor_count, whole):
@@ -450,13 +454,10 @@
         [hidden[:chunk_rows], hidden[chunk_rows:]], tensor_count, cut_weight
     )
     early, second, shares = lax.optimization_barrier((work(first, 0), second, shares))
-    middle = w_out.shape[0] // 2
     sent, early, far, shares = lax.optimization_barrier(
-        (work(second, 1), to_heads(early), send_share(shares, 2, slice(0, middle)), shares)
-    )
-    late, rest = lax.optimization_barrier(
-        (to_heads(sent), send_share(shares, 2, slice(middle, None)))
-    )
+        (work(second, 1), to_heads(early), send_share(shares, 2), shares)
+    )
+    late, rest = lax.optimization_barrier((to_heads(sent), send_share(shares, 3)))
     pieces = to_parts(early) + to_parts(late)
     out, near = lax.optimization_barrier(
         (attend(part, pieces, chunks, group, rows), send_share(shares, 1))
@@ -466,7 +467,7 @@
         weights = [lax.all_to_all(w_out, "tensor", split_axis=1, concat_axis=0, tiled=True)]
     else:
         _, last = lax.optimization_barrier((near, shares))
-        others = [send_share(last, step) for step in range(3, tensor_count)]
+        others = [send_share(last, number) for number in range(4, tensor_count + 1)]
         home, others = lax.optimization_barrier((home, others))
         weights = [shares[0], near, jnp.concatenate([far, rest], axis=0), *others]
         for step in range(1, group):

time: 200 us -> 198 us (0.990)
  local copies, waits for them, and re-layouts: 10.6 us -> 7.99 us
    slice x2 -> x0, local copies, waits for them, and re-layouts: 2.64 us -> none  [send_share(): return lax.ppermute(shares[step][rows], 'tensor', ring)]
  transfers between devices with their start and end apart: 37 -> 37, of which waited for: 16 -> 16; matrix products, arithmetic and copies ran while one was open for 5% -> 3% of each run, Pallas kernels for 20% -> 20%
where the time goes in v14:
time: 198 us; the launch traced here: 197 us
  waiting for transfers between devices  75.3 us (38%)
  starting transfers between devices  63.9 us (32%)
  Pallas kernels  47.2 us (24%)
  local copies, waits for them, and re-layouts  7.99 us (4%)
    ppermute x12, waiting for transfers between devices, line_gather(): from_right = lax.ppermute(last[at][1], 'tensor', left[:count - 1 - step])  48.6 us
    ppermute x12, starting transfers between devices, line_gather(): from_left = lax.ppermute(last[at][0], 'tensor', right[step:])  32.3 us
    pallas_call x2, Pallas kernels, project(): pl.pallas_call(partial(project_kernel, group, count), in_specs=[pl.BlockS...  24.1 us
    ppermute x4, waiting for transfers between devices, send_share(): return lax.ppermute(shares[number], 'tensor', ring)  18.5 us
    ppermute x12, starting transfers between devices, line_gather(): from_right = lax.ppermute(last[at][1], 'tensor', left[:count - 1 - step])  15.4 us
    pallas_call x1, Pallas kernels, attend(): pl.pallas_call(partial(attend_kernel, chunks, group, rows), in_specs=[pl....  11.3 us
    all_to_all x2, starting transfers between devices, to_heads(): return lax.all_to_all(sent, 'seq', split_axis=0, concat_axis=0)  7.58 us
    pallas_call x1, Pallas kernels, output(): pl.pallas_call(partial(output_kernel, group, count, cuts, blocks, halves)...  7.37 us
  transfers between devices with their start and end apart: 37, of which 16 were waited for; matrix products, arithmetic and copies ran while one was open for 3% of the time, Pallas kernels for 20%

profile of v14, /device:TPU:0, one launch (start us, length us, event | category | flops | bytes accessed | tf_op | source)
XLA Modules:
  0.0 196.7 jit_solution(9133722017025656123)
XLA Ops:
  0.0 1.3 fusion.4
  1.3 1.3 collective-permute-start.1
  2.6 6.4 %collective-permute-start = (bf16[256,1024]{1,0:T(8,128)(2,1)S(1)}, bf16[256,1024]{1,0:T(8,128)(2,1)}, u32[]{:S(2)}, u32[]{:S(2)}) collective-permute-start(bf16[256,1024]{1,0:T(8,128)(2,1)S(1)} %get-tuple-element.84.refs_3_), channel_id=1, source_target_pairs={{0,1},{1,2},{2,3},{4,5},{5,6},{6,7},{8,9},{9,10},{10,11},{12,13},{... | collective-permute-start | bytes 1572872 | tf_op jit(solution)/shard_map/ppermute | solution.py:40
  9.0 1.3 collective-permute-start.7
  10.3 5.4 %collective-permute-start.6 = (bf16[256,1024]{1,0:T(8,128)(2,1)S(1)}, bf16[256,1024]{1,0:T(8,128)(2,1)}, u32[]{:S(2)}, u32[]{:S(2)}) collective-permute-start(bf16[256,1024]{1,0:T(8,128)(2,1)S(1)} %get-tuple-element.56.refs_3_), channel_id=1, source_target_pairs={{0,1},{1,2},{2,3},{4,5},{5,6},{6,7},{8,9},{9,10},{10,11},{12,13},{... | collective-permute-start | bytes 1572872 | tf_op jit(solution)/shard_map/ppermute | solution.py:40
  15.6 3.5 %collective-permute-done.1.refs_5_ = bf16[256,1024]{1,0:T(8,128)(2,1)} collective-permute-done((bf16[256,1024]{1,0:T(8,128)(2,1)S(1)}, bf16[256,1024]{1,0:T(8,128)(2,1)}, u32[]{:S(2)}, u32[]{:S(2)}) %collective-permute-start.1) | collective-permute-done | bytes 524320 | tf_op jit(solution)/shard_map/ppermute | solution.py:41
  19.1 1.3 collective-permute-start.3
  20.5 1.4 collective-permute-start.2
  21.9 0.6 pad_add_fusion.1.place_ref
  22.5 4.4 %shard_map.74 = (bf16[512,512]{1,0:T(8,128)(2,1)}, bf16[512,512]{1,0:T(8,128)(2,1)}, bf16[256,512]{1,0:T(8,128)(2,1)}, bf16[256,512]{1,0:T(8,128)(2,1)}, bf16[512,512]{1,0:T(8,128)(2,1)}) custom-call(s32[2]{0:T(128)} %pad_add_fusion.1.place_ref, bf16[512,4096]{1,0:T(8,128)(2,1)} %w_ref.1), custom_call_target="tpu_custom_call" | custom-call | tf_op jit(solution)/shard_map/pallas_call | solution.py:377
  26.9 3.4 %collective-permute-done.7.refs_5_ = bf16[256,1024]{1,0:T(8,128)(2,1)} collective-permute-done((bf16[256,1024]{1,0:T(8,128)(2,1)S(1)}, bf16[256,1024]{1,0:T(8,128)(2,1)}, u32[]{:S(2)}, u32[]{:S(2)}) %collective-permute-start.7) | collective-permute-done | bytes 524320 | tf_op jit(solution)/shard_map/ppermute | solution.py:41
  30.3 0.2 collective-permute-done.6.refs_4_
  30.6 1.5 collective-permute-start.8
  32.0 1.3 collective-permute-start.9
  33.3 8.2 %collective-permute-done.3.refs_7_ = bf16[256,1024]{1,0:T(8,128)(2,1)} collective-permute-done((bf16[256,1024]{1,0:T(8,128)(2,1)}, bf16[256,1024]{1,0:T(8,128)(2,1)}, u32[]{:S(2)}, u32[]{:S(2)}) %collective-permute-start.3) | collective-permute-done | bytes 524320 | tf_op jit(solution)/shard_map/ppermute | solution.py:41
  41.6 1.3 collective-permute-start.5
  42.9 1.5 collective-permute-start.4
  44.3 0.6 reshape.54.gain_ref
  45.0 1.5 collective-permute-start.10
  46.5 7.6 %collective-permute-done.9.refs_7_ = bf16[256,1024]{1,0:T(8,128)(2,1)} collective-permute-done((bf16[256,1024]{1,0:T(8,128)(2,1)}, bf16[256,1024]{1,0:T(8,128)(2,1)}, u32[]{:S(2)}, u32[]{:S(2)}) %collective-permute-start.9) | collective-permute-done | bytes 524320 | tf_op jit(solution)/shard_map/ppermute | solution.py:41
  54.1 1.3 collective-permute-start.11
  55.4 0.8 copy.8.active_ref
  56.2 9.1 %collective-permute-done.5.refs_9_ = bf16[256,1024]{1,0:T(8,128)(2,1)} collective-permute-done((bf16[256,1024]{1,0:T(8,128)(2,1)}, bf16[256,1024]{1,0:T(8,128)(2,1)}, u32[]{:S(2)}, u32[]{:S(2)}) %collective-permute-start.5) | collective-permute-done | bytes 524320 | tf_op jit(solution)/shard_map/ppermute | solution.py:41
  65.4 12.1 %shard_map.73 = bf16[8,128,384]{2,1,0:T(8,128)(2,1)} custom-call(s32[1]{0:T(128)} %bitcast.me_ref, f32[4,1024]{1,0:T(4,128)} %reshape.54.gain_ref, s32[256,1]{1,0:T(8,128)} %copy.8.active_ref, bf16[4096,512]{1,0:T(8,128)(2,1)} %refs_0_.3, bf16[4096,512]{1,0:T(8,128)(2,1)} %refs_1_.3, bf16[4096,512]{1,0:T(8,128)(2,1)} %refs_2_.3, ...), custom_call_target="tpu_custom_call" | custom-call | flops 3221225472 | bytes 15466496 | tf_op jit(solution)/shard_map/pallas_call | solution.py:120
  77.5 3.7 %all-to-all-start = ((bf16[8,128,384]{2,1,0:T(8,128)(2,1)}), bf16[8,128,384]{2,1,0:T(8,128)(2,1)S(1)}, u32[]{:S(2)}, u32[]{:S(2)}) async-start(bf16[8,128,384]{2,1,0:T(8,128)(2,1)} %shard_map.73), calls=%async_computation | async-start | bytes 1572864 | tf_op jit(solution)/shard_map/all_to_all | solution.py:438
  81.2 0.8 copy.9.active_ref
  82.0 3.1 %collective-permute-start.12 = (bf16[256,512]{1,0:T(8,128)(2,1)}, bf16[256,512]{1,0:T(8,128)(2,1)}, u32[]{:S(2)}, u32[]{:S(2)}) collective-permute-start(bf16[256,512]{1,0:T(8,128)(2,1)} %get-tuple-element.64), channel_id=1, source_target_pairs={{0,2},{1,3},{2,0},{3,1},{4,6},{5,7},{6,4},{7,5},{8,10},{9,11},{10,... | collective-permute-start | bytes 786440 | tf_op jit(solution)/shard_map/ppermute | solution.py:402
  85.1 12.1 %shard_map.75 = bf16[8,128,384]{2,1,0:T(8,128)(2,1)} custom-call(s32[1]{0:T(128)} %bitcast.me_ref, f32[4,1024]{1,0:T(4,128)} %reshape.54.gain_ref, s32[256,1]{1,0:T(8,128)} %copy.9.active_ref, bf16[4096,512]{1,0:T(8,128)(2,1)} %refs_0_.3, bf16[4096,512]{1,0:T(8,128)(2,1)} %refs_1_.3, bf16[4096,512]{1,0:T(8,128)(2,1)} %refs_2_.3, bf16[256,1024]{1,0:T(8,128)(2,1)} %copy-done, ...), custom_call_target="tpu_custom_call" | custom-call | flops 3221225472 | bytes 15466496 | tf_op jit(solution)/shard_map/pallas_call | solution.py:120
  97.2 0.8 collective-permute-done.12
  98.0 3.8 %all-to-all-start.1 = ((bf16[8,128,384]{2,1,0:T(8,128)(2,1)}), bf16[8,128,384]{2,1,0:T(8,128)(2,1)S(1)}, u32[]{:S(2)}, u32[]{:S(2)}) async-start(bf16[8,128,384]{2,1,0:T(8,128)(2,1)} %shard_map.75), calls=%async_computation.1 | async-start | bytes 1572864 | tf_op jit(solution)/shard_map/all_to_all | solution.py:438
  101.9 0.5 collective-permute-start.13
  102.4 14.9 %collective-permute-done.14 = bf16[256,512]{1,0:T(8,128)(2,1)S(1)} collective-permute-done((bf16[256,512]{1,0:T(8,128)(2,1)}, bf16[256,512]{1,0:T(8,128)(2,1)S(1)}, u32[]{:S(2)}, u32[]{:S(2)}) %collective-permute-start.14) | collective-permute-done | bytes 262176 | tf_op jit(solution)/shard_map/ppermute | solution.py:402
  117.4 0.2 collective-permute-start.16
  117.7 0.4 copy-done.11
  118.1 0.3 copy-done.6
  118.3 0.9 copy-done.18
  119.2 0.6 collective-permute-done.15.refs_3_
  119.8 11.3 %shard_map.76 = bf16[8,256,128]{2,1,0:T(8,128)(2,1)} custom-call(s32[1]{0:T(128)} %bitcast.6.part_ref, bf16[8,128,384]{2,1,0:T(8,128)(2,1)} %copy-done.5, bf16[8,128,384]{2,1,0:T(8,128)(2,1)} %copy-done.18, bf16[8,128,384]{2,1,0:T(8,128)(2,1)} %copy-done.6, bf16[8,128,384]{2,1,0:T(8,128)(2,1)} %collective-permute-done.15.refs_3_), custom_call_target="tpu_custom_call" | custom-call | flops 3623878656 | bytes 4194304 | tf_op jit(solution)/shard_map/pallas_call | solution.py:248
  131.1 2.8 %collective-permute-done.16.refs_1_ = bf16[512,512]{1,0:T(8,128)(2,1)} collective-permute-done((bf16[512,512]{1,0:T(8,128)(2,1)}, bf16[512,512]{1,0:T(8,128)(2,1)}, u32[]{:S(2)}, u32[]{:S(2)}) %collective-permute-start.16) | collective-permute-done | bytes 524320 | tf_op jit(solution)/shard_map/ppermute | solution.py:402
  133.9 4.0 %all-to-all-start.2 = ((bf16[8,256,128]{2,1,0:T(8,128)(2,1)}), bf16[8,256,128]{2,1,0:T(8,128)(2,1)S(1)}, u32[]{:S(2)}, u32[]{:S(2)}) async-start(bf16[8,256,128]{2,1,0:T(8,128)(2,1)} %shard_map.76), calls=%async_computation.2 | async-start | bytes 1048576 | tf_op jit(solution)/shard_map/all_to_all | solution.py:465
  137.8 1.0 constant_dynamic-update-slice_fusion.1
  138.8 1.0 constant_dynamic-update-slice_fusion.refs_2_
  139.8 0.6 collective-permute-start.20
  140.4 7.1 %all-to-all-done.2 = bf16[8,256,128]{2,1,0:T(8,128)(2,1)S(1)} async-done(((bf16[8,256,128]{2,1,0:T(8,128)(2,1)}), bf16[8,256,128]{2,1,0:T(8,128)(2,1)S(1)}, u32[]{:S(2)}, u32[]{:S(2)}) %all-to-all-start.2) | async-done | bytes 524320 | tf_op jit(solution)/shard_map/all_to_all | solution.py:465
  147.6 1.3 collective-permute-start.29
  148.9 4.6 %collective-permute-start.28 = (bf16[4,256,128]{2,1,0:T(8,128)(2,1)S(1)}, bf16[4,256,128]{2,1,0:T(8,128)(2,1)S(1)}, u32[]{:S(2)}, u32[]{:S(2)}) collective-permute-start(bf16[4,256,128]{2,1,0:T(8,128)(2,1)S(1)} %get-tuple-element.85), channel_id=1, source_target_pairs={{0,1},{1,2},{2,3},{4,5},{5,6},{6,7},{8,9},{9,10},{10,11},{12,13},{... | collective-permute-start | bytes 786440 | tf_op jit(solution)/shard_map/ppermute | solution.py:40
  153.5 1.3 collective-permute-start.23
  154.9 4.6 %collective-permute-start.22 = (bf16[4,256,128]{2,1,0:T(8,128)(2,1)S(1)}, bf16[4,256,128]{2,1,0:T(8,128)(2,1)S(1)}, u32[]{:S(2)}, u32[]{:S(2)}) collective-permute-start(bf16[4,256,128]{2,1,0:T(8,128)(2,1)S(1)} %get-tuple-element.86), channel_id=1, source_target_pairs={{0,1},{1,2},{2,3},{4,5},{5,6},{6,7},{8,9},{9,10},{10,11},{12,13},{... | collective-permute-start | bytes 786440 | tf_op jit(solution)/shard_map/ppermute | solution.py:40
  159.5 1.3 collective-permute-start.31
  160.9 1.4 collective-permute-start.30
  162.2 1.3 collective-permute-start.25
  163.6 1.4 collective-permute-start.24
  164.9 5.5 %collective-permute-done.31 = bf16[4,256,128]{2,1,0:T(8,128)(2,1)} collective-permute-done((bf16[4,256,128]{2,1,0:T(8,128)(2,1)S(1)}, bf16[4,256,128]{2,1,0:T(8,128)(2,1)}, u32[]{:S(2)}, u32[]{:S(2)}) %collective-permute-start.31) | collective-permute-done | bytes 262176 | tf_op jit(solution)/shard_map/ppermute | solution.py:41
  170.5 1.3 collective-permute-start.33
  171.8 1.4 collective-permute-start.32
  173.2 4.0 %collective-permute-done.25 = bf16[4,256,128]{2,1,0:T(8,128)(2,1)} collective-permute-done((bf16[4,256,128]{2,1,0:T(8,128)(2,1)S(1)}, bf16[4,256,128]{2,1,0:T(8,128)(2,1)}, u32[]{:S(2)}, u32[]{:S(2)}) %collective-permute-start.25) | collective-permute-done | bytes 262176 | tf_op jit(solution)/shard_map/ppermute | solution.py:41
  177.1 1.3 collective-permute-start.27
  178.4 1.4 collective-permute-start.26
  179.8 0.9 copy.10.active_ref
  180.7 0.5 fusion.at_ref
  181.2 0.6 pad_add_fusion.me_ref
  181.9 3.0 %collective-permute-done.33 = bf16[4,256,128]{2,1,0:T(8,128)(2,1)} collective-permute-done((bf16[4,256,128]{2,1,0:T(8,128)(2,1)}, bf16[4,256,128]{2,1,0:T(8,128)(2,1)}, u32[]{:S(2)}, u32[]{:S(2)}) %collective-permute-start.33) | collective-permute-done | bytes 262176 | tf_op jit(solution)/shard_map/ppermute | solution.py:41
  184.8 4.2 %collective-permute-done.27 = bf16[4,256,128]{2,1,0:T(8,128)(2,1)} collective-permute-done((bf16[4,256,128]{2,1,0:T(8,128)(2,1)}, bf16[4,256,128]{2,1,0:T(8,128)(2,1)}, u32[]{:S(2)}, u32[]{:S(2)}) %collective-permute-start.27) | collective-permute-done | bytes 262176 | tf_op jit(solution)/shard_map/ppermute | solution.py:41
  189.1 7.4 %shard_map.77 = bf16[512,1024]{1,0:T(8,128)(2,1)} custom-call(s32[3]{0:T(128)} %pad_add_fusion.me_ref, s32[16]{0:T(128)} %fusion.at_ref, s32[512,1]{1,0:T(8,128)} %copy.10.active_ref, bf16[512,1024]{1,0:T(8,128)(2,1)} %hidden_ref.1, bf16[512,512]{1,0:T(8,128)(2,1)} %get-tuple-element.69.refs_0_, bf16[512,512]{1,0:T(8,128)(2,1)} %collective-permute-done.16.refs_1_, ...), custom_call_target="tpu_custom_call" | custom-call | flops 2147483648 | bytes 8388608 | tf_op jit(solution)/shard_map/pallas_call | solution.py:334
  (66 shorter events, 0.5 us)
Async XLA Ops:
  0.0 44.3 %copy-start.16 = (f32[4096]{0:T(1024)S(1)}, f32[4096]{0:T(1024)}, u32[]{:S(2)}) copy-start(f32[4096]{0:T(1024)} %param.9) | copy-start | bytes 49156
  0.0 45.0 %copy-start.17 = (s32[512]{0:T(512)S(1)}, s32[512]{0:T(512)}, u32[]{:S(2)}) copy-start(s32[512]{0:T(512)} %param.8) | copy-start | bytes 6148
  1.3 7.7 %copy-start.1 = (bf16[256,1024]{1,0:T(8,128)(2,1)}, bf16[256,1024]{1,0:T(8,128)(2,1)S(1)}, u32[]{:S(2)}) copy-start(bf16[256,1024]{1,0:T(8,128)(2,1)S(1)} %get-tuple-element.84.refs_3_) | copy-start | bytes 1572868
  1.3 76.1 %copy-start = (bf16[256,1024]{1,0:T(8,128)(2,1)}, bf16[256,1024]{1,0:T(8,128)(2,1)S(1)}, u32[]{:S(2)}) copy-start(bf16[256,1024]{1,0:T(8,128)(2,1)S(1)} %get-tuple-element.56.refs_3_) | copy-start | bytes 1572868
  1.3 17.8 %collective-permute-start.1 = (bf16[256,1024]{1,0:T(8,128)(2,1)S(1)}, bf16[256,1024]{1,0:T(8,128)(2,1)}, u32[]{:S(2)}, u32[]{:S(2)}) collective-permute-start(bf16[256,1024]{1,0:T(8,128)(2,1)S(1)} %get-tuple-element.84.refs_3_), channel_id=1, source_target_pairs={{1,0},{2,1},{3,2},{5,4},{6,5},{7,6},{9,8},{10,9},{11,10},{13,12},{... | collective-permute-start | bytes 1572872 | tf_op jit(solution)/shard_map/ppermute | solution.py:41
  2.6 17.9 %collective-permute-start = (bf16[256,1024]{1,0:T(8,128)(2,1)S(1)}, bf16[256,1024]{1,0:T(8,128)(2,1)}, u32[]{:S(2)}, u32[]{:S(2)}) collective-permute-start(bf16[256,1024]{1,0:T(8,128)(2,1)S(1)} %get-tuple-element.84.refs_3_), channel_id=1, source_target_pairs={{0,1},{1,2},{2,3},{4,5},{5,6},{6,7},{8,9},{9,10},{10,11},{12,13},{... | collective-permute-start | bytes 1572872 | tf_op jit(solution)/shard_map/ppermute | solution.py:40
  9.0 21.3 %collective-permute-start.7 = (bf16[256,1024]{1,0:T(8,128)(2,1)S(1)}, bf16[256,1024]{1,0:T(8,128)(2,1)}, u32[]{:S(2)}, u32[]{:S(2)}) collective-permute-start(bf16[256,1024]{1,0:T(8,128)(2,1)S(1)} %get-tuple-element.56.refs_3_), channel_id=1, source_target_pairs={{1,0},{2,1},{3,2},{5,4},{6,5},{7,6},{9,8},{10,9},{11,10},{13,12},{... | collective-permute-start | bytes 1572872 | tf_op jit(solution)/shard_map/ppermute | solution.py:41
  10.3 20.3 %collective-permute-start.6 = (bf16[256,1024]{1,0:T(8,128)(2,1)S(1)}, bf16[256,1024]{1,0:T(8,128)(2,1)}, u32[]{:S(2)}, u32[]{:S(2)}) collective-permute-start(bf16[256,1024]{1,0:T(8,128)(2,1)S(1)} %get-tuple-element.56.refs_3_), channel_id=1, source_target_pairs={{0,1},{1,2},{2,3},{4,5},{5,6},{6,7},{8,9},{9,10},{10,11},{12,13},{... | collective-permute-start | bytes 1572872 | tf_op jit(solution)/shard_map/ppermute | solution.py:40
  19.1 22.5 %collective-permute-start.3 = (bf16[256,1024]{1,0:T(8,128)(2,1)}, bf16[256,1024]{1,0:T(8,128)(2,1)}, u32[]{:S(2)}, u32[]{:S(2)}) collective-permute-start(bf16[256,1024]{1,0:T(8,128)(2,1)} %collective-permute-done.1.refs_5_), channel_id=1, source_target_pairs={{1,0},{2,1},{5,4},{6,5},{9,8},{10,9},{13,12},{14,13},{17,16},{18,1... | collective-permute-start | bytes 1572872 | tf_op jit(solution)/shard_map/ppermute | solution.py:41
  20.5 22.4 %collective-permute-start.2 = (bf16[256,1024]{1,0:T(8,128)(2,1)}, bf16[256,1024]{1,0:T(8,128)(2,1)}, u32[]{:S(2)}, u32[]{:S(2)}) collective-permute-start(bf16[256,1024]{1,0:T(8,128)(2,1)} %collective-permute-done.refs_4_), channel_id=1, source_target_pairs={{1,2},{2,3},{5,6},{6,7},{9,10},{10,11},{13,14},{14,15},{17,18},{18... | collective-permute-start | bytes 1572872 | tf_op jit(solution)/shard_map/ppermute | solution.py:40
  30.6 14.4 %collective-permute-start.8 = (bf16[256,1024]{1,0:T(8,128)(2,1)}, bf16[256,1024]{1,0:T(8,128)(2,1)}, u32[]{:S(2)}, u32[]{:S(2)}) collective-permute-start(bf16[256,1024]{1,0:T(8,128)(2,1)} %collective-permute-done.6.refs_4_), channel_id=1, source_target_pairs={{1,2},{2,3},{5,6},{6,7},{9,10},{10,11},{13,14},{14,15},{17,18},{18... | collective-permute-start | bytes 1572872 | tf_op jit(solution)/shard_map/ppermute | solution.py:40
  32.0 22.1 %collective-permute-start.9 = (bf16[256,1024]{1,0:T(8,128)(2,1)}, bf16[256,1024]{1,0:T(8,128)(2,1)}, u32[]{:S(2)}, u32[]{:S(2)}) collective-permute-start(bf16[256,1024]{1,0:T(8,128)(2,1)} %collective-permute-done.7.refs_5_), channel_id=1, source_target_pairs={{1,0},{2,1},{5,4},{6,5},{9,8},{10,9},{13,12},{14,13},{17,16},{18,1... | collective-permute-start | bytes 1572872 | tf_op jit(solution)/shard_map/ppermute | solution.py:41
  41.6 23.8 %collective-permute-start.5 = (bf16[256,1024]{1,0:T(8,128)(2,1)}, bf16[256,1024]{1,0:T(8,128)(2,1)}, u32[]{:S(2)}, u32[]{:S(2)}) collective-permute-start(bf16[256,1024]{1,0:T(8,128)(2,1)} %collective-permute-done.3.refs_7_), channel_id=1, source_target_pairs={{1,0},{5,4},{9,8},{13,12},{17,16},{21,20},{25,24},{29,28}} | collective-permute-start | bytes 1572872 | tf_op jit(solution)/shard_map/ppermute | solution.py:41
  42.9 22.5 %collective-permute-start.4 = (bf16[256,1024]{1,0:T(8,128)(2,1)}, bf16[256,1024]{1,0:T(8,128)(2,1)}, u32[]{:S(2)}, u32[]{:S(2)}) collective-permute-start(bf16[256,1024]{1,0:T(8,128)(2,1)} %collective-permute-done.2.refs_6_), channel_id=1, source_target_pairs={{2,3},{6,7},{10,11},{14,15},{18,19},{22,23},{26,27},{30,31}} | collective-permute-start | bytes 1572872 | tf_op jit(solution)/shard_map/ppermute | solution.py:40
  45.0 32.5 %collective-permute-start.10 = (bf16[256,1024]{1,0:T(8,128)(2,1)}, bf16[256,1024]{1,0:T(8,128)(2,1)}, u32[]{:S(2)}, u32[]{:S(2)}) collective-permute-start(bf16[256,1024]{1,0:T(8,128)(2,1)} %collective-permute-done.8.refs_6_), channel_id=1, source_target_pairs={{2,3},{6,7},{10,11},{14,15},{18,19},{22,23},{26,27},{30,31}} | collective-permute-start | bytes 1572872 | tf_op jit(solution)/shard_map/ppermute | solution.py:40
  54.1 23.3 %collective-permute-start.11 = (bf16[256,1024]{1,0:T(8,128)(2,1)}, bf16[256,1024]{1,0:T(8,128)(2,1)}, u32[]{:S(2)}, u32[]{:S(2)}) collective-permute-start(bf16[256,1024]{1,0:T(8,128)(2,1)} %collective-permute-done.9.refs_7_), channel_id=1, source_target_pairs={{1,0},{5,4},{9,8},{13,12},{17,16},{21,20},{25,24},{29,28}} | collective-permute-start | bytes 1572872 | tf_op jit(solution)/shard_map/ppermute | solution.py:41
  77.5 20.6 %all-to-all-start = ((bf16[8,128,384]{2,1,0:T(8,128)(2,1)}), bf16[8,128,384]{2,1,0:T(8,128)(2,1)S(1)}, u32[]{:S(2)}, u32[]{:S(2)}) async-start(bf16[8,128,384]{2,1,0:T(8,128)(2,1)} %shard_map.73), calls=%async_computation | async-start | bytes 1572864 | tf_op jit(solution)/shard_map/all_to_all | solution.py:438
  82.0 16.1 %collective-permute-start.12 = (bf16[256,512]{1,0:T(8,128)(2,1)}, bf16[256,512]{1,0:T(8,128)(2,1)}, u32[]{:S(2)}, u32[]{:S(2)}) collective-permute-start(bf16[256,512]{1,0:T(8,128)(2,1)} %get-tuple-element.64), channel_id=1, source_target_pairs={{0,2},{1,3},{2,0},{3,1},{4,6},{5,7},{6,4},{7,5},{8,10},{9,11},{10,... | collective-permute-start | bytes 786440 | tf_op jit(solution)/shard_map/ppermute | solution.py:402
  98.0 21.8 %copy-start.5 = (bf16[8,128,384]{2,1,0:T(8,128)(2,1)}, bf16[8,128,384]{2,1,0:T(8,128)(2,1)S(1)}, u32[]{:S(2)}) copy-start(bf16[8,128,384]{2,1,0:T(8,128)(2,1)S(1)} %all-to-all-done.refs_0_) | copy-start | bytes 2359300
  98.0 19.3 %all-to-all-start.1 = ((bf16[8,128,384]{2,1,0:T(8,128)(2,1)}), bf16[8,128,384]{2,1,0:T(8,128)(2,1)S(1)}, u32[]{:S(2)}, u32[]{:S(2)}) async-start(bf16[8,128,384]{2,1,0:T(8,128)(2,1)} %shard_map.75), calls=%async_computation.1 | async-start | bytes 1572864 | tf_op jit(solution)/shard_map/all_to_all | solution.py:438
  101.9 15.4 %collective-permute-start.14 = (bf16[256,512]{1,0:T(8,128)(2,1)}, bf16[256,512]{1,0:T(8,128)(2,1)S(1)}, u32[]{:S(2)}, u32[]{:S(2)}) collective-permute-start(bf16[256,512]{1,0:T(8,128)(2,1)} %get-tuple-element.72), channel_id=1, source_target_pairs={{0,2},{1,3},{2,0},{3,1},{4,6},{5,7},{6,4},{7,5},{8,10},{9,11},{10,... | collective-permute-start | bytes 786440 | tf_op jit(solution)/shard_map/ppermute | solution.py:402
  101.9 15.8 %collective-permute-start.13 = (bf16[8,128,384]{2,1,0:T(8,128)(2,1)S(1)}, bf16[8,128,384]{2,1,0:T(8,128)(2,1)S(1)}, u32[]{:S(2)}, u32[]{:S(2)}) collective-permute-start(bf16[8,128,384]{2,1,0:T(8,128)(2,1)S(1)} %all-to-all-done.refs_0_), channel_id=1, source_target_pairs={{0,4},{4,0},{8,12},{12,8},{16,20},{20,16},{24,28},{28,24},{1,5},{5... | collective-permute-start | bytes 2359304 | tf_op jit(solution)/shard_map/ppermute | solution.py:445
  117.3 0.7 copy-start.11
  117.3 1.0 copy-start.6
  117.3 2.5 %collective-permute-start.15 = (bf16[8,128,384]{2,1,0:T(8,128)(2,1)S(1)}, bf16[8,128,384]{2,1,0:T(8,128)(2,1)}, u32[]{:S(2)}, u32[]{:S(2)}) collective-permute-start(bf16[8,128,384]{2,1,0:T(8,128)(2,1)S(1)} %all-to-all-done.1.refs_2_), channel_id=1, source_target_pairs={{0,4},{4,0},{8,12},{12,8},{16,20},{20,16},{24,28},{28,24},{1,5},{5... | collective-permute-start | bytes 2359304 | tf_op jit(solution)/shard_map/ppermute | solution.py:445
  117.4 16.4 %collective-permute-start.16 = (bf16[512,512]{1,0:T(8,128)(2,1)}, bf16[512,512]{1,0:T(8,128)(2,1)}, u32[]{:S(2)}, u32[]{:S(2)}) collective-permute-start(bf16[512,512]{1,0:T(8,128)(2,1)} %get-tuple-element.74), channel_id=1, source_target_pairs={{0,1},{1,2},{2,3},{3,0},{4,5},{5,6},{6,7},{7,4},{8,9},{9,10},{10,1... | collective-permute-start | bytes 1572872 | tf_op jit(solution)/shard_map/ppermute | solution.py:402
  118.3 0.9 copy-start.18
  133.9 13.7 %collective-permute-start.17 = (bf16[512,512]{1,0:T(8,128)(2,1)}, bf16[512,512]{1,0:T(8,128)(2,1)S(1)}, u32[]{:S(2)}, u32[]{:S(2)}) collective-permute-start(bf16[512,512]{1,0:T(8,128)(2,1)} %get-tuple-element.80), channel_id=1, source_target_pairs={{0,3},{1,0},{2,1},{3,2},{4,7},{5,4},{6,5},{7,6},{8,11},{9,8},{10,9... | collective-permute-start | bytes 1572872 | tf_op jit(solution)/shard_map/ppermute | solution.py:402
  133.9 19.7 %collective-permute-start.18 = (bf16[512,512]{1,0:T(8,128)(2,1)}, bf16[512,512]{1,0:T(8,128)(2,1)S(1)}, u32[]{:S(2)}, u32[]{:S(2)}) collective-permute-start(bf16[512,512]{1,0:T(8,128)(2,1)} %get-tuple-element.69.refs_0_), channel_id=1, source_target_pairs={{0,4},{4,0},{8,12},{12,8},{16,20},{20,16},{24,28},{28,24},{1,5},{5... | collective-permute-start | bytes 1572872 | tf_op jit(solution)/shard_map/ppermute | solution.py:475
  133.9 13.7 %all-to-all-start.2 = ((bf16[8,256,128]{2,1,0:T(8,128)(2,1)}), bf16[8,256,128]{2,1,0:T(8,128)(2,1)S(1)}, u32[]{:S(2)}, u32[]{:S(2)}) async-start(bf16[8,256,128]{2,1,0:T(8,128)(2,1)} %shard_map.76), calls=%async_computation.2 | async-start | bytes 1048576 | tf_op jit(solution)/shard_map/all_to_all | solution.py:465
  139.8 49.3 %copy-start.2 = (bf16[512,512]{1,0:T(8,128)(2,1)}, bf16[512,512]{1,0:T(8,128)(2,1)S(1)}, u32[]{:S(2)}) copy-start(bf16[512,512]{1,0:T(8,128)(2,1)S(1)} %constant_dynamic-update-slice_fusion.refs_2_) | copy-start | bytes 1572868
  139.8 15.1 %collective-permute-start.20 = (bf16[512,512]{1,0:T(8,128)(2,1)S(1)}, bf16[512,512]{1,0:T(8,128)(2,1)S(1)}, u32[]{:S(2)}, u32[]{:S(2)}) collective-permute-start(bf16[512,512]{1,0:T(8,128)(2,1)S(1)} %constant_dynamic-update-slice_fusion.refs_2_), channel_id=1, source_target_pairs={{0,4},{4,0},{8,12},{12,8},{16,20},{20,16},{24,28},{28,24},{1,5},{5... | collective-permute-start | bytes 1572872 | tf_op jit(solution)/shard_map/ppermute | solution.py:475
  140.3 19.1 %collective-permute-start.19 = (bf16[512,512]{1,0:T(8,128)(2,1)}, bf16[512,512]{1,0:T(8,128)(2,1)}, u32[]{:S(2)}, u32[]{:S(2)}) collective-permute-start(bf16[512,512]{1,0:T(8,128)(2,1)} %collective-permute-done.16.refs_1_), channel_id=1, source_target_pairs={{0,4},{4,0},{8,12},{12,8},{16,20},{20,16},{24,28},{28,24},{1,5},{5... | collective-permute-start | bytes 1572872 | tf_op jit(solution)/shard_map/ppermute | solution.py:475
  147.6 16.0 %copy-start.7 = (bf16[512,512]{1,0:T(8,128)(2,1)}, bf16[512,512]{1,0:T(8,128)(2,1)S(1)}, u32[]{:S(2)}) copy-start(bf16[512,512]{1,0:T(8,128)(2,1)S(1)} %collective-permute-done.17.refs_3_) | copy-start | bytes 1572868
  147.6 13.2 %copy-start.4 = (bf16[4,256,128]{2,1,0:T(8,128)(2,1)}, bf16[4,256,128]{2,1,0:T(8,128)(2,1)S(1)}, u32[]{:S(2)}) copy-start(bf16[4,256,128]{2,1,0:T(8,128)(2,1)S(1)} %get-tuple-element.86) | copy-start | bytes 786436
  147.6 41.5 %copy-start.3 = (bf16[4,256,128]{2,1,0:T(8,128)(2,1)}, bf16[4,256,128]{2,1,0:T(8,128)(2,1)S(1)}, u32[]{:S(2)}) copy-start(bf16[4,256,128]{2,1,0:T(8,128)(2,1)S(1)} %get-tuple-element.85) | copy-start | bytes 786436
  147.6 11.9 %collective-permute-start.29 = (bf16[4,256,128]{2,1,0:T(8,128)(2,1)S(1)}, bf16[4,256,128]{2,1,0:T(8,128)(2,1)S(1)}, u32[]{:S(2)}, u32[]{:S(2)}) collective-permute-start(bf16[4,256,128]{2,1,0:T(8,128)(2,1)S(1)} %get-tuple-element.85), channel_id=1, source_target_pairs={{1,0},{2,1},{3,2},{5,4},{6,5},{7,6},{9,8},{10,9},{11,10},{13,12},{... | collective-permute-start | bytes 786440 | tf_op jit(solution)/shard_map/ppermute | solution.py:41
  148.9 11.9 %collective-permute-start.28 = (bf16[4,256,128]{2,1,0:T(8,128)(2,1)S(1)}, bf16[4,256,128]{2,1,0:T(8,128)(2,1)S(1)}, u32[]{:S(2)}, u32[]{:S(2)}) collective-permute-start(bf16[4,256,128]{2,1,0:T(8,128)(2,1)S(1)} %get-tuple-element.85), channel_id=1, source_target_pairs={{0,1},{1,2},{2,3},{4,5},{5,6},{6,7},{8,9},{9,10},{10,11},{12,13},{... | collective-permute-start | bytes 786440 | tf_op jit(solution)/shard_map/ppermute | solution.py:40
  153.5 28.3 %copy-start.8 = (bf16[512,512]{1,0:T(8,128)(2,1)}, bf16[512,512]{1,0:T(8,128)(2,1)S(1)}, u32[]{:S(2)}) copy-start(bf16[512,512]{1,0:T(8,128)(2,1)S(1)} %collective-permute-done.18.refs_4_) | copy-start | bytes 1572868
  153.5 8.7 %collective-permute-start.23 = (bf16[4,256,128]{2,1,0:T(8,128)(2,1)S(1)}, bf16[4,256,128]{2,1,0:T(8,128)(2,1)S(1)}, u32[]{:S(2)}, u32[]{:S(2)}) collective-permute-start(bf16[4,256,128]{2,1,0:T(8,128)(2,1)S(1)} %get-tuple-element.86), channel_id=1, source_target_pairs={{1,0},{2,1},{3,2},{5,4},{6,5},{7,6},{9,8},{10,9},{11,10},{13,12},{... | collective-permute-start | bytes 786440 | tf_op jit(solution)/shard_map/ppermute | solution.py:41
  154.8 30.0 %copy-start.9 = (bf16[512,512]{1,0:T(8,128)(2,1)}, bf16[512,512]{1,0:T(8,128)(2,1)S(1)}, u32[]{:S(2)}) copy-start(bf16[512,512]{1,0:T(8,128)(2,1)S(1)} %collective-permute-done.20.refs_6_) | copy-start | bytes 1572868
  154.9 8.7 %collective-permute-start.22 = (bf16[4,256,128]{2,1,0:T(8,128)(2,1)S(1)}, bf16[4,256,128]{2,1,0:T(8,128)(2,1)S(1)}, u32[]{:S(2)}, u32[]{:S(2)}) collective-permute-start(bf16[4,256,128]{2,1,0:T(8,128)(2,1)S(1)} %get-tuple-element.86), channel_id=1, source_target_pairs={{0,1},{1,2},{2,3},{4,5},{5,6},{6,7},{8,9},{9,10},{10,11},{12,13},{... | collective-permute-start | bytes 786440 | tf_op jit(solution)/shard_map/ppermute | solution.py:40
  159.4 22.4 %collective-permute-start.21 = (bf16[512,512]{1,0:T(8,128)(2,1)S(1)}, bf16[512,512]{1,0:T(8,128)(2,1)S(1)}, u32[]{:S(2)}, u32[]{:S(2)}) collective-permute-start(bf16[512,512]{1,0:T(8,128)(2,1)S(1)} %collective-permute-done.17.refs_3_), channel_id=1, source_target_pairs={{0,4},{4,0},{8,12},{12,8},{16,20},{20,16},{24,28},{28,24},{1,5},{5... | collective-permute-start | bytes 1572872 | tf_op jit(solution)/shard_map/ppermute | solution.py:475
  159.5 29.6 %copy-start.12 = (bf16[4,256,128]{2,1,0:T(8,128)(2,1)}, bf16[4,256,128]{2,1,0:T(8,128)(2,1)S(1)}, u32[]{:S(2)}) copy-start(bf16[4,256,128]{2,1,0:T(8,128)(2,1)S(1)} %collective-permute-done.29) | copy-start | bytes 786436
  159.5 10.9 %collective-permute-start.31 = (bf16[4,256,128]{2,1,0:T(8,128)(2,1)S(1)}, bf16[4,256,128]{2,1,0:T(8,128)(2,1)}, u32[]{:S(2)}, u32[]{:S(2)}) collective-permute-start(bf16[4,256,128]{2,1,0:T(8,128)(2,1)S(1)} %collective-permute-done.29), channel_id=1, source_target_pairs={{1,0},{2,1},{5,4},{6,5},{9,8},{10,9},{13,12},{14,13},{17,16},{18,1... | collective-permute-start | bytes 786440 | tf_op jit(solution)/shard_map/ppermute | solution.py:41
  160.9 9.6 %copy-start.13 = (bf16[4,256,128]{2,1,0:T(8,128)(2,1)}, bf16[4,256,128]{2,1,0:T(8,128)(2,1)S(1)}, u32[]{:S(2)}) copy-start(bf16[4,256,128]{2,1,0:T(8,128)(2,1)S(1)} %collective-permute-done.28) | copy-start | bytes 786436
  160.9 10.9 %collective-permute-start.30 = (bf16[4,256,128]{2,1,0:T(8,128)(2,1)S(1)}, bf16[4,256,128]{2,1,0:T(8,128)(2,1)}, u32[]{:S(2)}, u32[]{:S(2)}) collective-permute-start(bf16[4,256,128]{2,1,0:T(8,128)(2,1)S(1)} %collective-permute-done.28), channel_id=1, source_target_pairs={{1,2},{2,3},{5,6},{6,7},{9,10},{10,11},{13,14},{14,15},{17,18},{18... | collective-permute-start | bytes 786440 | tf_op jit(solution)/shard_map/ppermute | solution.py:40
  162.2 9.5 %copy-start.14 = (bf16[4,256,128]{2,1,0:T(8,128)(2,1)}, bf16[4,256,128]{2,1,0:T(8,128)(2,1)S(1)}, u32[]{:S(2)}) copy-start(bf16[4,256,128]{2,1,0:T(8,128)(2,1)S(1)} %collective-permute-done.23) | copy-start | bytes 786436
  162.2 14.9 %collective-permute-start.25 = (bf16[4,256,128]{2,1,0:T(8,128)(2,1)S(1)}, bf16[4,256,128]{2,1,0:T(8,128)(2,1)}, u32[]{:S(2)}, u32[]{:S(2)}) collective-permute-start(bf16[4,256,128]{2,1,0:T(8,128)(2,1)S(1)} %collective-permute-done.23), channel_id=1, source_target_pairs={{1,0},{2,1},{5,4},{6,5},{9,8},{10,9},{13,12},{14,13},{17,16},{18,1... | collective-permute-start | bytes 786440 | tf_op jit(solution)/shard_map/ppermute | solution.py:41
  163.5 13.6 %copy-start.15 = (bf16[4,256,128]{2,1,0:T(8,128)(2,1)}, bf16[4,256,128]{2,1,0:T(8,128)(2,1)S(1)}, u32[]{:S(2)}) copy-start(bf16[4,256,128]{2,1,0:T(8,128)(2,1)S(1)} %collective-permute-done.22) | copy-start | bytes 786436
  163.6 14.9 %collective-permute-start.24 = (bf16[4,256,128]{2,1,0:T(8,128)(2,1)S(1)}, bf16[4,256,128]{2,1,0:T(8,128)(2,1)}, u32[]{:S(2)}, u32[]{:S(2)}) collective-permute-start(bf16[4,256,128]{2,1,0:T(8,128)(2,1)S(1)} %collective-permute-done.22), channel_id=1, source_target_pairs={{1,2},{2,3},{5,6},{6,7},{9,10},{10,11},{13,14},{14,15},{17,18},{18... | collective-permute-start | bytes 786440 | tf_op jit(solution)/shard_map/ppermute | solution.py:40
  170.5 14.4 %collective-permute-start.33 = (bf16[4,256,128]{2,1,0:T(8,128)(2,1)}, bf16[4,256,128]{2,1,0:T(8,128)(2,1)}, u32[]{:S(2)}, u32[]{:S(2)}) collective-permute-start(bf16[4,256,128]{2,1,0:T(8,128)(2,1)} %collective-permute-done.31), channel_id=1, source_target_pairs={{1,0},{5,4},{9,8},{13,12},{17,16},{21,20},{25,24},{29,28}} | collective-permute-start | bytes 786440 | tf_op jit(solution)/shard_map/ppermute | solution.py:41
  171.8 13.1 %collective-permute-start.32 = (bf16[4,256,128]{2,1,0:T(8,128)(2,1)}, bf16[4,256,128]{2,1,0:T(8,128)(2,1)}, u32[]{:S(2)}, u32[]{:S(2)}) collective-permute-start(bf16[4,256,128]{2,1,0:T(8,128)(2,1)} %collective-permute-done.30), channel_id=1, source_target_pairs={{2,3},{6,7},{10,11},{14,15},{18,19},{22,23},{26,27},{30,31}} | collective-permute-start | bytes 786440 | tf_op jit(solution)/shard_map/ppermute | solution.py:40
  177.1 11.9 %collective-permute-start.27 = (bf16[4,256,128]{2,1,0:T(8,128)(2,1)}, bf16[4,256,128]{2,1,0:T(8,128)(2,1)}, u32[]{:S(2)}, u32[]{:S(2)}) collective-permute-start(bf16[4,256,128]{2,1,0:T(8,128)(2,1)} %collective-permute-done.25), channel_id=1, source_target_pairs={{1,0},{5,4},{9,8},{13,12},{17,16},{21,20},{25,24},{29,28}} | collective-permute-start | bytes 786440 | tf_op jit(solution)/shard_map/ppermute | solution.py:41
  178.4 10.6 %collective-permute-start.26 = (bf16[4,256,128]{2,1,0:T(8,128)(2,1)}, bf16[4,256,128]{2,1,0:T(8,128)(2,1)}, u32[]{:S(2)}, u32[]{:S(2)}) collective-permute-start(bf16[4,256,128]{2,1,0:T(8,128)(2,1)} %collective-permute-done.24), channel_id=1, source_target_pairs={{2,3},{6,7},{10,11},{14,15},{18,19},{22,23},{26,27},{30,31}} | collective-permute-start | bytes 786440 | tf_op jit(solution)/shard_map/ppermute | solution.py:40
  181.9 3.0 %copy-start.10 = (bf16[512,512]{1,0:T(8,128)(2,1)}, bf16[512,512]{1,0:T(8,128)(2,1)S(1)}, u32[]{:S(2)}) copy-start(bf16[512,512]{1,0:T(8,128)(2,1)S(1)} %collective-permute-done.21.refs_7_) | copy-start | bytes 1572868

commit v15 on v14

--- a/solution.py
+++ b/solution.py
@@ -44,7 +44,7 @@
     return found
 
 
-def project_kernel(group, count, me_ref, gain_ref, active_ref, *refs):
+def project_kernel(group, count, begin, me_ref, gain_ref, active_ref, *refs):
     matrices = refs[:3]
     pieces = refs[3:-5]
     out_ref, normed, held, piece_in, weight_in = refs[-5:]
@@ -98,7 +98,7 @@
             totals[which] = product if step == 0 else totals[which] + product
     for which, total in enumerate(totals):
         if which == 0:
-            total = jnp.where(active_ref[...] > 0, total, ASIDE)
+            total = jnp.where(active_ref[begin : begin + rows, :] > 0, total, ASIDE)
         total = total.astype(jnp.bfloat16)
         for head in range(total.shape[1] // HEAD):
             for part in range(group):
@@ -111,14 +111,13 @@
                     ] = total[first : first + part_rows, head * HEAD : (head + 1) * HEAD]
 
 
-def project(me, pieces, active, gain, wq, wk, wv, seq_count, group):
-    columns = pieces[0].shape[1]
-    rows = active.shape[0]
+def project(me, pieces, active, chunk, gain, wq, wk, wv, seq_count, group):
+    rows, columns = pieces[0].shape
     features, width = wq.shape
     count = features // columns
     vmem = pl.BlockSpec(memory_space=pltpu.VMEM)
     return pl.pallas_call(
-        partial(project_kernel, group, count),
+        partial(project_kernel, group, count, chunk * rows),
         in_specs=[pl.BlockSpec(memory_space=pltpu.SMEM), vmem, vmem]
         + [pl.BlockSpec(memory_space=pl.ANY)] * (3 + len(pieces)),
         out_specs=vmem,
@@ -429,9 +428,8 @@
     shares = weight_shares(w_out, seq_count, tensor_count, columns)
 
     def work(found, chunk):
-        here = active[chunk * chunk_rows : (chunk + 1) * chunk_rows]
         return project(
-            me.reshape(1), found, here, gain, w_query, w_key, w_value, seq_count, group
+            me.reshape(1), found, active, chunk, gain, w_query, w_key, w_value, seq_count, group
         )
 
     def to_heads(sent):

time: 198 us -> 197 us (level)
  no operation moved by 1% of the time
where the time goes in v15:
time: 197 us; the launch traced here: 196 us
  waiting for transfers between devices  76.1 us (39%)
  starting transfers between devices  63.9 us (32%)
  Pallas kernels  47.2 us (24%)
  local copies, waits for them, and re-layouts  6.35 us (3%)
    ppermute x12, waiting for transfers between devices, line_gather(): from_right = lax.ppermute(last[at][1], 'tensor', left[:count - 1 - step])  49.5 us
    ppermute x12, starting transfers between devices, line_gather(): from_left = lax.ppermute(last[at][0], 'tensor', right[step:])  32.3 us
    pallas_call x2, Pallas kernels, project(): pl.pallas_call(partial(project_kernel, group, count, chunk * rows), in_sp...  24.2 us
    ppermute x4, waiting for transfers between devices, send_share(): return lax.ppermute(shares[number], 'tensor', ring)  18.5 us
    ppermute x12, starting transfers between devices, line_gather(): from_right = lax.ppermute(last[at][1], 'tensor', left[:count - 1 - step])  15.4 us
    pallas_call x1, Pallas kernels, attend(): pl.pallas_call(partial(attend_kernel, chunks, group, rows), in_specs=[pl....  11.2 us
    all_to_all x2, starting transfers between devices, to_heads(): return lax.all_to_all(sent, 'seq', split_axis=0, concat_axis=0)  7.58 us
    pallas_call x1, Pallas kernels, output(): pl.pallas_call(partial(output_kernel, group, count, cuts, blocks, halves)...  7.37 us
  transfers between devices with their start and end apart: 37, of which 16 were waited for; matrix products, arithmetic and copies ran while one was open for 3% of the time, Pallas kernels for 20%

profile of v15, /device:TPU:0, one launch (start us, length us, event | category | flops | bytes accessed | tf_op | source)
XLA Modules:
  0.0 195.9 jit_solution(15589308845290827422)
XLA Ops:
  0.0 1.3 fusion.4
  1.3 1.3 collective-permute-start.1
  2.6 6.4 %collective-permute-start = (bf16[256,1024]{1,0:T(8,128)(2,1)S(1)}, bf16[256,1024]{1,0:T(8,128)(2,1)}, u32[]{:S(2)}, u32[]{:S(2)}) collective-permute-start(bf16[256,1024]{1,0:T(8,128)(2,1)S(1)} %get-tuple-element.84.refs_3_), channel_id=1, source_target_pairs={{0,1},{1,2},{2,3},{4,5},{5,6},{6,7},{8,9},{9,10},{10,11},{12,13},{... | collective-permute-start | bytes 1572872 | tf_op jit(solution)/shard_map/ppermute | solution.py:40
  9.0 1.3 collective-permute-start.7
  10.3 5.4 %collective-permute-start.6 = (bf16[256,1024]{1,0:T(8,128)(2,1)S(1)}, bf16[256,1024]{1,0:T(8,128)(2,1)}, u32[]{:S(2)}, u32[]{:S(2)}) collective-permute-start(bf16[256,1024]{1,0:T(8,128)(2,1)S(1)} %get-tuple-element.56.refs_3_), channel_id=1, source_target_pairs={{0,1},{1,2},{2,3},{4,5},{5,6},{6,7},{8,9},{9,10},{10,11},{12,13},{... | collective-permute-start | bytes 1572872 | tf_op jit(solution)/shard_map/ppermute | solution.py:40
  15.7 3.4 %collective-permute-done.1.refs_5_ = bf16[256,1024]{1,0:T(8,128)(2,1)} collective-permute-done((bf16[256,1024]{1,0:T(8,128)(2,1)S(1)}, bf16[256,1024]{1,0:T(8,128)(2,1)}, u32[]{:S(2)}, u32[]{:S(2)}) %collective-permute-start.1) | collective-permute-done | bytes 524320 | tf_op jit(solution)/shard_map/ppermute | solution.py:41
  19.1 1.3 collective-permute-start.3
  20.4 0.1 collective-permute-done.refs_4_
  20.5 1.5 collective-permute-start.2
  22.0 0.6 pad_add_fusion.1.place_ref
  22.5 4.4 %shard_map.74 = (bf16[512,512]{1,0:T(8,128)(2,1)}, bf16[512,512]{1,0:T(8,128)(2,1)}, bf16[256,512]{1,0:T(8,128)(2,1)}, bf16[256,512]{1,0:T(8,128)(2,1)}, bf16[512,512]{1,0:T(8,128)(2,1)}) custom-call(s32[2]{0:T(128)} %pad_add_fusion.1.place_ref, bf16[512,4096]{1,0:T(8,128)(2,1)} %w_ref.1), custom_call_target="tpu_custom_call" | custom-call | tf_op jit(solution)/shard_map/pallas_call | solution.py:376
  26.9 3.4 %collective-permute-done.7.refs_5_ = bf16[256,1024]{1,0:T(8,128)(2,1)} collective-permute-done((bf16[256,1024]{1,0:T(8,128)(2,1)S(1)}, bf16[256,1024]{1,0:T(8,128)(2,1)}, u32[]{:S(2)}, u32[]{:S(2)}) %collective-permute-start.7) | collective-permute-done | bytes 524320 | tf_op jit(solution)/shard_map/ppermute | solution.py:41
  30.3 0.2 collective-permute-done.6.refs_4_
  30.6 1.5 collective-permute-start.8
  32.0 1.3 collective-permute-start.9
  33.3 8.2 %collective-permute-done.3.refs_7_ = bf16[256,1024]{1,0:T(8,128)(2,1)} collective-permute-done((bf16[256,1024]{1,0:T(8,128)(2,1)}, bf16[256,1024]{1,0:T(8,128)(2,1)}, u32[]{:S(2)}, u32[]{:S(2)}) %collective-permute-start.3) | collective-permute-done | bytes 524320 | tf_op jit(solution)/shard_map/ppermute | solution.py:41
  41.6 1.3 collective-permute-start.5
  42.9 1.5 collective-permute-start.4
  44.4 0.6 reshape.55.gain_ref
  45.0 1.5 collective-permute-start.10
  46.5 7.7 %collective-permute-done.9.refs_7_ = bf16[256,1024]{1,0:T(8,128)(2,1)} collective-permute-done((bf16[256,1024]{1,0:T(8,128)(2,1)}, bf16[256,1024]{1,0:T(8,128)(2,1)}, u32[]{:S(2)}, u32[]{:S(2)}) %collective-permute-start.9) | collective-permute-done | bytes 524320 | tf_op jit(solution)/shard_map/ppermute | solution.py:41
  54.1 1.3 collective-permute-start.11
  55.4 0.9 copy.10.active_ref
  56.3 9.1 %collective-permute-done.5.refs_9_ = bf16[256,1024]{1,0:T(8,128)(2,1)} collective-permute-done((bf16[256,1024]{1,0:T(8,128)(2,1)}, bf16[256,1024]{1,0:T(8,128)(2,1)}, u32[]{:S(2)}, u32[]{:S(2)}) %collective-permute-start.5) | collective-permute-done | bytes 524320 | tf_op jit(solution)/shard_map/ppermute | solution.py:41
  65.4 12.1 %shard_map.73 = bf16[8,128,384]{2,1,0:T(8,128)(2,1)} custom-call(s32[1]{0:T(128)} %bitcast.me_ref, f32[4,1024]{1,0:T(4,128)} %reshape.55.gain_ref, s32[512,1]{1,0:T(8,128)} %copy.10.active_ref, bf16[4096,512]{1,0:T(8,128)(2,1)} %refs_0_.3, bf16[4096,512]{1,0:T(8,128)(2,1)} %refs_1_.3, bf16[4096,512]{1,0:T(8,128)(2,1)} %refs_2_.3, ...), custom_call_target="tpu_custom_call" | custom-call | flops 3221225472 | bytes 15466496 | tf_op jit(solution)/shard_map/pallas_call | solution.py:119
  77.5 3.7 %all-to-all-start = ((bf16[8,128,384]{2,1,0:T(8,128)(2,1)}), bf16[8,128,384]{2,1,0:T(8,128)(2,1)S(1)}, u32[]{:S(2)}, u32[]{:S(2)}) async-start(bf16[8,128,384]{2,1,0:T(8,128)(2,1)} %shard_map.73), calls=%async_computation | async-start | bytes 1572864 | tf_op jit(solution)/shard_map/all_to_all | solution.py:436
  81.2 3.1 %collective-permute-start.12 = (bf16[256,512]{1,0:T(8,128)(2,1)}, bf16[256,512]{1,0:T(8,128)(2,1)}, u32[]{:S(2)}, u32[]{:S(2)}) collective-permute-start(bf16[256,512]{1,0:T(8,128)(2,1)} %get-tuple-element.64), channel_id=1, source_target_pairs={{0,2},{1,3},{2,0},{3,1},{4,6},{5,7},{6,4},{7,5},{8,10},{9,11},{10,... | collective-permute-start | bytes 786440 | tf_op jit(solution)/shard_map/ppermute | solution.py:401
  84.4 12.1 %shard_map.75 = bf16[8,128,384]{2,1,0:T(8,128)(2,1)} custom-call(s32[1]{0:T(128)} %bitcast.me_ref, f32[4,1024]{1,0:T(4,128)} %reshape.55.gain_ref, s32[512,1]{1,0:T(8,128)} %copy.10.active_ref, bf16[4096,512]{1,0:T(8,128)(2,1)} %refs_0_.3, bf16[4096,512]{1,0:T(8,128)(2,1)} %refs_1_.3, bf16[4096,512]{1,0:T(8,128)(2,1)} %refs_2_.3, bf16[256,1024]{1,0:T(8,128)(2,1)} %copy-done, ...), custom_call_target="tpu_custom_call" | custom-call | flops 3221225472 | bytes 15466496 | tf_op jit(solution)/shard_map/pallas_call | solution.py:119
  96.5 0.8 collective-permute-done.12
  97.3 3.8 %all-to-all-start.1 = ((bf16[8,128,384]{2,1,0:T(8,128)(2,1)}), bf16[8,128,384]{2,1,0:T(8,128)(2,1)S(1)}, u32[]{:S(2)}, u32[]{:S(2)}) async-start(bf16[8,128,384]{2,1,0:T(8,128)(2,1)} %shard_map.75), calls=%async_computation.1 | async-start | bytes 1572864 | tf_op jit(solution)/shard_map/all_to_all | solution.py:436
  101.2 0.5 collective-permute-start.13
  101.7 14.9 %collective-permute-done.14 = bf16[256,512]{1,0:T(8,128)(2,1)S(1)} collective-permute-done((bf16[256,512]{1,0:T(8,128)(2,1)}, bf16[256,512]{1,0:T(8,128)(2,1)S(1)}, u32[]{:S(2)}, u32[]{:S(2)}) %collective-permute-start.14) | collective-permute-done | bytes 262176 | tf_op jit(solution)/shard_map/ppermute | solution.py:401
  116.7 0.2 collective-permute-start.16
  116.9 0.4 copy-done.11
  117.3 0.3 copy-done.6
  117.6 0.9 copy-done.18
  118.5 0.6 collective-permute-done.15.refs_3_
  119.1 11.2 %shard_map.76 = bf16[8,256,128]{2,1,0:T(8,128)(2,1)} custom-call(s32[1]{0:T(128)} %bitcast.4.part_ref, bf16[8,128,384]{2,1,0:T(8,128)(2,1)} %copy-done.5, bf16[8,128,384]{2,1,0:T(8,128)(2,1)} %copy-done.18, bf16[8,128,384]{2,1,0:T(8,128)(2,1)} %copy-done.6, bf16[8,128,384]{2,1,0:T(8,128)(2,1)} %collective-permute-done.15.refs_3_), custom_call_target="tpu_custom_call" | custom-call | flops 3623878656 | bytes 4194304 | tf_op jit(solution)/shard_map/pallas_call | solution.py:247
  130.3 2.8 %collective-permute-done.16.refs_1_ = bf16[512,512]{1,0:T(8,128)(2,1)} collective-permute-done((bf16[512,512]{1,0:T(8,128)(2,1)}, bf16[512,512]{1,0:T(8,128)(2,1)}, u32[]{:S(2)}, u32[]{:S(2)}) %collective-permute-start.16) | collective-permute-done | bytes 524320 | tf_op jit(solution)/shard_map/ppermute | solution.py:401
  133.1 4.0 %all-to-all-start.2 = ((bf16[8,256,128]{2,1,0:T(8,128)(2,1)}), bf16[8,256,128]{2,1,0:T(8,128)(2,1)S(1)}, u32[]{:S(2)}, u32[]{:S(2)}) async-start(bf16[8,256,128]{2,1,0:T(8,128)(2,1)} %shard_map.76), calls=%async_computation.2 | async-start | bytes 1048576 | tf_op jit(solution)/shard_map/all_to_all | solution.py:463
  137.1 1.0 constant_dynamic-update-slice_fusion.1
  138.0 1.0 constant_dynamic-update-slice_fusion.refs_2_
  139.0 0.6 collective-permute-start.20
  139.6 0.1 collective-permute-start.19
  139.7 7.1 %all-to-all-done.2 = bf16[8,256,128]{2,1,0:T(8,128)(2,1)S(1)} async-done(((bf16[8,256,128]{2,1,0:T(8,128)(2,1)}), bf16[8,256,128]{2,1,0:T(8,128)(2,1)S(1)}, u32[]{:S(2)}, u32[]{:S(2)}) %all-to-all-start.2) | async-done | bytes 524320 | tf_op jit(solution)/shard_map/all_to_all | solution.py:463
  146.9 1.3 collective-permute-start.29
  148.2 4.6 %collective-permute-start.28 = (bf16[4,256,128]{2,1,0:T(8,128)(2,1)S(1)}, bf16[4,256,128]{2,1,0:T(8,128)(2,1)S(1)}, u32[]{:S(2)}, u32[]{:S(2)}) collective-permute-start(bf16[4,256,128]{2,1,0:T(8,128)(2,1)S(1)} %get-tuple-element.85), channel_id=1, source_target_pairs={{0,1},{1,2},{2,3},{4,5},{5,6},{6,7},{8,9},{9,10},{10,11},{12,13},{... | collective-permute-start | bytes 786440 | tf_op jit(solution)/shard_map/ppermute | solution.py:40
  152.8 1.3 collective-permute-start.23
  154.1 4.6 %collective-permute-start.22 = (bf16[4,256,128]{2,1,0:T(8,128)(2,1)S(1)}, bf16[4,256,128]{2,1,0:T(8,128)(2,1)S(1)}, u32[]{:S(2)}, u32[]{:S(2)}) collective-permute-start(bf16[4,256,128]{2,1,0:T(8,128)(2,1)S(1)} %get-tuple-element.86), channel_id=1, source_target_pairs={{0,1},{1,2},{2,3},{4,5},{5,6},{6,7},{8,9},{9,10},{10,11},{12,13},{... | collective-permute-start | bytes 786440 | tf_op jit(solution)/shard_map/ppermute | solution.py:40
  158.8 1.3 collective-permute-start.31
  160.1 1.4 collective-permute-start.30
  161.5 1.3 collective-permute-start.25
  162.8 1.4 collective-permute-start.24
  164.2 5.5 %collective-permute-done.31 = bf16[4,256,128]{2,1,0:T(8,128)(2,1)} collective-permute-done((bf16[4,256,128]{2,1,0:T(8,128)(2,1)S(1)}, bf16[4,256,128]{2,1,0:T(8,128)(2,1)}, u32[]{:S(2)}, u32[]{:S(2)}) %collective-permute-start.31) | collective-permute-done | bytes 262176 | tf_op jit(solution)/shard_map/ppermute | solution.py:41
  169.7 1.3 collective-permute-start.33
  171.0 1.4 collective-permute-start.32
  172.4 4.0 %collective-permute-done.25 = bf16[4,256,128]{2,1,0:T(8,128)(2,1)} collective-permute-done((bf16[4,256,128]{2,1,0:T(8,128)(2,1)S(1)}, bf16[4,256,128]{2,1,0:T(8,128)(2,1)}, u32[]{:S(2)}, u32[]{:S(2)}) %collective-permute-start.25) | collective-permute-done | bytes 262176 | tf_op jit(solution)/shard_map/ppermute | solution.py:41
  176.4 1.3 collective-permute-start.27
  177.7 1.4 collective-permute-start.26
  179.1 0.5 fusion.at_ref
  179.6 0.6 pad_add_fusion.me_ref
  180.2 3.9 %collective-permute-done.33 = bf16[4,256,128]{2,1,0:T(8,128)(2,1)} collective-permute-done((bf16[4,256,128]{2,1,0:T(8,128)(2,1)}, bf16[4,256,128]{2,1,0:T(8,128)(2,1)}, u32[]{:S(2)}, u32[]{:S(2)}) %collective-permute-start.33) | collective-permute-done | bytes 262176 | tf_op jit(solution)/shard_map/ppermute | solution.py:41
  184.1 4.2 %collective-permute-done.27 = bf16[4,256,128]{2,1,0:T(8,128)(2,1)} collective-permute-done((bf16[4,256,128]{2,1,0:T(8,128)(2,1)}, bf16[4,256,128]{2,1,0:T(8,128)(2,1)}, u32[]{:S(2)}, u32[]{:S(2)}) %collective-permute-start.27) | collective-permute-done | bytes 262176 | tf_op jit(solution)/shard_map/ppermute | solution.py:41
  188.3 7.4 %shard_map.77 = bf16[512,1024]{1,0:T(8,128)(2,1)} custom-call(s32[3]{0:T(128)} %pad_add_fusion.me_ref, s32[16]{0:T(128)} %fusion.at_ref, s32[512,1]{1,0:T(8,128)} %copy.10.active_ref, bf16[512,1024]{1,0:T(8,128)(2,1)} %hidden_ref.1, bf16[512,512]{1,0:T(8,128)(2,1)} %get-tuple-element.69.refs_0_, bf16[512,512]{1,0:T(8,128)(2,1)} %collective-permute-done.16.refs_1_, ...), custom_call_target="tpu_custom_call" | custom-call | flops 2147483648 | bytes 8388608 | tf_op jit(solution)/shard_map/pallas_call | solution.py:333
  (63 shorter events, 0.3 us)
Async XLA Ops:
  0.0 44.4 %copy-start.16 = (f32[4096]{0:T(1024)S(1)}, f32[4096]{0:T(1024)}, u32[]{:S(2)}) copy-start(f32[4096]{0:T(1024)} %param.9) | copy-start | bytes 49156
  0.0 55.4 %copy-start.17 = (s32[512]{0:T(512)S(1)}, s32[512]{0:T(512)}, u32[]{:S(2)}) copy-start(s32[512]{0:T(512)} %param.8) | copy-start | bytes 6148
  1.3 7.7 %copy-start.1 = (bf16[256,1024]{1,0:T(8,128)(2,1)}, bf16[256,1024]{1,0:T(8,128)(2,1)S(1)}, u32[]{:S(2)}) copy-start(bf16[256,1024]{1,0:T(8,128)(2,1)S(1)} %get-tuple-element.84.refs_3_) | copy-start | bytes 1572868
  1.3 76.2 %copy-start = (bf16[256,1024]{1,0:T(8,128)(2,1)}, bf16[256,1024]{1,0:T(8,128)(2,1)S(1)}, u32[]{:S(2)}) copy-start(bf16[256,1024]{1,0:T(8,128)(2,1)S(1)} %get-tuple-element.56.refs_3_) | copy-start | bytes 1572868
  1.3 17.8 %collective-permute-start.1 = (bf16[256,1024]{1,0:T(8,128)(2,1)S(1)}, bf16[256,1024]{1,0:T(8,128)(2,1)}, u32[]{:S(2)}, u32[]{:S(2)}) collective-permute-start(bf16[256,1024]{1,0:T(8,128)(2,1)S(1)} %get-tuple-element.84.refs_3_), channel_id=1, source_target_pairs={{1,0},{2,1},{3,2},{5,4},{6,5},{7,6},{9,8},{10,9},{11,10},{13,12},{... | collective-permute-start | bytes 1572872 | tf_op jit(solution)/shard_map/ppermute | solution.py:41
  2.6 17.9 %collective-permute-start = (bf16[256,1024]{1,0:T(8,128)(2,1)S(1)}, bf16[256,1024]{1,0:T(8,128)(2,1)}, u32[]{:S(2)}, u32[]{:S(2)}) collective-permute-start(bf16[256,1024]{1,0:T(8,128)(2,1)S(1)} %get-tuple-element.84.refs_3_), channel_id=1, source_target_pairs={{0,1},{1,2},{2,3},{4,5},{5,6},{6,7},{8,9},{9,10},{10,11},{12,13},{... | collective-permute-start | bytes 1572872 | tf_op jit(solution)/shard_map/ppermute | solution.py:40
  9.0 21.3 %collective-permute-start.7 = (bf16[256,1024]{1,0:T(8,128)(2,1)S(1)}, bf16[256,1024]{1,0:T(8,128)(2,1)}, u32[]{:S(2)}, u32[]{:S(2)}) collective-permute-start(bf16[256,1024]{1,0:T(8,128)(2,1)S(1)} %get-tuple-element.56.refs_3_), channel_id=1, source_target_pairs={{1,0},{2,1},{3,2},{5,4},{6,5},{7,6},{9,8},{10,9},{11,10},{13,12},{... | collective-permute-start | bytes 1572872 | tf_op jit(solution)/shard_map/ppermute | solution.py:41
  10.3 20.3 %collective-permute-start.6 = (bf16[256,1024]{1,0:T(8,128)(2,1)S(1)}, bf16[256,1024]{1,0:T(8,128)(2,1)}, u32[]{:S(2)}, u32[]{:S(2)}) collective-permute-start(bf16[256,1024]{1,0:T(8,128)(2,1)S(1)} %get-tuple-element.56.refs_3_), channel_id=1, source_target_pairs={{0,1},{1,2},{2,3},{4,5},{5,6},{6,7},{8,9},{9,10},{10,11},{12,13},{... | collective-permute-start | bytes 1572872 | tf_op jit(solution)/shard_map/ppermute | solution.py:40
  19.1 22.5 %collective-permute-start.3 = (bf16[256,1024]{1,0:T(8,128)(2,1)}, bf16[256,1024]{1,0:T(8,128)(2,1)}, u32[]{:S(2)}, u32[]{:S(2)}) collective-permute-start(bf16[256,1024]{1,0:T(8,128)(2,1)} %collective-permute-done.1.refs_5_), channel_id=1, source_target_pairs={{1,0},{2,1},{5,4},{6,5},{9,8},{10,9},{13,12},{14,13},{17,16},{18,1... | collective-permute-start | bytes 1572872 | tf_op jit(solution)/shard_map/ppermute | solution.py:41
  20.5 22.4 %collective-permute-start.2 = (bf16[256,1024]{1,0:T(8,128)(2,1)}, bf16[256,1024]{1,0:T(8,128)(2,1)}, u32[]{:S(2)}, u32[]{:S(2)}) collective-permute-start(bf16[256,1024]{1,0:T(8,128)(2,1)} %collective-permute-done.refs_4_), channel_id=1, source_target_pairs={{1,2},{2,3},{5,6},{6,7},{9,10},{10,11},{13,14},{14,15},{17,18},{18... | collective-permute-start | bytes 1572872 | tf_op jit(solution)/shard_map/ppermute | solution.py:40
  30.6 14.4 %collective-permute-start.8 = (bf16[256,1024]{1,0:T(8,128)(2,1)}, bf16[256,1024]{1,0:T(8,128)(2,1)}, u32[]{:S(2)}, u32[]{:S(2)}) collective-permute-start(bf16[256,1024]{1,0:T(8,128)(2,1)} %collective-permute-done.6.refs_4_), channel_id=1, source_target_pairs={{1,2},{2,3},{5,6},{6,7},{9,10},{10,11},{13,14},{14,15},{17,18},{18... | collective-permute-start | bytes 1572872 | tf_op jit(solution)/shard_map/ppermute | solution.py:40
  32.0 22.1 %collective-permute-start.9 = (bf16[256,1024]{1,0:T(8,128)(2,1)}, bf16[256,1024]{1,0:T(8,128)(2,1)}, u32[]{:S(2)}, u32[]{:S(2)}) collective-permute-start(bf16[256,1024]{1,0:T(8,128)(2,1)} %collective-permute-done.7.refs_5_), channel_id=1, source_target_pairs={{1,0},{2,1},{5,4},{6,5},{9,8},{10,9},{13,12},{14,13},{17,16},{18,1... | collective-permute-start | bytes 1572872 | tf_op jit(solution)/shard_map/ppermute | solution.py:41
  41.6 23.8 %collective-permute-start.5 = (bf16[256,1024]{1,0:T(8,128)(2,1)}, bf16[256,1024]{1,0:T(8,128)(2,1)}, u32[]{:S(2)}, u32[]{:S(2)}) collective-permute-start(bf16[256,1024]{1,0:T(8,128)(2,1)} %collective-permute-done.3.refs_7_), channel_id=1, source_target_pairs={{1,0},{5,4},{9,8},{13,12},{17,16},{21,20},{25,24},{29,28}} | collective-permute-start | bytes 1572872 | tf_op jit(solution)/shard_map/ppermute | solution.py:41
  42.9 22.5 %collective-permute-start.4 = (bf16[256,1024]{1,0:T(8,128)(2,1)}, bf16[256,1024]{1,0:T(8,128)(2,1)}, u32[]{:S(2)}, u32[]{:S(2)}) collective-permute-start(bf16[256,1024]{1,0:T(8,128)(2,1)} %collective-permute-done.2.refs_6_), channel_id=1, source_target_pairs={{2,3},{6,7},{10,11},{14,15},{18,19},{22,23},{26,27},{30,31}} | collective-permute-start | bytes 1572872 | tf_op jit(solution)/shard_map/ppermute | solution.py:40
  45.0 32.5 %collective-permute-start.10 = (bf16[256,1024]{1,0:T(8,128)(2,1)}, bf16[256,1024]{1,0:T(8,128)(2,1)}, u32[]{:S(2)}, u32[]{:S(2)}) collective-permute-start(bf16[256,1024]{1,0:T(8,128)(2,1)} %collective-permute-done.8.refs_6_), channel_id=1, source_target_pairs={{2,3},{6,7},{10,11},{14,15},{18,19},{22,23},{26,27},{30,31}} | collective-permute-start | bytes 1572872 | tf_op jit(solution)/shard_map/ppermute | solution.py:40
  54.1 23.4 %collective-permute-start.11 = (bf16[256,1024]{1,0:T(8,128)(2,1)}, bf16[256,1024]{1,0:T(8,128)(2,1)}, u32[]{:S(2)}, u32[]{:S(2)}) collective-permute-start(bf16[256,1024]{1,0:T(8,128)(2,1)} %collective-permute-done.9.refs_7_), channel_id=1, source_target_pairs={{1,0},{5,4},{9,8},{13,12},{17,16},{21,20},{25,24},{29,28}} | collective-permute-start | bytes 1572872 | tf_op jit(solution)/shard_map/ppermute | solution.py:41
  77.5 19.8 %all-to-all-start = ((bf16[8,128,384]{2,1,0:T(8,128)(2,1)}), bf16[8,128,384]{2,1,0:T(8,128)(2,1)S(1)}, u32[]{:S(2)}, u32[]{:S(2)}) async-start(bf16[8,128,384]{2,1,0:T(8,128)(2,1)} %shard_map.73), calls=%async_computation | async-start | bytes 1572864 | tf_op jit(solution)/shard_map/all_to_all | solution.py:436
  81.2 16.1 %collective-permute-start.12 = (bf16[256,512]{1,0:T(8,128)(2,1)}, bf16[256,512]{1,0:T(8,128)(2,1)}, u32[]{:S(2)}, u32[]{:S(2)}) collective-permute-start(bf16[256,512]{1,0:T(8,128)(2,1)} %get-tuple-element.64), channel_id=1, source_target_pairs={{0,2},{1,3},{2,0},{3,1},{4,6},{5,7},{6,4},{7,5},{8,10},{9,11},{10,... | collective-permute-start | bytes 786440 | tf_op jit(solution)/shard_map/ppermute | solution.py:401
  97.3 21.8 %copy-start.5 = (bf16[8,128,384]{2,1,0:T(8,128)(2,1)}, bf16[8,128,384]{2,1,0:T(8,128)(2,1)S(1)}, u32[]{:S(2)}) copy-start(bf16[8,128,384]{2,1,0:T(8,128)(2,1)S(1)} %all-to-all-done.refs_0_) | copy-start | bytes 2359300
  97.3 19.3 %all-to-all-start.1 = ((bf16[8,128,384]{2,1,0:T(8,128)(2,1)}), bf16[8,128,384]{2,1,0:T(8,128)(2,1)S(1)}, u32[]{:S(2)}, u32[]{:S(2)}) async-start(bf16[8,128,384]{2,1,0:T(8,128)(2,1)} %shard_map.75), calls=%async_computation.1 | async-start | bytes 1572864 | tf_op jit(solution)/shard_map/all_to_all | solution.py:436
  101.1 15.4 %collective-permute-start.14 = (bf16[256,512]{1,0:T(8,128)(2,1)}, bf16[256,512]{1,0:T(8,128)(2,1)S(1)}, u32[]{:S(2)}, u32[]{:S(2)}) collective-permute-start(bf16[256,512]{1,0:T(8,128)(2,1)} %get-tuple-element.72), channel_id=1, source_target_pairs={{0,2},{1,3},{2,0},{3,1},{4,6},{5,7},{6,4},{7,5},{8,10},{9,11},{10,... | collective-permute-start | bytes 786440 | tf_op jit(solution)/shard_map/ppermute | solution.py:401
  101.2 15.8 %collective-permute-start.13 = (bf16[8,128,384]{2,1,0:T(8,128)(2,1)S(1)}, bf16[8,128,384]{2,1,0:T(8,128)(2,1)S(1)}, u32[]{:S(2)}, u32[]{:S(2)}) collective-permute-start(bf16[8,128,384]{2,1,0:T(8,128)(2,1)S(1)} %all-to-all-done.refs_0_), channel_id=1, source_target_pairs={{0,4},{4,0},{8,12},{12,8},{16,20},{20,16},{24,28},{28,24},{1,5},{5... | collective-permute-start | bytes 2359304 | tf_op jit(solution)/shard_map/ppermute | solution.py:443
  116.6 0.7 copy-start.11
  116.6 1.0 copy-start.6
  116.6 2.5 %collective-permute-start.15 = (bf16[8,128,384]{2,1,0:T(8,128)(2,1)S(1)}, bf16[8,128,384]{2,1,0:T(8,128)(2,1)}, u32[]{:S(2)}, u32[]{:S(2)}) collective-permute-start(bf16[8,128,384]{2,1,0:T(8,128)(2,1)S(1)} %all-to-all-done.1.refs_2_), channel_id=1, source_target_pairs={{0,4},{4,0},{8,12},{12,8},{16,20},{20,16},{24,28},{28,24},{1,5},{5... | collective-permute-start | bytes 2359304 | tf_op jit(solution)/shard_map/ppermute | solution.py:443
  116.7 16.4 %collective-permute-start.16 = (bf16[512,512]{1,0:T(8,128)(2,1)}, bf16[512,512]{1,0:T(8,128)(2,1)}, u32[]{:S(2)}, u32[]{:S(2)}) collective-permute-start(bf16[512,512]{1,0:T(8,128)(2,1)} %get-tuple-element.74), channel_id=1, source_target_pairs={{0,1},{1,2},{2,3},{3,0},{4,5},{5,6},{6,7},{7,4},{8,9},{9,10},{10,1... | collective-permute-start | bytes 1572872 | tf_op jit(solution)/shard_map/ppermute | solution.py:401
  117.6 0.9 copy-start.18
  133.1 13.7 %collective-permute-start.17 = (bf16[512,512]{1,0:T(8,128)(2,1)}, bf16[512,512]{1,0:T(8,128)(2,1)S(1)}, u32[]{:S(2)}, u32[]{:S(2)}) collective-permute-start(bf16[512,512]{1,0:T(8,128)(2,1)} %get-tuple-element.80), channel_id=1, source_target_pairs={{0,3},{1,0},{2,1},{3,2},{4,7},{5,4},{6,5},{7,6},{8,11},{9,8},{10,9... | collective-permute-start | bytes 1572872 | tf_op jit(solution)/shard_map/ppermute | solution.py:401
  133.1 19.7 %collective-permute-start.18 = (bf16[512,512]{1,0:T(8,128)(2,1)}, bf16[512,512]{1,0:T(8,128)(2,1)S(1)}, u32[]{:S(2)}, u32[]{:S(2)}) collective-permute-start(bf16[512,512]{1,0:T(8,128)(2,1)} %get-tuple-element.69.refs_0_), channel_id=1, source_target_pairs={{0,4},{4,0},{8,12},{12,8},{16,20},{20,16},{24,28},{28,24},{1,5},{5... | collective-permute-start | bytes 1572872 | tf_op jit(solution)/shard_map/ppermute | solution.py:473
  133.1 13.7 %all-to-all-start.2 = ((bf16[8,256,128]{2,1,0:T(8,128)(2,1)}), bf16[8,256,128]{2,1,0:T(8,128)(2,1)S(1)}, u32[]{:S(2)}, u32[]{:S(2)}) async-start(bf16[8,256,128]{2,1,0:T(8,128)(2,1)} %shard_map.76), calls=%async_computation.2 | async-start | bytes 1048576 | tf_op jit(solution)/shard_map/all_to_all | solution.py:463
  139.0 49.3 %copy-start.2 = (bf16[512,512]{1,0:T(8,128)(2,1)}, bf16[512,512]{1,0:T(8,128)(2,1)S(1)}, u32[]{:S(2)}) copy-start(bf16[512,512]{1,0:T(8,128)(2,1)S(1)} %constant_dynamic-update-slice_fusion.refs_2_) | copy-start | bytes 1572868
  139.0 15.1 %collective-permute-start.20 = (bf16[512,512]{1,0:T(8,128)(2,1)S(1)}, bf16[512,512]{1,0:T(8,128)(2,1)S(1)}, u32[]{:S(2)}, u32[]{:S(2)}) collective-permute-start(bf16[512,512]{1,0:T(8,128)(2,1)S(1)} %constant_dynamic-update-slice_fusion.refs_2_), channel_id=1, source_target_pairs={{0,4},{4,0},{8,12},{12,8},{16,20},{20,16},{24,28},{28,24},{1,5},{5... | collective-permute-start | bytes 1572872 | tf_op jit(solution)/shard_map/ppermute | solution.py:473
  139.6 19.1 %collective-permute-start.19 = (bf16[512,512]{1,0:T(8,128)(2,1)}, bf16[512,512]{1,0:T(8,128)(2,1)}, u32[]{:S(2)}, u32[]{:S(2)}) collective-permute-start(bf16[512,512]{1,0:T(8,128)(2,1)} %collective-permute-done.16.refs_1_), channel_id=1, source_target_pairs={{0,4},{4,0},{8,12},{12,8},{16,20},{20,16},{24,28},{28,24},{1,5},{5... | collective-permute-start | bytes 1572872 | tf_op jit(solution)/shard_map/ppermute | solution.py:473
  146.8 16.0 %copy-start.7 = (bf16[512,512]{1,0:T(8,128)(2,1)}, bf16[512,512]{1,0:T(8,128)(2,1)S(1)}, u32[]{:S(2)}) copy-start(bf16[512,512]{1,0:T(8,128)(2,1)S(1)} %collective-permute-done.17.refs_3_) | copy-start | bytes 1572868
  146.9 13.2 %copy-start.4 = (bf16[4,256,128]{2,1,0:T(8,128)(2,1)}, bf16[4,256,128]{2,1,0:T(8,128)(2,1)S(1)}, u32[]{:S(2)}) copy-start(bf16[4,256,128]{2,1,0:T(8,128)(2,1)S(1)} %get-tuple-element.86) | copy-start | bytes 786436
  146.9 41.4 %copy-start.3 = (bf16[4,256,128]{2,1,0:T(8,128)(2,1)}, bf16[4,256,128]{2,1,0:T(8,128)(2,1)S(1)}, u32[]{:S(2)}) copy-start(bf16[4,256,128]{2,1,0:T(8,128)(2,1)S(1)} %get-tuple-element.85) | copy-start | bytes 786436
  146.9 11.9 %collective-permute-start.29 = (bf16[4,256,128]{2,1,0:T(8,128)(2,1)S(1)}, bf16[4,256,128]{2,1,0:T(8,128)(2,1)S(1)}, u32[]{:S(2)}, u32[]{:S(2)}) collective-permute-start(bf16[4,256,128]{2,1,0:T(8,128)(2,1)S(1)} %get-tuple-element.85), channel_id=1, source_target_pairs={{1,0},{2,1},{3,2},{5,4},{6,5},{7,6},{9,8},{10,9},{11,10},{13,12},{... | collective-permute-start | bytes 786440 | tf_op jit(solution)/shard_map/ppermute | solution.py:41
  148.2 11.9 %collective-permute-start.28 = (bf16[4,256,128]{2,1,0:T(8,128)(2,1)S(1)}, bf16[4,256,128]{2,1,0:T(8,128)(2,1)S(1)}, u32[]{:S(2)}, u32[]{:S(2)}) collective-permute-start(bf16[4,256,128]{2,1,0:T(8,128)(2,1)S(1)} %get-tuple-element.85), channel_id=1, source_target_pairs={{0,1},{1,2},{2,3},{4,5},{5,6},{6,7},{8,9},{9,10},{10,11},{12,13},{... | collective-permute-start | bytes 786440 | tf_op jit(solution)/shard_map/ppermute | solution.py:40
  152.8 27.4 %copy-start.8 = (bf16[512,512]{1,0:T(8,128)(2,1)}, bf16[512,512]{1,0:T(8,128)(2,1)S(1)}, u32[]{:S(2)}) copy-start(bf16[512,512]{1,0:T(8,128)(2,1)S(1)} %collective-permute-done.18.refs_4_) | copy-start | bytes 1572868
  152.8 8.7 %collective-permute-start.23 = (bf16[4,256,128]{2,1,0:T(8,128)(2,1)S(1)}, bf16[4,256,128]{2,1,0:T(8,128)(2,1)S(1)}, u32[]{:S(2)}, u32[]{:S(2)}) collective-permute-start(bf16[4,256,128]{2,1,0:T(8,128)(2,1)S(1)} %get-tuple-element.86), channel_id=1, source_target_pairs={{1,0},{2,1},{3,2},{5,4},{6,5},{7,6},{9,8},{10,9},{11,10},{13,12},{... | collective-permute-start | bytes 786440 | tf_op jit(solution)/shard_map/ppermute | solution.py:41
  154.1 30.0 %copy-start.9 = (bf16[512,512]{1,0:T(8,128)(2,1)}, bf16[512,512]{1,0:T(8,128)(2,1)S(1)}, u32[]{:S(2)}) copy-start(bf16[512,512]{1,0:T(8,128)(2,1)S(1)} %collective-permute-done.20.refs_6_) | copy-start | bytes 1572868
  154.1 8.7 %collective-permute-start.22 = (bf16[4,256,128]{2,1,0:T(8,128)(2,1)S(1)}, bf16[4,256,128]{2,1,0:T(8,128)(2,1)S(1)}, u32[]{:S(2)}, u32[]{:S(2)}) collective-permute-start(bf16[4,256,128]{2,1,0:T(8,128)(2,1)S(1)} %get-tuple-element.86), channel_id=1, source_target_pairs={{0,1},{1,2},{2,3},{4,5},{5,6},{6,7},{8,9},{9,10},{10,11},{12,13},{... | collective-permute-start | bytes 786440 | tf_op jit(solution)/shard_map/ppermute | solution.py:40
  158.7 21.5 %collective-permute-start.21 = (bf16[512,512]{1,0:T(8,128)(2,1)S(1)}, bf16[512,512]{1,0:T(8,128)(2,1)S(1)}, u32[]{:S(2)}, u32[]{:S(2)}) collective-permute-start(bf16[512,512]{1,0:T(8,128)(2,1)S(1)} %collective-permute-done.17.refs_3_), channel_id=1, source_target_pairs={{0,4},{4,0},{8,12},{12,8},{16,20},{20,16},{24,28},{28,24},{1,5},{5... | collective-permute-start | bytes 1572872 | tf_op jit(solution)/shard_map/ppermute | solution.py:473
  158.8 29.5 %copy-start.12 = (bf16[4,256,128]{2,1,0:T(8,128)(2,1)}, bf16[4,256,128]{2,1,0:T(8,128)(2,1)S(1)}, u32[]{:S(2)}) copy-start(bf16[4,256,128]{2,1,0:T(8,128)(2,1)S(1)} %collective-permute-done.29) | copy-start | bytes 786436
  158.8 10.9 %collective-permute-start.31 = (bf16[4,256,128]{2,1,0:T(8,128)(2,1)S(1)}, bf16[4,256,128]{2,1,0:T(8,128)(2,1)}, u32[]{:S(2)}, u32[]{:S(2)}) collective-permute-start(bf16[4,256,128]{2,1,0:T(8,128)(2,1)S(1)} %collective-permute-done.29), channel_id=1, source_target_pairs={{1,0},{2,1},{5,4},{6,5},{9,8},{10,9},{13,12},{14,13},{17,16},{18,1... | collective-permute-start | bytes 786440 | tf_op jit(solution)/shard_map/ppermute | solution.py:41
  160.1 9.6 %copy-start.13 = (bf16[4,256,128]{2,1,0:T(8,128)(2,1)}, bf16[4,256,128]{2,1,0:T(8,128)(2,1)S(1)}, u32[]{:S(2)}) copy-start(bf16[4,256,128]{2,1,0:T(8,128)(2,1)S(1)} %collective-permute-done.28) | copy-start | bytes 786436
  160.1 10.9 %collective-permute-start.30 = (bf16[4,256,128]{2,1,0:T(8,128)(2,1)S(1)}, bf16[4,256,128]{2,1,0:T(8,128)(2,1)}, u32[]{:S(2)}, u32[]{:S(2)}) collective-permute-start(bf16[4,256,128]{2,1,0:T(8,128)(2,1)S(1)} %collective-permute-done.28), channel_id=1, source_target_pairs={{1,2},{2,3},{5,6},{6,7},{9,10},{10,11},{13,14},{14,15},{17,18},{18... | collective-permute-start | bytes 786440 | tf_op jit(solution)/shard_map/ppermute | solution.py:40
  161.5 9.6 %copy-start.14 = (bf16[4,256,128]{2,1,0:T(8,128)(2,1)}, bf16[4,256,128]{2,1,0:T(8,128)(2,1)S(1)}, u32[]{:S(2)}) copy-start(bf16[4,256,128]{2,1,0:T(8,128)(2,1)S(1)} %collective-permute-done.23) | copy-start | bytes 786436
  161.5 14.9 %collective-permute-start.25 = (bf16[4,256,128]{2,1,0:T(8,128)(2,1)S(1)}, bf16[4,256,128]{2,1,0:T(8,128)(2,1)}, u32[]{:S(2)}, u32[]{:S(2)}) collective-permute-start(bf16[4,256,128]{2,1,0:T(8,128)(2,1)S(1)} %collective-permute-done.23), channel_id=1, source_target_pairs={{1,0},{2,1},{5,4},{6,5},{9,8},{10,9},{13,12},{14,13},{17,16},{18,1... | collective-permute-start | bytes 786440 | tf_op jit(solution)/shard_map/ppermute | solution.py:41
  162.8 13.6 %copy-start.15 = (bf16[4,256,128]{2,1,0:T(8,128)(2,1)}, bf16[4,256,128]{2,1,0:T(8,128)(2,1)S(1)}, u32[]{:S(2)}) copy-start(bf16[4,256,128]{2,1,0:T(8,128)(2,1)S(1)} %collective-permute-done.22) | copy-start | bytes 786436
  162.8 14.9 %collective-permute-start.24 = (bf16[4,256,128]{2,1,0:T(8,128)(2,1)S(1)}, bf16[4,256,128]{2,1,0:T(8,128)(2,1)}, u32[]{:S(2)}, u32[]{:S(2)}) collective-permute-start(bf16[4,256,128]{2,1,0:T(8,128)(2,1)S(1)} %collective-permute-done.22), channel_id=1, source_target_pairs={{1,2},{2,3},{5,6},{6,7},{9,10},{10,11},{13,14},{14,15},{17,18},{18... | collective-permute-start | bytes 786440 | tf_op jit(solution)/shard_map/ppermute | solution.py:40
  169.7 14.3 %collective-permute-start.33 = (bf16[4,256,128]{2,1,0:T(8,128)(2,1)}, bf16[4,256,128]{2,1,0:T(8,128)(2,1)}, u32[]{:S(2)}, u32[]{:S(2)}) collective-permute-start(bf16[4,256,128]{2,1,0:T(8,128)(2,1)} %collective-permute-done.31), channel_id=1, source_target_pairs={{1,0},{5,4},{9,8},{13,12},{17,16},{21,20},{25,24},{29,28}} | collective-permute-start | bytes 786440 | tf_op jit(solution)/shard_map/ppermute | solution.py:41
  171.0 13.0 %collective-permute-start.32 = (bf16[4,256,128]{2,1,0:T(8,128)(2,1)}, bf16[4,256,128]{2,1,0:T(8,128)(2,1)}, u32[]{:S(2)}, u32[]{:S(2)}) collective-permute-start(bf16[4,256,128]{2,1,0:T(8,128)(2,1)} %collective-permute-done.30), channel_id=1, source_target_pairs={{2,3},{6,7},{10,11},{14,15},{18,19},{22,23},{26,27},{30,31}} | collective-permute-start | bytes 786440 | tf_op jit(solution)/shard_map/ppermute | solution.py:40
  176.4 11.9 %collective-permute-start.27 = (bf16[4,256,128]{2,1,0:T(8,128)(2,1)}, bf16[4,256,128]{2,1,0:T(8,128)(2,1)}, u32[]{:S(2)}, u32[]{:S(2)}) collective-permute-start(bf16[4,256,128]{2,1,0:T(8,128)(2,1)} %collective-permute-done.25), channel_id=1, source_target_pairs={{1,0},{5,4},{9,8},{13,12},{17,16},{21,20},{25,24},{29,28}} | collective-permute-start | bytes 786440 | tf_op jit(solution)/shard_map/ppermute | solution.py:41
  177.7 10.6 %collective-permute-start.26 = (bf16[4,256,128]{2,1,0:T(8,128)(2,1)}, bf16[4,256,128]{2,1,0:T(8,128)(2,1)}, u32[]{:S(2)}, u32[]{:S(2)}) collective-permute-start(bf16[4,256,128]{2,1,0:T(8,128)(2,1)} %collective-permute-done.24), channel_id=1, source_target_pairs={{2,3},{6,7},{10,11},{14,15},{18,19},{22,23},{26,27},{30,31}} | collective-permute-start | bytes 786440 | tf_op jit(solution)/shard_map/ppermute | solution.py:40
  180.2 3.9 %copy-start.10 = (bf16[512,512]{1,0:T(8,128)(2,1)}, bf16[512,512]{1,0:T(8,128)(2,1)S(1)}, u32[]{:S(2)}) copy-start(bf16[512,512]{1,0:T(8,128)(2,1)S(1)} %collective-permute-done.21.refs_7_) | copy-start | bytes 1572868
